TPU v7x, 32 devices: a whole 2x2x4 slice. The times are simulated.
32 devices in a mesh: grp: 4 (over x, core), exp: 8 (over z, y).
Axes of the slice: x: 2, y: 2, z: 4, core: 2. Of those that a mesh axis runs over, the one named last changes fastest.
Arguments:
- tokens: bfloat16 [8192, 2048], P(('grp', 'exp')), may hold values from -6 to 6
- expert_ids: int32 [8192, 1], P(('grp', 'exp')), may hold values from 0 to 7; in each aligned block of 256 rows (0 to 255, 256 to 511, ...) at most 64 rows name the same one
- gate_up_weight: bfloat16 [8, 2048, 1408], P('exp'), may hold values from -0.125 to 0.125
- down_weight: bfloat16 [8, 704, 2048], P('exp'), may hold values from -0.21875 to 0.21875
- grad_out: bfloat16 [8192, 2048], P(('grp', 'exp')), may hold values from -6 to 6
Outputs:
- mixed_out: bfloat16 [8192, 2048], P(('grp', 'exp'))
- grad_tokens: bfloat16 [8192, 2048], P(('grp', 'exp'))
- grad_gate_up: float32 [8, 2048, 1408], P('exp', 'grp')
- grad_down: float32 [8, 704, 2048], P('exp', None, 'grp')
Inputs may be any that keep to these rules, and one draw needn't show every extreme that they name: `expert_ids`: among the 256 rows of one device (aligned blocks of rows), no expert is named more than 64 times; some device names one expert exactly 64 times.
All inputs are finite; a program needn't handle non-finite values.
Results may differ from a plain program's by a relative error of at most 0.0053.
Values may be sent and summed in bfloat16 or wider, within the bound.
No kernel may reach another device: no remote copies, remote signals or barrier semaphores. Data moves between devices by JAX's collectives and lax.ppermute only.
A program may use at most 128 MiB of HBM per device.

v0:
```python
import jax
import jax.numpy as jnp
from jax import lax
from jax.sharding import PartitionSpec as P


def contract_rows(left, right):
    return lax.dot_general(
        left, right, (((0,), (0,)), ((), ())), preferred_element_type=jnp.float32
    )


def contract_cols(left, right):
    return lax.dot_general(
        left, right, (((1,), (1,)), ((), ())), preferred_element_type=jnp.float32
    )


def body(tokens, expert_ids, gate_up_weight, down_weight, grad_out):
    count_rows, width = tokens.shape
    experts = lax.axis_size("exp")
    capacity = 2 * count_rows // experts
    slots = experts * capacity
    route = expert_ids[:, 0]
    onehot = (route[:, None] == jnp.arange(experts, dtype=jnp.int32)[None, :]).astype(jnp.int32)
    ranks = jnp.sum((jnp.cumsum(onehot, axis=0) - 1) * onehot, axis=1)
    target = route * capacity + ranks
    placing = (target[None, :] == jnp.arange(slots, dtype=jnp.int32)[:, None]).astype(jnp.bfloat16)
    sent_x = jnp.dot(placing, tokens, preferred_element_type=jnp.float32).astype(jnp.bfloat16)
    sent_dy = jnp.dot(placing, grad_out, preferred_element_type=jnp.float32).astype(jnp.bfloat16)
    recv_x, recv_dy = (
        lax.all_to_all(
            sent_x.reshape(experts, capacity, width), "exp", split_axis=0, concat_axis=0, tiled=True
        ),
        lax.all_to_all(
            sent_dy.reshape(experts, capacity, width),
            "exp",
            split_axis=0,
            concat_axis=0,
            tiled=True,
        ),
    )
    slot_x = recv_x.reshape(slots, width)
    slot_dy = recv_dy.reshape(slots, width)
    weight_one = gate_up_weight[0]
    weight_two = down_weight[0]
    hidden_width = weight_two.shape[0]
    proj = jnp.dot(slot_x, weight_one, preferred_element_type=jnp.float32)
    gate = proj[:, :hidden_width]
    upper = proj[:, hidden_width:]
    sigma = jax.nn.sigmoid(gate)
    silu_gate = gate * sigma
    hidden = (silu_gate * upper).astype(jnp.bfloat16)
    branch = jnp.dot(hidden, weight_two, preferred_element_type=jnp.float32).astype(jnp.bfloat16)
    grad_hidden = contract_cols(slot_dy, weight_two)
    grad_proj = jnp.concatenate(
        [grad_hidden * upper * sigma * (1.0 + gate * (1.0 - sigma)), grad_hidden * silu_gate],
        axis=1,
    ).astype(jnp.bfloat16)
    grad_branch = contract_cols(grad_proj, weight_one).astype(jnp.bfloat16)
    back_out, back_grad = (
        lax.all_to_all(
            branch.reshape(experts, capacity, width), "exp", split_axis=0, concat_axis=0, tiled=True
        ),
        lax.all_to_all(
            grad_branch.reshape(experts, capacity, width),
            "exp",
            split_axis=0,
            concat_axis=0,
            tiled=True,
        ),
    )
    mixed_out = (
        tokens.astype(jnp.float32) + contract_rows(placing, back_out.reshape(slots, width))
    ).astype(jnp.bfloat16)
    grad_tokens = (
        grad_out.astype(jnp.float32) + contract_rows(placing, back_grad.reshape(slots, width))
    ).astype(jnp.bfloat16)
    grad_gate_up = lax.psum_scatter(
        contract_rows(slot_x, grad_proj), "grp", scatter_dimension=0, tiled=True
    )
    grad_down = lax.psum_scatter(
        contract_rows(hidden, slot_dy), "grp", scatter_dimension=1, tiled=True
    )
    return (mixed_out, grad_tokens, grad_gate_up[None], grad_down[None])


def solution(mesh):
    in_specs = (
        P(("grp", "exp"), None),
        P(("grp", "exp"), None),
        P("exp", None, None),
        P("exp", None, None),
        P(("grp", "exp"), None),
    )
    out_specs = (
        P(("grp", "exp"), None),
        P(("grp", "exp"), None),
        P("exp", "grp", None),
        P("exp", None, "grp"),
    )
    return jax.shard_map(body, mesh=mesh, in_specs=in_specs, out_specs=out_specs, check_vma=False)
```

profile of v0, /device:TPU:0, one launch (start us, length us, event | category | flops | bytes accessed | tf_op | source)
XLA Modules:
  0.0 290.3 jit_solution(1514517443010216063)
XLA Ops:
  7.2 0.0 copy-start
  7.2 0.8 fusion.19
  8.0 0.6 reduce-window.6
  8.6 0.2 slice_reduce_fusion
  8.8 0.8 fusion.18
  9.6 0.7 multiply_add_fusion
  10.3 3.3 %convolution_convert_fusion.1 = bf16[512,2048]{1,0:T(8,128)(2,1)} fusion(bf16[256,2048]{1,0:T(8,128)(2,1)} %param.5, s32[256]{0:T(256)S(1)} %multiply_add_fusion), kind=kOutput, calls=%fused_computation.5 | convolution fusion | flops 538050560 | bytes 3146752 | tf_op jit(solution)/shard_map/dot_general | solution.py:29
  13.6 7.3 %all-to-all-start = ((bf16[8,64,2048]{2,1,0:T(8,128)(2,1)}), bf16[8,64,2048]{2,1,0:T(8,128)(2,1)}, u32[]{:S(2)}, u32[]{:S(2)}) async-start(bf16[8,64,2048]{2,1,0:T(8,128)(2,1)} %bitcast.43), calls=%async_computation | async-start | bytes 4194304 | tf_op jit(solution)/shard_map/all_to_all | solution.py:32
  20.8 3.2 %convolution_convert_fusion = bf16[512,2048]{1,0:T(8,128)(2,1)} fusion(bf16[256,2048]{1,0:T(8,128)(2,1)} %param.9, s32[256]{0:T(256)S(1)} %multiply_add_fusion), kind=kOutput, calls=%fused_computation.4 | convolution fusion | flops 538050560 | bytes 3146752 | tf_op jit(solution)/shard_map/dot_general | solution.py:30
  24.1 45.1 %all-to-all-done = bf16[8,64,2048]{2,1,0:T(8,128)(2,1)} async-done(((bf16[8,64,2048]{2,1,0:T(8,128)(2,1)}), bf16[8,64,2048]{2,1,0:T(8,128)(2,1)}, u32[]{:S(2)}, u32[]{:S(2)}) %all-to-all-start) | async-done | bytes 2097184 | tf_op jit(solution)/shard_map/all_to_all | solution.py:32
  69.2 4.3 %all-to-all-start.2 = ((bf16[8,64,2048]{2,1,0:T(8,128)(2,1)}), bf16[8,64,2048]{2,1,0:T(8,128)(2,1)}, u32[]{:S(2)}, u32[]{:S(2)}) async-start(bf16[8,64,2048]{2,1,0:T(8,128)(2,1)} %bitcast.42), calls=%async_computation.2 | async-start | bytes 4194304 | tf_op jit(solution)/shard_map/all_to_all | solution.py:35
  73.5 0.0 reduce-scatter.5.cloned.1.call-start
  73.6 8.3 %fusion.2 = f32[512,1408]{1,0:T(8,128)} fusion(bf16[512,2048]{1,0:T(8,128)(2,1)} %bitcast.5, bf16[1,2048,1408]{2,1,0:T(8,128)(2,1)} %param.7), kind=kOutput, calls=%fused_computation.2 | convolution fusion | flops 2952790016 | bytes 10747904 | tf_op jit(solution)/shard_map/dot_general | solution.py:48
  81.8 39.5 %all-to-all-done.2 = bf16[8,64,2048]{2,1,0:T(8,128)(2,1)} async-done(((bf16[8,64,2048]{2,1,0:T(8,128)(2,1)}), bf16[8,64,2048]{2,1,0:T(8,128)(2,1)}, u32[]{:S(2)}, u32[]{:S(2)}) %all-to-all-start.2) | async-done | bytes 2097184 | tf_op jit(solution)/shard_map/all_to_all | solution.py:35
  121.4 0.0 copy-done
  121.4 5.8 %multiply_convert_fusion.1 = (bf16[512,704]{1,0:T(8,128)(2,1)}, bf16[512,704]{1,0:T(8,128)(2,1)}, bf16[512,704]{1,0:T(8,128)(2,1)S(1)}) fusion(f32[512,1408]{1,0:T(8,128)} %fusion.2, bf16[512,2048]{1,0:T(8,128)(2,1)} %bitcast.11, bf16[1,704,2048]{2,1,0:T(8,128)(2,1)S(1)} %copy-done), kind=kOutput, calls=%fused_computation.16 | convolution fusion | flops 1481801728 | bytes 10027008 | tf_op jit(solution)/shard_map/dot_general | solution.py:14
  127.2 0.0 copy-start.1
  127.2 0.9 copy-done.1
  128.1 5.7 %fusion.22 = f32[704,2048]{1,0:T(8,128)} fusion(bf16[512,704]{1,0:T(8,128)(2,1)S(1)} %get-tuple-element.6, bf16[512,2048]{1,0:T(8,128)(2,1)} %bitcast.11), kind=kOutput, calls=%fused_computation.36 | convolution fusion | flops 1476395008 | bytes 8585216 | tf_op jit(solution)/shard_map/dot_general | solution.py:8
  133.8 0.0 reduce-scatter.5.cloned.1.call-update
  133.8 0.2 reduce-scatter.3.cloned.1.call-start
  134.1 11.1 %fusion.13 = f32[2048,1408]{1,0:T(8,128)} fusion(bf16[512,2048]{1,0:T(8,128)(2,1)} %bitcast.5, bf16[512,704]{1,0:T(8,128)(2,1)} %get-tuple-element.5, bf16[512,704]{1,0:T(8,128)(2,1)} %get-tuple-element.4), kind=kOutput, calls=%fused_computation.21 | convolution fusion | flops 2955673600 | bytes 15073280 | tf_op jit(solution)/shard_map/dot_general | solution.py:8
  145.2 0.0 reduce-scatter.3.cloned.1.call-update
  145.2 8.1 %fusion.4 = bf16[512,2048]{1,0:T(8,128)(2,1)} fusion(bf16[1,2048,1408]{2,1,0:T(8,128)(2,1)} %param.7, bf16[512,704]{1,0:T(8,128)(2,1)} %get-tuple-element.5, bf16[512,704]{1,0:T(8,128)(2,1)} %get-tuple-element.4), kind=kOutput, calls=%fused_computation.7 | convolution fusion | flops 2956722176 | bytes 9306112 | tf_op jit(solution)/shard_map/dot_general | solution.py:14
  153.3 4.6 %all-to-all-start.3 = ((bf16[8,64,2048]{2,1,0:T(8,128)(2,1)}), bf16[8,64,2048]{2,1,0:T(8,128)(2,1)}, u32[]{:S(2)}, u32[]{:S(2)}) async-start(bf16[8,64,2048]{2,1,0:T(8,128)(2,1)} %bitcast.45), calls=%async_computation.3 | async-start | bytes 4194304 | tf_op jit(solution)/shard_map/all_to_all | solution.py:65
  157.9 4.2 %convolution_convert_fusion.2 = bf16[512,2048]{1,0:T(8,128)(2,1)} fusion(bf16[512,704]{1,0:T(8,128)(2,1)} %copy-done.1, bf16[1,704,2048]{2,1,0:T(8,128)(2,1)S(1)} %copy-done), kind=kOutput, calls=%fused_computation.6 | convolution fusion | flops 1477443584 | bytes 5701632 | tf_op jit(solution)/shard_map/dot_general | solution.py:54
  162.1 44.3 %all-to-all-done.3 = bf16[8,64,2048]{2,1,0:T(8,128)(2,1)} async-done(((bf16[8,64,2048]{2,1,0:T(8,128)(2,1)}), bf16[8,64,2048]{2,1,0:T(8,128)(2,1)}, u32[]{:S(2)}, u32[]{:S(2)}) %all-to-all-start.3) | async-done | bytes 2097184 | tf_op jit(solution)/shard_map/all_to_all | solution.py:65
  206.4 4.4 %all-to-all-start.1 = ((bf16[8,64,2048]{2,1,0:T(8,128)(2,1)}), bf16[8,64,2048]{2,1,0:T(8,128)(2,1)}, u32[]{:S(2)}, u32[]{:S(2)}) async-start(bf16[8,64,2048]{2,1,0:T(8,128)(2,1)} %bitcast.44), calls=%async_computation.1 | async-start | bytes 4194304 | tf_op jit(solution)/shard_map/all_to_all | solution.py:62
  210.8 3.6 %fusion.11 = bf16[256,2048]{1,0:T(8,128)(2,1)} fusion(bf16[512,2048]{1,0:T(8,128)(2,1)} %bitcast.13, bf16[256,2048]{1,0:T(8,128)(2,1)} %param.9, s32[256]{0:T(256)S(1)} %multiply_add_fusion), kind=kOutput, calls=%fused_computation.14 | convolution fusion | flops 538574848 | bytes 4195328 | tf_op jit(solution)/shard_map/dot_general | solution.py:8
  214.3 44.2 %all-to-all-done.1 = bf16[8,64,2048]{2,1,0:T(8,128)(2,1)} async-done(((bf16[8,64,2048]{2,1,0:T(8,128)(2,1)}), bf16[8,64,2048]{2,1,0:T(8,128)(2,1)}, u32[]{:S(2)}, u32[]{:S(2)}) %all-to-all-start.1) | async-done | bytes 2097184 | tf_op jit(solution)/shard_map/all_to_all | solution.py:62
  258.6 3.6 %fusion.10 = bf16[256,2048]{1,0:T(8,128)(2,1)} fusion(bf16[512,2048]{1,0:T(8,128)(2,1)} %bitcast.9, bf16[256,2048]{1,0:T(8,128)(2,1)} %param.5, s32[256]{0:T(256)S(1)} %multiply_add_fusion), kind=kOutput, calls=%fused_computation.13 | convolution fusion | flops 538574848 | bytes 4195328 | tf_op jit(solution)/shard_map/dot_general | solution.py:8
  262.2 0.0 reduce-scatter.5.cloned.1.call-done
  262.2 21.3 %reduce-scatter.3.cloned.1.call-done = f32[512,1408]{1,0:T(8,128)} async-done(((f32[2048,1408]{1,0:T(8,128)}), f32[512,1408]{1,0:T(8,128)}) %reduce-scatter.3.cloned.1.call-update) | async-done | bytes 2883600 | tf_op jit(solution)/shard_map/reduce_scatter | solution.py:79
  (2 shorter events, 0.0 us)
Async XLA Ops:
  7.2 114.2 %copy-start = (bf16[1,704,2048]{2,1,0:T(8,128)(2,1)S(1)}, bf16[1,704,2048]{2,1,0:T(8,128)(2,1)}, u32[]{:S(2)}) copy-start(bf16[1,704,2048]{2,1,0:T(8,128)(2,1)} %param.8) | copy-start | bytes 8650756
  13.6 55.6 %all-to-all-start = ((bf16[8,64,2048]{2,1,0:T(8,128)(2,1)}), bf16[8,64,2048]{2,1,0:T(8,128)(2,1)}, u32[]{:S(2)}, u32[]{:S(2)}) async-start(bf16[8,64,2048]{2,1,0:T(8,128)(2,1)} %bitcast.43), calls=%async_computation | async-start | bytes 4194304 | tf_op jit(solution)/shard_map/all_to_all | solution.py:32
  69.2 52.2 %all-to-all-start.2 = ((bf16[8,64,2048]{2,1,0:T(8,128)(2,1)}), bf16[8,64,2048]{2,1,0:T(8,128)(2,1)}, u32[]{:S(2)}, u32[]{:S(2)}) async-start(bf16[8,64,2048]{2,1,0:T(8,128)(2,1)} %bitcast.42), calls=%async_computation.2 | async-start | bytes 4194304 | tf_op jit(solution)/shard_map/all_to_all | solution.py:35
  73.5 188.6 %reduce-scatter.5.cloned.1.call-start = ((), (), s32[]{:S(2)}) async-start(), calls=%async_computation.7 | async-start | bytes 7208960 | tf_op jit(solution)/shard_map/reduce_scatter | solution.py:82
  127.2 0.9 copy-start.1
  133.8 149.6 %reduce-scatter.3.cloned.1.call-start = ((), (), s32[]{:S(2)}) async-start(), calls=%async_computation.6 | async-start | bytes 14417920 | tf_op jit(solution)/shard_map/reduce_scatter | solution.py:79
  153.3 53.1 %all-to-all-start.3 = ((bf16[8,64,2048]{2,1,0:T(8,128)(2,1)}), bf16[8,64,2048]{2,1,0:T(8,128)(2,1)}, u32[]{:S(2)}, u32[]{:S(2)}) async-start(bf16[8,64,2048]{2,1,0:T(8,128)(2,1)} %bitcast.45), calls=%async_computation.3 | async-start | bytes 4194304 | tf_op jit(solution)/shard_map/all_to_all | solution.py:65
  206.4 52.2 %all-to-all-start.1 = ((bf16[8,64,2048]{2,1,0:T(8,128)(2,1)}), bf16[8,64,2048]{2,1,0:T(8,128)(2,1)}, u32[]{:S(2)}, u32[]{:S(2)}) async-start(bf16[8,64,2048]{2,1,0:T(8,128)(2,1)} %bitcast.44), calls=%async_computation.1 | async-start | bytes 4194304 | tf_op jit(solution)/shard_map/all_to_all | solution.py:62
Sparse Core Ops, SparseCore 0:
  134.0 53.8 reduce-scatter.4
  191.2 92.1 reduce-scatter.2
where the time goes:
time: 291 us; the launch traced here: 290 us
  waiting for transfers between devices  194 us (67%)
  matrix products  56.9 us (20%)
  starting transfers between devices  20.8 us (7%)
  between operations  14.1 us (5%)
    all_to_all x1, waiting for transfers between devices, body(): lax.all_to_all(sent_x.reshape(experts, capacity, width), 'exp', split_axi...  45.1 us
    all_to_all x1, waiting for transfers between devices, body(): lax.all_to_all(grad_branch.reshape(experts, capacity, width), 'exp', spli...  44.3 us
    all_to_all x1, waiting for transfers between devices, body(): lax.all_to_all(branch.reshape(experts, capacity, width), 'exp', split_axi...  44.2 us
    all_to_all x1, waiting for transfers between devices, body(): lax.all_to_all(sent_dy.reshape(experts, capacity, width), 'exp', split_ax...  39.5 us
    dot_general x4, matrix products, contract_rows(): lax.dot_general(left, right, (((0,), (0,)), ((), ())), preferred_element_...  24 us
    reduce_scatter x1, waiting for transfers between devices, body(): lax.psum_scatter(contract_rows(slot_x, grad_proj), 'grp', scatter_dimensi...  21.3 us
    dot_general x2, matrix products, contract_cols(): lax.dot_general(left, right, (((1,), (1,)), ((), ())), preferred_element_...  13.9 us
    dot_general x1, matrix products, body(): proj = jnp.dot(slot_x, weight_one, preferred_element_type=jnp.float32)  8.26 us
  transfers between devices with their start and end apart: 6, of which 5 were waited for; matrix products, arithmetic and copies ran while one was open for 15% of the time, Pallas kernels for 0%

commit v1 on v0

v1 whole, which is shorter than its diff:
```python
import jax
import jax.numpy as jnp
from jax import lax
from jax.experimental import pallas as pl
from jax.experimental.pallas import tpu as pltpu
from jax.sharding import PartitionSpec as P

VMEM_BYTES = 48 * 1024 * 1024


def dot(left, right, dims):
    return lax.dot_general(left, right, (dims, ((), ())), preferred_element_type=jnp.float32)


def route_kernel(experts, cap, rel_ref, data_ref, place_ref, *block_refs):
    rows = rel_ref.shape[0]
    slots = experts * cap

    @pl.when(pl.program_id(0) == 0)
    def _():
        rel = rel_ref[...]
        onehot = lax.broadcasted_iota(jnp.int32, (rows, 128), 1) == rel
        before = lax.broadcasted_iota(jnp.int32, (rows, rows), 1) < lax.broadcasted_iota(jnp.int32, (rows, rows), 0)
        ranks = dot(before.astype(jnp.bfloat16), onehot.astype(jnp.bfloat16), ((1,), (0,)))
        rank = jnp.sum(jnp.where(onehot, ranks, 0.0), axis=1, keepdims=True).astype(jnp.int32)
        target = rel * cap + rank
        place_ref[...] = (lax.broadcasted_iota(jnp.int32, (rows, slots), 1) == target).astype(jnp.bfloat16)

    place_kernel(experts, cap, place_ref, data_ref, *block_refs)


def place_kernel(experts, cap, place_ref, data_ref, *block_refs):
    moved = dot(place_ref[...], data_ref[...], ((0,), (0,))).astype(jnp.bfloat16)
    for index in range(experts):
        block_refs[index][...] = moved[index * cap : (index + 1) * cap]


def combine_kernel(place_ref, data_ref, *refs):
    back = jnp.concatenate([ref[...] for ref in refs[:-1]], axis=0)
    total = data_ref[...].astype(jnp.float32) + dot(place_ref[...], back, ((1,), (0,)))
    refs[-1][...] = total.astype(jnp.bfloat16)


def params():
    return pltpu.CompilerParams(vmem_limit_bytes=VMEM_BYTES, dimension_semantics=("arbitrary",))


def cost(rows, slots, width):
    return pl.CostEstimate(
        flops=2 * rows * slots * width, bytes_accessed=2 * (rows + slots) * width, transcendentals=0
    )


def route_and_place(rel, data, experts, cap):
    rows, width = data.shape
    slots = experts * cap
    step = width // 4
    return pl.pallas_call(
        lambda *refs: route_kernel(experts, cap, *refs),
        grid=(width // step,),
        in_specs=[pl.BlockSpec((rows, 1), lambda i: (0, 0)), pl.BlockSpec((rows, step), lambda i: (0, i))],
        out_specs=[pl.BlockSpec((rows, slots), lambda i: (0, 0))]
        + [pl.BlockSpec((cap, step), lambda i: (0, i))] * experts,
        out_shape=[jax.ShapeDtypeStruct((rows, slots), jnp.bfloat16)]
        + [jax.ShapeDtypeStruct((cap, width), jnp.bfloat16)] * experts,
        compiler_params=params(),
        cost_estimate=cost(rows, slots, width),
        name="route_and_place",
    )(rel, data)


def place(placing, data, experts, cap):
    rows, width = data.shape
    slots = experts * cap
    step = width // 4
    return pl.pallas_call(
        lambda *refs: place_kernel(experts, cap, *refs),
        grid=(width // step,),
        in_specs=[pl.BlockSpec((rows, slots), lambda i: (0, 0)), pl.BlockSpec((rows, step), lambda i: (0, i))],
        out_specs=[pl.BlockSpec((cap, step), lambda i: (0, i))] * experts,
        out_shape=[jax.ShapeDtypeStruct((cap, width), jnp.bfloat16)] * experts,
        compiler_params=params(),
        cost_estimate=cost(rows, slots, width),
        name="place",
    )(placing, data)


def combine(placing, data, blocks):
    rows, width = data.shape
    cap = blocks[0].shape[0]
    slots = placing.shape[1]
    step = width // 4
    return pl.pallas_call(
        combine_kernel,
        grid=(width // step,),
        in_specs=[pl.BlockSpec((rows, slots), lambda i: (0, 0)), pl.BlockSpec((rows, step), lambda i: (0, i))]
        + [pl.BlockSpec((cap, step), lambda i: (0, i))] * len(blocks),
        out_specs=pl.BlockSpec((rows, step), lambda i: (0, i)),
        out_shape=jax.ShapeDtypeStruct((rows, width), jnp.bfloat16),
        compiler_params=params(),
        cost_estimate=cost(rows, slots, width),
        name="combine",
    )(placing, data, *blocks)


def exchange(blocks):
    experts = len(blocks)
    moved = {0: blocks[0]}
    for mask in range(experts - 1, 0, -1):
        moved[mask] = lax.ppermute(blocks[mask], "exp", [(i, i ^ mask) for i in range(experts)])
    return [moved[mask] for mask in range(experts)]


def halving_sum(parts):
    count = len(parts)
    bit = 1
    while bit < count:
        pairs = [(i, i ^ bit) for i in range(count)]
        for q in range(count - 2 * bit, -1, -2 * bit):
            got = [lax.ppermute(part.astype(jnp.bfloat16), "grp", pairs) for part in parts[q | bit]]
            parts[q] = [part + piece.astype(jnp.float32) for part, piece in zip(parts[q], got)]
        bit *= 2
    return parts[0]


def body(tokens, expert_ids, gate_up_weight, down_weight, grad_out):
    rows, width = tokens.shape
    experts = lax.axis_size("exp")
    groups = lax.axis_size("grp")
    cap = 2 * rows // experts
    rel = expert_ids ^ lax.axis_index("exp").astype(jnp.int32)
    placing, *sent_x = route_and_place(rel, tokens, experts, cap)
    sent_dy = place(placing, grad_out, experts, cap)
    slot_x = jnp.concatenate(exchange(sent_x), axis=0)
    slot_dy = jnp.concatenate(exchange(sent_dy), axis=0)
    weight_one = gate_up_weight[0]
    weight_two = down_weight[0]
    hidden_width = weight_two.shape[0]

    proj = dot(slot_x, weight_one, ((1,), (0,)))
    gate = proj[:, :hidden_width]
    upper = proj[:, hidden_width:]
    sigma = jax.nn.sigmoid(gate)
    silu_gate = gate * sigma
    hidden = (silu_gate * upper).astype(jnp.bfloat16)
    branch = dot(hidden, weight_two, ((1,), (0,))).astype(jnp.bfloat16)
    back_out = exchange([branch[i * cap : (i + 1) * cap] for i in range(experts)])

    grad_hidden = dot(slot_dy, weight_two, ((1,), (1,)))
    grad_proj = jnp.concatenate(
        [grad_hidden * upper * sigma * (1.0 + gate * (1.0 - sigma)), grad_hidden * silu_gate], axis=1
    ).astype(jnp.bfloat16)
    grad_branch = dot(grad_proj, weight_one, ((1,), (1,))).astype(jnp.bfloat16)
    back_grad = exchange([grad_branch[i * cap : (i + 1) * cap] for i in range(experts)])

    group = lax.axis_index("grp").astype(jnp.int32)
    share = width // groups
    parts = []
    for q in range(groups):
        start = (group ^ q) * share
        part_x = lax.dynamic_slice_in_dim(slot_x, start, share, 1)
        part_dy = lax.dynamic_slice_in_dim(slot_dy, start, share, 1)
        parts.append([dot(part_x, grad_proj, ((0,), (0,))), dot(hidden, part_dy, ((0,), (0,)))])
    grad_gate_up, grad_down = halving_sum(parts)

    mixed_out = combine(placing, tokens, back_out)
    grad_tokens = combine(placing, grad_out, back_grad)
    return (mixed_out, grad_tokens, grad_gate_up[None], grad_down[None])


def solution(mesh):
    in_specs = (
        P(("grp", "exp"), None),
        P(("grp", "exp"), None),
        P("exp", None, None),
        P("exp", None, None),
        P(("grp", "exp"), None),
    )
    out_specs = (
        P(("grp", "exp"), None),
        P(("grp", "exp"), None),
        P("exp", "grp", None),
        P("exp", None, "grp"),
    )
    return jax.shard_map(body, mesh=mesh, in_specs=in_specs, out_specs=out_specs, check_vma=False)
```

time: 291 us -> 270 us (0.928)
  waiting for transfers between devices: 194 us -> 105 us
  starting transfers between devices: 20.8 us -> 91.1 us
  local copies, waits for them, and re-layouts: 1.12 us -> 28.9 us
  matrix products: 56.9 us -> 31.3 us
  between operations: 14.1 us -> 1.16 us
  Pallas kernels: 0 us -> 11.8 us
    all_to_all x4 -> x0, waiting for transfers between devices: 173 us -> none  [the longest x1 45.1 us: body(): lax.all_to_all(sent_x.reshape(experts, capacity, width), 'exp', split_axi...]
    ppermute x0 -> x34, waiting for transfers between devices: none -> 105 us  [the longest x28 105 us: exchange(): lax.ppermute(blocks[mask], 'exp', [(i, i ^ mask) for i in range(experts)])]
    ppermute x0 -> x34, starting transfers between devices: none -> 91.1 us  [the longest x28 87.6 us: exchange(): lax.ppermute(blocks[mask], 'exp', [(i, i ^ mask) for i in range(experts)])]
    unnamed x4 -> x125, local copies, waits for them, and re-layouts: 0.91 us -> 26.9 us
    dot_general x10 -> x12, matrix products: 56.9 us -> 31.3 us  [dot(): lax.dot_general(left, right, (dims, ((), ())), preferred_element_type=jnp...]
    reduce_scatter x2 -> x0, waiting for transfers between devices: 21.3 us -> none  [the longest x1 21.3 us: body(): lax.psum_scatter(contract_rows(slot_x, grad_proj), 'grp', scatter_dimensi...]
    all_to_all x4 -> x0, starting transfers between devices: 20.6 us -> none  [the longest x1 7.28 us: body(): lax.all_to_all(sent_x.reshape(experts, capacity, width), 'exp', split_axi...]
    pallas_call x0 -> x4, Pallas kernels: none -> 11.8 us  [the longest x2 6.43 us: combine(): pl.pallas_call(combine_kernel, grid=(width // step,), in_specs=[pl.BlockS...]
  transfers between devices with their start and end apart: 6 -> 34, of which waited for: 5 -> 15; matrix products, arithmetic and copies ran while one was open for 15% -> 12% of each run, Pallas kernels for 0% -> 2%
where the time goes in v1:
time: 270 us
  waiting for transfers between devices  105 us (39%)
  starting transfers between devices  91.1 us (34%)
  matrix products  31.3 us (12%)
  local copies, waits for them, and re-layouts  28.9 us (11%)
  Pallas kernels  11.8 us (4%)
    ppermute x28, waiting for transfers between devices, exchange(): lax.ppermute(blocks[mask], 'exp', [(i, i ^ mask) for i in range(experts)])  105 us
    ppermute x28, starting transfers between devices, exchange(): lax.ppermute(blocks[mask], 'exp', [(i, i ^ mask) for i in range(experts)])  87.6 us
    dot_general x12, matrix products, dot(): lax.dot_general(left, right, (dims, ((), ())), preferred_element_type=jnp...  31.3 us
    unnamed x125, local copies, waits for them, and re-layouts  26.9 us
    pallas_call x2, Pallas kernels, combine(): pl.pallas_call(combine_kernel, grid=(width // step,), in_specs=[pl.BlockS...  6.43 us
  transfers between devices with their start and end apart: 34, of which 15 were waited for; matrix products, arithmetic and copies ran while one was open for 12% of the time, Pallas kernels for 2%

profile of v1, /device:TPU:0, one launch (start us, length us, event | category | flops | bytes accessed | tf_op | source)
XLA Modules:
  0.0 269.6 jit_solution(213755195786464105)
XLA Ops:
  0.6 1.0 copy.12
  1.7 1.3 copy-done.3
  3.0 2.9 %route_and_place.1 = (bf16[256,512]{1,0:T(8,128)(2,1)S(1)}, bf16[64,2048]{1,0:T(8,128)(2,1)S(1)}, bf16[64,2048]{1,0:T(8,128)(2,1)}, bf16[64,2048]{1,0:T(8,128)(2...) custom-call(s32[256,1]{1,0:T(8,128)S(1)} %broadcast_xor_fusion.refs_, ...), custom_call_target="tpu_custom_call" | custom-call | flops 536870912 | bytes 3145728 | tf_op jit(solution)/shard_map/route_and_place/pallas_call | solution.py:58
  5.9 2.5 place.1
  9.1 3.0 %collective-permute-start.14 = (bf16[64,2048]{1,0:T(8,128)(2,1)}, bf16[64,2048]{1,0:T(8,128)(2,1)}, u32[]{:S(2)}, u32[]{:S(2)}) collective-permute-start(bf16[64,2048]{1,0:T(8,128)(2,1)} %get-tuple-element.31), channel_id=1, source_target_pairs={{0,1},{1,0},{2,3},{3,2},{4,5},{5,4},{6,7},{7,6},{8,9},{9,8},{10,11... | collective-permute-start | bytes 786440 | tf_op jit(solution)/shard_map/ppermute | solution.py:110
  12.1 1.6 collective-permute-start.15
  13.7 1.9 collective-permute-start
  15.6 1.6 collective-permute-start.1
  18.6 11.3 %collective-permute-done = bf16[64,2048]{1,0:T(8,128)(2,1)} collective-permute-done((bf16[64,2048]{1,0:T(8,128)(2,1)}, bf16[64,2048]{1,0:T(8,128)(2,1)}, u32[]{:S(2)}, u32[]{:S(2)}) %collective-permute-start) | collective-permute-done | bytes 262176 | tf_op jit(solution)/shard_map/ppermute | solution.py:110
  29.9 2.8 %collective-permute-start.2 = (bf16[64,2048]{1,0:T(8,128)(2,1)}, bf16[64,2048]{1,0:T(8,128)(2,1)S(1)}, u32[]{:S(2)}, u32[]{:S(2)}) collective-permute-start(bf16[64,2048]{1,0:T(8,128)(2,1)} %copy-done.43), channel_id=1, source_target_pairs={{0,3},{1,2},{2,1},{3,0},{4,7},{5,6},{6,5},{7,4},{8,11},{9,10},{10,... | collective-permute-start | bytes 786440 | tf_op jit(solution)/shard_map/ppermute | solution.py:110
  32.7 1.7 constant_dynamic-update-slice_fusion.6
  34.4 2.6 collective-permute-start.3
  37.0 1.7 constant_dynamic-update-slice_fusion.5
  38.7 3.3 %collective-permute-done.2 = bf16[64,2048]{1,0:T(8,128)(2,1)S(1)} collective-permute-done((bf16[64,2048]{1,0:T(8,128)(2,1)}, bf16[64,2048]{1,0:T(8,128)(2,1)S(1)}, u32[]{:S(2)}, u32[]{:S(2)}) %collective-permute-start.2) | collective-permute-done | bytes 262176 | tf_op jit(solution)/shard_map/ppermute | solution.py:110
  42.0 2.1 collective-permute-start.4
  44.8 10.9 %collective-permute-done.3 = bf16[64,2048]{1,0:T(8,128)(2,1)S(1)} collective-permute-done((bf16[64,2048]{1,0:T(8,128)(2,1)}, bf16[64,2048]{1,0:T(8,128)(2,1)S(1)}, u32[]{:S(2)}, u32[]{:S(2)}) %collective-permute-start.3) | collective-permute-done | bytes 262176 | tf_op jit(solution)/shard_map/ppermute | solution.py:110
  55.7 2.2 collective-permute-start.5
  58.6 11.1 %collective-permute-done.4 = bf16[64,2048]{1,0:T(8,128)(2,1)S(1)} collective-permute-done((bf16[64,2048]{1,0:T(8,128)(2,1)}, bf16[64,2048]{1,0:T(8,128)(2,1)S(1)}, u32[]{:S(2)}, u32[]{:S(2)}) %collective-permute-start.4) | collective-permute-done | bytes 262176 | tf_op jit(solution)/shard_map/ppermute | solution.py:110
  69.7 3.1 %collective-permute-start.6 = (bf16[64,2048]{1,0:T(8,128)(2,1)S(1)}, bf16[64,2048]{1,0:T(8,128)(2,1)S(1)}, u32[]{:S(2)}, u32[]{:S(2)}) collective-permute-start(bf16[64,2048]{1,0:T(8,128)(2,1)S(1)} %copy-done.39), channel_id=1, source_target_pairs={{0,7},{1,6},{2,5},{3,4},{4,3},{5,2},{6,1},{7,0},{8,15},{9,14},{10,... | collective-permute-start | bytes 786440 | tf_op jit(solution)/shard_map/ppermute | solution.py:110
  73.5 3.1 %collective-permute-start.17 = (bf16[64,2048]{1,0:T(8,128)(2,1)S(1)}, bf16[64,2048]{1,0:T(8,128)(2,1)S(1)}, u32[]{:S(2)}, u32[]{:S(2)}) collective-permute-start(bf16[64,2048]{1,0:T(8,128)(2,1)S(1)} %copy-done.37), channel_id=1, source_target_pairs={{0,4},{1,5},{2,6},{3,7},{4,0},{5,1},{6,2},{7,3},{8,12},{9,13},{10,... | collective-permute-start | bytes 786440 | tf_op jit(solution)/shard_map/ppermute | solution.py:110
  77.3 3.2 %collective-permute-done.6 = bf16[64,2048]{1,0:T(8,128)(2,1)S(1)} collective-permute-done((bf16[64,2048]{1,0:T(8,128)(2,1)S(1)}, bf16[64,2048]{1,0:T(8,128)(2,1)S(1)}, u32[]{:S(2)}, u32[]{:S(2)}) %collective-permute-start.6) | collective-permute-done | bytes 262176 | tf_op jit(solution)/shard_map/ppermute | solution.py:110
  80.6 11.0 %collective-permute-start.18 = (bf16[64,2048]{1,0:T(8,128)(2,1)S(1)}, bf16[64,2048]{1,0:T(8,128)(2,1)S(1)}, u32[]{:S(2)}, u32[]{:S(2)}) collective-permute-start(bf16[64,2048]{1,0:T(8,128)(2,1)S(1)} %copy-done.35), channel_id=1, source_target_pairs={{0,5},{1,4},{2,7},{3,6},{4,1},{5,0},{6,3},{7,2},{8,13},{9,12},{10,... | collective-permute-start | bytes 786440 | tf_op jit(solution)/shard_map/ppermute | solution.py:110
  92.3 6.5 %fusion.2 = f32[512,1408]{1,0:T(8,128)S(1)} fusion(bf16[512,2048]{1,0:T(8,128)(2,1)} %constant_dynamic-update-slice_fusion, bf16[1,2048,1408]{2,1,0:T(8,128)(2,1)} %param.7), kind=kOutput, calls=%fused_computation.2 | convolution fusion | flops 2952790016 | bytes 10747904 | tf_op jit(solution)/shard_map/dot_general | solution.py:12
  98.8 4.5 %collective-permute-start.19 = (bf16[64,2048]{1,0:T(8,128)(2,1)S(1)}, bf16[64,2048]{1,0:T(8,128)(2,1)S(1)}, u32[]{:S(2)}, u32[]{:S(2)}) collective-permute-start(bf16[64,2048]{1,0:T(8,128)(2,1)S(1)} %copy-done.33), channel_id=1, source_target_pairs={{0,6},{1,7},{2,4},{3,5},{4,2},{5,3},{6,0},{7,1},{8,14},{9,15},{10,... | collective-permute-start | bytes 786440 | tf_op jit(solution)/shard_map/ppermute | solution.py:110
  103.4 1.0 constant_dynamic-update-slice_fusion.14
  104.8 1.0 constant_dynamic-update-slice_fusion.13
  105.8 1.0 constant_dynamic-update-slice_fusion.12
  106.8 5.0 %collective-permute-done.17 = bf16[64,2048]{1,0:T(8,128)(2,1)S(1)} collective-permute-done((bf16[64,2048]{1,0:T(8,128)(2,1)S(1)}, bf16[64,2048]{1,0:T(8,128)(2,1)S(1)}, u32[]{:S(2)}, u32[]{:S(2)}) %collective-permute-start.17) | collective-permute-done | bytes 262176 | tf_op jit(solution)/shard_map/ppermute | solution.py:110
  111.9 5.5 %collective-permute-done.18 = bf16[64,2048]{1,0:T(8,128)(2,1)S(1)} collective-permute-done((bf16[64,2048]{1,0:T(8,128)(2,1)S(1)}, bf16[64,2048]{1,0:T(8,128)(2,1)S(1)}, u32[]{:S(2)}, u32[]{:S(2)}) %collective-permute-start.18) | collective-permute-done | bytes 262176 | tf_op jit(solution)/shard_map/ppermute | solution.py:110
  117.5 2.3 multiply_convert_fusion.1
  120.9 3.9 %fusion.7 = bf16[512,2048]{1,0:T(8,128)(2,1)S(1)} fusion(bf16[1,2048,1408]{2,1,0:T(8,128)(2,1)S(1)} %bitcast.26, bf16[512,704]{1,0:T(8,128)(2,1)S(1)} %get-tuple-element.39, bf16[512,704]{1,0:T(8,128)(2,1)S(1)} %get-tuple-element.38), kind=kOutput, calls=%fused_computation.12 | convolution fusion | flops 2956722176 | bytes 9306112 | tf_op jit(solution)/shard_map/dot_general | solution.py:12
  124.8 1.0 convolution_convert_fusion
  127.3 1.6 collective-permute-start.21
  128.9 8.7 %collective-permute-start.22 = (bf16[64,2048]{1,0:T(8,128)(2,1)S(1)}, bf16[64,2048]{1,0:T(8,128)(2,1)S(1)}, u32[]{:S(2)}, u32[]{:S(2)}) collective-permute-start(bf16[64,2048]{1,0:T(8,128)(2,1)S(1)} %get-tuple-element.46), channel_id=1, source_target_pairs={{0,2},{1,3},{2,0},{3,1},{4,6},{5,7},{6,4},{7,5},{8,10},{9,11},{10,... | collective-permute-start | bytes 786440 | tf_op jit(solution)/shard_map/ppermute | solution.py:110
  137.6 1.8 convolution_convert_fusion.2
  139.4 1.0 fusion.34
  140.4 2.2 convolution_convert_fusion.1
  142.6 3.0 %collective-permute-start.24 = (bf16[64,2048]{1,0:T(8,128)(2,1)S(1)}, bf16[64,2048]{1,0:T(8,128)(2,1)S(1)}, u32[]{:S(2)}, u32[]{:S(2)}) collective-permute-start(bf16[64,2048]{1,0:T(8,128)(2,1)S(1)} %get-tuple-element.44), channel_id=1, source_target_pairs={{0,4},{1,5},{2,6},{3,7},{4,0},{5,1},{6,2},{7,3},{8,12},{9,13},{10,... | collective-permute-start | bytes 786440 | tf_op jit(solution)/shard_map/ppermute | solution.py:110
  145.6 2.2 collective-permute-start.25
  147.8 6.7 %collective-permute-done.23.refs_3_ = bf16[64,2048]{1,0:T(8,128)(2,1)S(1)} collective-permute-done((bf16[64,2048]{1,0:T(8,128)(2,1)S(1)}, bf16[64,2048]{1,0:T(8,128)(2,1)S(1)}, u32[]{:S(2)}, u32[]{:S(2)}) %collective-permute-start.23) | collective-permute-done | bytes 262176 | tf_op jit(solution)/shard_map/ppermute | solution.py:110
  154.5 1.5 collective-permute-start.26
  156.0 4.3 %collective-permute-start.27 = (bf16[64,2048]{1,0:T(8,128)(2,1)S(1)}, bf16[64,2048]{1,0:T(8,128)(2,1)S(1)}, u32[]{:S(2)}, u32[]{:S(2)}) collective-permute-start(bf16[64,2048]{1,0:T(8,128)(2,1)S(1)} %get-tuple-element.41), channel_id=1, source_target_pairs={{0,7},{1,6},{2,5},{3,4},{4,3},{5,2},{6,1},{7,0},{8,15},{9,14},{10,... | collective-permute-start | bytes 786440 | tf_op jit(solution)/shard_map/ppermute | solution.py:110
  160.3 2.2 fusion.6
  162.5 12.8 %collective-permute-done.24.refs_4_ = bf16[64,2048]{1,0:T(8,128)(2,1)S(1)} collective-permute-done((bf16[64,2048]{1,0:T(8,128)(2,1)S(1)}, bf16[64,2048]{1,0:T(8,128)(2,1)S(1)}, u32[]{:S(2)}, u32[]{:S(2)}) %collective-permute-start.24) | collective-permute-done | bytes 262176 | tf_op jit(solution)/shard_map/ppermute | solution.py:110
  175.3 6.6 %collective-permute-done.25.refs_5_ = bf16[64,2048]{1,0:T(8,128)(2,1)S(1)} collective-permute-done((bf16[64,2048]{1,0:T(8,128)(2,1)S(1)}, bf16[64,2048]{1,0:T(8,128)(2,1)S(1)}, u32[]{:S(2)}, u32[]{:S(2)}) %collective-permute-start.25) | collective-permute-done | bytes 262176 | tf_op jit(solution)/shard_map/ppermute | solution.py:110
  181.9 12.7 %collective-permute-start.11 = (bf16[64,2048]{1,0:T(8,128)(2,1)S(1)}, bf16[64,2048]{1,0:T(8,128)(2,1)S(1)}, u32[]{:S(2)}, u32[]{:S(2)}) collective-permute-start(bf16[64,2048]{1,0:T(8,128)(2,1)S(1)} %get-tuple-element.51), channel_id=1, source_target_pairs={{0,5},{1,4},{2,7},{3,6},{4,1},{5,0},{6,3},{7,2},{8,13},{9,12},{10,... | collective-permute-start | bytes 786440 | tf_op jit(solution)/shard_map/ppermute | solution.py:110
  194.6 1.5 collective-permute-start.30
  196.1 1.4 convolution_convert_fusion.4
  197.5 11.5 %collective-permute-done.10.refs_4_ = bf16[64,2048]{1,0:T(8,128)(2,1)S(1)} collective-permute-done((bf16[64,2048]{1,0:T(8,128)(2,1)S(1)}, bf16[64,2048]{1,0:T(8,128)(2,1)S(1)}, u32[]{:S(2)}, u32[]{:S(2)}) %collective-permute-start.10) | collective-permute-done | bytes 262176 | tf_op jit(solution)/shard_map/ppermute | solution.py:110
  209.7 2.4 collective-permute-start.12
  212.1 9.1 %collective-permute-done.11.refs_5_ = bf16[64,2048]{1,0:T(8,128)(2,1)S(1)} collective-permute-done((bf16[64,2048]{1,0:T(8,128)(2,1)S(1)}, bf16[64,2048]{1,0:T(8,128)(2,1)S(1)}, u32[]{:S(2)}, u32[]{:S(2)}) %collective-permute-start.11) | collective-permute-done | bytes 262176 | tf_op jit(solution)/shard_map/ppermute | solution.py:110
  221.9 2.4 collective-permute-start.13
  224.3 1.5 collective-permute-start.7
  225.7 1.4 fusion.16
  227.9 3.2 %collective-permute-done.13.refs_7_ = bf16[64,2048]{1,0:T(8,128)(2,1)S(1)} collective-permute-done((bf16[64,2048]{1,0:T(8,128)(2,1)S(1)}, bf16[64,2048]{1,0:T(8,128)(2,1)S(1)}, u32[]{:S(2)}, u32[]{:S(2)}) %collective-permute-start.13) | collective-permute-done | bytes 262176 | tf_op jit(solution)/shard_map/ppermute | solution.py:110
  231.8 1.5 collective-permute-start.33
  234.1 5.9 %collective-permute-start.8 = (bf16[64,2048]{1,0:T(8,128)(2,1)S(1)}, bf16[64,2048]{1,0:T(8,128)(2,1)S(1)}, u32[]{:S(2)}, u32[]{:S(2)}) collective-permute-start(bf16[64,2048]{1,0:T(8,128)(2,1)S(1)} %get-tuple-element.54), channel_id=1, source_target_pairs={{0,2},{1,3},{2,0},{3,1},{4,6},{5,7},{6,4},{7,5},{8,10},{9,11},{10,... | collective-permute-start | bytes 786440 | tf_op jit(solution)/shard_map/ppermute | solution.py:110
  240.0 4.8 %collective-permute-done.8.refs_2_ = bf16[64,2048]{1,0:T(8,128)(2,1)S(1)} collective-permute-done((bf16[64,2048]{1,0:T(8,128)(2,1)S(1)}, bf16[64,2048]{1,0:T(8,128)(2,1)S(1)}, u32[]{:S(2)}, u32[]{:S(2)}) %collective-permute-start.8) | collective-permute-done | bytes 262176 | tf_op jit(solution)/shard_map/ppermute | solution.py:110
  245.5 1.7 collective-permute-start.9
  247.2 1.2 copy-done.2
  255.1 2.6 combine.3
  257.8 3.9 %combine.2 = bf16[256,2048]{1,0:T(8,128)(2,1)} custom-call(bf16[256,512]{1,0:T(8,128)(2,1)S(1)} %get-tuple-element.21.place_ref.refs_0_, bf16[256,2048]{1,0:T(8,128)(2,1)S(1)} %copy-done.4, bf16[64,2048]{1,0:T(8,128)(2,1)S(1)} %copy-done.5, bf16[64,2048]{1,0:T(8,128)(2,1)S(1)} %copy-done.29, bf16[64,2048]{1,0:T(8,128)(2,1)S(1)} %copy-done.31, ...), custom_call_target="tpu_custom_call" | custom-call | flops 536870912 | bytes 3145728 | tf_op jit(solution)/shard_map/combine/pallas_call | solution.py:93
  261.7 3.3 %fusion.15 = f32[1,704,512]{2,1,0:T(8,128)} fusion(bf16[512,704]{1,0:T(8,128)(2,1)S(1)} %copy-done.45, bf16[704,512]{1,0:T(8,128)(2,1)} %collective-permute-done.33, bf16[704,512]{1,0:T(8,128)(2,1)} %collective-permute-done.31, bf16[512,2048]{1,0:T(8,128)(2,1)} %copy-done.47, s32[]{:T(128)S(6)} %select_n.16), kind=kOutput, calls=%fused_computation.24 | convolution fusion | flops 370540544 | bytes 4128772 | tf_op jit(solution)/shard_map/dot_general | solution.py:12
  265.0 4.7 %fusion.5 = f32[1,512,1408]{2,1,0:T(8,128)} fusion(bf16[512,1408]{1,0:T(8,128)(2,1)} %collective-permute-done.30, bf16[512,1408]{1,0:T(8,128)(2,1)} %collective-permute-done.28, bf16[512,2048]{1,0:T(8,128)(2,1)} %constant_dynamic-update-slice_fusion, s32[]{:T(128)S(6)} %select_n.16, bf16[512,704]{1,0:T(8,128)(2,1)S(1)} %copy-done.52, ...), kind=kOutput, calls=%fused_computation.7 | convolution fusion | flops 743964672 | bytes 7733252 | tf_op jit(solution)/shard_map/dot_general | solution.py:12
  (151 shorter events, 20.0 us)
Async XLA Ops:
  0.6 116.9 %copy-start = (bf16[1,704,2048]{2,1,0:T(8,128)(2,1)S(1)}, bf16[1,704,2048]{2,1,0:T(8,128)(2,1)}, u32[]{:S(2)}) copy-start(bf16[1,704,2048]{2,1,0:T(8,128)(2,1)} %param.8) | copy-start | bytes 8650756
  1.6 4.2 %copy-start.1 = (bf16[256,2048]{1,0:T(8,128)(2,1)S(1)}, bf16[256,2048]{1,0:T(8,128)(2,1)}, u32[]{:S(2)}) copy-start(bf16[256,2048]{1,0:T(8,128)(2,1)} %data_ref.3) | copy-start | bytes 3145732
  5.8 12.0 %copy-start.38 = (bf16[64,2048]{1,0:T(8,128)(2,1)}, bf16[64,2048]{1,0:T(8,128)(2,1)S(1)}, u32[]{:S(2)}) copy-start(bf16[64,2048]{1,0:T(8,128)(2,1)S(1)} %get-tuple-element.29) | copy-start | bytes 786436
  5.8 12.0 %copy-start.40 = (bf16[64,2048]{1,0:T(8,128)(2,1)}, bf16[64,2048]{1,0:T(8,128)(2,1)S(1)}, u32[]{:S(2)}) copy-start(bf16[64,2048]{1,0:T(8,128)(2,1)S(1)} %get-tuple-element.28) | copy-start | bytes 786436
  5.8 12.0 %copy-start.41 = (bf16[64,2048]{1,0:T(8,128)(2,1)}, bf16[64,2048]{1,0:T(8,128)(2,1)S(1)}, u32[]{:S(2)}) copy-start(bf16[64,2048]{1,0:T(8,128)(2,1)S(1)} %get-tuple-element.27) | copy-start | bytes 786436
  5.8 12.0 %copy-start.42 = (bf16[64,2048]{1,0:T(8,128)(2,1)}, bf16[64,2048]{1,0:T(8,128)(2,1)S(1)}, u32[]{:S(2)}) copy-start(bf16[64,2048]{1,0:T(8,128)(2,1)S(1)} %get-tuple-element.26) | copy-start | bytes 786436
  5.8 12.1 %copy-start.43 = (bf16[64,2048]{1,0:T(8,128)(2,1)}, bf16[64,2048]{1,0:T(8,128)(2,1)S(1)}, u32[]{:S(2)}) copy-start(bf16[64,2048]{1,0:T(8,128)(2,1)S(1)} %get-tuple-element.25) | copy-start | bytes 786436
  9.1 8.8 %copy-start.32 = (bf16[64,2048]{1,0:T(8,128)(2,1)}, bf16[64,2048]{1,0:T(8,128)(2,1)S(1)}, u32[]{:S(2)}) copy-start(bf16[64,2048]{1,0:T(8,128)(2,1)S(1)} %get-tuple-element.36) | copy-start | bytes 786436
  9.1 8.8 %copy-start.34 = (bf16[64,2048]{1,0:T(8,128)(2,1)}, bf16[64,2048]{1,0:T(8,128)(2,1)S(1)}, u32[]{:S(2)}) copy-start(bf16[64,2048]{1,0:T(8,128)(2,1)S(1)} %get-tuple-element.35) | copy-start | bytes 786436
  9.1 89.7 %collective-permute-start.14 = (bf16[64,2048]{1,0:T(8,128)(2,1)}, bf16[64,2048]{1,0:T(8,128)(2,1)}, u32[]{:S(2)}, u32[]{:S(2)}) collective-permute-start(bf16[64,2048]{1,0:T(8,128)(2,1)} %get-tuple-element.31), channel_id=1, source_target_pairs={{0,1},{1,0},{2,3},{3,2},{4,5},{5,4},{6,7},{7,6},{8,9},{9,8},{10,11... | collective-permute-start | bytes 786440 | tf_op jit(solution)/shard_map/ppermute | solution.py:110
  12.1 92.2 %collective-permute-start.15 = (bf16[64,2048]{1,0:T(8,128)(2,1)}, bf16[64,2048]{1,0:T(8,128)(2,1)}, u32[]{:S(2)}, u32[]{:S(2)}) collective-permute-start(bf16[64,2048]{1,0:T(8,128)(2,1)} %get-tuple-element.32), channel_id=1, source_target_pairs={{0,2},{1,3},{2,0},{3,1},{4,6},{5,7},{6,4},{7,5},{8,10},{9,11},{10,... | collective-permute-start | bytes 786440 | tf_op jit(solution)/shard_map/ppermute | solution.py:110
  13.7 92.2 %collective-permute-start.16 = (bf16[64,2048]{1,0:T(8,128)(2,1)}, bf16[64,2048]{1,0:T(8,128)(2,1)}, u32[]{:S(2)}, u32[]{:S(2)}) collective-permute-start(bf16[64,2048]{1,0:T(8,128)(2,1)} %get-tuple-element.33), channel_id=1, source_target_pairs={{0,3},{1,2},{2,1},{3,0},{4,7},{5,6},{6,5},{7,4},{8,11},{9,10},{10,... | collective-permute-start | bytes 786440 | tf_op jit(solution)/shard_map/ppermute | solution.py:110
  13.7 16.3 %collective-permute-start = (bf16[64,2048]{1,0:T(8,128)(2,1)}, bf16[64,2048]{1,0:T(8,128)(2,1)}, u32[]{:S(2)}, u32[]{:S(2)}) collective-permute-start(bf16[64,2048]{1,0:T(8,128)(2,1)} %get-tuple-element.23), channel_id=1, source_target_pairs={{0,1},{1,0},{2,3},{3,2},{4,5},{5,4},{6,7},{7,6},{8,9},{9,8},{10,11... | collective-permute-start | bytes 786440 | tf_op jit(solution)/shard_map/ppermute | solution.py:110
  15.6 18.8 %collective-permute-start.1 = (bf16[64,2048]{1,0:T(8,128)(2,1)}, bf16[64,2048]{1,0:T(8,128)(2,1)}, u32[]{:S(2)}, u32[]{:S(2)}) collective-permute-start(bf16[64,2048]{1,0:T(8,128)(2,1)} %get-tuple-element.24), channel_id=1, source_target_pairs={{0,2},{1,3},{2,0},{3,1},{4,6},{5,7},{6,4},{7,5},{8,10},{9,11},{10,... | collective-permute-start | bytes 786440 | tf_op jit(solution)/shard_map/ppermute | solution.py:110
  18.6 51.0 %copy-start.39 = (bf16[64,2048]{1,0:T(8,128)(2,1)S(1)}, bf16[64,2048]{1,0:T(8,128)(2,1)}, u32[]{:S(2)}) copy-start(bf16[64,2048]{1,0:T(8,128)(2,1)} %copy-done.38) | copy-start | bytes 786436
  18.6 54.9 %copy-start.37 = (bf16[64,2048]{1,0:T(8,128)(2,1)S(1)}, bf16[64,2048]{1,0:T(8,128)(2,1)}, u32[]{:S(2)}) copy-start(bf16[64,2048]{1,0:T(8,128)(2,1)} %copy-done.36) | copy-start | bytes 786436
  18.6 61.9 %copy-start.35 = (bf16[64,2048]{1,0:T(8,128)(2,1)S(1)}, bf16[64,2048]{1,0:T(8,128)(2,1)}, u32[]{:S(2)}) copy-start(bf16[64,2048]{1,0:T(8,128)(2,1)} %copy-done.34) | copy-start | bytes 786436
  29.9 12.1 %collective-permute-start.2 = (bf16[64,2048]{1,0:T(8,128)(2,1)}, bf16[64,2048]{1,0:T(8,128)(2,1)S(1)}, u32[]{:S(2)}, u32[]{:S(2)}) collective-permute-start(bf16[64,2048]{1,0:T(8,128)(2,1)} %copy-done.43), channel_id=1, source_target_pairs={{0,3},{1,2},{2,1},{3,0},{4,7},{5,6},{6,5},{7,4},{8,11},{9,10},{10,... | collective-permute-start | bytes 786440 | tf_op jit(solution)/shard_map/ppermute | solution.py:110
  34.4 21.3 %collective-permute-start.3 = (bf16[64,2048]{1,0:T(8,128)(2,1)}, bf16[64,2048]{1,0:T(8,128)(2,1)S(1)}, u32[]{:S(2)}, u32[]{:S(2)}) collective-permute-start(bf16[64,2048]{1,0:T(8,128)(2,1)} %copy-done.42), channel_id=1, source_target_pairs={{0,4},{1,5},{2,6},{3,7},{4,0},{5,1},{6,2},{7,3},{8,12},{9,13},{10,... | collective-permute-start | bytes 786440 | tf_op jit(solution)/shard_map/ppermute | solution.py:110
  42.0 27.7 %collective-permute-start.4 = (bf16[64,2048]{1,0:T(8,128)(2,1)}, bf16[64,2048]{1,0:T(8,128)(2,1)S(1)}, u32[]{:S(2)}, u32[]{:S(2)}) collective-permute-start(bf16[64,2048]{1,0:T(8,128)(2,1)} %copy-done.41), channel_id=1, source_target_pairs={{0,5},{1,4},{2,7},{3,6},{4,1},{5,0},{6,3},{7,2},{8,13},{9,12},{10,... | collective-permute-start | bytes 786440 | tf_op jit(solution)/shard_map/ppermute | solution.py:110
  55.7 17.9 %collective-permute-start.5 = (bf16[64,2048]{1,0:T(8,128)(2,1)}, bf16[64,2048]{1,0:T(8,128)(2,1)S(1)}, u32[]{:S(2)}, u32[]{:S(2)}) collective-permute-start(bf16[64,2048]{1,0:T(8,128)(2,1)} %copy-done.40), channel_id=1, source_target_pairs={{0,6},{1,7},{2,4},{3,5},{4,2},{5,3},{6,0},{7,1},{8,14},{9,15},{10,... | collective-permute-start | bytes 786440 | tf_op jit(solution)/shard_map/ppermute | solution.py:110
  69.7 10.9 %collective-permute-start.6 = (bf16[64,2048]{1,0:T(8,128)(2,1)S(1)}, bf16[64,2048]{1,0:T(8,128)(2,1)S(1)}, u32[]{:S(2)}, u32[]{:S(2)}) collective-permute-start(bf16[64,2048]{1,0:T(8,128)(2,1)S(1)} %copy-done.39), channel_id=1, source_target_pairs={{0,7},{1,6},{2,5},{3,4},{4,3},{5,2},{6,1},{7,0},{8,15},{9,14},{10,... | collective-permute-start | bytes 786440 | tf_op jit(solution)/shard_map/ppermute | solution.py:110
  73.5 38.3 %collective-permute-start.17 = (bf16[64,2048]{1,0:T(8,128)(2,1)S(1)}, bf16[64,2048]{1,0:T(8,128)(2,1)S(1)}, u32[]{:S(2)}, u32[]{:S(2)}) collective-permute-start(bf16[64,2048]{1,0:T(8,128)(2,1)S(1)} %copy-done.37), channel_id=1, source_target_pairs={{0,4},{1,5},{2,6},{3,7},{4,0},{5,1},{6,2},{7,3},{8,12},{9,13},{10,... | collective-permute-start | bytes 786440 | tf_op jit(solution)/shard_map/ppermute | solution.py:110
  80.6 36.8 %collective-permute-start.18 = (bf16[64,2048]{1,0:T(8,128)(2,1)S(1)}, bf16[64,2048]{1,0:T(8,128)(2,1)S(1)}, u32[]{:S(2)}, u32[]{:S(2)}) collective-permute-start(bf16[64,2048]{1,0:T(8,128)(2,1)S(1)} %copy-done.35), channel_id=1, source_target_pairs={{0,5},{1,4},{2,7},{3,6},{4,1},{5,0},{6,3},{7,2},{8,13},{9,12},{10,... | collective-permute-start | bytes 786440 | tf_op jit(solution)/shard_map/ppermute | solution.py:110
  92.3 6.5 %copy-start.33 = (bf16[64,2048]{1,0:T(8,128)(2,1)S(1)}, bf16[64,2048]{1,0:T(8,128)(2,1)}, u32[]{:S(2)}) copy-start(bf16[64,2048]{1,0:T(8,128)(2,1)} %copy-done.32) | copy-start | bytes 786436
  92.3 11.1 %copy-start.46 = (bf16[512,2048]{1,0:T(8,128)(2,1)S(1)}, bf16[512,2048]{1,0:T(8,128)(2,1)}, u32[]{:S(2)}) copy-start(bf16[512,2048]{1,0:T(8,128)(2,1)} %constant_dynamic-update-slice_fusion.15) | copy-start | bytes 6291460
  98.8 18.6 %collective-permute-start.19 = (bf16[64,2048]{1,0:T(8,128)(2,1)S(1)}, bf16[64,2048]{1,0:T(8,128)(2,1)S(1)}, u32[]{:S(2)}, u32[]{:S(2)}) collective-permute-start(bf16[64,2048]{1,0:T(8,128)(2,1)S(1)} %copy-done.33), channel_id=1, source_target_pairs={{0,6},{1,7},{2,4},{3,5},{4,2},{5,3},{6,0},{7,1},{8,14},{9,15},{10,... | collective-permute-start | bytes 786440 | tf_op jit(solution)/shard_map/ppermute | solution.py:110
  104.3 13.1 %collective-permute-start.20 = (bf16[64,2048]{1,0:T(8,128)(2,1)S(1)}, bf16[64,2048]{1,0:T(8,128)(2,1)S(1)}, u32[]{:S(2)}, u32[]{:S(2)}) collective-permute-start(bf16[64,2048]{1,0:T(8,128)(2,1)S(1)} %get-tuple-element.37), channel_id=1, source_target_pairs={{0,7},{1,6},{2,5},{3,4},{4,3},{5,2},{6,1},{7,0},{8,15},{9,14},{10,... | collective-permute-start | bytes 786440 | tf_op jit(solution)/shard_map/ppermute | solution.py:110
  117.5 108.2 %copy-start.47 = (bf16[512,2048]{1,0:T(8,128)(2,1)}, bf16[512,2048]{1,0:T(8,128)(2,1)S(1)}, u32[]{:S(2)}) copy-start(bf16[512,2048]{1,0:T(8,128)(2,1)S(1)} %constant_dynamic-update-slice_fusion.8) | copy-start | bytes 6291460
  117.5 3.4 %slice-start.1 = ((s8[5767168]{0:T(1024)(128)(4,1)}), s8[1572864]{0:T(1024)(128)(4,1)S(1)}, s32[]{:S(2)}) async-start(s8[5767168]{0:T(1024)(128)(4,1)} %bitcast.25), calls=%async_computation.1 | async-start | bytes 3145728
  119.9 40.4 %copy-start.49 = (bf16[512,704]{1,0:T(8,128)(2,1)}, bf16[512,704]{1,0:T(8,128)(2,1)S(1)}, u32[]{:S(2)}) copy-start(bf16[512,704]{1,0:T(8,128)(2,1)S(1)} %get-tuple-element.38) | copy-start | bytes 2162692
  119.9 40.4 %copy-start.51 = (bf16[512,704]{1,0:T(8,128)(2,1)}, bf16[512,704]{1,0:T(8,128)(2,1)S(1)}, u32[]{:S(2)}) copy-start(bf16[512,704]{1,0:T(8,128)(2,1)S(1)} %get-tuple-element.39) | copy-start | bytes 2162692
  119.9 105.8 %copy-start.44 = (bf16[512,704]{1,0:T(8,128)(2,1)}, bf16[512,704]{1,0:T(8,128)(2,1)S(1)}, u32[]{:S(2)}) copy-start(bf16[512,704]{1,0:T(8,128)(2,1)S(1)} %get-tuple-element.40) | copy-start | bytes 2162692
  120.9 3.9 %copy-start.48 = (bf16[512,2048]{1,0:T(8,128)(2,1)S(1)}, bf16[512,2048]{1,0:T(8,128)(2,1)}, u32[]{:S(2)}) copy-start(bf16[512,2048]{1,0:T(8,128)(2,1)} %constant_dynamic-update-slice_fusion) | copy-start | bytes 6291460
  126.5 97.8 %collective-permute-start.32 = (bf16[704,512]{1,0:T(8,128)(2,1)S(1)}, bf16[704,512]{1,0:T(8,128)(2,1)S(1)}, u32[]{:S(2)}, u32[]{:S(2)}) collective-permute-start(bf16[704,512]{1,0:T(8,128)(2,1)S(1)} %convolution_convert_fusion.3), channel_id=1, source_target_pairs={{0,8},{8,0},{16,24},{24,16},{1,9},{9,1},{17,25},{25,17},{2,10},{10... | collective-permute-start | bytes 2162696 | tf_op jit(solution)/shard_map/ppermute | solution.py:120
  126.6 29.4 %collective-permute-start.29 = (bf16[512,1408]{1,0:T(8,128)(2,1)S(1)}, bf16[512,1408]{1,0:T(8,128)(2,1)S(1)}, u32[]{:S(2)}, u32[]{:S(2)}) collective-permute-start(bf16[512,1408]{1,0:T(8,128)(2,1)S(1)} %convolution_convert_fusion), channel_id=1, source_target_pairs={{0,8},{8,0},{16,24},{24,16},{1,9},{9,1},{17,25},{25,17},{2,10},{10... | collective-permute-start | bytes 4325384 | tf_op jit(solution)/shard_map/ppermute | solution.py:120
  127.3 15.3 %collective-permute-start.21 = (bf16[64,2048]{1,0:T(8,128)(2,1)S(1)}, bf16[64,2048]{1,0:T(8,128)(2,1)S(1)}, u32[]{:S(2)}, u32[]{:S(2)}) collective-permute-start(bf16[64,2048]{1,0:T(8,128)(2,1)S(1)} %get-tuple-element.47), channel_id=1, source_target_pairs={{0,1},{1,0},{2,3},{3,2},{4,5},{5,4},{6,7},{7,6},{8,9},{9,8},{10,11... | collective-permute-start | bytes 786440 | tf_op jit(solution)/shard_map/ppermute | solution.py:110
  128.9 16.7 %collective-permute-start.22 = (bf16[64,2048]{1,0:T(8,128)(2,1)S(1)}, bf16[64,2048]{1,0:T(8,128)(2,1)S(1)}, u32[]{:S(2)}, u32[]{:S(2)}) collective-permute-start(bf16[64,2048]{1,0:T(8,128)(2,1)S(1)} %get-tuple-element.46), channel_id=1, source_target_pairs={{0,2},{1,3},{2,0},{3,1},{4,6},{5,7},{6,4},{7,5},{8,10},{9,11},{10,... | collective-permute-start | bytes 786440 | tf_op jit(solution)/shard_map/ppermute | solution.py:110
  137.6 16.9 %collective-permute-start.23 = (bf16[64,2048]{1,0:T(8,128)(2,1)S(1)}, bf16[64,2048]{1,0:T(8,128)(2,1)S(1)}, u32[]{:S(2)}, u32[]{:S(2)}) collective-permute-start(bf16[64,2048]{1,0:T(8,128)(2,1)S(1)} %get-tuple-element.45), channel_id=1, source_target_pairs={{0,3},{1,2},{2,1},{3,0},{4,7},{5,6},{6,5},{7,4},{8,11},{9,10},{10,... | collective-permute-start | bytes 786440 | tf_op jit(solution)/shard_map/ppermute | solution.py:110
  142.6 19.9 %copy-start.6 = (bf16[64,2048]{1,0:T(8,128)(2,1)}, bf16[64,2048]{1,0:T(8,128)(2,1)S(1)}, u32[]{:S(2)}) copy-start(bf16[64,2048]{1,0:T(8,128)(2,1)S(1)} %collective-permute-done.21.refs_1_) | copy-start | bytes 786436
  142.6 32.7 %collective-permute-start.24 = (bf16[64,2048]{1,0:T(8,128)(2,1)S(1)}, bf16[64,2048]{1,0:T(8,128)(2,1)S(1)}, u32[]{:S(2)}, u32[]{:S(2)}) collective-permute-start(bf16[64,2048]{1,0:T(8,128)(2,1)S(1)} %get-tuple-element.44), channel_id=1, source_target_pairs={{0,4},{1,5},{2,6},{3,7},{4,0},{5,1},{6,2},{7,3},{8,12},{9,13},{10,... | collective-permute-start | bytes 786440 | tf_op jit(solution)/shard_map/ppermute | solution.py:110
  145.6 16.9 %copy-start.8 = (bf16[64,2048]{1,0:T(8,128)(2,1)}, bf16[64,2048]{1,0:T(8,128)(2,1)S(1)}, u32[]{:S(2)}) copy-start(bf16[64,2048]{1,0:T(8,128)(2,1)S(1)} %collective-permute-done.22.refs_2_) | copy-start | bytes 786436
  145.6 36.3 %collective-permute-start.25 = (bf16[64,2048]{1,0:T(8,128)(2,1)S(1)}, bf16[64,2048]{1,0:T(8,128)(2,1)S(1)}, u32[]{:S(2)}, u32[]{:S(2)}) collective-permute-start(bf16[64,2048]{1,0:T(8,128)(2,1)S(1)} %get-tuple-element.43), channel_id=1, source_target_pairs={{0,5},{1,4},{2,7},{3,6},{4,1},{5,0},{6,3},{7,2},{8,13},{9,12},{10,... | collective-permute-start | bytes 786440 | tf_op jit(solution)/shard_map/ppermute | solution.py:110
  154.5 8.0 %copy-start.10 = (bf16[64,2048]{1,0:T(8,128)(2,1)}, bf16[64,2048]{1,0:T(8,128)(2,1)S(1)}, u32[]{:S(2)}) copy-start(bf16[64,2048]{1,0:T(8,128)(2,1)S(1)} %collective-permute-done.23.refs_3_) | copy-start | bytes 786436
  154.5 27.4 %collective-permute-start.26 = (bf16[64,2048]{1,0:T(8,128)(2,1)S(1)}, bf16[64,2048]{1,0:T(8,128)(2,1)S(1)}, u32[]{:S(2)}, u32[]{:S(2)}) collective-permute-start(bf16[64,2048]{1,0:T(8,128)(2,1)S(1)} %get-tuple-element.42), channel_id=1, source_target_pairs={{0,6},{1,7},{2,4},{3,5},{4,2},{5,3},{6,0},{7,1},{8,14},{9,15},{10,... | collective-permute-start | bytes 786440 | tf_op jit(solution)/shard_map/ppermute | solution.py:110
  156.0 38.6 %collective-permute-start.27 = (bf16[64,2048]{1,0:T(8,128)(2,1)S(1)}, bf16[64,2048]{1,0:T(8,128)(2,1)S(1)}, u32[]{:S(2)}, u32[]{:S(2)}) collective-permute-start(bf16[64,2048]{1,0:T(8,128)(2,1)S(1)} %get-tuple-element.41), channel_id=1, source_target_pairs={{0,7},{1,6},{2,5},{3,4},{4,3},{5,2},{6,1},{7,0},{8,15},{9,14},{10,... | collective-permute-start | bytes 786440 | tf_op jit(solution)/shard_map/ppermute | solution.py:110
  175.3 51.9 %copy-start.12 = (bf16[64,2048]{1,0:T(8,128)(2,1)}, bf16[64,2048]{1,0:T(8,128)(2,1)S(1)}, u32[]{:S(2)}) copy-start(bf16[64,2048]{1,0:T(8,128)(2,1)S(1)} %collective-permute-done.24.refs_4_) | copy-start | bytes 786436
  175.3 89.7 %collective-permute-start.28 = (bf16[512,1408]{1,0:T(8,128)(2,1)}, bf16[512,1408]{1,0:T(8,128)(2,1)}, u32[]{:S(2)}, u32[]{:S(2)}) collective-permute-start(bf16[512,1408]{1,0:T(8,128)(2,1)} %convolution_convert_fusion.1), channel_id=1, source_target_pairs={{0,8},{8,0},{16,24},{24,16},{1,9},{9,1},{17,25},{25,17},{2,10},{10... | collective-permute-start | bytes 4325384 | tf_op jit(solution)/shard_map/ppermute | solution.py:120
  181.9 45.3 %copy-start.14 = (bf16[64,2048]{1,0:T(8,128)(2,1)}, bf16[64,2048]{1,0:T(8,128)(2,1)S(1)}, u32[]{:S(2)}) copy-start(bf16[64,2048]{1,0:T(8,128)(2,1)S(1)} %collective-permute-done.25.refs_5_) | copy-start | bytes 786436
  181.9 27.1 %collective-permute-start.10 = (bf16[64,2048]{1,0:T(8,128)(2,1)S(1)}, bf16[64,2048]{1,0:T(8,128)(2,1)S(1)}, u32[]{:S(2)}, u32[]{:S(2)}) collective-permute-start(bf16[64,2048]{1,0:T(8,128)(2,1)S(1)} %get-tuple-element.52), channel_id=1, source_target_pairs={{0,4},{1,5},{2,6},{3,7},{4,0},{5,1},{6,2},{7,3},{8,12},{9,13},{10,... | collective-permute-start | bytes 786440 | tf_op jit(solution)/shard_map/ppermute | solution.py:110
  181.9 45.3 %copy-start.16 = (bf16[64,2048]{1,0:T(8,128)(2,1)}, bf16[64,2048]{1,0:T(8,128)(2,1)S(1)}, u32[]{:S(2)}) copy-start(bf16[64,2048]{1,0:T(8,128)(2,1)S(1)} %collective-permute-done.26.refs_6_) | copy-start | bytes 786436
  181.9 39.3 %collective-permute-start.11 = (bf16[64,2048]{1,0:T(8,128)(2,1)S(1)}, bf16[64,2048]{1,0:T(8,128)(2,1)S(1)}, u32[]{:S(2)}, u32[]{:S(2)}) collective-permute-start(bf16[64,2048]{1,0:T(8,128)(2,1)S(1)} %get-tuple-element.51), channel_id=1, source_target_pairs={{0,5},{1,4},{2,7},{3,6},{4,1},{5,0},{6,3},{7,2},{8,13},{9,12},{10,... | collective-permute-start | bytes 786440 | tf_op jit(solution)/shard_map/ppermute | solution.py:110
  194.6 32.6 %copy-start.18 = (bf16[64,2048]{1,0:T(8,128)(2,1)}, bf16[64,2048]{1,0:T(8,128)(2,1)S(1)}, u32[]{:S(2)}) copy-start(bf16[64,2048]{1,0:T(8,128)(2,1)S(1)} %collective-permute-done.27.refs_7_) | copy-start | bytes 786436
  194.6 70.4 %collective-permute-start.30 = (bf16[512,1408]{1,0:T(8,128)(2,1)}, bf16[512,1408]{1,0:T(8,128)(2,1)}, u32[]{:S(2)}, u32[]{:S(2)}) collective-permute-start(bf16[512,1408]{1,0:T(8,128)(2,1)} %fusion.6), channel_id=1, source_target_pairs={{0,16},{8,24},{16,0},{24,8},{1,17},{9,25},{17,1},{25,9},{2,18},{10... | collective-permute-start | bytes 4325384 | tf_op jit(solution)/shard_map/ppermute | solution.py:120
  209.7 17.5 %collective-permute-start.12 = (bf16[64,2048]{1,0:T(8,128)(2,1)S(1)}, bf16[64,2048]{1,0:T(8,128)(2,1)S(1)}, u32[]{:S(2)}, u32[]{:S(2)}) collective-permute-start(bf16[64,2048]{1,0:T(8,128)(2,1)S(1)} %get-tuple-element.50), channel_id=1, source_target_pairs={{0,6},{1,7},{2,4},{3,5},{4,2},{5,3},{6,0},{7,1},{8,14},{9,15},{10,... | collective-permute-start | bytes 786440 | tf_op jit(solution)/shard_map/ppermute | solution.py:110
  221.9 9.2 %collective-permute-start.13 = (bf16[64,2048]{1,0:T(8,128)(2,1)S(1)}, bf16[64,2048]{1,0:T(8,128)(2,1)S(1)}, u32[]{:S(2)}, u32[]{:S(2)}) collective-permute-start(bf16[64,2048]{1,0:T(8,128)(2,1)S(1)} %get-tuple-element.49), channel_id=1, source_target_pairs={{0,7},{1,6},{2,5},{3,4},{4,3},{5,2},{6,1},{7,0},{8,15},{9,14},{10,... | collective-permute-start | bytes 786440 | tf_op jit(solution)/shard_map/ppermute | solution.py:110
  224.3 9.2 %collective-permute-start.7 = (bf16[64,2048]{1,0:T(8,128)(2,1)S(1)}, bf16[64,2048]{1,0:T(8,128)(2,1)S(1)}, u32[]{:S(2)}, u32[]{:S(2)}) collective-permute-start(bf16[64,2048]{1,0:T(8,128)(2,1)S(1)} %get-tuple-element.55), channel_id=1, source_target_pairs={{0,1},{1,0},{2,3},{3,2},{4,5},{5,4},{6,7},{7,6},{8,9},{9,8},{10,11... | collective-permute-start | bytes 786440 | tf_op jit(solution)/shard_map/ppermute | solution.py:110
  227.9 33.8 %collective-permute-start.31 = (bf16[704,512]{1,0:T(8,128)(2,1)}, bf16[704,512]{1,0:T(8,128)(2,1)}, u32[]{:S(2)}, u32[]{:S(2)}) collective-permute-start(bf16[704,512]{1,0:T(8,128)(2,1)} %convolution_convert_fusion.4), channel_id=1, source_target_pairs={{0,8},{8,0},{16,24},{24,16},{1,9},{9,1},{17,25},{25,17},{2,10},{10... | collective-permute-start | bytes 2162696 | tf_op jit(solution)/shard_map/ppermute | solution.py:120
  231.8 29.8 %collective-permute-start.33 = (bf16[704,512]{1,0:T(8,128)(2,1)}, bf16[704,512]{1,0:T(8,128)(2,1)}, u32[]{:S(2)}, u32[]{:S(2)}) collective-permute-start(bf16[704,512]{1,0:T(8,128)(2,1)} %fusion.16), channel_id=1, source_target_pairs={{0,16},{8,24},{16,0},{24,8},{1,17},{9,25},{17,1},{25,9},{2,18},{10... | collective-permute-start | bytes 2162696 | tf_op jit(solution)/shard_map/ppermute | solution.py:120
  234.1 10.7 %collective-permute-start.8 = (bf16[64,2048]{1,0:T(8,128)(2,1)S(1)}, bf16[64,2048]{1,0:T(8,128)(2,1)S(1)}, u32[]{:S(2)}, u32[]{:S(2)}) collective-permute-start(bf16[64,2048]{1,0:T(8,128)(2,1)S(1)} %get-tuple-element.54), channel_id=1, source_target_pairs={{0,2},{1,3},{2,0},{3,1},{4,6},{5,7},{6,4},{7,5},{8,10},{9,11},{10,... | collective-permute-start | bytes 786440 | tf_op jit(solution)/shard_map/ppermute | solution.py:110
  245.5 12.2 %collective-permute-start.9 = (bf16[64,2048]{1,0:T(8,128)(2,1)}, bf16[64,2048]{1,0:T(8,128)(2,1)}, u32[]{:S(2)}, u32[]{:S(2)}) collective-permute-start(bf16[64,2048]{1,0:T(8,128)(2,1)} %get-tuple-element.53), channel_id=1, source_target_pairs={{0,3},{1,2},{2,1},{3,0},{4,7},{5,6},{6,5},{7,4},{8,11},{9,10},{10,... | collective-permute-start | bytes 786440 | tf_op jit(solution)/shard_map/ppermute | solution.py:110
  257.8 3.9 %copy-start.45 = (bf16[512,704]{1,0:T(8,128)(2,1)S(1)}, bf16[512,704]{1,0:T(8,128)(2,1)}, u32[]{:S(2)}) copy-start(bf16[512,704]{1,0:T(8,128)(2,1)} %copy-done.44) | copy-start | bytes 2162692
  261.7 3.3 %copy-start.50 = (bf16[512,704]{1,0:T(8,128)(2,1)S(1)}, bf16[512,704]{1,0:T(8,128)(2,1)}, u32[]{:S(2)}) copy-start(bf16[512,704]{1,0:T(8,128)(2,1)} %copy-done.49) | copy-start | bytes 2162692
  261.7 3.3 %copy-start.52 = (bf16[512,704]{1,0:T(8,128)(2,1)S(1)}, bf16[512,704]{1,0:T(8,128)(2,1)}, u32[]{:S(2)}) copy-start(bf16[512,704]{1,0:T(8,128)(2,1)} %copy-done.51) | copy-start | bytes 2162692
  (25 other events, 38.1 us)

commit v2 on v1

v2 whole, which is shorter than its diff:
```python
import jax
import jax.numpy as jnp
from jax import lax
from jax.experimental import pallas as pl
from jax.experimental.pallas import tpu as pltpu
from jax.sharding import PartitionSpec as P

VMEM_BYTES = 48 * 1024 * 1024
SMALL = pl.CostEstimate(flops=1024, bytes_accessed=1024, transcendentals=0)
ROWS = 256


def dot(left, right, dims):
    return lax.dot_general(left, right, (dims, ((), ())), preferred_element_type=jnp.float32)


def params(grid=True):
    return pltpu.CompilerParams(
        vmem_limit_bytes=VMEM_BYTES, dimension_semantics=("arbitrary",) if grid else None
    )


def like(shape, dtype=jnp.bfloat16):
    return jax.ShapeDtypeStruct(shape, dtype)


def route_kernel(experts, cap, rel_ref, data_ref, place_ref, *block_refs):
    rows = rel_ref.shape[0]
    slots = experts * cap

    @pl.when(pl.program_id(0) == 0)
    def _():
        rel = rel_ref[...]
        onehot = lax.broadcasted_iota(jnp.int32, (rows, 128), 1) == rel
        before = lax.broadcasted_iota(jnp.int32, (rows, rows), 1) < lax.broadcasted_iota(jnp.int32, (rows, rows), 0)
        ranks = dot(before.astype(jnp.bfloat16), onehot.astype(jnp.bfloat16), ((1,), (0,)))
        rank = jnp.sum(jnp.where(onehot, ranks, 0.0), axis=1, keepdims=True).astype(jnp.int32)
        target = rel * cap + rank
        place_ref[...] = (lax.broadcasted_iota(jnp.int32, (rows, slots), 1) == target).astype(jnp.bfloat16)

    place_kernel(experts, cap, place_ref, data_ref, *block_refs)


def place_kernel(experts, cap, place_ref, data_ref, *block_refs):
    moved = dot(place_ref[...], data_ref[...], ((0,), (0,))).astype(jnp.bfloat16)
    for index in range(experts):
        block_refs[index][...] = moved[index * cap : (index + 1) * cap]


def combine_kernel(place_ref, data_ref, *refs):
    back = jnp.concatenate([ref[...] for ref in refs[:-1]], axis=0)
    total = data_ref[...].astype(jnp.float32) + dot(place_ref[...], back, ((1,), (0,)))
    refs[-1][...] = total.astype(jnp.bfloat16)


def join_rows(block_refs, out_ref):
    cap = block_refs[0].shape[0]
    for index, block_ref in enumerate(block_refs):
        out_ref[index * cap : (index + 1) * cap] = block_ref[...]


def split_rows(left_ref, right_ref, dims, outs):
    cap = outs[0].shape[0]
    each = max(1, ROWS // cap)
    for first in range(0, len(outs), each):
        result = dot(left_ref[first * cap : (first + each) * cap], right_ref[...], dims).astype(jnp.bfloat16)
        for index in range(each):
            outs[first + index][...] = result[index * cap : (index + 1) * cap]


def forward_kernel(*refs):
    count = (len(refs) - 6) // 2
    one_ref, two_ref, slot_ref, hidden_ref, upper_ref, silu_ref = refs[count : count + 6]
    wide = two_ref.shape[0]
    join_rows(refs[:count], slot_ref)

    @pl.loop(0, slot_ref.shape[0] // ROWS)
    def _(step):
        here = pl.ds(pl.multiple_of(step * ROWS, ROWS), ROWS)
        proj = dot(slot_ref[here], one_ref[...], ((1,), (0,)))
        gate = proj[:, :wide]
        upper = proj[:, wide:]
        sigma = 1.0 / (1.0 + jnp.exp(-gate))
        silu = gate * sigma
        hidden_ref[here] = (silu * upper).astype(jnp.bfloat16)
        upper_ref[here] = upper * sigma * (1.0 + gate * (1.0 - sigma))
        silu_ref[here] = silu

    split_rows(hidden_ref, two_ref, ((1,), (0,)), refs[count + 6 :])


def grad_proj_kernel(*refs):
    two_ref, upper_ref, silu_ref, slot_ref, out_ref = refs[-5:]
    join_rows(refs[:-5], slot_ref)

    @pl.loop(0, slot_ref.shape[0] // ROWS)
    def _(step):
        here = pl.ds(pl.multiple_of(step * ROWS, ROWS), ROWS)
        grad_hidden = dot(slot_ref[here], two_ref[...], ((1,), (1,)))
        both = jnp.concatenate([grad_hidden * upper_ref[here], grad_hidden * silu_ref[here]], axis=1)
        out_ref[here] = both.astype(jnp.bfloat16)


def grad_branch_kernel(grad_ref, one_ref, *outs):
    split_rows(grad_ref, one_ref, ((1,), (1,)), outs)


def weight_kernel(number_ref, x_ref, dy_ref, grad_ref, hidden_ref, *refs):
    up_ref, down_ref = refs[-2:]
    up = dot(x_ref[...], grad_ref[...], ((0,), (0,)))
    down = dot(hidden_ref[...], dy_ref[...], ((0,), (0,)))
    for index in range(0, len(refs) - 2, 2):
        up = up + refs[index][...].astype(jnp.float32)
        down = down + refs[index + 1][...].astype(jnp.float32)
    up_ref[...] = up.astype(up_ref.dtype)
    down_ref[...] = down.astype(down_ref.dtype)


def route_and_place(rel, data, experts, cap):
    rows, width = data.shape
    slots = experts * cap
    step = width // 4
    return pl.pallas_call(
        lambda *refs: route_kernel(experts, cap, *refs),
        grid=(width // step,),
        in_specs=[pl.BlockSpec((rows, 1), lambda i: (0, 0)), pl.BlockSpec((rows, step), lambda i: (0, i))],
        out_specs=[pl.BlockSpec((rows, slots), lambda i: (0, 0))]
        + [pl.BlockSpec((cap, step), lambda i: (0, i))] * experts,
        out_shape=[like((rows, slots))] + [like((cap, width))] * experts,
        compiler_params=params(),
        cost_estimate=SMALL,
        name="route_and_place",
    )(rel, data)


def place(placing, data, experts, cap):
    rows, width = data.shape
    slots = experts * cap
    step = width // 4
    return pl.pallas_call(
        lambda *refs: place_kernel(experts, cap, *refs),
        grid=(width // step,),
        in_specs=[pl.BlockSpec((rows, slots), lambda i: (0, 0)), pl.BlockSpec((rows, step), lambda i: (0, i))],
        out_specs=[pl.BlockSpec((cap, step), lambda i: (0, i))] * experts,
        out_shape=[like((cap, width))] * experts,
        compiler_params=params(),
        cost_estimate=SMALL,
        name="place",
    )(placing, data)


def combine(placing, data, blocks):
    rows, width = data.shape
    cap = blocks[0].shape[0]
    slots = placing.shape[1]
    step = width // 4
    return pl.pallas_call(
        combine_kernel,
        grid=(width // step,),
        in_specs=[pl.BlockSpec((rows, slots), lambda i: (0, 0)), pl.BlockSpec((rows, step), lambda i: (0, i))]
        + [pl.BlockSpec((cap, step), lambda i: (0, i))] * len(blocks),
        out_specs=pl.BlockSpec((rows, step), lambda i: (0, i)),
        out_shape=like((rows, width)),
        compiler_params=params(),
        cost_estimate=SMALL,
        name="combine",
    )(placing, data, *blocks)


def forward(blocks, weight_one, weight_two):
    slots = len(blocks) * blocks[0].shape[0]
    wide, width = weight_two.shape
    return pl.pallas_call(
        forward_kernel,
        out_shape=[
            like((slots, width)),
            like((slots, wide)),
            like((slots, wide), jnp.float32),
            like((slots, wide), jnp.float32),
        ]
        + [like(blocks[0].shape)] * len(blocks),
        compiler_params=params(False),
        cost_estimate=SMALL,
        name="forward",
    )(*blocks, weight_one, weight_two)


def grad_of_proj(blocks, weight_two, upper, silu):
    slots = len(blocks) * blocks[0].shape[0]
    wide, width = weight_two.shape
    return pl.pallas_call(
        grad_proj_kernel,
        out_shape=[like((slots, width)), like((slots, 2 * wide))],
        compiler_params=params(False),
        cost_estimate=SMALL,
        name="grad_proj",
    )(*blocks, weight_two, upper, silu)


def grad_of_branch(grad_proj, weight_one, experts, cap):
    return pl.pallas_call(
        grad_branch_kernel,
        out_shape=[like((cap, weight_one.shape[0]))] * experts,
        compiler_params=params(False),
        cost_estimate=SMALL,
        name="grad_branch",
    )(grad_proj, weight_one)


def weight_part(number, groups, slot_x, slot_dy, grad_proj, hidden, received, dtype):
    slots, width = slot_x.shape
    share = width // groups
    wide = hidden.shape[1]
    outs = [like((share, 2 * wide), dtype), like((wide, share), dtype)]

    def whole(array):
        return pl.BlockSpec(array.shape, lambda i, number_ref: (0, 0))

    column = pl.BlockSpec((slots, share), lambda i, number_ref: (0, number_ref[0]))
    return pl.pallas_call(
        weight_kernel,
        grid_spec=pltpu.PrefetchScalarGridSpec(
            num_scalar_prefetch=1,
            grid=(1,),
            in_specs=[column, column, whole(grad_proj), whole(hidden)] + [whole(piece) for piece in received],
            out_specs=[whole(out) for out in outs],
        ),
        out_shape=outs,
        compiler_params=params(),
        cost_estimate=SMALL,
        name="weight_part",
    )(number, slot_x, slot_dy, grad_proj, hidden, *received)


def after(value, *earlier):
    return lax.optimization_barrier((value, *earlier))[0]


class Lane:
    def __init__(self, window):
        self.window = window
        self.done = []

    def send(self, value, axis, pairs, *earlier):
        if len(self.done) >= self.window:
            earlier = (self.done[-self.window], *earlier)
        if earlier:
            value = after(value, *earlier)
        self.done.append(lax.ppermute(value, axis, pairs))
        return self.done[-1]


def exchange(blocks, far, held={}):
    experts = len(blocks)
    half = experts // 2
    moved = {0: blocks[0]}
    for mask in range(half - 1, -1, -1):
        pairs = [(i, i ^ (mask + half)) for i in range(experts)]
        moved[mask + half] = far.send(blocks[mask + half], "exp", pairs, *held.get(mask, ()))
        if mask:
            pairs = [(i, i ^ mask) for i in range(experts)]
            moved[mask] = lax.ppermute(after(blocks[mask], far.done[-1]), "exp", pairs)
    return [moved[mask] for mask in range(experts)]


def body(tokens, expert_ids, gate_up_weight, down_weight, grad_out):
    rows, width = tokens.shape
    experts = lax.axis_size("exp")
    groups = lax.axis_size("grp")
    cap = 2 * rows // experts
    weight_one = gate_up_weight[0]
    weight_two = down_weight[0]
    far = Lane(2)
    rel = expert_ids ^ lax.axis_index("exp").astype(jnp.int32)
    group = lax.axis_index("grp").astype(jnp.int32)

    placing, *sent_x = route_and_place(rel, tokens, experts, cap)
    sent_dy = place(placing, grad_out, experts, cap)
    blocks_x = exchange(sent_x, far)
    slot_x, hidden, upper, silu, *branch = forward(blocks_x, weight_one, weight_two)

    blocks_dy = exchange(sent_dy, far, {1: (hidden,)})
    slot_dy, grad_proj = grad_of_proj(blocks_dy, weight_two, upper, silu)
    grad_branch = grad_of_branch(grad_proj, weight_one, experts, cap)

    count = len(far.done)
    lanes = {}
    made = {}

    def weight_sum(q, bit):
        received = []
        low = bit // 2
        while low:
            pairs = [(i, i ^ low) for i in range(groups)]
            lane = lanes.setdefault(low, Lane(1))
            received += [lane.send(piece, "grp", pairs) for piece in weight_sum(q | low, low)]
            low //= 2
        dtype = jnp.float32 if bit == groups else jnp.bfloat16
        grad = grad_proj if made else after(grad_proj, first_out)
        made[q] = weight_part((group ^ q)[None], groups, slot_x, slot_dy, grad, hidden, received, dtype)
        return made[q]

    back_out = exchange(branch, far, {1: (grad_proj,), 0: (grad_branch[0],)})
    first_out = far.done[count]
    mixed_out = combine(placing, tokens, back_out)
    grad_gate_up, grad_down = weight_sum(0, groups)
    back_grad = exchange(grad_branch, far, {0: (mixed_out,)})
    back_grad[0] = after(back_grad[0], grad_gate_up)
    grad_tokens = combine(placing, grad_out, back_grad)
    return (mixed_out, grad_tokens, grad_gate_up[None], grad_down[None])


def solution(mesh):
    in_specs = (
        P(("grp", "exp"), None),
        P(("grp", "exp"), None),
        P("exp", None, None),
        P("exp", None, None),
        P(("grp", "exp"), None),
    )
    out_specs = (
        P(("grp", "exp"), None),
        P(("grp", "exp"), None),
        P("exp", "grp", None),
        P("exp", None, "grp"),
    )
    return jax.shard_map(body, mesh=mesh, in_specs=in_specs, out_specs=out_specs, check_vma=False)
```

time: 270 us -> 237 us (0.88)
  Pallas kernels: 11.8 us -> 47.5 us
  matrix products: 31.3 us -> 0 us
  waiting for transfers between devices: 105 us -> 78.2 us
  local copies, waits for them, and re-layouts: 28.9 us -> 23.7 us
  starting transfers between devices: 91.1 us -> 86.2 us
    pallas_call x0 -> x7, Pallas kernels: none -> 36.5 us  [the longest x4 15.3 us: weight_part(): pl.pallas_call(weight_kernel, grid_spec=pltpu.PrefetchScalarGridSpec(num_...]
    dot_general x12 -> x0, matrix products: 31.3 us -> none  [dot(): lax.dot_general(left, right, (dims, ((), ())), preferred_element_type=jnp...]
    ppermute x34, waiting for transfers between devices: 105 us -> 78.2 us  [the longest x22 56.4 us: send(): self.done.append(lax.ppermute(value, axis, pairs))]
    ppermute x34, starting transfers between devices: 91.1 us -> 86.2 us  [the longest x22 69.5 us: send(): self.done.append(lax.ppermute(value, axis, pairs))]
    unnamed x125 -> x77, local copies, waits for them, and re-layouts: 26.9 us -> 23.7 us
  transfers between devices with their start and end apart: 34 -> 34, of which waited for: 15 -> 18; matrix products, arithmetic and copies ran while one was open for 12% -> 0% of each run, Pallas kernels for 2% -> 15%
where the time goes in v2:
time: 237 us; the launch traced here: 236 us
  starting transfers between devices  86.2 us (36%)
  waiting for transfers between devices  78.2 us (33%)
  Pallas kernels  47.5 us (20%)
  local copies, waits for them, and re-layouts  23.7 us (10%)
    ppermute x22, starting transfers between devices, send(): self.done.append(lax.ppermute(value, axis, pairs))  69.5 us
    ppermute x22, waiting for transfers between devices, send(): self.done.append(lax.ppermute(value, axis, pairs))  56.4 us
    unnamed x77, local copies, waits for them, and re-layouts  23.7 us
    ppermute x12, waiting for transfers between devices, exchange(): moved[mask] = lax.ppermute(after(blocks[mask], far.done[-1]), 'exp', pairs)  21.8 us
    ppermute x12, starting transfers between devices, exchange(): moved[mask] = lax.ppermute(after(blocks[mask], far.done[-1]), 'exp', pairs)  16.7 us
    pallas_call x4, Pallas kernels, weight_part(): pl.pallas_call(weight_kernel, grid_spec=pltpu.PrefetchScalarGridSpec(num_...  15.3 us
    pallas_call x1, Pallas kernels, forward(): pl.pallas_call(forward_kernel, out_shape=[like((slots, width)), like((slo...  10.3 us
    pallas_call x2, Pallas kernels, combine(): pl.pallas_call(combine_kernel, grid=(width // step,), in_specs=[pl.BlockS...  6.4 us
  transfers between devices with their start and end apart: 34, of which 18 were waited for; matrix products, arithmetic and copies ran while one was open for 0% of the time, Pallas kernels for 15%

profile of v2, /device:TPU:0, one launch (start us, length us, event | category | flops | bytes accessed | tf_op | source)
XLA Modules:
  0.0 236.4 jit_solution(12562138523691557378)
XLA Ops:
  0.6 0.9 copy.10
  1.6 1.2 copy-done.1
  2.8 2.1 route_and_place.1
  4.9 6.1 %collective-permute-start = (bf16[64,2048]{1,0:T(8,128)(2,1)S(1)}, bf16[64,2048]{1,0:T(8,128)(2,1)S(1)}, u32[]{:S(2)}, u32[]{:S(2)}) collective-permute-start(bf16[64,2048]{1,0:T(8,128)(2,1)S(1)} %get-tuple-element.87), channel_id=1, source_target_pairs={{0,7},{1,6},{2,5},{3,4},{4,3},{5,2},{6,1},{7,0},{8,15},{9,14},{10,... | collective-permute-start | bytes 786440 | tf_op jit(solution)/shard_map/ppermute | solution.py:249
  11.2 7.0 %collective-permute-done.refs_7_ = bf16[64,2048]{1,0:T(8,128)(2,1)S(1)} collective-permute-done((bf16[64,2048]{1,0:T(8,128)(2,1)S(1)}, bf16[64,2048]{1,0:T(8,128)(2,1)S(1)}, u32[]{:S(2)}, u32[]{:S(2)}) %collective-permute-start) | collective-permute-done | bytes 262176 | tf_op jit(solution)/shard_map/ppermute | solution.py:249
  18.2 13.1 %collective-permute-start.1 = (bf16[64,2048]{1,0:T(8,128)(2,1)S(1)}, bf16[64,2048]{1,0:T(8,128)(2,1)S(1)}, u32[]{:S(2)}, u32[]{:S(2)}) collective-permute-start(bf16[64,2048]{1,0:T(8,128)(2,1)S(1)} %get-tuple-element.88), channel_id=1, source_target_pairs={{0,5},{1,4},{2,7},{3,6},{4,1},{5,0},{6,3},{7,2},{8,13},{9,12},{10,... | collective-permute-start | bytes 786440 | tf_op jit(solution)/shard_map/ppermute | solution.py:249
  31.3 11.1 %collective-permute-start.6 = (bf16[64,2048]{1,0:T(8,128)(2,1)S(1)}, bf16[64,2048]{1,0:T(8,128)(2,1)S(1)}, u32[]{:S(2)}, u32[]{:S(2)}) collective-permute-start(bf16[64,2048]{1,0:T(8,128)(2,1)S(1)} %get-tuple-element.96), channel_id=1, source_target_pairs={{0,4},{1,5},{2,6},{3,7},{4,0},{5,1},{6,2},{7,3},{8,12},{9,13},{10,... | collective-permute-start | bytes 786440 | tf_op jit(solution)/shard_map/ppermute | solution.py:249
  42.3 8.8 %collective-permute-done.1.refs_5_ = bf16[64,2048]{1,0:T(8,128)(2,1)S(1)} collective-permute-done((bf16[64,2048]{1,0:T(8,128)(2,1)S(1)}, bf16[64,2048]{1,0:T(8,128)(2,1)S(1)}, u32[]{:S(2)}, u32[]{:S(2)}) %collective-permute-start.1) | collective-permute-done | bytes 262176 | tf_op jit(solution)/shard_map/ppermute | solution.py:249
  51.2 1.4 collective-permute-start.2
  52.6 2.5 %place.1 = (bf16[64,2048]{1,0:T(8,128)(2,1)S(1)}, bf16[64,2048]{1,0:T(8,128)(2,1)S(1)}, bf16[64,2048]{1,0:T(8,128)(2,1)}, bf16[64,2048]{1,0:T(8,128)(2,1)}, bf16...) custom-call(bf16[256,512]{1,0:T(8,128)(2,1)S(1)} %get-tuple-element., ...), custom_call_target="tpu_custom_call" | custom-call | flops 1024 | bytes 1024 | tf_op jit(solution)/shard_map/place/pallas_call | solution.py:140
  55.8 2.6 %collective-permute-start.7 = (bf16[64,2048]{1,0:T(8,128)(2,1)S(1)}, bf16[64,2048]{1,0:T(8,128)(2,1)S(1)}, u32[]{:S(2)}, u32[]{:S(2)}) collective-permute-start(bf16[64,2048]{1,0:T(8,128)(2,1)S(1)} %get-tuple-element.103), channel_id=1, source_target_pairs={{0,7},{1,6},{2,5},{3,4},{4,3},{5,2},{6,1},{7,0},{8,15},{9,14},{10,... | collective-permute-start | bytes 786440 | tf_op jit(solution)/shard_map/ppermute | solution.py:249
  58.3 6.7 %collective-permute-done.6.refs_4_ = bf16[64,2048]{1,0:T(8,128)(2,1)S(1)} collective-permute-done((bf16[64,2048]{1,0:T(8,128)(2,1)S(1)}, bf16[64,2048]{1,0:T(8,128)(2,1)S(1)}, u32[]{:S(2)}, u32[]{:S(2)}) %collective-permute-start.6) | collective-permute-done | bytes 262176 | tf_op jit(solution)/shard_map/ppermute | solution.py:249
  65.1 2.7 %collective-permute-start.11 = (bf16[64,2048]{1,0:T(8,128)(2,1)S(1)}, bf16[64,2048]{1,0:T(8,128)(2,1)S(1)}, u32[]{:S(2)}, u32[]{:S(2)}) collective-permute-start(bf16[64,2048]{1,0:T(8,128)(2,1)S(1)} %get-tuple-element.112), channel_id=1, source_target_pairs={{0,6},{1,7},{2,4},{3,5},{4,2},{5,3},{6,0},{7,1},{8,14},{9,15},{10,... | collective-permute-start | bytes 786440 | tf_op jit(solution)/shard_map/ppermute | solution.py:249
  67.8 10.3 %forward.1 = (bf16[512,2048]{1,0:T(8,128)(2,1)}, bf16[512,704]{1,0:T(8,128)(2,1)S(1)}, f32[512,704]{1,0:T(8,128)}, f32[512,704]{1,0:T(8,128)}, bf16[64,2048]{1,0...) custom-call(bf16[64,2048]{1,0:T(8,128)(2,1)S(1)} %get-tuple-element., ...), custom_call_target="tpu_custom_call" | custom-call | flops 1024 | bytes 1024 | tf_op jit(solution)/shard_map/forward/pallas_call | solution.py:173
  78.8 0.7 copy-done.24
  79.5 0.7 copy-done.26
  82.3 0.7 copy-done.34
  84.5 1.7 collective-permute-start.14
  86.2 4.1 %collective-permute-start.13 = (bf16[64,2048]{1,0:T(8,128)(2,1)}, bf16[64,2048]{1,0:T(8,128)(2,1)S(1)}, u32[]{:S(2)}, u32[]{:S(2)}) collective-permute-start(bf16[64,2048]{1,0:T(8,128)(2,1)} %get-tuple-element.115), channel_id=1, source_target_pairs={{0,3},{1,2},{2,1},{3,0},{4,7},{5,6},{6,5},{7,4},{8,11},{9,10},{10,... | collective-permute-start | bytes 786440 | tf_op jit(solution)/shard_map/ppermute | solution.py:262
  90.3 9.1 %collective-permute-done.8.refs_5_ = bf16[64,2048]{1,0:T(8,128)(2,1)S(1)} collective-permute-done((bf16[64,2048]{1,0:T(8,128)(2,1)S(1)}, bf16[64,2048]{1,0:T(8,128)(2,1)S(1)}, u32[]{:S(2)}, u32[]{:S(2)}) %collective-permute-start.8) | collective-permute-done | bytes 262176 | tf_op jit(solution)/shard_map/ppermute | solution.py:249
  100.1 6.9 %collective-permute-start.9 = (bf16[64,2048]{1,0:T(8,128)(2,1)}, bf16[64,2048]{1,0:T(8,128)(2,1)}, u32[]{:S(2)}, u32[]{:S(2)}) collective-permute-start(bf16[64,2048]{1,0:T(8,128)(2,1)} %get-tuple-element.106), channel_id=1, source_target_pairs={{0,7},{1,6},{2,5},{3,4},{4,3},{5,2},{6,1},{7,0},{8,15},{9,14},{10,... | collective-permute-start | bytes 786440 | tf_op jit(solution)/shard_map/ppermute | solution.py:249
  107.0 0.7 copy-done.14
  109.1 1.3 collective-permute-done.10.refs_1_
  111.1 1.4 copy-done.3
  112.5 0.9 copy-done.7
  113.5 0.9 copy-done.9
  114.4 0.9 copy-done.11
  115.4 0.9 copy-done.13
  116.3 0.9 copy-done.15
  117.3 0.9 copy-done.17
  118.2 0.9 copy-done.19
  119.2 0.9 copy-done.21
  120.1 4.9 %grad_proj.1 = (bf16[512,2048]{1,0:T(8,128)(2,1)}, bf16[512,1408]{1,0:T(8,128)(2,1)S(1)}) custom-call(bf16[64,2048]{1,0:T(8,128)(2,1)S(1)} %copy-done.7, bf16[64,2048]{1,0:T(8,128)(2,1)S(1)} %copy-done.21, bf16[64,2048]{1,0:T(8,128)(2,1)S(1)} %copy-done.15, bf16[64,2048]{1,0:T(8,128)(2,1)S(1)} %copy-done.19, bf16[64,2048]{1,0:T(8,128)(2,1)S(1)} %copy-done.17, ...), custom_call_target="tpu_custom_call" | custom-call | flops 1024 | bytes 1024 | tf_op jit(solution)/shard_map/grad_proj/pallas_call | solution.py:191
  125.0 3.4 %weight_part.4 = (bf16[512,1408]{1,0:T(8,128)(2,1)S(1)}, bf16[704,512]{1,0:T(8,128)(2,1)}) custom-call(s32[1]{0:T(128)} %bitcast.4.number_ref, bf16[512,2048]{1,0:T(8,128)(2,1)} %get-tuple-element.132.x_ref, bf16[512,2048]{1,0:T(8,128)(2,1)} %get-tuple-element.133.dy_ref, bf16[512,1408]{1,0:T(8,128)(2,1)S(1)} %get-tuple-element.134.grad_ref, ...), custom_call_target="tpu_custom_call" | custom-call | flops 1024 | bytes 1024 | tf_op jit(solution)/shard_map/weight_part/pallas_call | solution.py:220
  128.5 3.2 %collective-permute-done.21.refs_0_ = bf16[512,1408]{1,0:T(8,128)(2,1)S(1)} collective-permute-done((bf16[512,1408]{1,0:T(8,128)(2,1)S(1)}, bf16[512,1408]{1,0:T(8,128)(2,1)S(1)}, u32[]{:S(2)}, u32[]{:S(2)}) %collective-permute-start.21) | collective-permute-done | bytes 1441824 | tf_op jit(solution)/shard_map/ppermute | solution.py:249
  131.7 1.1 copy-done.37
  132.9 2.4 %collective-permute-done.22.refs_1_ = bf16[704,512]{1,0:T(8,128)(2,1)} collective-permute-done((bf16[704,512]{1,0:T(8,128)(2,1)}, bf16[704,512]{1,0:T(8,128)(2,1)}, u32[]{:S(2)}, u32[]{:S(2)}) %collective-permute-start.22) | collective-permute-done | bytes 720928 | tf_op jit(solution)/shard_map/ppermute | solution.py:249
  135.3 4.0 %weight_part.5 = (bf16[512,1408]{1,0:T(8,128)(2,1)}, bf16[704,512]{1,0:T(8,128)(2,1)S(1)}) custom-call(s32[1]{0:T(128)} %bitcast.3.number_ref, bf16[512,2048]{1,0:T(8,128)(2,1)} %get-tuple-element.132.x_ref, bf16[512,2048]{1,0:T(8,128)(2,1)} %get-tuple-element.133.dy_ref, bf16[512,1408]{1,0:T(8,128)(2,1)S(1)} %get-tuple-element.134.grad_ref, ...), custom_call_target="tpu_custom_call" | custom-call | flops 1024 | bytes 1024 | tf_op jit(solution)/shard_map/weight_part/pallas_call | solution.py:220
  139.3 0.9 copy-done.22
  140.2 1.5 collective-permute-start.23
  141.6 2.6 %weight_part.6 = (bf16[512,1408]{1,0:T(8,128)(2,1)S(1)}, bf16[704,512]{1,0:T(8,128)(2,1)S(1)}) custom-call(s32[1]{0:T(128)} %bitcast.5.number_ref, bf16[512,2048]{1,0:T(8,128)(2,1)} %get-tuple-element.132.x_ref, bf16[512,2048]{1,0:T(8,128)(2,1)} %get-tuple-element.133.dy_ref, bf16[512,1408]{1,0:T(8,128)(2,1)S(1)} %get-tuple-element.134.grad_ref, ...), custom_call_target="tpu_custom_call" | custom-call | flops 1024 | bytes 1024 | tf_op jit(solution)/shard_map/weight_part/pallas_call | solution.py:220
  144.4 1.6 collective-permute-start.17
  146.0 1.3 collective-permute-start.15
  147.3 6.1 %grad_branch.1 = (bf16[64,2048]{1,0:T(8,128)(2,1)S(1)}, bf16[64,2048]{1,0:T(8,128)(2,1)S(1)}, bf16[64,2048]{1,0:T(8,128)(2,1)S(1)}, bf16[64,2048]{1,0:T(8,128)(2...) custom-call(bf16[512,1408]{1,0:T(8,128)(2,1)S(1)} %get-tuple-element, ...), custom_call_target="tpu_custom_call" | custom-call | flops 1024 | bytes 1024 | tf_op jit(solution)/shard_map/grad_branch/pallas_call | solution.py:201
  153.4 2.1 collective-permute-done.17.refs_6_
  155.5 10.6 %collective-permute-start.20 = (bf16[64,2048]{1,0:T(8,128)(2,1)S(1)}, bf16[64,2048]{1,0:T(8,128)(2,1)S(1)}, u32[]{:S(2)}, u32[]{:S(2)}) collective-permute-start(bf16[64,2048]{1,0:T(8,128)(2,1)S(1)} %copy-done.31), channel_id=1, source_target_pairs={{0,4},{1,5},{2,6},{3,7},{4,0},{5,1},{6,2},{7,3},{8,12},{9,13},{10,... | collective-permute-start | bytes 786440 | tf_op jit(solution)/shard_map/ppermute | solution.py:249
  166.1 8.0 %collective-permute-done.23.refs_0_ = bf16[512,1408]{1,0:T(8,128)(2,1)} collective-permute-done((bf16[512,1408]{1,0:T(8,128)(2,1)}, bf16[512,1408]{1,0:T(8,128)(2,1)}, u32[]{:S(2)}, u32[]{:S(2)}) %collective-permute-start.23) | collective-permute-done | bytes 1441824 | tf_op jit(solution)/shard_map/ppermute | solution.py:249
  174.1 1.5 collective-permute-start.24
  175.6 1.1 collective-permute-done.15.refs_5_
  176.7 2.5 %collective-permute-start.27 = (bf16[64,2048]{1,0:T(8,128)(2,1)S(1)}, bf16[64,2048]{1,0:T(8,128)(2,1)S(1)}, u32[]{:S(2)}, u32[]{:S(2)}) collective-permute-start(bf16[64,2048]{1,0:T(8,128)(2,1)S(1)} %get-tuple-element.150), channel_id=1, source_target_pairs={{0,7},{1,6},{2,5},{3,4},{4,3},{5,2},{6,1},{7,0},{8,15},{9,14},{10,... | collective-permute-start | bytes 786440 | tf_op jit(solution)/shard_map/ppermute | solution.py:249
  179.6 1.4 collective-permute-done.20.refs_4_
  181.0 12.4 %collective-permute-done.19.refs_3_ = bf16[64,2048]{1,0:T(8,128)(2,1)S(1)} collective-permute-done((bf16[64,2048]{1,0:T(8,128)(2,1)S(1)}, bf16[64,2048]{1,0:T(8,128)(2,1)S(1)}, u32[]{:S(2)}, u32[]{:S(2)}) %collective-permute-start.19) | collective-permute-done | bytes 262176 | tf_op jit(solution)/shard_map/ppermute | solution.py:262
  193.4 2.8 %collective-permute-start.30 = (bf16[64,2048]{1,0:T(8,128)(2,1)S(1)}, bf16[64,2048]{1,0:T(8,128)(2,1)S(1)}, u32[]{:S(2)}, u32[]{:S(2)}) collective-permute-start(bf16[64,2048]{1,0:T(8,128)(2,1)S(1)} %get-tuple-element.155), channel_id=1, source_target_pairs={{0,6},{1,7},{2,4},{3,5},{4,2},{5,3},{6,0},{7,1},{8,14},{9,15},{10,... | collective-permute-start | bytes 786440 | tf_op jit(solution)/shard_map/ppermute | solution.py:249
  196.2 1.4 collective-permute-done.18.refs_2_
  197.6 2.1 collective-permute-start.28
  199.7 1.9 collective-permute-done.16.refs_1_
  201.6 3.9 %combine.2 = bf16[256,2048]{1,0:T(8,128)(2,1)} custom-call(bf16[256,512]{1,0:T(8,128)(2,1)S(1)} %get-tuple-element.83.refs_0_.place_ref, bf16[256,2048]{1,0:T(8,128)(2,1)S(1)} %copy-done.2, bf16[64,2048]{1,0:T(8,128)(2,1)S(1)} %copy-done.5, bf16[64,2048]{1,0:T(8,128)(2,1)S(1)} %collective-permute-done.16.refs_1_, ...), custom_call_target="tpu_custom_call" | custom-call | flops 1024 | bytes 1024 | tf_op jit(solution)/shard_map/combine/pallas_call | solution.py:157
  205.4 9.0 %collective-permute-start.31 = (bf16[64,2048]{1,0:T(8,128)(2,1)S(1)}, bf16[64,2048]{1,0:T(8,128)(2,1)S(1)}, u32[]{:S(2)}, u32[]{:S(2)}) collective-permute-start(bf16[64,2048]{1,0:T(8,128)(2,1)S(1)} %get-tuple-element.156), channel_id=1, source_target_pairs={{0,2},{1,3},{2,0},{3,1},{4,6},{5,7},{6,4},{7,5},{8,10},{9,11},{10,... | collective-permute-start | bytes 786440 | tf_op jit(solution)/shard_map/ppermute | solution.py:262
  214.4 1.2 collective-permute-start.33
  215.6 6.2 %collective-permute-done.28.refs_5_ = bf16[64,2048]{1,0:T(8,128)(2,1)S(1)} collective-permute-done((bf16[64,2048]{1,0:T(8,128)(2,1)S(1)}, bf16[64,2048]{1,0:T(8,128)(2,1)S(1)}, u32[]{:S(2)}, u32[]{:S(2)}) %collective-permute-start.28) | collective-permute-done | bytes 262176 | tf_op jit(solution)/shard_map/ppermute | solution.py:249
  221.8 1.8 collective-permute-start.29
  223.6 5.2 %weight_part.7 = (f32[512,1408]{1,0:T(8,128)}, f32[704,512]{1,0:T(8,128)}) custom-call(s32[1]{0:T(128)} %bitcast.2.number_ref, bf16[512,2048]{1,0:T(8,128)(2,1)} %get-tuple-element.132.x_ref, bf16[512,2048]{1,0:T(8,128)(2,1)} %get-tuple-element.133.dy_ref, bf16[512,1408]{1,0:T(8,128)(2,1)S(1)} %get-tuple-element.134.grad_ref, ...), custom_call_target="tpu_custom_call" | custom-call | flops 1024 | bytes 1024 | tf_op jit(solution)/shard_map/weight_part/pallas_call | solution.py:220
  229.6 4.2 %collective-permute-done.32.refs_3_ = bf16[64,2048]{1,0:T(8,128)(2,1)S(1)} collective-permute-done((bf16[64,2048]{1,0:T(8,128)(2,1)S(1)}, bf16[64,2048]{1,0:T(8,128)(2,1)S(1)}, u32[]{:S(2)}, u32[]{:S(2)}) %collective-permute-start.32) | collective-permute-done | bytes 262176 | tf_op jit(solution)/shard_map/ppermute | solution.py:262
  233.8 2.5 %combine.3 = bf16[256,2048]{1,0:T(8,128)(2,1)} custom-call(bf16[256,512]{1,0:T(8,128)(2,1)S(1)} %get-tuple-element.83.refs_0_.place_ref, bf16[256,2048]{1,0:T(8,128)(2,1)S(1)} %copy-done, bf16[64,2048]{1,0:T(8,128)(2,1)S(1)} %get-tuple-element.146.refs_0_, bf16[64,2048]{1,0:T(8,128)(2,1)S(1)} %collective-permute-done.29.refs_1_, ...), custom_call_target="tpu_custom_call" | custom-call | flops 1024 | bytes 1024 | tf_op jit(solution)/shard_map/combine/pallas_call | solution.py:157
  (93 shorter events, 9.4 us)
Async XLA Ops:
  0.6 51.9 %copy-start = (bf16[256,2048]{1,0:T(8,128)(2,1)S(1)}, bf16[256,2048]{1,0:T(8,128)(2,1)}, u32[]{:S(2)}) copy-start(bf16[256,2048]{1,0:T(8,128)(2,1)} %data_ref.3) | copy-start | bytes 3145732
  1.6 1.2 copy-start.1
  4.9 13.3 %collective-permute-start = (bf16[64,2048]{1,0:T(8,128)(2,1)S(1)}, bf16[64,2048]{1,0:T(8,128)(2,1)S(1)}, u32[]{:S(2)}, u32[]{:S(2)}) collective-permute-start(bf16[64,2048]{1,0:T(8,128)(2,1)S(1)} %get-tuple-element.87), channel_id=1, source_target_pairs={{0,7},{1,6},{2,5},{3,4},{4,3},{5,2},{6,1},{7,0},{8,15},{9,14},{10,... | collective-permute-start | bytes 786440 | tf_op jit(solution)/shard_map/ppermute | solution.py:249
  10.9 20.3 %collective-permute-start.3 = (bf16[64,2048]{1,0:T(8,128)(2,1)S(1)}, bf16[64,2048]{1,0:T(8,128)(2,1)S(1)}, u32[]{:S(2)}, u32[]{:S(2)}) collective-permute-start(bf16[64,2048]{1,0:T(8,128)(2,1)S(1)} %get-tuple-element.91), channel_id=1, source_target_pairs={{0,6},{1,7},{2,4},{3,5},{4,2},{5,3},{6,0},{7,1},{8,14},{9,15},{10,... | collective-permute-start | bytes 786440 | tf_op jit(solution)/shard_map/ppermute | solution.py:249
  18.2 33.0 %collective-permute-start.1 = (bf16[64,2048]{1,0:T(8,128)(2,1)S(1)}, bf16[64,2048]{1,0:T(8,128)(2,1)S(1)}, u32[]{:S(2)}, u32[]{:S(2)}) collective-permute-start(bf16[64,2048]{1,0:T(8,128)(2,1)S(1)} %get-tuple-element.88), channel_id=1, source_target_pairs={{0,5},{1,4},{2,7},{3,6},{4,1},{5,0},{6,3},{7,2},{8,13},{9,12},{10,... | collective-permute-start | bytes 786440 | tf_op jit(solution)/shard_map/ppermute | solution.py:249
  31.3 36.5 %collective-permute-start.5 = (bf16[64,2048]{1,0:T(8,128)(2,1)S(1)}, bf16[64,2048]{1,0:T(8,128)(2,1)S(1)}, u32[]{:S(2)}, u32[]{:S(2)}) collective-permute-start(bf16[64,2048]{1,0:T(8,128)(2,1)S(1)} %get-tuple-element.94), channel_id=1, source_target_pairs={{0,3},{1,2},{2,1},{3,0},{4,7},{5,6},{6,5},{7,4},{8,11},{9,10},{10,... | collective-permute-start | bytes 786440 | tf_op jit(solution)/shard_map/ppermute | solution.py:262
  31.3 33.8 %collective-permute-start.6 = (bf16[64,2048]{1,0:T(8,128)(2,1)S(1)}, bf16[64,2048]{1,0:T(8,128)(2,1)S(1)}, u32[]{:S(2)}, u32[]{:S(2)}) collective-permute-start(bf16[64,2048]{1,0:T(8,128)(2,1)S(1)} %get-tuple-element.96), channel_id=1, source_target_pairs={{0,4},{1,5},{2,6},{3,7},{4,0},{5,1},{6,2},{7,3},{8,12},{9,13},{10,... | collective-permute-start | bytes 786440 | tf_op jit(solution)/shard_map/ppermute | solution.py:249
  42.3 25.4 %collective-permute-start.4 = (bf16[64,2048]{1,0:T(8,128)(2,1)S(1)}, bf16[64,2048]{1,0:T(8,128)(2,1)S(1)}, u32[]{:S(2)}, u32[]{:S(2)}) collective-permute-start(bf16[64,2048]{1,0:T(8,128)(2,1)S(1)} %get-tuple-element.92), channel_id=1, source_target_pairs={{0,2},{1,3},{2,0},{3,1},{4,6},{5,7},{6,4},{7,5},{8,10},{9,11},{10,... | collective-permute-start | bytes 786440 | tf_op jit(solution)/shard_map/ppermute | solution.py:262
  51.2 16.6 %collective-permute-start.2 = (bf16[64,2048]{1,0:T(8,128)(2,1)S(1)}, bf16[64,2048]{1,0:T(8,128)(2,1)S(1)}, u32[]{:S(2)}, u32[]{:S(2)}) collective-permute-start(bf16[64,2048]{1,0:T(8,128)(2,1)S(1)} %get-tuple-element.89), channel_id=1, source_target_pairs={{0,1},{1,0},{2,3},{3,2},{4,5},{5,4},{6,7},{7,6},{8,9},{9,8},{10,11... | collective-permute-start | bytes 786440 | tf_op jit(solution)/shard_map/ppermute | solution.py:262
  55.0 0.7 copy-start.6
  55.8 27.3 %collective-permute-start.7 = (bf16[64,2048]{1,0:T(8,128)(2,1)S(1)}, bf16[64,2048]{1,0:T(8,128)(2,1)S(1)}, u32[]{:S(2)}, u32[]{:S(2)}) collective-permute-start(bf16[64,2048]{1,0:T(8,128)(2,1)S(1)} %get-tuple-element.103), channel_id=1, source_target_pairs={{0,7},{1,6},{2,5},{3,4},{4,3},{5,2},{6,1},{7,0},{8,15},{9,14},{10,... | collective-permute-start | bytes 786440 | tf_op jit(solution)/shard_map/ppermute | solution.py:249
  65.1 18.7 %collective-permute-start.11 = (bf16[64,2048]{1,0:T(8,128)(2,1)S(1)}, bf16[64,2048]{1,0:T(8,128)(2,1)S(1)}, u32[]{:S(2)}, u32[]{:S(2)}) collective-permute-start(bf16[64,2048]{1,0:T(8,128)(2,1)S(1)} %get-tuple-element.112), channel_id=1, source_target_pairs={{0,6},{1,7},{2,4},{3,5},{4,2},{5,3},{6,0},{7,1},{8,14},{9,15},{10,... | collective-permute-start | bytes 786440 | tf_op jit(solution)/shard_map/ppermute | solution.py:249
  78.8 0.7 copy-start.24
  79.5 0.7 copy-start.26
  82.3 0.7 copy-start.34
  83.1 0.7 copy-start.8
  83.8 15.6 %collective-permute-start.8 = (bf16[64,2048]{1,0:T(8,128)(2,1)S(1)}, bf16[64,2048]{1,0:T(8,128)(2,1)S(1)}, u32[]{:S(2)}, u32[]{:S(2)}) collective-permute-start(bf16[64,2048]{1,0:T(8,128)(2,1)S(1)} %get-tuple-element.105), channel_id=1, source_target_pairs={{0,5},{1,4},{2,7},{3,6},{4,1},{5,0},{6,3},{7,2},{8,13},{9,12},{10,... | collective-permute-start | bytes 786440 | tf_op jit(solution)/shard_map/ppermute | solution.py:249
  84.5 22.5 %collective-permute-start.12 = (bf16[64,2048]{1,0:T(8,128)(2,1)}, bf16[64,2048]{1,0:T(8,128)(2,1)S(1)}, u32[]{:S(2)}, u32[]{:S(2)}) collective-permute-start(bf16[64,2048]{1,0:T(8,128)(2,1)} %get-tuple-element.113), channel_id=1, source_target_pairs={{0,2},{1,3},{2,0},{3,1},{4,6},{5,7},{6,4},{7,5},{8,10},{9,11},{10,... | collective-permute-start | bytes 786440 | tf_op jit(solution)/shard_map/ppermute | solution.py:262
  84.5 23.2 %collective-permute-start.14 = (bf16[64,2048]{1,0:T(8,128)(2,1)}, bf16[64,2048]{1,0:T(8,128)(2,1)S(1)}, u32[]{:S(2)}, u32[]{:S(2)}) collective-permute-start(bf16[64,2048]{1,0:T(8,128)(2,1)} %get-tuple-element.117), channel_id=1, source_target_pairs={{0,4},{1,5},{2,6},{3,7},{4,0},{5,1},{6,2},{7,3},{8,12},{9,13},{10,... | collective-permute-start | bytes 786440 | tf_op jit(solution)/shard_map/ppermute | solution.py:249
  86.2 22.2 %collective-permute-start.13 = (bf16[64,2048]{1,0:T(8,128)(2,1)}, bf16[64,2048]{1,0:T(8,128)(2,1)S(1)}, u32[]{:S(2)}, u32[]{:S(2)}) collective-permute-start(bf16[64,2048]{1,0:T(8,128)(2,1)} %get-tuple-element.115), channel_id=1, source_target_pairs={{0,3},{1,2},{2,1},{3,0},{4,7},{5,6},{6,5},{7,4},{8,11},{9,10},{10,... | collective-permute-start | bytes 786440 | tf_op jit(solution)/shard_map/ppermute | solution.py:262
  100.1 10.3 %collective-permute-start.10 = (bf16[64,2048]{1,0:T(8,128)(2,1)S(1)}, bf16[64,2048]{1,0:T(8,128)(2,1)S(1)}, u32[]{:S(2)}, u32[]{:S(2)}) collective-permute-start(bf16[64,2048]{1,0:T(8,128)(2,1)S(1)} %get-tuple-element.109), channel_id=1, source_target_pairs={{0,1},{1,0},{2,3},{3,2},{4,5},{5,4},{6,7},{7,6},{8,9},{9,8},{10,11... | collective-permute-start | bytes 786440 | tf_op jit(solution)/shard_map/ppermute | solution.py:262
  100.1 24.9 %collective-permute-start.9 = (bf16[64,2048]{1,0:T(8,128)(2,1)}, bf16[64,2048]{1,0:T(8,128)(2,1)}, u32[]{:S(2)}, u32[]{:S(2)}) collective-permute-start(bf16[64,2048]{1,0:T(8,128)(2,1)} %get-tuple-element.106), channel_id=1, source_target_pairs={{0,7},{1,6},{2,5},{3,4},{4,3},{5,2},{6,1},{7,0},{8,15},{9,14},{10,... | collective-permute-start | bytes 786440 | tf_op jit(solution)/shard_map/ppermute | solution.py:249
  107.0 0.7 copy-start.14
  107.7 0.7 copy-start.16
  111.1 1.4 copy-start.3
  112.5 0.9 copy-start.7
  113.5 0.9 copy-start.9
  114.4 0.9 copy-start.11
  115.4 0.9 copy-start.13
  116.3 0.9 copy-start.15
  117.3 0.9 copy-start.17
  118.2 0.9 copy-start.19
  119.2 0.9 copy-start.21
  128.5 3.2 %collective-permute-start.21 = (bf16[512,1408]{1,0:T(8,128)(2,1)S(1)}, bf16[512,1408]{1,0:T(8,128)(2,1)S(1)}, u32[]{:S(2)}, u32[]{:S(2)}) collective-permute-start(bf16[512,1408]{1,0:T(8,128)(2,1)S(1)} %get-tuple-element.135), channel_id=1, source_target_pairs={{0,8},{8,0},{16,24},{24,16},{1,9},{9,1},{17,25},{25,17},{2,10},{10... | collective-permute-start | bytes 4325384 | tf_op jit(solution)/shard_map/ppermute | solution.py:249
  131.7 1.1 copy-start.37
  132.8 2.5 %collective-permute-start.22 = (bf16[704,512]{1,0:T(8,128)(2,1)}, bf16[704,512]{1,0:T(8,128)(2,1)}, u32[]{:S(2)}, u32[]{:S(2)}) collective-permute-start(bf16[704,512]{1,0:T(8,128)(2,1)} %get-tuple-element.137), channel_id=1, source_target_pairs={{0,8},{8,0},{16,24},{24,16},{1,9},{9,1},{17,25},{25,17},{2,10},{10... | collective-permute-start | bytes 2162696 | tf_op jit(solution)/shard_map/ppermute | solution.py:249
  139.3 0.9 copy-start.22
  140.2 33.9 %collective-permute-start.23 = (bf16[512,1408]{1,0:T(8,128)(2,1)}, bf16[512,1408]{1,0:T(8,128)(2,1)}, u32[]{:S(2)}, u32[]{:S(2)}) collective-permute-start(bf16[512,1408]{1,0:T(8,128)(2,1)} %get-tuple-element.138), channel_id=1, source_target_pairs={{0,16},{8,24},{16,0},{24,8},{1,17},{9,25},{17,1},{25,9},{2,18},{10... | collective-permute-start | bytes 4325384 | tf_op jit(solution)/shard_map/ppermute | solution.py:249
  141.6 2.7 %copy-start.35 = (bf16[64,2048]{1,0:T(8,128)(2,1)S(1)}, bf16[64,2048]{1,0:T(8,128)(2,1)}, u32[]{:S(2)}) copy-start(bf16[64,2048]{1,0:T(8,128)(2,1)} %copy-done.34) | copy-start | bytes 786436
  141.6 4.3 %copy-start.33 = (bf16[64,2048]{1,0:T(8,128)(2,1)S(1)}, bf16[64,2048]{1,0:T(8,128)(2,1)}, u32[]{:S(2)}) copy-start(bf16[64,2048]{1,0:T(8,128)(2,1)} %copy-done.32) | copy-start | bytes 786436
  144.3 35.0 %collective-permute-start.25 = (bf16[512,1408]{1,0:T(8,128)(2,1)S(1)}, bf16[512,1408]{1,0:T(8,128)(2,1)S(1)}, u32[]{:S(2)}, u32[]{:S(2)}) collective-permute-start(bf16[512,1408]{1,0:T(8,128)(2,1)S(1)} %get-tuple-element.142), channel_id=1, source_target_pairs={{0,8},{8,0},{16,24},{24,16},{1,9},{9,1},{17,25},{25,17},{2,10},{10... | collective-permute-start | bytes 4325384 | tf_op jit(solution)/shard_map/ppermute | solution.py:249
  144.4 11.1 %collective-permute-start.17 = (bf16[64,2048]{1,0:T(8,128)(2,1)S(1)}, bf16[64,2048]{1,0:T(8,128)(2,1)S(1)}, u32[]{:S(2)}, u32[]{:S(2)}) collective-permute-start(bf16[64,2048]{1,0:T(8,128)(2,1)S(1)} %copy-done.35), channel_id=1, source_target_pairs={{0,6},{1,7},{2,4},{3,5},{4,2},{5,3},{6,0},{7,1},{8,14},{9,15},{10,... | collective-permute-start | bytes 786440 | tf_op jit(solution)/shard_map/ppermute | solution.py:249
  145.9 9.5 %copy-start.31 = (bf16[64,2048]{1,0:T(8,128)(2,1)S(1)}, bf16[64,2048]{1,0:T(8,128)(2,1)}, u32[]{:S(2)}) copy-start(bf16[64,2048]{1,0:T(8,128)(2,1)} %copy-done.30) | copy-start | bytes 786436
  145.9 28.2 %copy-start.23 = (bf16[704,512]{1,0:T(8,128)(2,1)S(1)}, bf16[704,512]{1,0:T(8,128)(2,1)}, u32[]{:S(2)}) copy-start(bf16[704,512]{1,0:T(8,128)(2,1)} %copy-done.22) | copy-start | bytes 2162692
  145.9 29.6 %copy-start.29 = (bf16[64,2048]{1,0:T(8,128)(2,1)S(1)}, bf16[64,2048]{1,0:T(8,128)(2,1)}, u32[]{:S(2)}) copy-start(bf16[64,2048]{1,0:T(8,128)(2,1)} %copy-done.28) | copy-start | bytes 786436
  146.0 33.3 %copy-start.27 = (bf16[64,2048]{1,0:T(8,128)(2,1)S(1)}, bf16[64,2048]{1,0:T(8,128)(2,1)}, u32[]{:S(2)}) copy-start(bf16[64,2048]{1,0:T(8,128)(2,1)} %copy-done.26) | copy-start | bytes 786436
  146.0 47.5 %copy-start.25 = (bf16[64,2048]{1,0:T(8,128)(2,1)S(1)}, bf16[64,2048]{1,0:T(8,128)(2,1)}, u32[]{:S(2)}) copy-start(bf16[64,2048]{1,0:T(8,128)(2,1)} %copy-done.24) | copy-start | bytes 786436
  146.0 55.6 %copy-start.2 = (bf16[256,2048]{1,0:T(8,128)(2,1)S(1)}, bf16[256,2048]{1,0:T(8,128)(2,1)}, u32[]{:S(2)}) copy-start(bf16[256,2048]{1,0:T(8,128)(2,1)} %data_ref.2) | copy-start | bytes 3145732
  146.0 55.6 %copy-start.5 = (bf16[64,2048]{1,0:T(8,128)(2,1)S(1)}, bf16[64,2048]{1,0:T(8,128)(2,1)}, u32[]{:S(2)}) copy-start(bf16[64,2048]{1,0:T(8,128)(2,1)} %copy-done.4) | copy-start | bytes 786436
  146.0 30.7 %collective-permute-start.15 = (bf16[64,2048]{1,0:T(8,128)(2,1)S(1)}, bf16[64,2048]{1,0:T(8,128)(2,1)S(1)}, u32[]{:S(2)}, u32[]{:S(2)}) collective-permute-start(bf16[64,2048]{1,0:T(8,128)(2,1)S(1)} %copy-done.33), channel_id=1, source_target_pairs={{0,5},{1,4},{2,7},{3,6},{4,1},{5,0},{6,3},{7,2},{8,13},{9,12},{10,... | collective-permute-start | bytes 786440 | tf_op jit(solution)/shard_map/ppermute | solution.py:249
  155.5 25.5 %collective-permute-start.20 = (bf16[64,2048]{1,0:T(8,128)(2,1)S(1)}, bf16[64,2048]{1,0:T(8,128)(2,1)S(1)}, u32[]{:S(2)}, u32[]{:S(2)}) collective-permute-start(bf16[64,2048]{1,0:T(8,128)(2,1)S(1)} %copy-done.31), channel_id=1, source_target_pairs={{0,4},{1,5},{2,6},{3,7},{4,0},{5,1},{6,2},{7,3},{8,12},{9,13},{10,... | collective-permute-start | bytes 786440 | tf_op jit(solution)/shard_map/ppermute | solution.py:249
  174.1 47.7 %collective-permute-start.24 = (bf16[704,512]{1,0:T(8,128)(2,1)S(1)}, bf16[704,512]{1,0:T(8,128)(2,1)S(1)}, u32[]{:S(2)}, u32[]{:S(2)}) collective-permute-start(bf16[704,512]{1,0:T(8,128)(2,1)S(1)} %copy-done.23), channel_id=1, source_target_pairs={{0,16},{8,24},{16,0},{24,8},{1,17},{9,25},{17,1},{25,9},{2,18},{10... | collective-permute-start | bytes 2162696 | tf_op jit(solution)/shard_map/ppermute | solution.py:249
  175.6 17.8 %collective-permute-start.19 = (bf16[64,2048]{1,0:T(8,128)(2,1)S(1)}, bf16[64,2048]{1,0:T(8,128)(2,1)S(1)}, u32[]{:S(2)}, u32[]{:S(2)}) collective-permute-start(bf16[64,2048]{1,0:T(8,128)(2,1)S(1)} %copy-done.29), channel_id=1, source_target_pairs={{0,3},{1,2},{2,1},{3,0},{4,7},{5,6},{6,5},{7,4},{8,11},{9,10},{10,... | collective-permute-start | bytes 786440 | tf_op jit(solution)/shard_map/ppermute | solution.py:262
  176.7 16.7 %collective-permute-start.27 = (bf16[64,2048]{1,0:T(8,128)(2,1)S(1)}, bf16[64,2048]{1,0:T(8,128)(2,1)S(1)}, u32[]{:S(2)}, u32[]{:S(2)}) collective-permute-start(bf16[64,2048]{1,0:T(8,128)(2,1)S(1)} %get-tuple-element.150), channel_id=1, source_target_pairs={{0,7},{1,6},{2,5},{3,4},{4,3},{5,2},{6,1},{7,0},{8,15},{9,14},{10,... | collective-permute-start | bytes 786440 | tf_op jit(solution)/shard_map/ppermute | solution.py:249
  179.3 26.2 %copy-start.36 = (bf16[512,1408]{1,0:T(8,128)(2,1)}, bf16[512,1408]{1,0:T(8,128)(2,1)S(1)}, u32[]{:S(2)}) copy-start(bf16[512,1408]{1,0:T(8,128)(2,1)S(1)} %collective-permute-done.25.refs_2_) | copy-start | bytes 4325380
  179.3 18.3 %collective-permute-start.18 = (bf16[64,2048]{1,0:T(8,128)(2,1)S(1)}, bf16[64,2048]{1,0:T(8,128)(2,1)S(1)}, u32[]{:S(2)}, u32[]{:S(2)}) collective-permute-start(bf16[64,2048]{1,0:T(8,128)(2,1)S(1)} %copy-done.27), channel_id=1, source_target_pairs={{0,2},{1,3},{2,0},{3,1},{4,6},{5,7},{6,4},{7,5},{8,10},{9,11},{10,... | collective-permute-start | bytes 786440 | tf_op jit(solution)/shard_map/ppermute | solution.py:262
  181.0 42.6 %collective-permute-start.26 = (bf16[704,512]{1,0:T(8,128)(2,1)S(1)}, bf16[704,512]{1,0:T(8,128)(2,1)S(1)}, u32[]{:S(2)}, u32[]{:S(2)}) collective-permute-start(bf16[704,512]{1,0:T(8,128)(2,1)S(1)} %get-tuple-element.144), channel_id=1, source_target_pairs={{0,8},{8,0},{16,24},{24,16},{1,9},{9,1},{17,25},{25,17},{2,10},{10... | collective-permute-start | bytes 2162696 | tf_op jit(solution)/shard_map/ppermute | solution.py:249
  193.4 8.1 %collective-permute-start.16 = (bf16[64,2048]{1,0:T(8,128)(2,1)S(1)}, bf16[64,2048]{1,0:T(8,128)(2,1)S(1)}, u32[]{:S(2)}, u32[]{:S(2)}) collective-permute-start(bf16[64,2048]{1,0:T(8,128)(2,1)S(1)} %copy-done.25), channel_id=1, source_target_pairs={{0,1},{1,0},{2,3},{3,2},{4,5},{5,4},{6,7},{7,6},{8,9},{9,8},{10,11... | collective-permute-start | bytes 786440 | tf_op jit(solution)/shard_map/ppermute | solution.py:262
  193.4 12.0 %collective-permute-start.30 = (bf16[64,2048]{1,0:T(8,128)(2,1)S(1)}, bf16[64,2048]{1,0:T(8,128)(2,1)S(1)}, u32[]{:S(2)}, u32[]{:S(2)}) collective-permute-start(bf16[64,2048]{1,0:T(8,128)(2,1)S(1)} %get-tuple-element.155), channel_id=1, source_target_pairs={{0,6},{1,7},{2,4},{3,5},{4,2},{5,3},{6,0},{7,1},{8,14},{9,15},{10,... | collective-permute-start | bytes 786440 | tf_op jit(solution)/shard_map/ppermute | solution.py:249
  197.6 24.2 %collective-permute-start.28 = (bf16[64,2048]{1,0:T(8,128)(2,1)S(1)}, bf16[64,2048]{1,0:T(8,128)(2,1)S(1)}, u32[]{:S(2)}, u32[]{:S(2)}) collective-permute-start(bf16[64,2048]{1,0:T(8,128)(2,1)S(1)} %get-tuple-element.151), channel_id=1, source_target_pairs={{0,5},{1,4},{2,7},{3,6},{4,1},{5,0},{6,3},{7,2},{8,13},{9,12},{10,... | collective-permute-start | bytes 786440 | tf_op jit(solution)/shard_map/ppermute | solution.py:249
  205.4 23.9 %collective-permute-start.31 = (bf16[64,2048]{1,0:T(8,128)(2,1)S(1)}, bf16[64,2048]{1,0:T(8,128)(2,1)S(1)}, u32[]{:S(2)}, u32[]{:S(2)}) collective-permute-start(bf16[64,2048]{1,0:T(8,128)(2,1)S(1)} %get-tuple-element.156), channel_id=1, source_target_pairs={{0,2},{1,3},{2,0},{3,1},{4,6},{5,7},{6,4},{7,5},{8,10},{9,11},{10,... | collective-permute-start | bytes 786440 | tf_op jit(solution)/shard_map/ppermute | solution.py:262
  214.4 15.2 %collective-permute-start.33 = (bf16[64,2048]{1,0:T(8,128)(2,1)S(1)}, bf16[64,2048]{1,0:T(8,128)(2,1)S(1)}, u32[]{:S(2)}, u32[]{:S(2)}) collective-permute-start(bf16[64,2048]{1,0:T(8,128)(2,1)S(1)} %get-tuple-element.160), channel_id=1, source_target_pairs={{0,4},{1,5},{2,6},{3,7},{4,0},{5,1},{6,2},{7,3},{8,12},{9,13},{10,... | collective-permute-start | bytes 786440 | tf_op jit(solution)/shard_map/ppermute | solution.py:249
  221.8 12.0 %collective-permute-start.32 = (bf16[64,2048]{1,0:T(8,128)(2,1)S(1)}, bf16[64,2048]{1,0:T(8,128)(2,1)S(1)}, u32[]{:S(2)}, u32[]{:S(2)}) collective-permute-start(bf16[64,2048]{1,0:T(8,128)(2,1)S(1)} %get-tuple-element.158), channel_id=1, source_target_pairs={{0,3},{1,2},{2,1},{3,0},{4,7},{5,6},{6,5},{7,4},{8,11},{9,10},{10,... | collective-permute-start | bytes 786440 | tf_op jit(solution)/shard_map/ppermute | solution.py:262
  221.8 12.0 %collective-permute-start.29 = (bf16[64,2048]{1,0:T(8,128)(2,1)S(1)}, bf16[64,2048]{1,0:T(8,128)(2,1)S(1)}, u32[]{:S(2)}, u32[]{:S(2)}) collective-permute-start(bf16[64,2048]{1,0:T(8,128)(2,1)S(1)} %get-tuple-element.152), channel_id=1, source_target_pairs={{0,1},{1,0},{2,3},{3,2},{4,5},{5,4},{6,7},{7,6},{8,9},{9,8},{10,11... | collective-permute-start | bytes 786440 | tf_op jit(solution)/shard_map/ppermute | solution.py:262
  (8 other events, 5.6 us)

commit v3 on v2

v3 whole, which is shorter than its diff:
```python
import jax
import jax.numpy as jnp
from jax import lax
from jax.experimental import pallas as pl
from jax.experimental.pallas import tpu as pltpu
from jax.sharding import PartitionSpec as P

SMALL = pl.CostEstimate(flops=1024, bytes_accessed=1024, transcendentals=0)
ROWS = 256


def dot(left, right, dims):
    return lax.dot_general(left, right, (dims, ((), ())), preferred_element_type=jnp.float32)


def params(mebibytes):
    return pltpu.CompilerParams(vmem_limit_bytes=mebibytes * 1024 * 1024, dimension_semantics=("arbitrary",))


def whole(array):
    return pl.BlockSpec(array.shape, lambda *index: (0,) * len(array.shape), pipeline_mode=pl.Buffered(1))


def like(shape, dtype=jnp.bfloat16):
    return jax.ShapeDtypeStruct(shape, dtype)


def route_kernel(experts, cap, rel_ref, data_ref, place_ref, *block_refs):
    rows = rel_ref.shape[1]
    slots = experts * cap

    @pl.when(pl.program_id(0) == 0)
    def _():
        rel = rel_ref[...]
        onehot = lax.broadcasted_iota(jnp.int32, (max(experts, 16), rows), 0) == rel
        before = lax.broadcasted_iota(jnp.int32, (rows, rows), 0) < lax.broadcasted_iota(jnp.int32, (rows, rows), 1)
        ranks = dot(onehot.astype(jnp.bfloat16), before.astype(jnp.bfloat16), ((1,), (0,)))
        rank = jnp.sum(jnp.where(onehot, ranks, 0.0), axis=0, keepdims=True).astype(jnp.int32)
        target = rel * cap + rank
        place_ref[...] = (lax.broadcasted_iota(jnp.int32, (slots, rows), 0) == target).astype(jnp.bfloat16)

    place_kernel(cap, place_ref, data_ref, *block_refs)


def place_kernel(cap, place_ref, data_ref, *block_refs):
    moved = dot(place_ref[...], data_ref[...], ((1,), (0,))).astype(jnp.bfloat16)
    for index, block_ref in enumerate(block_refs):
        block_ref[...] = moved[index * cap : (index + 1) * cap]


def combine_kernel(place_ref, data_ref, *refs):
    back = jnp.concatenate([ref[...] for ref in refs[:-1]], axis=0)
    total = data_ref[...].astype(jnp.float32) + dot(place_ref[...], back, ((0,), (0,)))
    refs[-1][...] = total.astype(jnp.bfloat16)


def join_rows(block_refs, out_ref):
    cap = block_refs[0].shape[0]
    for index, block_ref in enumerate(block_refs):
        out_ref[index * cap : (index + 1) * cap] = block_ref[...]


def split_rows(left_ref, right_ref, dims, outs):
    cap = outs[0].shape[0]
    each = max(1, ROWS // cap)
    for first in range(0, len(outs), each):
        result = dot(left_ref[first * cap : (first + each) * cap], right_ref[...], dims).astype(jnp.bfloat16)
        for index in range(each):
            outs[first + index][...] = result[index * cap : (index + 1) * cap]


def forward_kernel(*refs):
    count = (len(refs) - 6) // 2
    one_ref, two_ref, slot_ref, hidden_ref, upper_ref, silu_ref = refs[count : count + 6]
    wide = two_ref.shape[0]
    join_rows(refs[:count], slot_ref)

    @pl.loop(0, slot_ref.shape[0] // ROWS)
    def _(step):
        here = pl.ds(pl.multiple_of(step * ROWS, ROWS), ROWS)
        proj = dot(slot_ref[here], one_ref[...], ((1,), (0,)))
        gate = proj[:, :wide]
        upper = proj[:, wide:]
        sigma = 1.0 / (1.0 + jnp.exp(-gate))
        silu = gate * sigma
        hidden_ref[here] = (silu * upper).astype(jnp.bfloat16)
        upper_ref[here] = upper * sigma * (1.0 + gate * (1.0 - sigma))
        silu_ref[here] = silu

    split_rows(hidden_ref, two_ref, ((1,), (0,)), refs[count + 6 :])


def grad_proj_kernel(*refs):
    two_ref, upper_ref, silu_ref, slot_ref, out_ref = refs[-5:]
    join_rows(refs[:-5], slot_ref)

    @pl.loop(0, slot_ref.shape[0] // ROWS)
    def _(step):
        here = pl.ds(pl.multiple_of(step * ROWS, ROWS), ROWS)
        grad_hidden = dot(slot_ref[here], two_ref[...], ((1,), (1,)))
        both = jnp.concatenate([grad_hidden * upper_ref[here], grad_hidden * silu_ref[here]], axis=1)
        out_ref[here] = both.astype(jnp.bfloat16)


def grad_branch_kernel(grad_ref, one_ref, *outs):
    split_rows(grad_ref, one_ref, ((1,), (1,)), outs)


def weight_kernel(number_ref, x_ref, dy_ref, grad_ref, hidden_ref, *refs):
    out_ref = refs[-1]
    wide, half = grad_ref.shape[1], hidden_ref.shape[1]
    up = dot(x_ref[...], grad_ref[...], ((0,), (0,)))
    down = dot(dy_ref[...], hidden_ref[...], ((0,), (0,)))
    for ref in refs[:-1]:
        up = up + ref[:, :wide].astype(jnp.float32)
        down = down + ref[:, wide : wide + half].astype(jnp.float32)
    out_ref[:, :wide] = up.astype(jnp.bfloat16)
    out_ref[:, wide : wide + half] = down.astype(jnp.bfloat16)


def weight_end_kernel(number_ref, x_ref, dy_ref, grad_ref, hidden_ref, *refs):
    up_ref, down_ref = refs[-2:]
    share, wide = up_ref.shape
    up = dot(x_ref[...], grad_ref[...], ((0,), (0,)))
    down = dot(hidden_ref[...], dy_ref[...], ((0,), (0,)))
    row = lax.broadcasted_iota(jnp.int32, (share, share), 0)
    unit = (row == lax.broadcasted_iota(jnp.int32, (share, share), 1)).astype(jnp.bfloat16)
    for ref in refs[:-2]:
        up = up + ref[:, :wide].astype(jnp.float32)
        down = down + dot(ref[:, wide : wide + down.shape[0]], unit, ((0,), (0,)))
    up_ref[...] = up
    down_ref[...] = down


def route_and_place(rel, data, experts, cap):
    rows, width = data.shape
    slots = experts * cap
    step = width // 4
    return pl.pallas_call(
        lambda *refs: route_kernel(experts, cap, *refs),
        grid=(width // step,),
        in_specs=[whole(rel), pl.BlockSpec((rows, step), lambda i: (0, i))],
        out_specs=[pl.BlockSpec((slots, rows), lambda i: (0, 0))]
        + [pl.BlockSpec((cap, step), lambda i: (0, i))] * experts,
        out_shape=[like((slots, rows))] + [like((cap, width))] * experts,
        compiler_params=params(8),
        cost_estimate=SMALL,
        name="route_and_place",
    )(rel, data)


def place(placing, data, experts, cap):
    rows, width = data.shape
    step = width // 4
    return pl.pallas_call(
        lambda *refs: place_kernel(cap, *refs),
        grid=(width // step,),
        in_specs=[whole(placing), pl.BlockSpec((rows, step), lambda i: (0, i))],
        out_specs=[pl.BlockSpec((cap, step), lambda i: (0, i))] * experts,
        out_shape=[like((cap, width))] * experts,
        compiler_params=params(8),
        cost_estimate=SMALL,
        name="place",
    )(placing, data)


def combine(placing, data, blocks):
    rows, width = data.shape
    cap = blocks[0].shape[0]
    step = width // 4
    return pl.pallas_call(
        combine_kernel,
        grid=(width // step,),
        in_specs=[whole(placing), pl.BlockSpec((rows, step), lambda i: (0, i))]
        + [pl.BlockSpec((cap, step), lambda i: (0, i))] * len(blocks),
        out_specs=pl.BlockSpec((rows, step), lambda i: (0, i)),
        out_shape=like((rows, width)),
        compiler_params=params(8),
        cost_estimate=SMALL,
        name="combine",
    )(placing, data, *blocks)


def call(kernel, name, mebibytes, outs, *arrays):
    return pl.pallas_call(
        kernel,
        grid=(1,),
        in_specs=[whole(array) for array in arrays],
        out_specs=[whole(out) for out in outs],
        out_shape=outs,
        compiler_params=params(mebibytes),
        cost_estimate=SMALL,
        name=name,
    )(*arrays)


def weight_part(number, groups, slot_x, slot_dy, grad_proj, hidden, received, end):
    slots, width = slot_x.shape
    share = width // groups
    wide = hidden.shape[1]
    outs = [like((share, pl.cdiv(3 * wide, 128) * 128))]
    if end:
        outs = [like((share, 2 * wide), jnp.float32), like((wide, share), jnp.float32)]
    column = pl.BlockSpec((slots, share), lambda i, number_ref: (0, number_ref[0]), pipeline_mode=pl.Buffered(1))
    return pl.pallas_call(
        weight_end_kernel if end else weight_kernel,
        grid_spec=pltpu.PrefetchScalarGridSpec(
            num_scalar_prefetch=1,
            grid=(1,),
            in_specs=[column, column, whole(grad_proj), whole(hidden)] + [whole(piece) for piece in received],
            out_specs=[whole(out) for out in outs],
        ),
        out_shape=outs,
        compiler_params=params(20),
        cost_estimate=SMALL,
        name="weight_part",
    )(number, slot_x, slot_dy, grad_proj, hidden, *received)


def after(value, *earlier):
    if not earlier:
        return value
    return lax.optimization_barrier((value, *earlier))[0]


class Lane:
    def __init__(self, window):
        self.window = window
        self.done = []

    def send(self, value, axis, pairs, *earlier):
        if len(self.done) >= self.window:
            earlier = (self.done[-self.window], *earlier)
        self.done.append(lax.ppermute(after(value, *earlier), axis, pairs))
        return self.done[-1]


def exchange(blocks, far, held={}):
    experts = len(blocks)
    half = experts // 2
    moved = {0: blocks[0]}
    for mask in range(half - 1, -1, -1):
        pairs = [(i, i ^ (mask + half)) for i in range(experts)]
        moved[mask + half] = far.send(blocks[mask + half], "exp", pairs, *held.get(mask, ()))
        if mask:
            pairs = [(i, i ^ mask) for i in range(experts)]
            moved[mask] = lax.ppermute(after(blocks[mask], far.done[-1]), "exp", pairs)
    return [moved[mask] for mask in range(experts)]


def body(tokens, expert_ids, gate_up_weight, down_weight, grad_out):
    rows, width = tokens.shape
    experts = lax.axis_size("exp")
    groups = lax.axis_size("grp")
    cap = 2 * rows // experts
    weight_one = gate_up_weight[0]
    weight_two = down_weight[0]
    wide = weight_two.shape[0]
    slots = experts * cap
    block = like((cap, width))
    far = Lane(3)
    rel = expert_ids.reshape(1, rows) ^ lax.axis_index("exp").astype(jnp.int32)
    group = lax.axis_index("grp").astype(jnp.int32)

    placing, *sent_x = route_and_place(rel, tokens, experts, cap)
    sent_dy = place(placing, grad_out, experts, cap)
    blocks_x = exchange(sent_x, far)
    outs = [like((slots, width)), like((slots, wide))] + [like((slots, wide), jnp.float32)] * 2 + [block] * experts
    slot_x, hidden, upper, silu, *branch = call(forward_kernel, "forward", 26, outs, *blocks_x, weight_one, weight_two)

    blocks_dy = exchange(sent_dy, far, {0: (hidden,)})
    outs = [like((slots, width)), like((slots, 2 * wide))]
    slot_dy, grad_proj = call(grad_proj_kernel, "grad_proj", 16, outs, *blocks_dy, weight_two, upper, silu)
    grad_branch = call(grad_branch_kernel, "grad_branch", 14, [block] * experts, grad_proj, weight_one)

    first_out = len(far.done)
    back_out = exchange(branch, far, {0: (grad_proj,)})
    lanes = {}
    far_out = far.done[first_out:]
    near_out = back_out[experts // 2 - 1 : 0 : -1]
    gates = iter([far_out[:2], [far_out[2], near_out[0], grad_branch[0]], [far_out[3], near_out[1]]])

    def weight_sum(q, bit):
        received = []
        low = bit // 2
        while low:
            pairs = [(i, i ^ low) for i in range(groups)]
            (piece,) = weight_sum(q | low, low)
            received.append(lanes.setdefault(low, Lane(1)).send(piece, "grp", pairs))
            low //= 2
        grad = after(grad_proj, *([] if bit == groups else next(gates, [])))
        return weight_part((group ^ q)[None], groups, slot_x, slot_dy, grad, hidden, received, bit == groups)

    grad_gate_up, grad_down = weight_sum(0, groups)
    mixed_out = combine(placing, tokens, back_out)
    back_grad = exchange(grad_branch, far, {0: (mixed_out,)})
    back_grad[0] = after(back_grad[0], grad_gate_up)
    grad_tokens = combine(placing, grad_out, back_grad)
    return (mixed_out, grad_tokens, grad_gate_up[None], grad_down[None])


def solution(mesh):
    in_specs = (
        P(("grp", "exp"), None),
        P(("grp", "exp"), None),
        P("exp", None, None),
        P("exp", None, None),
        P(("grp", "exp"), None),
    )
    out_specs = (
        P(("grp", "exp"), None),
        P(("grp", "exp"), None),
        P("exp", "grp", None),
        P("exp", None, "grp"),
    )
    return jax.shard_map(body, mesh=mesh, in_specs=in_specs, out_specs=out_specs, check_vma=False)
```

time: 237 us -> 239 us (level)
  waiting for transfers between devices: 78.2 us -> 58.4 us
  starting transfers between devices: 86.2 us -> 105 us
  local copies, waits for them, and re-layouts: 23.7 us -> 34.8 us
  Pallas kernels: 47.5 us -> 38.4 us
    ppermute x12, starting transfers between devices: 16.7 us -> 49.4 us  [exchange(): moved[mask] = lax.ppermute(after(blocks[mask], far.done[-1]), 'exp', pairs)]
    ppermute x22 -> x19, starting transfers between devices: 69.5 us -> 55.2 us  [send(): self.done.append(lax.ppermute(after(value, *earlier), axis, pairs))]
    ppermute x22 -> x19, waiting for transfers between devices: 56.4 us -> 44.9 us  [send(): self.done.append(lax.ppermute(after(value, *earlier), axis, pairs))]
    unnamed x77 -> x114, local copies, waits for them, and re-layouts: 23.7 us -> 34.8 us
    pallas_call x10, Pallas kernels: 45.4 us -> 36.6 us  [the longest x4 14.5 us: weight_part(): pl.pallas_call(weight_end_kernel if end else weight_kernel, grid_spec=plt...]
    ppermute x12, waiting for transfers between devices: 21.8 us -> 13.5 us  [exchange(): moved[mask] = lax.ppermute(after(blocks[mask], far.done[-1]), 'exp', pairs)]
  transfers between devices with their start and end apart: 34 -> 31, of which waited for: 18 -> 11; matrix products, arithmetic and copies ran while one was open for 0% -> 0% of each run, Pallas kernels for 15% -> 13%
where the time goes in v3:
time: 239 us; the launch traced here: 238 us
  starting transfers between devices  105 us (44%)
  waiting for transfers between devices  58.4 us (24%)
  Pallas kernels  38.4 us (16%)
  local copies, waits for them, and re-layouts  34.8 us (15%)
    ppermute x19, starting transfers between devices, send(): self.done.append(lax.ppermute(after(value, *earlier), axis, pairs))  55.2 us
    ppermute x12, starting transfers between devices, exchange(): moved[mask] = lax.ppermute(after(blocks[mask], far.done[-1]), 'exp', pairs)  49.4 us
    ppermute x19, waiting for transfers between devices, send(): self.done.append(lax.ppermute(after(value, *earlier), axis, pairs))  44.9 us
    unnamed x114, local copies, waits for them, and re-layouts  34.8 us
    pallas_call x4, Pallas kernels, weight_part(): pl.pallas_call(weight_end_kernel if end else weight_kernel, grid_spec=plt...  14.5 us
    ppermute x12, waiting for transfers between devices, exchange(): moved[mask] = lax.ppermute(after(blocks[mask], far.done[-1]), 'exp', pairs)  13.5 us
    pallas_call x3, Pallas kernels, call(): pl.pallas_call(kernel, grid=(1,), in_specs=[whole(array) for array in arr...  12.9 us
    pallas_call x2, Pallas kernels, combine(): pl.pallas_call(combine_kernel, grid=(width // step,), in_specs=[whole(pla...  6.86 us
  transfers between devices with their start and end apart: 31, of which 11 were waited for; matrix products, arithmetic and copies ran while one was open for 0% of the time, Pallas kernels for 13%

profile of v3, /device:TPU:0, one launch (start us, length us, event | category | flops | bytes accessed | tf_op | source)
XLA Modules:
  0.0 238.0 jit_solution(9964823801027562385)
XLA Ops:
  1.3 1.2 copy-done.13
  2.5 1.8 route_and_place.1
  4.4 6.1 %collective-permute-start.4 = (bf16[64,2048]{1,0:T(8,128)(2,1)S(1)}, bf16[64,2048]{1,0:T(8,128)(2,1)S(1)}, u32[]{:S(2)}, u32[]{:S(2)}) collective-permute-start(bf16[64,2048]{1,0:T(8,128)(2,1)S(1)} %get-tuple-element.84), channel_id=1, source_target_pairs={{0,7},{1,6},{2,5},{3,4},{4,3},{5,2},{6,1},{7,0},{8,15},{9,14},{10,... | collective-permute-start | bytes 786440 | tf_op jit(solution)/shard_map/ppermute | solution.py:234
  10.4 1.9 collective-permute-start.2
  12.3 5.4 %collective-permute-done.4.refs_7_ = bf16[64,2048]{1,0:T(8,128)(2,1)S(1)} collective-permute-done((bf16[64,2048]{1,0:T(8,128)(2,1)S(1)}, bf16[64,2048]{1,0:T(8,128)(2,1)S(1)}, u32[]{:S(2)}, u32[]{:S(2)}) %collective-permute-start.4) | collective-permute-done | bytes 262176 | tf_op jit(solution)/shard_map/ppermute | solution.py:234
  17.7 17.7 %collective-permute-start.6 = (bf16[64,2048]{1,0:T(8,128)(2,1)S(1)}, bf16[64,2048]{1,0:T(8,128)(2,1)S(1)}, u32[]{:S(2)}, u32[]{:S(2)}) collective-permute-start(bf16[64,2048]{1,0:T(8,128)(2,1)S(1)} %get-tuple-element.87), channel_id=1, source_target_pairs={{0,4},{1,5},{2,6},{3,7},{4,0},{5,1},{6,2},{7,3},{8,12},{9,13},{10,... | collective-permute-start | bytes 786440 | tf_op jit(solution)/shard_map/ppermute | solution.py:234
  35.4 1.2 copy-done.11
  36.6 2.3 place.1
  39.7 5.3 %collective-permute-done.refs_5_ = bf16[64,2048]{1,0:T(8,128)(2,1)S(1)} collective-permute-done((bf16[64,2048]{1,0:T(8,128)(2,1)S(1)}, bf16[64,2048]{1,0:T(8,128)(2,1)S(1)}, u32[]{:S(2)}, u32[]{:S(2)}) %collective-permute-start) | collective-permute-done | bytes 262176 | tf_op jit(solution)/shard_map/ppermute | solution.py:234
  44.9 2.6 %collective-permute-start.14 = (bf16[64,2048]{1,0:T(8,128)(2,1)S(1)}, bf16[64,2048]{1,0:T(8,128)(2,1)S(1)}, u32[]{:S(2)}, u32[]{:S(2)}) collective-permute-start(bf16[64,2048]{1,0:T(8,128)(2,1)S(1)} %get-tuple-element.107), channel_id=1, source_target_pairs={{0,6},{1,7},{2,4},{3,5},{4,2},{5,3},{6,0},{7,1},{8,14},{9,15},{10,... | collective-permute-start | bytes 786440 | tf_op jit(solution)/shard_map/ppermute | solution.py:234
  47.6 2.1 collective-permute-start.7
  50.2 15.3 %collective-permute-start.3 = (bf16[64,2048]{1,0:T(8,128)(2,1)S(1)}, bf16[64,2048]{1,0:T(8,128)(2,1)S(1)}, u32[]{:S(2)}, u32[]{:S(2)}) collective-permute-start(bf16[64,2048]{1,0:T(8,128)(2,1)S(1)} %get-tuple-element.82), channel_id=1, source_target_pairs={{0,2},{1,3},{2,0},{3,1},{4,6},{5,7},{6,4},{7,5},{8,10},{9,11},{10,... | collective-permute-start | bytes 786440 | tf_op jit(solution)/shard_map/ppermute | solution.py:247
  65.6 1.8 collective-permute-done.6.refs_4_
  68.1 7.4 %collective-permute-start.11 = (bf16[64,2048]{1,0:T(8,128)(2,1)S(1)}, bf16[64,2048]{1,0:T(8,128)(2,1)S(1)}, u32[]{:S(2)}, u32[]{:S(2)}) collective-permute-start(bf16[64,2048]{1,0:T(8,128)(2,1)S(1)} %get-tuple-element.101), channel_id=1, source_target_pairs={{0,5},{1,4},{2,7},{3,6},{4,1},{5,0},{6,3},{7,2},{8,13},{9,12},{10,... | collective-permute-start | bytes 786440 | tf_op jit(solution)/shard_map/ppermute | solution.py:234
  76.2 12.3 %collective-permute-start.18 = (bf16[64,2048]{1,0:T(8,128)(2,1)S(1)}, bf16[64,2048]{1,0:T(8,128)(2,1)S(1)}, u32[]{:S(2)}, u32[]{:S(2)}) collective-permute-start(bf16[64,2048]{1,0:T(8,128)(2,1)S(1)} %get-tuple-element.115), channel_id=1, source_target_pairs={{0,2},{1,3},{2,0},{3,1},{4,6},{5,7},{6,4},{7,5},{8,10},{9,11},{10,... | collective-permute-start | bytes 786440 | tf_op jit(solution)/shard_map/ppermute | solution.py:247
  88.4 0.8 collective-permute-start.19
  89.3 2.6 %copy-done.3 = bf16[1,2048,1408]{2,1,0:T(8,128)(2,1)S(1)} copy-done((bf16[1,2048,1408]{2,1,0:T(8,128)(2,1)S(1)}, bf16[1,2048,1408]{2,1,0:T(8,128)(2,1)}, u32[]{:S(2)}) %copy-start.3) | copy-done | bytes 5767192
  91.9 1.8 copy-done.9
  93.7 7.0 %forward.1 = (bf16[512,2048]{1,0:T(8,128)(2,1)S(1)}, bf16[512,704]{1,0:T(8,128)(2,1)S(1)}, f32[512,704]{1,0:T(8,128)S(1)}, f32[512,704]{1,0:T(8,128)S(1)}, bf16[...) custom-call(bf16[64,2048]{1,0:T(8,128)(2,1)S(1)} %get-tuple-element., ...), custom_call_target="tpu_custom_call" | custom-call | flops 1024 | bytes 1024 | tf_op jit(solution)/shard_map/forward/pallas_call | solution.py:185
  100.7 0.9 copy-done.5
  101.6 1.1 copy-done.17
  102.7 1.2 copy-done.19
  105.3 3.2 %collective-permute-start.8 = (bf16[64,2048]{1,0:T(8,128)(2,1)S(1)}, bf16[64,2048]{1,0:T(8,128)(2,1)S(1)}, u32[]{:S(2)}, u32[]{:S(2)}) collective-permute-start(bf16[64,2048]{1,0:T(8,128)(2,1)S(1)} %get-tuple-element.95), channel_id=1, source_target_pairs={{0,4},{1,5},{2,6},{3,7},{4,0},{5,1},{6,2},{7,3},{8,12},{9,13},{10,... | collective-permute-start | bytes 786440 | tf_op jit(solution)/shard_map/ppermute | solution.py:234
  108.5 1.3 collective-permute-start.15
  110.5 1.3 collective-permute-start.17
  112.6 2.7 %collective-permute-start.12 = (bf16[64,2048]{1,0:T(8,128)(2,1)}, bf16[64,2048]{1,0:T(8,128)(2,1)}, u32[]{:S(2)}, u32[]{:S(2)}) collective-permute-start(bf16[64,2048]{1,0:T(8,128)(2,1)} %get-tuple-element.102), channel_id=1, source_target_pairs={{0,6},{1,7},{2,4},{3,5},{4,2},{5,3},{6,0},{7,1},{8,14},{9,15},{10,... | collective-permute-start | bytes 786440 | tf_op jit(solution)/shard_map/ppermute | solution.py:234
  115.9 14.6 %collective-permute-done.8.refs_4_ = bf16[64,2048]{1,0:T(8,128)(2,1)S(1)} collective-permute-done((bf16[64,2048]{1,0:T(8,128)(2,1)S(1)}, bf16[64,2048]{1,0:T(8,128)(2,1)S(1)}, u32[]{:S(2)}, u32[]{:S(2)}) %collective-permute-start.8) | collective-permute-done | bytes 262176 | tf_op jit(solution)/shard_map/ppermute | solution.py:234
  132.0 1.8 copy-done.10
  133.8 1.4 copy-done.18
  135.2 1.4 copy-done.20
  136.6 0.9 copy-done.24
  137.6 0.9 copy-done.28
  138.5 0.9 copy-done.30
  139.5 0.9 copy-done.32
  140.4 0.9 copy-done.34
  141.4 0.9 copy-done.36
  142.3 0.9 copy-done.38
  143.3 0.9 copy-done.40
  144.2 2.5 %grad_proj.1 = (bf16[512,2048]{1,0:T(8,128)(2,1)S(1)}, bf16[512,1408]{1,0:T(8,128)(2,1)S(1)}) custom-call(bf16[64,2048]{1,0:T(8,128)(2,1)S(1)} %copy-done.24, bf16[64,2048]{1,0:T(8,128)(2,1)S(1)} %copy-done.40, bf16[64,2048]{1,0:T(8,128)(2,1)S(1)} %copy-done.34, bf16[64,2048]{1,0:T(8,128)(2,1)S(1)} %copy-done.36, bf16[64,2048]{1,0:T(8,128)(2,1)S(1)} %copy-done.38, ...), custom_call_target="tpu_custom_call" | custom-call | flops 1024 | bytes 1024 | tf_op jit(solution)/shard_map/grad_proj/pallas_call | solution.py:185
  146.8 2.9 %weight_part.4 = bf16[512,2176]{1,0:T(8,128)(2,1)} custom-call(s32[1]{0:T(128)} %bitcast.5.number_ref, bf16[512,2048]{1,0:T(8,128)(2,1)S(1)} %get-tuple-element.123.x_ref, bf16[512,2048]{1,0:T(8,128)(2,1)S(1)} %get-tuple-element.124.dy_ref, bf16[512,1408]{1,0:T(8,128)(2,1)S(1)} %get-tuple-element.127.grad_ref, bf16[512,704]{1,0:T(8,128)(2,1)S(1)} %copy-done.6), custom_call_target="tpu_custom_call" | custom-call | flops 1024 | bytes 1024 | tf_op jit(solution)/shard_map/weight_part/pallas_call | solution.py:205
  149.6 3.7 %collective-permute-start.16 = (bf16[64,2048]{1,0:T(8,128)(2,1)}, bf16[64,2048]{1,0:T(8,128)(2,1)}, u32[]{:S(2)}, u32[]{:S(2)}) collective-permute-start(bf16[64,2048]{1,0:T(8,128)(2,1)} %get-tuple-element.109), channel_id=1, source_target_pairs={{0,3},{1,2},{2,1},{3,0},{4,7},{5,6},{6,5},{7,4},{8,11},{9,10},{10,... | collective-permute-start | bytes 786440 | tf_op jit(solution)/shard_map/ppermute | solution.py:247
  153.3 2.2 collective-permute-start.13
  155.5 2.6 %copy-done.4 = bf16[1,2048,1408]{2,1,0:T(8,128)(2,1)S(1)} copy-done((bf16[1,2048,1408]{2,1,0:T(8,128)(2,1)S(1)}, bf16[1,2048,1408]{2,1,0:T(8,128)(2,1)}, u32[]{:S(2)}) %copy-start.4) | copy-done | bytes 5767192
  158.1 3.4 %grad_branch.1 = (bf16[64,2048]{1,0:T(8,128)(2,1)S(1)}, bf16[64,2048]{1,0:T(8,128)(2,1)S(1)}, bf16[64,2048]{1,0:T(8,128)(2,1)S(1)}, bf16[64,2048]{1,0:T(8,128)(2...) custom-call(bf16[512,1408]{1,0:T(8,128)(2,1)S(1)} %get-tuple-element, ...), custom_call_target="tpu_custom_call" | custom-call | flops 1024 | bytes 1024 | tf_op jit(solution)/shard_map/grad_branch/pallas_call | solution.py:185
  161.6 3.7 %collective-permute-done.9.refs_5_ = bf16[64,2048]{1,0:T(8,128)(2,1)} collective-permute-done((bf16[64,2048]{1,0:T(8,128)(2,1)}, bf16[64,2048]{1,0:T(8,128)(2,1)}, u32[]{:S(2)}, u32[]{:S(2)}) %collective-permute-start.9) | collective-permute-done | bytes 262176 | tf_op jit(solution)/shard_map/ppermute | solution.py:234
  165.3 1.2 collective-permute-done.16.refs_3_
  166.5 4.5 %weight_part.5 = bf16[512,2176]{1,0:T(8,128)(2,1)} custom-call(s32[1]{0:T(128)} %bitcast.4.number_ref, bf16[512,2048]{1,0:T(8,128)(2,1)S(1)} %get-tuple-element.123.x_ref, bf16[512,2048]{1,0:T(8,128)(2,1)S(1)} %copy-done.1, bf16[512,1408]{1,0:T(8,128)(2,1)S(1)} %get-tuple-element.127.grad_ref, bf16[512,704]{1,0:T(8,128)(2,1)S(1)} %copy-done.7, ...), custom_call_target="tpu_custom_call" | custom-call | flops 1024 | bytes 1024 | tf_op jit(solution)/shard_map/weight_part/pallas_call | solution.py:205
  171.1 1.7 collective-permute-start.22
  172.8 3.4 %collective-permute-done.20.refs_4_ = bf16[64,2048]{1,0:T(8,128)(2,1)} collective-permute-done((bf16[64,2048]{1,0:T(8,128)(2,1)}, bf16[64,2048]{1,0:T(8,128)(2,1)}, u32[]{:S(2)}, u32[]{:S(2)}) %collective-permute-start.20) | collective-permute-done | bytes 262176 | tf_op jit(solution)/shard_map/ppermute | solution.py:234
  176.2 1.6 copy-done.2
  177.8 1.1 copy-done.8
  179.0 1.5 weight_part.6
  180.6 1.6 collective-permute-start.10
  182.2 1.6 collective-permute-start.28
  183.8 2.1 collective-permute-start.26
  185.9 9.0 %collective-permute-done.10.refs_1_ = bf16[64,2048]{1,0:T(8,128)(2,1)S(1)} collective-permute-done((bf16[64,2048]{1,0:T(8,128)(2,1)S(1)}, bf16[64,2048]{1,0:T(8,128)(2,1)S(1)}, u32[]{:S(2)}, u32[]{:S(2)}) %collective-permute-start.10) | collective-permute-done | bytes 262176 | tf_op jit(solution)/shard_map/ppermute | solution.py:247
  195.0 4.2 %combine.2 = bf16[256,2048]{1,0:T(8,128)(2,1)} custom-call(bf16[512,256]{1,0:T(8,128)(2,1)S(1)} %copy-done.16, bf16[256,2048]{1,0:T(8,128)(2,1)S(1)} %copy-done.14, bf16[64,2048]{1,0:T(8,128)(2,1)S(1)} %copy-done.22, bf16[64,2048]{1,0:T(8,128)(2,1)S(1)} %collective-permute-done.10.refs_1_, bf16[64,2048]{1,0:T(8,128)(2,1)} %collective-permute-done.13.refs_2_, ...), custom_call_target="tpu_custom_call" | custom-call | flops 1024 | bytes 1024 | tf_op jit(solution)/shard_map/combine/pallas_call | solution.py:171
  199.2 10.3 %collective-permute-start.29 = (bf16[64,2048]{1,0:T(8,128)(2,1)S(1)}, bf16[64,2048]{1,0:T(8,128)(2,1)S(1)}, u32[]{:S(2)}, u32[]{:S(2)}) collective-permute-start(bf16[64,2048]{1,0:T(8,128)(2,1)S(1)} %copy-done.50), channel_id=1, source_target_pairs={{0,3},{1,2},{2,1},{3,0},{4,7},{5,6},{6,5},{7,4},{8,11},{9,10},{10,... | collective-permute-start | bytes 786440 | tf_op jit(solution)/shard_map/ppermute | solution.py:247
  209.5 4.8 %collective-permute-start.30 = (bf16[64,2048]{1,0:T(8,128)(2,1)S(1)}, bf16[64,2048]{1,0:T(8,128)(2,1)S(1)}, u32[]{:S(2)}, u32[]{:S(2)}) collective-permute-start(bf16[64,2048]{1,0:T(8,128)(2,1)S(1)} %copy-done.48), channel_id=1, source_target_pairs={{0,4},{1,5},{2,6},{3,7},{4,0},{5,1},{6,2},{7,3},{8,12},{9,13},{10,... | collective-permute-start | bytes 786440 | tf_op jit(solution)/shard_map/ppermute | solution.py:234
  214.3 10.7 %collective-permute-done.24.refs_5_ = bf16[64,2048]{1,0:T(8,128)(2,1)S(1)} collective-permute-done((bf16[64,2048]{1,0:T(8,128)(2,1)S(1)}, bf16[64,2048]{1,0:T(8,128)(2,1)S(1)}, u32[]{:S(2)}, u32[]{:S(2)}) %collective-permute-start.24) | collective-permute-done | bytes 262176 | tf_op jit(solution)/shard_map/ppermute | solution.py:234
  225.1 1.4 collective-permute-start.25
  226.5 5.7 %weight_part.7 = (f32[512,1408]{1,0:T(8,128)}, f32[704,512]{1,0:T(8,128)}) custom-call(s32[1]{0:T(128)} %bitcast.3.number_ref, bf16[512,2048]{1,0:T(8,128)(2,1)S(1)} %get-tuple-element.123.x_ref, bf16[512,2048]{1,0:T(8,128)(2,1)S(1)} %copy-done.2, bf16[512,1408]{1,0:T(8,128)(2,1)S(1)} %get-tuple-element.127.grad_ref, bf16[512,704]{1,0:T(8,128)(2,1)S(1)} %copy-done.8, ...), custom_call_target="tpu_custom_call" | custom-call | flops 1024 | bytes 1024 | tf_op jit(solution)/shard_map/weight_part/pallas_call | solution.py:205
  232.2 3.2 %collective-permute-done.27.refs_2_ = bf16[64,2048]{1,0:T(8,128)(2,1)S(1)} collective-permute-done((bf16[64,2048]{1,0:T(8,128)(2,1)S(1)}, bf16[64,2048]{1,0:T(8,128)(2,1)S(1)}, u32[]{:S(2)}, u32[]{:S(2)}) %collective-permute-start.27) | collective-permute-done | bytes 262176 | tf_op jit(solution)/shard_map/ppermute | solution.py:247
  235.4 2.6 %combine.3 = bf16[256,2048]{1,0:T(8,128)(2,1)} custom-call(bf16[512,256]{1,0:T(8,128)(2,1)S(1)} %copy-done.16, bf16[256,2048]{1,0:T(8,128)(2,1)S(1)} %copy-done.12, bf16[64,2048]{1,0:T(8,128)(2,1)S(1)} %copy-done.26, bf16[64,2048]{1,0:T(8,128)(2,1)S(1)} %collective-permute-done.25.refs_1_, bf16[64,2048]{1,0:T(8,128)(2,1)S(1)} %collective-permute-done.27.refs_2_, ...), custom_call_target="tpu_custom_call" | custom-call | flops 1024 | bytes 1024 | tf_op jit(solution)/shard_map/combine/pallas_call | solution.py:171
  (124 shorter events, 8.7 us)
Async XLA Ops:
  4.3 84.9 %copy-start.15 = (bf16[512,256]{1,0:T(8,128)(2,1)}, bf16[512,256]{1,0:T(8,128)(2,1)S(1)}, u32[]{:S(2)}) copy-start(bf16[512,256]{1,0:T(8,128)(2,1)S(1)} %get-tuple-element.75.refs_0_.place_ref) | copy-start | bytes 786436
  4.4 13.3 %collective-permute-start.4 = (bf16[64,2048]{1,0:T(8,128)(2,1)S(1)}, bf16[64,2048]{1,0:T(8,128)(2,1)S(1)}, u32[]{:S(2)}, u32[]{:S(2)}) collective-permute-start(bf16[64,2048]{1,0:T(8,128)(2,1)S(1)} %get-tuple-element.84), channel_id=1, source_target_pairs={{0,7},{1,6},{2,5},{3,4},{4,3},{5,2},{6,1},{7,0},{8,15},{9,14},{10,... | collective-permute-start | bytes 786440 | tf_op jit(solution)/shard_map/ppermute | solution.py:234
  10.4 34.5 %collective-permute-start = (bf16[64,2048]{1,0:T(8,128)(2,1)S(1)}, bf16[64,2048]{1,0:T(8,128)(2,1)S(1)}, u32[]{:S(2)}, u32[]{:S(2)}) collective-permute-start(bf16[64,2048]{1,0:T(8,128)(2,1)S(1)} %get-tuple-element.78), channel_id=1, source_target_pairs={{0,5},{1,4},{2,7},{3,6},{4,1},{5,0},{6,3},{7,2},{8,13},{9,12},{10,... | collective-permute-start | bytes 786440 | tf_op jit(solution)/shard_map/ppermute | solution.py:234
  10.4 37.1 %collective-permute-start.2 = (bf16[64,2048]{1,0:T(8,128)(2,1)S(1)}, bf16[64,2048]{1,0:T(8,128)(2,1)S(1)}, u32[]{:S(2)}, u32[]{:S(2)}) collective-permute-start(bf16[64,2048]{1,0:T(8,128)(2,1)S(1)} %get-tuple-element.81), channel_id=1, source_target_pairs={{0,6},{1,7},{2,4},{3,5},{4,2},{5,3},{6,0},{7,1},{8,14},{9,15},{10,... | collective-permute-start | bytes 786440 | tf_op jit(solution)/shard_map/ppermute | solution.py:234
  17.7 49.7 %collective-permute-start.6 = (bf16[64,2048]{1,0:T(8,128)(2,1)S(1)}, bf16[64,2048]{1,0:T(8,128)(2,1)S(1)}, u32[]{:S(2)}, u32[]{:S(2)}) collective-permute-start(bf16[64,2048]{1,0:T(8,128)(2,1)S(1)} %get-tuple-element.87), channel_id=1, source_target_pairs={{0,4},{1,5},{2,6},{3,7},{4,0},{5,1},{6,2},{7,3},{8,12},{9,13},{10,... | collective-permute-start | bytes 786440 | tf_op jit(solution)/shard_map/ppermute | solution.py:234
  44.9 22.5 %collective-permute-start.14 = (bf16[64,2048]{1,0:T(8,128)(2,1)S(1)}, bf16[64,2048]{1,0:T(8,128)(2,1)S(1)}, u32[]{:S(2)}, u32[]{:S(2)}) collective-permute-start(bf16[64,2048]{1,0:T(8,128)(2,1)S(1)} %get-tuple-element.107), channel_id=1, source_target_pairs={{0,6},{1,7},{2,4},{3,5},{4,2},{5,3},{6,0},{7,1},{8,14},{9,15},{10,... | collective-permute-start | bytes 786440 | tf_op jit(solution)/shard_map/ppermute | solution.py:234
  47.6 27.9 %collective-permute-start.7 = (bf16[64,2048]{1,0:T(8,128)(2,1)S(1)}, bf16[64,2048]{1,0:T(8,128)(2,1)S(1)}, u32[]{:S(2)}, u32[]{:S(2)}) collective-permute-start(bf16[64,2048]{1,0:T(8,128)(2,1)S(1)} %get-tuple-element.93), channel_id=1, source_target_pairs={{0,7},{1,6},{2,5},{3,4},{4,3},{5,2},{6,1},{7,0},{8,15},{9,14},{10,... | collective-permute-start | bytes 786440 | tf_op jit(solution)/shard_map/ppermute | solution.py:234
  49.6 38.8 %collective-permute-start.1 = (bf16[64,2048]{1,0:T(8,128)(2,1)S(1)}, bf16[64,2048]{1,0:T(8,128)(2,1)S(1)}, u32[]{:S(2)}, u32[]{:S(2)}) collective-permute-start(bf16[64,2048]{1,0:T(8,128)(2,1)S(1)} %get-tuple-element.79), channel_id=1, source_target_pairs={{0,1},{1,0},{2,3},{3,2},{4,5},{5,4},{6,7},{7,6},{8,9},{9,8},{10,11... | collective-permute-start | bytes 786440 | tf_op jit(solution)/shard_map/ppermute | solution.py:247
  50.2 39.0 %collective-permute-start.3 = (bf16[64,2048]{1,0:T(8,128)(2,1)S(1)}, bf16[64,2048]{1,0:T(8,128)(2,1)S(1)}, u32[]{:S(2)}, u32[]{:S(2)}) collective-permute-start(bf16[64,2048]{1,0:T(8,128)(2,1)S(1)} %get-tuple-element.82), channel_id=1, source_target_pairs={{0,2},{1,3},{2,0},{3,1},{4,6},{5,7},{6,4},{7,5},{8,10},{9,11},{10,... | collective-permute-start | bytes 786440 | tf_op jit(solution)/shard_map/ppermute | solution.py:247
  67.4 21.8 %collective-permute-start.5 = (bf16[64,2048]{1,0:T(8,128)(2,1)S(1)}, bf16[64,2048]{1,0:T(8,128)(2,1)S(1)}, u32[]{:S(2)}, u32[]{:S(2)}) collective-permute-start(bf16[64,2048]{1,0:T(8,128)(2,1)S(1)} %get-tuple-element.85), channel_id=1, source_target_pairs={{0,3},{1,2},{2,1},{3,0},{4,7},{5,6},{6,5},{7,4},{8,11},{9,10},{10,... | collective-permute-start | bytes 786440 | tf_op jit(solution)/shard_map/ppermute | solution.py:247
  68.1 41.7 %collective-permute-start.11 = (bf16[64,2048]{1,0:T(8,128)(2,1)S(1)}, bf16[64,2048]{1,0:T(8,128)(2,1)S(1)}, u32[]{:S(2)}, u32[]{:S(2)}) collective-permute-start(bf16[64,2048]{1,0:T(8,128)(2,1)S(1)} %get-tuple-element.101), channel_id=1, source_target_pairs={{0,5},{1,4},{2,7},{3,6},{4,1},{5,0},{6,3},{7,2},{8,13},{9,12},{10,... | collective-permute-start | bytes 786440 | tf_op jit(solution)/shard_map/ppermute | solution.py:234
  76.2 35.7 %collective-permute-start.18 = (bf16[64,2048]{1,0:T(8,128)(2,1)S(1)}, bf16[64,2048]{1,0:T(8,128)(2,1)S(1)}, u32[]{:S(2)}, u32[]{:S(2)}) collective-permute-start(bf16[64,2048]{1,0:T(8,128)(2,1)S(1)} %get-tuple-element.115), channel_id=1, source_target_pairs={{0,2},{1,3},{2,0},{3,1},{4,6},{5,7},{6,4},{7,5},{8,10},{9,11},{10,... | collective-permute-start | bytes 786440 | tf_op jit(solution)/shard_map/ppermute | solution.py:247
  88.4 26.8 %collective-permute-start.19 = (bf16[64,2048]{1,0:T(8,128)(2,1)}, bf16[64,2048]{1,0:T(8,128)(2,1)S(1)}, u32[]{:S(2)}, u32[]{:S(2)}) collective-permute-start(bf16[64,2048]{1,0:T(8,128)(2,1)} %get-tuple-element.117), channel_id=1, source_target_pairs={{0,3},{1,2},{2,1},{3,0},{4,7},{5,6},{6,5},{7,4},{8,11},{9,10},{10,... | collective-permute-start | bytes 786440 | tf_op jit(solution)/shard_map/ppermute | solution.py:247
  89.2 2.6 %copy-start.3 = (bf16[1,2048,1408]{2,1,0:T(8,128)(2,1)S(1)}, bf16[1,2048,1408]{2,1,0:T(8,128)(2,1)}, u32[]{:S(2)}) copy-start(bf16[1,2048,1408]{2,1,0:T(8,128)(2,1)} %param.7) | copy-start | bytes 17301508
  91.9 1.8 copy-start.9
  105.3 25.3 %collective-permute-start.8 = (bf16[64,2048]{1,0:T(8,128)(2,1)S(1)}, bf16[64,2048]{1,0:T(8,128)(2,1)S(1)}, u32[]{:S(2)}, u32[]{:S(2)}) collective-permute-start(bf16[64,2048]{1,0:T(8,128)(2,1)S(1)} %get-tuple-element.95), channel_id=1, source_target_pairs={{0,4},{1,5},{2,6},{3,7},{4,0},{5,1},{6,2},{7,3},{8,12},{9,13},{10,... | collective-permute-start | bytes 786440 | tf_op jit(solution)/shard_map/ppermute | solution.py:234
  108.5 38.2 %collective-permute-start.15 = (bf16[64,2048]{1,0:T(8,128)(2,1)}, bf16[64,2048]{1,0:T(8,128)(2,1)}, u32[]{:S(2)}, u32[]{:S(2)}) collective-permute-start(bf16[64,2048]{1,0:T(8,128)(2,1)} %get-tuple-element.108), channel_id=1, source_target_pairs={{0,7},{1,6},{2,5},{3,4},{4,3},{5,2},{6,1},{7,0},{8,15},{9,14},{10,... | collective-permute-start | bytes 786440 | tf_op jit(solution)/shard_map/ppermute | solution.py:234
  110.5 20.8 %collective-permute-start.17 = (bf16[64,2048]{1,0:T(8,128)(2,1)S(1)}, bf16[64,2048]{1,0:T(8,128)(2,1)S(1)}, u32[]{:S(2)}, u32[]{:S(2)}) collective-permute-start(bf16[64,2048]{1,0:T(8,128)(2,1)S(1)} %get-tuple-element.113), channel_id=1, source_target_pairs={{0,1},{1,0},{2,3},{3,2},{4,5},{5,4},{6,7},{7,6},{8,9},{9,8},{10,11... | collective-permute-start | bytes 786440 | tf_op jit(solution)/shard_map/ppermute | solution.py:247
  112.6 34.2 %collective-permute-start.12 = (bf16[64,2048]{1,0:T(8,128)(2,1)}, bf16[64,2048]{1,0:T(8,128)(2,1)}, u32[]{:S(2)}, u32[]{:S(2)}) collective-permute-start(bf16[64,2048]{1,0:T(8,128)(2,1)} %get-tuple-element.102), channel_id=1, source_target_pairs={{0,6},{1,7},{2,4},{3,5},{4,2},{5,3},{6,0},{7,1},{8,14},{9,15},{10,... | collective-permute-start | bytes 786440 | tf_op jit(solution)/shard_map/ppermute | solution.py:234
  132.0 1.8 copy-start.10
  133.8 1.4 copy-start.18
  135.2 1.4 copy-start.20
  144.2 2.5 %copy-start.6 = (bf16[512,704]{1,0:T(8,128)(2,1)S(1)}, bf16[512,704]{1,0:T(8,128)(2,1)}, u32[]{:S(2)}) copy-start(bf16[512,704]{1,0:T(8,128)(2,1)} %copy-done.5) | copy-start | bytes 2162692
  146.7 2.9 %copy-start = (bf16[512,2048]{1,0:T(8,128)(2,1)}, bf16[512,2048]{1,0:T(8,128)(2,1)S(1)}, u32[]{:S(2)}) copy-start(bf16[512,2048]{1,0:T(8,128)(2,1)S(1)} %get-tuple-element.124.dy_ref) | copy-start | bytes 6291460
  149.6 16.9 %collective-permute-start.21 = (bf16[512,2176]{1,0:T(8,128)(2,1)}, bf16[512,2176]{1,0:T(8,128)(2,1)}, u32[]{:S(2)}, u32[]{:S(2)}) collective-permute-start(bf16[512,2176]{1,0:T(8,128)(2,1)} %weight_part.4), channel_id=1, source_target_pairs={{0,8},{8,0},{16,24},{24,16},{1,9},{9,1},{17,25},{25,17},{2,10},{10... | collective-permute-start | bytes 6684680 | tf_op jit(solution)/shard_map/ppermute | solution.py:234
  149.6 15.7 %collective-permute-start.9 = (bf16[64,2048]{1,0:T(8,128)(2,1)}, bf16[64,2048]{1,0:T(8,128)(2,1)}, u32[]{:S(2)}, u32[]{:S(2)}) collective-permute-start(bf16[64,2048]{1,0:T(8,128)(2,1)} %get-tuple-element.96), channel_id=1, source_target_pairs={{0,5},{1,4},{2,7},{3,6},{4,1},{5,0},{6,3},{7,2},{8,13},{9,12},{10,... | collective-permute-start | bytes 786440 | tf_op jit(solution)/shard_map/ppermute | solution.py:234
  149.6 16.9 %collective-permute-start.16 = (bf16[64,2048]{1,0:T(8,128)(2,1)}, bf16[64,2048]{1,0:T(8,128)(2,1)}, u32[]{:S(2)}, u32[]{:S(2)}) collective-permute-start(bf16[64,2048]{1,0:T(8,128)(2,1)} %get-tuple-element.109), channel_id=1, source_target_pairs={{0,3},{1,2},{2,1},{3,0},{4,7},{5,6},{6,5},{7,4},{8,11},{9,10},{10,... | collective-permute-start | bytes 786440 | tf_op jit(solution)/shard_map/ppermute | solution.py:247
  153.3 22.8 %collective-permute-start.20 = (bf16[64,2048]{1,0:T(8,128)(2,1)}, bf16[64,2048]{1,0:T(8,128)(2,1)}, u32[]{:S(2)}, u32[]{:S(2)}) collective-permute-start(bf16[64,2048]{1,0:T(8,128)(2,1)} %get-tuple-element.121), channel_id=1, source_target_pairs={{0,4},{1,5},{2,6},{3,7},{4,0},{5,1},{6,2},{7,3},{8,12},{9,13},{10,... | collective-permute-start | bytes 786440 | tf_op jit(solution)/shard_map/ppermute | solution.py:234
  153.3 22.9 %collective-permute-start.13 = (bf16[64,2048]{1,0:T(8,128)(2,1)}, bf16[64,2048]{1,0:T(8,128)(2,1)}, u32[]{:S(2)}, u32[]{:S(2)}) collective-permute-start(bf16[64,2048]{1,0:T(8,128)(2,1)} %get-tuple-element.103), channel_id=1, source_target_pairs={{0,2},{1,3},{2,0},{3,1},{4,6},{5,7},{6,4},{7,5},{8,10},{9,11},{10,... | collective-permute-start | bytes 786440 | tf_op jit(solution)/shard_map/ppermute | solution.py:247
  155.5 2.6 %copy-start.4 = (bf16[1,2048,1408]{2,1,0:T(8,128)(2,1)S(1)}, bf16[1,2048,1408]{2,1,0:T(8,128)(2,1)}, u32[]{:S(2)}) copy-start(bf16[1,2048,1408]{2,1,0:T(8,128)(2,1)} %param.7) | copy-start | bytes 17301508
  158.1 8.4 %copy-start.1 = (bf16[512,2048]{1,0:T(8,128)(2,1)S(1)}, bf16[512,2048]{1,0:T(8,128)(2,1)}, u32[]{:S(2)}) copy-start(bf16[512,2048]{1,0:T(8,128)(2,1)} %copy-done) | copy-start | bytes 6291460
  158.1 8.4 %copy-start.7 = (bf16[512,704]{1,0:T(8,128)(2,1)S(1)}, bf16[512,704]{1,0:T(8,128)(2,1)}, u32[]{:S(2)}) copy-start(bf16[512,704]{1,0:T(8,128)(2,1)} %copy-done.5) | copy-start | bytes 2162692
  161.6 9.5 %copy-start.25 = (bf16[64,2048]{1,0:T(8,128)(2,1)}, bf16[64,2048]{1,0:T(8,128)(2,1)S(1)}, u32[]{:S(2)}) copy-start(bf16[64,2048]{1,0:T(8,128)(2,1)S(1)} %get-tuple-element.130.refs_0_) | copy-start | bytes 786436
  161.6 9.5 %copy-start.43 = (bf16[64,2048]{1,0:T(8,128)(2,1)}, bf16[64,2048]{1,0:T(8,128)(2,1)S(1)}, u32[]{:S(2)}) copy-start(bf16[64,2048]{1,0:T(8,128)(2,1)S(1)} %get-tuple-element.134) | copy-start | bytes 786436
  161.6 9.5 %copy-start.45 = (bf16[64,2048]{1,0:T(8,128)(2,1)}, bf16[64,2048]{1,0:T(8,128)(2,1)S(1)}, u32[]{:S(2)}) copy-start(bf16[64,2048]{1,0:T(8,128)(2,1)S(1)} %get-tuple-element.138) | copy-start | bytes 786436
  161.6 9.5 %copy-start.47 = (bf16[64,2048]{1,0:T(8,128)(2,1)}, bf16[64,2048]{1,0:T(8,128)(2,1)S(1)}, u32[]{:S(2)}) copy-start(bf16[64,2048]{1,0:T(8,128)(2,1)S(1)} %get-tuple-element.144) | copy-start | bytes 786436
  161.6 9.5 %copy-start.49 = (bf16[64,2048]{1,0:T(8,128)(2,1)}, bf16[64,2048]{1,0:T(8,128)(2,1)S(1)}, u32[]{:S(2)}) copy-start(bf16[64,2048]{1,0:T(8,128)(2,1)S(1)} %get-tuple-element.142) | copy-start | bytes 786436
  161.6 9.5 %copy-start.51 = (bf16[64,2048]{1,0:T(8,128)(2,1)}, bf16[64,2048]{1,0:T(8,128)(2,1)S(1)}, u32[]{:S(2)}) copy-start(bf16[64,2048]{1,0:T(8,128)(2,1)S(1)} %get-tuple-element.133) | copy-start | bytes 786436
  161.6 9.5 %copy-start.53 = (bf16[64,2048]{1,0:T(8,128)(2,1)}, bf16[64,2048]{1,0:T(8,128)(2,1)S(1)}, u32[]{:S(2)}) copy-start(bf16[64,2048]{1,0:T(8,128)(2,1)S(1)} %get-tuple-element.137) | copy-start | bytes 786436
  161.6 9.5 %copy-start.55 = (bf16[64,2048]{1,0:T(8,128)(2,1)}, bf16[64,2048]{1,0:T(8,128)(2,1)S(1)}, u32[]{:S(2)}) copy-start(bf16[64,2048]{1,0:T(8,128)(2,1)S(1)} %get-tuple-element.141) | copy-start | bytes 786436
  171.1 54.0 %collective-permute-start.22 = (bf16[512,2176]{1,0:T(8,128)(2,1)}, bf16[512,2176]{1,0:T(8,128)(2,1)}, u32[]{:S(2)}, u32[]{:S(2)}) collective-permute-start(bf16[512,2176]{1,0:T(8,128)(2,1)} %weight_part.5), channel_id=1, source_target_pairs={{0,16},{8,24},{16,0},{24,8},{1,17},{9,25},{17,1},{25,9},{2,18},{10... | collective-permute-start | bytes 6684680 | tf_op jit(solution)/shard_map/ppermute | solution.py:234
  176.2 1.6 copy-start.2
  178.9 1.6 copy-start.42
  178.9 3.2 %copy-start.56 = (bf16[64,2048]{1,0:T(8,128)(2,1)S(1)}, bf16[64,2048]{1,0:T(8,128)(2,1)}, u32[]{:S(2)}) copy-start(bf16[64,2048]{1,0:T(8,128)(2,1)} %copy-done.55) | copy-start | bytes 786436
  178.9 4.9 %copy-start.54 = (bf16[64,2048]{1,0:T(8,128)(2,1)S(1)}, bf16[64,2048]{1,0:T(8,128)(2,1)}, u32[]{:S(2)}) copy-start(bf16[64,2048]{1,0:T(8,128)(2,1)} %copy-done.53) | copy-start | bytes 786436
  178.9 16.0 %copy-start.52 = (bf16[64,2048]{1,0:T(8,128)(2,1)S(1)}, bf16[64,2048]{1,0:T(8,128)(2,1)}, u32[]{:S(2)}) copy-start(bf16[64,2048]{1,0:T(8,128)(2,1)} %copy-done.51) | copy-start | bytes 786436
  178.9 16.0 %copy-start.14 = (bf16[256,2048]{1,0:T(8,128)(2,1)S(1)}, bf16[256,2048]{1,0:T(8,128)(2,1)}, u32[]{:S(2)}) copy-start(bf16[256,2048]{1,0:T(8,128)(2,1)} %data_ref.2) | copy-start | bytes 3145732
  179.0 15.9 %copy-start.16 = (bf16[512,256]{1,0:T(8,128)(2,1)S(1)}, bf16[512,256]{1,0:T(8,128)(2,1)}, u32[]{:S(2)}) copy-start(bf16[512,256]{1,0:T(8,128)(2,1)} %copy-done.15) | copy-start | bytes 786436
  179.0 15.9 %copy-start.22 = (bf16[64,2048]{1,0:T(8,128)(2,1)S(1)}, bf16[64,2048]{1,0:T(8,128)(2,1)}, u32[]{:S(2)}) copy-start(bf16[64,2048]{1,0:T(8,128)(2,1)} %copy-done.21) | copy-start | bytes 786436
  180.5 46.0 %collective-permute-start.23 = (bf16[512,2176]{1,0:T(8,128)(2,1)S(1)}, bf16[512,2176]{1,0:T(8,128)(2,1)S(1)}, u32[]{:S(2)}, u32[]{:S(2)}) collective-permute-start(bf16[512,2176]{1,0:T(8,128)(2,1)S(1)} %weight_part.6), channel_id=1, source_target_pairs={{0,8},{8,0},{16,24},{24,16},{1,9},{9,1},{17,25},{25,17},{2,10},{10... | collective-permute-start | bytes 6684680 | tf_op jit(solution)/shard_map/ppermute | solution.py:234
  180.6 14.3 %collective-permute-start.10 = (bf16[64,2048]{1,0:T(8,128)(2,1)S(1)}, bf16[64,2048]{1,0:T(8,128)(2,1)S(1)}, u32[]{:S(2)}, u32[]{:S(2)}) collective-permute-start(bf16[64,2048]{1,0:T(8,128)(2,1)S(1)} %copy-done.42), channel_id=1, source_target_pairs={{0,1},{1,0},{2,3},{3,2},{4,5},{5,4},{6,7},{7,6},{8,9},{9,8},{10,11... | collective-permute-start | bytes 786440 | tf_op jit(solution)/shard_map/ppermute | solution.py:247
  182.2 17.0 %collective-permute-start.28 = (bf16[64,2048]{1,0:T(8,128)(2,1)S(1)}, bf16[64,2048]{1,0:T(8,128)(2,1)S(1)}, u32[]{:S(2)}, u32[]{:S(2)}) collective-permute-start(bf16[64,2048]{1,0:T(8,128)(2,1)S(1)} %copy-done.56), channel_id=1, source_target_pairs={{0,7},{1,6},{2,5},{3,4},{4,3},{5,2},{6,1},{7,0},{8,15},{9,14},{10,... | collective-permute-start | bytes 786440 | tf_op jit(solution)/shard_map/ppermute | solution.py:234
  183.8 25.7 %collective-permute-start.26 = (bf16[64,2048]{1,0:T(8,128)(2,1)S(1)}, bf16[64,2048]{1,0:T(8,128)(2,1)S(1)}, u32[]{:S(2)}, u32[]{:S(2)}) collective-permute-start(bf16[64,2048]{1,0:T(8,128)(2,1)S(1)} %copy-done.54), channel_id=1, source_target_pairs={{0,6},{1,7},{2,4},{3,5},{4,2},{5,3},{6,0},{7,1},{8,14},{9,15},{10,... | collective-permute-start | bytes 786440 | tf_op jit(solution)/shard_map/ppermute | solution.py:234
  194.9 30.2 %collective-permute-start.24 = (bf16[64,2048]{1,0:T(8,128)(2,1)S(1)}, bf16[64,2048]{1,0:T(8,128)(2,1)S(1)}, u32[]{:S(2)}, u32[]{:S(2)}) collective-permute-start(bf16[64,2048]{1,0:T(8,128)(2,1)S(1)} %copy-done.52), channel_id=1, source_target_pairs={{0,5},{1,4},{2,7},{3,6},{4,1},{5,0},{6,3},{7,2},{8,13},{9,12},{10,... | collective-permute-start | bytes 786440 | tf_op jit(solution)/shard_map/ppermute | solution.py:234
  194.9 4.3 %copy-start.50 = (bf16[64,2048]{1,0:T(8,128)(2,1)S(1)}, bf16[64,2048]{1,0:T(8,128)(2,1)}, u32[]{:S(2)}) copy-start(bf16[64,2048]{1,0:T(8,128)(2,1)} %copy-done.49) | copy-start | bytes 786436
  194.9 14.6 %copy-start.48 = (bf16[64,2048]{1,0:T(8,128)(2,1)S(1)}, bf16[64,2048]{1,0:T(8,128)(2,1)}, u32[]{:S(2)}) copy-start(bf16[64,2048]{1,0:T(8,128)(2,1)} %copy-done.47) | copy-start | bytes 786436
  194.9 30.1 %copy-start.46 = (bf16[64,2048]{1,0:T(8,128)(2,1)S(1)}, bf16[64,2048]{1,0:T(8,128)(2,1)}, u32[]{:S(2)}) copy-start(bf16[64,2048]{1,0:T(8,128)(2,1)} %copy-done.45) | copy-start | bytes 786436
  194.9 30.1 %copy-start.44 = (bf16[64,2048]{1,0:T(8,128)(2,1)S(1)}, bf16[64,2048]{1,0:T(8,128)(2,1)}, u32[]{:S(2)}) copy-start(bf16[64,2048]{1,0:T(8,128)(2,1)} %copy-done.43) | copy-start | bytes 786436
  199.2 33.0 %collective-permute-start.29 = (bf16[64,2048]{1,0:T(8,128)(2,1)S(1)}, bf16[64,2048]{1,0:T(8,128)(2,1)S(1)}, u32[]{:S(2)}, u32[]{:S(2)}) collective-permute-start(bf16[64,2048]{1,0:T(8,128)(2,1)S(1)} %copy-done.50), channel_id=1, source_target_pairs={{0,3},{1,2},{2,1},{3,0},{4,7},{5,6},{6,5},{7,4},{8,11},{9,10},{10,... | collective-permute-start | bytes 786440 | tf_op jit(solution)/shard_map/ppermute | solution.py:247
  209.5 22.7 %collective-permute-start.30 = (bf16[64,2048]{1,0:T(8,128)(2,1)S(1)}, bf16[64,2048]{1,0:T(8,128)(2,1)S(1)}, u32[]{:S(2)}, u32[]{:S(2)}) collective-permute-start(bf16[64,2048]{1,0:T(8,128)(2,1)S(1)} %copy-done.48), channel_id=1, source_target_pairs={{0,4},{1,5},{2,6},{3,7},{4,0},{5,1},{6,2},{7,3},{8,12},{9,13},{10,... | collective-permute-start | bytes 786440 | tf_op jit(solution)/shard_map/ppermute | solution.py:234
  225.1 10.3 %collective-permute-start.27 = (bf16[64,2048]{1,0:T(8,128)(2,1)S(1)}, bf16[64,2048]{1,0:T(8,128)(2,1)S(1)}, u32[]{:S(2)}, u32[]{:S(2)}) collective-permute-start(bf16[64,2048]{1,0:T(8,128)(2,1)S(1)} %copy-done.46), channel_id=1, source_target_pairs={{0,2},{1,3},{2,0},{3,1},{4,6},{5,7},{6,4},{7,5},{8,10},{9,11},{10,... | collective-permute-start | bytes 786440 | tf_op jit(solution)/shard_map/ppermute | solution.py:247
  225.1 10.3 %collective-permute-start.25 = (bf16[64,2048]{1,0:T(8,128)(2,1)S(1)}, bf16[64,2048]{1,0:T(8,128)(2,1)S(1)}, u32[]{:S(2)}, u32[]{:S(2)}) collective-permute-start(bf16[64,2048]{1,0:T(8,128)(2,1)S(1)} %copy-done.44), channel_id=1, source_target_pairs={{0,1},{1,0},{2,3},{3,2},{4,5},{5,4},{6,7},{7,6},{8,9},{9,8},{10,11... | collective-permute-start | bytes 786440 | tf_op jit(solution)/shard_map/ppermute | solution.py:247
  226.5 8.9 %copy-start.12 = (bf16[256,2048]{1,0:T(8,128)(2,1)S(1)}, bf16[256,2048]{1,0:T(8,128)(2,1)}, u32[]{:S(2)}) copy-start(bf16[256,2048]{1,0:T(8,128)(2,1)} %data_ref.3) | copy-start | bytes 3145732
  226.5 8.9 %copy-start.26 = (bf16[64,2048]{1,0:T(8,128)(2,1)S(1)}, bf16[64,2048]{1,0:T(8,128)(2,1)}, u32[]{:S(2)}) copy-start(bf16[64,2048]{1,0:T(8,128)(2,1)} %copy-done.25) | copy-start | bytes 786436
  (24 other events, 21.4 us)

commit v4 on v0

v4 whole, which is shorter than its diff:
```python
import jax
import jax.numpy as jnp
from jax import lax
from jax.experimental import pallas as pl
from jax.experimental.pallas import tpu as pltpu
from jax.sharding import PartitionSpec as P

SMALL = pl.CostEstimate(flops=1024, bytes_accessed=1024, transcendentals=0)
BF16 = jnp.bfloat16
F32 = jnp.float32
ROWS = ((0,), (0,))
COLS = ((1,), (1,))
PLAIN = ((1,), (0,))


def dot(left, right, dims):
    return lax.dot_general(left, right, (dims, ((), ())), preferred_element_type=F32)


def like(shape, dtype=BF16):
    return jax.ShapeDtypeStruct(shape, dtype)


def call(kernel, name, mebibytes, outs, scratch, arrays, small=(), scalars=()):
    hbm = pl.BlockSpec(memory_space=pltpu.HBM)
    return pl.pallas_call(
        kernel,
        in_specs=[pl.BlockSpec(memory_space=pltpu.SMEM)] * len(scalars)
        + [pl.BlockSpec(memory_space=pltpu.VMEM)] * len(small)
        + [hbm] * len(arrays),
        out_specs=[hbm] * len(outs),
        out_shape=outs,
        scratch_shapes=scratch,
        compiler_params=pltpu.CompilerParams(vmem_limit_bytes=mebibytes * 1024 * 1024),
        cost_estimate=SMALL,
        name=name,
    )(*scalars, *small, *arrays)


class Copies:
    def __init__(self, sems):
        self.sems = sems
        self.used = 0

    def start(self, source, target):
        copy = pltpu.make_async_copy(source, target, self.sems.at[self.used])
        self.used += 1
        copy.start()
        return copy


def wait(copies):
    for copy in copies:
        copy.wait()


def place_kernel(part, cap, rel_ref, tokens_ref, grad_ref, *refs):
    blocks, (data, moved, sems) = refs[:-3], refs[-3:]
    experts = len(blocks)
    rows, width = tokens_ref.shape
    copies = Copies(sems)
    loads = [copies.start(ref, data.at[:, side * width : (side + 1) * width]) for side, ref in enumerate((tokens_ref, grad_ref))]
    placing = placing_of(rel_ref[...], experts, part, cap)
    stores = []
    for side in range(2):
        here = slice(side * width, (side + 1) * width)
        loads[side].wait()
        moved[:, here] = dot(placing, data[:, here], PLAIN).astype(BF16)
        for index, block in enumerate(blocks):
            stores.append(copies.start(moved.at[index * cap : (index + 1) * cap, here], block.at[:, here]))
    wait(stores)


def placing_of(rel, experts, part, cap):
    rows = rel.shape[1]
    onehot = lax.broadcasted_iota(jnp.int32, (max(experts, 16), rows), 0) == rel
    before = lax.broadcasted_iota(jnp.int32, (rows, rows), 0) < lax.broadcasted_iota(jnp.int32, (rows, rows), 1)
    ranks = dot(onehot.astype(BF16), before.astype(BF16), PLAIN)
    rank = jnp.sum(jnp.where(onehot, ranks, 0.0), axis=0, keepdims=True).astype(jnp.int32) - part * cap
    target = jnp.where((rank >= 0) & (rank < cap), rel * cap + rank, -1)
    return (lax.broadcasted_iota(jnp.int32, (experts * cap, rows), 0) == target).astype(BF16)


def expert_kernel(*refs):
    count = (len(refs) - 12) // 2
    blocks, (one_ref, two_ref), outs = refs[:count], refs[count : count + 2], refs[count + 2 : 2 * count + 2]
    slot_out, proj_out, hidden_out, slot, one, two, back, proj, hidden, sems = refs[2 * count + 2 :]
    cap = blocks[0].shape[0]
    wide, width = two.shape
    copies = Copies(sems)
    loads = [copies.start(block, slot.at[index * cap : (index + 1) * cap]) for index, block in enumerate(blocks)]
    one_load = copies.start(one_ref, one)
    two_load = copies.start(two_ref, two)
    wait(loads)
    stores = [copies.start(slot, slot_out)]
    one_load.wait()
    both = dot(slot[:, :width], one[...], PLAIN)
    gate, upper = both[:, :wide], both[:, wide:]
    sigma = 1.0 / (1.0 + jnp.exp(-gate))
    silu = gate * sigma
    hidden[...] = (silu * upper).astype(BF16)
    stores.append(copies.start(hidden, hidden_out))
    two_load.wait()
    grad_hidden = dot(slot[:, width:], two[...], COLS)
    proj[...] = jnp.concatenate(
        [grad_hidden * upper * sigma * (1.0 + gate * (1.0 - sigma)), grad_hidden * silu], axis=1
    ).astype(BF16)
    stores.append(copies.start(proj, proj_out))
    back[:, :width] = dot(hidden[...], two[...], PLAIN).astype(BF16)
    back[:, width:] = dot(proj[...], one[...], COLS).astype(BF16)
    stores += [copies.start(back.at[index * cap : (index + 1) * cap], out) for index, out in enumerate(outs)]
    wait(stores)


def weight_kernel(end, parts, pieces, number_ref, *refs):
    sources, refs = refs[: 3 * parts], refs[3 * parts :]
    more, refs = refs[: sum(pieces)], refs[sum(pieces) :]
    results, sems = refs[-3 if end else -2 : -1], refs[-1]
    outs, (x, dy, proj, hidden, received) = refs[: -6 - len(results)], refs[-6 - len(results) : -1 - len(results)]
    cap = x.shape[0] // parts
    share, wide = x.shape[1], hidden.shape[1]
    width = sources[0].shape[1] // 2
    first = pl.multiple_of(number_ref[0] * share, share)
    copies = Copies(sems)
    loads = []
    for part in range(parts):
        slot_ref, proj_ref, hidden_ref = sources[3 * part : 3 * part + 3]
        here = slice(part * cap, (part + 1) * cap)
        loads.append(copies.start(slot_ref.at[:, pl.ds(first, share)], x.at[here]))
        loads.append(copies.start(slot_ref.at[:, pl.ds(pl.multiple_of(first + width, share), share)], dy.at[here]))
        loads.append(copies.start(proj_ref, proj.at[here]))
        loads.append(copies.start(hidden_ref, hidden.at[here]))
    more_loads = []
    for index, number in enumerate(pieces):
        row = 0
        for ref in more[:number]:
            more_loads.append(copies.start(ref, received.at[index, row : row + ref.shape[0]]))
            row += ref.shape[0]
        more = more[number:]
    wait(loads)
    up = dot(x[...], proj[...], ROWS)
    down = dot(hidden[...], dy[...], ROWS) if end else dot(dy[...], hidden[...], ROWS)
    wait(more_loads)
    for index in range(len(pieces)):
        up = up + received[index, :, : 2 * wide].astype(F32)
        extra = received[index, :, 2 * wide : 3 * wide]
        if end:
            row = lax.broadcasted_iota(jnp.int32, (share, share), 0)
            unit = (row == lax.broadcasted_iota(jnp.int32, (share, share), 1)).astype(BF16)
            down = down + dot(extra, unit, ROWS)
        else:
            down = down + extra.astype(F32)
    if end:
        results[0][...] = up
        results[1][...] = down
        wait([copies.start(result, out) for result, out in zip(results, outs)])
        return
    results[0][:, : 2 * wide] = up.astype(BF16)
    results[0][:, 2 * wide : 3 * wide] = down.astype(BF16)
    stores, row = [], 0
    for out in outs:
        stores.append(copies.start(results[0].at[row : row + out.shape[0]], out))
        row += out.shape[0]
    wait(stores)


def combine_kernel(part, cap, rel_ref, tokens_ref, grad_ref, *refs):
    blocks, (mixed_out, grad_out, data, back, sems) = refs[:-5], refs[-5:]
    width = tokens_ref.shape[1]
    copies = Copies(sems)
    loads = [copies.start(ref, data.at[:, side * width : (side + 1) * width]) for side, ref in enumerate((tokens_ref, grad_ref))]
    loads += [copies.start(block, back.at[index * cap : (index + 1) * cap]) for index, block in enumerate(blocks)]
    placing = placing_of(rel_ref[...], len(blocks), part, cap)
    wait(loads)
    stores = []
    for side, out in enumerate((mixed_out, grad_out)):
        here = slice(side * width, (side + 1) * width)
        data[:, here] = (data[:, here].astype(F32) + dot(placing, back[:, here], ROWS)).astype(BF16)
        stores.append(copies.start(data.at[:, here], out))
    wait(stores)


def after(value, *earlier):
    if not earlier:
        return value
    return lax.optimization_barrier((value, *earlier))[0]


class Lane:
    def __init__(self, window):
        self.window = window
        self.done = []

    def send(self, value, axis, pairs, *earlier):
        if len(self.done) >= self.window:
            earlier = (self.done[-self.window], *earlier)
        self.done.append(lax.ppermute(after(value, *earlier), axis, pairs))
        return self.done[-1]


def exchange(blocks, far, held={}):
    experts = len(blocks)
    half = experts // 2
    moved = {0: blocks[0]}
    for mask in range(half - 1, -1, -1):
        pairs = [(i, i ^ (mask + half)) for i in range(experts)]
        moved[mask + half] = far.send(blocks[mask + half], "exp", pairs, *held.get(mask, ()))
        if mask:
            pairs = [(i, i ^ mask) for i in range(experts)]
            moved[mask] = lax.ppermute(after(blocks[mask], far.done[-1]), "exp", pairs)
    return [moved[mask] for mask in range(experts)]


def body(tokens, expert_ids, gate_up_weight, down_weight, grad_out):
    rows, width = tokens.shape
    experts = lax.axis_size("exp")
    groups = lax.axis_size("grp")
    capacity = 2 * rows // experts
    parts = 2 if capacity % 32 == 0 else 1
    cap = capacity // parts
    slots = experts * cap
    weight_one = gate_up_weight[0]
    weight_two = down_weight[0]
    wide = weight_two.shape[0]
    share = width // groups
    pair = like((cap, 2 * width))
    sems = pltpu.SemaphoreType.DMA
    far = Lane(3)
    rel = expert_ids.reshape(1, rows) ^ lax.axis_index("exp").astype(jnp.int32)
    group = lax.axis_index("grp").astype(jnp.int32)

    def place(part):
        return call(
            lambda *refs: place_kernel(part, cap, *refs),
            "place",
            20,
            [pair] * experts,
            [pltpu.VMEM((rows, 2 * width), BF16), pltpu.VMEM((slots, 2 * width), BF16), sems((2 + 2 * experts,))],
            [tokens, grad_out],
            [rel],
        )

    def expert(blocks):
        shapes = [(slots, 2 * width), (slots, 2 * wide), (slots, wide)]
        back = [pltpu.VMEM(shape, BF16) for shape in shapes]
        scratch = [back[0], pltpu.VMEM(weight_one.shape, BF16), pltpu.VMEM(weight_two.shape, BF16)]
        outs = call(
            expert_kernel,
            "expert",
            44,
            [pair] * experts + [like(shape) for shape in shapes],
            scratch + back + [sems((5 + 2 * experts,))],
            [*blocks, weight_one, weight_two],
        )
        return outs[:experts], outs[experts:]

    def weight_part(number, kept, received, end, heads):
        shape = (share, pl.cdiv(3 * wide, 128) * 128)
        finals = [like((share, 2 * wide), F32), like((wide, share), F32)]
        rows_of = [heads, share - heads] if heads else [share]
        outs = finals if end else [like((count, shape[1])) for count in rows_of]
        total = parts * slots
        scratch = [pltpu.VMEM((total, width), BF16) for width in (share, share, 2 * wide, wide)]
        scratch.append(pltpu.VMEM((max(1, len(received)), *shape), BF16))
        scratch += [pltpu.VMEM(out.shape, out.dtype) for out in (finals if end else [like(shape)])]
        sources = [array for arrays in kept + received for array in arrays]
        scratch.append(sems((len(sources) + parts + len(outs),)))
        pieces = [len(arrays) for arrays in received]
        return call(
            lambda *refs: weight_kernel(end, parts, pieces, *refs),
            "weight_part",
            32,
            outs,
            scratch,
            sources,
            scalars=[number[None]],
        )

    def combine(part, first, second, blocks):
        return call(
            lambda *refs: combine_kernel(part, cap, *refs),
            "combine",
            20,
            [like((rows, width))] * 2,
            [pltpu.VMEM((rows, 2 * width), BF16), pltpu.VMEM((slots, 2 * width), BF16), sems((4 + experts,))],
            [first, second, *blocks],
            [rel],
        )

    sent = [place(part) for part in range(parts)]
    results = []
    for part in range(parts):
        held = {0: (results[-1][0][0],)} if results else {}
        results.append(expert(exchange(sent[part], far, held)))
    kept = [result[1] for result in results]

    count = len(far.done)
    back = [exchange(results[0][0], far)]
    far_out = far.done[count:]
    near_out = back[0][experts // 2 - 1 : 0 : -1]
    gates = iter([[], far_out[2:3] + near_out[:1], far_out[3:] + near_out[1:2]])
    lanes = {}

    def weight_sum(q, bit):
        received = []
        low = bit // 2
        while low:
            pairs = [(i, i ^ low) for i in range(groups)]
            lane = lanes.setdefault(low, Lane(1))
            head, *rest = weight_sum(q | low, low)
            head = lane.send(head, "grp", pairs)
            received.append([head] + [lane.send(piece, "grp", pairs, *far_out[:2]) for piece in rest])
            low //= 2
        first = after(kept[0][0], *([] if bit == groups else next(gates, [])))
        heads = 16 if q == groups - 1 else 0
        return weight_part(group ^ q, [[first, *kept[0][1:]], *kept[1:]], received, bit == groups, heads)

    grad_gate_up, grad_down = weight_sum(0, groups)
    mixed, grad = tokens, grad_out
    for part in range(1, parts):
        mixed, grad = combine(part - 1, mixed, grad, back[-1])
        back.append(exchange(results[part][0], far, {0: (mixed,)}))
    back[-1][0] = after(back[-1][0], grad_gate_up)
    mixed, grad = combine(parts - 1, mixed, grad, back[-1])
    return (mixed, grad, grad_gate_up[None], grad_down[None])


def solution(mesh):
    in_specs = (
        P(("grp", "exp"), None),
        P(("grp", "exp"), None),
        P("exp", None, None),
        P("exp", None, None),
        P(("grp", "exp"), None),
    )
    out_specs = (
        P(("grp", "exp"), None),
        P(("grp", "exp"), None),
        P("exp", "grp", None),
        P("exp", None, "grp"),
    )
    return jax.shard_map(body, mesh=mesh, in_specs=in_specs, out_specs=out_specs, check_vma=False)
```

time: 291 us -> 248 us (0.85)
  waiting for transfers between devices: 194 us -> 63.4 us
  starting transfers between devices: 20.8 us -> 105 us
  matrix products: 56.9 us -> 0 us
  Pallas kernels: 0 us -> 49.3 us
  local copies, waits for them, and re-layouts: 1.12 us -> 26.8 us
  between operations: 14.1 us -> 1.29 us
    all_to_all x4 -> x0, waiting for transfers between devices: 173 us -> none  [the longest x1 45.1 us: body(): lax.all_to_all(sent_x.reshape(experts, capacity, width), 'exp', split_axi...]
    ppermute x0 -> x32, starting transfers between devices: none -> 105 us  [the longest x20 57.4 us: send(): self.done.append(lax.ppermute(after(value, *earlier), axis, pairs))]
    ppermute x0 -> x32, waiting for transfers between devices: none -> 63.4 us  [the longest x20 50.3 us: send(): self.done.append(lax.ppermute(after(value, *earlier), axis, pairs))]
    dot_general x10 -> x0, matrix products: 56.9 us -> none  [the longest x4 24 us: contract_rows(): lax.dot_general(left, right, (((0,), (0,)), ((), ())), preferred_element_...]
    pallas_call x0 -> x10, Pallas kernels: none -> 49.3 us  [call(): pl.pallas_call(kernel, in_specs=[pl.BlockSpec(memory_space=pltpu.SMEM)] *...]
    unnamed x4 -> x104, local copies, waits for them, and re-layouts: 0.91 us -> 26.8 us
    reduce_scatter x2 -> x0, waiting for transfers between devices: 21.3 us -> none  [the longest x1 21.3 us: body(): lax.psum_scatter(contract_rows(slot_x, grad_proj), 'grp', scatter_dimensi...]
    all_to_all x4 -> x0, starting transfers between devices: 20.6 us -> none  [the longest x1 7.28 us: body(): lax.all_to_all(sent_x.reshape(experts, capacity, width), 'exp', split_axi...]
  transfers between devices with their start and end apart: 6 -> 32, of which waited for: 5 -> 10; matrix products, arithmetic and copies ran while one was open for 15% -> 0% of each run, Pallas kernels for 0% -> 18%
where the time goes in v4:
time: 248 us; the launch traced here: 247 us
  starting transfers between devices  105 us (42%)
  waiting for transfers between devices  63.4 us (26%)
  Pallas kernels  49.3 us (20%)
  local copies, waits for them, and re-layouts  26.8 us (11%)
    ppermute x20, starting transfers between devices, send(): self.done.append(lax.ppermute(after(value, *earlier), axis, pairs))  57.4 us
    ppermute x20, waiting for transfers between devices, send(): self.done.append(lax.ppermute(after(value, *earlier), axis, pairs))  50.3 us
    pallas_call x10, Pallas kernels, call(): pl.pallas_call(kernel, in_specs=[pl.BlockSpec(memory_space=pltpu.SMEM)] *...  49.3 us
    ppermute x12, starting transfers between devices, exchange(): moved[mask] = lax.ppermute(after(blocks[mask], far.done[-1]), 'exp', pairs)  47.7 us
    unnamed x104, local copies, waits for them, and re-layouts  26.8 us
    ppermute x12, waiting for transfers between devices, exchange(): moved[mask] = lax.ppermute(after(blocks[mask], far.done[-1]), 'exp', pairs)  13.1 us
  transfers between devices with their start and end apart: 32, of which 10 were waited for; matrix products, arithmetic and copies ran while one was open for 0% of the time, Pallas kernels for 18%

profile of v4, /device:TPU:0, one launch (start us, length us, event | category | flops | bytes accessed | tf_op | source)
XLA Modules:
  0.0 246.7 jit_solution(9976399360433859812)
XLA Ops:
  0.6 0.8 xor_bitcast_fusion.refs_0_
  1.5 1.3 copy-done.5
  2.7 1.2 copy-done.7
  4.0 2.2 place.2
  6.2 6.1 %collective-permute-start.4 = (bf16[32,4096]{1,0:T(8,128)(2,1)S(1)}, bf16[32,4096]{1,0:T(8,128)(2,1)S(1)}, u32[]{:S(2)}, u32[]{:S(2)}) collective-permute-start(bf16[32,4096]{1,0:T(8,128)(2,1)S(1)} %get-tuple-element.88), channel_id=1, source_target_pairs={{0,7},{1,6},{2,5},{3,4},{4,3},{5,2},{6,1},{7,0},{8,15},{9,14},{10,... | collective-permute-start | bytes 786440 | tf_op jit(solution)/shard_map/ppermute | solution.py:197
  12.2 1.9 collective-permute-start.2
  14.1 5.4 %collective-permute-done.4.refs_7_ = bf16[32,4096]{1,0:T(8,128)(2,1)S(1)} collective-permute-done((bf16[32,4096]{1,0:T(8,128)(2,1)S(1)}, bf16[32,4096]{1,0:T(8,128)(2,1)S(1)}, u32[]{:S(2)}, u32[]{:S(2)}) %collective-permute-start.4) | collective-permute-done | bytes 262176 | tf_op jit(solution)/shard_map/ppermute | solution.py:197
  19.5 17.7 %collective-permute-start.6 = (bf16[32,4096]{1,0:T(8,128)(2,1)S(1)}, bf16[32,4096]{1,0:T(8,128)(2,1)S(1)}, u32[]{:S(2)}, u32[]{:S(2)}) collective-permute-start(bf16[32,4096]{1,0:T(8,128)(2,1)S(1)} %get-tuple-element.91), channel_id=1, source_target_pairs={{0,4},{1,5},{2,6},{3,7},{4,0},{5,1},{6,2},{7,3},{8,12},{9,13},{10,... | collective-permute-start | bytes 786440 | tf_op jit(solution)/shard_map/ppermute | solution.py:197
  37.2 2.5 %place.3 = (bf16[32,4096]{1,0:T(8,128)(2,1)S(1)}, bf16[32,4096]{1,0:T(8,128)(2,1)}, bf16[32,4096]{1,0:T(8,128)(2,1)S(1)}, bf16[32,4096]{1,0:T(8,128)(2,1)}, bf16...) custom-call(s32[1,256]{1,0:T(1,128)S(1)} %xor_bitcast_fusion.refs_0_, ...), custom_call_target="tpu_custom_call" | custom-call | flops 1024 | bytes 1024 | tf_op jit(solution)/shard_map/place/pallas_call | solution.py:26
  40.4 6.3 %collective-permute-done.refs_5_ = bf16[32,4096]{1,0:T(8,128)(2,1)S(1)} collective-permute-done((bf16[32,4096]{1,0:T(8,128)(2,1)S(1)}, bf16[32,4096]{1,0:T(8,128)(2,1)S(1)}, u32[]{:S(2)}, u32[]{:S(2)}) %collective-permute-start) | collective-permute-done | bytes 262176 | tf_op jit(solution)/shard_map/ppermute | solution.py:197
  46.7 2.6 %collective-permute-start.14 = (bf16[32,4096]{1,0:T(8,128)(2,1)S(1)}, bf16[32,4096]{1,0:T(8,128)(2,1)S(1)}, u32[]{:S(2)}, u32[]{:S(2)}) collective-permute-start(bf16[32,4096]{1,0:T(8,128)(2,1)S(1)} %get-tuple-element.110), channel_id=1, source_target_pairs={{0,6},{1,7},{2,4},{3,5},{4,2},{5,3},{6,0},{7,1},{8,14},{9,15},{10,... | collective-permute-start | bytes 786440 | tf_op jit(solution)/shard_map/ppermute | solution.py:197
  49.4 2.1 collective-permute-start.7
  52.0 15.4 %collective-permute-start.3 = (bf16[32,4096]{1,0:T(8,128)(2,1)S(1)}, bf16[32,4096]{1,0:T(8,128)(2,1)S(1)}, u32[]{:S(2)}, u32[]{:S(2)}) collective-permute-start(bf16[32,4096]{1,0:T(8,128)(2,1)S(1)} %get-tuple-element.86), channel_id=1, source_target_pairs={{0,2},{1,3},{2,0},{3,1},{4,6},{5,7},{6,4},{7,5},{8,10},{9,11},{10,... | collective-permute-start | bytes 786440 | tf_op jit(solution)/shard_map/ppermute | solution.py:210
  67.4 1.8 collective-permute-done.6.refs_4_
  69.2 0.7 copy-done.22
  69.9 7.4 %collective-permute-start.11 = (bf16[32,4096]{1,0:T(8,128)(2,1)S(1)}, bf16[32,4096]{1,0:T(8,128)(2,1)S(1)}, u32[]{:S(2)}, u32[]{:S(2)}) collective-permute-start(bf16[32,4096]{1,0:T(8,128)(2,1)S(1)} %get-tuple-element.104), channel_id=1, source_target_pairs={{0,5},{1,4},{2,7},{3,6},{4,1},{5,0},{6,3},{7,2},{8,13},{9,12},{10,... | collective-permute-start | bytes 786440 | tf_op jit(solution)/shard_map/ppermute | solution.py:197
  77.3 0.7 copy-done.24
  78.0 12.2 %collective-permute-start.19 = (bf16[32,4096]{1,0:T(8,128)(2,1)S(1)}, bf16[32,4096]{1,0:T(8,128)(2,1)S(1)}, u32[]{:S(2)}, u32[]{:S(2)}) collective-permute-start(bf16[32,4096]{1,0:T(8,128)(2,1)S(1)} %get-tuple-element.121), channel_id=1, source_target_pairs={{0,2},{1,3},{2,0},{3,1},{4,6},{5,7},{6,4},{7,5},{8,10},{9,11},{10,... | collective-permute-start | bytes 786440 | tf_op jit(solution)/shard_map/ppermute | solution.py:210
  90.3 0.8 collective-permute-start.20
  91.1 10.8 %expert.2 = (bf16[32,4096]{1,0:T(8,128)(2,1)S(1)}, bf16[32,4096]{1,0:T(8,128)(2,1)S(1)}, bf16[32,4096]{1,0:T(8,128)(2,1)}, bf16[32,4096]{1,0:T(8,128)(2,1)}, bf1...) custom-call(bf16[32,4096]{1,0:T(8,128)(2,1)S(1)} %get-tuple-element., ...), custom_call_target="tpu_custom_call" | custom-call | flops 1024 | bytes 1024 | tf_op jit(solution)/shard_map/expert/pallas_call | solution.py:26
  101.9 0.7 copy-done.9
  102.7 0.7 copy-done.18
  104.0 3.2 %collective-permute-start.8 = (bf16[32,4096]{1,0:T(8,128)(2,1)}, bf16[32,4096]{1,0:T(8,128)(2,1)S(1)}, u32[]{:S(2)}, u32[]{:S(2)}) collective-permute-start(bf16[32,4096]{1,0:T(8,128)(2,1)} %get-tuple-element.98), channel_id=1, source_target_pairs={{0,4},{1,5},{2,6},{3,7},{4,0},{5,1},{6,2},{7,3},{8,12},{9,13},{10,... | collective-permute-start | bytes 786440 | tf_op jit(solution)/shard_map/ppermute | solution.py:197
  108.5 2.1 collective-permute-start.15
  110.6 0.7 copy-done.28
  111.3 2.7 %collective-permute-start.12 = (bf16[32,4096]{1,0:T(8,128)(2,1)}, bf16[32,4096]{1,0:T(8,128)(2,1)}, u32[]{:S(2)}, u32[]{:S(2)}) collective-permute-start(bf16[32,4096]{1,0:T(8,128)(2,1)} %get-tuple-element.105), channel_id=1, source_target_pairs={{0,6},{1,7},{2,4},{3,5},{4,2},{5,3},{6,0},{7,1},{8,14},{9,15},{10,... | collective-permute-start | bytes 786440 | tf_op jit(solution)/shard_map/ppermute | solution.py:197
  114.0 0.7 copy-done.30
  114.7 14.9 %collective-permute-done.8.refs_4_ = bf16[32,4096]{1,0:T(8,128)(2,1)S(1)} collective-permute-done((bf16[32,4096]{1,0:T(8,128)(2,1)}, bf16[32,4096]{1,0:T(8,128)(2,1)S(1)}, u32[]{:S(2)}, u32[]{:S(2)}) %collective-permute-start.8) | collective-permute-done | bytes 262176 | tf_op jit(solution)/shard_map/ppermute | solution.py:197
  130.3 1.8 copy-done.4
  132.1 0.9 copy-done.21
  133.1 0.9 copy-done.23
  134.0 0.9 copy-done.25
  135.0 0.9 copy-done.27
  135.9 0.9 copy-done.29
  136.9 0.9 copy-done.31
  137.8 0.9 copy-done.33
  138.8 9.9 %expert.3 = (bf16[32,4096]{1,0:T(8,128)(2,1)S(1)}, bf16[32,4096]{1,0:T(8,128)(2,1)S(1)}, bf16[32,4096]{1,0:T(8,128)(2,1)S(1)}, bf16[32,4096]{1,0:T(8,128)(2,1)S(...) custom-call(bf16[32,4096]{1,0:T(8,128)(2,1)S(1)} %copy-done.21, ...), custom_call_target="tpu_custom_call" | custom-call | flops 1024 | bytes 1024 | tf_op jit(solution)/shard_map/expert/pallas_call | solution.py:26
  148.8 4.0 %weight_part.4 = (bf16[16,2176]{1,0:T(8,128)(2,1)S(1)}, bf16[496,2176]{1,0:T(8,128)(2,1)}) custom-call(s32[1]{0:T(128)} %bitcast.5.refs_0_, bf16[256,4096]{1,0:T(8,128)(2,1)S(1)} %get-tuple-element.135.refs_1_, bf16[256,1408]{1,0:T(8,128)(2,1)S(1)} %get-tuple-element.126.refs_2_, bf16[256,704]{1,0:T(8,128)(2,1)S(1)} %copy-done.10, ...), custom_call_target="tpu_custom_call" | custom-call | flops 1024 | bytes 1024 | tf_op jit(solution)/shard_map/weight_part/pallas_call | solution.py:26
  153.0 1.2 collective-permute-done.21.refs_7_
  155.0 3.6 %collective-permute-start.16 = (bf16[32,4096]{1,0:T(8,128)(2,1)}, bf16[32,4096]{1,0:T(8,128)(2,1)}, u32[]{:S(2)}, u32[]{:S(2)}) collective-permute-start(bf16[32,4096]{1,0:T(8,128)(2,1)} %get-tuple-element.112), channel_id=1, source_target_pairs={{0,3},{1,2},{2,1},{3,0},{4,7},{5,6},{6,5},{7,4},{8,11},{9,10},{10,... | collective-permute-start | bytes 786440 | tf_op jit(solution)/shard_map/ppermute | solution.py:210
  158.7 2.2 collective-permute-start.13
  160.9 9.8 %collective-permute-done.9.refs_8_ = bf16[32,4096]{1,0:T(8,128)(2,1)} collective-permute-done((bf16[32,4096]{1,0:T(8,128)(2,1)}, bf16[32,4096]{1,0:T(8,128)(2,1)}, u32[]{:S(2)}, u32[]{:S(2)}) %collective-permute-start.9) | collective-permute-done | bytes 262176 | tf_op jit(solution)/shard_map/ppermute | solution.py:197
  170.7 1.3 collective-permute-done.16.refs_6_
  172.0 1.6 copy-done.1
  173.6 1.0 copy-done.11
  174.6 1.0 copy-done.14
  175.6 0.9 copy-done.35
  176.4 5.6 %weight_part.5 = bf16[512,2176]{1,0:T(8,128)(2,1)} custom-call(s32[1]{0:T(128)} %bitcast.4.refs_0_, bf16[256,4096]{1,0:T(8,128)(2,1)S(1)} %get-tuple-element.135.refs_1_, bf16[256,1408]{1,0:T(8,128)(2,1)S(1)} %get-tuple-element.126.refs_2_, bf16[256,704]{1,0:T(8,128)(2,1)S(1)} %copy-done.11, bf16[256,4096]{1,0:T(8,128)(2,1)S(1)} %copy-done.1, ...), custom_call_target="tpu_custom_call" | custom-call | flops 1024 | bytes 1024 | tf_op jit(solution)/shard_map/weight_part/pallas_call | solution.py:26
  182.1 1.5 collective-permute-start.23
  183.6 1.6 copy-done.2
  185.2 1.0 copy-done.12
  186.2 1.0 copy-done.15
  187.2 2.9 %weight_part.6 = bf16[512,2176]{1,0:T(8,128)(2,1)S(1)} custom-call(s32[1]{0:T(128)} %bitcast.6.refs_0_, bf16[256,4096]{1,0:T(8,128)(2,1)S(1)} %get-tuple-element.135.refs_1_, bf16[256,1408]{1,0:T(8,128)(2,1)S(1)} %get-tuple-element.126.refs_2_, bf16[256,704]{1,0:T(8,128)(2,1)S(1)} %copy-done.12, bf16[256,4096]{1,0:T(8,128)(2,1)S(1)} %copy-done.2, ...), custom_call_target="tpu_custom_call" | custom-call | flops 1024 | bytes 1024 | tf_op jit(solution)/shard_map/weight_part/pallas_call | solution.py:26
  190.8 3.2 %collective-permute-start.29 = (bf16[32,4096]{1,0:T(8,128)(2,1)S(1)}, bf16[32,4096]{1,0:T(8,128)(2,1)S(1)}, u32[]{:S(2)}, u32[]{:S(2)}) collective-permute-start(bf16[32,4096]{1,0:T(8,128)(2,1)S(1)} %copy-done.51), channel_id=1, source_target_pairs={{0,7},{1,6},{2,5},{3,4},{4,3},{5,2},{6,1},{7,0},{8,15},{9,14},{10,... | collective-permute-start | bytes 786440 | tf_op jit(solution)/shard_map/ppermute | solution.py:197
  194.0 1.6 collective-permute-start.27
  195.6 9.0 %collective-permute-done.10.refs_4_ = bf16[32,4096]{1,0:T(8,128)(2,1)S(1)} collective-permute-done((bf16[32,4096]{1,0:T(8,128)(2,1)S(1)}, bf16[32,4096]{1,0:T(8,128)(2,1)S(1)}, u32[]{:S(2)}, u32[]{:S(2)}) %collective-permute-start.10) | collective-permute-done | bytes 262176 | tf_op jit(solution)/shard_map/ppermute | solution.py:210
  204.6 2.9 %combine.2 = (bf16[256,2048]{1,0:T(8,128)(2,1)S(1)}, bf16[256,2048]{1,0:T(8,128)(2,1)S(1)}) custom-call(s32[1,256]{1,0:T(1,128)S(1)} %xor_bitcast_fusion.refs_0_, bf16[256,2048]{1,0:T(8,128)(2,1)S(1)} %copy-done.6, bf16[256,2048]{1,0:T(8,128)(2,1)S(1)} %copy-done.8, bf16[32,4096]{1,0:T(8,128)(2,1)S(1)} %copy-done.19, ...), custom_call_target="tpu_custom_call" | custom-call | flops 1024 | bytes 1024 | tf_op jit(solution)/shard_map/combine/pallas_call | solution.py:26
  207.5 10.7 %collective-permute-start.30 = (bf16[32,4096]{1,0:T(8,128)(2,1)S(1)}, bf16[32,4096]{1,0:T(8,128)(2,1)S(1)}, u32[]{:S(2)}, u32[]{:S(2)}) collective-permute-start(bf16[32,4096]{1,0:T(8,128)(2,1)S(1)} %copy-done.43), channel_id=1, source_target_pairs={{0,3},{1,2},{2,1},{3,0},{4,7},{5,6},{6,5},{7,4},{8,11},{9,10},{10,... | collective-permute-start | bytes 786440 | tf_op jit(solution)/shard_map/ppermute | solution.py:210
  218.2 5.0 %collective-permute-start.31 = (bf16[32,4096]{1,0:T(8,128)(2,1)S(1)}, bf16[32,4096]{1,0:T(8,128)(2,1)S(1)}, u32[]{:S(2)}, u32[]{:S(2)}) collective-permute-start(bf16[32,4096]{1,0:T(8,128)(2,1)S(1)} %copy-done.41), channel_id=1, source_target_pairs={{0,4},{1,5},{2,6},{3,7},{4,0},{5,1},{6,2},{7,3},{8,12},{9,13},{10,... | collective-permute-start | bytes 786440 | tf_op jit(solution)/shard_map/ppermute | solution.py:197
  223.3 10.8 %collective-permute-done.25.refs_8_ = bf16[32,4096]{1,0:T(8,128)(2,1)S(1)} collective-permute-done((bf16[32,4096]{1,0:T(8,128)(2,1)S(1)}, bf16[32,4096]{1,0:T(8,128)(2,1)S(1)}, u32[]{:S(2)}, u32[]{:S(2)}) %collective-permute-start.25) | collective-permute-done | bytes 262176 | tf_op jit(solution)/shard_map/ppermute | solution.py:197
  234.1 1.1 collective-permute-start.26
  235.2 6.0 %weight_part.7 = (f32[512,1408]{1,0:T(8,128)}, f32[704,512]{1,0:T(8,128)}) custom-call(s32[1]{0:T(128)} %bitcast.3.refs_0_, bf16[256,4096]{1,0:T(8,128)(2,1)S(1)} %get-tuple-element.135.refs_1_, bf16[256,1408]{1,0:T(8,128)(2,1)S(1)} %get-tuple-element.126.refs_2_, bf16[256,704]{1,0:T(8,128)(2,1)S(1)} %copy-done.12, bf16[256,4096]{1,0:T(8,128)(2,1)S(1)} %copy-done.2, ...), custom_call_target="tpu_custom_call" | custom-call | flops 1024 | bytes 1024 | tf_op jit(solution)/shard_map/weight_part/pallas_call | solution.py:26
  241.2 2.9 %collective-permute-done.28.refs_5_ = bf16[32,4096]{1,0:T(8,128)(2,1)S(1)} collective-permute-done((bf16[32,4096]{1,0:T(8,128)(2,1)S(1)}, bf16[32,4096]{1,0:T(8,128)(2,1)S(1)}, u32[]{:S(2)}, u32[]{:S(2)}) %collective-permute-start.28) | collective-permute-done | bytes 262176 | tf_op jit(solution)/shard_map/ppermute | solution.py:210
  244.1 2.5 %combine.3 = (bf16[256,2048]{1,0:T(8,128)(2,1)}, bf16[256,2048]{1,0:T(8,128)(2,1)}) custom-call(s32[1,256]{1,0:T(1,128)S(1)} %xor_bitcast_fusion.refs_0_, bf16[256,2048]{1,0:T(8,128)(2,1)S(1)} %get-tuple-element.115.refs_1_, bf16[256,2048]{1,0:T(8,128)(2,1)S(1)} %get-tuple-element.116.refs_2_, bf16[32,4096]{1,0:T(8,128)(2,1)S(1)} %copy-done.17, ...), custom_call_target="tpu_custom_call" | custom-call | flops 1024 | bytes 1024 | tf_op jit(solution)/shard_map/combine/pallas_call | solution.py:26
  (115 shorter events, 5.6 us)
Async XLA Ops:
  0.6 90.5 %copy-start.3 = (bf16[1,704,2048]{2,1,0:T(8,128)(2,1)S(1)}, bf16[1,704,2048]{2,1,0:T(8,128)(2,1)}, u32[]{:S(2)}) copy-start(bf16[1,704,2048]{2,1,0:T(8,128)(2,1)} %param.8) | copy-start | bytes 8650756
  1.5 1.3 copy-start.5
  2.7 1.2 copy-start.7
  6.2 13.3 %collective-permute-start.4 = (bf16[32,4096]{1,0:T(8,128)(2,1)S(1)}, bf16[32,4096]{1,0:T(8,128)(2,1)S(1)}, u32[]{:S(2)}, u32[]{:S(2)}) collective-permute-start(bf16[32,4096]{1,0:T(8,128)(2,1)S(1)} %get-tuple-element.88), channel_id=1, source_target_pairs={{0,7},{1,6},{2,5},{3,4},{4,3},{5,2},{6,1},{7,0},{8,15},{9,14},{10,... | collective-permute-start | bytes 786440 | tf_op jit(solution)/shard_map/ppermute | solution.py:197
  12.2 34.5 %collective-permute-start = (bf16[32,4096]{1,0:T(8,128)(2,1)S(1)}, bf16[32,4096]{1,0:T(8,128)(2,1)S(1)}, u32[]{:S(2)}, u32[]{:S(2)}) collective-permute-start(bf16[32,4096]{1,0:T(8,128)(2,1)S(1)} %get-tuple-element.82), channel_id=1, source_target_pairs={{0,5},{1,4},{2,7},{3,6},{4,1},{5,0},{6,3},{7,2},{8,13},{9,12},{10,... | collective-permute-start | bytes 786440 | tf_op jit(solution)/shard_map/ppermute | solution.py:197
  12.2 37.1 %collective-permute-start.2 = (bf16[32,4096]{1,0:T(8,128)(2,1)S(1)}, bf16[32,4096]{1,0:T(8,128)(2,1)S(1)}, u32[]{:S(2)}, u32[]{:S(2)}) collective-permute-start(bf16[32,4096]{1,0:T(8,128)(2,1)S(1)} %get-tuple-element.85), channel_id=1, source_target_pairs={{0,6},{1,7},{2,4},{3,5},{4,2},{5,3},{6,0},{7,1},{8,14},{9,15},{10,... | collective-permute-start | bytes 786440 | tf_op jit(solution)/shard_map/ppermute | solution.py:197
  19.5 49.7 %collective-permute-start.6 = (bf16[32,4096]{1,0:T(8,128)(2,1)S(1)}, bf16[32,4096]{1,0:T(8,128)(2,1)S(1)}, u32[]{:S(2)}, u32[]{:S(2)}) collective-permute-start(bf16[32,4096]{1,0:T(8,128)(2,1)S(1)} %get-tuple-element.91), channel_id=1, source_target_pairs={{0,4},{1,5},{2,6},{3,7},{4,0},{5,1},{6,2},{7,3},{8,12},{9,13},{10,... | collective-permute-start | bytes 786440 | tf_op jit(solution)/shard_map/ppermute | solution.py:197
  46.7 22.5 %collective-permute-start.14 = (bf16[32,4096]{1,0:T(8,128)(2,1)S(1)}, bf16[32,4096]{1,0:T(8,128)(2,1)S(1)}, u32[]{:S(2)}, u32[]{:S(2)}) collective-permute-start(bf16[32,4096]{1,0:T(8,128)(2,1)S(1)} %get-tuple-element.110), channel_id=1, source_target_pairs={{0,6},{1,7},{2,4},{3,5},{4,2},{5,3},{6,0},{7,1},{8,14},{9,15},{10,... | collective-permute-start | bytes 786440 | tf_op jit(solution)/shard_map/ppermute | solution.py:197
  49.4 28.0 %collective-permute-start.7 = (bf16[32,4096]{1,0:T(8,128)(2,1)S(1)}, bf16[32,4096]{1,0:T(8,128)(2,1)S(1)}, u32[]{:S(2)}, u32[]{:S(2)}) collective-permute-start(bf16[32,4096]{1,0:T(8,128)(2,1)S(1)} %get-tuple-element.97), channel_id=1, source_target_pairs={{0,7},{1,6},{2,5},{3,4},{4,3},{5,2},{6,1},{7,0},{8,15},{9,14},{10,... | collective-permute-start | bytes 786440 | tf_op jit(solution)/shard_map/ppermute | solution.py:197
  51.4 38.9 %collective-permute-start.1 = (bf16[32,4096]{1,0:T(8,128)(2,1)S(1)}, bf16[32,4096]{1,0:T(8,128)(2,1)S(1)}, u32[]{:S(2)}, u32[]{:S(2)}) collective-permute-start(bf16[32,4096]{1,0:T(8,128)(2,1)S(1)} %get-tuple-element.83), channel_id=1, source_target_pairs={{0,1},{1,0},{2,3},{3,2},{4,5},{5,4},{6,7},{7,6},{8,9},{9,8},{10,11... | collective-permute-start | bytes 786440 | tf_op jit(solution)/shard_map/ppermute | solution.py:210
  52.0 39.1 %collective-permute-start.3 = (bf16[32,4096]{1,0:T(8,128)(2,1)S(1)}, bf16[32,4096]{1,0:T(8,128)(2,1)S(1)}, u32[]{:S(2)}, u32[]{:S(2)}) collective-permute-start(bf16[32,4096]{1,0:T(8,128)(2,1)S(1)} %get-tuple-element.86), channel_id=1, source_target_pairs={{0,2},{1,3},{2,0},{3,1},{4,6},{5,7},{6,4},{7,5},{8,10},{9,11},{10,... | collective-permute-start | bytes 786440 | tf_op jit(solution)/shard_map/ppermute | solution.py:210
  69.2 21.9 %collective-permute-start.5 = (bf16[32,4096]{1,0:T(8,128)(2,1)S(1)}, bf16[32,4096]{1,0:T(8,128)(2,1)S(1)}, u32[]{:S(2)}, u32[]{:S(2)}) collective-permute-start(bf16[32,4096]{1,0:T(8,128)(2,1)S(1)} %get-tuple-element.89), channel_id=1, source_target_pairs={{0,3},{1,2},{2,1},{3,0},{4,7},{5,6},{6,5},{7,4},{8,11},{9,10},{10,... | collective-permute-start | bytes 786440 | tf_op jit(solution)/shard_map/ppermute | solution.py:210
  69.9 37.3 %collective-permute-start.11 = (bf16[32,4096]{1,0:T(8,128)(2,1)S(1)}, bf16[32,4096]{1,0:T(8,128)(2,1)S(1)}, u32[]{:S(2)}, u32[]{:S(2)}) collective-permute-start(bf16[32,4096]{1,0:T(8,128)(2,1)S(1)} %get-tuple-element.104), channel_id=1, source_target_pairs={{0,5},{1,4},{2,7},{3,6},{4,1},{5,0},{6,3},{7,2},{8,13},{9,12},{10,... | collective-permute-start | bytes 786440 | tf_op jit(solution)/shard_map/ppermute | solution.py:197
  78.0 32.6 %collective-permute-start.19 = (bf16[32,4096]{1,0:T(8,128)(2,1)S(1)}, bf16[32,4096]{1,0:T(8,128)(2,1)S(1)}, u32[]{:S(2)}, u32[]{:S(2)}) collective-permute-start(bf16[32,4096]{1,0:T(8,128)(2,1)S(1)} %get-tuple-element.121), channel_id=1, source_target_pairs={{0,2},{1,3},{2,0},{3,1},{4,6},{5,7},{6,4},{7,5},{8,10},{9,11},{10,... | collective-permute-start | bytes 786440 | tf_op jit(solution)/shard_map/ppermute | solution.py:210
  90.3 23.7 %collective-permute-start.20 = (bf16[32,4096]{1,0:T(8,128)(2,1)}, bf16[32,4096]{1,0:T(8,128)(2,1)S(1)}, u32[]{:S(2)}, u32[]{:S(2)}) collective-permute-start(bf16[32,4096]{1,0:T(8,128)(2,1)} %get-tuple-element.123), channel_id=1, source_target_pairs={{0,3},{1,2},{2,1},{3,0},{4,7},{5,6},{6,5},{7,4},{8,11},{9,10},{10,... | collective-permute-start | bytes 786440 | tf_op jit(solution)/shard_map/ppermute | solution.py:210
  104.0 25.6 %collective-permute-start.8 = (bf16[32,4096]{1,0:T(8,128)(2,1)}, bf16[32,4096]{1,0:T(8,128)(2,1)S(1)}, u32[]{:S(2)}, u32[]{:S(2)}) collective-permute-start(bf16[32,4096]{1,0:T(8,128)(2,1)} %get-tuple-element.98), channel_id=1, source_target_pairs={{0,4},{1,5},{2,6},{3,7},{4,0},{5,1},{6,2},{7,3},{8,12},{9,13},{10,... | collective-permute-start | bytes 786440 | tf_op jit(solution)/shard_map/ppermute | solution.py:197
  108.0 22.3 %collective-permute-start.18 = (bf16[32,4096]{1,0:T(8,128)(2,1)}, bf16[32,4096]{1,0:T(8,128)(2,1)}, u32[]{:S(2)}, u32[]{:S(2)}) collective-permute-start(bf16[32,4096]{1,0:T(8,128)(2,1)} %get-tuple-element.119), channel_id=1, source_target_pairs={{0,1},{1,0},{2,3},{3,2},{4,5},{5,4},{6,7},{7,6},{8,9},{9,8},{10,11... | collective-permute-start | bytes 786440 | tf_op jit(solution)/shard_map/ppermute | solution.py:210
  108.5 44.6 %collective-permute-start.15 = (bf16[32,4096]{1,0:T(8,128)(2,1)}, bf16[32,4096]{1,0:T(8,128)(2,1)}, u32[]{:S(2)}, u32[]{:S(2)}) collective-permute-start(bf16[32,4096]{1,0:T(8,128)(2,1)} %get-tuple-element.111), channel_id=1, source_target_pairs={{0,7},{1,6},{2,5},{3,4},{4,3},{5,2},{6,1},{7,0},{8,15},{9,14},{10,... | collective-permute-start | bytes 786440 | tf_op jit(solution)/shard_map/ppermute | solution.py:197
  111.3 41.7 %collective-permute-start.12 = (bf16[32,4096]{1,0:T(8,128)(2,1)}, bf16[32,4096]{1,0:T(8,128)(2,1)}, u32[]{:S(2)}, u32[]{:S(2)}) collective-permute-start(bf16[32,4096]{1,0:T(8,128)(2,1)} %get-tuple-element.105), channel_id=1, source_target_pairs={{0,6},{1,7},{2,4},{3,5},{4,2},{5,3},{6,0},{7,1},{8,14},{9,15},{10,... | collective-permute-start | bytes 786440 | tf_op jit(solution)/shard_map/ppermute | solution.py:197
  130.3 1.8 copy-start.4
  138.8 10.1 %copy-start.10 = (bf16[256,704]{1,0:T(8,128)(2,1)S(1)}, bf16[256,704]{1,0:T(8,128)(2,1)}, u32[]{:S(2)}) copy-start(bf16[256,704]{1,0:T(8,128)(2,1)} %copy-done.9) | copy-start | bytes 1081348
  148.7 4.1 %copy-start = (bf16[256,4096]{1,0:T(8,128)(2,1)}, bf16[256,4096]{1,0:T(8,128)(2,1)S(1)}, u32[]{:S(2)}) copy-start(bf16[256,4096]{1,0:T(8,128)(2,1)S(1)} %get-tuple-element.128.refs_4_) | copy-start | bytes 6291460
  148.7 4.1 %copy-start.13 = (bf16[256,704]{1,0:T(8,128)(2,1)}, bf16[256,704]{1,0:T(8,128)(2,1)S(1)}, u32[]{:S(2)}) copy-start(bf16[256,704]{1,0:T(8,128)(2,1)S(1)} %get-tuple-element.130.refs_6_) | copy-start | bytes 1081348
  148.7 4.1 %copy-start.16 = (bf16[32,4096]{1,0:T(8,128)(2,1)}, bf16[32,4096]{1,0:T(8,128)(2,1)S(1)}, u32[]{:S(2)}) copy-start(bf16[32,4096]{1,0:T(8,128)(2,1)S(1)} %get-tuple-element.138.refs_3_) | copy-start | bytes 786436
  148.7 4.1 %copy-start.36 = (bf16[32,4096]{1,0:T(8,128)(2,1)}, bf16[32,4096]{1,0:T(8,128)(2,1)S(1)}, u32[]{:S(2)}) copy-start(bf16[32,4096]{1,0:T(8,128)(2,1)S(1)} %get-tuple-element.142) | copy-start | bytes 786436
  148.8 4.1 %copy-start.38 = (bf16[32,4096]{1,0:T(8,128)(2,1)}, bf16[32,4096]{1,0:T(8,128)(2,1)S(1)}, u32[]{:S(2)}) copy-start(bf16[32,4096]{1,0:T(8,128)(2,1)S(1)} %get-tuple-element.146) | copy-start | bytes 786436
  148.8 4.1 %copy-start.40 = (bf16[32,4096]{1,0:T(8,128)(2,1)}, bf16[32,4096]{1,0:T(8,128)(2,1)S(1)}, u32[]{:S(2)}) copy-start(bf16[32,4096]{1,0:T(8,128)(2,1)S(1)} %get-tuple-element.152) | copy-start | bytes 786436
  148.8 4.1 %copy-start.42 = (bf16[32,4096]{1,0:T(8,128)(2,1)}, bf16[32,4096]{1,0:T(8,128)(2,1)S(1)}, u32[]{:S(2)}) copy-start(bf16[32,4096]{1,0:T(8,128)(2,1)S(1)} %get-tuple-element.150) | copy-start | bytes 786436
  148.8 4.1 %copy-start.46 = (bf16[32,4096]{1,0:T(8,128)(2,1)}, bf16[32,4096]{1,0:T(8,128)(2,1)S(1)}, u32[]{:S(2)}) copy-start(bf16[32,4096]{1,0:T(8,128)(2,1)S(1)} %get-tuple-element.141) | copy-start | bytes 786436
  148.8 4.1 %copy-start.48 = (bf16[32,4096]{1,0:T(8,128)(2,1)}, bf16[32,4096]{1,0:T(8,128)(2,1)S(1)}, u32[]{:S(2)}) copy-start(bf16[32,4096]{1,0:T(8,128)(2,1)S(1)} %get-tuple-element.145) | copy-start | bytes 786436
  148.8 4.1 %copy-start.50 = (bf16[32,4096]{1,0:T(8,128)(2,1)}, bf16[32,4096]{1,0:T(8,128)(2,1)S(1)}, u32[]{:S(2)}) copy-start(bf16[32,4096]{1,0:T(8,128)(2,1)S(1)} %get-tuple-element.149) | copy-start | bytes 786436
  152.9 1.3 collective-permute-start.21
  154.9 17.1 %collective-permute-start.22 = (bf16[496,2176]{1,0:T(8,128)(2,1)}, bf16[496,2176]{1,0:T(8,128)(2,1)}, u32[]{:S(2)}, u32[]{:S(2)}) collective-permute-start(bf16[496,2176]{1,0:T(8,128)(2,1)} %get-tuple-element.134), channel_id=1, source_target_pairs={{0,8},{8,0},{16,24},{24,16},{1,9},{9,1},{17,25},{25,17},{2,10},{10... | collective-permute-start | bytes 6475784 | tf_op jit(solution)/shard_map/ppermute | solution.py:197
  155.0 15.7 %collective-permute-start.9 = (bf16[32,4096]{1,0:T(8,128)(2,1)}, bf16[32,4096]{1,0:T(8,128)(2,1)}, u32[]{:S(2)}, u32[]{:S(2)}) collective-permute-start(bf16[32,4096]{1,0:T(8,128)(2,1)} %get-tuple-element.99), channel_id=1, source_target_pairs={{0,5},{1,4},{2,7},{3,6},{4,1},{5,0},{6,3},{7,2},{8,13},{9,12},{10,... | collective-permute-start | bytes 786440 | tf_op jit(solution)/shard_map/ppermute | solution.py:197
  155.0 16.9 %collective-permute-start.16 = (bf16[32,4096]{1,0:T(8,128)(2,1)}, bf16[32,4096]{1,0:T(8,128)(2,1)}, u32[]{:S(2)}, u32[]{:S(2)}) collective-permute-start(bf16[32,4096]{1,0:T(8,128)(2,1)} %get-tuple-element.112), channel_id=1, source_target_pairs={{0,3},{1,2},{2,1},{3,0},{4,7},{5,6},{6,5},{7,4},{8,11},{9,10},{10,... | collective-permute-start | bytes 786440 | tf_op jit(solution)/shard_map/ppermute | solution.py:210
  158.6 25.0 %collective-permute-start.17 = (bf16[32,4096]{1,0:T(8,128)(2,1)}, bf16[32,4096]{1,0:T(8,128)(2,1)}, u32[]{:S(2)}, u32[]{:S(2)}) collective-permute-start(bf16[32,4096]{1,0:T(8,128)(2,1)} %get-tuple-element.114), channel_id=1, source_target_pairs={{0,4},{1,5},{2,6},{3,7},{4,0},{5,1},{6,2},{7,3},{8,12},{9,13},{10,... | collective-permute-start | bytes 786440 | tf_op jit(solution)/shard_map/ppermute | solution.py:197
  158.7 25.0 %collective-permute-start.13 = (bf16[32,4096]{1,0:T(8,128)(2,1)}, bf16[32,4096]{1,0:T(8,128)(2,1)}, u32[]{:S(2)}, u32[]{:S(2)}) collective-permute-start(bf16[32,4096]{1,0:T(8,128)(2,1)} %get-tuple-element.106), channel_id=1, source_target_pairs={{0,2},{1,3},{2,0},{3,1},{4,6},{5,7},{6,4},{7,5},{8,10},{9,11},{10,... | collective-permute-start | bytes 786440 | tf_op jit(solution)/shard_map/ppermute | solution.py:210
  172.0 1.6 copy-start.1
  173.6 1.0 copy-start.11
  174.6 1.0 copy-start.14
  182.1 52.0 %collective-permute-start.23 = (bf16[512,2176]{1,0:T(8,128)(2,1)}, bf16[512,2176]{1,0:T(8,128)(2,1)}, u32[]{:S(2)}, u32[]{:S(2)}) collective-permute-start(bf16[512,2176]{1,0:T(8,128)(2,1)} %weight_part.5), channel_id=1, source_target_pairs={{0,16},{8,24},{16,0},{24,8},{1,17},{9,25},{17,1},{25,9},{2,18},{10... | collective-permute-start | bytes 6684680 | tf_op jit(solution)/shard_map/ppermute | solution.py:197
  183.6 1.6 copy-start.2
  185.2 1.0 copy-start.12
  187.2 3.1 %copy-start.45 = (bf16[32,4096]{1,0:T(8,128)(2,1)S(1)}, bf16[32,4096]{1,0:T(8,128)(2,1)}, u32[]{:S(2)}) copy-start(bf16[32,4096]{1,0:T(8,128)(2,1)} %copy-done.44) | copy-start | bytes 786436
  187.2 3.6 %copy-start.51 = (bf16[32,4096]{1,0:T(8,128)(2,1)S(1)}, bf16[32,4096]{1,0:T(8,128)(2,1)}, u32[]{:S(2)}) copy-start(bf16[32,4096]{1,0:T(8,128)(2,1)} %copy-done.50) | copy-start | bytes 786436
  187.2 6.8 %copy-start.49 = (bf16[32,4096]{1,0:T(8,128)(2,1)S(1)}, bf16[32,4096]{1,0:T(8,128)(2,1)}, u32[]{:S(2)}) copy-start(bf16[32,4096]{1,0:T(8,128)(2,1)} %copy-done.48) | copy-start | bytes 786436
  187.2 17.4 %copy-start.47 = (bf16[32,4096]{1,0:T(8,128)(2,1)S(1)}, bf16[32,4096]{1,0:T(8,128)(2,1)}, u32[]{:S(2)}) copy-start(bf16[32,4096]{1,0:T(8,128)(2,1)} %copy-done.46) | copy-start | bytes 786436
  187.2 17.4 %copy-start.6 = (bf16[256,2048]{1,0:T(8,128)(2,1)S(1)}, bf16[256,2048]{1,0:T(8,128)(2,1)}, u32[]{:S(2)}) copy-start(bf16[256,2048]{1,0:T(8,128)(2,1)} %refs_1_.5) | copy-start | bytes 3145732
  187.2 17.4 %copy-start.8 = (bf16[256,2048]{1,0:T(8,128)(2,1)S(1)}, bf16[256,2048]{1,0:T(8,128)(2,1)}, u32[]{:S(2)}) copy-start(bf16[256,2048]{1,0:T(8,128)(2,1)} %refs_2_.5) | copy-start | bytes 3145732
  187.2 17.4 %copy-start.19 = (bf16[32,4096]{1,0:T(8,128)(2,1)S(1)}, bf16[32,4096]{1,0:T(8,128)(2,1)}, u32[]{:S(2)}) copy-start(bf16[32,4096]{1,0:T(8,128)(2,1)} %copy-done.18) | copy-start | bytes 786436
  190.1 17.4 %copy-start.43 = (bf16[32,4096]{1,0:T(8,128)(2,1)S(1)}, bf16[32,4096]{1,0:T(8,128)(2,1)}, u32[]{:S(2)}) copy-start(bf16[32,4096]{1,0:T(8,128)(2,1)} %copy-done.42) | copy-start | bytes 786436
  190.1 28.1 %copy-start.41 = (bf16[32,4096]{1,0:T(8,128)(2,1)S(1)}, bf16[32,4096]{1,0:T(8,128)(2,1)}, u32[]{:S(2)}) copy-start(bf16[32,4096]{1,0:T(8,128)(2,1)} %copy-done.40) | copy-start | bytes 786436
  190.2 43.9 %copy-start.39 = (bf16[32,4096]{1,0:T(8,128)(2,1)S(1)}, bf16[32,4096]{1,0:T(8,128)(2,1)}, u32[]{:S(2)}) copy-start(bf16[32,4096]{1,0:T(8,128)(2,1)} %copy-done.38) | copy-start | bytes 786436
  190.2 43.9 %copy-start.37 = (bf16[32,4096]{1,0:T(8,128)(2,1)S(1)}, bf16[32,4096]{1,0:T(8,128)(2,1)}, u32[]{:S(2)}) copy-start(bf16[32,4096]{1,0:T(8,128)(2,1)} %copy-done.36) | copy-start | bytes 786436
  190.2 45.0 %collective-permute-start.24 = (bf16[512,2176]{1,0:T(8,128)(2,1)S(1)}, bf16[512,2176]{1,0:T(8,128)(2,1)S(1)}, u32[]{:S(2)}, u32[]{:S(2)}) collective-permute-start(bf16[512,2176]{1,0:T(8,128)(2,1)S(1)} %weight_part.6), channel_id=1, source_target_pairs={{0,8},{8,0},{16,24},{24,16},{1,9},{9,1},{17,25},{25,17},{2,10},{10... | collective-permute-start | bytes 6684680 | tf_op jit(solution)/shard_map/ppermute | solution.py:197
  190.3 14.3 %collective-permute-start.10 = (bf16[32,4096]{1,0:T(8,128)(2,1)S(1)}, bf16[32,4096]{1,0:T(8,128)(2,1)S(1)}, u32[]{:S(2)}, u32[]{:S(2)}) collective-permute-start(bf16[32,4096]{1,0:T(8,128)(2,1)S(1)} %copy-done.45), channel_id=1, source_target_pairs={{0,1},{1,0},{2,3},{3,2},{4,5},{5,4},{6,7},{7,6},{8,9},{9,8},{10,11... | collective-permute-start | bytes 786440 | tf_op jit(solution)/shard_map/ppermute | solution.py:210
  190.8 16.7 %collective-permute-start.29 = (bf16[32,4096]{1,0:T(8,128)(2,1)S(1)}, bf16[32,4096]{1,0:T(8,128)(2,1)S(1)}, u32[]{:S(2)}, u32[]{:S(2)}) collective-permute-start(bf16[32,4096]{1,0:T(8,128)(2,1)S(1)} %copy-done.51), channel_id=1, source_target_pairs={{0,7},{1,6},{2,5},{3,4},{4,3},{5,2},{6,1},{7,0},{8,15},{9,14},{10,... | collective-permute-start | bytes 786440 | tf_op jit(solution)/shard_map/ppermute | solution.py:197
  194.0 24.2 %collective-permute-start.27 = (bf16[32,4096]{1,0:T(8,128)(2,1)S(1)}, bf16[32,4096]{1,0:T(8,128)(2,1)S(1)}, u32[]{:S(2)}, u32[]{:S(2)}) collective-permute-start(bf16[32,4096]{1,0:T(8,128)(2,1)S(1)} %copy-done.49), channel_id=1, source_target_pairs={{0,6},{1,7},{2,4},{3,5},{4,2},{5,3},{6,0},{7,1},{8,14},{9,15},{10,... | collective-permute-start | bytes 786440 | tf_op jit(solution)/shard_map/ppermute | solution.py:197
  204.6 29.4 %collective-permute-start.25 = (bf16[32,4096]{1,0:T(8,128)(2,1)S(1)}, bf16[32,4096]{1,0:T(8,128)(2,1)S(1)}, u32[]{:S(2)}, u32[]{:S(2)}) collective-permute-start(bf16[32,4096]{1,0:T(8,128)(2,1)S(1)} %copy-done.47), channel_id=1, source_target_pairs={{0,5},{1,4},{2,7},{3,6},{4,1},{5,0},{6,3},{7,2},{8,13},{9,12},{10,... | collective-permute-start | bytes 786440 | tf_op jit(solution)/shard_map/ppermute | solution.py:197
  207.5 33.7 %collective-permute-start.30 = (bf16[32,4096]{1,0:T(8,128)(2,1)S(1)}, bf16[32,4096]{1,0:T(8,128)(2,1)S(1)}, u32[]{:S(2)}, u32[]{:S(2)}) collective-permute-start(bf16[32,4096]{1,0:T(8,128)(2,1)S(1)} %copy-done.43), channel_id=1, source_target_pairs={{0,3},{1,2},{2,1},{3,0},{4,7},{5,6},{6,5},{7,4},{8,11},{9,10},{10,... | collective-permute-start | bytes 786440 | tf_op jit(solution)/shard_map/ppermute | solution.py:210
  218.2 23.0 %collective-permute-start.31 = (bf16[32,4096]{1,0:T(8,128)(2,1)S(1)}, bf16[32,4096]{1,0:T(8,128)(2,1)S(1)}, u32[]{:S(2)}, u32[]{:S(2)}) collective-permute-start(bf16[32,4096]{1,0:T(8,128)(2,1)S(1)} %copy-done.41), channel_id=1, source_target_pairs={{0,4},{1,5},{2,6},{3,7},{4,0},{5,1},{6,2},{7,3},{8,12},{9,13},{10,... | collective-permute-start | bytes 786440 | tf_op jit(solution)/shard_map/ppermute | solution.py:197
  234.0 10.0 %collective-permute-start.28 = (bf16[32,4096]{1,0:T(8,128)(2,1)S(1)}, bf16[32,4096]{1,0:T(8,128)(2,1)S(1)}, u32[]{:S(2)}, u32[]{:S(2)}) collective-permute-start(bf16[32,4096]{1,0:T(8,128)(2,1)S(1)} %copy-done.39), channel_id=1, source_target_pairs={{0,2},{1,3},{2,0},{3,1},{4,6},{5,7},{6,4},{7,5},{8,10},{9,11},{10,... | collective-permute-start | bytes 786440 | tf_op jit(solution)/shard_map/ppermute | solution.py:210
  234.1 10.0 %collective-permute-start.26 = (bf16[32,4096]{1,0:T(8,128)(2,1)S(1)}, bf16[32,4096]{1,0:T(8,128)(2,1)S(1)}, u32[]{:S(2)}, u32[]{:S(2)}) collective-permute-start(bf16[32,4096]{1,0:T(8,128)(2,1)S(1)} %copy-done.37), channel_id=1, source_target_pairs={{0,1},{1,0},{2,3},{3,2},{4,5},{5,4},{6,7},{7,6},{8,9},{9,8},{10,11... | collective-permute-start | bytes 786440 | tf_op jit(solution)/shard_map/ppermute | solution.py:210
  235.2 8.9 %copy-start.17 = (bf16[32,4096]{1,0:T(8,128)(2,1)S(1)}, bf16[32,4096]{1,0:T(8,128)(2,1)}, u32[]{:S(2)}) copy-start(bf16[32,4096]{1,0:T(8,128)(2,1)} %copy-done.16) | copy-start | bytes 786436
  (20 other events, 16.3 us)

commit v5 on v4

--- a/solution.py
+++ b/solution.py
@@ -202,12 +202,13 @@
     experts = len(blocks)
     half = experts // 2
     moved = {0: blocks[0]}
+    earlier = far.done[-1:]
     for mask in range(half - 1, -1, -1):
         pairs = [(i, i ^ (mask + half)) for i in range(experts)]
         moved[mask + half] = far.send(blocks[mask + half], "exp", pairs, *held.get(mask, ()))
-        if mask:
-            pairs = [(i, i ^ mask) for i in range(experts)]
-            moved[mask] = lax.ppermute(after(blocks[mask], far.done[-1]), "exp", pairs)
+    for mask in range(half - 1, 0, -1):
+        pairs = [(i, i ^ mask) for i in range(experts)]
+        moved[mask] = lax.ppermute(after(blocks[mask], *earlier), "exp", pairs)
     return [moved[mask] for mask in range(experts)]
 
 
@@ -225,7 +226,7 @@
     share = width // groups
     pair = like((cap, 2 * width))
     sems = pltpu.SemaphoreType.DMA
-    far = Lane(3)
+    far = Lane(2)
     rel = expert_ids.reshape(1, rows) ^ lax.axis_index("exp").astype(jnp.int32)
     group = lax.axis_index("grp").astype(jnp.int32)
 
@@ -233,7 +234,7 @@
         return call(
             lambda *refs: place_kernel(part, cap, *refs),
             "place",
-            20,
+            slots * 5 // 128,
             [pair] * experts,
             [pltpu.VMEM((rows, 2 * width), BF16), pltpu.VMEM((slots, 2 * width), BF16), sems((2 + 2 * experts,))],
             [tokens, grad_out],
@@ -247,7 +248,7 @@
         outs = call(
             expert_kernel,
             "expert",
-            44,
+            2 + slots * 5 // 64,
             [pair] * experts + [like(shape) for shape in shapes],
             scratch + back + [sems((5 + 2 * experts,))],
             [*blocks, weight_one, weight_two],
@@ -269,7 +270,7 @@
         return call(
             lambda *refs: weight_kernel(end, parts, pieces, *refs),
             "weight_part",
-            32,
+            18,
             outs,
             scratch,
             sources,
@@ -280,7 +281,7 @@
         return call(
             lambda *refs: combine_kernel(part, cap, *refs),
             "combine",
-            20,
+            slots * 5 // 128,
             [like((rows, width))] * 2,
             [pltpu.VMEM((rows, 2 * width), BF16), pltpu.VMEM((slots, 2 * width), BF16), sems((4 + experts,))],
             [first, second, *blocks],
@@ -298,28 +299,25 @@
     back = [exchange(results[0][0], far)]
     far_out = far.done[count:]
     near_out = back[0][experts // 2 - 1 : 0 : -1]
-    gates = iter([[], far_out[2:3] + near_out[:1], far_out[3:] + near_out[1:2]])
-    lanes = {}
-
-    def weight_sum(q, bit):
-        received = []
-        low = bit // 2
-        while low:
-            pairs = [(i, i ^ low) for i in range(groups)]
-            lane = lanes.setdefault(low, Lane(1))
-            head, *rest = weight_sum(q | low, low)
-            head = lane.send(head, "grp", pairs)
-            received.append([head] + [lane.send(piece, "grp", pairs, *far_out[:2]) for piece in rest])
-            low //= 2
-        first = after(kept[0][0], *([] if bit == groups else next(gates, [])))
-        heads = 16 if q == groups - 1 else 0
-        return weight_part(group ^ q, [[first, *kept[0][1:]], *kept[1:]], received, bit == groups, heads)
-
-    grad_gate_up, grad_down = weight_sum(0, groups)
+
+    received = {q: [] for q in range(groups)}
+    sums = kept[0][0]
+    for q in sorted(range(1, groups), key=lambda q: (q & -q, -q)):
+        low = q & -q
+        first_of_all = q == groups - 1
+        if low == 2 and received[q ^ low]:
+            sums = after(sums, *far_out[2:3], *near_out[:1])
+        sent = weight_part(group ^ q, [[sums, *kept[0][1:]], *kept[1:]], received[q], False, 16 if first_of_all else 0)
+        sums = after(sums, sent[0])
+        lane = Lane(1)
+        pairs = [(i, i ^ low) for i in range(groups)]
+        received[q ^ low].append([lane.send(piece, "grp", pairs, *(far_out[:2] if index else ())) for index, piece in enumerate(sent)])
+
     mixed, grad = tokens, grad_out
     for part in range(1, parts):
         mixed, grad = combine(part - 1, mixed, grad, back[-1])
-        back.append(exchange(results[part][0], far, {0: (mixed,)}))
+        back.append(exchange(results[part][0], far, {0: (mixed, *received[0][-1])}))
+    grad_gate_up, grad_down = weight_part(group, [[sums, *kept[0][1:]], *kept[1:]], received[0], True, 0)
     back[-1][0] = after(back[-1][0], grad_gate_up)
     mixed, grad = combine(parts - 1, mixed, grad, back[-1])
     return (mixed, grad, grad_gate_up[None], grad_down[None])

time: 248 us -> 243 us (0.980)
  starting transfers between devices: 105 us -> 84 us
  waiting for transfers between devices: 63.4 us -> 83.5 us
  Pallas kernels: 49.3 us -> 43.6 us
    ppermute x12, starting transfers between devices: 47.7 us -> 22 us  [exchange(): moved[mask] = lax.ppermute(after(blocks[mask], *earlier), 'exp', pairs)]
    ppermute x20, waiting for transfers between devices: 50.3 us -> 64.4 us  [send(): self.done.append(lax.ppermute(after(value, *earlier), axis, pairs))]
    ppermute x12, waiting for transfers between devices: 13.1 us -> 19.1 us  [exchange(): moved[mask] = lax.ppermute(after(blocks[mask], *earlier), 'exp', pairs)]
    pallas_call x10, Pallas kernels: 49.3 us -> 43.6 us  [call(): pl.pallas_call(kernel, in_specs=[pl.BlockSpec(memory_space=pltpu.SMEM)] *...]
    ppermute x20, starting transfers between devices: 57.4 us -> 61.9 us  [send(): self.done.append(lax.ppermute(after(value, *earlier), axis, pairs))]
    unnamed x104 -> x110, local copies, waits for them, and re-layouts: 26.8 us -> 29.1 us
  transfers between devices with their start and end apart: 32 -> 32, of which waited for: 10 -> 14; matrix products, arithmetic and copies ran while one was open for 0% -> 0% of each run, Pallas kernels for 18% -> 14%
where the time goes in v5:
time: 243 us; the launch traced here: 242 us
  starting transfers between devices  84 us (35%)
  waiting for transfers between devices  83.5 us (34%)
  Pallas kernels  43.6 us (18%)
  local copies, waits for them, and re-layouts  29.1 us (12%)
    ppermute x20, waiting for transfers between devices, send(): self.done.append(lax.ppermute(after(value, *earlier), axis, pairs))  64.4 us
    ppermute x20, starting transfers between devices, send(): self.done.append(lax.ppermute(after(value, *earlier), axis, pairs))  61.9 us
    pallas_call x10, Pallas kernels, call(): pl.pallas_call(kernel, in_specs=[pl.BlockSpec(memory_space=pltpu.SMEM)] *...  43.6 us
    unnamed x110, local copies, waits for them, and re-layouts  29.1 us
    ppermute x12, starting transfers between devices, exchange(): moved[mask] = lax.ppermute(after(blocks[mask], *earlier), 'exp', pairs)  22 us
    ppermute x12, waiting for transfers between devices, exchange(): moved[mask] = lax.ppermute(after(blocks[mask], *earlier), 'exp', pairs)  19.1 us
  transfers between devices with their start and end apart: 32, of which 14 were waited for; matrix products, arithmetic and copies ran while one was open for 0% of the time, Pallas kernels for 14%

profile of v5, /device:TPU:0, one launch (start us, length us, event | category | flops | bytes accessed | tf_op | source)
XLA Modules:
  0.0 242.3 jit_solution(5071222216079759532)
XLA Ops:
  0.6 0.8 xor_bitcast_fusion.refs_0_
  1.5 1.3 copy-done.6
  2.7 1.2 copy-done.8
  4.0 2.2 place.2
  6.2 6.1 %collective-permute-start.5 = (bf16[32,4096]{1,0:T(8,128)(2,1)S(1)}, bf16[32,4096]{1,0:T(8,128)(2,1)S(1)}, u32[]{:S(2)}, u32[]{:S(2)}) collective-permute-start(bf16[32,4096]{1,0:T(8,128)(2,1)S(1)} %get-tuple-element.87), channel_id=1, source_target_pairs={{0,7},{1,6},{2,5},{3,4},{4,3},{5,2},{6,1},{7,0},{8,15},{9,14},{10,... | collective-permute-start | bytes 786440 | tf_op jit(solution)/shard_map/ppermute | solution.py:197
  12.5 7.0 %collective-permute-done.5.refs_7_ = bf16[32,4096]{1,0:T(8,128)(2,1)S(1)} collective-permute-done((bf16[32,4096]{1,0:T(8,128)(2,1)S(1)}, bf16[32,4096]{1,0:T(8,128)(2,1)S(1)}, u32[]{:S(2)}, u32[]{:S(2)}) %collective-permute-start.5) | collective-permute-done | bytes 262176 | tf_op jit(solution)/shard_map/ppermute | solution.py:197
  19.5 13.1 %collective-permute-start.6 = (bf16[32,4096]{1,0:T(8,128)(2,1)S(1)}, bf16[32,4096]{1,0:T(8,128)(2,1)S(1)}, u32[]{:S(2)}, u32[]{:S(2)}) collective-permute-start(bf16[32,4096]{1,0:T(8,128)(2,1)S(1)} %get-tuple-element.88), channel_id=1, source_target_pairs={{0,5},{1,4},{2,7},{3,6},{4,1},{5,0},{6,3},{7,2},{8,13},{9,12},{10,... | collective-permute-start | bytes 786440 | tf_op jit(solution)/shard_map/ppermute | solution.py:197
  32.6 10.3 %collective-permute-start.4 = (bf16[32,4096]{1,0:T(8,128)(2,1)S(1)}, bf16[32,4096]{1,0:T(8,128)(2,1)S(1)}, u32[]{:S(2)}, u32[]{:S(2)}) collective-permute-start(bf16[32,4096]{1,0:T(8,128)(2,1)S(1)} %get-tuple-element.85), channel_id=1, source_target_pairs={{0,4},{1,5},{2,6},{3,7},{4,0},{5,1},{6,2},{7,3},{8,12},{9,13},{10,... | collective-permute-start | bytes 786440 | tf_op jit(solution)/shard_map/ppermute | solution.py:197
  43.4 3.0 %collective-permute-start.2 = (bf16[32,4096]{1,0:T(8,128)(2,1)S(1)}, bf16[32,4096]{1,0:T(8,128)(2,1)S(1)}, u32[]{:S(2)}, u32[]{:S(2)}) collective-permute-start(bf16[32,4096]{1,0:T(8,128)(2,1)S(1)} %get-tuple-element.82), channel_id=1, source_target_pairs={{0,3},{1,2},{2,1},{3,0},{4,7},{5,6},{6,5},{7,4},{8,11},{9,10},{10,... | collective-permute-start | bytes 786440 | tf_op jit(solution)/shard_map/ppermute | solution.py:211
  46.4 2.5 %place.3 = (bf16[32,4096]{1,0:T(8,128)(2,1)S(1)}, bf16[32,4096]{1,0:T(8,128)(2,1)}, bf16[32,4096]{1,0:T(8,128)(2,1)}, bf16[32,4096]{1,0:T(8,128)(2,1)}, bf16[32,...) custom-call(s32[1,256]{1,0:T(1,128)S(1)} %xor_bitcast_fusion.refs_0_, ...), custom_call_target="tpu_custom_call" | custom-call | flops 1024 | bytes 1024 | tf_op jit(solution)/shard_map/place/pallas_call | solution.py:26
  49.6 2.8 %collective-permute-done.6.refs_5_ = bf16[32,4096]{1,0:T(8,128)(2,1)S(1)} collective-permute-done((bf16[32,4096]{1,0:T(8,128)(2,1)S(1)}, bf16[32,4096]{1,0:T(8,128)(2,1)S(1)}, u32[]{:S(2)}, u32[]{:S(2)}) %collective-permute-start.6) | collective-permute-done | bytes 262176 | tf_op jit(solution)/shard_map/ppermute | solution.py:197
  52.4 3.6 %collective-permute-start.14 = (bf16[32,4096]{1,0:T(8,128)(2,1)S(1)}, bf16[32,4096]{1,0:T(8,128)(2,1)S(1)}, u32[]{:S(2)}, u32[]{:S(2)}) collective-permute-start(bf16[32,4096]{1,0:T(8,128)(2,1)S(1)} %get-tuple-element.108), channel_id=1, source_target_pairs={{0,7},{1,6},{2,5},{3,4},{4,3},{5,2},{6,1},{7,0},{8,15},{9,14},{10,... | collective-permute-start | bytes 786440 | tf_op jit(solution)/shard_map/ppermute | solution.py:197
  55.9 2.8 %collective-permute-done.4.refs_4_ = bf16[32,4096]{1,0:T(8,128)(2,1)S(1)} collective-permute-done((bf16[32,4096]{1,0:T(8,128)(2,1)S(1)}, bf16[32,4096]{1,0:T(8,128)(2,1)S(1)}, u32[]{:S(2)}, u32[]{:S(2)}) %collective-permute-start.4) | collective-permute-done | bytes 262176 | tf_op jit(solution)/shard_map/ppermute | solution.py:197
  58.8 3.7 %collective-permute-start.7 = (bf16[32,4096]{1,0:T(8,128)(2,1)S(1)}, bf16[32,4096]{1,0:T(8,128)(2,1)S(1)}, u32[]{:S(2)}, u32[]{:S(2)}) collective-permute-start(bf16[32,4096]{1,0:T(8,128)(2,1)S(1)} %get-tuple-element.93), channel_id=1, source_target_pairs={{0,6},{1,7},{2,4},{3,5},{4,2},{5,3},{6,0},{7,1},{8,14},{9,15},{10,... | collective-permute-start | bytes 786440 | tf_op jit(solution)/shard_map/ppermute | solution.py:197
  62.5 8.9 %collective-permute-done.1.refs_2_ = bf16[32,4096]{1,0:T(8,128)(2,1)S(1)} collective-permute-done((bf16[32,4096]{1,0:T(8,128)(2,1)S(1)}, bf16[32,4096]{1,0:T(8,128)(2,1)S(1)}, u32[]{:S(2)}, u32[]{:S(2)}) %collective-permute-start.1) | collective-permute-done | bytes 262176 | tf_op jit(solution)/shard_map/ppermute | solution.py:211
  71.4 3.8 %collective-permute-done.2.refs_3_ = bf16[32,4096]{1,0:T(8,128)(2,1)S(1)} collective-permute-done((bf16[32,4096]{1,0:T(8,128)(2,1)S(1)}, bf16[32,4096]{1,0:T(8,128)(2,1)S(1)}, u32[]{:S(2)}, u32[]{:S(2)}) %collective-permute-start.2) | collective-permute-done | bytes 262176 | tf_op jit(solution)/shard_map/ppermute | solution.py:211
  75.2 2.6 %copy-done.2 = bf16[1,2048,1408]{2,1,0:T(8,128)(2,1)S(1)} copy-done((bf16[1,2048,1408]{2,1,0:T(8,128)(2,1)S(1)}, bf16[1,2048,1408]{2,1,0:T(8,128)(2,1)}, u32[]{:S(2)}) %copy-start.2) | copy-done | bytes 5767192
  77.9 8.7 %expert.2 = (bf16[32,4096]{1,0:T(8,128)(2,1)S(1)}, bf16[32,4096]{1,0:T(8,128)(2,1)S(1)}, bf16[32,4096]{1,0:T(8,128)(2,1)S(1)}, bf16[32,4096]{1,0:T(8,128)(2,1)},...) custom-call(bf16[32,4096]{1,0:T(8,128)(2,1)S(1)} %get-tuple-element., ...), custom_call_target="tpu_custom_call" | custom-call | flops 1024 | bytes 1024 | tf_op jit(solution)/shard_map/expert/pallas_call | solution.py:26
  86.6 0.7 copy-done.10
  90.2 0.7 copy-done.21
  91.6 2.8 %collective-permute-start.8 = (bf16[32,4096]{1,0:T(8,128)(2,1)S(1)}, bf16[32,4096]{1,0:T(8,128)(2,1)S(1)}, u32[]{:S(2)}, u32[]{:S(2)}) collective-permute-start(bf16[32,4096]{1,0:T(8,128)(2,1)S(1)} %get-tuple-element.94), channel_id=1, source_target_pairs={{0,4},{1,5},{2,6},{3,7},{4,0},{5,1},{6,2},{7,3},{8,12},{9,13},{10,... | collective-permute-start | bytes 786440 | tf_op jit(solution)/shard_map/ppermute | solution.py:197
  94.4 1.6 collective-permute-start.18
  96.0 1.9 collective-permute-start.20
  97.9 10.9 %collective-permute-done.15.refs_5_ = bf16[32,4096]{1,0:T(8,128)(2,1)S(1)} collective-permute-done((bf16[32,4096]{1,0:T(8,128)(2,1)S(1)}, bf16[32,4096]{1,0:T(8,128)(2,1)S(1)}, u32[]{:S(2)}, u32[]{:S(2)}) %collective-permute-start.15) | collective-permute-done | bytes 262176 | tf_op jit(solution)/shard_map/ppermute | solution.py:197
  109.5 1.3 collective-permute-done.8.refs_4_
  111.5 4.9 %collective-permute-start.12 = (bf16[32,4096]{1,0:T(8,128)(2,1)}, bf16[32,4096]{1,0:T(8,128)(2,1)}, u32[]{:S(2)}, u32[]{:S(2)}) collective-permute-start(bf16[32,4096]{1,0:T(8,128)(2,1)} %get-tuple-element.102), channel_id=1, source_target_pairs={{0,6},{1,7},{2,4},{3,5},{4,2},{5,3},{6,0},{7,1},{8,14},{9,15},{10,... | collective-permute-start | bytes 786440 | tf_op jit(solution)/shard_map/ppermute | solution.py:197
  116.3 1.4 collective-permute-start.16
  119.2 2.6 %copy-done.3 = bf16[1,2048,1408]{2,1,0:T(8,128)(2,1)S(1)} copy-done((bf16[1,2048,1408]{2,1,0:T(8,128)(2,1)S(1)}, bf16[1,2048,1408]{2,1,0:T(8,128)(2,1)}, u32[]{:S(2)}) %copy-start.3) | copy-done | bytes 5767192
  121.8 1.8 copy-done.5
  123.6 0.9 copy-done.20
  124.6 0.9 copy-done.22
  125.5 0.9 copy-done.24
  126.5 0.9 copy-done.26
  127.4 0.9 copy-done.28
  128.4 0.9 copy-done.30
  129.3 0.9 copy-done.32
  130.3 8.3 %expert.3 = (bf16[32,4096]{1,0:T(8,128)(2,1)S(1)}, bf16[32,4096]{1,0:T(8,128)(2,1)S(1)}, bf16[32,4096]{1,0:T(8,128)(2,1)S(1)}, bf16[32,4096]{1,0:T(8,128)(2,1)S(...) custom-call(bf16[32,4096]{1,0:T(8,128)(2,1)S(1)} %copy-done.20, ...), custom_call_target="tpu_custom_call" | custom-call | flops 1024 | bytes 1024 | tf_op jit(solution)/shard_map/expert/pallas_call | solution.py:26
  138.7 4.0 %weight_part.4 = (bf16[16,2176]{1,0:T(8,128)(2,1)S(1)}, bf16[496,2176]{1,0:T(8,128)(2,1)}) custom-call(s32[1]{0:T(128)} %bitcast.4.refs_0_, bf16[256,4096]{1,0:T(8,128)(2,1)S(1)} %get-tuple-element.134.refs_1_, bf16[256,1408]{1,0:T(8,128)(2,1)S(1)} %get-tuple-element.123.refs_2_, bf16[256,704]{1,0:T(8,128)(2,1)S(1)} %copy-done.11, ...), custom_call_target="tpu_custom_call" | custom-call | flops 1024 | bytes 1024 | tf_op jit(solution)/shard_map/weight_part/pallas_call | solution.py:26
  142.9 1.2 collective-permute-done.21.refs_7_
  145.0 2.6 %collective-permute-start.17 = (bf16[32,4096]{1,0:T(8,128)(2,1)}, bf16[32,4096]{1,0:T(8,128)(2,1)}, u32[]{:S(2)}, u32[]{:S(2)}) collective-permute-start(bf16[32,4096]{1,0:T(8,128)(2,1)} %get-tuple-element.111), channel_id=1, source_target_pairs={{0,5},{1,4},{2,7},{3,6},{4,1},{5,0},{6,3},{7,2},{8,13},{9,12},{10,... | collective-permute-start | bytes 786440 | tf_op jit(solution)/shard_map/ppermute | solution.py:197
  147.5 1.6 copy-done.1
  149.1 1.0 copy-done.12
  150.1 1.0 copy-done.14
  151.1 2.9 %weight_part.5 = bf16[512,2176]{1,0:T(8,128)(2,1)S(1)} custom-call(s32[1]{0:T(128)} %bitcast.5.refs_0_, bf16[256,4096]{1,0:T(8,128)(2,1)S(1)} %get-tuple-element.134.refs_1_, bf16[256,1408]{1,0:T(8,128)(2,1)S(1)} %get-tuple-element.123.refs_2_, bf16[256,704]{1,0:T(8,128)(2,1)S(1)} %copy-done.12, bf16[256,4096]{1,0:T(8,128)(2,1)S(1)} %copy-done.1, ...), custom_call_target="tpu_custom_call" | custom-call | flops 1024 | bytes 1024 | tf_op jit(solution)/shard_map/weight_part/pallas_call | solution.py:26
  154.0 6.4 %collective-permute-done.11.refs_6_ = bf16[32,4096]{1,0:T(8,128)(2,1)} collective-permute-done((bf16[32,4096]{1,0:T(8,128)(2,1)}, bf16[32,4096]{1,0:T(8,128)(2,1)}, u32[]{:S(2)}, u32[]{:S(2)}) %collective-permute-start.11) | collective-permute-done | bytes 262176 | tf_op jit(solution)/shard_map/ppermute | solution.py:211
  160.4 4.6 %weight_part.6 = bf16[512,2176]{1,0:T(8,128)(2,1)S(1)} custom-call(s32[1]{0:T(128)} %bitcast.6.refs_0_, bf16[256,4096]{1,0:T(8,128)(2,1)S(1)} %get-tuple-element.134.refs_1_, bf16[256,1408]{1,0:T(8,128)(2,1)S(1)} %get-tuple-element.123.refs_2_, bf16[256,704]{1,0:T(8,128)(2,1)S(1)} %copy-done.12, bf16[256,4096]{1,0:T(8,128)(2,1)S(1)} %copy-done.1, ...), custom_call_target="tpu_custom_call" | custom-call | flops 1024 | bytes 1024 | tf_op jit(solution)/shard_map/weight_part/pallas_call | solution.py:26
  165.1 1.6 collective-permute-start.24
  166.7 1.2 collective-permute-start.13
  167.9 1.3 collective-permute-start.9
  169.2 2.8 %collective-permute-start.10 = (bf16[32,4096]{1,0:T(8,128)(2,1)S(1)}, bf16[32,4096]{1,0:T(8,128)(2,1)S(1)}, u32[]{:S(2)}, u32[]{:S(2)}) collective-permute-start(bf16[32,4096]{1,0:T(8,128)(2,1)S(1)} %copy-done.36), channel_id=1, source_target_pairs={{0,2},{1,3},{2,0},{3,1},{4,6},{5,7},{6,4},{7,5},{8,10},{9,11},{10,... | collective-permute-start | bytes 786440 | tf_op jit(solution)/shard_map/ppermute | solution.py:211
  172.1 9.9 %collective-permute-done.13.refs_7_ = bf16[32,4096]{1,0:T(8,128)(2,1)S(1)} collective-permute-done((bf16[32,4096]{1,0:T(8,128)(2,1)S(1)}, bf16[32,4096]{1,0:T(8,128)(2,1)S(1)}, u32[]{:S(2)}, u32[]{:S(2)}) %collective-permute-start.13) | collective-permute-done | bytes 262176 | tf_op jit(solution)/shard_map/ppermute | solution.py:197
  182.0 3.1 %collective-permute-start.30 = (bf16[32,4096]{1,0:T(8,128)(2,1)S(1)}, bf16[32,4096]{1,0:T(8,128)(2,1)S(1)}, u32[]{:S(2)}, u32[]{:S(2)}) collective-permute-start(bf16[32,4096]{1,0:T(8,128)(2,1)S(1)} %copy-done.54), channel_id=1, source_target_pairs={{0,7},{1,6},{2,5},{3,4},{4,3},{5,2},{6,1},{7,0},{8,15},{9,14},{10,... | collective-permute-start | bytes 786440 | tf_op jit(solution)/shard_map/ppermute | solution.py:197
  185.1 2.4 collective-permute-start.28
  187.5 2.7 %combine.2 = (bf16[256,2048]{1,0:T(8,128)(2,1)S(1)}, bf16[256,2048]{1,0:T(8,128)(2,1)S(1)}) custom-call(s32[1,256]{1,0:T(1,128)S(1)} %xor_bitcast_fusion.refs_0_, bf16[256,2048]{1,0:T(8,128)(2,1)S(1)} %copy-done.7, bf16[256,2048]{1,0:T(8,128)(2,1)S(1)} %copy-done.9, bf16[32,4096]{1,0:T(8,128)(2,1)S(1)} %copy-done.16, ...), custom_call_target="tpu_custom_call" | custom-call | flops 1024 | bytes 1024 | tf_op jit(solution)/shard_map/combine/pallas_call | solution.py:26
  190.3 3.7 %collective-permute-done.30.refs_10_ = bf16[32,4096]{1,0:T(8,128)(2,1)S(1)} collective-permute-done((bf16[32,4096]{1,0:T(8,128)(2,1)S(1)}, bf16[32,4096]{1,0:T(8,128)(2,1)S(1)}, u32[]{:S(2)}, u32[]{:S(2)}) %collective-permute-start.30) | collective-permute-done | bytes 262176 | tf_op jit(solution)/shard_map/ppermute | solution.py:197
  194.1 9.4 %collective-permute-start.26 = (bf16[32,4096]{1,0:T(8,128)(2,1)S(1)}, bf16[32,4096]{1,0:T(8,128)(2,1)S(1)}, u32[]{:S(2)}, u32[]{:S(2)}) collective-permute-start(bf16[32,4096]{1,0:T(8,128)(2,1)S(1)} %copy-done.48), channel_id=1, source_target_pairs={{0,2},{1,3},{2,0},{3,1},{4,6},{5,7},{6,4},{7,5},{8,10},{9,11},{10,... | collective-permute-start | bytes 786440 | tf_op jit(solution)/shard_map/ppermute | solution.py:211
  203.5 1.4 collective-permute-start.25
  204.9 10.2 %collective-permute-done.24.refs_8_ = bf16[512,2176]{1,0:T(8,128)(2,1)S(1)} collective-permute-done((bf16[512,2176]{1,0:T(8,128)(2,1)S(1)}, bf16[512,2176]{1,0:T(8,128)(2,1)S(1)}, u32[]{:S(2)}, u32[]{:S(2)}) %collective-permute-start.24) | collective-permute-done | bytes 2228256 | tf_op jit(solution)/shard_map/ppermute | solution.py:197
  215.1 1.4 collective-permute-start.31
  216.5 3.4 %collective-permute-start.29 = (bf16[32,4096]{1,0:T(8,128)(2,1)S(1)}, bf16[32,4096]{1,0:T(8,128)(2,1)S(1)}, u32[]{:S(2)}, u32[]{:S(2)}) collective-permute-start(bf16[32,4096]{1,0:T(8,128)(2,1)S(1)} %copy-done.40), channel_id=1, source_target_pairs={{0,4},{1,5},{2,6},{3,7},{4,0},{5,1},{6,2},{7,3},{8,12},{9,13},{10,... | collective-permute-start | bytes 786440 | tf_op jit(solution)/shard_map/ppermute | solution.py:197
  219.9 5.2 %weight_part.7 = (f32[512,1408]{1,0:T(8,128)}, f32[704,512]{1,0:T(8,128)}) custom-call(s32[1]{0:T(128)} %bitcast.3.refs_0_, bf16[256,4096]{1,0:T(8,128)(2,1)S(1)} %get-tuple-element.134.refs_1_, bf16[256,1408]{1,0:T(8,128)(2,1)S(1)} %get-tuple-element.123.refs_2_, bf16[256,704]{1,0:T(8,128)(2,1)S(1)} %copy-done.12, bf16[256,4096]{1,0:T(8,128)(2,1)S(1)} %copy-done.1, ...), custom_call_target="tpu_custom_call" | custom-call | flops 1024 | bytes 1024 | tf_op jit(solution)/shard_map/weight_part/pallas_call | solution.py:26
  225.2 11.3 %collective-permute-done.31.refs_8_ = bf16[32,4096]{1,0:T(8,128)(2,1)S(1)} collective-permute-done((bf16[32,4096]{1,0:T(8,128)(2,1)S(1)}, bf16[32,4096]{1,0:T(8,128)(2,1)S(1)}, u32[]{:S(2)}, u32[]{:S(2)}) %collective-permute-start.31) | collective-permute-done | bytes 262176 | tf_op jit(solution)/shard_map/ppermute | solution.py:197
  236.4 3.2 %collective-permute-done.29.refs_7_ = bf16[32,4096]{1,0:T(8,128)(2,1)S(1)} collective-permute-done((bf16[32,4096]{1,0:T(8,128)(2,1)S(1)}, bf16[32,4096]{1,0:T(8,128)(2,1)S(1)}, u32[]{:S(2)}, u32[]{:S(2)}) %collective-permute-start.29) | collective-permute-done | bytes 262176 | tf_op jit(solution)/shard_map/ppermute | solution.py:197
  239.6 2.5 %combine.3 = (bf16[256,2048]{1,0:T(8,128)(2,1)}, bf16[256,2048]{1,0:T(8,128)(2,1)}) custom-call(s32[1,256]{1,0:T(1,128)S(1)} %xor_bitcast_fusion.refs_0_, bf16[256,2048]{1,0:T(8,128)(2,1)S(1)} %get-tuple-element.112.refs_1_, bf16[256,2048]{1,0:T(8,128)(2,1)S(1)} %get-tuple-element.113.refs_2_, bf16[32,4096]{1,0:T(8,128)(2,1)S(1)} %copy-done.18, ...), custom_call_target="tpu_custom_call" | custom-call | flops 1024 | bytes 1024 | tf_op jit(solution)/shard_map/combine/pallas_call | solution.py:26
  (121 shorter events, 8.9 us)
Async XLA Ops:
  0.6 74.6 %copy-start.4 = (bf16[1,704,2048]{2,1,0:T(8,128)(2,1)S(1)}, bf16[1,704,2048]{2,1,0:T(8,128)(2,1)}, u32[]{:S(2)}) copy-start(bf16[1,704,2048]{2,1,0:T(8,128)(2,1)} %param.8) | copy-start | bytes 8650756
  1.5 1.3 copy-start.6
  6.2 13.3 %collective-permute-start.5 = (bf16[32,4096]{1,0:T(8,128)(2,1)S(1)}, bf16[32,4096]{1,0:T(8,128)(2,1)S(1)}, u32[]{:S(2)}, u32[]{:S(2)}) collective-permute-start(bf16[32,4096]{1,0:T(8,128)(2,1)S(1)} %get-tuple-element.87), channel_id=1, source_target_pairs={{0,7},{1,6},{2,5},{3,4},{4,3},{5,2},{6,1},{7,0},{8,15},{9,14},{10,... | collective-permute-start | bytes 786440 | tf_op jit(solution)/shard_map/ppermute | solution.py:197
  12.2 20.3 %collective-permute-start.3 = (bf16[32,4096]{1,0:T(8,128)(2,1)S(1)}, bf16[32,4096]{1,0:T(8,128)(2,1)S(1)}, u32[]{:S(2)}, u32[]{:S(2)}) collective-permute-start(bf16[32,4096]{1,0:T(8,128)(2,1)S(1)} %get-tuple-element.84), channel_id=1, source_target_pairs={{0,6},{1,7},{2,4},{3,5},{4,2},{5,3},{6,0},{7,1},{8,14},{9,15},{10,... | collective-permute-start | bytes 786440 | tf_op jit(solution)/shard_map/ppermute | solution.py:197
  19.5 32.9 %collective-permute-start.6 = (bf16[32,4096]{1,0:T(8,128)(2,1)S(1)}, bf16[32,4096]{1,0:T(8,128)(2,1)S(1)}, u32[]{:S(2)}, u32[]{:S(2)}) collective-permute-start(bf16[32,4096]{1,0:T(8,128)(2,1)S(1)} %get-tuple-element.88), channel_id=1, source_target_pairs={{0,5},{1,4},{2,7},{3,6},{4,1},{5,0},{6,3},{7,2},{8,13},{9,12},{10,... | collective-permute-start | bytes 786440 | tf_op jit(solution)/shard_map/ppermute | solution.py:197
  32.6 26.2 %collective-permute-start.4 = (bf16[32,4096]{1,0:T(8,128)(2,1)S(1)}, bf16[32,4096]{1,0:T(8,128)(2,1)S(1)}, u32[]{:S(2)}, u32[]{:S(2)}) collective-permute-start(bf16[32,4096]{1,0:T(8,128)(2,1)S(1)} %get-tuple-element.85), channel_id=1, source_target_pairs={{0,4},{1,5},{2,6},{3,7},{4,0},{5,1},{6,2},{7,3},{8,12},{9,13},{10,... | collective-permute-start | bytes 786440 | tf_op jit(solution)/shard_map/ppermute | solution.py:197
  42.9 19.6 %collective-permute-start = (bf16[32,4096]{1,0:T(8,128)(2,1)S(1)}, bf16[32,4096]{1,0:T(8,128)(2,1)S(1)}, u32[]{:S(2)}, u32[]{:S(2)}) collective-permute-start(bf16[32,4096]{1,0:T(8,128)(2,1)S(1)} %get-tuple-element.80), channel_id=1, source_target_pairs={{0,1},{1,0},{2,3},{3,2},{4,5},{5,4},{6,7},{7,6},{8,9},{9,8},{10,11... | collective-permute-start | bytes 786440 | tf_op jit(solution)/shard_map/ppermute | solution.py:211
  43.4 28.0 %collective-permute-start.1 = (bf16[32,4096]{1,0:T(8,128)(2,1)S(1)}, bf16[32,4096]{1,0:T(8,128)(2,1)S(1)}, u32[]{:S(2)}, u32[]{:S(2)}) collective-permute-start(bf16[32,4096]{1,0:T(8,128)(2,1)S(1)} %get-tuple-element.81), channel_id=1, source_target_pairs={{0,2},{1,3},{2,0},{3,1},{4,6},{5,7},{6,4},{7,5},{8,10},{9,11},{10,... | collective-permute-start | bytes 786440 | tf_op jit(solution)/shard_map/ppermute | solution.py:211
  43.4 31.8 %collective-permute-start.2 = (bf16[32,4096]{1,0:T(8,128)(2,1)S(1)}, bf16[32,4096]{1,0:T(8,128)(2,1)S(1)}, u32[]{:S(2)}, u32[]{:S(2)}) collective-permute-start(bf16[32,4096]{1,0:T(8,128)(2,1)S(1)} %get-tuple-element.82), channel_id=1, source_target_pairs={{0,3},{1,2},{2,1},{3,0},{4,7},{5,6},{6,5},{7,4},{8,11},{9,10},{10,... | collective-permute-start | bytes 786440 | tf_op jit(solution)/shard_map/ppermute | solution.py:211
  52.4 37.8 %collective-permute-start.14 = (bf16[32,4096]{1,0:T(8,128)(2,1)S(1)}, bf16[32,4096]{1,0:T(8,128)(2,1)S(1)}, u32[]{:S(2)}, u32[]{:S(2)}) collective-permute-start(bf16[32,4096]{1,0:T(8,128)(2,1)S(1)} %get-tuple-element.108), channel_id=1, source_target_pairs={{0,7},{1,6},{2,5},{3,4},{4,3},{5,2},{6,1},{7,0},{8,15},{9,14},{10,... | collective-permute-start | bytes 786440 | tf_op jit(solution)/shard_map/ppermute | solution.py:197
  58.8 32.2 %collective-permute-start.7 = (bf16[32,4096]{1,0:T(8,128)(2,1)S(1)}, bf16[32,4096]{1,0:T(8,128)(2,1)S(1)}, u32[]{:S(2)}, u32[]{:S(2)}) collective-permute-start(bf16[32,4096]{1,0:T(8,128)(2,1)S(1)} %get-tuple-element.93), channel_id=1, source_target_pairs={{0,6},{1,7},{2,4},{3,5},{4,2},{5,3},{6,0},{7,1},{8,14},{9,15},{10,... | collective-permute-start | bytes 786440 | tf_op jit(solution)/shard_map/ppermute | solution.py:197
  75.2 2.6 %copy-start.2 = (bf16[1,2048,1408]{2,1,0:T(8,128)(2,1)S(1)}, bf16[1,2048,1408]{2,1,0:T(8,128)(2,1)}, u32[]{:S(2)}) copy-start(bf16[1,2048,1408]{2,1,0:T(8,128)(2,1)} %param.7) | copy-start | bytes 17301508
  90.9 17.9 %collective-permute-start.15 = (bf16[32,4096]{1,0:T(8,128)(2,1)S(1)}, bf16[32,4096]{1,0:T(8,128)(2,1)S(1)}, u32[]{:S(2)}, u32[]{:S(2)}) collective-permute-start(bf16[32,4096]{1,0:T(8,128)(2,1)S(1)} %get-tuple-element.109), channel_id=1, source_target_pairs={{0,5},{1,4},{2,7},{3,6},{4,1},{5,0},{6,3},{7,2},{8,13},{9,12},{10,... | collective-permute-start | bytes 786440 | tf_op jit(solution)/shard_map/ppermute | solution.py:197
  91.6 19.1 %collective-permute-start.8 = (bf16[32,4096]{1,0:T(8,128)(2,1)S(1)}, bf16[32,4096]{1,0:T(8,128)(2,1)S(1)}, u32[]{:S(2)}, u32[]{:S(2)}) collective-permute-start(bf16[32,4096]{1,0:T(8,128)(2,1)S(1)} %get-tuple-element.94), channel_id=1, source_target_pairs={{0,4},{1,5},{2,6},{3,7},{4,0},{5,1},{6,2},{7,3},{8,12},{9,13},{10,... | collective-permute-start | bytes 786440 | tf_op jit(solution)/shard_map/ppermute | solution.py:197
  94.4 23.3 %collective-permute-start.18 = (bf16[32,4096]{1,0:T(8,128)(2,1)}, bf16[32,4096]{1,0:T(8,128)(2,1)S(1)}, u32[]{:S(2)}, u32[]{:S(2)}) collective-permute-start(bf16[32,4096]{1,0:T(8,128)(2,1)} %get-tuple-element.116), channel_id=1, source_target_pairs={{0,1},{1,0},{2,3},{3,2},{4,5},{5,4},{6,7},{7,6},{8,9},{9,8},{10,11... | collective-permute-start | bytes 786440 | tf_op jit(solution)/shard_map/ppermute | solution.py:211
  96.0 22.4 %collective-permute-start.19 = (bf16[32,4096]{1,0:T(8,128)(2,1)}, bf16[32,4096]{1,0:T(8,128)(2,1)S(1)}, u32[]{:S(2)}, u32[]{:S(2)}) collective-permute-start(bf16[32,4096]{1,0:T(8,128)(2,1)} %get-tuple-element.118), channel_id=1, source_target_pairs={{0,2},{1,3},{2,0},{3,1},{4,6},{5,7},{6,4},{7,5},{8,10},{9,11},{10,... | collective-permute-start | bytes 786440 | tf_op jit(solution)/shard_map/ppermute | solution.py:211
  96.0 23.1 %collective-permute-start.20 = (bf16[32,4096]{1,0:T(8,128)(2,1)}, bf16[32,4096]{1,0:T(8,128)(2,1)}, u32[]{:S(2)}, u32[]{:S(2)}) collective-permute-start(bf16[32,4096]{1,0:T(8,128)(2,1)} %get-tuple-element.120), channel_id=1, source_target_pairs={{0,3},{1,2},{2,1},{3,0},{4,7},{5,6},{6,5},{7,4},{8,11},{9,10},{10,... | collective-permute-start | bytes 786440 | tf_op jit(solution)/shard_map/ppermute | solution.py:211
  111.5 33.3 %collective-permute-start.12 = (bf16[32,4096]{1,0:T(8,128)(2,1)}, bf16[32,4096]{1,0:T(8,128)(2,1)}, u32[]{:S(2)}, u32[]{:S(2)}) collective-permute-start(bf16[32,4096]{1,0:T(8,128)(2,1)} %get-tuple-element.102), channel_id=1, source_target_pairs={{0,6},{1,7},{2,4},{3,5},{4,2},{5,3},{6,0},{7,1},{8,14},{9,15},{10,... | collective-permute-start | bytes 786440 | tf_op jit(solution)/shard_map/ppermute | solution.py:197
  116.3 28.5 %collective-permute-start.16 = (bf16[32,4096]{1,0:T(8,128)(2,1)}, bf16[32,4096]{1,0:T(8,128)(2,1)}, u32[]{:S(2)}, u32[]{:S(2)}) collective-permute-start(bf16[32,4096]{1,0:T(8,128)(2,1)} %get-tuple-element.110), channel_id=1, source_target_pairs={{0,7},{1,6},{2,5},{3,4},{4,3},{5,2},{6,1},{7,0},{8,15},{9,14},{10,... | collective-permute-start | bytes 786440 | tf_op jit(solution)/shard_map/ppermute | solution.py:197
  119.2 2.6 %copy-start.3 = (bf16[1,2048,1408]{2,1,0:T(8,128)(2,1)S(1)}, bf16[1,2048,1408]{2,1,0:T(8,128)(2,1)}, u32[]{:S(2)}) copy-start(bf16[1,2048,1408]{2,1,0:T(8,128)(2,1)} %param.7) | copy-start | bytes 17301508
  121.8 1.8 copy-start.5
  130.3 8.5 %copy-start.11 = (bf16[256,704]{1,0:T(8,128)(2,1)S(1)}, bf16[256,704]{1,0:T(8,128)(2,1)}, u32[]{:S(2)}) copy-start(bf16[256,704]{1,0:T(8,128)(2,1)} %copy-done.10) | copy-start | bytes 1081348
  138.6 4.1 %copy-start = (bf16[256,4096]{1,0:T(8,128)(2,1)}, bf16[256,4096]{1,0:T(8,128)(2,1)S(1)}, u32[]{:S(2)}) copy-start(bf16[256,4096]{1,0:T(8,128)(2,1)S(1)} %get-tuple-element.125.refs_4_) | copy-start | bytes 6291460
  138.6 4.1 %copy-start.13 = (bf16[256,704]{1,0:T(8,128)(2,1)}, bf16[256,704]{1,0:T(8,128)(2,1)S(1)}, u32[]{:S(2)}) copy-start(bf16[256,704]{1,0:T(8,128)(2,1)S(1)} %get-tuple-element.127.refs_6_) | copy-start | bytes 1081348
  138.6 4.1 %copy-start.17 = (bf16[32,4096]{1,0:T(8,128)(2,1)}, bf16[32,4096]{1,0:T(8,128)(2,1)S(1)}, u32[]{:S(2)}) copy-start(bf16[32,4096]{1,0:T(8,128)(2,1)S(1)} %get-tuple-element.136.refs_3_) | copy-start | bytes 786436
  138.6 4.1 %copy-start.39 = (bf16[32,4096]{1,0:T(8,128)(2,1)}, bf16[32,4096]{1,0:T(8,128)(2,1)S(1)}, u32[]{:S(2)}) copy-start(bf16[32,4096]{1,0:T(8,128)(2,1)S(1)} %get-tuple-element.146) | copy-start | bytes 786436
  138.7 4.1 %copy-start.41 = (bf16[32,4096]{1,0:T(8,128)(2,1)}, bf16[32,4096]{1,0:T(8,128)(2,1)S(1)}, u32[]{:S(2)}) copy-start(bf16[32,4096]{1,0:T(8,128)(2,1)S(1)} %get-tuple-element.150) | copy-start | bytes 786436
  138.7 4.1 %copy-start.45 = (bf16[32,4096]{1,0:T(8,128)(2,1)}, bf16[32,4096]{1,0:T(8,128)(2,1)S(1)}, u32[]{:S(2)}) copy-start(bf16[32,4096]{1,0:T(8,128)(2,1)S(1)} %get-tuple-element.138) | copy-start | bytes 786436
  138.7 4.1 %copy-start.47 = (bf16[32,4096]{1,0:T(8,128)(2,1)}, bf16[32,4096]{1,0:T(8,128)(2,1)S(1)}, u32[]{:S(2)}) copy-start(bf16[32,4096]{1,0:T(8,128)(2,1)S(1)} %get-tuple-element.140) | copy-start | bytes 786436
  138.7 4.1 %copy-start.49 = (bf16[32,4096]{1,0:T(8,128)(2,1)}, bf16[32,4096]{1,0:T(8,128)(2,1)S(1)}, u32[]{:S(2)}) copy-start(bf16[32,4096]{1,0:T(8,128)(2,1)S(1)} %get-tuple-element.142) | copy-start | bytes 786436
  138.7 4.1 %copy-start.51 = (bf16[32,4096]{1,0:T(8,128)(2,1)}, bf16[32,4096]{1,0:T(8,128)(2,1)S(1)}, u32[]{:S(2)}) copy-start(bf16[32,4096]{1,0:T(8,128)(2,1)S(1)} %get-tuple-element.145) | copy-start | bytes 786436
  138.7 4.1 %copy-start.53 = (bf16[32,4096]{1,0:T(8,128)(2,1)}, bf16[32,4096]{1,0:T(8,128)(2,1)S(1)}, u32[]{:S(2)}) copy-start(bf16[32,4096]{1,0:T(8,128)(2,1)S(1)} %get-tuple-element.149) | copy-start | bytes 786436
  142.8 1.3 collective-permute-start.21
  144.8 15.6 %collective-permute-start.22 = (bf16[496,2176]{1,0:T(8,128)(2,1)}, bf16[496,2176]{1,0:T(8,128)(2,1)}, u32[]{:S(2)}, u32[]{:S(2)}) collective-permute-start(bf16[496,2176]{1,0:T(8,128)(2,1)} %get-tuple-element.133), channel_id=1, source_target_pairs={{0,8},{8,0},{16,24},{24,16},{1,9},{9,1},{17,25},{25,17},{2,10},{10... | collective-permute-start | bytes 6475784 | tf_op jit(solution)/shard_map/ppermute | solution.py:197
  144.9 15.4 %collective-permute-start.11 = (bf16[32,4096]{1,0:T(8,128)(2,1)}, bf16[32,4096]{1,0:T(8,128)(2,1)}, u32[]{:S(2)}, u32[]{:S(2)}) collective-permute-start(bf16[32,4096]{1,0:T(8,128)(2,1)} %get-tuple-element.99), channel_id=1, source_target_pairs={{0,3},{1,2},{2,1},{3,0},{4,7},{5,6},{6,5},{7,4},{8,11},{9,10},{10,... | collective-permute-start | bytes 786440 | tf_op jit(solution)/shard_map/ppermute | solution.py:211
  145.0 15.4 %collective-permute-start.17 = (bf16[32,4096]{1,0:T(8,128)(2,1)}, bf16[32,4096]{1,0:T(8,128)(2,1)}, u32[]{:S(2)}, u32[]{:S(2)}) collective-permute-start(bf16[32,4096]{1,0:T(8,128)(2,1)} %get-tuple-element.111), channel_id=1, source_target_pairs={{0,5},{1,4},{2,7},{3,6},{4,1},{5,0},{6,3},{7,2},{8,13},{9,12},{10,... | collective-permute-start | bytes 786440 | tf_op jit(solution)/shard_map/ppermute | solution.py:197
  147.5 1.6 copy-start.1
  151.1 9.3 %copy-start.34 = (bf16[16,2176]{1,0:T(8,128)(2,1)S(1)}, bf16[16,2176]{1,0:T(8,128)(2,1)}, u32[]{:S(2)}) copy-start(bf16[16,2176]{1,0:T(8,128)(2,1)} %copy-done.33) | copy-start | bytes 208900
  160.4 6.3 %copy-start.44 = (bf16[32,4096]{1,0:T(8,128)(2,1)S(1)}, bf16[32,4096]{1,0:T(8,128)(2,1)}, u32[]{:S(2)}) copy-start(bf16[32,4096]{1,0:T(8,128)(2,1)} %copy-done.43) | copy-start | bytes 786436
  160.4 7.5 %copy-start.38 = (bf16[32,4096]{1,0:T(8,128)(2,1)S(1)}, bf16[32,4096]{1,0:T(8,128)(2,1)}, u32[]{:S(2)}) copy-start(bf16[32,4096]{1,0:T(8,128)(2,1)} %copy-done.37) | copy-start | bytes 786436
  160.4 8.8 %copy-start.36 = (bf16[32,4096]{1,0:T(8,128)(2,1)S(1)}, bf16[32,4096]{1,0:T(8,128)(2,1)}, u32[]{:S(2)}) copy-start(bf16[32,4096]{1,0:T(8,128)(2,1)} %copy-done.35) | copy-start | bytes 786436
  160.4 21.6 %copy-start.54 = (bf16[32,4096]{1,0:T(8,128)(2,1)S(1)}, bf16[32,4096]{1,0:T(8,128)(2,1)}, u32[]{:S(2)}) copy-start(bf16[32,4096]{1,0:T(8,128)(2,1)} %copy-done.53) | copy-start | bytes 786436
  160.4 24.7 %copy-start.52 = (bf16[32,4096]{1,0:T(8,128)(2,1)S(1)}, bf16[32,4096]{1,0:T(8,128)(2,1)}, u32[]{:S(2)}) copy-start(bf16[32,4096]{1,0:T(8,128)(2,1)} %copy-done.51) | copy-start | bytes 786436
  160.4 27.1 %copy-start.7 = (bf16[256,2048]{1,0:T(8,128)(2,1)S(1)}, bf16[256,2048]{1,0:T(8,128)(2,1)}, u32[]{:S(2)}) copy-start(bf16[256,2048]{1,0:T(8,128)(2,1)} %refs_1_.5) | copy-start | bytes 3145732
  160.4 27.1 %copy-start.9 = (bf16[256,2048]{1,0:T(8,128)(2,1)S(1)}, bf16[256,2048]{1,0:T(8,128)(2,1)}, u32[]{:S(2)}) copy-start(bf16[256,2048]{1,0:T(8,128)(2,1)} %refs_2_.5) | copy-start | bytes 3145732
  160.4 27.0 %copy-start.16 = (bf16[32,4096]{1,0:T(8,128)(2,1)S(1)}, bf16[32,4096]{1,0:T(8,128)(2,1)}, u32[]{:S(2)}) copy-start(bf16[32,4096]{1,0:T(8,128)(2,1)} %copy-done.15) | copy-start | bytes 786436
  165.1 25.2 %copy-start.50 = (bf16[32,4096]{1,0:T(8,128)(2,1)S(1)}, bf16[32,4096]{1,0:T(8,128)(2,1)}, u32[]{:S(2)}) copy-start(bf16[32,4096]{1,0:T(8,128)(2,1)} %copy-done.49) | copy-start | bytes 786436
  165.1 29.0 %copy-start.48 = (bf16[32,4096]{1,0:T(8,128)(2,1)S(1)}, bf16[32,4096]{1,0:T(8,128)(2,1)}, u32[]{:S(2)}) copy-start(bf16[32,4096]{1,0:T(8,128)(2,1)} %copy-done.47) | copy-start | bytes 786436
  165.1 38.4 %copy-start.46 = (bf16[32,4096]{1,0:T(8,128)(2,1)S(1)}, bf16[32,4096]{1,0:T(8,128)(2,1)}, u32[]{:S(2)}) copy-start(bf16[32,4096]{1,0:T(8,128)(2,1)} %copy-done.45) | copy-start | bytes 786436
  165.1 50.0 %copy-start.42 = (bf16[32,4096]{1,0:T(8,128)(2,1)S(1)}, bf16[32,4096]{1,0:T(8,128)(2,1)}, u32[]{:S(2)}) copy-start(bf16[32,4096]{1,0:T(8,128)(2,1)} %copy-done.41) | copy-start | bytes 786436
  165.1 51.4 %copy-start.40 = (bf16[32,4096]{1,0:T(8,128)(2,1)S(1)}, bf16[32,4096]{1,0:T(8,128)(2,1)}, u32[]{:S(2)}) copy-start(bf16[32,4096]{1,0:T(8,128)(2,1)} %copy-done.39) | copy-start | bytes 786436
  165.1 50.0 %collective-permute-start.24 = (bf16[512,2176]{1,0:T(8,128)(2,1)S(1)}, bf16[512,2176]{1,0:T(8,128)(2,1)S(1)}, u32[]{:S(2)}, u32[]{:S(2)}) collective-permute-start(bf16[512,2176]{1,0:T(8,128)(2,1)S(1)} %weight_part.6), channel_id=1, source_target_pairs={{0,16},{8,24},{16,0},{24,8},{1,17},{9,25},{17,1},{25,9},{2,18},{10... | collective-permute-start | bytes 6684680 | tf_op jit(solution)/shard_map/ppermute | solution.py:197
  166.7 49.9 %collective-permute-start.23 = (bf16[512,2176]{1,0:T(8,128)(2,1)S(1)}, bf16[512,2176]{1,0:T(8,128)(2,1)S(1)}, u32[]{:S(2)}, u32[]{:S(2)}) collective-permute-start(bf16[512,2176]{1,0:T(8,128)(2,1)S(1)} %weight_part.5), channel_id=1, source_target_pairs={{0,8},{8,0},{16,24},{24,16},{1,9},{9,1},{17,25},{25,17},{2,10},{10... | collective-permute-start | bytes 6684680 | tf_op jit(solution)/shard_map/ppermute | solution.py:197
  166.7 15.3 %collective-permute-start.13 = (bf16[32,4096]{1,0:T(8,128)(2,1)S(1)}, bf16[32,4096]{1,0:T(8,128)(2,1)S(1)}, u32[]{:S(2)}, u32[]{:S(2)}) collective-permute-start(bf16[32,4096]{1,0:T(8,128)(2,1)S(1)} %copy-done.44), channel_id=1, source_target_pairs={{0,4},{1,5},{2,6},{3,7},{4,0},{5,1},{6,2},{7,3},{8,12},{9,13},{10,... | collective-permute-start | bytes 786440 | tf_op jit(solution)/shard_map/ppermute | solution.py:197
  167.9 17.2 %collective-permute-start.9 = (bf16[32,4096]{1,0:T(8,128)(2,1)S(1)}, bf16[32,4096]{1,0:T(8,128)(2,1)S(1)}, u32[]{:S(2)}, u32[]{:S(2)}) collective-permute-start(bf16[32,4096]{1,0:T(8,128)(2,1)S(1)} %copy-done.38), channel_id=1, source_target_pairs={{0,1},{1,0},{2,3},{3,2},{4,5},{5,4},{6,7},{7,6},{8,9},{9,8},{10,11... | collective-permute-start | bytes 786440 | tf_op jit(solution)/shard_map/ppermute | solution.py:211
  169.2 18.2 %collective-permute-start.10 = (bf16[32,4096]{1,0:T(8,128)(2,1)S(1)}, bf16[32,4096]{1,0:T(8,128)(2,1)S(1)}, u32[]{:S(2)}, u32[]{:S(2)}) collective-permute-start(bf16[32,4096]{1,0:T(8,128)(2,1)S(1)} %copy-done.36), channel_id=1, source_target_pairs={{0,2},{1,3},{2,0},{3,1},{4,6},{5,7},{6,4},{7,5},{8,10},{9,11},{10,... | collective-permute-start | bytes 786440 | tf_op jit(solution)/shard_map/ppermute | solution.py:211
  182.0 12.0 %collective-permute-start.30 = (bf16[32,4096]{1,0:T(8,128)(2,1)S(1)}, bf16[32,4096]{1,0:T(8,128)(2,1)S(1)}, u32[]{:S(2)}, u32[]{:S(2)}) collective-permute-start(bf16[32,4096]{1,0:T(8,128)(2,1)S(1)} %copy-done.54), channel_id=1, source_target_pairs={{0,7},{1,6},{2,5},{3,4},{4,3},{5,2},{6,1},{7,0},{8,15},{9,14},{10,... | collective-permute-start | bytes 786440 | tf_op jit(solution)/shard_map/ppermute | solution.py:197
  185.1 18.4 %collective-permute-start.28 = (bf16[32,4096]{1,0:T(8,128)(2,1)S(1)}, bf16[32,4096]{1,0:T(8,128)(2,1)S(1)}, u32[]{:S(2)}, u32[]{:S(2)}) collective-permute-start(bf16[32,4096]{1,0:T(8,128)(2,1)S(1)} %copy-done.52), channel_id=1, source_target_pairs={{0,6},{1,7},{2,4},{3,5},{4,2},{5,3},{6,0},{7,1},{8,14},{9,15},{10,... | collective-permute-start | bytes 786440 | tf_op jit(solution)/shard_map/ppermute | solution.py:197
  190.2 34.9 %collective-permute-start.27 = (bf16[32,4096]{1,0:T(8,128)(2,1)S(1)}, bf16[32,4096]{1,0:T(8,128)(2,1)S(1)}, u32[]{:S(2)}, u32[]{:S(2)}) collective-permute-start(bf16[32,4096]{1,0:T(8,128)(2,1)S(1)} %copy-done.50), channel_id=1, source_target_pairs={{0,3},{1,2},{2,1},{3,0},{4,7},{5,6},{6,5},{7,4},{8,11},{9,10},{10,... | collective-permute-start | bytes 786440 | tf_op jit(solution)/shard_map/ppermute | solution.py:211
  194.1 31.1 %collective-permute-start.26 = (bf16[32,4096]{1,0:T(8,128)(2,1)S(1)}, bf16[32,4096]{1,0:T(8,128)(2,1)S(1)}, u32[]{:S(2)}, u32[]{:S(2)}) collective-permute-start(bf16[32,4096]{1,0:T(8,128)(2,1)S(1)} %copy-done.48), channel_id=1, source_target_pairs={{0,2},{1,3},{2,0},{3,1},{4,6},{5,7},{6,4},{7,5},{8,10},{9,11},{10,... | collective-permute-start | bytes 786440 | tf_op jit(solution)/shard_map/ppermute | solution.py:211
  203.5 21.6 %collective-permute-start.25 = (bf16[32,4096]{1,0:T(8,128)(2,1)S(1)}, bf16[32,4096]{1,0:T(8,128)(2,1)S(1)}, u32[]{:S(2)}, u32[]{:S(2)}) collective-permute-start(bf16[32,4096]{1,0:T(8,128)(2,1)S(1)} %copy-done.46), channel_id=1, source_target_pairs={{0,1},{1,0},{2,3},{3,2},{4,5},{5,4},{6,7},{7,6},{8,9},{9,8},{10,11... | collective-permute-start | bytes 786440 | tf_op jit(solution)/shard_map/ppermute | solution.py:211
  215.1 21.3 %collective-permute-start.31 = (bf16[32,4096]{1,0:T(8,128)(2,1)S(1)}, bf16[32,4096]{1,0:T(8,128)(2,1)S(1)}, u32[]{:S(2)}, u32[]{:S(2)}) collective-permute-start(bf16[32,4096]{1,0:T(8,128)(2,1)S(1)} %copy-done.42), channel_id=1, source_target_pairs={{0,5},{1,4},{2,7},{3,6},{4,1},{5,0},{6,3},{7,2},{8,13},{9,12},{10,... | collective-permute-start | bytes 786440 | tf_op jit(solution)/shard_map/ppermute | solution.py:197
  216.5 23.1 %collective-permute-start.29 = (bf16[32,4096]{1,0:T(8,128)(2,1)S(1)}, bf16[32,4096]{1,0:T(8,128)(2,1)S(1)}, u32[]{:S(2)}, u32[]{:S(2)}) collective-permute-start(bf16[32,4096]{1,0:T(8,128)(2,1)S(1)} %copy-done.40), channel_id=1, source_target_pairs={{0,4},{1,5},{2,6},{3,7},{4,0},{5,1},{6,2},{7,3},{8,12},{9,13},{10,... | collective-permute-start | bytes 786440 | tf_op jit(solution)/shard_map/ppermute | solution.py:197
  219.9 19.7 %copy-start.18 = (bf16[32,4096]{1,0:T(8,128)(2,1)S(1)}, bf16[32,4096]{1,0:T(8,128)(2,1)}, u32[]{:S(2)}) copy-start(bf16[32,4096]{1,0:T(8,128)(2,1)} %copy-done.17) | copy-start | bytes 786436
  (23 other events, 19.0 us)

commit v6 on v5

--- a/solution.py
+++ b/solution.py
@@ -5,6 +5,7 @@
 from jax.experimental.pallas import tpu as pltpu
 from jax.sharding import PartitionSpec as P
 
+VMEM_BYTES = 64 * 1024 * 1024
 SMALL = pl.CostEstimate(flops=1024, bytes_accessed=1024, transcendentals=0)
 BF16 = jnp.bfloat16
 F32 = jnp.float32
@@ -21,7 +22,7 @@
     return jax.ShapeDtypeStruct(shape, dtype)
 
 
-def call(kernel, name, mebibytes, outs, scratch, arrays, small=(), scalars=()):
+def call(kernel, name, outs, scratch, arrays, small=(), scalars=()):
     hbm = pl.BlockSpec(memory_space=pltpu.HBM)
     return pl.pallas_call(
         kernel,
@@ -31,7 +32,7 @@
         out_specs=[hbm] * len(outs),
         out_shape=outs,
         scratch_shapes=scratch,
-        compiler_params=pltpu.CompilerParams(vmem_limit_bytes=mebibytes * 1024 * 1024),
+        compiler_params=pltpu.CompilerParams(vmem_limit_bytes=VMEM_BYTES),
         cost_estimate=SMALL,
         name=name,
     )(*scalars, *small, *arrays)
@@ -234,7 +235,6 @@
         return call(
             lambda *refs: place_kernel(part, cap, *refs),
             "place",
-            slots * 5 // 128,
             [pair] * experts,
             [pltpu.VMEM((rows, 2 * width), BF16), pltpu.VMEM((slots, 2 * width), BF16), sems((2 + 2 * experts,))],
             [tokens, grad_out],
@@ -248,7 +248,6 @@
         outs = call(
             expert_kernel,
             "expert",
-            2 + slots * 5 // 64,
             [pair] * experts + [like(shape) for shape in shapes],
             scratch + back + [sems((5 + 2 * experts,))],
             [*blocks, weight_one, weight_two],
@@ -270,7 +269,6 @@
         return call(
             lambda *refs: weight_kernel(end, parts, pieces, *refs),
             "weight_part",
-            18,
             outs,
             scratch,
             sources,
@@ -281,7 +279,6 @@
         return call(
             lambda *refs: combine_kernel(part, cap, *refs),
             "combine",
-            slots * 5 // 128,
             [like((rows, width))] * 2,
             [pltpu.VMEM((rows, 2 * width), BF16), pltpu.VMEM((slots, 2 * width), BF16), sems((4 + experts,))],
             [first, second, *blocks],

time: 243 us -> 235 us (0.967)
  local copies, waits for them, and re-layouts: 29.1 us -> 0 us
  Pallas kernels: 43.6 us -> 61.5 us
  starting transfers between devices: 84 us -> 91.4 us
  waiting for transfers between devices: 83.5 us -> 79.4 us
    unnamed x110 -> x0, local copies, waits for them, and re-layouts: 29.1 us -> none
    pallas_call x10, Pallas kernels: 43.6 us -> 61.5 us  [call(): pl.pallas_call(kernel, in_specs=[pl.BlockSpec(memory_space=pltpu.SMEM)] *...]
    ppermute x20, starting transfers between devices: 61.9 us -> 73.2 us  [send(): self.done.append(lax.ppermute(after(value, *earlier), axis, pairs))]
    ppermute x20, waiting for transfers between devices: 64.4 us -> 57.9 us  [send(): self.done.append(lax.ppermute(after(value, *earlier), axis, pairs))]
    ppermute x12, starting transfers between devices: 22 us -> 18.3 us  [exchange(): moved[mask] = lax.ppermute(after(blocks[mask], *earlier), 'exp', pairs)]
  transfers between devices with their start and end apart: 32 -> 32, of which waited for: 14 -> 14; matrix products, arithmetic and copies ran while one was open for 0% -> 0% of each run, Pallas kernels for 14% -> 20%
where the time goes in v6:
time: 235 us
  starting transfers between devices  91.4 us (39%)
  waiting for transfers between devices  79.4 us (34%)
  Pallas kernels  61.5 us (26%)
    ppermute x20, starting transfers between devices, send(): self.done.append(lax.ppermute(after(value, *earlier), axis, pairs))  73.2 us
    pallas_call x10, Pallas kernels, call(): pl.pallas_call(kernel, in_specs=[pl.BlockSpec(memory_space=pltpu.SMEM)] *...  61.5 us
    ppermute x20, waiting for transfers between devices, send(): self.done.append(lax.ppermute(after(value, *earlier), axis, pairs))  57.9 us
    ppermute x12, waiting for transfers between devices, exchange(): moved[mask] = lax.ppermute(after(blocks[mask], *earlier), 'exp', pairs)  21.5 us
    ppermute x12, starting transfers between devices, exchange(): moved[mask] = lax.ppermute(after(blocks[mask], *earlier), 'exp', pairs)  18.3 us
  transfers between devices with their start and end apart: 32, of which 14 were waited for; matrix products, arithmetic and copies ran while one was open for 0% of the time, Pallas kernels for 20%

profile of v6, /device:TPU:0, one launch (start us, length us, event | category | flops | bytes accessed | tf_op | source)
XLA Modules:
  0.0 234.5 jit_solution(8404322888726206029)
XLA Ops:
  0.6 1.3 xor_bitcast_fusion.refs_0_
  1.9 3.9 %place.2 = (bf16[32,4096]{1,0:T(8,128)(2,1)}, bf16[32,4096]{1,0:T(8,128)(2,1)}, bf16[32,4096]{1,0:T(8,128)(2,1)}, bf16[32,4096]{1,0:T(8,128)(2,1)}, bf16[32,4096...) custom-call(s32[1,256]{1,0:T(1,128)} %xor_bitcast_fusion.refs_0_, ...), custom_call_target="tpu_custom_call" | custom-call | flops 1024 | bytes 1024 | tf_op jit(solution)/shard_map/place/pallas_call | solution.py:27
  5.8 6.1 %collective-permute-start.5 = (bf16[32,4096]{1,0:T(8,128)(2,1)}, bf16[32,4096]{1,0:T(8,128)(2,1)}, u32[]{:S(2)}, u32[]{:S(2)}) collective-permute-start(bf16[32,4096]{1,0:T(8,128)(2,1)} %get-tuple-element.87), channel_id=1, source_target_pairs={{0,7},{1,6},{2,5},{3,4},{4,3},{5,2},{6,1},{7,0},{8,15},{9,14},{10,... | collective-permute-start | bytes 786440 | tf_op jit(solution)/shard_map/ppermute | solution.py:198
  11.9 0.2 collective-permute-start.3
  12.1 7.3 %collective-permute-done.5.refs_7_ = bf16[32,4096]{1,0:T(8,128)(2,1)} collective-permute-done((bf16[32,4096]{1,0:T(8,128)(2,1)}, bf16[32,4096]{1,0:T(8,128)(2,1)}, u32[]{:S(2)}, u32[]{:S(2)}) %collective-permute-start.5) | collective-permute-done | bytes 262176 | tf_op jit(solution)/shard_map/ppermute | solution.py:198
  19.4 13.1 %collective-permute-start.6 = (bf16[32,4096]{1,0:T(8,128)(2,1)}, bf16[32,4096]{1,0:T(8,128)(2,1)}, u32[]{:S(2)}, u32[]{:S(2)}) collective-permute-start(bf16[32,4096]{1,0:T(8,128)(2,1)} %get-tuple-element.88), channel_id=1, source_target_pairs={{0,5},{1,4},{2,7},{3,6},{4,1},{5,0},{6,3},{7,2},{8,13},{9,12},{10,... | collective-permute-start | bytes 786440 | tf_op jit(solution)/shard_map/ppermute | solution.py:198
  32.5 10.3 %collective-permute-start.4 = (bf16[32,4096]{1,0:T(8,128)(2,1)}, bf16[32,4096]{1,0:T(8,128)(2,1)}, u32[]{:S(2)}, u32[]{:S(2)}) collective-permute-start(bf16[32,4096]{1,0:T(8,128)(2,1)} %get-tuple-element.85), channel_id=1, source_target_pairs={{0,4},{1,5},{2,6},{3,7},{4,0},{5,1},{6,2},{7,3},{8,12},{9,13},{10,... | collective-permute-start | bytes 786440 | tf_op jit(solution)/shard_map/ppermute | solution.py:198
  42.8 0.5 collective-permute-start
  43.3 0.0 collective-permute-start.1
  43.4 3.0 %collective-permute-start.2 = (bf16[32,4096]{1,0:T(8,128)(2,1)}, bf16[32,4096]{1,0:T(8,128)(2,1)}, u32[]{:S(2)}, u32[]{:S(2)}) collective-permute-start(bf16[32,4096]{1,0:T(8,128)(2,1)} %get-tuple-element.82), channel_id=1, source_target_pairs={{0,3},{1,2},{2,1},{3,0},{4,7},{5,6},{6,5},{7,4},{8,11},{9,10},{10,... | collective-permute-start | bytes 786440 | tf_op jit(solution)/shard_map/ppermute | solution.py:212
  46.3 3.9 %place.3 = (bf16[32,4096]{1,0:T(8,128)(2,1)}, bf16[32,4096]{1,0:T(8,128)(2,1)}, bf16[32,4096]{1,0:T(8,128)(2,1)}, bf16[32,4096]{1,0:T(8,128)(2,1)}, bf16[32,4096...) custom-call(s32[1,256]{1,0:T(1,128)} %xor_bitcast_fusion.refs_0_, ...), custom_call_target="tpu_custom_call" | custom-call | flops 1024 | bytes 1024 | tf_op jit(solution)/shard_map/place/pallas_call | solution.py:27
  50.3 2.0 collective-permute-done.6.refs_5_
  52.3 3.6 %collective-permute-start.14 = (bf16[32,4096]{1,0:T(8,128)(2,1)}, bf16[32,4096]{1,0:T(8,128)(2,1)}, u32[]{:S(2)}, u32[]{:S(2)}) collective-permute-start(bf16[32,4096]{1,0:T(8,128)(2,1)} %get-tuple-element.108), channel_id=1, source_target_pairs={{0,7},{1,6},{2,5},{3,4},{4,3},{5,2},{6,1},{7,0},{8,15},{9,14},{10,... | collective-permute-start | bytes 786440 | tf_op jit(solution)/shard_map/ppermute | solution.py:198
  55.9 2.5 %collective-permute-done.4.refs_4_ = bf16[32,4096]{1,0:T(8,128)(2,1)} collective-permute-done((bf16[32,4096]{1,0:T(8,128)(2,1)}, bf16[32,4096]{1,0:T(8,128)(2,1)}, u32[]{:S(2)}, u32[]{:S(2)}) %collective-permute-start.4) | collective-permute-done | bytes 262176 | tf_op jit(solution)/shard_map/ppermute | solution.py:198
  58.4 3.7 %collective-permute-start.7 = (bf16[32,4096]{1,0:T(8,128)(2,1)}, bf16[32,4096]{1,0:T(8,128)(2,1)}, u32[]{:S(2)}, u32[]{:S(2)}) collective-permute-start(bf16[32,4096]{1,0:T(8,128)(2,1)} %get-tuple-element.93), channel_id=1, source_target_pairs={{0,6},{1,7},{2,4},{3,5},{4,2},{5,3},{6,0},{7,1},{8,14},{9,15},{10,... | collective-permute-start | bytes 786440 | tf_op jit(solution)/shard_map/ppermute | solution.py:198
  62.1 0.7 collective-permute-done.1.refs_2_
  62.8 12.4 %collective-permute-done.2.refs_3_ = bf16[32,4096]{1,0:T(8,128)(2,1)} collective-permute-done((bf16[32,4096]{1,0:T(8,128)(2,1)}, bf16[32,4096]{1,0:T(8,128)(2,1)}, u32[]{:S(2)}, u32[]{:S(2)}) %collective-permute-start.2) | collective-permute-done | bytes 262176 | tf_op jit(solution)/shard_map/ppermute | solution.py:212
  75.2 11.1 %expert.2 = (bf16[32,4096]{1,0:T(8,128)(2,1)}, bf16[32,4096]{1,0:T(8,128)(2,1)}, bf16[32,4096]{1,0:T(8,128)(2,1)}, bf16[32,4096]{1,0:T(8,128)(2,1)}, bf16[32,409...) custom-call(bf16[32,4096]{1,0:T(8,128)(2,1)} %get-tuple-element.79.r, ...), custom_call_target="tpu_custom_call" | custom-call | flops 1024 | bytes 1024 | tf_op jit(solution)/shard_map/expert/pallas_call | solution.py:27
  86.3 0.0 collective-permute-done.14.refs_7_
  86.3 0.1 collective-permute-start.15
  86.4 2.8 %collective-permute-start.8 = (bf16[32,4096]{1,0:T(8,128)(2,1)}, bf16[32,4096]{1,0:T(8,128)(2,1)}, u32[]{:S(2)}, u32[]{:S(2)}) collective-permute-start(bf16[32,4096]{1,0:T(8,128)(2,1)} %get-tuple-element.94), channel_id=1, source_target_pairs={{0,4},{1,5},{2,6},{3,7},{4,0},{5,1},{6,2},{7,3},{8,12},{9,13},{10,... | collective-permute-start | bytes 786440 | tf_op jit(solution)/shard_map/ppermute | solution.py:198
  89.1 1.6 collective-permute-start.18
  90.7 0.0 collective-permute-start.19
  90.7 1.9 collective-permute-start.20
  92.6 11.7 %collective-permute-done.15.refs_5_ = bf16[32,4096]{1,0:T(8,128)(2,1)} collective-permute-done((bf16[32,4096]{1,0:T(8,128)(2,1)}, bf16[32,4096]{1,0:T(8,128)(2,1)}, u32[]{:S(2)}, u32[]{:S(2)}) %collective-permute-start.15) | collective-permute-done | bytes 262176 | tf_op jit(solution)/shard_map/ppermute | solution.py:198
  104.3 3.3 %collective-permute-done.8.refs_4_ = bf16[32,4096]{1,0:T(8,128)(2,1)} collective-permute-done((bf16[32,4096]{1,0:T(8,128)(2,1)}, bf16[32,4096]{1,0:T(8,128)(2,1)}, u32[]{:S(2)}, u32[]{:S(2)}) %collective-permute-start.8) | collective-permute-done | bytes 262176 | tf_op jit(solution)/shard_map/ppermute | solution.py:198
  107.6 2.4 %collective-permute-start.12 = (bf16[32,4096]{1,0:T(8,128)(2,1)}, bf16[32,4096]{1,0:T(8,128)(2,1)}, u32[]{:S(2)}, u32[]{:S(2)}) collective-permute-start(bf16[32,4096]{1,0:T(8,128)(2,1)} %get-tuple-element.102), channel_id=1, source_target_pairs={{0,6},{1,7},{2,4},{3,5},{4,2},{5,3},{6,0},{7,1},{8,14},{9,15},{10,... | collective-permute-start | bytes 786440 | tf_op jit(solution)/shard_map/ppermute | solution.py:198
  110.0 2.6 %collective-permute-start.16 = (bf16[32,4096]{1,0:T(8,128)(2,1)}, bf16[32,4096]{1,0:T(8,128)(2,1)}, u32[]{:S(2)}, u32[]{:S(2)}) collective-permute-start(bf16[32,4096]{1,0:T(8,128)(2,1)} %get-tuple-element.110), channel_id=1, source_target_pairs={{0,7},{1,6},{2,5},{3,4},{4,3},{5,2},{6,1},{7,0},{8,15},{9,14},{10,... | collective-permute-start | bytes 786440 | tf_op jit(solution)/shard_map/ppermute | solution.py:198
  112.6 0.0 collective-permute-done.18.refs_1_
  112.6 0.0 collective-permute-done.19.refs_2_
  112.6 11.3 %expert.3 = (bf16[32,4096]{1,0:T(8,128)(2,1)}, bf16[32,4096]{1,0:T(8,128)(2,1)}, bf16[32,4096]{1,0:T(8,128)(2,1)}, bf16[32,4096]{1,0:T(8,128)(2,1)}, bf16[32,409...) custom-call(bf16[32,4096]{1,0:T(8,128)(2,1)} %get-tuple-element.114., ...), custom_call_target="tpu_custom_call" | custom-call | flops 1024 | bytes 1024 | tf_op jit(solution)/shard_map/expert/pallas_call | solution.py:27
  123.9 4.8 %weight_part.4 = (bf16[16,2176]{1,0:T(8,128)(2,1)}, bf16[496,2176]{1,0:T(8,128)(2,1)}) custom-call(s32[1]{0:T(128)} %bitcast.4.refs_0_, bf16[256,4096]{1,0:T(8,128)(2,1)} %get-tuple-element.134.refs_1_, bf16[256,1408]{1,0:T(8,128)(2,1)} %get-tuple-element.123.refs_2_, bf16[256,704]{1,0:T(8,128)(2,1)} %get-tuple-element.124.refs_3_, ...), custom_call_target="tpu_custom_call" | custom-call | flops 1024 | bytes 1024 | tf_op jit(solution)/shard_map/weight_part/pallas_call | solution.py:27
  128.8 0.1 collective-permute-start.21
  128.8 1.6 collective-permute-done.21.refs_7_
  130.4 0.0 collective-permute-done.12.refs_9_
  130.4 0.0 collective-permute-done.16.refs_10_
  130.4 0.2 collective-permute-start.22
  130.6 2.7 %collective-permute-start.17 = (bf16[32,4096]{1,0:T(8,128)(2,1)}, bf16[32,4096]{1,0:T(8,128)(2,1)}, u32[]{:S(2)}, u32[]{:S(2)}) collective-permute-start(bf16[32,4096]{1,0:T(8,128)(2,1)} %get-tuple-element.111), channel_id=1, source_target_pairs={{0,5},{1,4},{2,7},{3,6},{4,1},{5,0},{6,3},{7,2},{8,13},{9,12},{10,... | collective-permute-start | bytes 786440 | tf_op jit(solution)/shard_map/ppermute | solution.py:198
  133.3 4.7 %weight_part.5 = bf16[512,2176]{1,0:T(8,128)(2,1)} custom-call(s32[1]{0:T(128)} %bitcast.5.refs_0_, bf16[256,4096]{1,0:T(8,128)(2,1)} %get-tuple-element.134.refs_1_, bf16[256,1408]{1,0:T(8,128)(2,1)} %get-tuple-element.123.refs_2_, bf16[256,704]{1,0:T(8,128)(2,1)} %get-tuple-element.124.refs_3_, bf16[256,4096]{1,0:T(8,128)(2,1)} %get-tuple-element.125.refs_4_, ...), custom_call_target="tpu_custom_call" | custom-call | flops 1024 | bytes 1024 | tf_op jit(solution)/shard_map/weight_part/pallas_call | solution.py:27
  138.1 7.9 %collective-permute-done.11.refs_6_ = bf16[32,4096]{1,0:T(8,128)(2,1)} collective-permute-done((bf16[32,4096]{1,0:T(8,128)(2,1)}, bf16[32,4096]{1,0:T(8,128)(2,1)}, u32[]{:S(2)}, u32[]{:S(2)}) %collective-permute-start.11) | collective-permute-done | bytes 262176 | tf_op jit(solution)/shard_map/ppermute | solution.py:212
  146.0 0.0 collective-permute-done.17.refs_8_
  146.0 5.6 %weight_part.6 = bf16[512,2176]{1,0:T(8,128)(2,1)} custom-call(s32[1]{0:T(128)} %bitcast.6.refs_0_, bf16[256,4096]{1,0:T(8,128)(2,1)} %get-tuple-element.134.refs_1_, bf16[256,1408]{1,0:T(8,128)(2,1)} %get-tuple-element.123.refs_2_, bf16[256,704]{1,0:T(8,128)(2,1)} %get-tuple-element.124.refs_3_, bf16[256,4096]{1,0:T(8,128)(2,1)} %get-tuple-element.125.refs_4_, ...), custom_call_target="tpu_custom_call" | custom-call | flops 1024 | bytes 1024 | tf_op jit(solution)/shard_map/weight_part/pallas_call | solution.py:27
  151.6 1.5 collective-permute-start.24
  153.1 10.8 %collective-permute-start.13 = (bf16[32,4096]{1,0:T(8,128)(2,1)}, bf16[32,4096]{1,0:T(8,128)(2,1)}, u32[]{:S(2)}, u32[]{:S(2)}) collective-permute-start(bf16[32,4096]{1,0:T(8,128)(2,1)} %get-tuple-element.103), channel_id=1, source_target_pairs={{0,4},{1,5},{2,6},{3,7},{4,0},{5,1},{6,2},{7,3},{8,12},{9,13},{10,... | collective-permute-start | bytes 786440 | tf_op jit(solution)/shard_map/ppermute | solution.py:198
  164.0 0.0 collective-permute-start.9
  164.0 0.0 collective-permute-start.10
  164.0 13.0 %collective-permute-done.13.refs_7_ = bf16[32,4096]{1,0:T(8,128)(2,1)} collective-permute-done((bf16[32,4096]{1,0:T(8,128)(2,1)}, bf16[32,4096]{1,0:T(8,128)(2,1)}, u32[]{:S(2)}, u32[]{:S(2)}) %collective-permute-start.13) | collective-permute-done | bytes 262176 | tf_op jit(solution)/shard_map/ppermute | solution.py:198
  177.0 0.0 collective-permute-start.30
  177.0 0.0 collective-permute-done.9.refs_4_
  177.0 0.7 collective-permute-start.28
  177.7 0.5 collective-permute-done.10.refs_5_
  178.2 4.8 %combine.2 = (bf16[256,2048]{1,0:T(8,128)(2,1)}, bf16[256,2048]{1,0:T(8,128)(2,1)}) custom-call(s32[1,256]{1,0:T(1,128)} %xor_bitcast_fusion.refs_0_, bf16[256,2048]{1,0:T(8,128)(2,1)} %refs_1_.5, bf16[256,2048]{1,0:T(8,128)(2,1)} %refs_2_.5, bf16[32,4096]{1,0:T(8,128)(2,1)} %get-tuple-element.89.refs_3_, bf16[32,4096]{1,0:T(8,128)(2,1)} %collective-permute-done.9.refs_4_, ...), custom_call_target="tpu_custom_call" | custom-call | flops 1024 | bytes 1024 | tf_op jit(solution)/shard_map/combine/pallas_call | solution.py:27
  183.0 0.8 collective-permute-start.27
  183.8 5.5 %collective-permute-done.30.refs_10_ = bf16[32,4096]{1,0:T(8,128)(2,1)} collective-permute-done((bf16[32,4096]{1,0:T(8,128)(2,1)}, bf16[32,4096]{1,0:T(8,128)(2,1)}, u32[]{:S(2)}, u32[]{:S(2)}) %collective-permute-start.30) | collective-permute-done | bytes 262176 | tf_op jit(solution)/shard_map/ppermute | solution.py:198
  189.3 7.2 %collective-permute-start.26 = (bf16[32,4096]{1,0:T(8,128)(2,1)}, bf16[32,4096]{1,0:T(8,128)(2,1)}, u32[]{:S(2)}, u32[]{:S(2)}) collective-permute-start(bf16[32,4096]{1,0:T(8,128)(2,1)} %get-tuple-element.140), channel_id=1, source_target_pairs={{0,2},{1,3},{2,0},{3,1},{4,6},{5,7},{6,4},{7,5},{8,10},{9,11},{10,... | collective-permute-start | bytes 786440 | tf_op jit(solution)/shard_map/ppermute | solution.py:212
  196.5 0.0 collective-permute-done.28.refs_9_
  196.5 3.3 %collective-permute-start.25 = (bf16[32,4096]{1,0:T(8,128)(2,1)}, bf16[32,4096]{1,0:T(8,128)(2,1)}, u32[]{:S(2)}, u32[]{:S(2)}) collective-permute-start(bf16[32,4096]{1,0:T(8,128)(2,1)} %get-tuple-element.138), channel_id=1, source_target_pairs={{0,1},{1,0},{2,3},{3,2},{4,5},{5,4},{6,7},{7,6},{8,9},{9,8},{10,11... | collective-permute-start | bytes 786440 | tf_op jit(solution)/shard_map/ppermute | solution.py:212
  199.8 2.1 collective-permute-done.24.refs_8_
  201.9 1.5 collective-permute-start.31
  203.3 0.0 collective-permute-done.23.refs_7_
  203.3 10.8 %collective-permute-start.29 = (bf16[32,4096]{1,0:T(8,128)(2,1)}, bf16[32,4096]{1,0:T(8,128)(2,1)}, u32[]{:S(2)}, u32[]{:S(2)}) collective-permute-start(bf16[32,4096]{1,0:T(8,128)(2,1)} %get-tuple-element.146), channel_id=1, source_target_pairs={{0,4},{1,5},{2,6},{3,7},{4,0},{5,1},{6,2},{7,3},{8,12},{9,13},{10,... | collective-permute-start | bytes 786440 | tf_op jit(solution)/shard_map/ppermute | solution.py:198
  214.2 6.7 %weight_part.7 = (f32[512,1408]{1,0:T(8,128)}, f32[704,512]{1,0:T(8,128)}) custom-call(s32[1]{0:T(128)} %bitcast.3.refs_0_, bf16[256,4096]{1,0:T(8,128)(2,1)} %get-tuple-element.134.refs_1_, bf16[256,1408]{1,0:T(8,128)(2,1)} %get-tuple-element.123.refs_2_, bf16[256,704]{1,0:T(8,128)(2,1)} %get-tuple-element.124.refs_3_, ...), custom_call_target="tpu_custom_call" | custom-call | flops 1024 | bytes 1024 | tf_op jit(solution)/shard_map/weight_part/pallas_call | solution.py:27
  220.9 8.8 %collective-permute-done.29.refs_7_ = bf16[32,4096]{1,0:T(8,128)(2,1)} collective-permute-done((bf16[32,4096]{1,0:T(8,128)(2,1)}, bf16[32,4096]{1,0:T(8,128)(2,1)}, u32[]{:S(2)}, u32[]{:S(2)}) %collective-permute-start.29) | collective-permute-done | bytes 262176 | tf_op jit(solution)/shard_map/ppermute | solution.py:198
  229.7 4.7 %combine.3 = (bf16[256,2048]{1,0:T(8,128)(2,1)}, bf16[256,2048]{1,0:T(8,128)(2,1)}) custom-call(s32[1,256]{1,0:T(1,128)} %xor_bitcast_fusion.refs_0_, bf16[256,2048]{1,0:T(8,128)(2,1)} %get-tuple-element.112.refs_1_, bf16[256,2048]{1,0:T(8,128)(2,1)} %get-tuple-element.113.refs_2_, bf16[32,4096]{1,0:T(8,128)(2,1)} %get-tuple-element.136.refs_3_, ...), custom_call_target="tpu_custom_call" | custom-call | flops 1024 | bytes 1024 | tf_op jit(solution)/shard_map/combine/pallas_call | solution.py:27
  (11 shorter events, 0.0 us)
Async XLA Ops:
  5.8 13.6 %collective-permute-start.5 = (bf16[32,4096]{1,0:T(8,128)(2,1)}, bf16[32,4096]{1,0:T(8,128)(2,1)}, u32[]{:S(2)}, u32[]{:S(2)}) collective-permute-start(bf16[32,4096]{1,0:T(8,128)(2,1)} %get-tuple-element.87), channel_id=1, source_target_pairs={{0,7},{1,6},{2,5},{3,4},{4,3},{5,2},{6,1},{7,0},{8,15},{9,14},{10,... | collective-permute-start | bytes 786440 | tf_op jit(solution)/shard_map/ppermute | solution.py:198
  11.9 20.6 %collective-permute-start.3 = (bf16[32,4096]{1,0:T(8,128)(2,1)}, bf16[32,4096]{1,0:T(8,128)(2,1)}, u32[]{:S(2)}, u32[]{:S(2)}) collective-permute-start(bf16[32,4096]{1,0:T(8,128)(2,1)} %get-tuple-element.84), channel_id=1, source_target_pairs={{0,6},{1,7},{2,4},{3,5},{4,2},{5,3},{6,0},{7,1},{8,14},{9,15},{10,... | collective-permute-start | bytes 786440 | tf_op jit(solution)/shard_map/ppermute | solution.py:198
  19.4 32.9 %collective-permute-start.6 = (bf16[32,4096]{1,0:T(8,128)(2,1)}, bf16[32,4096]{1,0:T(8,128)(2,1)}, u32[]{:S(2)}, u32[]{:S(2)}) collective-permute-start(bf16[32,4096]{1,0:T(8,128)(2,1)} %get-tuple-element.88), channel_id=1, source_target_pairs={{0,5},{1,4},{2,7},{3,6},{4,1},{5,0},{6,3},{7,2},{8,13},{9,12},{10,... | collective-permute-start | bytes 786440 | tf_op jit(solution)/shard_map/ppermute | solution.py:198
  32.5 25.9 %collective-permute-start.4 = (bf16[32,4096]{1,0:T(8,128)(2,1)}, bf16[32,4096]{1,0:T(8,128)(2,1)}, u32[]{:S(2)}, u32[]{:S(2)}) collective-permute-start(bf16[32,4096]{1,0:T(8,128)(2,1)} %get-tuple-element.85), channel_id=1, source_target_pairs={{0,4},{1,5},{2,6},{3,7},{4,0},{5,1},{6,2},{7,3},{8,12},{9,13},{10,... | collective-permute-start | bytes 786440 | tf_op jit(solution)/shard_map/ppermute | solution.py:198
  42.8 19.3 %collective-permute-start = (bf16[32,4096]{1,0:T(8,128)(2,1)}, bf16[32,4096]{1,0:T(8,128)(2,1)}, u32[]{:S(2)}, u32[]{:S(2)}) collective-permute-start(bf16[32,4096]{1,0:T(8,128)(2,1)} %get-tuple-element.80), channel_id=1, source_target_pairs={{0,1},{1,0},{2,3},{3,2},{4,5},{5,4},{6,7},{7,6},{8,9},{9,8},{10,11... | collective-permute-start | bytes 786440 | tf_op jit(solution)/shard_map/ppermute | solution.py:212
  43.3 19.4 %collective-permute-start.1 = (bf16[32,4096]{1,0:T(8,128)(2,1)}, bf16[32,4096]{1,0:T(8,128)(2,1)}, u32[]{:S(2)}, u32[]{:S(2)}) collective-permute-start(bf16[32,4096]{1,0:T(8,128)(2,1)} %get-tuple-element.81), channel_id=1, source_target_pairs={{0,2},{1,3},{2,0},{3,1},{4,6},{5,7},{6,4},{7,5},{8,10},{9,11},{10,... | collective-permute-start | bytes 786440 | tf_op jit(solution)/shard_map/ppermute | solution.py:212
  43.4 31.8 %collective-permute-start.2 = (bf16[32,4096]{1,0:T(8,128)(2,1)}, bf16[32,4096]{1,0:T(8,128)(2,1)}, u32[]{:S(2)}, u32[]{:S(2)}) collective-permute-start(bf16[32,4096]{1,0:T(8,128)(2,1)} %get-tuple-element.82), channel_id=1, source_target_pairs={{0,3},{1,2},{2,1},{3,0},{4,7},{5,6},{6,5},{7,4},{8,11},{9,10},{10,... | collective-permute-start | bytes 786440 | tf_op jit(solution)/shard_map/ppermute | solution.py:212
  52.3 33.9 %collective-permute-start.14 = (bf16[32,4096]{1,0:T(8,128)(2,1)}, bf16[32,4096]{1,0:T(8,128)(2,1)}, u32[]{:S(2)}, u32[]{:S(2)}) collective-permute-start(bf16[32,4096]{1,0:T(8,128)(2,1)} %get-tuple-element.108), channel_id=1, source_target_pairs={{0,7},{1,6},{2,5},{3,4},{4,3},{5,2},{6,1},{7,0},{8,15},{9,14},{10,... | collective-permute-start | bytes 786440 | tf_op jit(solution)/shard_map/ppermute | solution.py:198
  58.4 28.0 %collective-permute-start.7 = (bf16[32,4096]{1,0:T(8,128)(2,1)}, bf16[32,4096]{1,0:T(8,128)(2,1)}, u32[]{:S(2)}, u32[]{:S(2)}) collective-permute-start(bf16[32,4096]{1,0:T(8,128)(2,1)} %get-tuple-element.93), channel_id=1, source_target_pairs={{0,6},{1,7},{2,4},{3,5},{4,2},{5,3},{6,0},{7,1},{8,14},{9,15},{10,... | collective-permute-start | bytes 786440 | tf_op jit(solution)/shard_map/ppermute | solution.py:198
  86.3 18.1 %collective-permute-start.15 = (bf16[32,4096]{1,0:T(8,128)(2,1)}, bf16[32,4096]{1,0:T(8,128)(2,1)}, u32[]{:S(2)}, u32[]{:S(2)}) collective-permute-start(bf16[32,4096]{1,0:T(8,128)(2,1)} %get-tuple-element.109), channel_id=1, source_target_pairs={{0,5},{1,4},{2,7},{3,6},{4,1},{5,0},{6,3},{7,2},{8,13},{9,12},{10,... | collective-permute-start | bytes 786440 | tf_op jit(solution)/shard_map/ppermute | solution.py:198
  86.4 21.2 %collective-permute-start.8 = (bf16[32,4096]{1,0:T(8,128)(2,1)}, bf16[32,4096]{1,0:T(8,128)(2,1)}, u32[]{:S(2)}, u32[]{:S(2)}) collective-permute-start(bf16[32,4096]{1,0:T(8,128)(2,1)} %get-tuple-element.94), channel_id=1, source_target_pairs={{0,4},{1,5},{2,6},{3,7},{4,0},{5,1},{6,2},{7,3},{8,12},{9,13},{10,... | collective-permute-start | bytes 786440 | tf_op jit(solution)/shard_map/ppermute | solution.py:198
  89.1 23.5 %collective-permute-start.18 = (bf16[32,4096]{1,0:T(8,128)(2,1)}, bf16[32,4096]{1,0:T(8,128)(2,1)}, u32[]{:S(2)}, u32[]{:S(2)}) collective-permute-start(bf16[32,4096]{1,0:T(8,128)(2,1)} %get-tuple-element.116), channel_id=1, source_target_pairs={{0,1},{1,0},{2,3},{3,2},{4,5},{5,4},{6,7},{7,6},{8,9},{9,8},{10,11... | collective-permute-start | bytes 786440 | tf_op jit(solution)/shard_map/ppermute | solution.py:212
  90.7 21.9 %collective-permute-start.19 = (bf16[32,4096]{1,0:T(8,128)(2,1)}, bf16[32,4096]{1,0:T(8,128)(2,1)}, u32[]{:S(2)}, u32[]{:S(2)}) collective-permute-start(bf16[32,4096]{1,0:T(8,128)(2,1)} %get-tuple-element.118), channel_id=1, source_target_pairs={{0,2},{1,3},{2,0},{3,1},{4,6},{5,7},{6,4},{7,5},{8,10},{9,11},{10,... | collective-permute-start | bytes 786440 | tf_op jit(solution)/shard_map/ppermute | solution.py:212
  90.7 21.9 %collective-permute-start.20 = (bf16[32,4096]{1,0:T(8,128)(2,1)}, bf16[32,4096]{1,0:T(8,128)(2,1)}, u32[]{:S(2)}, u32[]{:S(2)}) collective-permute-start(bf16[32,4096]{1,0:T(8,128)(2,1)} %get-tuple-element.120), channel_id=1, source_target_pairs={{0,3},{1,2},{2,1},{3,0},{4,7},{5,6},{6,5},{7,4},{8,11},{9,10},{10,... | collective-permute-start | bytes 786440 | tf_op jit(solution)/shard_map/ppermute | solution.py:212
  107.6 22.8 %collective-permute-start.12 = (bf16[32,4096]{1,0:T(8,128)(2,1)}, bf16[32,4096]{1,0:T(8,128)(2,1)}, u32[]{:S(2)}, u32[]{:S(2)}) collective-permute-start(bf16[32,4096]{1,0:T(8,128)(2,1)} %get-tuple-element.102), channel_id=1, source_target_pairs={{0,6},{1,7},{2,4},{3,5},{4,2},{5,3},{6,0},{7,1},{8,14},{9,15},{10,... | collective-permute-start | bytes 786440 | tf_op jit(solution)/shard_map/ppermute | solution.py:198
  110.0 20.4 %collective-permute-start.16 = (bf16[32,4096]{1,0:T(8,128)(2,1)}, bf16[32,4096]{1,0:T(8,128)(2,1)}, u32[]{:S(2)}, u32[]{:S(2)}) collective-permute-start(bf16[32,4096]{1,0:T(8,128)(2,1)} %get-tuple-element.110), channel_id=1, source_target_pairs={{0,7},{1,6},{2,5},{3,4},{4,3},{5,2},{6,1},{7,0},{8,15},{9,14},{10,... | collective-permute-start | bytes 786440 | tf_op jit(solution)/shard_map/ppermute | solution.py:198
  128.8 1.7 collective-permute-start.21
  130.4 15.6 %collective-permute-start.22 = (bf16[496,2176]{1,0:T(8,128)(2,1)}, bf16[496,2176]{1,0:T(8,128)(2,1)}, u32[]{:S(2)}, u32[]{:S(2)}) collective-permute-start(bf16[496,2176]{1,0:T(8,128)(2,1)} %get-tuple-element.133), channel_id=1, source_target_pairs={{0,8},{8,0},{16,24},{24,16},{1,9},{9,1},{17,25},{25,17},{2,10},{10... | collective-permute-start | bytes 6475784 | tf_op jit(solution)/shard_map/ppermute | solution.py:198
  130.6 15.4 %collective-permute-start.11 = (bf16[32,4096]{1,0:T(8,128)(2,1)}, bf16[32,4096]{1,0:T(8,128)(2,1)}, u32[]{:S(2)}, u32[]{:S(2)}) collective-permute-start(bf16[32,4096]{1,0:T(8,128)(2,1)} %get-tuple-element.99), channel_id=1, source_target_pairs={{0,3},{1,2},{2,1},{3,0},{4,7},{5,6},{6,5},{7,4},{8,11},{9,10},{10,... | collective-permute-start | bytes 786440 | tf_op jit(solution)/shard_map/ppermute | solution.py:212
  130.6 15.4 %collective-permute-start.17 = (bf16[32,4096]{1,0:T(8,128)(2,1)}, bf16[32,4096]{1,0:T(8,128)(2,1)}, u32[]{:S(2)}, u32[]{:S(2)}) collective-permute-start(bf16[32,4096]{1,0:T(8,128)(2,1)} %get-tuple-element.111), channel_id=1, source_target_pairs={{0,5},{1,4},{2,7},{3,6},{4,1},{5,0},{6,3},{7,2},{8,13},{9,12},{10,... | collective-permute-start | bytes 786440 | tf_op jit(solution)/shard_map/ppermute | solution.py:198
  151.6 50.3 %collective-permute-start.24 = (bf16[512,2176]{1,0:T(8,128)(2,1)}, bf16[512,2176]{1,0:T(8,128)(2,1)}, u32[]{:S(2)}, u32[]{:S(2)}) collective-permute-start(bf16[512,2176]{1,0:T(8,128)(2,1)} %weight_part.6), channel_id=1, source_target_pairs={{0,16},{8,24},{16,0},{24,8},{1,17},{9,25},{17,1},{25,9},{2,18},{10... | collective-permute-start | bytes 6684680 | tf_op jit(solution)/shard_map/ppermute | solution.py:198
  153.1 50.2 %collective-permute-start.23 = (bf16[512,2176]{1,0:T(8,128)(2,1)}, bf16[512,2176]{1,0:T(8,128)(2,1)}, u32[]{:S(2)}, u32[]{:S(2)}) collective-permute-start(bf16[512,2176]{1,0:T(8,128)(2,1)} %weight_part.5), channel_id=1, source_target_pairs={{0,8},{8,0},{16,24},{24,16},{1,9},{9,1},{17,25},{25,17},{2,10},{10... | collective-permute-start | bytes 6684680 | tf_op jit(solution)/shard_map/ppermute | solution.py:198
  153.1 23.8 %collective-permute-start.13 = (bf16[32,4096]{1,0:T(8,128)(2,1)}, bf16[32,4096]{1,0:T(8,128)(2,1)}, u32[]{:S(2)}, u32[]{:S(2)}) collective-permute-start(bf16[32,4096]{1,0:T(8,128)(2,1)} %get-tuple-element.103), channel_id=1, source_target_pairs={{0,4},{1,5},{2,6},{3,7},{4,0},{5,1},{6,2},{7,3},{8,12},{9,13},{10,... | collective-permute-start | bytes 786440 | tf_op jit(solution)/shard_map/ppermute | solution.py:198
  164.0 13.0 %collective-permute-start.9 = (bf16[32,4096]{1,0:T(8,128)(2,1)}, bf16[32,4096]{1,0:T(8,128)(2,1)}, u32[]{:S(2)}, u32[]{:S(2)}) collective-permute-start(bf16[32,4096]{1,0:T(8,128)(2,1)} %get-tuple-element.95), channel_id=1, source_target_pairs={{0,1},{1,0},{2,3},{3,2},{4,5},{5,4},{6,7},{7,6},{8,9},{9,8},{10,11... | collective-permute-start | bytes 786440 | tf_op jit(solution)/shard_map/ppermute | solution.py:212
  164.0 14.2 %collective-permute-start.10 = (bf16[32,4096]{1,0:T(8,128)(2,1)}, bf16[32,4096]{1,0:T(8,128)(2,1)}, u32[]{:S(2)}, u32[]{:S(2)}) collective-permute-start(bf16[32,4096]{1,0:T(8,128)(2,1)} %get-tuple-element.97), channel_id=1, source_target_pairs={{0,2},{1,3},{2,0},{3,1},{4,6},{5,7},{6,4},{7,5},{8,10},{9,11},{10,... | collective-permute-start | bytes 786440 | tf_op jit(solution)/shard_map/ppermute | solution.py:212
  177.0 12.3 %collective-permute-start.30 = (bf16[32,4096]{1,0:T(8,128)(2,1)}, bf16[32,4096]{1,0:T(8,128)(2,1)}, u32[]{:S(2)}, u32[]{:S(2)}) collective-permute-start(bf16[32,4096]{1,0:T(8,128)(2,1)} %get-tuple-element.149), channel_id=1, source_target_pairs={{0,7},{1,6},{2,5},{3,4},{4,3},{5,2},{6,1},{7,0},{8,15},{9,14},{10,... | collective-permute-start | bytes 786440 | tf_op jit(solution)/shard_map/ppermute | solution.py:198
  177.0 19.5 %collective-permute-start.28 = (bf16[32,4096]{1,0:T(8,128)(2,1)}, bf16[32,4096]{1,0:T(8,128)(2,1)}, u32[]{:S(2)}, u32[]{:S(2)}) collective-permute-start(bf16[32,4096]{1,0:T(8,128)(2,1)} %get-tuple-element.145), channel_id=1, source_target_pairs={{0,6},{1,7},{2,4},{3,5},{4,2},{5,3},{6,0},{7,1},{8,14},{9,15},{10,... | collective-permute-start | bytes 786440 | tf_op jit(solution)/shard_map/ppermute | solution.py:198
  183.0 37.9 %collective-permute-start.27 = (bf16[32,4096]{1,0:T(8,128)(2,1)}, bf16[32,4096]{1,0:T(8,128)(2,1)}, u32[]{:S(2)}, u32[]{:S(2)}) collective-permute-start(bf16[32,4096]{1,0:T(8,128)(2,1)} %get-tuple-element.142), channel_id=1, source_target_pairs={{0,3},{1,2},{2,1},{3,0},{4,7},{5,6},{6,5},{7,4},{8,11},{9,10},{10,... | collective-permute-start | bytes 786440 | tf_op jit(solution)/shard_map/ppermute | solution.py:212
  189.3 31.5 %collective-permute-start.26 = (bf16[32,4096]{1,0:T(8,128)(2,1)}, bf16[32,4096]{1,0:T(8,128)(2,1)}, u32[]{:S(2)}, u32[]{:S(2)}) collective-permute-start(bf16[32,4096]{1,0:T(8,128)(2,1)} %get-tuple-element.140), channel_id=1, source_target_pairs={{0,2},{1,3},{2,0},{3,1},{4,6},{5,7},{6,4},{7,5},{8,10},{9,11},{10,... | collective-permute-start | bytes 786440 | tf_op jit(solution)/shard_map/ppermute | solution.py:212
  196.5 24.3 %collective-permute-start.25 = (bf16[32,4096]{1,0:T(8,128)(2,1)}, bf16[32,4096]{1,0:T(8,128)(2,1)}, u32[]{:S(2)}, u32[]{:S(2)}) collective-permute-start(bf16[32,4096]{1,0:T(8,128)(2,1)} %get-tuple-element.138), channel_id=1, source_target_pairs={{0,1},{1,0},{2,3},{3,2},{4,5},{5,4},{6,7},{7,6},{8,9},{9,8},{10,11... | collective-permute-start | bytes 786440 | tf_op jit(solution)/shard_map/ppermute | solution.py:212
  201.9 19.0 %collective-permute-start.31 = (bf16[32,4096]{1,0:T(8,128)(2,1)}, bf16[32,4096]{1,0:T(8,128)(2,1)}, u32[]{:S(2)}, u32[]{:S(2)}) collective-permute-start(bf16[32,4096]{1,0:T(8,128)(2,1)} %get-tuple-element.150), channel_id=1, source_target_pairs={{0,5},{1,4},{2,7},{3,6},{4,1},{5,0},{6,3},{7,2},{8,13},{9,12},{10,... | collective-permute-start | bytes 786440 | tf_op jit(solution)/shard_map/ppermute | solution.py:198
  203.3 26.3 %collective-permute-start.29 = (bf16[32,4096]{1,0:T(8,128)(2,1)}, bf16[32,4096]{1,0:T(8,128)(2,1)}, u32[]{:S(2)}, u32[]{:S(2)}) collective-permute-start(bf16[32,4096]{1,0:T(8,128)(2,1)} %get-tuple-element.146), channel_id=1, source_target_pairs={{0,4},{1,5},{2,6},{3,7},{4,0},{5,1},{6,2},{7,3},{8,12},{9,13},{10,... | collective-permute-start | bytes 786440 | tf_op jit(solution)/shard_map/ppermute | solution.py:198

commit v7 on v6

--- a/solution.py
+++ b/solution.py
@@ -1,5 +1,6 @@
 import jax
 import jax.numpy as jnp
+import numpy as np
 from jax import lax
 from jax.experimental import pallas as pl
 from jax.experimental.pallas import tpu as pltpu
@@ -55,13 +56,14 @@
         copy.wait()
 
 
-def place_kernel(part, cap, rel_ref, tokens_ref, grad_ref, *refs):
+def place_kernel(part, cap, me_ref, table_ref, ids_ref, tokens_ref, grad_ref, *refs):
     blocks, (data, moved, sems) = refs[:-3], refs[-3:]
-    experts = len(blocks)
-    rows, width = tokens_ref.shape
+    width = tokens_ref.shape[1]
     copies = Copies(sems)
-    loads = [copies.start(ref, data.at[:, side * width : (side + 1) * width]) for side, ref in enumerate((tokens_ref, grad_ref))]
-    placing = placing_of(rel_ref[...], experts, part, cap)
+    loads = [
+        copies.start(ref, data.at[:, side * width : (side + 1) * width]) for side, ref in enumerate((tokens_ref, grad_ref))
+    ]
+    placing = placing_of(me_ref, table_ref, ids_ref, len(blocks), part, cap)
     stores = []
     for side in range(2):
         here = slice(side * width, (side + 1) * width)
@@ -72,8 +74,13 @@
     wait(stores)
 
 
-def placing_of(rel, experts, part, cap):
-    rows = rel.shape[1]
+def placing_of(me_ref, table_ref, ids_ref, experts, part, cap):
+    ids = ids_ref[...]
+    rows = ids.shape[1]
+    me = me_ref[0]
+    rel = jnp.zeros((1, rows), jnp.int32)
+    for expert in range(experts):
+        rel = jnp.where(ids == expert, table_ref[me, expert], rel)
     onehot = lax.broadcasted_iota(jnp.int32, (max(experts, 16), rows), 0) == rel
     before = lax.broadcasted_iota(jnp.int32, (rows, rows), 0) < lax.broadcasted_iota(jnp.int32, (rows, rows), 1)
     ranks = dot(onehot.astype(BF16), before.astype(BF16), PLAIN)
@@ -165,13 +172,13 @@
     wait(stores)
 
 
-def combine_kernel(part, cap, rel_ref, tokens_ref, grad_ref, *refs):
+def combine_kernel(part, cap, me_ref, table_ref, ids_ref, tokens_ref, grad_ref, *refs):
     blocks, (mixed_out, grad_out, data, back, sems) = refs[:-5], refs[-5:]
     width = tokens_ref.shape[1]
     copies = Copies(sems)
     loads = [copies.start(ref, data.at[:, side * width : (side + 1) * width]) for side, ref in enumerate((tokens_ref, grad_ref))]
     loads += [copies.start(block, back.at[index * cap : (index + 1) * cap]) for index, block in enumerate(blocks)]
-    placing = placing_of(rel_ref[...], len(blocks), part, cap)
+    placing = placing_of(me_ref, table_ref, ids_ref, len(blocks), part, cap)
     wait(loads)
     stores = []
     for side, out in enumerate((mixed_out, grad_out)):
@@ -199,18 +206,31 @@
         return self.done[-1]
 
 
-def exchange(blocks, far, held={}):
-    experts = len(blocks)
+def rounds_of(experts):
     half = experts // 2
-    moved = {0: blocks[0]}
-    earlier = far.done[-1:]
-    for mask in range(half - 1, -1, -1):
-        pairs = [(i, i ^ (mask + half)) for i in range(experts)]
-        moved[mask + half] = far.send(blocks[mask + half], "exp", pairs, *held.get(mask, ()))
-    for mask in range(half - 1, 0, -1):
-        pairs = [(i, i ^ mask) for i in range(experts)]
-        moved[mask] = lax.ppermute(after(blocks[mask], *earlier), "exp", pairs)
-    return [moved[mask] for mask in range(experts)]
+    rounds = [list(range(experts))]
+    for near in range(1, half):
+        units = [unit for unit in range(1, half) if bin(unit & near).count("1") % 2 == 0]
+        for turn in range(2):
+            far_now = [bin(place & units[0]).count("1") % 2 == turn if units else not turn for place in range(experts)]
+            rounds.append([place ^ (near + half if far else near) for place, far in zip(range(experts), far_now)])
+    rounds.append([place ^ half for place in range(experts)])
+    return rounds
+
+
+def table_of(rounds):
+    table = np.zeros((len(rounds), len(rounds)), np.int32)
+    for number, partners in enumerate(rounds):
+        for place, partner in enumerate(partners):
+            table[place, partner] = number
+    return table
+
+
+def exchange(blocks, rounds, lane, held={}):
+    moved = [blocks[0]]
+    for number in range(1, len(rounds)):
+        moved.append(lane.send(blocks[number], "exp", list(enumerate(rounds[number])), *held.get(number, ())))
+    return moved
 
 
 def body(tokens, expert_ids, gate_up_weight, down_weight, grad_out):
@@ -227,8 +247,12 @@
     share = width // groups
     pair = like((cap, 2 * width))
     sems = pltpu.SemaphoreType.DMA
-    far = Lane(2)
-    rel = expert_ids.reshape(1, rows) ^ lax.axis_index("exp").astype(jnp.int32)
+    lane = Lane(4)
+    last = experts - 1
+    ids = expert_ids.reshape(1, rows)
+    me = lax.axis_index("exp").astype(jnp.int32)[None]
+    rounds = rounds_of(experts)
+    table = jnp.asarray(table_of(rounds))
     group = lax.axis_index("grp").astype(jnp.int32)
 
     def place(part):
@@ -238,7 +262,8 @@
             [pair] * experts,
             [pltpu.VMEM((rows, 2 * width), BF16), pltpu.VMEM((slots, 2 * width), BF16), sems((2 + 2 * experts,))],
             [tokens, grad_out],
-            [rel],
+            [ids],
+            [me, table],
         )
 
     def expert(blocks):
@@ -282,20 +307,20 @@
             [like((rows, width))] * 2,
             [pltpu.VMEM((rows, 2 * width), BF16), pltpu.VMEM((slots, 2 * width), BF16), sems((4 + experts,))],
             [first, second, *blocks],
-            [rel],
+            [ids],
+            [me, table],
         )
 
     sent = [place(part) for part in range(parts)]
     results = []
     for part in range(parts):
-        held = {0: (results[-1][0][0],)} if results else {}
-        results.append(expert(exchange(sent[part], far, held)))
+        held = {last: (results[-1][0][0],)} if results else {}
+        results.append(expert(exchange(sent[part], rounds, lane, held)))
     kept = [result[1] for result in results]
 
-    count = len(far.done)
-    back = [exchange(results[0][0], far)]
-    far_out = far.done[count:]
-    near_out = back[0][experts // 2 - 1 : 0 : -1]
+    count = len(lane.done)
+    back = [exchange(results[0][0], rounds, lane)]
+    done = lane.done[count:]
 
     received = {q: [] for q in range(groups)}
     sums = kept[0][0]
@@ -303,17 +328,18 @@
         low = q & -q
         first_of_all = q == groups - 1
         if low == 2 and received[q ^ low]:
-            sums = after(sums, *far_out[2:3], *near_out[:1])
+            sums = after(sums, *done[3:5])
         sent = weight_part(group ^ q, [[sums, *kept[0][1:]], *kept[1:]], received[q], False, 16 if first_of_all else 0)
         sums = after(sums, sent[0])
-        lane = Lane(1)
         pairs = [(i, i ^ low) for i in range(groups)]
-        received[q ^ low].append([lane.send(piece, "grp", pairs, *(far_out[:2] if index else ())) for index, piece in enumerate(sent)])
+        short = Lane(1)
+        held = [(), done[:3]]
+        received[q ^ low].append([short.send(piece, "grp", pairs, *more) for piece, more in zip(sent, held)])
 
     mixed, grad = tokens, grad_out
     for part in range(1, parts):
         mixed, grad = combine(part - 1, mixed, grad, back[-1])
-        back.append(exchange(results[part][0], far, {0: (mixed, *received[0][-1])}))
+        back.append(exchange(results[part][0], rounds, lane, {last: (mixed, *received[0][-1])}))
     grad_gate_up, grad_down = weight_part(group, [[sums, *kept[0][1:]], *kept[1:]], received[0], True, 0)
     back[-1][0] = after(back[-1][0], grad_gate_up)
     mixed, grad = combine(parts - 1, mixed, grad, back[-1])

time: 235 us -> 225 us (0.957)
  waiting for transfers between devices: 79.4 us -> 74.8 us
  starting transfers between devices: 91.4 us -> 87.4 us
    ppermute x12 -> x0, waiting for transfers between devices: 21.5 us -> none  [exchange(): moved[mask] = lax.ppermute(after(blocks[mask], *earlier), 'exp', pairs)]
    ppermute x12 -> x0, starting transfers between devices: 18.3 us -> none  [exchange(): moved[mask] = lax.ppermute(after(blocks[mask], *earlier), 'exp', pairs)]
    ppermute x20 -> x32, waiting for transfers between devices: 57.9 us -> 74.8 us  [send(): self.done.append(lax.ppermute(after(value, *earlier), axis, pairs))]
    ppermute x20 -> x32, starting transfers between devices: 73.2 us -> 87.4 us  [send(): self.done.append(lax.ppermute(after(value, *earlier), axis, pairs))]
  transfers between devices with their start and end apart: 32 -> 32, of which waited for: 14 -> 12; matrix products, arithmetic and copies ran while one was open for 0% -> 0% of each run, Pallas kernels for 20% -> 21%
where the time goes in v7:
time: 225 us
  starting transfers between devices  87.4 us (39%)
  waiting for transfers between devices  74.8 us (33%)
  Pallas kernels  61.8 us (27%)
    ppermute x32, starting transfers between devices, send(): self.done.append(lax.ppermute(after(value, *earlier), axis, pairs))  87.4 us
    ppermute x32, waiting for transfers between devices, send(): self.done.append(lax.ppermute(after(value, *earlier), axis, pairs))  74.8 us
    pallas_call x10, Pallas kernels, call(): pl.pallas_call(kernel, in_specs=[pl.BlockSpec(memory_space=pltpu.SMEM)] *...  61.8 us
  transfers between devices with their start and end apart: 32, of which 12 were waited for; matrix products, arithmetic and copies ran while one was open for 0% of the time, Pallas kernels for 21%

profile of v7, /device:TPU:0, one launch (start us, length us, event | category | flops | bytes accessed | tf_op | source)
XLA Modules:
  0.0 224.9 jit_solution(13056992138152820511)
XLA Ops:
  0.6 4.0 %place.2 = (bf16[32,4096]{1,0:T(8,128)(2,1)}, bf16[32,4096]{1,0:T(8,128)(2,1)}, bf16[32,4096]{1,0:T(8,128)(2,1)}, bf16[32,4096]{1,0:T(8,128)(2,1)}, bf16[32,4096...) custom-call(s32[1]{0:T(128)} %bitcast.refs_0_, ...), custom_call_target="tpu_custom_call" | custom-call | flops 1024 | bytes 1024 | tf_op jit(solution)/shard_map/place/pallas_call | solution.py:28
  4.6 5.1 %collective-permute-start = (bf16[32,4096]{1,0:T(8,128)(2,1)}, bf16[32,4096]{1,0:T(8,128)(2,1)}, u32[]{:S(2)}, u32[]{:S(2)}) collective-permute-start(bf16[32,4096]{1,0:T(8,128)(2,1)} %get-tuple-element.81), channel_id=1, source_target_pairs={{0,5},{1,4},{2,3},{3,2},{4,1},{5,0},{6,7},{7,6},{8,13},{9,12},{10,... | collective-permute-start | bytes 786440 | tf_op jit(solution)/shard_map/ppermute | solution.py:205
  9.7 0.5 collective-permute-start.1
  10.2 1.3 collective-permute-start.2
  11.5 0.2 collective-permute-start.3
  11.8 11.0 %collective-permute-done.refs_1_ = bf16[32,4096]{1,0:T(8,128)(2,1)} collective-permute-done((bf16[32,4096]{1,0:T(8,128)(2,1)}, bf16[32,4096]{1,0:T(8,128)(2,1)}, u32[]{:S(2)}, u32[]{:S(2)}) %collective-permute-start) | collective-permute-done | bytes 262176 | tf_op jit(solution)/shard_map/ppermute | solution.py:205
  22.8 0.0 collective-permute-start.4
  22.8 0.0 collective-permute-done.1.refs_2_
  22.8 7.0 %collective-permute-start.5 = (bf16[32,4096]{1,0:T(8,128)(2,1)}, bf16[32,4096]{1,0:T(8,128)(2,1)}, u32[]{:S(2)}, u32[]{:S(2)}) collective-permute-start(bf16[32,4096]{1,0:T(8,128)(2,1)} %get-tuple-element.88), channel_id=1, source_target_pairs={{0,3},{1,6},{2,5},{3,0},{4,7},{5,2},{6,1},{7,4},{8,11},{9,14},{10,... | collective-permute-start | bytes 786440 | tf_op jit(solution)/shard_map/ppermute | solution.py:205
  29.8 4.0 %place.3 = (bf16[32,4096]{1,0:T(8,128)(2,1)}, bf16[32,4096]{1,0:T(8,128)(2,1)}, bf16[32,4096]{1,0:T(8,128)(2,1)}, bf16[32,4096]{1,0:T(8,128)(2,1)}, bf16[32,4096...) custom-call(s32[1]{0:T(128)} %bitcast.refs_0_, ...), custom_call_target="tpu_custom_call" | custom-call | flops 1024 | bytes 1024 | tf_op jit(solution)/shard_map/place/pallas_call | solution.py:28
  33.8 0.0 collective-permute-done.2.refs_3_
  33.8 7.8 %collective-permute-start.6 = (bf16[32,4096]{1,0:T(8,128)(2,1)}, bf16[32,4096]{1,0:T(8,128)(2,1)}, u32[]{:S(2)}, u32[]{:S(2)}) collective-permute-start(bf16[32,4096]{1,0:T(8,128)(2,1)} %get-tuple-element.90), channel_id=1, source_target_pairs={{0,4},{1,5},{2,6},{3,7},{4,0},{5,1},{6,2},{7,3},{8,12},{9,13},{10,... | collective-permute-start | bytes 786440 | tf_op jit(solution)/shard_map/ppermute | solution.py:205
  41.5 0.0 collective-permute-done.3.refs_4_
  41.6 0.0 collective-permute-start.9
  41.6 0.0 collective-permute-done.4.refs_5_
  41.6 1.7 collective-permute-start.12
  43.2 0.0 collective-permute-done.5.refs_6_
  43.2 15.6 %collective-permute-start.15 = (bf16[32,4096]{1,0:T(8,128)(2,1)}, bf16[32,4096]{1,0:T(8,128)(2,1)}, u32[]{:S(2)}, u32[]{:S(2)}) collective-permute-start(bf16[32,4096]{1,0:T(8,128)(2,1)} %get-tuple-element.111), channel_id=1, source_target_pairs={{0,6},{1,3},{2,4},{3,1},{4,2},{5,7},{6,0},{7,5},{8,14},{9,11},{10,... | collective-permute-start | bytes 786440 | tf_op jit(solution)/shard_map/ppermute | solution.py:205
  58.8 8.9 %collective-permute-start.7 = (bf16[32,4096]{1,0:T(8,128)(2,1)}, bf16[32,4096]{1,0:T(8,128)(2,1)}, u32[]{:S(2)}, u32[]{:S(2)}) collective-permute-start(bf16[32,4096]{1,0:T(8,128)(2,1)} %get-tuple-element.94), channel_id=1, source_target_pairs={{0,2},{1,7},{2,0},{3,5},{4,6},{5,3},{6,4},{7,1},{8,10},{9,15},{10,... | collective-permute-start | bytes 786440 | tf_op jit(solution)/shard_map/ppermute | solution.py:205
  67.7 8.5 %collective-permute-done.9.refs_1_ = bf16[32,4096]{1,0:T(8,128)(2,1)} collective-permute-done((bf16[32,4096]{1,0:T(8,128)(2,1)}, bf16[32,4096]{1,0:T(8,128)(2,1)}, u32[]{:S(2)}, u32[]{:S(2)}) %collective-permute-start.9) | collective-permute-done | bytes 262176 | tf_op jit(solution)/shard_map/ppermute | solution.py:205
  76.3 0.0 collective-permute-start.10
  76.3 0.0 collective-permute-done.12.refs_2_
  76.3 0.0 collective-permute-start.13
  76.3 11.1 %expert.2 = (bf16[32,4096]{1,0:T(8,128)(2,1)}, bf16[32,4096]{1,0:T(8,128)(2,1)}, bf16[32,4096]{1,0:T(8,128)(2,1)}, bf16[32,4096]{1,0:T(8,128)(2,1)}, bf16[32,409...) custom-call(bf16[32,4096]{1,0:T(8,128)(2,1)} %get-tuple-element.80.r, ...), custom_call_target="tpu_custom_call" | custom-call | flops 1024 | bytes 1024 | tf_op jit(solution)/shard_map/expert/pallas_call | solution.py:28
  87.4 0.0 collective-permute-done.15.refs_3_
  87.4 5.3 %collective-permute-start.16 = (bf16[32,4096]{1,0:T(8,128)(2,1)}, bf16[32,4096]{1,0:T(8,128)(2,1)}, u32[]{:S(2)}, u32[]{:S(2)}) collective-permute-start(bf16[32,4096]{1,0:T(8,128)(2,1)} %get-tuple-element.112), channel_id=1, source_target_pairs={{0,4},{1,5},{2,6},{3,7},{4,0},{5,1},{6,2},{7,3},{8,12},{9,13},{10,... | collective-permute-start | bytes 786440 | tf_op jit(solution)/shard_map/ppermute | solution.py:205
  92.7 0.0 collective-permute-start.11
  92.7 7.4 %collective-permute-start.8 = (bf16[32,4096]{1,0:T(8,128)(2,1)}, bf16[32,4096]{1,0:T(8,128)(2,1)}, u32[]{:S(2)}, u32[]{:S(2)}) collective-permute-start(bf16[32,4096]{1,0:T(8,128)(2,1)} %get-tuple-element.95), channel_id=1, source_target_pairs={{0,5},{1,4},{2,3},{3,2},{4,1},{5,0},{6,7},{7,6},{8,13},{9,12},{10,... | collective-permute-start | bytes 786440 | tf_op jit(solution)/shard_map/ppermute | solution.py:205
  100.1 1.0 collective-permute-start.14
  101.2 13.0 %collective-permute-done.16.refs_7_ = bf16[32,4096]{1,0:T(8,128)(2,1)} collective-permute-done((bf16[32,4096]{1,0:T(8,128)(2,1)}, bf16[32,4096]{1,0:T(8,128)(2,1)}, u32[]{:S(2)}, u32[]{:S(2)}) %collective-permute-start.16) | collective-permute-done | bytes 262176 | tf_op jit(solution)/shard_map/ppermute | solution.py:205
  114.2 11.3 %expert.3 = (bf16[32,4096]{1,0:T(8,128)(2,1)}, bf16[32,4096]{1,0:T(8,128)(2,1)}, bf16[32,4096]{1,0:T(8,128)(2,1)}, bf16[32,4096]{1,0:T(8,128)(2,1)}, bf16[32,409...) custom-call(bf16[32,4096]{1,0:T(8,128)(2,1)} %get-tuple-element.122., ...), custom_call_target="tpu_custom_call" | custom-call | flops 1024 | bytes 1024 | tf_op jit(solution)/shard_map/expert/pallas_call | solution.py:28
  125.5 4.8 %weight_part.4 = (bf16[16,2176]{1,0:T(8,128)(2,1)}, bf16[496,2176]{1,0:T(8,128)(2,1)}) custom-call(s32[1]{0:T(128)} %bitcast.5.refs_0_, bf16[256,4096]{1,0:T(8,128)(2,1)} %get-tuple-element.136.refs_1_, bf16[256,1408]{1,0:T(8,128)(2,1)} %get-tuple-element.125.refs_2_, bf16[256,704]{1,0:T(8,128)(2,1)} %get-tuple-element.126.refs_3_, ...), custom_call_target="tpu_custom_call" | custom-call | flops 1024 | bytes 1024 | tf_op jit(solution)/shard_map/weight_part/pallas_call | solution.py:28
  130.3 0.1 collective-permute-start.21
  130.4 0.0 collective-permute-done.11.refs_7_
  130.4 1.6 collective-permute-done.21.refs_7_
  132.0 0.0 collective-permute-done.14.refs_8_
  132.0 0.2 collective-permute-start.22
  132.2 0.0 collective-permute-start.17
  132.2 0.0 collective-permute-start.18
  132.2 4.7 %weight_part.5 = bf16[512,2176]{1,0:T(8,128)(2,1)} custom-call(s32[1]{0:T(128)} %bitcast.6.refs_0_, bf16[256,4096]{1,0:T(8,128)(2,1)} %get-tuple-element.136.refs_1_, bf16[256,1408]{1,0:T(8,128)(2,1)} %get-tuple-element.125.refs_2_, bf16[256,704]{1,0:T(8,128)(2,1)} %get-tuple-element.126.refs_3_, bf16[256,4096]{1,0:T(8,128)(2,1)} %get-tuple-element.127.refs_4_, ...), custom_call_target="tpu_custom_call" | custom-call | flops 1024 | bytes 1024 | tf_op jit(solution)/shard_map/weight_part/pallas_call | solution.py:28
  136.9 4.7 %collective-permute-done.17.refs_9_ = bf16[32,4096]{1,0:T(8,128)(2,1)} collective-permute-done((bf16[32,4096]{1,0:T(8,128)(2,1)}, bf16[32,4096]{1,0:T(8,128)(2,1)}, u32[]{:S(2)}, u32[]{:S(2)}) %collective-permute-start.17) | collective-permute-done | bytes 262176 | tf_op jit(solution)/shard_map/ppermute | solution.py:205
  141.6 2.9 %collective-permute-done.18.refs_10_ = bf16[32,4096]{1,0:T(8,128)(2,1)} collective-permute-done((bf16[32,4096]{1,0:T(8,128)(2,1)}, bf16[32,4096]{1,0:T(8,128)(2,1)}, u32[]{:S(2)}, u32[]{:S(2)}) %collective-permute-start.18) | collective-permute-done | bytes 262176 | tf_op jit(solution)/shard_map/ppermute | solution.py:205
  144.5 0.0 collective-permute-done.22.refs_8_
  144.5 5.6 %weight_part.6 = bf16[512,2176]{1,0:T(8,128)(2,1)} custom-call(s32[1]{0:T(128)} %bitcast.7.refs_0_, bf16[256,4096]{1,0:T(8,128)(2,1)} %get-tuple-element.136.refs_1_, bf16[256,1408]{1,0:T(8,128)(2,1)} %get-tuple-element.125.refs_2_, bf16[256,704]{1,0:T(8,128)(2,1)} %get-tuple-element.126.refs_3_, bf16[256,4096]{1,0:T(8,128)(2,1)} %get-tuple-element.127.refs_4_, ...), custom_call_target="tpu_custom_call" | custom-call | flops 1024 | bytes 1024 | tf_op jit(solution)/shard_map/weight_part/pallas_call | solution.py:28
  150.1 1.0 collective-permute-start.24
  151.1 0.0 collective-permute-start.23
  151.1 2.0 collective-permute-start.19
  153.1 3.7 %collective-permute-start.20 = (bf16[32,4096]{1,0:T(8,128)(2,1)}, bf16[32,4096]{1,0:T(8,128)(2,1)}, u32[]{:S(2)}, u32[]{:S(2)}) collective-permute-start(bf16[32,4096]{1,0:T(8,128)(2,1)} %get-tuple-element.119), channel_id=1, source_target_pairs={{0,4},{1,5},{2,6},{3,7},{4,0},{5,1},{6,2},{7,3},{8,12},{9,13},{10,... | collective-permute-start | bytes 786440 | tf_op jit(solution)/shard_map/ppermute | solution.py:205
  156.8 0.0 collective-permute-start.26
  156.8 4.3 %collective-permute-done.19.refs_11_ = bf16[32,4096]{1,0:T(8,128)(2,1)} collective-permute-done((bf16[32,4096]{1,0:T(8,128)(2,1)}, bf16[32,4096]{1,0:T(8,128)(2,1)}, u32[]{:S(2)}, u32[]{:S(2)}) %collective-permute-start.19) | collective-permute-done | bytes 262176 | tf_op jit(solution)/shard_map/ppermute | solution.py:205
  161.1 11.5 %collective-permute-start.25 = (bf16[32,4096]{1,0:T(8,128)(2,1)}, bf16[32,4096]{1,0:T(8,128)(2,1)}, u32[]{:S(2)}, u32[]{:S(2)}) collective-permute-start(bf16[32,4096]{1,0:T(8,128)(2,1)} %get-tuple-element.140), channel_id=1, source_target_pairs={{0,5},{1,4},{2,3},{3,2},{4,1},{5,0},{6,7},{7,6},{8,13},{9,12},{10,... | collective-permute-start | bytes 786440 | tf_op jit(solution)/shard_map/ppermute | solution.py:205
  172.6 8.4 %collective-permute-done.20.refs_12_ = bf16[32,4096]{1,0:T(8,128)(2,1)} collective-permute-done((bf16[32,4096]{1,0:T(8,128)(2,1)}, bf16[32,4096]{1,0:T(8,128)(2,1)}, u32[]{:S(2)}, u32[]{:S(2)}) %collective-permute-start.20) | collective-permute-done | bytes 262176 | tf_op jit(solution)/shard_map/ppermute | solution.py:205
  181.1 0.0 collective-permute-start.27
  181.1 4.8 %combine.2 = (bf16[256,2048]{1,0:T(8,128)(2,1)}, bf16[256,2048]{1,0:T(8,128)(2,1)}) custom-call(s32[1]{0:T(128)} %bitcast.refs_0_, s32[8,8]{1,0:T(8,128)} %constant.16.clone.refs_1_, s32[1,256]{1,0:T(1,128)} %bitcast.16, bf16[256,2048]{1,0:T(8,128)(2,1)} %refs_3_.5, bf16[256,2048]{1,0:T(8,128)(2,1)} %refs_4_.5, bf16[32,4096]{1,0:T(8,128)(2,1)} %get-tuple-element.91.refs_5_, ...), custom_call_target="tpu_custom_call" | custom-call | flops 1024 | bytes 1024 | tf_op jit(solution)/shard_map/combine/pallas_call | solution.py:28
  185.9 3.4 %collective-permute-start.28 = (bf16[32,4096]{1,0:T(8,128)(2,1)}, bf16[32,4096]{1,0:T(8,128)(2,1)}, u32[]{:S(2)}, u32[]{:S(2)}) collective-permute-start(bf16[32,4096]{1,0:T(8,128)(2,1)} %get-tuple-element.146), channel_id=1, source_target_pairs={{0,2},{1,7},{2,0},{3,5},{4,6},{5,3},{6,4},{7,1},{8,10},{9,15},{10,... | collective-permute-start | bytes 786440 | tf_op jit(solution)/shard_map/ppermute | solution.py:205
  189.3 2.2 collective-permute-done.27.refs_8_
  191.5 2.8 %collective-permute-start.29 = (bf16[32,4096]{1,0:T(8,128)(2,1)}, bf16[32,4096]{1,0:T(8,128)(2,1)}, u32[]{:S(2)}, u32[]{:S(2)}) collective-permute-start(bf16[32,4096]{1,0:T(8,128)(2,1)} %get-tuple-element.148), channel_id=1, source_target_pairs={{0,7},{1,2},{2,1},{3,4},{4,3},{5,6},{6,5},{7,0},{8,15},{9,10},{10,... | collective-permute-start | bytes 786440 | tf_op jit(solution)/shard_map/ppermute | solution.py:205
  194.2 6.3 %collective-permute-done.24.refs_8_ = bf16[512,2176]{1,0:T(8,128)(2,1)} collective-permute-done((bf16[512,2176]{1,0:T(8,128)(2,1)}, bf16[512,2176]{1,0:T(8,128)(2,1)}, u32[]{:S(2)}, u32[]{:S(2)}) %collective-permute-start.24) | collective-permute-done | bytes 2228256 | tf_op jit(solution)/shard_map/ppermute | solution.py:205
  200.6 1.0 collective-permute-start.31
  201.5 6.7 %weight_part.7 = (f32[512,1408]{1,0:T(8,128)}, f32[704,512]{1,0:T(8,128)}) custom-call(s32[1]{0:T(128)} %bitcast.4.refs_0_, bf16[256,4096]{1,0:T(8,128)(2,1)} %get-tuple-element.136.refs_1_, bf16[256,1408]{1,0:T(8,128)(2,1)} %get-tuple-element.125.refs_2_, bf16[256,704]{1,0:T(8,128)(2,1)} %get-tuple-element.126.refs_3_, ...), custom_call_target="tpu_custom_call" | custom-call | flops 1024 | bytes 1024 | tf_op jit(solution)/shard_map/weight_part/pallas_call | solution.py:28
  208.2 0.0 collective-permute-done.28.refs_9_
  208.2 3.9 %collective-permute-done.29.refs_10_ = bf16[32,4096]{1,0:T(8,128)(2,1)} collective-permute-done((bf16[32,4096]{1,0:T(8,128)(2,1)}, bf16[32,4096]{1,0:T(8,128)(2,1)}, u32[]{:S(2)}, u32[]{:S(2)}) %collective-permute-start.29) | collective-permute-done | bytes 262176 | tf_op jit(solution)/shard_map/ppermute | solution.py:205
  212.1 7.9 %collective-permute-done.31.refs_12_ = bf16[32,4096]{1,0:T(8,128)(2,1)} collective-permute-done((bf16[32,4096]{1,0:T(8,128)(2,1)}, bf16[32,4096]{1,0:T(8,128)(2,1)}, u32[]{:S(2)}, u32[]{:S(2)}) %collective-permute-start.31) | collective-permute-done | bytes 262176 | tf_op jit(solution)/shard_map/ppermute | solution.py:205
  220.0 4.7 %combine.3 = (bf16[256,2048]{1,0:T(8,128)(2,1)}, bf16[256,2048]{1,0:T(8,128)(2,1)}) custom-call(s32[1]{0:T(128)} %bitcast.refs_0_, s32[8,8]{1,0:T(8,128)} %constant.16.clone.refs_1_, s32[1,256]{1,0:T(1,128)} %bitcast.17, bf16[256,2048]{1,0:T(8,128)(2,1)} %get-tuple-element.120.refs_3_, bf16[256,2048]{1,0:T(8,128)(2,1)} %get-tuple-element.121.refs_4_, ...), custom_call_target="tpu_custom_call" | custom-call | flops 1024 | bytes 1024 | tf_op jit(solution)/shard_map/combine/pallas_call | solution.py:28
  (10 shorter events, 0.0 us)
Async XLA Ops:
  4.6 18.2 %collective-permute-start = (bf16[32,4096]{1,0:T(8,128)(2,1)}, bf16[32,4096]{1,0:T(8,128)(2,1)}, u32[]{:S(2)}, u32[]{:S(2)}) collective-permute-start(bf16[32,4096]{1,0:T(8,128)(2,1)} %get-tuple-element.81), channel_id=1, source_target_pairs={{0,5},{1,4},{2,3},{3,2},{4,1},{5,0},{6,7},{7,6},{8,13},{9,12},{10,... | collective-permute-start | bytes 786440 | tf_op jit(solution)/shard_map/ppermute | solution.py:205
  9.7 13.1 %collective-permute-start.1 = (bf16[32,4096]{1,0:T(8,128)(2,1)}, bf16[32,4096]{1,0:T(8,128)(2,1)}, u32[]{:S(2)}, u32[]{:S(2)}) collective-permute-start(bf16[32,4096]{1,0:T(8,128)(2,1)} %get-tuple-element.82), channel_id=1, source_target_pairs={{0,1},{1,0},{2,7},{3,6},{4,5},{5,4},{6,3},{7,2},{8,9},{9,8},{10,15... | collective-permute-start | bytes 786440 | tf_op jit(solution)/shard_map/ppermute | solution.py:205
  10.2 23.6 %collective-permute-start.2 = (bf16[32,4096]{1,0:T(8,128)(2,1)}, bf16[32,4096]{1,0:T(8,128)(2,1)}, u32[]{:S(2)}, u32[]{:S(2)}) collective-permute-start(bf16[32,4096]{1,0:T(8,128)(2,1)} %get-tuple-element.83), channel_id=1, source_target_pairs={{0,6},{1,3},{2,4},{3,1},{4,2},{5,7},{6,0},{7,5},{8,14},{9,11},{10,... | collective-permute-start | bytes 786440 | tf_op jit(solution)/shard_map/ppermute | solution.py:205
  11.5 30.0 %collective-permute-start.3 = (bf16[32,4096]{1,0:T(8,128)(2,1)}, bf16[32,4096]{1,0:T(8,128)(2,1)}, u32[]{:S(2)}, u32[]{:S(2)}) collective-permute-start(bf16[32,4096]{1,0:T(8,128)(2,1)} %get-tuple-element.84), channel_id=1, source_target_pairs={{0,2},{1,7},{2,0},{3,5},{4,6},{5,3},{6,4},{7,1},{8,10},{9,15},{10,... | collective-permute-start | bytes 786440 | tf_op jit(solution)/shard_map/ppermute | solution.py:205
  22.8 18.7 %collective-permute-start.4 = (bf16[32,4096]{1,0:T(8,128)(2,1)}, bf16[32,4096]{1,0:T(8,128)(2,1)}, u32[]{:S(2)}, u32[]{:S(2)}) collective-permute-start(bf16[32,4096]{1,0:T(8,128)(2,1)} %get-tuple-element.86), channel_id=1, source_target_pairs={{0,7},{1,2},{2,1},{3,4},{4,3},{5,6},{6,5},{7,0},{8,15},{9,10},{10,... | collective-permute-start | bytes 786440 | tf_op jit(solution)/shard_map/ppermute | solution.py:205
  22.8 20.4 %collective-permute-start.5 = (bf16[32,4096]{1,0:T(8,128)(2,1)}, bf16[32,4096]{1,0:T(8,128)(2,1)}, u32[]{:S(2)}, u32[]{:S(2)}) collective-permute-start(bf16[32,4096]{1,0:T(8,128)(2,1)} %get-tuple-element.88), channel_id=1, source_target_pairs={{0,3},{1,6},{2,5},{3,0},{4,7},{5,2},{6,1},{7,4},{8,11},{9,14},{10,... | collective-permute-start | bytes 786440 | tf_op jit(solution)/shard_map/ppermute | solution.py:205
  33.8 25.0 %collective-permute-start.6 = (bf16[32,4096]{1,0:T(8,128)(2,1)}, bf16[32,4096]{1,0:T(8,128)(2,1)}, u32[]{:S(2)}, u32[]{:S(2)}) collective-permute-start(bf16[32,4096]{1,0:T(8,128)(2,1)} %get-tuple-element.90), channel_id=1, source_target_pairs={{0,4},{1,5},{2,6},{3,7},{4,0},{5,1},{6,2},{7,3},{8,12},{9,13},{10,... | collective-permute-start | bytes 786440 | tf_op jit(solution)/shard_map/ppermute | solution.py:205
  41.6 34.7 %collective-permute-start.9 = (bf16[32,4096]{1,0:T(8,128)(2,1)}, bf16[32,4096]{1,0:T(8,128)(2,1)}, u32[]{:S(2)}, u32[]{:S(2)}) collective-permute-start(bf16[32,4096]{1,0:T(8,128)(2,1)} %get-tuple-element.99), channel_id=1, source_target_pairs={{0,5},{1,4},{2,3},{3,2},{4,1},{5,0},{6,7},{7,6},{8,13},{9,12},{10,... | collective-permute-start | bytes 786440 | tf_op jit(solution)/shard_map/ppermute | solution.py:205
  41.6 34.7 %collective-permute-start.12 = (bf16[32,4096]{1,0:T(8,128)(2,1)}, bf16[32,4096]{1,0:T(8,128)(2,1)}, u32[]{:S(2)}, u32[]{:S(2)}) collective-permute-start(bf16[32,4096]{1,0:T(8,128)(2,1)} %get-tuple-element.105), channel_id=1, source_target_pairs={{0,1},{1,0},{2,7},{3,6},{4,5},{5,4},{6,3},{7,2},{8,9},{9,8},{10,15... | collective-permute-start | bytes 786440 | tf_op jit(solution)/shard_map/ppermute | solution.py:205
  43.2 44.2 %collective-permute-start.15 = (bf16[32,4096]{1,0:T(8,128)(2,1)}, bf16[32,4096]{1,0:T(8,128)(2,1)}, u32[]{:S(2)}, u32[]{:S(2)}) collective-permute-start(bf16[32,4096]{1,0:T(8,128)(2,1)} %get-tuple-element.111), channel_id=1, source_target_pairs={{0,6},{1,3},{2,4},{3,1},{4,2},{5,7},{6,0},{7,5},{8,14},{9,11},{10,... | collective-permute-start | bytes 786440 | tf_op jit(solution)/shard_map/ppermute | solution.py:205
  58.8 33.9 %collective-permute-start.7 = (bf16[32,4096]{1,0:T(8,128)(2,1)}, bf16[32,4096]{1,0:T(8,128)(2,1)}, u32[]{:S(2)}, u32[]{:S(2)}) collective-permute-start(bf16[32,4096]{1,0:T(8,128)(2,1)} %get-tuple-element.94), channel_id=1, source_target_pairs={{0,2},{1,7},{2,0},{3,5},{4,6},{5,3},{6,4},{7,1},{8,10},{9,15},{10,... | collective-permute-start | bytes 786440 | tf_op jit(solution)/shard_map/ppermute | solution.py:205
  76.3 16.5 %collective-permute-start.10 = (bf16[32,4096]{1,0:T(8,128)(2,1)}, bf16[32,4096]{1,0:T(8,128)(2,1)}, u32[]{:S(2)}, u32[]{:S(2)}) collective-permute-start(bf16[32,4096]{1,0:T(8,128)(2,1)} %get-tuple-element.100), channel_id=1, source_target_pairs={{0,7},{1,2},{2,1},{3,4},{4,3},{5,6},{6,5},{7,0},{8,15},{9,10},{10,... | collective-permute-start | bytes 786440 | tf_op jit(solution)/shard_map/ppermute | solution.py:205
  76.3 23.9 %collective-permute-start.13 = (bf16[32,4096]{1,0:T(8,128)(2,1)}, bf16[32,4096]{1,0:T(8,128)(2,1)}, u32[]{:S(2)}, u32[]{:S(2)}) collective-permute-start(bf16[32,4096]{1,0:T(8,128)(2,1)} %get-tuple-element.106), channel_id=1, source_target_pairs={{0,3},{1,6},{2,5},{3,0},{4,7},{5,2},{6,1},{7,4},{8,11},{9,14},{10,... | collective-permute-start | bytes 786440 | tf_op jit(solution)/shard_map/ppermute | solution.py:205
  87.4 26.8 %collective-permute-start.16 = (bf16[32,4096]{1,0:T(8,128)(2,1)}, bf16[32,4096]{1,0:T(8,128)(2,1)}, u32[]{:S(2)}, u32[]{:S(2)}) collective-permute-start(bf16[32,4096]{1,0:T(8,128)(2,1)} %get-tuple-element.112), channel_id=1, source_target_pairs={{0,4},{1,5},{2,6},{3,7},{4,0},{5,1},{6,2},{7,3},{8,12},{9,13},{10,... | collective-permute-start | bytes 786440 | tf_op jit(solution)/shard_map/ppermute | solution.py:205
  92.7 37.7 %collective-permute-start.11 = (bf16[32,4096]{1,0:T(8,128)(2,1)}, bf16[32,4096]{1,0:T(8,128)(2,1)}, u32[]{:S(2)}, u32[]{:S(2)}) collective-permute-start(bf16[32,4096]{1,0:T(8,128)(2,1)} %get-tuple-element.101), channel_id=1, source_target_pairs={{0,1},{1,0},{2,7},{3,6},{4,5},{5,4},{6,3},{7,2},{8,9},{9,8},{10,15... | collective-permute-start | bytes 786440 | tf_op jit(solution)/shard_map/ppermute | solution.py:205
  92.7 37.7 %collective-permute-start.8 = (bf16[32,4096]{1,0:T(8,128)(2,1)}, bf16[32,4096]{1,0:T(8,128)(2,1)}, u32[]{:S(2)}, u32[]{:S(2)}) collective-permute-start(bf16[32,4096]{1,0:T(8,128)(2,1)} %get-tuple-element.95), channel_id=1, source_target_pairs={{0,5},{1,4},{2,3},{3,2},{4,1},{5,0},{6,7},{7,6},{8,13},{9,12},{10,... | collective-permute-start | bytes 786440 | tf_op jit(solution)/shard_map/ppermute | solution.py:205
  100.1 31.9 %collective-permute-start.14 = (bf16[32,4096]{1,0:T(8,128)(2,1)}, bf16[32,4096]{1,0:T(8,128)(2,1)}, u32[]{:S(2)}, u32[]{:S(2)}) collective-permute-start(bf16[32,4096]{1,0:T(8,128)(2,1)} %get-tuple-element.107), channel_id=1, source_target_pairs={{0,6},{1,3},{2,4},{3,1},{4,2},{5,7},{6,0},{7,5},{8,14},{9,11},{10,... | collective-permute-start | bytes 786440 | tf_op jit(solution)/shard_map/ppermute | solution.py:205
  130.3 1.7 collective-permute-start.21
  132.0 12.5 %collective-permute-start.22 = (bf16[496,2176]{1,0:T(8,128)(2,1)}, bf16[496,2176]{1,0:T(8,128)(2,1)}, u32[]{:S(2)}, u32[]{:S(2)}) collective-permute-start(bf16[496,2176]{1,0:T(8,128)(2,1)} %get-tuple-element.135), channel_id=1, source_target_pairs={{0,8},{8,0},{16,24},{24,16},{1,9},{9,1},{17,25},{25,17},{2,10},{10... | collective-permute-start | bytes 6475784 | tf_op jit(solution)/shard_map/ppermute | solution.py:205
  132.2 9.4 %collective-permute-start.17 = (bf16[32,4096]{1,0:T(8,128)(2,1)}, bf16[32,4096]{1,0:T(8,128)(2,1)}, u32[]{:S(2)}, u32[]{:S(2)}) collective-permute-start(bf16[32,4096]{1,0:T(8,128)(2,1)} %get-tuple-element.113), channel_id=1, source_target_pairs={{0,2},{1,7},{2,0},{3,5},{4,6},{5,3},{6,4},{7,1},{8,10},{9,15},{10,... | collective-permute-start | bytes 786440 | tf_op jit(solution)/shard_map/ppermute | solution.py:205
  132.2 12.3 %collective-permute-start.18 = (bf16[32,4096]{1,0:T(8,128)(2,1)}, bf16[32,4096]{1,0:T(8,128)(2,1)}, u32[]{:S(2)}, u32[]{:S(2)}) collective-permute-start(bf16[32,4096]{1,0:T(8,128)(2,1)} %get-tuple-element.115), channel_id=1, source_target_pairs={{0,7},{1,2},{2,1},{3,4},{4,3},{5,6},{6,5},{7,0},{8,15},{9,10},{10,... | collective-permute-start | bytes 786440 | tf_op jit(solution)/shard_map/ppermute | solution.py:205
  150.1 50.5 %collective-permute-start.24 = (bf16[512,2176]{1,0:T(8,128)(2,1)}, bf16[512,2176]{1,0:T(8,128)(2,1)}, u32[]{:S(2)}, u32[]{:S(2)}) collective-permute-start(bf16[512,2176]{1,0:T(8,128)(2,1)} %weight_part.6), channel_id=1, source_target_pairs={{0,16},{8,24},{16,0},{24,8},{1,17},{9,25},{17,1},{25,9},{2,18},{10... | collective-permute-start | bytes 6684680 | tf_op jit(solution)/shard_map/ppermute | solution.py:205
  151.1 50.5 %collective-permute-start.23 = (bf16[512,2176]{1,0:T(8,128)(2,1)}, bf16[512,2176]{1,0:T(8,128)(2,1)}, u32[]{:S(2)}, u32[]{:S(2)}) collective-permute-start(bf16[512,2176]{1,0:T(8,128)(2,1)} %weight_part.5), channel_id=1, source_target_pairs={{0,8},{8,0},{16,24},{24,16},{1,9},{9,1},{17,25},{25,17},{2,10},{10... | collective-permute-start | bytes 6684680 | tf_op jit(solution)/shard_map/ppermute | solution.py:205
  151.1 10.0 %collective-permute-start.19 = (bf16[32,4096]{1,0:T(8,128)(2,1)}, bf16[32,4096]{1,0:T(8,128)(2,1)}, u32[]{:S(2)}, u32[]{:S(2)}) collective-permute-start(bf16[32,4096]{1,0:T(8,128)(2,1)} %get-tuple-element.117), channel_id=1, source_target_pairs={{0,3},{1,6},{2,5},{3,0},{4,7},{5,2},{6,1},{7,4},{8,11},{9,14},{10,... | collective-permute-start | bytes 786440 | tf_op jit(solution)/shard_map/ppermute | solution.py:205
  153.1 27.9 %collective-permute-start.20 = (bf16[32,4096]{1,0:T(8,128)(2,1)}, bf16[32,4096]{1,0:T(8,128)(2,1)}, u32[]{:S(2)}, u32[]{:S(2)}) collective-permute-start(bf16[32,4096]{1,0:T(8,128)(2,1)} %get-tuple-element.119), channel_id=1, source_target_pairs={{0,4},{1,5},{2,6},{3,7},{4,0},{5,1},{6,2},{7,3},{8,12},{9,13},{10,... | collective-permute-start | bytes 786440 | tf_op jit(solution)/shard_map/ppermute | solution.py:205
  156.8 29.1 %collective-permute-start.26 = (bf16[32,4096]{1,0:T(8,128)(2,1)}, bf16[32,4096]{1,0:T(8,128)(2,1)}, u32[]{:S(2)}, u32[]{:S(2)}) collective-permute-start(bf16[32,4096]{1,0:T(8,128)(2,1)} %get-tuple-element.142), channel_id=1, source_target_pairs={{0,1},{1,0},{2,7},{3,6},{4,5},{5,4},{6,3},{7,2},{8,9},{9,8},{10,15... | collective-permute-start | bytes 786440 | tf_op jit(solution)/shard_map/ppermute | solution.py:205
  161.1 28.2 %collective-permute-start.25 = (bf16[32,4096]{1,0:T(8,128)(2,1)}, bf16[32,4096]{1,0:T(8,128)(2,1)}, u32[]{:S(2)}, u32[]{:S(2)}) collective-permute-start(bf16[32,4096]{1,0:T(8,128)(2,1)} %get-tuple-element.140), channel_id=1, source_target_pairs={{0,5},{1,4},{2,3},{3,2},{4,1},{5,0},{6,7},{7,6},{8,13},{9,12},{10,... | collective-permute-start | bytes 786440 | tf_op jit(solution)/shard_map/ppermute | solution.py:205
  181.1 10.4 %collective-permute-start.27 = (bf16[32,4096]{1,0:T(8,128)(2,1)}, bf16[32,4096]{1,0:T(8,128)(2,1)}, u32[]{:S(2)}, u32[]{:S(2)}) collective-permute-start(bf16[32,4096]{1,0:T(8,128)(2,1)} %get-tuple-element.144), channel_id=1, source_target_pairs={{0,6},{1,3},{2,4},{3,1},{4,2},{5,7},{6,0},{7,5},{8,14},{9,11},{10,... | collective-permute-start | bytes 786440 | tf_op jit(solution)/shard_map/ppermute | solution.py:205
  185.9 22.3 %collective-permute-start.28 = (bf16[32,4096]{1,0:T(8,128)(2,1)}, bf16[32,4096]{1,0:T(8,128)(2,1)}, u32[]{:S(2)}, u32[]{:S(2)}) collective-permute-start(bf16[32,4096]{1,0:T(8,128)(2,1)} %get-tuple-element.146), channel_id=1, source_target_pairs={{0,2},{1,7},{2,0},{3,5},{4,6},{5,3},{6,4},{7,1},{8,10},{9,15},{10,... | collective-permute-start | bytes 786440 | tf_op jit(solution)/shard_map/ppermute | solution.py:205
  189.3 18.9 %collective-permute-start.30 = (bf16[32,4096]{1,0:T(8,128)(2,1)}, bf16[32,4096]{1,0:T(8,128)(2,1)}, u32[]{:S(2)}, u32[]{:S(2)}) collective-permute-start(bf16[32,4096]{1,0:T(8,128)(2,1)} %get-tuple-element.150), channel_id=1, source_target_pairs={{0,3},{1,6},{2,5},{3,0},{4,7},{5,2},{6,1},{7,4},{8,11},{9,14},{10,... | collective-permute-start | bytes 786440 | tf_op jit(solution)/shard_map/ppermute | solution.py:205
  191.5 20.6 %collective-permute-start.29 = (bf16[32,4096]{1,0:T(8,128)(2,1)}, bf16[32,4096]{1,0:T(8,128)(2,1)}, u32[]{:S(2)}, u32[]{:S(2)}) collective-permute-start(bf16[32,4096]{1,0:T(8,128)(2,1)} %get-tuple-element.148), channel_id=1, source_target_pairs={{0,7},{1,2},{2,1},{3,4},{4,3},{5,6},{6,5},{7,0},{8,15},{9,10},{10,... | collective-permute-start | bytes 786440 | tf_op jit(solution)/shard_map/ppermute | solution.py:205
  200.6 19.5 %collective-permute-start.31 = (bf16[32,4096]{1,0:T(8,128)(2,1)}, bf16[32,4096]{1,0:T(8,128)(2,1)}, u32[]{:S(2)}, u32[]{:S(2)}) collective-permute-start(bf16[32,4096]{1,0:T(8,128)(2,1)} %get-tuple-element.152), channel_id=1, source_target_pairs={{0,4},{1,5},{2,6},{3,7},{4,0},{5,1},{6,2},{7,3},{8,12},{9,13},{10,... | collective-permute-start | bytes 786440 | tf_op jit(solution)/shard_map/ppermute | solution.py:205

commit v8 on v7

--- a/solution.py
+++ b/solution.py
@@ -7,6 +7,7 @@
 from jax.sharding import PartitionSpec as P
 
 VMEM_BYTES = 64 * 1024 * 1024
+PIECES = 4
 SMALL = pl.CostEstimate(flops=1024, bytes_accessed=1024, transcendentals=0)
 BF16 = jnp.bfloat16
 F32 = jnp.float32
@@ -58,20 +59,27 @@
 
 def place_kernel(part, cap, me_ref, table_ref, ids_ref, tokens_ref, grad_ref, *refs):
     blocks, (data, moved, sems) = refs[:-3], refs[-3:]
-    width = tokens_ref.shape[1]
     copies = Copies(sems)
-    loads = [
-        copies.start(ref, data.at[:, side * width : (side + 1) * width]) for side, ref in enumerate((tokens_ref, grad_ref))
-    ]
+    pieces = pieces_of(tokens_ref, grad_ref)
+    loads = [copies.start(ref.at[:, there], data.at[:, here]) for ref, there, here in pieces]
     placing = placing_of(me_ref, table_ref, ids_ref, len(blocks), part, cap)
     stores = []
-    for side in range(2):
-        here = slice(side * width, (side + 1) * width)
-        loads[side].wait()
+    for load, (_, _, here) in zip(loads, pieces):
+        load.wait()
         moved[:, here] = dot(placing, data[:, here], PLAIN).astype(BF16)
         for index, block in enumerate(blocks):
             stores.append(copies.start(moved.at[index * cap : (index + 1) * cap, here], block.at[:, here]))
     wait(stores)
+
+
+def pieces_of(first_ref, second_ref):
+    width = first_ref.shape[1]
+    step = width // (PIECES // 2)
+    return [
+        (ref, slice(start, start + step), slice(side * width + start, side * width + start + step))
+        for side, ref in enumerate((first_ref, second_ref))
+        for start in range(0, width, step)
+    ]
 
 
 def placing_of(me_ref, table_ref, ids_ref, experts, part, cap):
@@ -97,10 +105,12 @@
     wide, width = two.shape
     copies = Copies(sems)
     loads = [copies.start(block, slot.at[index * cap : (index + 1) * cap]) for index, block in enumerate(blocks)]
+    two_load = copies.start(two_ref, two)
     one_load = copies.start(one_ref, one)
-    two_load = copies.start(two_ref, two)
     wait(loads)
     stores = [copies.start(slot, slot_out)]
+    two_load.wait()
+    grad_hidden = dot(slot[:, width:], two[...], COLS)
     one_load.wait()
     both = dot(slot[:, :width], one[...], PLAIN)
     gate, upper = both[:, :wide], both[:, wide:]
@@ -108,8 +118,6 @@
     silu = gate * sigma
     hidden[...] = (silu * upper).astype(BF16)
     stores.append(copies.start(hidden, hidden_out))
-    two_load.wait()
-    grad_hidden = dot(slot[:, width:], two[...], COLS)
     proj[...] = jnp.concatenate(
         [grad_hidden * upper * sigma * (1.0 + gate * (1.0 - sigma)), grad_hidden * silu], axis=1
     ).astype(BF16)
@@ -174,17 +182,19 @@
 
 def combine_kernel(part, cap, me_ref, table_ref, ids_ref, tokens_ref, grad_ref, *refs):
     blocks, (mixed_out, grad_out, data, back, sems) = refs[:-5], refs[-5:]
-    width = tokens_ref.shape[1]
     copies = Copies(sems)
-    loads = [copies.start(ref, data.at[:, side * width : (side + 1) * width]) for side, ref in enumerate((tokens_ref, grad_ref))]
-    loads += [copies.start(block, back.at[index * cap : (index + 1) * cap]) for index, block in enumerate(blocks)]
+    pieces = pieces_of(tokens_ref, grad_ref)
+    loads = []
+    for ref, there, here in pieces:
+        loads.append([copies.start(ref.at[:, there], data.at[:, here])])
+        for index, block in enumerate(blocks):
+            loads[-1].append(copies.start(block.at[:, here], back.at[index * cap : (index + 1) * cap, here]))
     placing = placing_of(me_ref, table_ref, ids_ref, len(blocks), part, cap)
-    wait(loads)
     stores = []
-    for side, out in enumerate((mixed_out, grad_out)):
-        here = slice(side * width, (side + 1) * width)
+    for load, (_, there, here), (out, _, _) in zip(loads, pieces, pieces_of(mixed_out, grad_out)):
+        wait(load)
         data[:, here] = (data[:, here].astype(F32) + dot(placing, back[:, here], ROWS)).astype(BF16)
-        stores.append(copies.start(data.at[:, here], out))
+        stores.append(copies.start(data.at[:, here], out.at[:, there]))
     wait(stores)
 
 
@@ -260,7 +270,7 @@
             lambda *refs: place_kernel(part, cap, *refs),
             "place",
             [pair] * experts,
-            [pltpu.VMEM((rows, 2 * width), BF16), pltpu.VMEM((slots, 2 * width), BF16), sems((2 + 2 * experts,))],
+            [pltpu.VMEM((rows, 2 * width), BF16), pltpu.VMEM((slots, 2 * width), BF16), sems((PIECES * (1 + experts),))],
             [tokens, grad_out],
             [ids],
             [me, table],
@@ -305,7 +315,7 @@
             lambda *refs: combine_kernel(part, cap, *refs),
             "combine",
             [like((rows, width))] * 2,
-            [pltpu.VMEM((rows, 2 * width), BF16), pltpu.VMEM((slots, 2 * width), BF16), sems((4 + experts,))],
+            [pltpu.VMEM((rows, 2 * width), BF16), pltpu.VMEM((slots, 2 * width), BF16), sems((PIECES * (2 + experts),))],
             [first, second, *blocks],
             [ids],
             [me, table],
@@ -324,17 +334,15 @@
 
     received = {q: [] for q in range(groups)}
     sums = kept[0][0]
+    held = {groups - 1: done[:3], 2: done[3:6]}
     for q in sorted(range(1, groups), key=lambda q: (q & -q, -q)):
         low = q & -q
-        first_of_all = q == groups - 1
-        if low == 2 and received[q ^ low]:
-            sums = after(sums, *done[3:5])
-        sent = weight_part(group ^ q, [[sums, *kept[0][1:]], *kept[1:]], received[q], False, 16 if first_of_all else 0)
+        sent = weight_part(group ^ q, [[sums, *kept[0][1:]], *kept[1:]], received[q], False, 16 if q in held else 0)
         sums = after(sums, sent[0])
         pairs = [(i, i ^ low) for i in range(groups)]
         short = Lane(1)
-        held = [(), done[:3]]
-        received[q ^ low].append([short.send(piece, "grp", pairs, *more) for piece, more in zip(sent, held)])
+        received[q ^ low].append([short.send(sent[0], "grp", pairs)])
+        received[q ^ low][-1] += [short.send(piece, "grp", pairs, *held[q]) for piece in sent[1:]]
 
     mixed, grad = tokens, grad_out
     for part in range(1, parts):

time: 225 us -> 220 us (0.978)
  starting transfers between devices: 87.4 us -> 83.5 us
    ppermute x32 -> x33, starting transfers between devices: 87.4 us -> 83.5 us  [send(): self.done.append(lax.ppermute(after(value, *earlier), axis, pairs))]
    ppermute x32 -> x33, waiting for transfers between devices: 74.8 us -> 73 us  [send(): self.done.append(lax.ppermute(after(value, *earlier), axis, pairs))]
  transfers between devices with their start and end apart: 32 -> 33, of which waited for: 12 -> 10; matrix products, arithmetic and copies ran while one was open for 0% -> 0% of each run, Pallas kernels for 21% -> 24%
where the time goes in v8:
time: 220 us; the launch traced here: 219 us
  starting transfers between devices  83.5 us (38%)
  waiting for transfers between devices  73 us (33%)
  Pallas kernels  61 us (28%)
    ppermute x33, starting transfers between devices, send(): self.done.append(lax.ppermute(after(value, *earlier), axis, pairs))  83.5 us
    ppermute x33, waiting for transfers between devices, send(): self.done.append(lax.ppermute(after(value, *earlier), axis, pairs))  73 us
    pallas_call x10, Pallas kernels, call(): pl.pallas_call(kernel, in_specs=[pl.BlockSpec(memory_space=pltpu.SMEM)] *...  61 us
  transfers between devices with their start and end apart: 33, of which 10 were waited for; matrix products, arithmetic and copies ran while one was open for 0% of the time, Pallas kernels for 24%

profile of v8, /device:TPU:0, one launch (start us, length us, event | category | flops | bytes accessed | tf_op | source)
XLA Modules:
  0.0 218.5 jit_solution(8651404376462404884)
XLA Ops:
  0.6 4.1 %place.2 = (bf16[32,4096]{1,0:T(8,128)(2,1)}, bf16[32,4096]{1,0:T(8,128)(2,1)}, bf16[32,4096]{1,0:T(8,128)(2,1)}, bf16[32,4096]{1,0:T(8,128)(2,1)}, bf16[32,4096...) custom-call(s32[1]{0:T(128)} %bitcast.refs_0_, ...), custom_call_target="tpu_custom_call" | custom-call | flops 1024 | bytes 1024 | tf_op jit(solution)/shard_map/place/pallas_call | solution.py:29
  4.8 5.1 %collective-permute-start = (bf16[32,4096]{1,0:T(8,128)(2,1)}, bf16[32,4096]{1,0:T(8,128)(2,1)}, u32[]{:S(2)}, u32[]{:S(2)}) collective-permute-start(bf16[32,4096]{1,0:T(8,128)(2,1)} %get-tuple-element.83), channel_id=1, source_target_pairs={{0,5},{1,4},{2,3},{3,2},{4,1},{5,0},{6,7},{7,6},{8,13},{9,12},{10,... | collective-permute-start | bytes 786440 | tf_op jit(solution)/shard_map/ppermute | solution.py:215
  9.8 0.5 collective-permute-start.1
  10.3 1.3 collective-permute-start.2
  11.7 0.2 collective-permute-start.3
  11.9 11.0 %collective-permute-done.refs_1_ = bf16[32,4096]{1,0:T(8,128)(2,1)} collective-permute-done((bf16[32,4096]{1,0:T(8,128)(2,1)}, bf16[32,4096]{1,0:T(8,128)(2,1)}, u32[]{:S(2)}, u32[]{:S(2)}) %collective-permute-start) | collective-permute-done | bytes 262176 | tf_op jit(solution)/shard_map/ppermute | solution.py:215
  23.0 0.0 collective-permute-start.4
  23.0 0.0 collective-permute-done.1.refs_2_
  23.0 7.0 %collective-permute-start.5 = (bf16[32,4096]{1,0:T(8,128)(2,1)}, bf16[32,4096]{1,0:T(8,128)(2,1)}, u32[]{:S(2)}, u32[]{:S(2)}) collective-permute-start(bf16[32,4096]{1,0:T(8,128)(2,1)} %get-tuple-element.90), channel_id=1, source_target_pairs={{0,3},{1,6},{2,5},{3,0},{4,7},{5,2},{6,1},{7,4},{8,11},{9,14},{10,... | collective-permute-start | bytes 786440 | tf_op jit(solution)/shard_map/ppermute | solution.py:215
  29.9 4.1 %place.3 = (bf16[32,4096]{1,0:T(8,128)(2,1)}, bf16[32,4096]{1,0:T(8,128)(2,1)}, bf16[32,4096]{1,0:T(8,128)(2,1)}, bf16[32,4096]{1,0:T(8,128)(2,1)}, bf16[32,4096...) custom-call(s32[1]{0:T(128)} %bitcast.refs_0_, ...), custom_call_target="tpu_custom_call" | custom-call | flops 1024 | bytes 1024 | tf_op jit(solution)/shard_map/place/pallas_call | solution.py:29
  34.1 0.0 collective-permute-done.2.refs_3_
  34.1 7.6 %collective-permute-start.6 = (bf16[32,4096]{1,0:T(8,128)(2,1)}, bf16[32,4096]{1,0:T(8,128)(2,1)}, u32[]{:S(2)}, u32[]{:S(2)}) collective-permute-start(bf16[32,4096]{1,0:T(8,128)(2,1)} %get-tuple-element.92), channel_id=1, source_target_pairs={{0,4},{1,5},{2,6},{3,7},{4,0},{5,1},{6,2},{7,3},{8,12},{9,13},{10,... | collective-permute-start | bytes 786440 | tf_op jit(solution)/shard_map/ppermute | solution.py:215
  41.7 0.0 collective-permute-done.3.refs_4_
  41.7 0.0 collective-permute-start.9
  41.7 0.0 collective-permute-done.4.refs_5_
  41.7 1.7 collective-permute-start.12
  43.4 0.0 collective-permute-done.5.refs_6_
  43.4 15.6 %collective-permute-start.15 = (bf16[32,4096]{1,0:T(8,128)(2,1)}, bf16[32,4096]{1,0:T(8,128)(2,1)}, u32[]{:S(2)}, u32[]{:S(2)}) collective-permute-start(bf16[32,4096]{1,0:T(8,128)(2,1)} %get-tuple-element.113), channel_id=1, source_target_pairs={{0,6},{1,3},{2,4},{3,1},{4,2},{5,7},{6,0},{7,5},{8,14},{9,11},{10,... | collective-permute-start | bytes 786440 | tf_op jit(solution)/shard_map/ppermute | solution.py:215
  59.0 0.0 collective-permute-done.6.refs_7_
  59.0 8.9 %collective-permute-start.7 = (bf16[32,4096]{1,0:T(8,128)(2,1)}, bf16[32,4096]{1,0:T(8,128)(2,1)}, u32[]{:S(2)}, u32[]{:S(2)}) collective-permute-start(bf16[32,4096]{1,0:T(8,128)(2,1)} %get-tuple-element.96), channel_id=1, source_target_pairs={{0,2},{1,7},{2,0},{3,5},{4,6},{5,3},{6,4},{7,1},{8,10},{9,15},{10,... | collective-permute-start | bytes 786440 | tf_op jit(solution)/shard_map/ppermute | solution.py:215
  67.9 8.5 %collective-permute-done.9.refs_1_ = bf16[32,4096]{1,0:T(8,128)(2,1)} collective-permute-done((bf16[32,4096]{1,0:T(8,128)(2,1)}, bf16[32,4096]{1,0:T(8,128)(2,1)}, u32[]{:S(2)}, u32[]{:S(2)}) %collective-permute-start.9) | collective-permute-done | bytes 262176 | tf_op jit(solution)/shard_map/ppermute | solution.py:215
  76.4 0.0 collective-permute-start.10
  76.4 0.0 collective-permute-done.12.refs_2_
  76.4 0.0 collective-permute-start.13
  76.4 11.0 %expert.2 = (bf16[32,4096]{1,0:T(8,128)(2,1)}, bf16[32,4096]{1,0:T(8,128)(2,1)}, bf16[32,4096]{1,0:T(8,128)(2,1)}, bf16[32,4096]{1,0:T(8,128)(2,1)}, bf16[32,409...) custom-call(bf16[32,4096]{1,0:T(8,128)(2,1)} %get-tuple-element.82.r, ...), custom_call_target="tpu_custom_call" | custom-call | flops 1024 | bytes 1024 | tf_op jit(solution)/shard_map/expert/pallas_call | solution.py:29
  87.5 5.3 %collective-permute-start.16 = (bf16[32,4096]{1,0:T(8,128)(2,1)}, bf16[32,4096]{1,0:T(8,128)(2,1)}, u32[]{:S(2)}, u32[]{:S(2)}) collective-permute-start(bf16[32,4096]{1,0:T(8,128)(2,1)} %get-tuple-element.114), channel_id=1, source_target_pairs={{0,4},{1,5},{2,6},{3,7},{4,0},{5,1},{6,2},{7,3},{8,12},{9,13},{10,... | collective-permute-start | bytes 786440 | tf_op jit(solution)/shard_map/ppermute | solution.py:215
  92.8 0.0 collective-permute-start.11
  92.8 7.5 %collective-permute-start.8 = (bf16[32,4096]{1,0:T(8,128)(2,1)}, bf16[32,4096]{1,0:T(8,128)(2,1)}, u32[]{:S(2)}, u32[]{:S(2)}) collective-permute-start(bf16[32,4096]{1,0:T(8,128)(2,1)} %get-tuple-element.97), channel_id=1, source_target_pairs={{0,5},{1,4},{2,3},{3,2},{4,1},{5,0},{6,7},{7,6},{8,13},{9,12},{10,... | collective-permute-start | bytes 786440 | tf_op jit(solution)/shard_map/ppermute | solution.py:215
  100.3 1.0 collective-permute-start.14
  101.3 13.0 %collective-permute-done.16.refs_7_ = bf16[32,4096]{1,0:T(8,128)(2,1)} collective-permute-done((bf16[32,4096]{1,0:T(8,128)(2,1)}, bf16[32,4096]{1,0:T(8,128)(2,1)}, u32[]{:S(2)}, u32[]{:S(2)}) %collective-permute-start.16) | collective-permute-done | bytes 262176 | tf_op jit(solution)/shard_map/ppermute | solution.py:215
  114.3 11.3 %expert.3 = (bf16[32,4096]{1,0:T(8,128)(2,1)}, bf16[32,4096]{1,0:T(8,128)(2,1)}, bf16[32,4096]{1,0:T(8,128)(2,1)}, bf16[32,4096]{1,0:T(8,128)(2,1)}, bf16[32,409...) custom-call(bf16[32,4096]{1,0:T(8,128)(2,1)} %get-tuple-element.124., ...), custom_call_target="tpu_custom_call" | custom-call | flops 1024 | bytes 1024 | tf_op jit(solution)/shard_map/expert/pallas_call | solution.py:29
  125.6 4.8 %weight_part.4 = (bf16[16,2176]{1,0:T(8,128)(2,1)}, bf16[496,2176]{1,0:T(8,128)(2,1)}) custom-call(s32[1]{0:T(128)} %bitcast.5.refs_0_, bf16[256,4096]{1,0:T(8,128)(2,1)} %get-tuple-element.138.refs_1_, bf16[256,1408]{1,0:T(8,128)(2,1)} %get-tuple-element.127.refs_2_, bf16[256,704]{1,0:T(8,128)(2,1)} %get-tuple-element.128.refs_3_, ...), custom_call_target="tpu_custom_call" | custom-call | flops 1024 | bytes 1024 | tf_op jit(solution)/shard_map/weight_part/pallas_call | solution.py:29
  130.4 0.1 collective-permute-start.21
  130.5 0.0 collective-permute-done.8.refs_6_
  130.5 1.6 collective-permute-done.21.refs_7_
  132.1 0.2 collective-permute-start.22
  132.2 1.9 collective-permute-start.18
  134.1 4.7 %weight_part.5 = bf16[512,2176]{1,0:T(8,128)(2,1)} custom-call(s32[1]{0:T(128)} %bitcast.6.refs_0_, bf16[256,4096]{1,0:T(8,128)(2,1)} %get-tuple-element.138.refs_1_, bf16[256,1408]{1,0:T(8,128)(2,1)} %get-tuple-element.127.refs_2_, bf16[256,704]{1,0:T(8,128)(2,1)} %get-tuple-element.128.refs_3_, bf16[256,4096]{1,0:T(8,128)(2,1)} %get-tuple-element.129.refs_4_, ...), custom_call_target="tpu_custom_call" | custom-call | flops 1024 | bytes 1024 | tf_op jit(solution)/shard_map/weight_part/pallas_call | solution.py:29
  138.9 5.6 %weight_part.6 = (bf16[16,2176]{1,0:T(8,128)(2,1)}, bf16[496,2176]{1,0:T(8,128)(2,1)}) custom-call(s32[1]{0:T(128)} %bitcast.7.refs_0_, bf16[256,4096]{1,0:T(8,128)(2,1)} %get-tuple-element.138.refs_1_, bf16[256,1408]{1,0:T(8,128)(2,1)} %get-tuple-element.127.refs_2_, bf16[256,704]{1,0:T(8,128)(2,1)} %get-tuple-element.128.refs_3_, ...), custom_call_target="tpu_custom_call" | custom-call | flops 1024 | bytes 1024 | tf_op jit(solution)/shard_map/weight_part/pallas_call | solution.py:29
  144.5 1.0 collective-permute-start.24
  145.5 1.8 collective-permute-done.17.refs_9_
  147.3 0.3 collective-permute-done.19.refs_11_
  147.6 2.5 %collective-permute-done.18.refs_10_ = bf16[32,4096]{1,0:T(8,128)(2,1)} collective-permute-done((bf16[32,4096]{1,0:T(8,128)(2,1)}, bf16[32,4096]{1,0:T(8,128)(2,1)}, u32[]{:S(2)}, u32[]{:S(2)}) %collective-permute-start.18) | collective-permute-done | bytes 262176 | tf_op jit(solution)/shard_map/ppermute | solution.py:215
  150.1 0.0 collective-permute-done.24.refs_8_
  150.2 0.9 collective-permute-start.25
  151.1 0.0 collective-permute-start.23
  151.1 1.8 collective-permute-start.20
  152.8 1.9 collective-permute-start.27
  154.8 2.4 %collective-permute-start.26 = (bf16[32,4096]{1,0:T(8,128)(2,1)}, bf16[32,4096]{1,0:T(8,128)(2,1)}, u32[]{:S(2)}, u32[]{:S(2)}) collective-permute-start(bf16[32,4096]{1,0:T(8,128)(2,1)} %get-tuple-element.144), channel_id=1, source_target_pairs={{0,5},{1,4},{2,3},{3,2},{4,1},{5,0},{6,7},{7,6},{8,13},{9,12},{10,... | collective-permute-start | bytes 786440 | tf_op jit(solution)/shard_map/ppermute | solution.py:215
  157.1 15.5 %collective-permute-done.20.refs_12_ = bf16[32,4096]{1,0:T(8,128)(2,1)} collective-permute-done((bf16[32,4096]{1,0:T(8,128)(2,1)}, bf16[32,4096]{1,0:T(8,128)(2,1)}, u32[]{:S(2)}, u32[]{:S(2)}) %collective-permute-start.20) | collective-permute-done | bytes 262176 | tf_op jit(solution)/shard_map/ppermute | solution.py:215
  172.6 2.3 %collective-permute-start.28 = (bf16[32,4096]{1,0:T(8,128)(2,1)}, bf16[32,4096]{1,0:T(8,128)(2,1)}, u32[]{:S(2)}, u32[]{:S(2)}) collective-permute-start(bf16[32,4096]{1,0:T(8,128)(2,1)} %get-tuple-element.148), channel_id=1, source_target_pairs={{0,6},{1,3},{2,4},{3,1},{4,2},{5,7},{6,0},{7,5},{8,14},{9,11},{10,... | collective-permute-start | bytes 786440 | tf_op jit(solution)/shard_map/ppermute | solution.py:215
  175.0 4.4 %combine.2 = (bf16[256,2048]{1,0:T(8,128)(2,1)}, bf16[256,2048]{1,0:T(8,128)(2,1)}) custom-call(s32[1]{0:T(128)} %bitcast.refs_0_, s32[8,8]{1,0:T(8,128)} %constant.16.clone.refs_1_, s32[1,256]{1,0:T(1,128)} %bitcast.16, bf16[256,2048]{1,0:T(8,128)(2,1)} %refs_3_.5, bf16[256,2048]{1,0:T(8,128)(2,1)} %refs_4_.5, bf16[32,4096]{1,0:T(8,128)(2,1)} %get-tuple-element.93.refs_5_, ...), custom_call_target="tpu_custom_call" | custom-call | flops 1024 | bytes 1024 | tf_op jit(solution)/shard_map/combine/pallas_call | solution.py:29
  179.3 0.0 collective-permute-done.27.refs_7_
  179.3 4.0 %collective-permute-start.29 = (bf16[32,4096]{1,0:T(8,128)(2,1)}, bf16[32,4096]{1,0:T(8,128)(2,1)}, u32[]{:S(2)}, u32[]{:S(2)}) collective-permute-start(bf16[32,4096]{1,0:T(8,128)(2,1)} %get-tuple-element.150), channel_id=1, source_target_pairs={{0,2},{1,7},{2,0},{3,5},{4,6},{5,3},{6,4},{7,1},{8,10},{9,15},{10,... | collective-permute-start | bytes 786440 | tf_op jit(solution)/shard_map/ppermute | solution.py:215
  183.4 0.0 collective-permute-done.28.refs_8_
  183.4 4.4 %collective-permute-start.30 = (bf16[32,4096]{1,0:T(8,128)(2,1)}, bf16[32,4096]{1,0:T(8,128)(2,1)}, u32[]{:S(2)}, u32[]{:S(2)}) collective-permute-start(bf16[32,4096]{1,0:T(8,128)(2,1)} %get-tuple-element.152), channel_id=1, source_target_pairs={{0,7},{1,2},{2,1},{3,4},{4,3},{5,6},{6,5},{7,0},{8,15},{9,10},{10,... | collective-permute-start | bytes 786440 | tf_op jit(solution)/shard_map/ppermute | solution.py:215
  187.8 11.3 %collective-permute-done.25.refs_9_ = bf16[496,2176]{1,0:T(8,128)(2,1)} collective-permute-done((bf16[496,2176]{1,0:T(8,128)(2,1)}, bf16[496,2176]{1,0:T(8,128)(2,1)}, u32[]{:S(2)}, u32[]{:S(2)}) %collective-permute-start.25) | collective-permute-done | bytes 2158624 | tf_op jit(solution)/shard_map/ppermute | solution.py:215
  199.1 0.9 collective-permute-start.32
  200.0 0.0 collective-permute-done.23.refs_7_
  200.0 6.7 %weight_part.7 = (f32[512,1408]{1,0:T(8,128)}, f32[704,512]{1,0:T(8,128)}) custom-call(s32[1]{0:T(128)} %bitcast.4.refs_0_, bf16[256,4096]{1,0:T(8,128)(2,1)} %get-tuple-element.138.refs_1_, bf16[256,1408]{1,0:T(8,128)(2,1)} %get-tuple-element.127.refs_2_, bf16[256,704]{1,0:T(8,128)(2,1)} %get-tuple-element.128.refs_3_, ...), custom_call_target="tpu_custom_call" | custom-call | flops 1024 | bytes 1024 | tf_op jit(solution)/shard_map/weight_part/pallas_call | solution.py:29
  206.7 0.0 collective-permute-done.31.refs_11_
  206.7 0.0 collective-permute-done.30.refs_10_
  206.8 7.3 %collective-permute-done.32.refs_12_ = bf16[32,4096]{1,0:T(8,128)(2,1)} collective-permute-done((bf16[32,4096]{1,0:T(8,128)(2,1)}, bf16[32,4096]{1,0:T(8,128)(2,1)}, u32[]{:S(2)}, u32[]{:S(2)}) %collective-permute-start.32) | collective-permute-done | bytes 262176 | tf_op jit(solution)/shard_map/ppermute | solution.py:215
  214.0 4.3 %combine.3 = (bf16[256,2048]{1,0:T(8,128)(2,1)}, bf16[256,2048]{1,0:T(8,128)(2,1)}) custom-call(s32[1]{0:T(128)} %bitcast.refs_0_, s32[8,8]{1,0:T(8,128)} %constant.16.clone.refs_1_, s32[1,256]{1,0:T(1,128)} %bitcast.17, bf16[256,2048]{1,0:T(8,128)(2,1)} %get-tuple-element.122.refs_3_, bf16[256,2048]{1,0:T(8,128)(2,1)} %get-tuple-element.123.refs_4_, ...), custom_call_target="tpu_custom_call" | custom-call | flops 1024 | bytes 1024 | tf_op jit(solution)/shard_map/combine/pallas_call | solution.py:29
  (12 shorter events, 0.0 us)
Async XLA Ops:
  4.8 18.2 %collective-permute-start = (bf16[32,4096]{1,0:T(8,128)(2,1)}, bf16[32,4096]{1,0:T(8,128)(2,1)}, u32[]{:S(2)}, u32[]{:S(2)}) collective-permute-start(bf16[32,4096]{1,0:T(8,128)(2,1)} %get-tuple-element.83), channel_id=1, source_target_pairs={{0,5},{1,4},{2,3},{3,2},{4,1},{5,0},{6,7},{7,6},{8,13},{9,12},{10,... | collective-permute-start | bytes 786440 | tf_op jit(solution)/shard_map/ppermute | solution.py:215
  9.8 13.1 %collective-permute-start.1 = (bf16[32,4096]{1,0:T(8,128)(2,1)}, bf16[32,4096]{1,0:T(8,128)(2,1)}, u32[]{:S(2)}, u32[]{:S(2)}) collective-permute-start(bf16[32,4096]{1,0:T(8,128)(2,1)} %get-tuple-element.84), channel_id=1, source_target_pairs={{0,1},{1,0},{2,7},{3,6},{4,5},{5,4},{6,3},{7,2},{8,9},{9,8},{10,15... | collective-permute-start | bytes 786440 | tf_op jit(solution)/shard_map/ppermute | solution.py:215
  10.3 23.7 %collective-permute-start.2 = (bf16[32,4096]{1,0:T(8,128)(2,1)}, bf16[32,4096]{1,0:T(8,128)(2,1)}, u32[]{:S(2)}, u32[]{:S(2)}) collective-permute-start(bf16[32,4096]{1,0:T(8,128)(2,1)} %get-tuple-element.85), channel_id=1, source_target_pairs={{0,6},{1,3},{2,4},{3,1},{4,2},{5,7},{6,0},{7,5},{8,14},{9,11},{10,... | collective-permute-start | bytes 786440 | tf_op jit(solution)/shard_map/ppermute | solution.py:215
  11.7 30.0 %collective-permute-start.3 = (bf16[32,4096]{1,0:T(8,128)(2,1)}, bf16[32,4096]{1,0:T(8,128)(2,1)}, u32[]{:S(2)}, u32[]{:S(2)}) collective-permute-start(bf16[32,4096]{1,0:T(8,128)(2,1)} %get-tuple-element.86), channel_id=1, source_target_pairs={{0,2},{1,7},{2,0},{3,5},{4,6},{5,3},{6,4},{7,1},{8,10},{9,15},{10,... | collective-permute-start | bytes 786440 | tf_op jit(solution)/shard_map/ppermute | solution.py:215
  23.0 18.8 %collective-permute-start.4 = (bf16[32,4096]{1,0:T(8,128)(2,1)}, bf16[32,4096]{1,0:T(8,128)(2,1)}, u32[]{:S(2)}, u32[]{:S(2)}) collective-permute-start(bf16[32,4096]{1,0:T(8,128)(2,1)} %get-tuple-element.88), channel_id=1, source_target_pairs={{0,7},{1,2},{2,1},{3,4},{4,3},{5,6},{6,5},{7,0},{8,15},{9,10},{10,... | collective-permute-start | bytes 786440 | tf_op jit(solution)/shard_map/ppermute | solution.py:215
  23.0 20.4 %collective-permute-start.5 = (bf16[32,4096]{1,0:T(8,128)(2,1)}, bf16[32,4096]{1,0:T(8,128)(2,1)}, u32[]{:S(2)}, u32[]{:S(2)}) collective-permute-start(bf16[32,4096]{1,0:T(8,128)(2,1)} %get-tuple-element.90), channel_id=1, source_target_pairs={{0,3},{1,6},{2,5},{3,0},{4,7},{5,2},{6,1},{7,4},{8,11},{9,14},{10,... | collective-permute-start | bytes 786440 | tf_op jit(solution)/shard_map/ppermute | solution.py:215
  34.1 24.9 %collective-permute-start.6 = (bf16[32,4096]{1,0:T(8,128)(2,1)}, bf16[32,4096]{1,0:T(8,128)(2,1)}, u32[]{:S(2)}, u32[]{:S(2)}) collective-permute-start(bf16[32,4096]{1,0:T(8,128)(2,1)} %get-tuple-element.92), channel_id=1, source_target_pairs={{0,4},{1,5},{2,6},{3,7},{4,0},{5,1},{6,2},{7,3},{8,12},{9,13},{10,... | collective-permute-start | bytes 786440 | tf_op jit(solution)/shard_map/ppermute | solution.py:215
  41.7 34.7 %collective-permute-start.9 = (bf16[32,4096]{1,0:T(8,128)(2,1)}, bf16[32,4096]{1,0:T(8,128)(2,1)}, u32[]{:S(2)}, u32[]{:S(2)}) collective-permute-start(bf16[32,4096]{1,0:T(8,128)(2,1)} %get-tuple-element.101), channel_id=1, source_target_pairs={{0,5},{1,4},{2,3},{3,2},{4,1},{5,0},{6,7},{7,6},{8,13},{9,12},{10,... | collective-permute-start | bytes 786440 | tf_op jit(solution)/shard_map/ppermute | solution.py:215
  41.7 34.7 %collective-permute-start.12 = (bf16[32,4096]{1,0:T(8,128)(2,1)}, bf16[32,4096]{1,0:T(8,128)(2,1)}, u32[]{:S(2)}, u32[]{:S(2)}) collective-permute-start(bf16[32,4096]{1,0:T(8,128)(2,1)} %get-tuple-element.107), channel_id=1, source_target_pairs={{0,1},{1,0},{2,7},{3,6},{4,5},{5,4},{6,3},{7,2},{8,9},{9,8},{10,15... | collective-permute-start | bytes 786440 | tf_op jit(solution)/shard_map/ppermute | solution.py:215
  43.4 44.1 %collective-permute-start.15 = (bf16[32,4096]{1,0:T(8,128)(2,1)}, bf16[32,4096]{1,0:T(8,128)(2,1)}, u32[]{:S(2)}, u32[]{:S(2)}) collective-permute-start(bf16[32,4096]{1,0:T(8,128)(2,1)} %get-tuple-element.113), channel_id=1, source_target_pairs={{0,6},{1,3},{2,4},{3,1},{4,2},{5,7},{6,0},{7,5},{8,14},{9,11},{10,... | collective-permute-start | bytes 786440 | tf_op jit(solution)/shard_map/ppermute | solution.py:215
  59.0 33.8 %collective-permute-start.7 = (bf16[32,4096]{1,0:T(8,128)(2,1)}, bf16[32,4096]{1,0:T(8,128)(2,1)}, u32[]{:S(2)}, u32[]{:S(2)}) collective-permute-start(bf16[32,4096]{1,0:T(8,128)(2,1)} %get-tuple-element.96), channel_id=1, source_target_pairs={{0,2},{1,7},{2,0},{3,5},{4,6},{5,3},{6,4},{7,1},{8,10},{9,15},{10,... | collective-permute-start | bytes 786440 | tf_op jit(solution)/shard_map/ppermute | solution.py:215
  76.4 16.4 %collective-permute-start.10 = (bf16[32,4096]{1,0:T(8,128)(2,1)}, bf16[32,4096]{1,0:T(8,128)(2,1)}, u32[]{:S(2)}, u32[]{:S(2)}) collective-permute-start(bf16[32,4096]{1,0:T(8,128)(2,1)} %get-tuple-element.102), channel_id=1, source_target_pairs={{0,7},{1,2},{2,1},{3,4},{4,3},{5,6},{6,5},{7,0},{8,15},{9,10},{10,... | collective-permute-start | bytes 786440 | tf_op jit(solution)/shard_map/ppermute | solution.py:215
  76.4 23.9 %collective-permute-start.13 = (bf16[32,4096]{1,0:T(8,128)(2,1)}, bf16[32,4096]{1,0:T(8,128)(2,1)}, u32[]{:S(2)}, u32[]{:S(2)}) collective-permute-start(bf16[32,4096]{1,0:T(8,128)(2,1)} %get-tuple-element.108), channel_id=1, source_target_pairs={{0,3},{1,6},{2,5},{3,0},{4,7},{5,2},{6,1},{7,4},{8,11},{9,14},{10,... | collective-permute-start | bytes 786440 | tf_op jit(solution)/shard_map/ppermute | solution.py:215
  87.5 26.8 %collective-permute-start.16 = (bf16[32,4096]{1,0:T(8,128)(2,1)}, bf16[32,4096]{1,0:T(8,128)(2,1)}, u32[]{:S(2)}, u32[]{:S(2)}) collective-permute-start(bf16[32,4096]{1,0:T(8,128)(2,1)} %get-tuple-element.114), channel_id=1, source_target_pairs={{0,4},{1,5},{2,6},{3,7},{4,0},{5,1},{6,2},{7,3},{8,12},{9,13},{10,... | collective-permute-start | bytes 786440 | tf_op jit(solution)/shard_map/ppermute | solution.py:215
  92.8 37.7 %collective-permute-start.11 = (bf16[32,4096]{1,0:T(8,128)(2,1)}, bf16[32,4096]{1,0:T(8,128)(2,1)}, u32[]{:S(2)}, u32[]{:S(2)}) collective-permute-start(bf16[32,4096]{1,0:T(8,128)(2,1)} %get-tuple-element.103), channel_id=1, source_target_pairs={{0,1},{1,0},{2,7},{3,6},{4,5},{5,4},{6,3},{7,2},{8,9},{9,8},{10,15... | collective-permute-start | bytes 786440 | tf_op jit(solution)/shard_map/ppermute | solution.py:215
  92.8 37.7 %collective-permute-start.8 = (bf16[32,4096]{1,0:T(8,128)(2,1)}, bf16[32,4096]{1,0:T(8,128)(2,1)}, u32[]{:S(2)}, u32[]{:S(2)}) collective-permute-start(bf16[32,4096]{1,0:T(8,128)(2,1)} %get-tuple-element.97), channel_id=1, source_target_pairs={{0,5},{1,4},{2,3},{3,2},{4,1},{5,0},{6,7},{7,6},{8,13},{9,12},{10,... | collective-permute-start | bytes 786440 | tf_op jit(solution)/shard_map/ppermute | solution.py:215
  100.3 31.8 %collective-permute-start.14 = (bf16[32,4096]{1,0:T(8,128)(2,1)}, bf16[32,4096]{1,0:T(8,128)(2,1)}, u32[]{:S(2)}, u32[]{:S(2)}) collective-permute-start(bf16[32,4096]{1,0:T(8,128)(2,1)} %get-tuple-element.109), channel_id=1, source_target_pairs={{0,6},{1,3},{2,4},{3,1},{4,2},{5,7},{6,0},{7,5},{8,14},{9,11},{10,... | collective-permute-start | bytes 786440 | tf_op jit(solution)/shard_map/ppermute | solution.py:215
  130.4 1.7 collective-permute-start.21
  132.1 6.8 %collective-permute-start.22 = (bf16[496,2176]{1,0:T(8,128)(2,1)}, bf16[496,2176]{1,0:T(8,128)(2,1)}, u32[]{:S(2)}, u32[]{:S(2)}) collective-permute-start(bf16[496,2176]{1,0:T(8,128)(2,1)} %get-tuple-element.136), channel_id=1, source_target_pairs={{0,8},{8,0},{16,24},{24,16},{1,9},{9,1},{17,25},{25,17},{2,10},{10... | collective-permute-start | bytes 6475784 | tf_op jit(solution)/shard_map/ppermute | solution.py:215
  132.2 15.1 %collective-permute-start.17 = (bf16[32,4096]{1,0:T(8,128)(2,1)}, bf16[32,4096]{1,0:T(8,128)(2,1)}, u32[]{:S(2)}, u32[]{:S(2)}) collective-permute-start(bf16[32,4096]{1,0:T(8,128)(2,1)} %get-tuple-element.115), channel_id=1, source_target_pairs={{0,2},{1,7},{2,0},{3,5},{4,6},{5,3},{6,4},{7,1},{8,10},{9,15},{10,... | collective-permute-start | bytes 786440 | tf_op jit(solution)/shard_map/ppermute | solution.py:215
  132.2 15.4 %collective-permute-start.19 = (bf16[32,4096]{1,0:T(8,128)(2,1)}, bf16[32,4096]{1,0:T(8,128)(2,1)}, u32[]{:S(2)}, u32[]{:S(2)}) collective-permute-start(bf16[32,4096]{1,0:T(8,128)(2,1)} %get-tuple-element.119), channel_id=1, source_target_pairs={{0,3},{1,6},{2,5},{3,0},{4,7},{5,2},{6,1},{7,4},{8,11},{9,14},{10,... | collective-permute-start | bytes 786440 | tf_op jit(solution)/shard_map/ppermute | solution.py:215
  132.2 17.9 %collective-permute-start.18 = (bf16[32,4096]{1,0:T(8,128)(2,1)}, bf16[32,4096]{1,0:T(8,128)(2,1)}, u32[]{:S(2)}, u32[]{:S(2)}) collective-permute-start(bf16[32,4096]{1,0:T(8,128)(2,1)} %get-tuple-element.117), channel_id=1, source_target_pairs={{0,7},{1,2},{2,1},{3,4},{4,3},{5,6},{6,5},{7,0},{8,15},{9,10},{10,... | collective-permute-start | bytes 786440 | tf_op jit(solution)/shard_map/ppermute | solution.py:215
  144.5 5.6 %collective-permute-start.24 = (bf16[16,2176]{1,0:T(8,128)(2,1)}, bf16[16,2176]{1,0:T(8,128)(2,1)}, u32[]{:S(2)}, u32[]{:S(2)}) collective-permute-start(bf16[16,2176]{1,0:T(8,128)(2,1)} %get-tuple-element.137), channel_id=1, source_target_pairs={{0,16},{8,24},{16,0},{24,8},{1,17},{9,25},{17,1},{25,9},{2,18},{10... | collective-permute-start | bytes 208904 | tf_op jit(solution)/shard_map/ppermute | solution.py:215
  150.2 48.9 %collective-permute-start.25 = (bf16[496,2176]{1,0:T(8,128)(2,1)}, bf16[496,2176]{1,0:T(8,128)(2,1)}, u32[]{:S(2)}, u32[]{:S(2)}) collective-permute-start(bf16[496,2176]{1,0:T(8,128)(2,1)} %get-tuple-element.140), channel_id=1, source_target_pairs={{0,16},{8,24},{16,0},{24,8},{1,17},{9,25},{17,1},{25,9},{2,18},{10... | collective-permute-start | bytes 6475784 | tf_op jit(solution)/shard_map/ppermute | solution.py:215
  151.1 49.0 %collective-permute-start.23 = (bf16[512,2176]{1,0:T(8,128)(2,1)}, bf16[512,2176]{1,0:T(8,128)(2,1)}, u32[]{:S(2)}, u32[]{:S(2)}) collective-permute-start(bf16[512,2176]{1,0:T(8,128)(2,1)} %weight_part.5), channel_id=1, source_target_pairs={{0,8},{8,0},{16,24},{24,16},{1,9},{9,1},{17,25},{25,17},{2,10},{10... | collective-permute-start | bytes 6684680 | tf_op jit(solution)/shard_map/ppermute | solution.py:215
  151.1 21.6 %collective-permute-start.20 = (bf16[32,4096]{1,0:T(8,128)(2,1)}, bf16[32,4096]{1,0:T(8,128)(2,1)}, u32[]{:S(2)}, u32[]{:S(2)}) collective-permute-start(bf16[32,4096]{1,0:T(8,128)(2,1)} %get-tuple-element.121), channel_id=1, source_target_pairs={{0,4},{1,5},{2,6},{3,7},{4,0},{5,1},{6,2},{7,3},{8,12},{9,13},{10,... | collective-permute-start | bytes 786440 | tf_op jit(solution)/shard_map/ppermute | solution.py:215
  152.8 26.5 %collective-permute-start.27 = (bf16[32,4096]{1,0:T(8,128)(2,1)}, bf16[32,4096]{1,0:T(8,128)(2,1)}, u32[]{:S(2)}, u32[]{:S(2)}) collective-permute-start(bf16[32,4096]{1,0:T(8,128)(2,1)} %get-tuple-element.146), channel_id=1, source_target_pairs={{0,1},{1,0},{2,7},{3,6},{4,5},{5,4},{6,3},{7,2},{8,9},{9,8},{10,15... | collective-permute-start | bytes 786440 | tf_op jit(solution)/shard_map/ppermute | solution.py:215
  154.8 28.6 %collective-permute-start.26 = (bf16[32,4096]{1,0:T(8,128)(2,1)}, bf16[32,4096]{1,0:T(8,128)(2,1)}, u32[]{:S(2)}, u32[]{:S(2)}) collective-permute-start(bf16[32,4096]{1,0:T(8,128)(2,1)} %get-tuple-element.144), channel_id=1, source_target_pairs={{0,5},{1,4},{2,3},{3,2},{4,1},{5,0},{6,7},{7,6},{8,13},{9,12},{10,... | collective-permute-start | bytes 786440 | tf_op jit(solution)/shard_map/ppermute | solution.py:215
  172.6 10.7 %collective-permute-start.28 = (bf16[32,4096]{1,0:T(8,128)(2,1)}, bf16[32,4096]{1,0:T(8,128)(2,1)}, u32[]{:S(2)}, u32[]{:S(2)}) collective-permute-start(bf16[32,4096]{1,0:T(8,128)(2,1)} %get-tuple-element.148), channel_id=1, source_target_pairs={{0,6},{1,3},{2,4},{3,1},{4,2},{5,7},{6,0},{7,5},{8,14},{9,11},{10,... | collective-permute-start | bytes 786440 | tf_op jit(solution)/shard_map/ppermute | solution.py:215
  179.3 27.4 %collective-permute-start.29 = (bf16[32,4096]{1,0:T(8,128)(2,1)}, bf16[32,4096]{1,0:T(8,128)(2,1)}, u32[]{:S(2)}, u32[]{:S(2)}) collective-permute-start(bf16[32,4096]{1,0:T(8,128)(2,1)} %get-tuple-element.150), channel_id=1, source_target_pairs={{0,2},{1,7},{2,0},{3,5},{4,6},{5,3},{6,4},{7,1},{8,10},{9,15},{10,... | collective-permute-start | bytes 786440 | tf_op jit(solution)/shard_map/ppermute | solution.py:215
  183.4 23.4 %collective-permute-start.31 = (bf16[32,4096]{1,0:T(8,128)(2,1)}, bf16[32,4096]{1,0:T(8,128)(2,1)}, u32[]{:S(2)}, u32[]{:S(2)}) collective-permute-start(bf16[32,4096]{1,0:T(8,128)(2,1)} %get-tuple-element.154), channel_id=1, source_target_pairs={{0,3},{1,6},{2,5},{3,0},{4,7},{5,2},{6,1},{7,4},{8,11},{9,14},{10,... | collective-permute-start | bytes 786440 | tf_op jit(solution)/shard_map/ppermute | solution.py:215
  183.4 23.4 %collective-permute-start.30 = (bf16[32,4096]{1,0:T(8,128)(2,1)}, bf16[32,4096]{1,0:T(8,128)(2,1)}, u32[]{:S(2)}, u32[]{:S(2)}) collective-permute-start(bf16[32,4096]{1,0:T(8,128)(2,1)} %get-tuple-element.152), channel_id=1, source_target_pairs={{0,7},{1,2},{2,1},{3,4},{4,3},{5,6},{6,5},{7,0},{8,15},{9,10},{10,... | collective-permute-start | bytes 786440 | tf_op jit(solution)/shard_map/ppermute | solution.py:215
  199.1 14.9 %collective-permute-start.32 = (bf16[32,4096]{1,0:T(8,128)(2,1)}, bf16[32,4096]{1,0:T(8,128)(2,1)}, u32[]{:S(2)}, u32[]{:S(2)}) collective-permute-start(bf16[32,4096]{1,0:T(8,128)(2,1)} %get-tuple-element.156), channel_id=1, source_target_pairs={{0,4},{1,5},{2,6},{3,7},{4,0},{5,1},{6,2},{7,3},{8,12},{9,13},{10,... | collective-permute-start | bytes 786440 | tf_op jit(solution)/shard_map/ppermute | solution.py:215

commit v9 on v8

--- a/solution.py
+++ b/solution.py
@@ -1,6 +1,5 @@
 import jax
 import jax.numpy as jnp
-import numpy as np
 from jax import lax
 from jax.experimental import pallas as pl
 from jax.experimental.pallas import tpu as pltpu
@@ -24,20 +23,18 @@
     return jax.ShapeDtypeStruct(shape, dtype)
 
 
-def call(kernel, name, outs, scratch, arrays, small=(), scalars=()):
+def call(kernel, name, outs, scratch, arrays, scalars=()):
     hbm = pl.BlockSpec(memory_space=pltpu.HBM)
     return pl.pallas_call(
         kernel,
-        in_specs=[pl.BlockSpec(memory_space=pltpu.SMEM)] * len(scalars)
-        + [pl.BlockSpec(memory_space=pltpu.VMEM)] * len(small)
-        + [hbm] * len(arrays),
+        in_specs=[pl.BlockSpec(memory_space=pltpu.SMEM)] * len(scalars) + [hbm] * len(arrays),
         out_specs=[hbm] * len(outs),
         out_shape=outs,
         scratch_shapes=scratch,
         compiler_params=pltpu.CompilerParams(vmem_limit_bytes=VMEM_BYTES),
         cost_estimate=SMALL,
         name=name,
-    )(*scalars, *small, *arrays)
+    )(*scalars, *arrays)
 
 
 class Copies:
@@ -57,18 +54,19 @@
         copy.wait()
 
 
-def place_kernel(part, cap, me_ref, table_ref, ids_ref, tokens_ref, grad_ref, *refs):
-    blocks, (data, moved, sems) = refs[:-3], refs[-3:]
+def place_kernel(part, cap, ids_ref, tokens_ref, grad_ref, *refs):
+    blocks, (ids, data, moved, sems) = refs[:-4], refs[-4:]
     copies = Copies(sems)
+    ids_load = copies.start(ids_ref, ids)
     pieces = pieces_of(tokens_ref, grad_ref)
     loads = [copies.start(ref.at[:, there], data.at[:, here]) for ref, there, here in pieces]
-    placing = placing_of(me_ref, table_ref, ids_ref, len(blocks), part, cap)
+    ids_load.wait()
+    placing = placing_of(ids[...], len(blocks), part, cap)
     stores = []
     for load, (_, _, here) in zip(loads, pieces):
         load.wait()
         moved[:, here] = dot(placing, data[:, here], PLAIN).astype(BF16)
-        for index, block in enumerate(blocks):
-            stores.append(copies.start(moved.at[index * cap : (index + 1) * cap, here], block.at[:, here]))
+        stores += store_rows(copies, moved, blocks, here)
     wait(stores)
 
 
@@ -82,13 +80,12 @@
     ]
 
 
-def placing_of(me_ref, table_ref, ids_ref, experts, part, cap):
-    ids = ids_ref[...]
+def placing_of(ids, experts, part, cap):
     rows = ids.shape[1]
-    me = me_ref[0]
     rel = jnp.zeros((1, rows), jnp.int32)
-    for expert in range(experts):
-        rel = jnp.where(ids == expert, table_ref[me, expert], rel)
+    me = lax.axis_index("exp").astype(jnp.int32)
+    for mask in range(1, experts):
+        rel = jnp.where(ids == (me ^ mask), round_of(me, mask, experts), rel)
     onehot = lax.broadcasted_iota(jnp.int32, (max(experts, 16), rows), 0) == rel
     before = lax.broadcasted_iota(jnp.int32, (rows, rows), 0) < lax.broadcasted_iota(jnp.int32, (rows, rows), 1)
     ranks = dot(onehot.astype(BF16), before.astype(BF16), PLAIN)
@@ -106,13 +103,16 @@
     copies = Copies(sems)
     loads = [copies.start(block, slot.at[index * cap : (index + 1) * cap]) for index, block in enumerate(blocks)]
     two_load = copies.start(two_ref, two)
-    one_load = copies.start(one_ref, one)
+    half = width // 2
+    one_loads = [copies.start(one_ref.at[start : start + half], one.at[start : start + half]) for start in (0, half)]
     wait(loads)
     stores = [copies.start(slot, slot_out)]
     two_load.wait()
     grad_hidden = dot(slot[:, width:], two[...], COLS)
-    one_load.wait()
-    both = dot(slot[:, :width], one[...], PLAIN)
+    one_loads[0].wait()
+    both = dot(slot[:, :half], one[:half], PLAIN)
+    one_loads[1].wait()
+    both = both + dot(slot[:, half:width], one[half:], PLAIN)
     gate, upper = both[:, :wide], both[:, wide:]
     sigma = 1.0 / (1.0 + jnp.exp(-gate))
     silu = gate * sigma
@@ -123,9 +123,15 @@
     ).astype(BF16)
     stores.append(copies.start(proj, proj_out))
     back[:, :width] = dot(hidden[...], two[...], PLAIN).astype(BF16)
+    stores += store_rows(copies, back, outs, slice(0, width))
     back[:, width:] = dot(proj[...], one[...], COLS).astype(BF16)
-    stores += [copies.start(back.at[index * cap : (index + 1) * cap], out) for index, out in enumerate(outs)]
+    stores += store_rows(copies, back, outs, slice(width, 2 * width))
     wait(stores)
+
+
+def store_rows(copies, source, outs, here):
+    cap = outs[0].shape[0]
+    return [copies.start(source.at[index * cap : (index + 1) * cap, here], out.at[:, here]) for index, out in enumerate(outs)]
 
 
 def weight_kernel(end, parts, pieces, number_ref, *refs):
@@ -180,16 +186,18 @@
     wait(stores)
 
 
-def combine_kernel(part, cap, me_ref, table_ref, ids_ref, tokens_ref, grad_ref, *refs):
-    blocks, (mixed_out, grad_out, data, back, sems) = refs[:-5], refs[-5:]
+def combine_kernel(part, cap, ids_ref, tokens_ref, grad_ref, *refs):
+    blocks, (mixed_out, grad_out, ids, data, back, sems) = refs[:-6], refs[-6:]
     copies = Copies(sems)
+    ids_load = copies.start(ids_ref, ids)
     pieces = pieces_of(tokens_ref, grad_ref)
     loads = []
     for ref, there, here in pieces:
         loads.append([copies.start(ref.at[:, there], data.at[:, here])])
         for index, block in enumerate(blocks):
             loads[-1].append(copies.start(block.at[:, here], back.at[index * cap : (index + 1) * cap, here]))
-    placing = placing_of(me_ref, table_ref, ids_ref, len(blocks), part, cap)
+    ids_load.wait()
+    placing = placing_of(ids[...], len(blocks), part, cap)
     stores = []
     for load, (_, there, here), (out, _, _) in zip(loads, pieces, pieces_of(mixed_out, grad_out)):
         wait(load)
@@ -217,29 +225,31 @@
 
 
 def rounds_of(experts):
+    rounds = [[0] * experts for _ in range(experts)]
+    for place in range(experts):
+        for mask in range(experts):
+            rounds[round_of(place, mask, experts)][place] = place ^ mask
+    return rounds
+
+
+def round_of(place, mask, experts):
     half = experts // 2
-    rounds = [list(range(experts))]
-    for near in range(1, half):
-        units = [unit for unit in range(1, half) if bin(unit & near).count("1") % 2 == 0]
-        for turn in range(2):
-            far_now = [bin(place & units[0]).count("1") % 2 == turn if units else not turn for place in range(experts)]
-            rounds.append([place ^ (near + half if far else near) for place, far in zip(range(experts), far_now)])
-    rounds.append([place ^ half for place in range(experts)])
-    return rounds
-
-
-def table_of(rounds):
-    table = np.zeros((len(rounds), len(rounds)), np.int32)
-    for number, partners in enumerate(rounds):
-        for place, partner in enumerate(partners):
-            table[place, partner] = number
-    return table
-
-
-def exchange(blocks, rounds, lane, held={}):
-    moved = [blocks[0]]
-    for number in range(1, len(rounds)):
-        moved.append(lane.send(blocks[number], "exp", list(enumerate(rounds[number])), *held.get(number, ())))
+    near = mask % half
+    if near == 0:
+        return experts - 1 if mask else 0
+    units = [unit for unit in range(1, half) if bin(unit & near).count("1") % 2 == 0]
+    turn = 0
+    for bit in range(half.bit_length() if units else 0):
+        if units[0] >> bit & 1:
+            turn = turn ^ ((place >> bit) & 1)
+    return 2 * near - 1 + (turn if mask >= half else 1 - turn)
+
+
+def exchange(blocks, rounds, lane, numbers, *earlier):
+    moved = []
+    for number in numbers:
+        more = earlier if number == numbers[-1] else ()
+        moved.append(lane.send(blocks[number], "exp", list(enumerate(rounds[number])), *more))
     return moved
 
 
@@ -257,12 +267,12 @@
     share = width // groups
     pair = like((cap, 2 * width))
     sems = pltpu.SemaphoreType.DMA
+    ids_here = pltpu.VMEM((1, rows), jnp.int32)
+    halves = [pltpu.VMEM((count, 2 * width), BF16) for count in (rows, slots)]
     lane = Lane(4)
-    last = experts - 1
+    numbers = range(1, experts)
     ids = expert_ids.reshape(1, rows)
-    me = lax.axis_index("exp").astype(jnp.int32)[None]
     rounds = rounds_of(experts)
-    table = jnp.asarray(table_of(rounds))
     group = lax.axis_index("grp").astype(jnp.int32)
 
     def place(part):
@@ -270,10 +280,8 @@
             lambda *refs: place_kernel(part, cap, *refs),
             "place",
             [pair] * experts,
-            [pltpu.VMEM((rows, 2 * width), BF16), pltpu.VMEM((slots, 2 * width), BF16), sems((PIECES * (1 + experts),))],
-            [tokens, grad_out],
-            [ids],
-            [me, table],
+            [ids_here, *halves, sems((1 + PIECES * (1 + experts),))],
+            [ids, tokens, grad_out],
         )
 
     def expert(blocks):
@@ -284,7 +292,7 @@
             expert_kernel,
             "expert",
             [pair] * experts + [like(shape) for shape in shapes],
-            scratch + back + [sems((5 + 2 * experts,))],
+            scratch + back + [sems((6 + 3 * experts,))],
             [*blocks, weight_one, weight_two],
         )
         return outs[:experts], outs[experts:]
@@ -315,26 +323,30 @@
             lambda *refs: combine_kernel(part, cap, *refs),
             "combine",
             [like((rows, width))] * 2,
-            [pltpu.VMEM((rows, 2 * width), BF16), pltpu.VMEM((slots, 2 * width), BF16), sems((PIECES * (2 + experts),))],
-            [first, second, *blocks],
-            [ids],
-            [me, table],
+            [ids_here, *halves, sems((1 + PIECES * (2 + experts),))],
+            [ids, first, second, *blocks],
         )
 
     sent = [place(part) for part in range(parts)]
     results = []
     for part in range(parts):
-        held = {last: (results[-1][0][0],)} if results else {}
-        results.append(expert(exchange(sent[part], rounds, lane, held)))
+        earlier = [results[-1][0][0]] if results else []
+        results.append(expert([sent[part][0]] + exchange(sent[part], rounds, lane, numbers, *earlier)))
     kept = [result[1] for result in results]
 
     count = len(lane.done)
-    back = [exchange(results[0][0], rounds, lane)]
+    mixed, grad = tokens, grad_out
+    back = []
+    for part in range(parts):
+        if back:
+            mixed, grad = combine(part - 1, mixed, grad, back)
+        blocks = results[part][0]
+        back = [blocks[0]] + exchange(blocks, rounds, lane, numbers if part < parts - 1 else numbers[:-1])
     done = lane.done[count:]
 
     received = {q: [] for q in range(groups)}
     sums = kept[0][0]
-    held = {groups - 1: done[:3], 2: done[3:6]}
+    held = {groups - 1: done[:3], 2: done[3:5]}
     for q in sorted(range(1, groups), key=lambda q: (q & -q, -q)):
         low = q & -q
         sent = weight_part(group ^ q, [[sums, *kept[0][1:]], *kept[1:]], received[q], False, 16 if q in held else 0)
@@ -344,13 +356,10 @@
         received[q ^ low].append([short.send(sent[0], "grp", pairs)])
         received[q ^ low][-1] += [short.send(piece, "grp", pairs, *held[q]) for piece in sent[1:]]
 
-    mixed, grad = tokens, grad_out
-    for part in range(1, parts):
-        mixed, grad = combine(part - 1, mixed, grad, back[-1])
-        back.append(exchange(results[part][0], rounds, lane, {last: (mixed, *received[0][-1])}))
     grad_gate_up, grad_down = weight_part(group, [[sums, *kept[0][1:]], *kept[1:]], received[0], True, 0)
-    back[-1][0] = after(back[-1][0], grad_gate_up)
-    mixed, grad = combine(parts - 1, mixed, grad, back[-1])
+    back += exchange(blocks, rounds, lane, numbers[-1:], mixed, lane.done[-3])
+    back[0] = after(back[0], grad_gate_up)
+    mixed, grad = combine(parts - 1, mixed, grad, back)
     return (mixed, grad, grad_gate_up[None], grad_down[None])
 
 

time: 220 us -> 218 us (level)
  starting transfers between devices: 83.5 us -> 95.4 us
  waiting for transfers between devices: 73 us -> 63.5 us
  Pallas kernels: 61 us -> 57.9 us
    ppermute x33, starting transfers between devices: 83.5 us -> 95.4 us  [send(): self.done.append(lax.ppermute(after(value, *earlier), axis, pairs))]
    ppermute x33, waiting for transfers between devices: 73 us -> 63.5 us  [send(): self.done.append(lax.ppermute(after(value, *earlier), axis, pairs))]
    pallas_call x10, Pallas kernels: 61 us -> 57.9 us  [call(): pl.pallas_call(kernel, in_specs=[pl.BlockSpec(memory_space=pltpu.SMEM)] *...]
  transfers between devices with their start and end apart: 33 -> 33, of which waited for: 10 -> 12; matrix products, arithmetic and copies ran while one was open for 0% -> 0% of each run, Pallas kernels for 24% -> 23%
where the time goes in v9:
time: 218 us
  starting transfers between devices  95.4 us (44%)
  waiting for transfers between devices  63.5 us (29%)
  Pallas kernels  57.9 us (27%)
    ppermute x33, starting transfers between devices, send(): self.done.append(lax.ppermute(after(value, *earlier), axis, pairs))  95.4 us
    ppermute x33, waiting for transfers between devices, send(): self.done.append(lax.ppermute(after(value, *earlier), axis, pairs))  63.5 us
    pallas_call x10, Pallas kernels, call(): pl.pallas_call(kernel, in_specs=[pl.BlockSpec(memory_space=pltpu.SMEM)] *...  57.9 us
  transfers between devices with their start and end apart: 33, of which 12 were waited for; matrix products, arithmetic and copies ran while one was open for 0% of the time, Pallas kernels for 23%

profile of v9, /device:TPU:0, one launch (start us, length us, event | category | flops | bytes accessed | tf_op | source)
XLA Modules:
  0.0 217.8 jit_solution(1643522361035018406)
XLA Ops:
  0.6 3.4 %place.2 = (bf16[32,4096]{1,0:T(8,128)(2,1)}, bf16[32,4096]{1,0:T(8,128)(2,1)}, bf16[32,4096]{1,0:T(8,128)(2,1)}, bf16[32,4096]{1,0:T(8,128)(2,1)}, bf16[32,4096...) custom-call(s32[1,256]{1,0:T(1,128)} %bitcast.13, ...), custom_call_target="tpu_custom_call" | custom-call | flops 1024 | bytes 1024 | tf_op jit(solution)/shard_map/place/pallas_call | solution.py:28
  4.1 5.1 %collective-permute-start = (bf16[32,4096]{1,0:T(8,128)(2,1)}, bf16[32,4096]{1,0:T(8,128)(2,1)}, u32[]{:S(2)}, u32[]{:S(2)}) collective-permute-start(bf16[32,4096]{1,0:T(8,128)(2,1)} %get-tuple-element.83), channel_id=1, source_target_pairs={{0,5},{1,4},{2,3},{3,2},{4,1},{5,0},{6,7},{7,6},{8,13},{9,12},{10,... | collective-permute-start | bytes 786440 | tf_op jit(solution)/shard_map/ppermute | solution.py:223
  9.1 0.5 collective-permute-start.1
  9.6 1.3 collective-permute-start.2
  11.0 0.2 collective-permute-start.3
  11.2 11.0 %collective-permute-done.refs_1_ = bf16[32,4096]{1,0:T(8,128)(2,1)} collective-permute-done((bf16[32,4096]{1,0:T(8,128)(2,1)}, bf16[32,4096]{1,0:T(8,128)(2,1)}, u32[]{:S(2)}, u32[]{:S(2)}) %collective-permute-start) | collective-permute-done | bytes 262176 | tf_op jit(solution)/shard_map/ppermute | solution.py:223
  22.2 0.0 collective-permute-start.4
  22.2 7.0 %collective-permute-start.5 = (bf16[32,4096]{1,0:T(8,128)(2,1)}, bf16[32,4096]{1,0:T(8,128)(2,1)}, u32[]{:S(2)}, u32[]{:S(2)}) collective-permute-start(bf16[32,4096]{1,0:T(8,128)(2,1)} %get-tuple-element.90), channel_id=1, source_target_pairs={{0,3},{1,6},{2,5},{3,0},{4,7},{5,2},{6,1},{7,4},{8,11},{9,14},{10,... | collective-permute-start | bytes 786440 | tf_op jit(solution)/shard_map/ppermute | solution.py:223
  29.2 3.4 %place.3 = (bf16[32,4096]{1,0:T(8,128)(2,1)}, bf16[32,4096]{1,0:T(8,128)(2,1)}, bf16[32,4096]{1,0:T(8,128)(2,1)}, bf16[32,4096]{1,0:T(8,128)(2,1)}, bf16[32,4096...) custom-call(s32[1,256]{1,0:T(1,128)} %bitcast.14, ...), custom_call_target="tpu_custom_call" | custom-call | flops 1024 | bytes 1024 | tf_op jit(solution)/shard_map/place/pallas_call | solution.py:28
  32.7 0.0 collective-permute-done.2.refs_3_
  32.7 8.3 %collective-permute-start.6 = (bf16[32,4096]{1,0:T(8,128)(2,1)}, bf16[32,4096]{1,0:T(8,128)(2,1)}, u32[]{:S(2)}, u32[]{:S(2)}) collective-permute-start(bf16[32,4096]{1,0:T(8,128)(2,1)} %get-tuple-element.92), channel_id=1, source_target_pairs={{0,4},{1,5},{2,6},{3,7},{4,0},{5,1},{6,2},{7,3},{8,12},{9,13},{10,... | collective-permute-start | bytes 786440 | tf_op jit(solution)/shard_map/ppermute | solution.py:223
  41.0 0.0 collective-permute-done.3.refs_4_
  41.0 0.0 collective-permute-start.9
  41.0 0.0 collective-permute-done.4.refs_5_
  41.0 1.7 collective-permute-start.12
  42.7 0.0 collective-permute-done.5.refs_6_
  42.7 15.6 %collective-permute-start.15 = (bf16[32,4096]{1,0:T(8,128)(2,1)}, bf16[32,4096]{1,0:T(8,128)(2,1)}, u32[]{:S(2)}, u32[]{:S(2)}) collective-permute-start(bf16[32,4096]{1,0:T(8,128)(2,1)} %get-tuple-element.113), channel_id=1, source_target_pairs={{0,6},{1,3},{2,4},{3,1},{4,2},{5,7},{6,0},{7,5},{8,14},{9,11},{10,... | collective-permute-start | bytes 786440 | tf_op jit(solution)/shard_map/ppermute | solution.py:223
  58.3 0.0 collective-permute-done.6.refs_7_
  58.3 8.9 %collective-permute-start.7 = (bf16[32,4096]{1,0:T(8,128)(2,1)}, bf16[32,4096]{1,0:T(8,128)(2,1)}, u32[]{:S(2)}, u32[]{:S(2)}) collective-permute-start(bf16[32,4096]{1,0:T(8,128)(2,1)} %get-tuple-element.96), channel_id=1, source_target_pairs={{0,2},{1,7},{2,0},{3,5},{4,6},{5,3},{6,4},{7,1},{8,10},{9,15},{10,... | collective-permute-start | bytes 786440 | tf_op jit(solution)/shard_map/ppermute | solution.py:223
  67.2 8.5 %collective-permute-done.9.refs_1_ = bf16[32,4096]{1,0:T(8,128)(2,1)} collective-permute-done((bf16[32,4096]{1,0:T(8,128)(2,1)}, bf16[32,4096]{1,0:T(8,128)(2,1)}, u32[]{:S(2)}, u32[]{:S(2)}) %collective-permute-start.9) | collective-permute-done | bytes 262176 | tf_op jit(solution)/shard_map/ppermute | solution.py:223
  75.7 0.0 collective-permute-start.10
  75.7 0.0 collective-permute-done.12.refs_2_
  75.7 10.9 %expert.2 = (bf16[32,4096]{1,0:T(8,128)(2,1)}, bf16[32,4096]{1,0:T(8,128)(2,1)}, bf16[32,4096]{1,0:T(8,128)(2,1)}, bf16[32,4096]{1,0:T(8,128)(2,1)}, bf16[32,409...) custom-call(bf16[32,4096]{1,0:T(8,128)(2,1)} %get-tuple-element.82.r, ...), custom_call_target="tpu_custom_call" | custom-call | flops 1024 | bytes 1024 | tf_op jit(solution)/shard_map/expert/pallas_call | solution.py:28
  86.6 0.0 collective-permute-done.15.refs_3_
  86.6 5.3 %collective-permute-start.16 = (bf16[32,4096]{1,0:T(8,128)(2,1)}, bf16[32,4096]{1,0:T(8,128)(2,1)}, u32[]{:S(2)}, u32[]{:S(2)}) collective-permute-start(bf16[32,4096]{1,0:T(8,128)(2,1)} %get-tuple-element.114), channel_id=1, source_target_pairs={{0,4},{1,5},{2,6},{3,7},{4,0},{5,1},{6,2},{7,3},{8,12},{9,13},{10,... | collective-permute-start | bytes 786440 | tf_op jit(solution)/shard_map/ppermute | solution.py:223
  92.0 0.0 collective-permute-done.7.refs_4_
  92.0 0.0 collective-permute-done.10.refs_5_
  92.0 0.0 collective-permute-start.11
  92.0 7.6 %collective-permute-start.8 = (bf16[32,4096]{1,0:T(8,128)(2,1)}, bf16[32,4096]{1,0:T(8,128)(2,1)}, u32[]{:S(2)}, u32[]{:S(2)}) collective-permute-start(bf16[32,4096]{1,0:T(8,128)(2,1)} %get-tuple-element.97), channel_id=1, source_target_pairs={{0,5},{1,4},{2,3},{3,2},{4,1},{5,0},{6,7},{7,6},{8,13},{9,12},{10,... | collective-permute-start | bytes 786440 | tf_op jit(solution)/shard_map/ppermute | solution.py:223
  99.6 0.0 collective-permute-done.13.refs_6_
  99.6 1.0 collective-permute-start.14
  100.6 13.0 %collective-permute-done.16.refs_7_ = bf16[32,4096]{1,0:T(8,128)(2,1)} collective-permute-done((bf16[32,4096]{1,0:T(8,128)(2,1)}, bf16[32,4096]{1,0:T(8,128)(2,1)}, u32[]{:S(2)}, u32[]{:S(2)}) %collective-permute-start.16) | collective-permute-done | bytes 262176 | tf_op jit(solution)/shard_map/ppermute | solution.py:223
  113.6 11.1 %expert.3 = (bf16[32,4096]{1,0:T(8,128)(2,1)}, bf16[32,4096]{1,0:T(8,128)(2,1)}, bf16[32,4096]{1,0:T(8,128)(2,1)}, bf16[32,4096]{1,0:T(8,128)(2,1)}, bf16[32,409...) custom-call(bf16[32,4096]{1,0:T(8,128)(2,1)} %get-tuple-element.124., ...), custom_call_target="tpu_custom_call" | custom-call | flops 1024 | bytes 1024 | tf_op jit(solution)/shard_map/expert/pallas_call | solution.py:28
  124.7 4.8 %weight_part.4 = (bf16[16,2176]{1,0:T(8,128)(2,1)}, bf16[496,2176]{1,0:T(8,128)(2,1)}) custom-call(s32[1]{0:T(128)} %bitcast.4.refs_0_, bf16[256,4096]{1,0:T(8,128)(2,1)} %get-tuple-element.138.refs_1_, bf16[256,1408]{1,0:T(8,128)(2,1)} %get-tuple-element.127.refs_2_, bf16[256,704]{1,0:T(8,128)(2,1)} %get-tuple-element.128.refs_3_, ...), custom_call_target="tpu_custom_call" | custom-call | flops 1024 | bytes 1024 | tf_op jit(solution)/shard_map/weight_part/pallas_call | solution.py:28
  129.5 0.1 collective-permute-start.21
  129.6 0.0 collective-permute-done.8.refs_4_
  129.6 1.6 collective-permute-done.21.refs_7_
  131.2 0.2 collective-permute-start.22
  131.4 4.7 %weight_part.5 = bf16[512,2176]{1,0:T(8,128)(2,1)} custom-call(s32[1]{0:T(128)} %bitcast.5.refs_0_, bf16[256,4096]{1,0:T(8,128)(2,1)} %get-tuple-element.138.refs_1_, bf16[256,1408]{1,0:T(8,128)(2,1)} %get-tuple-element.127.refs_2_, bf16[256,704]{1,0:T(8,128)(2,1)} %get-tuple-element.128.refs_3_, bf16[256,4096]{1,0:T(8,128)(2,1)} %get-tuple-element.129.refs_4_, ...), custom_call_target="tpu_custom_call" | custom-call | flops 1024 | bytes 1024 | tf_op jit(solution)/shard_map/weight_part/pallas_call | solution.py:28
  136.1 5.6 %weight_part.6 = (bf16[16,2176]{1,0:T(8,128)(2,1)}, bf16[496,2176]{1,0:T(8,128)(2,1)}) custom-call(s32[1]{0:T(128)} %bitcast.6.refs_0_, bf16[256,4096]{1,0:T(8,128)(2,1)} %get-tuple-element.138.refs_1_, bf16[256,1408]{1,0:T(8,128)(2,1)} %get-tuple-element.127.refs_2_, bf16[256,704]{1,0:T(8,128)(2,1)} %get-tuple-element.128.refs_3_, ...), custom_call_target="tpu_custom_call" | custom-call | flops 1024 | bytes 1024 | tf_op jit(solution)/shard_map/weight_part/pallas_call | solution.py:28
  141.7 1.0 collective-permute-start.24
  142.7 0.1 collective-permute-start.23
  142.8 0.8 collective-permute-done.18.refs_8_
  143.7 2.9 %collective-permute-done.24.refs_8_ = bf16[16,2176]{1,0:T(8,128)(2,1)} collective-permute-done((bf16[16,2176]{1,0:T(8,128)(2,1)}, bf16[16,2176]{1,0:T(8,128)(2,1)}, u32[]{:S(2)}, u32[]{:S(2)}) %collective-permute-start.24) | collective-permute-done | bytes 69664 | tf_op jit(solution)/shard_map/ppermute | solution.py:223
  146.5 0.9 collective-permute-start.25
  147.5 0.9 collective-permute-start.19
  148.4 4.3 %collective-permute-start.20 = (bf16[32,4096]{1,0:T(8,128)(2,1)}, bf16[32,4096]{1,0:T(8,128)(2,1)}, u32[]{:S(2)}, u32[]{:S(2)}) collective-permute-start(bf16[32,4096]{1,0:T(8,128)(2,1)} %get-tuple-element.121), channel_id=1, source_target_pairs={{0,4},{1,5},{2,6},{3,7},{4,0},{5,1},{6,2},{7,3},{8,12},{9,13},{10,... | collective-permute-start | bytes 786440 | tf_op jit(solution)/shard_map/ppermute | solution.py:223
  152.6 0.0 collective-permute-start.27
  152.6 4.4 %collective-permute-done.19.refs_9_ = bf16[32,4096]{1,0:T(8,128)(2,1)} collective-permute-done((bf16[32,4096]{1,0:T(8,128)(2,1)}, bf16[32,4096]{1,0:T(8,128)(2,1)}, u32[]{:S(2)}, u32[]{:S(2)}) %collective-permute-start.19) | collective-permute-done | bytes 262176 | tf_op jit(solution)/shard_map/ppermute | solution.py:223
  157.1 13.0 %collective-permute-start.26 = (bf16[32,4096]{1,0:T(8,128)(2,1)}, bf16[32,4096]{1,0:T(8,128)(2,1)}, u32[]{:S(2)}, u32[]{:S(2)}) collective-permute-start(bf16[32,4096]{1,0:T(8,128)(2,1)} %get-tuple-element.144), channel_id=1, source_target_pairs={{0,5},{1,4},{2,3},{3,2},{4,1},{5,0},{6,7},{7,6},{8,13},{9,12},{10,... | collective-permute-start | bytes 786440 | tf_op jit(solution)/shard_map/ppermute | solution.py:223
  170.1 5.9 %collective-permute-done.20.refs_10_ = bf16[32,4096]{1,0:T(8,128)(2,1)} collective-permute-done((bf16[32,4096]{1,0:T(8,128)(2,1)}, bf16[32,4096]{1,0:T(8,128)(2,1)}, u32[]{:S(2)}, u32[]{:S(2)}) %collective-permute-start.20) | collective-permute-done | bytes 262176 | tf_op jit(solution)/shard_map/ppermute | solution.py:223
  176.0 0.0 collective-permute-start.28
  176.0 7.5 %collective-permute-start.29 = (bf16[32,4096]{1,0:T(8,128)(2,1)}, bf16[32,4096]{1,0:T(8,128)(2,1)}, u32[]{:S(2)}, u32[]{:S(2)}) collective-permute-start(bf16[32,4096]{1,0:T(8,128)(2,1)} %get-tuple-element.150), channel_id=1, source_target_pairs={{0,2},{1,7},{2,0},{3,5},{4,6},{5,3},{6,4},{7,1},{8,10},{9,15},{10,... | collective-permute-start | bytes 786440 | tf_op jit(solution)/shard_map/ppermute | solution.py:223
  183.5 3.6 %combine.2 = (bf16[256,2048]{1,0:T(8,128)(2,1)}, bf16[256,2048]{1,0:T(8,128)(2,1)}) custom-call(s32[1,256]{1,0:T(1,128)} %bitcast.15, bf16[256,2048]{1,0:T(8,128)(2,1)} %refs_1_.5, bf16[256,2048]{1,0:T(8,128)(2,1)} %refs_2_.5, bf16[32,4096]{1,0:T(8,128)(2,1)} %get-tuple-element.93.refs_3_, bf16[32,4096]{1,0:T(8,128)(2,1)} %collective-permute-done.8.refs_4_, ...), custom_call_target="tpu_custom_call" | custom-call | flops 1024 | bytes 1024 | tf_op jit(solution)/shard_map/combine/pallas_call | solution.py:28
  187.2 0.0 collective-permute-done.26.refs_4_
  187.2 0.1 collective-permute-start.31
  187.3 4.5 %collective-permute-start.30 = (bf16[32,4096]{1,0:T(8,128)(2,1)}, bf16[32,4096]{1,0:T(8,128)(2,1)}, u32[]{:S(2)}, u32[]{:S(2)}) collective-permute-start(bf16[32,4096]{1,0:T(8,128)(2,1)} %get-tuple-element.152), channel_id=1, source_target_pairs={{0,7},{1,2},{2,1},{3,4},{4,3},{5,6},{6,5},{7,0},{8,15},{9,10},{10,... | collective-permute-start | bytes 786440 | tf_op jit(solution)/shard_map/ppermute | solution.py:223
  191.8 3.0 %collective-permute-done.29.refs_7_ = bf16[32,4096]{1,0:T(8,128)(2,1)} collective-permute-done((bf16[32,4096]{1,0:T(8,128)(2,1)}, bf16[32,4096]{1,0:T(8,128)(2,1)}, u32[]{:S(2)}, u32[]{:S(2)}) %collective-permute-start.29) | collective-permute-done | bytes 262176 | tf_op jit(solution)/shard_map/ppermute | solution.py:223
  194.8 0.3 collective-permute-start.32
  195.1 0.1 collective-permute-done.25.refs_9_
  195.3 6.7 %weight_part.7 = (f32[512,1408]{1,0:T(8,128)}, f32[704,512]{1,0:T(8,128)}) custom-call(s32[1]{0:T(128)} %bitcast.3.refs_0_, bf16[256,4096]{1,0:T(8,128)(2,1)} %get-tuple-element.138.refs_1_, bf16[256,1408]{1,0:T(8,128)(2,1)} %get-tuple-element.127.refs_2_, bf16[256,704]{1,0:T(8,128)(2,1)} %get-tuple-element.128.refs_3_, ...), custom_call_target="tpu_custom_call" | custom-call | flops 1024 | bytes 1024 | tf_op jit(solution)/shard_map/weight_part/pallas_call | solution.py:28
  202.0 4.7 %collective-permute-done.30.refs_8_ = bf16[32,4096]{1,0:T(8,128)(2,1)} collective-permute-done((bf16[32,4096]{1,0:T(8,128)(2,1)}, bf16[32,4096]{1,0:T(8,128)(2,1)}, u32[]{:S(2)}, u32[]{:S(2)}) %collective-permute-start.30) | collective-permute-done | bytes 262176 | tf_op jit(solution)/shard_map/ppermute | solution.py:223
  206.7 7.4 %collective-permute-done.32.refs_10_ = bf16[32,4096]{1,0:T(8,128)(2,1)} collective-permute-done((bf16[32,4096]{1,0:T(8,128)(2,1)}, bf16[32,4096]{1,0:T(8,128)(2,1)}, u32[]{:S(2)}, u32[]{:S(2)}) %collective-permute-start.32) | collective-permute-done | bytes 262176 | tf_op jit(solution)/shard_map/ppermute | solution.py:223
  214.0 3.6 %combine.3 = (bf16[256,2048]{1,0:T(8,128)(2,1)}, bf16[256,2048]{1,0:T(8,128)(2,1)}) custom-call(s32[1,256]{1,0:T(1,128)} %bitcast.16, bf16[256,2048]{1,0:T(8,128)(2,1)} %get-tuple-element.122.refs_1_, bf16[256,2048]{1,0:T(8,128)(2,1)} %get-tuple-element.123.refs_2_, bf16[32,4096]{1,0:T(8,128)(2,1)} %get-tuple-element.142.refs_3_, ...), custom_call_target="tpu_custom_call" | custom-call | flops 1024 | bytes 1024 | tf_op jit(solution)/shard_map/combine/pallas_call | solution.py:28
  (12 shorter events, 0.0 us)
Async XLA Ops:
  4.1 18.2 %collective-permute-start = (bf16[32,4096]{1,0:T(8,128)(2,1)}, bf16[32,4096]{1,0:T(8,128)(2,1)}, u32[]{:S(2)}, u32[]{:S(2)}) collective-permute-start(bf16[32,4096]{1,0:T(8,128)(2,1)} %get-tuple-element.83), channel_id=1, source_target_pairs={{0,5},{1,4},{2,3},{3,2},{4,1},{5,0},{6,7},{7,6},{8,13},{9,12},{10,... | collective-permute-start | bytes 786440 | tf_op jit(solution)/shard_map/ppermute | solution.py:223
  9.1 13.1 %collective-permute-start.1 = (bf16[32,4096]{1,0:T(8,128)(2,1)}, bf16[32,4096]{1,0:T(8,128)(2,1)}, u32[]{:S(2)}, u32[]{:S(2)}) collective-permute-start(bf16[32,4096]{1,0:T(8,128)(2,1)} %get-tuple-element.84), channel_id=1, source_target_pairs={{0,1},{1,0},{2,7},{3,6},{4,5},{5,4},{6,3},{7,2},{8,9},{9,8},{10,15... | collective-permute-start | bytes 786440 | tf_op jit(solution)/shard_map/ppermute | solution.py:223
  9.6 23.0 %collective-permute-start.2 = (bf16[32,4096]{1,0:T(8,128)(2,1)}, bf16[32,4096]{1,0:T(8,128)(2,1)}, u32[]{:S(2)}, u32[]{:S(2)}) collective-permute-start(bf16[32,4096]{1,0:T(8,128)(2,1)} %get-tuple-element.85), channel_id=1, source_target_pairs={{0,6},{1,3},{2,4},{3,1},{4,2},{5,7},{6,0},{7,5},{8,14},{9,11},{10,... | collective-permute-start | bytes 786440 | tf_op jit(solution)/shard_map/ppermute | solution.py:223
  11.0 30.0 %collective-permute-start.3 = (bf16[32,4096]{1,0:T(8,128)(2,1)}, bf16[32,4096]{1,0:T(8,128)(2,1)}, u32[]{:S(2)}, u32[]{:S(2)}) collective-permute-start(bf16[32,4096]{1,0:T(8,128)(2,1)} %get-tuple-element.86), channel_id=1, source_target_pairs={{0,2},{1,7},{2,0},{3,5},{4,6},{5,3},{6,4},{7,1},{8,10},{9,15},{10,... | collective-permute-start | bytes 786440 | tf_op jit(solution)/shard_map/ppermute | solution.py:223
  22.2 18.8 %collective-permute-start.4 = (bf16[32,4096]{1,0:T(8,128)(2,1)}, bf16[32,4096]{1,0:T(8,128)(2,1)}, u32[]{:S(2)}, u32[]{:S(2)}) collective-permute-start(bf16[32,4096]{1,0:T(8,128)(2,1)} %get-tuple-element.88), channel_id=1, source_target_pairs={{0,7},{1,2},{2,1},{3,4},{4,3},{5,6},{6,5},{7,0},{8,15},{9,10},{10,... | collective-permute-start | bytes 786440 | tf_op jit(solution)/shard_map/ppermute | solution.py:223
  22.2 20.4 %collective-permute-start.5 = (bf16[32,4096]{1,0:T(8,128)(2,1)}, bf16[32,4096]{1,0:T(8,128)(2,1)}, u32[]{:S(2)}, u32[]{:S(2)}) collective-permute-start(bf16[32,4096]{1,0:T(8,128)(2,1)} %get-tuple-element.90), channel_id=1, source_target_pairs={{0,3},{1,6},{2,5},{3,0},{4,7},{5,2},{6,1},{7,4},{8,11},{9,14},{10,... | collective-permute-start | bytes 786440 | tf_op jit(solution)/shard_map/ppermute | solution.py:223
  32.7 25.6 %collective-permute-start.6 = (bf16[32,4096]{1,0:T(8,128)(2,1)}, bf16[32,4096]{1,0:T(8,128)(2,1)}, u32[]{:S(2)}, u32[]{:S(2)}) collective-permute-start(bf16[32,4096]{1,0:T(8,128)(2,1)} %get-tuple-element.92), channel_id=1, source_target_pairs={{0,4},{1,5},{2,6},{3,7},{4,0},{5,1},{6,2},{7,3},{8,12},{9,13},{10,... | collective-permute-start | bytes 786440 | tf_op jit(solution)/shard_map/ppermute | solution.py:223
  41.0 34.7 %collective-permute-start.9 = (bf16[32,4096]{1,0:T(8,128)(2,1)}, bf16[32,4096]{1,0:T(8,128)(2,1)}, u32[]{:S(2)}, u32[]{:S(2)}) collective-permute-start(bf16[32,4096]{1,0:T(8,128)(2,1)} %get-tuple-element.101), channel_id=1, source_target_pairs={{0,5},{1,4},{2,3},{3,2},{4,1},{5,0},{6,7},{7,6},{8,13},{9,12},{10,... | collective-permute-start | bytes 786440 | tf_op jit(solution)/shard_map/ppermute | solution.py:223
  41.0 34.7 %collective-permute-start.12 = (bf16[32,4096]{1,0:T(8,128)(2,1)}, bf16[32,4096]{1,0:T(8,128)(2,1)}, u32[]{:S(2)}, u32[]{:S(2)}) collective-permute-start(bf16[32,4096]{1,0:T(8,128)(2,1)} %get-tuple-element.107), channel_id=1, source_target_pairs={{0,1},{1,0},{2,7},{3,6},{4,5},{5,4},{6,3},{7,2},{8,9},{9,8},{10,15... | collective-permute-start | bytes 786440 | tf_op jit(solution)/shard_map/ppermute | solution.py:223
  42.7 43.9 %collective-permute-start.15 = (bf16[32,4096]{1,0:T(8,128)(2,1)}, bf16[32,4096]{1,0:T(8,128)(2,1)}, u32[]{:S(2)}, u32[]{:S(2)}) collective-permute-start(bf16[32,4096]{1,0:T(8,128)(2,1)} %get-tuple-element.113), channel_id=1, source_target_pairs={{0,6},{1,3},{2,4},{3,1},{4,2},{5,7},{6,0},{7,5},{8,14},{9,11},{10,... | collective-permute-start | bytes 786440 | tf_op jit(solution)/shard_map/ppermute | solution.py:223
  58.3 33.7 %collective-permute-start.7 = (bf16[32,4096]{1,0:T(8,128)(2,1)}, bf16[32,4096]{1,0:T(8,128)(2,1)}, u32[]{:S(2)}, u32[]{:S(2)}) collective-permute-start(bf16[32,4096]{1,0:T(8,128)(2,1)} %get-tuple-element.96), channel_id=1, source_target_pairs={{0,2},{1,7},{2,0},{3,5},{4,6},{5,3},{6,4},{7,1},{8,10},{9,15},{10,... | collective-permute-start | bytes 786440 | tf_op jit(solution)/shard_map/ppermute | solution.py:223
  75.7 16.3 %collective-permute-start.10 = (bf16[32,4096]{1,0:T(8,128)(2,1)}, bf16[32,4096]{1,0:T(8,128)(2,1)}, u32[]{:S(2)}, u32[]{:S(2)}) collective-permute-start(bf16[32,4096]{1,0:T(8,128)(2,1)} %get-tuple-element.102), channel_id=1, source_target_pairs={{0,7},{1,2},{2,1},{3,4},{4,3},{5,6},{6,5},{7,0},{8,15},{9,10},{10,... | collective-permute-start | bytes 786440 | tf_op jit(solution)/shard_map/ppermute | solution.py:223
  75.7 23.9 %collective-permute-start.13 = (bf16[32,4096]{1,0:T(8,128)(2,1)}, bf16[32,4096]{1,0:T(8,128)(2,1)}, u32[]{:S(2)}, u32[]{:S(2)}) collective-permute-start(bf16[32,4096]{1,0:T(8,128)(2,1)} %get-tuple-element.108), channel_id=1, source_target_pairs={{0,3},{1,6},{2,5},{3,0},{4,7},{5,2},{6,1},{7,4},{8,11},{9,14},{10,... | collective-permute-start | bytes 786440 | tf_op jit(solution)/shard_map/ppermute | solution.py:223
  86.6 27.0 %collective-permute-start.16 = (bf16[32,4096]{1,0:T(8,128)(2,1)}, bf16[32,4096]{1,0:T(8,128)(2,1)}, u32[]{:S(2)}, u32[]{:S(2)}) collective-permute-start(bf16[32,4096]{1,0:T(8,128)(2,1)} %get-tuple-element.114), channel_id=1, source_target_pairs={{0,4},{1,5},{2,6},{3,7},{4,0},{5,1},{6,2},{7,3},{8,12},{9,13},{10,... | collective-permute-start | bytes 786440 | tf_op jit(solution)/shard_map/ppermute | solution.py:223
  92.0 37.7 %collective-permute-start.11 = (bf16[32,4096]{1,0:T(8,128)(2,1)}, bf16[32,4096]{1,0:T(8,128)(2,1)}, u32[]{:S(2)}, u32[]{:S(2)}) collective-permute-start(bf16[32,4096]{1,0:T(8,128)(2,1)} %get-tuple-element.103), channel_id=1, source_target_pairs={{0,1},{1,0},{2,7},{3,6},{4,5},{5,4},{6,3},{7,2},{8,9},{9,8},{10,15... | collective-permute-start | bytes 786440 | tf_op jit(solution)/shard_map/ppermute | solution.py:223
  92.0 37.7 %collective-permute-start.8 = (bf16[32,4096]{1,0:T(8,128)(2,1)}, bf16[32,4096]{1,0:T(8,128)(2,1)}, u32[]{:S(2)}, u32[]{:S(2)}) collective-permute-start(bf16[32,4096]{1,0:T(8,128)(2,1)} %get-tuple-element.97), channel_id=1, source_target_pairs={{0,5},{1,4},{2,3},{3,2},{4,1},{5,0},{6,7},{7,6},{8,13},{9,12},{10,... | collective-permute-start | bytes 786440 | tf_op jit(solution)/shard_map/ppermute | solution.py:223
  99.6 31.6 %collective-permute-start.14 = (bf16[32,4096]{1,0:T(8,128)(2,1)}, bf16[32,4096]{1,0:T(8,128)(2,1)}, u32[]{:S(2)}, u32[]{:S(2)}) collective-permute-start(bf16[32,4096]{1,0:T(8,128)(2,1)} %get-tuple-element.109), channel_id=1, source_target_pairs={{0,6},{1,3},{2,4},{3,1},{4,2},{5,7},{6,0},{7,5},{8,14},{9,11},{10,... | collective-permute-start | bytes 786440 | tf_op jit(solution)/shard_map/ppermute | solution.py:223
  129.5 1.7 collective-permute-start.21
  131.2 4.9 %collective-permute-start.22 = (bf16[496,2176]{1,0:T(8,128)(2,1)}, bf16[496,2176]{1,0:T(8,128)(2,1)}, u32[]{:S(2)}, u32[]{:S(2)}) collective-permute-start(bf16[496,2176]{1,0:T(8,128)(2,1)} %get-tuple-element.136), channel_id=1, source_target_pairs={{0,8},{8,0},{16,24},{24,16},{1,9},{9,1},{17,25},{25,17},{2,10},{10... | collective-permute-start | bytes 6475784 | tf_op jit(solution)/shard_map/ppermute | solution.py:223
  131.4 11.4 %collective-permute-start.17 = (bf16[32,4096]{1,0:T(8,128)(2,1)}, bf16[32,4096]{1,0:T(8,128)(2,1)}, u32[]{:S(2)}, u32[]{:S(2)}) collective-permute-start(bf16[32,4096]{1,0:T(8,128)(2,1)} %get-tuple-element.115), channel_id=1, source_target_pairs={{0,2},{1,7},{2,0},{3,5},{4,6},{5,3},{6,4},{7,1},{8,10},{9,15},{10,... | collective-permute-start | bytes 786440 | tf_op jit(solution)/shard_map/ppermute | solution.py:223
  131.4 12.3 %collective-permute-start.18 = (bf16[32,4096]{1,0:T(8,128)(2,1)}, bf16[32,4096]{1,0:T(8,128)(2,1)}, u32[]{:S(2)}, u32[]{:S(2)}) collective-permute-start(bf16[32,4096]{1,0:T(8,128)(2,1)} %get-tuple-element.117), channel_id=1, source_target_pairs={{0,7},{1,2},{2,1},{3,4},{4,3},{5,6},{6,5},{7,0},{8,15},{9,10},{10,... | collective-permute-start | bytes 786440 | tf_op jit(solution)/shard_map/ppermute | solution.py:223
  141.7 4.8 %collective-permute-start.24 = (bf16[16,2176]{1,0:T(8,128)(2,1)}, bf16[16,2176]{1,0:T(8,128)(2,1)}, u32[]{:S(2)}, u32[]{:S(2)}) collective-permute-start(bf16[16,2176]{1,0:T(8,128)(2,1)} %get-tuple-element.137), channel_id=1, source_target_pairs={{0,16},{8,24},{16,0},{24,8},{1,17},{9,25},{17,1},{25,9},{2,18},{10... | collective-permute-start | bytes 208904 | tf_op jit(solution)/shard_map/ppermute | solution.py:223
  142.7 52.4 %collective-permute-start.23 = (bf16[512,2176]{1,0:T(8,128)(2,1)}, bf16[512,2176]{1,0:T(8,128)(2,1)}, u32[]{:S(2)}, u32[]{:S(2)}) collective-permute-start(bf16[512,2176]{1,0:T(8,128)(2,1)} %weight_part.5), channel_id=1, source_target_pairs={{0,8},{8,0},{16,24},{24,16},{1,9},{9,1},{17,25},{25,17},{2,10},{10... | collective-permute-start | bytes 6684680 | tf_op jit(solution)/shard_map/ppermute | solution.py:223
  146.5 48.7 %collective-permute-start.25 = (bf16[496,2176]{1,0:T(8,128)(2,1)}, bf16[496,2176]{1,0:T(8,128)(2,1)}, u32[]{:S(2)}, u32[]{:S(2)}) collective-permute-start(bf16[496,2176]{1,0:T(8,128)(2,1)} %get-tuple-element.140), channel_id=1, source_target_pairs={{0,16},{8,24},{16,0},{24,8},{1,17},{9,25},{17,1},{25,9},{2,18},{10... | collective-permute-start | bytes 6475784 | tf_op jit(solution)/shard_map/ppermute | solution.py:223
  147.5 9.6 %collective-permute-start.19 = (bf16[32,4096]{1,0:T(8,128)(2,1)}, bf16[32,4096]{1,0:T(8,128)(2,1)}, u32[]{:S(2)}, u32[]{:S(2)}) collective-permute-start(bf16[32,4096]{1,0:T(8,128)(2,1)} %get-tuple-element.119), channel_id=1, source_target_pairs={{0,3},{1,6},{2,5},{3,0},{4,7},{5,2},{6,1},{7,4},{8,11},{9,14},{10,... | collective-permute-start | bytes 786440 | tf_op jit(solution)/shard_map/ppermute | solution.py:223
  148.4 27.6 %collective-permute-start.20 = (bf16[32,4096]{1,0:T(8,128)(2,1)}, bf16[32,4096]{1,0:T(8,128)(2,1)}, u32[]{:S(2)}, u32[]{:S(2)}) collective-permute-start(bf16[32,4096]{1,0:T(8,128)(2,1)} %get-tuple-element.121), channel_id=1, source_target_pairs={{0,4},{1,5},{2,6},{3,7},{4,0},{5,1},{6,2},{7,3},{8,12},{9,13},{10,... | collective-permute-start | bytes 786440 | tf_op jit(solution)/shard_map/ppermute | solution.py:223
  152.6 23.3 %collective-permute-start.27 = (bf16[32,4096]{1,0:T(8,128)(2,1)}, bf16[32,4096]{1,0:T(8,128)(2,1)}, u32[]{:S(2)}, u32[]{:S(2)}) collective-permute-start(bf16[32,4096]{1,0:T(8,128)(2,1)} %get-tuple-element.146), channel_id=1, source_target_pairs={{0,1},{1,0},{2,7},{3,6},{4,5},{5,4},{6,3},{7,2},{8,9},{9,8},{10,15... | collective-permute-start | bytes 786440 | tf_op jit(solution)/shard_map/ppermute | solution.py:223
  157.1 30.1 %collective-permute-start.26 = (bf16[32,4096]{1,0:T(8,128)(2,1)}, bf16[32,4096]{1,0:T(8,128)(2,1)}, u32[]{:S(2)}, u32[]{:S(2)}) collective-permute-start(bf16[32,4096]{1,0:T(8,128)(2,1)} %get-tuple-element.144), channel_id=1, source_target_pairs={{0,5},{1,4},{2,3},{3,2},{4,1},{5,0},{6,7},{7,6},{8,13},{9,12},{10,... | collective-permute-start | bytes 786440 | tf_op jit(solution)/shard_map/ppermute | solution.py:223
  176.0 11.3 %collective-permute-start.28 = (bf16[32,4096]{1,0:T(8,128)(2,1)}, bf16[32,4096]{1,0:T(8,128)(2,1)}, u32[]{:S(2)}, u32[]{:S(2)}) collective-permute-start(bf16[32,4096]{1,0:T(8,128)(2,1)} %get-tuple-element.148), channel_id=1, source_target_pairs={{0,6},{1,3},{2,4},{3,1},{4,2},{5,7},{6,0},{7,5},{8,14},{9,11},{10,... | collective-permute-start | bytes 786440 | tf_op jit(solution)/shard_map/ppermute | solution.py:223
  176.0 18.8 %collective-permute-start.29 = (bf16[32,4096]{1,0:T(8,128)(2,1)}, bf16[32,4096]{1,0:T(8,128)(2,1)}, u32[]{:S(2)}, u32[]{:S(2)}) collective-permute-start(bf16[32,4096]{1,0:T(8,128)(2,1)} %get-tuple-element.150), channel_id=1, source_target_pairs={{0,2},{1,7},{2,0},{3,5},{4,6},{5,3},{6,4},{7,1},{8,10},{9,15},{10,... | collective-permute-start | bytes 786440 | tf_op jit(solution)/shard_map/ppermute | solution.py:223
  187.2 14.8 %collective-permute-start.31 = (bf16[32,4096]{1,0:T(8,128)(2,1)}, bf16[32,4096]{1,0:T(8,128)(2,1)}, u32[]{:S(2)}, u32[]{:S(2)}) collective-permute-start(bf16[32,4096]{1,0:T(8,128)(2,1)} %get-tuple-element.154), channel_id=1, source_target_pairs={{0,3},{1,6},{2,5},{3,0},{4,7},{5,2},{6,1},{7,4},{8,11},{9,14},{10,... | collective-permute-start | bytes 786440 | tf_op jit(solution)/shard_map/ppermute | solution.py:223
  187.3 19.4 %collective-permute-start.30 = (bf16[32,4096]{1,0:T(8,128)(2,1)}, bf16[32,4096]{1,0:T(8,128)(2,1)}, u32[]{:S(2)}, u32[]{:S(2)}) collective-permute-start(bf16[32,4096]{1,0:T(8,128)(2,1)} %get-tuple-element.152), channel_id=1, source_target_pairs={{0,7},{1,2},{2,1},{3,4},{4,3},{5,6},{6,5},{7,0},{8,15},{9,10},{10,... | collective-permute-start | bytes 786440 | tf_op jit(solution)/shard_map/ppermute | solution.py:223
  194.8 19.2 %collective-permute-start.32 = (bf16[32,4096]{1,0:T(8,128)(2,1)}, bf16[32,4096]{1,0:T(8,128)(2,1)}, u32[]{:S(2)}, u32[]{:S(2)}) collective-permute-start(bf16[32,4096]{1,0:T(8,128)(2,1)} %get-tuple-element.156), channel_id=1, source_target_pairs={{0,4},{1,5},{2,6},{3,7},{4,0},{5,1},{6,2},{7,3},{8,12},{9,13},{10,... | collective-permute-start | bytes 786440 | tf_op jit(solution)/shard_map/ppermute | solution.py:223

commit v10 on v9

--- a/solution.py
+++ b/solution.py
@@ -346,7 +346,7 @@
 
     received = {q: [] for q in range(groups)}
     sums = kept[0][0]
-    held = {groups - 1: done[:3], 2: done[3:5]}
+    held = {groups - 1: done[:4], 2: done[4:6]}
     for q in sorted(range(1, groups), key=lambda q: (q & -q, -q)):
         low = q & -q
         sent = weight_part(group ^ q, [[sums, *kept[0][1:]], *kept[1:]], received[q], False, 16 if q in held else 0)

time: 218 us -> 216 us (level)
  starting transfers between devices: 95.4 us -> 83.9 us
  waiting for transfers between devices: 63.5 us -> 72.8 us
    ppermute x33, starting transfers between devices: 95.4 us -> 83.9 us  [send(): self.done.append(lax.ppermute(after(value, *earlier), axis, pairs))]
    ppermute x33, waiting for transfers between devices: 63.5 us -> 72.8 us  [send(): self.done.append(lax.ppermute(after(value, *earlier), axis, pairs))]
  transfers between devices with their start and end apart: 33 -> 33, of which waited for: 12 -> 10; matrix products, arithmetic and copies ran while one was open for 0% -> 0% of each run, Pallas kernels for 23% -> 24%
where the time goes in v10:
time: 216 us
  starting transfers between devices  83.9 us (39%)
  waiting for transfers between devices  72.8 us (34%)
  Pallas kernels  57.9 us (27%)
    ppermute x33, starting transfers between devices, send(): self.done.append(lax.ppermute(after(value, *earlier), axis, pairs))  83.9 us
    ppermute x33, waiting for transfers between devices, send(): self.done.append(lax.ppermute(after(value, *earlier), axis, pairs))  72.8 us
    pallas_call x10, Pallas kernels, call(): pl.pallas_call(kernel, in_specs=[pl.BlockSpec(memory_space=pltpu.SMEM)] *...  57.9 us
  transfers between devices with their start and end apart: 33, of which 10 were waited for; matrix products, arithmetic and copies ran while one was open for 0% of the time, Pallas kernels for 24%

profile of v10, /device:TPU:0, one launch (start us, length us, event | category | flops | bytes accessed | tf_op | source)
XLA Modules:
  0.0 215.7 jit_solution(10102839359642298349)
XLA Ops:
  0.6 3.4 %place.2 = (bf16[32,4096]{1,0:T(8,128)(2,1)}, bf16[32,4096]{1,0:T(8,128)(2,1)}, bf16[32,4096]{1,0:T(8,128)(2,1)}, bf16[32,4096]{1,0:T(8,128)(2,1)}, bf16[32,4096...) custom-call(s32[1,256]{1,0:T(1,128)} %bitcast.13, ...), custom_call_target="tpu_custom_call" | custom-call | flops 1024 | bytes 1024 | tf_op jit(solution)/shard_map/place/pallas_call | solution.py:28
  4.1 5.1 %collective-permute-start = (bf16[32,4096]{1,0:T(8,128)(2,1)}, bf16[32,4096]{1,0:T(8,128)(2,1)}, u32[]{:S(2)}, u32[]{:S(2)}) collective-permute-start(bf16[32,4096]{1,0:T(8,128)(2,1)} %get-tuple-element.83), channel_id=1, source_target_pairs={{0,5},{1,4},{2,3},{3,2},{4,1},{5,0},{6,7},{7,6},{8,13},{9,12},{10,... | collective-permute-start | bytes 786440 | tf_op jit(solution)/shard_map/ppermute | solution.py:223
  9.1 0.5 collective-permute-start.1
  9.6 1.3 collective-permute-start.2
  11.0 0.2 collective-permute-start.3
  11.2 11.0 %collective-permute-done.refs_1_ = bf16[32,4096]{1,0:T(8,128)(2,1)} collective-permute-done((bf16[32,4096]{1,0:T(8,128)(2,1)}, bf16[32,4096]{1,0:T(8,128)(2,1)}, u32[]{:S(2)}, u32[]{:S(2)}) %collective-permute-start) | collective-permute-done | bytes 262176 | tf_op jit(solution)/shard_map/ppermute | solution.py:223
  22.2 0.0 collective-permute-start.4
  22.2 7.0 %collective-permute-start.5 = (bf16[32,4096]{1,0:T(8,128)(2,1)}, bf16[32,4096]{1,0:T(8,128)(2,1)}, u32[]{:S(2)}, u32[]{:S(2)}) collective-permute-start(bf16[32,4096]{1,0:T(8,128)(2,1)} %get-tuple-element.90), channel_id=1, source_target_pairs={{0,3},{1,6},{2,5},{3,0},{4,7},{5,2},{6,1},{7,4},{8,11},{9,14},{10,... | collective-permute-start | bytes 786440 | tf_op jit(solution)/shard_map/ppermute | solution.py:223
  29.2 3.4 %place.3 = (bf16[32,4096]{1,0:T(8,128)(2,1)}, bf16[32,4096]{1,0:T(8,128)(2,1)}, bf16[32,4096]{1,0:T(8,128)(2,1)}, bf16[32,4096]{1,0:T(8,128)(2,1)}, bf16[32,4096...) custom-call(s32[1,256]{1,0:T(1,128)} %bitcast.14, ...), custom_call_target="tpu_custom_call" | custom-call | flops 1024 | bytes 1024 | tf_op jit(solution)/shard_map/place/pallas_call | solution.py:28
  32.7 8.3 %collective-permute-start.6 = (bf16[32,4096]{1,0:T(8,128)(2,1)}, bf16[32,4096]{1,0:T(8,128)(2,1)}, u32[]{:S(2)}, u32[]{:S(2)}) collective-permute-start(bf16[32,4096]{1,0:T(8,128)(2,1)} %get-tuple-element.92), channel_id=1, source_target_pairs={{0,4},{1,5},{2,6},{3,7},{4,0},{5,1},{6,2},{7,3},{8,12},{9,13},{10,... | collective-permute-start | bytes 786440 | tf_op jit(solution)/shard_map/ppermute | solution.py:223
  41.0 0.0 collective-permute-done.3.refs_4_
  41.0 0.0 collective-permute-start.9
  41.0 0.0 collective-permute-done.4.refs_5_
  41.0 1.7 collective-permute-start.12
  42.7 0.0 collective-permute-done.5.refs_6_
  42.7 15.6 %collective-permute-start.15 = (bf16[32,4096]{1,0:T(8,128)(2,1)}, bf16[32,4096]{1,0:T(8,128)(2,1)}, u32[]{:S(2)}, u32[]{:S(2)}) collective-permute-start(bf16[32,4096]{1,0:T(8,128)(2,1)} %get-tuple-element.113), channel_id=1, source_target_pairs={{0,6},{1,3},{2,4},{3,1},{4,2},{5,7},{6,0},{7,5},{8,14},{9,11},{10,... | collective-permute-start | bytes 786440 | tf_op jit(solution)/shard_map/ppermute | solution.py:223
  58.3 0.0 collective-permute-done.6.refs_7_
  58.3 8.9 %collective-permute-start.7 = (bf16[32,4096]{1,0:T(8,128)(2,1)}, bf16[32,4096]{1,0:T(8,128)(2,1)}, u32[]{:S(2)}, u32[]{:S(2)}) collective-permute-start(bf16[32,4096]{1,0:T(8,128)(2,1)} %get-tuple-element.96), channel_id=1, source_target_pairs={{0,2},{1,7},{2,0},{3,5},{4,6},{5,3},{6,4},{7,1},{8,10},{9,15},{10,... | collective-permute-start | bytes 786440 | tf_op jit(solution)/shard_map/ppermute | solution.py:223
  67.2 8.5 %collective-permute-done.9.refs_1_ = bf16[32,4096]{1,0:T(8,128)(2,1)} collective-permute-done((bf16[32,4096]{1,0:T(8,128)(2,1)}, bf16[32,4096]{1,0:T(8,128)(2,1)}, u32[]{:S(2)}, u32[]{:S(2)}) %collective-permute-start.9) | collective-permute-done | bytes 262176 | tf_op jit(solution)/shard_map/ppermute | solution.py:223
  75.7 10.9 %expert.2 = (bf16[32,4096]{1,0:T(8,128)(2,1)}, bf16[32,4096]{1,0:T(8,128)(2,1)}, bf16[32,4096]{1,0:T(8,128)(2,1)}, bf16[32,4096]{1,0:T(8,128)(2,1)}, bf16[32,409...) custom-call(bf16[32,4096]{1,0:T(8,128)(2,1)} %get-tuple-element.82.r, ...), custom_call_target="tpu_custom_call" | custom-call | flops 1024 | bytes 1024 | tf_op jit(solution)/shard_map/expert/pallas_call | solution.py:28
  86.6 0.1 collective-permute-start.13
  86.7 0.0 collective-permute-done.15.refs_3_
  86.7 5.3 %collective-permute-start.16 = (bf16[32,4096]{1,0:T(8,128)(2,1)}, bf16[32,4096]{1,0:T(8,128)(2,1)}, u32[]{:S(2)}, u32[]{:S(2)}) collective-permute-start(bf16[32,4096]{1,0:T(8,128)(2,1)} %get-tuple-element.114), channel_id=1, source_target_pairs={{0,4},{1,5},{2,6},{3,7},{4,0},{5,1},{6,2},{7,3},{8,12},{9,13},{10,... | collective-permute-start | bytes 786440 | tf_op jit(solution)/shard_map/ppermute | solution.py:223
  92.0 0.0 collective-permute-done.7.refs_4_
  92.0 1.5 collective-permute-start.8
  93.5 0.8 collective-permute-done.13.refs_6_
  94.3 16.1 %collective-permute-done.16.refs_7_ = bf16[32,4096]{1,0:T(8,128)(2,1)} collective-permute-done((bf16[32,4096]{1,0:T(8,128)(2,1)}, bf16[32,4096]{1,0:T(8,128)(2,1)}, u32[]{:S(2)}, u32[]{:S(2)}) %collective-permute-start.16) | collective-permute-done | bytes 262176 | tf_op jit(solution)/shard_map/ppermute | solution.py:223
  110.3 0.1 collective-permute-start.17
  110.5 2.9 %collective-permute-start.14 = (bf16[32,4096]{1,0:T(8,128)(2,1)}, bf16[32,4096]{1,0:T(8,128)(2,1)}, u32[]{:S(2)}, u32[]{:S(2)}) collective-permute-start(bf16[32,4096]{1,0:T(8,128)(2,1)} %get-tuple-element.109), channel_id=1, source_target_pairs={{0,6},{1,3},{2,4},{3,1},{4,2},{5,7},{6,0},{7,5},{8,14},{9,11},{10,... | collective-permute-start | bytes 786440 | tf_op jit(solution)/shard_map/ppermute | solution.py:223
  113.3 11.1 %expert.3 = (bf16[32,4096]{1,0:T(8,128)(2,1)}, bf16[32,4096]{1,0:T(8,128)(2,1)}, bf16[32,4096]{1,0:T(8,128)(2,1)}, bf16[32,4096]{1,0:T(8,128)(2,1)}, bf16[32,409...) custom-call(bf16[32,4096]{1,0:T(8,128)(2,1)} %get-tuple-element.124., ...), custom_call_target="tpu_custom_call" | custom-call | flops 1024 | bytes 1024 | tf_op jit(solution)/shard_map/expert/pallas_call | solution.py:28
  124.4 4.8 %weight_part.4 = (bf16[16,2176]{1,0:T(8,128)(2,1)}, bf16[496,2176]{1,0:T(8,128)(2,1)}) custom-call(s32[1]{0:T(128)} %bitcast.4.refs_0_, bf16[256,4096]{1,0:T(8,128)(2,1)} %get-tuple-element.138.refs_1_, bf16[256,1408]{1,0:T(8,128)(2,1)} %get-tuple-element.127.refs_2_, bf16[256,704]{1,0:T(8,128)(2,1)} %get-tuple-element.128.refs_3_, ...), custom_call_target="tpu_custom_call" | custom-call | flops 1024 | bytes 1024 | tf_op jit(solution)/shard_map/weight_part/pallas_call | solution.py:28
  129.2 0.1 collective-permute-start.21
  129.3 0.0 collective-permute-done.8.refs_4_
  129.3 1.6 collective-permute-done.21.refs_7_
  130.9 0.0 collective-permute-done.17.refs_7_
  130.9 0.2 collective-permute-start.22
  131.1 0.0 collective-permute-start.19
  131.1 2.9 %collective-permute-start.18 = (bf16[32,4096]{1,0:T(8,128)(2,1)}, bf16[32,4096]{1,0:T(8,128)(2,1)}, u32[]{:S(2)}, u32[]{:S(2)}) collective-permute-start(bf16[32,4096]{1,0:T(8,128)(2,1)} %get-tuple-element.117), channel_id=1, source_target_pairs={{0,7},{1,2},{2,1},{3,4},{4,3},{5,6},{6,5},{7,0},{8,15},{9,10},{10,... | collective-permute-start | bytes 786440 | tf_op jit(solution)/shard_map/ppermute | solution.py:223
  134.0 4.7 %weight_part.5 = bf16[512,2176]{1,0:T(8,128)(2,1)} custom-call(s32[1]{0:T(128)} %bitcast.5.refs_0_, bf16[256,4096]{1,0:T(8,128)(2,1)} %get-tuple-element.138.refs_1_, bf16[256,1408]{1,0:T(8,128)(2,1)} %get-tuple-element.127.refs_2_, bf16[256,704]{1,0:T(8,128)(2,1)} %get-tuple-element.128.refs_3_, bf16[256,4096]{1,0:T(8,128)(2,1)} %get-tuple-element.129.refs_4_, ...), custom_call_target="tpu_custom_call" | custom-call | flops 1024 | bytes 1024 | tf_op jit(solution)/shard_map/weight_part/pallas_call | solution.py:28
  138.8 0.0 collective-permute-done.22.refs_8_
  138.8 5.6 %weight_part.6 = (bf16[16,2176]{1,0:T(8,128)(2,1)}, bf16[496,2176]{1,0:T(8,128)(2,1)}) custom-call(s32[1]{0:T(128)} %bitcast.6.refs_0_, bf16[256,4096]{1,0:T(8,128)(2,1)} %get-tuple-element.138.refs_1_, bf16[256,1408]{1,0:T(8,128)(2,1)} %get-tuple-element.127.refs_2_, bf16[256,704]{1,0:T(8,128)(2,1)} %get-tuple-element.128.refs_3_, ...), custom_call_target="tpu_custom_call" | custom-call | flops 1024 | bytes 1024 | tf_op jit(solution)/shard_map/weight_part/pallas_call | solution.py:28
  144.4 1.6 collective-permute-start.24
  145.9 1.0 collective-permute-done.18.refs_8_
  147.0 2.1 collective-permute-done.24.refs_8_
  149.1 1.5 collective-permute-start.25
  150.6 1.5 collective-permute-start.20
  152.0 0.0 collective-permute-start.27
  152.0 2.9 %collective-permute-start.26 = (bf16[32,4096]{1,0:T(8,128)(2,1)}, bf16[32,4096]{1,0:T(8,128)(2,1)}, u32[]{:S(2)}, u32[]{:S(2)}) collective-permute-start(bf16[32,4096]{1,0:T(8,128)(2,1)} %get-tuple-element.144), channel_id=1, source_target_pairs={{0,5},{1,4},{2,3},{3,2},{4,1},{5,0},{6,7},{7,6},{8,13},{9,12},{10,... | collective-permute-start | bytes 786440 | tf_op jit(solution)/shard_map/ppermute | solution.py:223
  154.9 15.2 %collective-permute-done.20.refs_10_ = bf16[32,4096]{1,0:T(8,128)(2,1)} collective-permute-done((bf16[32,4096]{1,0:T(8,128)(2,1)}, bf16[32,4096]{1,0:T(8,128)(2,1)}, u32[]{:S(2)}, u32[]{:S(2)}) %collective-permute-start.20) | collective-permute-done | bytes 262176 | tf_op jit(solution)/shard_map/ppermute | solution.py:223
  170.1 2.0 collective-permute-start.28
  172.1 8.5 %collective-permute-start.29 = (bf16[32,4096]{1,0:T(8,128)(2,1)}, bf16[32,4096]{1,0:T(8,128)(2,1)}, u32[]{:S(2)}, u32[]{:S(2)}) collective-permute-start(bf16[32,4096]{1,0:T(8,128)(2,1)} %get-tuple-element.150), channel_id=1, source_target_pairs={{0,2},{1,7},{2,0},{3,5},{4,6},{5,3},{6,4},{7,1},{8,10},{9,15},{10,... | collective-permute-start | bytes 786440 | tf_op jit(solution)/shard_map/ppermute | solution.py:223
  180.6 3.6 %combine.2 = (bf16[256,2048]{1,0:T(8,128)(2,1)}, bf16[256,2048]{1,0:T(8,128)(2,1)}) custom-call(s32[1,256]{1,0:T(1,128)} %bitcast.15, bf16[256,2048]{1,0:T(8,128)(2,1)} %refs_1_.5, bf16[256,2048]{1,0:T(8,128)(2,1)} %refs_2_.5, bf16[32,4096]{1,0:T(8,128)(2,1)} %get-tuple-element.93.refs_3_, bf16[32,4096]{1,0:T(8,128)(2,1)} %collective-permute-done.8.refs_4_, ...), custom_call_target="tpu_custom_call" | custom-call | flops 1024 | bytes 1024 | tf_op jit(solution)/shard_map/combine/pallas_call | solution.py:28
  184.2 0.0 collective-permute-done.26.refs_4_
  184.2 0.1 collective-permute-start.31
  184.3 3.8 %collective-permute-start.30 = (bf16[32,4096]{1,0:T(8,128)(2,1)}, bf16[32,4096]{1,0:T(8,128)(2,1)}, u32[]{:S(2)}, u32[]{:S(2)}) collective-permute-start(bf16[32,4096]{1,0:T(8,128)(2,1)} %get-tuple-element.152), channel_id=1, source_target_pairs={{0,7},{1,2},{2,1},{3,4},{4,3},{5,6},{6,5},{7,0},{8,15},{9,10},{10,... | collective-permute-start | bytes 786440 | tf_op jit(solution)/shard_map/ppermute | solution.py:223
  188.1 0.0 collective-permute-done.29.refs_7_
  188.1 0.6 collective-permute-start.32
  188.7 0.0 collective-permute-done.23.refs_7_
  188.7 8.2 %collective-permute-done.25.refs_9_ = bf16[496,2176]{1,0:T(8,128)(2,1)} collective-permute-done((bf16[496,2176]{1,0:T(8,128)(2,1)}, bf16[496,2176]{1,0:T(8,128)(2,1)}, u32[]{:S(2)}, u32[]{:S(2)}) %collective-permute-start.25) | collective-permute-done | bytes 2158624 | tf_op jit(solution)/shard_map/ppermute | solution.py:223
  196.9 6.7 %weight_part.7 = (f32[512,1408]{1,0:T(8,128)}, f32[704,512]{1,0:T(8,128)}) custom-call(s32[1]{0:T(128)} %bitcast.3.refs_0_, bf16[256,4096]{1,0:T(8,128)(2,1)} %get-tuple-element.138.refs_1_, bf16[256,1408]{1,0:T(8,128)(2,1)} %get-tuple-element.127.refs_2_, bf16[256,704]{1,0:T(8,128)(2,1)} %get-tuple-element.128.refs_3_, ...), custom_call_target="tpu_custom_call" | custom-call | flops 1024 | bytes 1024 | tf_op jit(solution)/shard_map/weight_part/pallas_call | solution.py:28
  203.5 0.0 collective-permute-done.31.refs_9_
  203.6 0.0 collective-permute-done.30.refs_8_
  203.6 8.3 %collective-permute-done.32.refs_10_ = bf16[32,4096]{1,0:T(8,128)(2,1)} collective-permute-done((bf16[32,4096]{1,0:T(8,128)(2,1)}, bf16[32,4096]{1,0:T(8,128)(2,1)}, u32[]{:S(2)}, u32[]{:S(2)}) %collective-permute-start.32) | collective-permute-done | bytes 262176 | tf_op jit(solution)/shard_map/ppermute | solution.py:223
  211.9 3.6 %combine.3 = (bf16[256,2048]{1,0:T(8,128)(2,1)}, bf16[256,2048]{1,0:T(8,128)(2,1)}) custom-call(s32[1,256]{1,0:T(1,128)} %bitcast.16, bf16[256,2048]{1,0:T(8,128)(2,1)} %get-tuple-element.122.refs_1_, bf16[256,2048]{1,0:T(8,128)(2,1)} %get-tuple-element.123.refs_2_, bf16[32,4096]{1,0:T(8,128)(2,1)} %get-tuple-element.142.refs_3_, ...), custom_call_target="tpu_custom_call" | custom-call | flops 1024 | bytes 1024 | tf_op jit(solution)/shard_map/combine/pallas_call | solution.py:28
  (12 shorter events, 0.0 us)
Async XLA Ops:
  4.1 18.2 %collective-permute-start = (bf16[32,4096]{1,0:T(8,128)(2,1)}, bf16[32,4096]{1,0:T(8,128)(2,1)}, u32[]{:S(2)}, u32[]{:S(2)}) collective-permute-start(bf16[32,4096]{1,0:T(8,128)(2,1)} %get-tuple-element.83), channel_id=1, source_target_pairs={{0,5},{1,4},{2,3},{3,2},{4,1},{5,0},{6,7},{7,6},{8,13},{9,12},{10,... | collective-permute-start | bytes 786440 | tf_op jit(solution)/shard_map/ppermute | solution.py:223
  9.1 13.1 %collective-permute-start.1 = (bf16[32,4096]{1,0:T(8,128)(2,1)}, bf16[32,4096]{1,0:T(8,128)(2,1)}, u32[]{:S(2)}, u32[]{:S(2)}) collective-permute-start(bf16[32,4096]{1,0:T(8,128)(2,1)} %get-tuple-element.84), channel_id=1, source_target_pairs={{0,1},{1,0},{2,7},{3,6},{4,5},{5,4},{6,3},{7,2},{8,9},{9,8},{10,15... | collective-permute-start | bytes 786440 | tf_op jit(solution)/shard_map/ppermute | solution.py:223
  9.6 23.0 %collective-permute-start.2 = (bf16[32,4096]{1,0:T(8,128)(2,1)}, bf16[32,4096]{1,0:T(8,128)(2,1)}, u32[]{:S(2)}, u32[]{:S(2)}) collective-permute-start(bf16[32,4096]{1,0:T(8,128)(2,1)} %get-tuple-element.85), channel_id=1, source_target_pairs={{0,6},{1,3},{2,4},{3,1},{4,2},{5,7},{6,0},{7,5},{8,14},{9,11},{10,... | collective-permute-start | bytes 786440 | tf_op jit(solution)/shard_map/ppermute | solution.py:223
  11.0 30.0 %collective-permute-start.3 = (bf16[32,4096]{1,0:T(8,128)(2,1)}, bf16[32,4096]{1,0:T(8,128)(2,1)}, u32[]{:S(2)}, u32[]{:S(2)}) collective-permute-start(bf16[32,4096]{1,0:T(8,128)(2,1)} %get-tuple-element.86), channel_id=1, source_target_pairs={{0,2},{1,7},{2,0},{3,5},{4,6},{5,3},{6,4},{7,1},{8,10},{9,15},{10,... | collective-permute-start | bytes 786440 | tf_op jit(solution)/shard_map/ppermute | solution.py:223
  22.2 18.8 %collective-permute-start.4 = (bf16[32,4096]{1,0:T(8,128)(2,1)}, bf16[32,4096]{1,0:T(8,128)(2,1)}, u32[]{:S(2)}, u32[]{:S(2)}) collective-permute-start(bf16[32,4096]{1,0:T(8,128)(2,1)} %get-tuple-element.88), channel_id=1, source_target_pairs={{0,7},{1,2},{2,1},{3,4},{4,3},{5,6},{6,5},{7,0},{8,15},{9,10},{10,... | collective-permute-start | bytes 786440 | tf_op jit(solution)/shard_map/ppermute | solution.py:223
  22.2 20.4 %collective-permute-start.5 = (bf16[32,4096]{1,0:T(8,128)(2,1)}, bf16[32,4096]{1,0:T(8,128)(2,1)}, u32[]{:S(2)}, u32[]{:S(2)}) collective-permute-start(bf16[32,4096]{1,0:T(8,128)(2,1)} %get-tuple-element.90), channel_id=1, source_target_pairs={{0,3},{1,6},{2,5},{3,0},{4,7},{5,2},{6,1},{7,4},{8,11},{9,14},{10,... | collective-permute-start | bytes 786440 | tf_op jit(solution)/shard_map/ppermute | solution.py:223
  32.7 25.6 %collective-permute-start.6 = (bf16[32,4096]{1,0:T(8,128)(2,1)}, bf16[32,4096]{1,0:T(8,128)(2,1)}, u32[]{:S(2)}, u32[]{:S(2)}) collective-permute-start(bf16[32,4096]{1,0:T(8,128)(2,1)} %get-tuple-element.92), channel_id=1, source_target_pairs={{0,4},{1,5},{2,6},{3,7},{4,0},{5,1},{6,2},{7,3},{8,12},{9,13},{10,... | collective-permute-start | bytes 786440 | tf_op jit(solution)/shard_map/ppermute | solution.py:223
  41.0 34.7 %collective-permute-start.9 = (bf16[32,4096]{1,0:T(8,128)(2,1)}, bf16[32,4096]{1,0:T(8,128)(2,1)}, u32[]{:S(2)}, u32[]{:S(2)}) collective-permute-start(bf16[32,4096]{1,0:T(8,128)(2,1)} %get-tuple-element.101), channel_id=1, source_target_pairs={{0,5},{1,4},{2,3},{3,2},{4,1},{5,0},{6,7},{7,6},{8,13},{9,12},{10,... | collective-permute-start | bytes 786440 | tf_op jit(solution)/shard_map/ppermute | solution.py:223
  41.0 45.6 %collective-permute-start.12 = (bf16[32,4096]{1,0:T(8,128)(2,1)}, bf16[32,4096]{1,0:T(8,128)(2,1)}, u32[]{:S(2)}, u32[]{:S(2)}) collective-permute-start(bf16[32,4096]{1,0:T(8,128)(2,1)} %get-tuple-element.107), channel_id=1, source_target_pairs={{0,1},{1,0},{2,7},{3,6},{4,5},{5,4},{6,3},{7,2},{8,9},{9,8},{10,15... | collective-permute-start | bytes 786440 | tf_op jit(solution)/shard_map/ppermute | solution.py:223
  42.7 44.0 %collective-permute-start.15 = (bf16[32,4096]{1,0:T(8,128)(2,1)}, bf16[32,4096]{1,0:T(8,128)(2,1)}, u32[]{:S(2)}, u32[]{:S(2)}) collective-permute-start(bf16[32,4096]{1,0:T(8,128)(2,1)} %get-tuple-element.113), channel_id=1, source_target_pairs={{0,6},{1,3},{2,4},{3,1},{4,2},{5,7},{6,0},{7,5},{8,14},{9,11},{10,... | collective-permute-start | bytes 786440 | tf_op jit(solution)/shard_map/ppermute | solution.py:223
  58.3 33.7 %collective-permute-start.7 = (bf16[32,4096]{1,0:T(8,128)(2,1)}, bf16[32,4096]{1,0:T(8,128)(2,1)}, u32[]{:S(2)}, u32[]{:S(2)}) collective-permute-start(bf16[32,4096]{1,0:T(8,128)(2,1)} %get-tuple-element.96), channel_id=1, source_target_pairs={{0,2},{1,7},{2,0},{3,5},{4,6},{5,3},{6,4},{7,1},{8,10},{9,15},{10,... | collective-permute-start | bytes 786440 | tf_op jit(solution)/shard_map/ppermute | solution.py:223
  75.7 16.3 %collective-permute-start.10 = (bf16[32,4096]{1,0:T(8,128)(2,1)}, bf16[32,4096]{1,0:T(8,128)(2,1)}, u32[]{:S(2)}, u32[]{:S(2)}) collective-permute-start(bf16[32,4096]{1,0:T(8,128)(2,1)} %get-tuple-element.102), channel_id=1, source_target_pairs={{0,7},{1,2},{2,1},{3,4},{4,3},{5,6},{6,5},{7,0},{8,15},{9,10},{10,... | collective-permute-start | bytes 786440 | tf_op jit(solution)/shard_map/ppermute | solution.py:223
  86.6 7.7 %collective-permute-start.13 = (bf16[32,4096]{1,0:T(8,128)(2,1)}, bf16[32,4096]{1,0:T(8,128)(2,1)}, u32[]{:S(2)}, u32[]{:S(2)}) collective-permute-start(bf16[32,4096]{1,0:T(8,128)(2,1)} %get-tuple-element.108), channel_id=1, source_target_pairs={{0,3},{1,6},{2,5},{3,0},{4,7},{5,2},{6,1},{7,4},{8,11},{9,14},{10,... | collective-permute-start | bytes 786440 | tf_op jit(solution)/shard_map/ppermute | solution.py:223
  86.7 23.7 %collective-permute-start.16 = (bf16[32,4096]{1,0:T(8,128)(2,1)}, bf16[32,4096]{1,0:T(8,128)(2,1)}, u32[]{:S(2)}, u32[]{:S(2)}) collective-permute-start(bf16[32,4096]{1,0:T(8,128)(2,1)} %get-tuple-element.114), channel_id=1, source_target_pairs={{0,4},{1,5},{2,6},{3,7},{4,0},{5,1},{6,2},{7,3},{8,12},{9,13},{10,... | collective-permute-start | bytes 786440 | tf_op jit(solution)/shard_map/ppermute | solution.py:223
  92.0 37.4 %collective-permute-start.11 = (bf16[32,4096]{1,0:T(8,128)(2,1)}, bf16[32,4096]{1,0:T(8,128)(2,1)}, u32[]{:S(2)}, u32[]{:S(2)}) collective-permute-start(bf16[32,4096]{1,0:T(8,128)(2,1)} %get-tuple-element.103), channel_id=1, source_target_pairs={{0,1},{1,0},{2,7},{3,6},{4,5},{5,4},{6,3},{7,2},{8,9},{9,8},{10,15... | collective-permute-start | bytes 786440 | tf_op jit(solution)/shard_map/ppermute | solution.py:223
  92.0 37.4 %collective-permute-start.8 = (bf16[32,4096]{1,0:T(8,128)(2,1)}, bf16[32,4096]{1,0:T(8,128)(2,1)}, u32[]{:S(2)}, u32[]{:S(2)}) collective-permute-start(bf16[32,4096]{1,0:T(8,128)(2,1)} %get-tuple-element.97), channel_id=1, source_target_pairs={{0,5},{1,4},{2,3},{3,2},{4,1},{5,0},{6,7},{7,6},{8,13},{9,12},{10,... | collective-permute-start | bytes 786440 | tf_op jit(solution)/shard_map/ppermute | solution.py:223
  110.3 20.6 %collective-permute-start.17 = (bf16[32,4096]{1,0:T(8,128)(2,1)}, bf16[32,4096]{1,0:T(8,128)(2,1)}, u32[]{:S(2)}, u32[]{:S(2)}) collective-permute-start(bf16[32,4096]{1,0:T(8,128)(2,1)} %get-tuple-element.115), channel_id=1, source_target_pairs={{0,2},{1,7},{2,0},{3,5},{4,6},{5,3},{6,4},{7,1},{8,10},{9,15},{10,... | collective-permute-start | bytes 786440 | tf_op jit(solution)/shard_map/ppermute | solution.py:223
  110.5 20.4 %collective-permute-start.14 = (bf16[32,4096]{1,0:T(8,128)(2,1)}, bf16[32,4096]{1,0:T(8,128)(2,1)}, u32[]{:S(2)}, u32[]{:S(2)}) collective-permute-start(bf16[32,4096]{1,0:T(8,128)(2,1)} %get-tuple-element.109), channel_id=1, source_target_pairs={{0,6},{1,3},{2,4},{3,1},{4,2},{5,7},{6,0},{7,5},{8,14},{9,11},{10,... | collective-permute-start | bytes 786440 | tf_op jit(solution)/shard_map/ppermute | solution.py:223
  129.2 1.7 collective-permute-start.21
  130.9 7.8 %collective-permute-start.22 = (bf16[496,2176]{1,0:T(8,128)(2,1)}, bf16[496,2176]{1,0:T(8,128)(2,1)}, u32[]{:S(2)}, u32[]{:S(2)}) collective-permute-start(bf16[496,2176]{1,0:T(8,128)(2,1)} %get-tuple-element.136), channel_id=1, source_target_pairs={{0,8},{8,0},{16,24},{24,16},{1,9},{9,1},{17,25},{25,17},{2,10},{10... | collective-permute-start | bytes 6475784 | tf_op jit(solution)/shard_map/ppermute | solution.py:223
  131.1 14.9 %collective-permute-start.19 = (bf16[32,4096]{1,0:T(8,128)(2,1)}, bf16[32,4096]{1,0:T(8,128)(2,1)}, u32[]{:S(2)}, u32[]{:S(2)}) collective-permute-start(bf16[32,4096]{1,0:T(8,128)(2,1)} %get-tuple-element.119), channel_id=1, source_target_pairs={{0,3},{1,6},{2,5},{3,0},{4,7},{5,2},{6,1},{7,4},{8,11},{9,14},{10,... | collective-permute-start | bytes 786440 | tf_op jit(solution)/shard_map/ppermute | solution.py:223
  131.1 15.9 %collective-permute-start.18 = (bf16[32,4096]{1,0:T(8,128)(2,1)}, bf16[32,4096]{1,0:T(8,128)(2,1)}, u32[]{:S(2)}, u32[]{:S(2)}) collective-permute-start(bf16[32,4096]{1,0:T(8,128)(2,1)} %get-tuple-element.117), channel_id=1, source_target_pairs={{0,7},{1,2},{2,1},{3,4},{4,3},{5,6},{6,5},{7,0},{8,15},{9,10},{10,... | collective-permute-start | bytes 786440 | tf_op jit(solution)/shard_map/ppermute | solution.py:223
  144.4 4.7 %collective-permute-start.24 = (bf16[16,2176]{1,0:T(8,128)(2,1)}, bf16[16,2176]{1,0:T(8,128)(2,1)}, u32[]{:S(2)}, u32[]{:S(2)}) collective-permute-start(bf16[16,2176]{1,0:T(8,128)(2,1)} %get-tuple-element.137), channel_id=1, source_target_pairs={{0,16},{8,24},{16,0},{24,8},{1,17},{9,25},{17,1},{25,9},{2,18},{10... | collective-permute-start | bytes 208904 | tf_op jit(solution)/shard_map/ppermute | solution.py:223
  145.9 42.8 %collective-permute-start.23 = (bf16[512,2176]{1,0:T(8,128)(2,1)}, bf16[512,2176]{1,0:T(8,128)(2,1)}, u32[]{:S(2)}, u32[]{:S(2)}) collective-permute-start(bf16[512,2176]{1,0:T(8,128)(2,1)} %weight_part.5), channel_id=1, source_target_pairs={{0,8},{8,0},{16,24},{24,16},{1,9},{9,1},{17,25},{25,17},{2,10},{10... | collective-permute-start | bytes 6684680 | tf_op jit(solution)/shard_map/ppermute | solution.py:223
  149.1 47.8 %collective-permute-start.25 = (bf16[496,2176]{1,0:T(8,128)(2,1)}, bf16[496,2176]{1,0:T(8,128)(2,1)}, u32[]{:S(2)}, u32[]{:S(2)}) collective-permute-start(bf16[496,2176]{1,0:T(8,128)(2,1)} %get-tuple-element.140), channel_id=1, source_target_pairs={{0,16},{8,24},{16,0},{24,8},{1,17},{9,25},{17,1},{25,9},{2,18},{10... | collective-permute-start | bytes 6475784 | tf_op jit(solution)/shard_map/ppermute | solution.py:223
  150.6 19.6 %collective-permute-start.20 = (bf16[32,4096]{1,0:T(8,128)(2,1)}, bf16[32,4096]{1,0:T(8,128)(2,1)}, u32[]{:S(2)}, u32[]{:S(2)}) collective-permute-start(bf16[32,4096]{1,0:T(8,128)(2,1)} %get-tuple-element.121), channel_id=1, source_target_pairs={{0,4},{1,5},{2,6},{3,7},{4,0},{5,1},{6,2},{7,3},{8,12},{9,13},{10,... | collective-permute-start | bytes 786440 | tf_op jit(solution)/shard_map/ppermute | solution.py:223
  152.0 20.1 %collective-permute-start.27 = (bf16[32,4096]{1,0:T(8,128)(2,1)}, bf16[32,4096]{1,0:T(8,128)(2,1)}, u32[]{:S(2)}, u32[]{:S(2)}) collective-permute-start(bf16[32,4096]{1,0:T(8,128)(2,1)} %get-tuple-element.146), channel_id=1, source_target_pairs={{0,1},{1,0},{2,7},{3,6},{4,5},{5,4},{6,3},{7,2},{8,9},{9,8},{10,15... | collective-permute-start | bytes 786440 | tf_op jit(solution)/shard_map/ppermute | solution.py:223
  152.0 32.2 %collective-permute-start.26 = (bf16[32,4096]{1,0:T(8,128)(2,1)}, bf16[32,4096]{1,0:T(8,128)(2,1)}, u32[]{:S(2)}, u32[]{:S(2)}) collective-permute-start(bf16[32,4096]{1,0:T(8,128)(2,1)} %get-tuple-element.144), channel_id=1, source_target_pairs={{0,5},{1,4},{2,3},{3,2},{4,1},{5,0},{6,7},{7,6},{8,13},{9,12},{10,... | collective-permute-start | bytes 786440 | tf_op jit(solution)/shard_map/ppermute | solution.py:223
  170.1 14.2 %collective-permute-start.28 = (bf16[32,4096]{1,0:T(8,128)(2,1)}, bf16[32,4096]{1,0:T(8,128)(2,1)}, u32[]{:S(2)}, u32[]{:S(2)}) collective-permute-start(bf16[32,4096]{1,0:T(8,128)(2,1)} %get-tuple-element.148), channel_id=1, source_target_pairs={{0,6},{1,3},{2,4},{3,1},{4,2},{5,7},{6,0},{7,5},{8,14},{9,11},{10,... | collective-permute-start | bytes 786440 | tf_op jit(solution)/shard_map/ppermute | solution.py:223
  172.1 16.0 %collective-permute-start.29 = (bf16[32,4096]{1,0:T(8,128)(2,1)}, bf16[32,4096]{1,0:T(8,128)(2,1)}, u32[]{:S(2)}, u32[]{:S(2)}) collective-permute-start(bf16[32,4096]{1,0:T(8,128)(2,1)} %get-tuple-element.150), channel_id=1, source_target_pairs={{0,2},{1,7},{2,0},{3,5},{4,6},{5,3},{6,4},{7,1},{8,10},{9,15},{10,... | collective-permute-start | bytes 786440 | tf_op jit(solution)/shard_map/ppermute | solution.py:223
  184.2 19.3 %collective-permute-start.31 = (bf16[32,4096]{1,0:T(8,128)(2,1)}, bf16[32,4096]{1,0:T(8,128)(2,1)}, u32[]{:S(2)}, u32[]{:S(2)}) collective-permute-start(bf16[32,4096]{1,0:T(8,128)(2,1)} %get-tuple-element.154), channel_id=1, source_target_pairs={{0,3},{1,6},{2,5},{3,0},{4,7},{5,2},{6,1},{7,4},{8,11},{9,14},{10,... | collective-permute-start | bytes 786440 | tf_op jit(solution)/shard_map/ppermute | solution.py:223
  184.3 19.2 %collective-permute-start.30 = (bf16[32,4096]{1,0:T(8,128)(2,1)}, bf16[32,4096]{1,0:T(8,128)(2,1)}, u32[]{:S(2)}, u32[]{:S(2)}) collective-permute-start(bf16[32,4096]{1,0:T(8,128)(2,1)} %get-tuple-element.152), channel_id=1, source_target_pairs={{0,7},{1,2},{2,1},{3,4},{4,3},{5,6},{6,5},{7,0},{8,15},{9,10},{10,... | collective-permute-start | bytes 786440 | tf_op jit(solution)/shard_map/ppermute | solution.py:223
  188.1 23.8 %collective-permute-start.32 = (bf16[32,4096]{1,0:T(8,128)(2,1)}, bf16[32,4096]{1,0:T(8,128)(2,1)}, u32[]{:S(2)}, u32[]{:S(2)}) collective-permute-start(bf16[32,4096]{1,0:T(8,128)(2,1)} %get-tuple-element.156), channel_id=1, source_target_pairs={{0,4},{1,5},{2,6},{3,7},{4,0},{5,1},{6,2},{7,3},{8,12},{9,13},{10,... | collective-permute-start | bytes 786440 | tf_op jit(solution)/shard_map/ppermute | solution.py:223

commit v11 on v10

--- a/solution.py
+++ b/solution.py
@@ -54,14 +54,14 @@
         copy.wait()
 
 
-def place_kernel(part, cap, ids_ref, tokens_ref, grad_ref, *refs):
+def place_kernel(start, cap, ids_ref, tokens_ref, grad_ref, *refs):
     blocks, (ids, data, moved, sems) = refs[:-4], refs[-4:]
     copies = Copies(sems)
     ids_load = copies.start(ids_ref, ids)
     pieces = pieces_of(tokens_ref, grad_ref)
     loads = [copies.start(ref.at[:, there], data.at[:, here]) for ref, there, here in pieces]
     ids_load.wait()
-    placing = placing_of(ids[...], len(blocks), part, cap)
+    placing = placing_of(ids[...], len(blocks), start, cap)
     stores = []
     for load, (_, _, here) in zip(loads, pieces):
         load.wait()
@@ -80,7 +80,7 @@
     ]
 
 
-def placing_of(ids, experts, part, cap):
+def placing_of(ids, experts, start, cap):
     rows = ids.shape[1]
     rel = jnp.zeros((1, rows), jnp.int32)
     me = lax.axis_index("exp").astype(jnp.int32)
@@ -89,7 +89,7 @@
     onehot = lax.broadcasted_iota(jnp.int32, (max(experts, 16), rows), 0) == rel
     before = lax.broadcasted_iota(jnp.int32, (rows, rows), 0) < lax.broadcasted_iota(jnp.int32, (rows, rows), 1)
     ranks = dot(onehot.astype(BF16), before.astype(BF16), PLAIN)
-    rank = jnp.sum(jnp.where(onehot, ranks, 0.0), axis=0, keepdims=True).astype(jnp.int32) - part * cap
+    rank = jnp.sum(jnp.where(onehot, ranks, 0.0), axis=0, keepdims=True).astype(jnp.int32) - start
     target = jnp.where((rank >= 0) & (rank < cap), rel * cap + rank, -1)
     return (lax.broadcasted_iota(jnp.int32, (experts * cap, rows), 0) == target).astype(BF16)
 
@@ -139,15 +139,16 @@
     more, refs = refs[: sum(pieces)], refs[sum(pieces) :]
     results, sems = refs[-3 if end else -2 : -1], refs[-1]
     outs, (x, dy, proj, hidden, received) = refs[: -6 - len(results)], refs[-6 - len(results) : -1 - len(results)]
-    cap = x.shape[0] // parts
     share, wide = x.shape[1], hidden.shape[1]
     width = sources[0].shape[1] // 2
     first = pl.multiple_of(number_ref[0] * share, share)
     copies = Copies(sems)
     loads = []
+    total = 0
     for part in range(parts):
         slot_ref, proj_ref, hidden_ref = sources[3 * part : 3 * part + 3]
-        here = slice(part * cap, (part + 1) * cap)
+        here = slice(total, total + slot_ref.shape[0])
+        total = here.stop
         loads.append(copies.start(slot_ref.at[:, pl.ds(first, share)], x.at[here]))
         loads.append(copies.start(slot_ref.at[:, pl.ds(pl.multiple_of(first + width, share), share)], dy.at[here]))
         loads.append(copies.start(proj_ref, proj.at[here]))
@@ -160,33 +161,42 @@
             row += ref.shape[0]
         more = more[number:]
     wait(loads)
-    up = dot(x[...], proj[...], ROWS)
-    down = dot(hidden[...], dy[...], ROWS) if end else dot(dy[...], hidden[...], ROWS)
     wait(more_loads)
-    for index in range(len(pieces)):
-        up = up + received[index, :, : 2 * wide].astype(F32)
-        extra = received[index, :, 2 * wide : 3 * wide]
+    step = min(share, 128)
+    stores = []
+    for start in range(0, share, step):
+        here = slice(start, start + step)
+        up = dot(x[:, here], proj[...], ROWS)
+        for index in range(len(pieces)):
+            up = up + received[index, here, : 2 * wide].astype(F32)
         if end:
-            row = lax.broadcasted_iota(jnp.int32, (share, share), 0)
-            unit = (row == lax.broadcasted_iota(jnp.int32, (share, share), 1)).astype(BF16)
-            down = down + dot(extra, unit, ROWS)
-        else:
-            down = down + extra.astype(F32)
+            results[0][here] = up
+            stores.append(copies.start(results[0].at[here], outs[0].at[here]))
+            continue
+        down = dot(dy[:, here], hidden[...], ROWS)
+        for index in range(len(pieces)):
+            down = down + received[index, here, 2 * wide : 3 * wide].astype(F32)
+        results[0][here, : 2 * wide] = up.astype(BF16)
+        results[0][here, 2 * wide : 3 * wide] = down.astype(BF16)
+        row = 0
+        for out in outs:
+            first_row, last_row = max(row, start), min(row + out.shape[0], start + step)
+            if first_row < last_row:
+                there = out.at[first_row - row : last_row - row]
+                stores.append(copies.start(results[0].at[first_row:last_row], there))
+            row += out.shape[0]
     if end:
-        results[0][...] = up
+        down = dot(hidden[...], dy[...], ROWS)
+        row = lax.broadcasted_iota(jnp.int32, (share, share), 0)
+        unit = (row == lax.broadcasted_iota(jnp.int32, (share, share), 1)).astype(BF16)
+        for index in range(len(pieces)):
+            down = down + dot(received[index, :, 2 * wide : 3 * wide], unit, ROWS)
         results[1][...] = down
-        wait([copies.start(result, out) for result, out in zip(results, outs)])
-        return
-    results[0][:, : 2 * wide] = up.astype(BF16)
-    results[0][:, 2 * wide : 3 * wide] = down.astype(BF16)
-    stores, row = [], 0
-    for out in outs:
-        stores.append(copies.start(results[0].at[row : row + out.shape[0]], out))
-        row += out.shape[0]
+        stores.append(copies.start(results[1], outs[1]))
     wait(stores)
 
 
-def combine_kernel(part, cap, ids_ref, tokens_ref, grad_ref, *refs):
+def combine_kernel(start, cap, ids_ref, tokens_ref, grad_ref, *refs):
     blocks, (mixed_out, grad_out, ids, data, back, sems) = refs[:-6], refs[-6:]
     copies = Copies(sems)
     ids_load = copies.start(ids_ref, ids)
@@ -197,7 +207,7 @@
         for index, block in enumerate(blocks):
             loads[-1].append(copies.start(block.at[:, here], back.at[index * cap : (index + 1) * cap, here]))
     ids_load.wait()
-    placing = placing_of(ids[...], len(blocks), part, cap)
+    placing = placing_of(ids[...], len(blocks), start, cap)
     stores = []
     for load, (_, there, here), (out, _, _) in zip(loads, pieces, pieces_of(mixed_out, grad_out)):
         wait(load)
@@ -258,40 +268,43 @@
     experts = lax.axis_size("exp")
     groups = lax.axis_size("grp")
     capacity = 2 * rows // experts
-    parts = 2 if capacity % 32 == 0 else 1
-    cap = capacity // parts
-    slots = experts * cap
+    first = capacity * 3 // 4
+    cuts = [(0, first), (first, capacity - first)] if capacity % 64 == 0 else [(0, capacity)]
+    parts = len(cuts)
     weight_one = gate_up_weight[0]
     weight_two = down_weight[0]
     wide = weight_two.shape[0]
     share = width // groups
-    pair = like((cap, 2 * width))
     sems = pltpu.SemaphoreType.DMA
     ids_here = pltpu.VMEM((1, rows), jnp.int32)
-    halves = [pltpu.VMEM((count, 2 * width), BF16) for count in (rows, slots)]
+
+    def halves(cap):
+        return [pltpu.VMEM((count, 2 * width), BF16) for count in (rows, experts * cap)]
+
     lane = Lane(4)
     numbers = range(1, experts)
     ids = expert_ids.reshape(1, rows)
     rounds = rounds_of(experts)
     group = lax.axis_index("grp").astype(jnp.int32)
 
-    def place(part):
+    def place(start, cap):
         return call(
-            lambda *refs: place_kernel(part, cap, *refs),
+            lambda *refs: place_kernel(start, cap, *refs),
             "place",
-            [pair] * experts,
-            [ids_here, *halves, sems((1 + PIECES * (1 + experts),))],
+            [like((cap, 2 * width))] * experts,
+            [ids_here, *halves(cap), sems((1 + PIECES * (1 + experts),))],
             [ids, tokens, grad_out],
         )
 
     def expert(blocks):
+        slots = experts * blocks[0].shape[0]
         shapes = [(slots, 2 * width), (slots, 2 * wide), (slots, wide)]
         back = [pltpu.VMEM(shape, BF16) for shape in shapes]
         scratch = [back[0], pltpu.VMEM(weight_one.shape, BF16), pltpu.VMEM(weight_two.shape, BF16)]
         outs = call(
             expert_kernel,
             "expert",
-            [pair] * experts + [like(shape) for shape in shapes],
+            [like(blocks[0].shape)] * experts + [like(shape) for shape in shapes],
             scratch + back + [sems((6 + 3 * experts,))],
             [*blocks, weight_one, weight_two],
         )
@@ -302,12 +315,12 @@
         finals = [like((share, 2 * wide), F32), like((wide, share), F32)]
         rows_of = [heads, share - heads] if heads else [share]
         outs = finals if end else [like((count, shape[1])) for count in rows_of]
-        total = parts * slots
+        total = experts * capacity
         scratch = [pltpu.VMEM((total, width), BF16) for width in (share, share, 2 * wide, wide)]
         scratch.append(pltpu.VMEM((max(1, len(received)), *shape), BF16))
         scratch += [pltpu.VMEM(out.shape, out.dtype) for out in (finals if end else [like(shape)])]
         sources = [array for arrays in kept + received for array in arrays]
-        scratch.append(sems((len(sources) + parts + len(outs),)))
+        scratch.append(sems((len(sources) + parts + len(outs) + 4 * groups,)))
         pieces = [len(arrays) for arrays in received]
         return call(
             lambda *refs: weight_kernel(end, parts, pieces, *refs),
@@ -318,16 +331,16 @@
             scalars=[number[None]],
         )
 
-    def combine(part, first, second, blocks):
+    def combine(start, cap, first, second, blocks):
         return call(
-            lambda *refs: combine_kernel(part, cap, *refs),
+            lambda *refs: combine_kernel(start, cap, *refs),
             "combine",
             [like((rows, width))] * 2,
-            [ids_here, *halves, sems((1 + PIECES * (2 + experts),))],
+            [ids_here, *halves(cap), sems((1 + PIECES * (2 + experts),))],
             [ids, first, second, *blocks],
         )
 
-    sent = [place(part) for part in range(parts)]
+    sent = [place(*cut) for cut in cuts]
     results = []
     for part in range(parts):
         earlier = [results[-1][0][0]] if results else []
@@ -339,14 +352,14 @@
     back = []
     for part in range(parts):
         if back:
-            mixed, grad = combine(part - 1, mixed, grad, back)
+            mixed, grad = combine(*cuts[part - 1], mixed, grad, back)
         blocks = results[part][0]
         back = [blocks[0]] + exchange(blocks, rounds, lane, numbers if part < parts - 1 else numbers[:-1])
     done = lane.done[count:]
 
     received = {q: [] for q in range(groups)}
     sums = kept[0][0]
-    held = {groups - 1: done[:4], 2: done[4:6]}
+    held = {groups - 1: done[:2], 2: done[2:4]}
     for q in sorted(range(1, groups), key=lambda q: (q & -q, -q)):
         low = q & -q
         sent = weight_part(group ^ q, [[sums, *kept[0][1:]], *kept[1:]], received[q], False, 16 if q in held else 0)
@@ -359,7 +372,7 @@
     grad_gate_up, grad_down = weight_part(group, [[sums, *kept[0][1:]], *kept[1:]], received[0], True, 0)
     back += exchange(blocks, rounds, lane, numbers[-1:], mixed, lane.done[-3])
     back[0] = after(back[0], grad_gate_up)
-    mixed, grad = combine(parts - 1, mixed, grad, back)
+    mixed, grad = combine(*cuts[-1], mixed, grad, back)
     return (mixed, grad, grad_gate_up[None], grad_down[None])
 
 

time: 216 us -> 241 us (1.12)
  waiting for transfers between devices: 72.8 us -> 88.7 us
  starting transfers between devices: 83.9 us -> 92.1 us
    ppermute x33, waiting for transfers between devices: 72.8 us -> 88.7 us  [send(): self.done.append(lax.ppermute(after(value, *earlier), axis, pairs))]
    ppermute x33, starting transfers between devices: 83.9 us -> 92.1 us  [send(): self.done.append(lax.ppermute(after(value, *earlier), axis, pairs))]
  transfers between devices with their start and end apart: 33 -> 33, of which waited for: 10 -> 10; matrix products, arithmetic and copies ran while one was open for 0% -> 0% of each run, Pallas kernels for 24% -> 21%
where the time goes in v11:
time: 241 us
  starting transfers between devices  92.1 us (38%)
  waiting for transfers between devices  88.7 us (37%)
  Pallas kernels  59 us (24%)
    ppermute x33, starting transfers between devices, send(): self.done.append(lax.ppermute(after(value, *earlier), axis, pairs))  92.1 us
    ppermute x33, waiting for transfers between devices, send(): self.done.append(lax.ppermute(after(value, *earlier), axis, pairs))  88.7 us
    pallas_call x10, Pallas kernels, call(): pl.pallas_call(kernel, in_specs=[pl.BlockSpec(memory_space=pltpu.SMEM)] *...  59 us
  transfers between devices with their start and end apart: 33, of which 10 were waited for; matrix products, arithmetic and copies ran while one was open for 0% of the time, Pallas kernels for 21%

profile of v11, /device:TPU:0, one launch (start us, length us, event | category | flops | bytes accessed | tf_op | source)
XLA Modules:
  0.0 240.7 jit_solution(8982543662507116918)
XLA Ops:
  0.6 3.8 %place.2 = (bf16[48,4096]{1,0:T(8,128)(2,1)}, bf16[48,4096]{1,0:T(8,128)(2,1)}, bf16[48,4096]{1,0:T(8,128)(2,1)}, bf16[48,4096]{1,0:T(8,128)(2,1)}, bf16[48,4096...) custom-call(s32[1,256]{1,0:T(1,128)} %bitcast.13, ...), custom_call_target="tpu_custom_call" | custom-call | flops 1024 | bytes 1024 | tf_op jit(solution)/shard_map/place/pallas_call | solution.py:28
  4.4 5.1 %collective-permute-start.2 = (bf16[48,4096]{1,0:T(8,128)(2,1)}, bf16[48,4096]{1,0:T(8,128)(2,1)}, u32[]{:S(2)}, u32[]{:S(2)}) collective-permute-start(bf16[48,4096]{1,0:T(8,128)(2,1)} %get-tuple-element.85), channel_id=1, source_target_pairs={{0,6},{1,3},{2,4},{3,1},{4,2},{5,7},{6,0},{7,5},{8,14},{9,11},{10,... | collective-permute-start | bytes 1179656 | tf_op jit(solution)/shard_map/ppermute | solution.py:233
  9.5 1.5 collective-permute-start
  11.1 0.0 collective-permute-start.1
  11.1 0.6 collective-permute-start.3
  11.6 8.3 %collective-permute-done.2.refs_3_ = bf16[48,4096]{1,0:T(8,128)(2,1)} collective-permute-done((bf16[48,4096]{1,0:T(8,128)(2,1)}, bf16[48,4096]{1,0:T(8,128)(2,1)}, u32[]{:S(2)}, u32[]{:S(2)}) %collective-permute-start.2) | collective-permute-done | bytes 393248 | tf_op jit(solution)/shard_map/ppermute | solution.py:233
  19.9 17.8 %collective-permute-start.6 = (bf16[48,4096]{1,0:T(8,128)(2,1)}, bf16[48,4096]{1,0:T(8,128)(2,1)}, u32[]{:S(2)}, u32[]{:S(2)}) collective-permute-start(bf16[48,4096]{1,0:T(8,128)(2,1)} %get-tuple-element.92), channel_id=1, source_target_pairs={{0,4},{1,5},{2,6},{3,7},{4,0},{5,1},{6,2},{7,3},{8,12},{9,13},{10,... | collective-permute-start | bytes 1179656 | tf_op jit(solution)/shard_map/ppermute | solution.py:233
  37.7 11.3 %collective-permute-done.refs_1_ = bf16[48,4096]{1,0:T(8,128)(2,1)} collective-permute-done((bf16[48,4096]{1,0:T(8,128)(2,1)}, bf16[48,4096]{1,0:T(8,128)(2,1)}, u32[]{:S(2)}, u32[]{:S(2)}) %collective-permute-start) | collective-permute-done | bytes 393248 | tf_op jit(solution)/shard_map/ppermute | solution.py:233
  49.0 0.0 collective-permute-start.4
  49.0 0.0 collective-permute-done.1.refs_2_
  49.0 4.8 %collective-permute-start.5 = (bf16[48,4096]{1,0:T(8,128)(2,1)}, bf16[48,4096]{1,0:T(8,128)(2,1)}, u32[]{:S(2)}, u32[]{:S(2)}) collective-permute-start(bf16[48,4096]{1,0:T(8,128)(2,1)} %get-tuple-element.90), channel_id=1, source_target_pairs={{0,3},{1,6},{2,5},{3,0},{4,7},{5,2},{6,1},{7,4},{8,11},{9,14},{10,... | collective-permute-start | bytes 1179656 | tf_op jit(solution)/shard_map/ppermute | solution.py:233
  53.8 3.0 %place.3 = (bf16[16,4096]{1,0:T(8,128)(2,1)}, bf16[16,4096]{1,0:T(8,128)(2,1)}, bf16[16,4096]{1,0:T(8,128)(2,1)}, bf16[16,4096]{1,0:T(8,128)(2,1)}, bf16[16,4096...) custom-call(s32[1,256]{1,0:T(1,128)} %bitcast.14, ...), custom_call_target="tpu_custom_call" | custom-call | flops 1024 | bytes 1024 | tf_op jit(solution)/shard_map/place/pallas_call | solution.py:28
  56.8 0.0 collective-permute-done.3.refs_4_
  56.9 9.7 %collective-permute-start.9 = (bf16[16,4096]{1,0:T(8,128)(2,1)}, bf16[16,4096]{1,0:T(8,128)(2,1)}, u32[]{:S(2)}, u32[]{:S(2)}) collective-permute-start(bf16[16,4096]{1,0:T(8,128)(2,1)} %get-tuple-element.101), channel_id=1, source_target_pairs={{0,5},{1,4},{2,3},{3,2},{4,1},{5,0},{6,7},{7,6},{8,13},{9,12},{10,... | collective-permute-start | bytes 393224 | tf_op jit(solution)/shard_map/ppermute | solution.py:233
  66.6 18.1 %collective-permute-done.9.refs_1_ = bf16[16,4096]{1,0:T(8,128)(2,1)} collective-permute-done((bf16[16,4096]{1,0:T(8,128)(2,1)}, bf16[16,4096]{1,0:T(8,128)(2,1)}, u32[]{:S(2)}, u32[]{:S(2)}) %collective-permute-start.9) | collective-permute-done | bytes 131104 | tf_op jit(solution)/shard_map/ppermute | solution.py:233
  84.6 0.0 collective-permute-start.10
  84.6 0.0 collective-permute-done.6.refs_7_
  84.6 0.0 collective-permute-start.7
  84.6 0.0 collective-permute-done.4.refs_5_
  84.7 0.0 collective-permute-done.5.refs_6_
  84.7 14.4 %expert.2 = (bf16[48,4096]{1,0:T(8,128)(2,1)}, bf16[48,4096]{1,0:T(8,128)(2,1)}, bf16[48,4096]{1,0:T(8,128)(2,1)}, bf16[48,4096]{1,0:T(8,128)(2,1)}, bf16[48,409...) custom-call(bf16[48,4096]{1,0:T(8,128)(2,1)} %get-tuple-element.82.r, ...), custom_call_target="tpu_custom_call" | custom-call | flops 1024 | bytes 1024 | tf_op jit(solution)/shard_map/expert/pallas_call | solution.py:28
  99.1 0.0 collective-permute-done.10.refs_5_
  99.1 5.3 %collective-permute-start.11 = (bf16[48,4096]{1,0:T(8,128)(2,1)}, bf16[48,4096]{1,0:T(8,128)(2,1)}, u32[]{:S(2)}, u32[]{:S(2)}) collective-permute-start(bf16[48,4096]{1,0:T(8,128)(2,1)} %get-tuple-element.103), channel_id=1, source_target_pairs={{0,1},{1,0},{2,7},{3,6},{4,5},{5,4},{6,3},{7,2},{8,9},{9,8},{10,15... | collective-permute-start | bytes 1179656 | tf_op jit(solution)/shard_map/ppermute | solution.py:233
  104.5 0.2 collective-permute-start.12
  104.6 3.7 %collective-permute-start.15 = (bf16[16,4096]{1,0:T(8,128)(2,1)}, bf16[16,4096]{1,0:T(8,128)(2,1)}, u32[]{:S(2)}, u32[]{:S(2)}) collective-permute-start(bf16[16,4096]{1,0:T(8,128)(2,1)} %get-tuple-element.113), channel_id=1, source_target_pairs={{0,6},{1,3},{2,4},{3,1},{4,2},{5,7},{6,0},{7,5},{8,14},{9,11},{10,... | collective-permute-start | bytes 393224 | tf_op jit(solution)/shard_map/ppermute | solution.py:233
  108.3 7.3 %collective-permute-done.12.refs_2_ = bf16[16,4096]{1,0:T(8,128)(2,1)} collective-permute-done((bf16[16,4096]{1,0:T(8,128)(2,1)}, bf16[16,4096]{1,0:T(8,128)(2,1)}, u32[]{:S(2)}, u32[]{:S(2)}) %collective-permute-start.12) | collective-permute-done | bytes 131104 | tf_op jit(solution)/shard_map/ppermute | solution.py:233
  115.6 4.0 %collective-permute-start.13 = (bf16[16,4096]{1,0:T(8,128)(2,1)}, bf16[16,4096]{1,0:T(8,128)(2,1)}, u32[]{:S(2)}, u32[]{:S(2)}) collective-permute-start(bf16[16,4096]{1,0:T(8,128)(2,1)} %get-tuple-element.108), channel_id=1, source_target_pairs={{0,3},{1,6},{2,5},{3,0},{4,7},{5,2},{6,1},{7,4},{8,11},{9,14},{10,... | collective-permute-start | bytes 393224 | tf_op jit(solution)/shard_map/ppermute | solution.py:233
  119.6 0.0 collective-permute-done.15.refs_3_
  119.6 11.4 %collective-permute-start.16 = (bf16[16,4096]{1,0:T(8,128)(2,1)}, bf16[16,4096]{1,0:T(8,128)(2,1)}, u32[]{:S(2)}, u32[]{:S(2)}) collective-permute-start(bf16[16,4096]{1,0:T(8,128)(2,1)} %get-tuple-element.114), channel_id=1, source_target_pairs={{0,4},{1,5},{2,6},{3,7},{4,0},{5,1},{6,2},{7,3},{8,12},{9,13},{10,... | collective-permute-start | bytes 393224 | tf_op jit(solution)/shard_map/ppermute | solution.py:233
  131.0 5.6 %collective-permute-done.16.refs_7_ = bf16[16,4096]{1,0:T(8,128)(2,1)} collective-permute-done((bf16[16,4096]{1,0:T(8,128)(2,1)}, bf16[16,4096]{1,0:T(8,128)(2,1)}, u32[]{:S(2)}, u32[]{:S(2)}) %collective-permute-start.16) | collective-permute-done | bytes 131104 | tf_op jit(solution)/shard_map/ppermute | solution.py:233
  136.6 9.2 %expert.3 = (bf16[16,4096]{1,0:T(8,128)(2,1)}, bf16[16,4096]{1,0:T(8,128)(2,1)}, bf16[16,4096]{1,0:T(8,128)(2,1)}, bf16[16,4096]{1,0:T(8,128)(2,1)}, bf16[16,409...) custom-call(bf16[16,4096]{1,0:T(8,128)(2,1)} %get-tuple-element.124., ...), custom_call_target="tpu_custom_call" | custom-call | flops 1024 | bytes 1024 | tf_op jit(solution)/shard_map/expert/pallas_call | solution.py:28
  145.8 4.4 %weight_part.4 = (bf16[16,2176]{1,0:T(8,128)(2,1)}, bf16[496,2176]{1,0:T(8,128)(2,1)}) custom-call(s32[1]{0:T(128)} %bitcast.4.refs_0_, bf16[384,4096]{1,0:T(8,128)(2,1)} %get-tuple-element.138.refs_1_, bf16[384,1408]{1,0:T(8,128)(2,1)} %get-tuple-element.127.refs_2_, bf16[384,704]{1,0:T(8,128)(2,1)} %get-tuple-element.128.refs_3_, ...), custom_call_target="tpu_custom_call" | custom-call | flops 1024 | bytes 1024 | tf_op jit(solution)/shard_map/weight_part/pallas_call | solution.py:28
  150.2 0.1 collective-permute-start.21
  150.3 1.6 collective-permute-done.21.refs_7_
  151.9 0.2 collective-permute-start.22
  152.0 0.0 collective-permute-start.17
  152.1 2.5 %collective-permute-start.14 = (bf16[48,4096]{1,0:T(8,128)(2,1)}, bf16[48,4096]{1,0:T(8,128)(2,1)}, u32[]{:S(2)}, u32[]{:S(2)}) collective-permute-start(bf16[48,4096]{1,0:T(8,128)(2,1)} %get-tuple-element.109), channel_id=1, source_target_pairs={{0,6},{1,3},{2,4},{3,1},{4,2},{5,7},{6,0},{7,5},{8,14},{9,11},{10,... | collective-permute-start | bytes 1179656 | tf_op jit(solution)/shard_map/ppermute | solution.py:233
  154.5 4.3 %weight_part.5 = bf16[512,2176]{1,0:T(8,128)(2,1)} custom-call(s32[1]{0:T(128)} %bitcast.5.refs_0_, bf16[384,4096]{1,0:T(8,128)(2,1)} %get-tuple-element.138.refs_1_, bf16[384,1408]{1,0:T(8,128)(2,1)} %get-tuple-element.127.refs_2_, bf16[384,704]{1,0:T(8,128)(2,1)} %get-tuple-element.128.refs_3_, bf16[128,4096]{1,0:T(8,128)(2,1)} %get-tuple-element.129.refs_4_, ...), custom_call_target="tpu_custom_call" | custom-call | flops 1024 | bytes 1024 | tf_op jit(solution)/shard_map/weight_part/pallas_call | solution.py:28
  158.9 5.2 %weight_part.6 = (bf16[16,2176]{1,0:T(8,128)(2,1)}, bf16[496,2176]{1,0:T(8,128)(2,1)}) custom-call(s32[1]{0:T(128)} %bitcast.6.refs_0_, bf16[384,4096]{1,0:T(8,128)(2,1)} %get-tuple-element.138.refs_1_, bf16[384,1408]{1,0:T(8,128)(2,1)} %get-tuple-element.127.refs_2_, bf16[384,704]{1,0:T(8,128)(2,1)} %get-tuple-element.128.refs_3_, ...), custom_call_target="tpu_custom_call" | custom-call | flops 1024 | bytes 1024 | tf_op jit(solution)/shard_map/weight_part/pallas_call | solution.py:28
  164.0 1.6 collective-permute-start.24
  165.6 0.0 collective-permute-start.23
  165.6 0.0 collective-permute-done.17.refs_7_
  165.6 7.4 %collective-permute-done.14.refs_6_ = bf16[48,4096]{1,0:T(8,128)(2,1)} collective-permute-done((bf16[48,4096]{1,0:T(8,128)(2,1)}, bf16[48,4096]{1,0:T(8,128)(2,1)}, u32[]{:S(2)}, u32[]{:S(2)}) %collective-permute-start.14) | collective-permute-done | bytes 393248 | tf_op jit(solution)/shard_map/ppermute | solution.py:233
  173.0 1.5 collective-permute-start.25
  174.5 0.5 collective-permute-start.19
  175.0 3.8 %collective-permute-start.18 = (bf16[48,4096]{1,0:T(8,128)(2,1)}, bf16[48,4096]{1,0:T(8,128)(2,1)}, u32[]{:S(2)}, u32[]{:S(2)}) collective-permute-start(bf16[48,4096]{1,0:T(8,128)(2,1)} %get-tuple-element.117), channel_id=1, source_target_pairs={{0,7},{1,2},{2,1},{3,4},{4,3},{5,6},{6,5},{7,0},{8,15},{9,10},{10,... | collective-permute-start | bytes 1179656 | tf_op jit(solution)/shard_map/ppermute | solution.py:233
  178.8 0.1 collective-permute-start.20
  178.9 18.2 %collective-permute-done.19.refs_9_ = bf16[48,4096]{1,0:T(8,128)(2,1)} collective-permute-done((bf16[48,4096]{1,0:T(8,128)(2,1)}, bf16[48,4096]{1,0:T(8,128)(2,1)}, u32[]{:S(2)}, u32[]{:S(2)}) %collective-permute-start.19) | collective-permute-done | bytes 393248 | tf_op jit(solution)/shard_map/ppermute | solution.py:233
  197.1 9.6 %collective-permute-start.26 = (bf16[16,4096]{1,0:T(8,128)(2,1)}, bf16[16,4096]{1,0:T(8,128)(2,1)}, u32[]{:S(2)}, u32[]{:S(2)}) collective-permute-start(bf16[16,4096]{1,0:T(8,128)(2,1)} %get-tuple-element.144), channel_id=1, source_target_pairs={{0,5},{1,4},{2,3},{3,2},{4,1},{5,0},{6,7},{7,6},{8,13},{9,12},{10,... | collective-permute-start | bytes 393224 | tf_op jit(solution)/shard_map/ppermute | solution.py:233
  206.7 0.0 collective-permute-done.18.refs_8_
  206.7 0.0 collective-permute-start.27
  206.7 9.0 %collective-permute-done.20.refs_10_ = bf16[48,4096]{1,0:T(8,128)(2,1)} collective-permute-done((bf16[48,4096]{1,0:T(8,128)(2,1)}, bf16[48,4096]{1,0:T(8,128)(2,1)}, u32[]{:S(2)}, u32[]{:S(2)}) %collective-permute-start.20) | collective-permute-done | bytes 393248 | tf_op jit(solution)/shard_map/ppermute | solution.py:233
  215.8 0.4 collective-permute-start.28
  216.2 4.3 %combine.2 = (bf16[256,2048]{1,0:T(8,128)(2,1)}, bf16[256,2048]{1,0:T(8,128)(2,1)}) custom-call(s32[1,256]{1,0:T(1,128)} %bitcast.15, bf16[256,2048]{1,0:T(8,128)(2,1)} %refs_1_.5, bf16[256,2048]{1,0:T(8,128)(2,1)} %refs_2_.5, bf16[48,4096]{1,0:T(8,128)(2,1)} %get-tuple-element.93.refs_3_, bf16[48,4096]{1,0:T(8,128)(2,1)} %collective-permute-done.8.refs_4_, ...), custom_call_target="tpu_custom_call" | custom-call | flops 1024 | bytes 1024 | tf_op jit(solution)/shard_map/combine/pallas_call | solution.py:28
  220.5 0.0 collective-permute-done.27.refs_5_
  220.5 7.1 %collective-permute-start.30 = (bf16[16,4096]{1,0:T(8,128)(2,1)}, bf16[16,4096]{1,0:T(8,128)(2,1)}, u32[]{:S(2)}, u32[]{:S(2)}) collective-permute-start(bf16[16,4096]{1,0:T(8,128)(2,1)} %get-tuple-element.152), channel_id=1, source_target_pairs={{0,7},{1,2},{2,1},{3,4},{4,3},{5,6},{6,5},{7,0},{8,15},{9,10},{10,... | collective-permute-start | bytes 393224 | tf_op jit(solution)/shard_map/ppermute | solution.py:233
  227.7 0.0 collective-permute-done.28.refs_6_
  227.7 0.6 collective-permute-start.32
  228.3 0.0 collective-permute-done.23.refs_7_
  228.3 0.0 collective-permute-done.25.refs_9_
  228.3 6.8 %weight_part.7 = (f32[512,1408]{1,0:T(8,128)}, f32[704,512]{1,0:T(8,128)}) custom-call(s32[1]{0:T(128)} %bitcast.3.refs_0_, bf16[384,4096]{1,0:T(8,128)(2,1)} %get-tuple-element.138.refs_1_, bf16[384,1408]{1,0:T(8,128)(2,1)} %get-tuple-element.127.refs_2_, bf16[384,704]{1,0:T(8,128)(2,1)} %get-tuple-element.128.refs_3_, ...), custom_call_target="tpu_custom_call" | custom-call | flops 1024 | bytes 1024 | tf_op jit(solution)/shard_map/weight_part/pallas_call | solution.py:28
  235.1 0.0 collective-permute-done.30.refs_8_
  235.2 1.9 collective-permute-done.32.refs_10_
  237.0 3.5 %combine.3 = (bf16[256,2048]{1,0:T(8,128)(2,1)}, bf16[256,2048]{1,0:T(8,128)(2,1)}) custom-call(s32[1,256]{1,0:T(1,128)} %bitcast.16, bf16[256,2048]{1,0:T(8,128)(2,1)} %get-tuple-element.122.refs_1_, bf16[256,2048]{1,0:T(8,128)(2,1)} %get-tuple-element.123.refs_2_, bf16[16,4096]{1,0:T(8,128)(2,1)} %get-tuple-element.142.refs_3_, ...), custom_call_target="tpu_custom_call" | custom-call | flops 1024 | bytes 1024 | tf_op jit(solution)/shard_map/combine/pallas_call | solution.py:28
  (12 shorter events, 0.0 us)
Async XLA Ops:
  4.4 15.5 %collective-permute-start.2 = (bf16[48,4096]{1,0:T(8,128)(2,1)}, bf16[48,4096]{1,0:T(8,128)(2,1)}, u32[]{:S(2)}, u32[]{:S(2)}) collective-permute-start(bf16[48,4096]{1,0:T(8,128)(2,1)} %get-tuple-element.85), channel_id=1, source_target_pairs={{0,6},{1,3},{2,4},{3,1},{4,2},{5,7},{6,0},{7,5},{8,14},{9,11},{10,... | collective-permute-start | bytes 1179656 | tf_op jit(solution)/shard_map/ppermute | solution.py:233
  9.5 39.4 %collective-permute-start = (bf16[48,4096]{1,0:T(8,128)(2,1)}, bf16[48,4096]{1,0:T(8,128)(2,1)}, u32[]{:S(2)}, u32[]{:S(2)}) collective-permute-start(bf16[48,4096]{1,0:T(8,128)(2,1)} %get-tuple-element.83), channel_id=1, source_target_pairs={{0,5},{1,4},{2,3},{3,2},{4,1},{5,0},{6,7},{7,6},{8,13},{9,12},{10,... | collective-permute-start | bytes 1179656 | tf_op jit(solution)/shard_map/ppermute | solution.py:233
  11.1 37.9 %collective-permute-start.1 = (bf16[48,4096]{1,0:T(8,128)(2,1)}, bf16[48,4096]{1,0:T(8,128)(2,1)}, u32[]{:S(2)}, u32[]{:S(2)}) collective-permute-start(bf16[48,4096]{1,0:T(8,128)(2,1)} %get-tuple-element.84), channel_id=1, source_target_pairs={{0,1},{1,0},{2,7},{3,6},{4,5},{5,4},{6,3},{7,2},{8,9},{9,8},{10,15... | collective-permute-start | bytes 1179656 | tf_op jit(solution)/shard_map/ppermute | solution.py:233
  11.1 45.8 %collective-permute-start.3 = (bf16[48,4096]{1,0:T(8,128)(2,1)}, bf16[48,4096]{1,0:T(8,128)(2,1)}, u32[]{:S(2)}, u32[]{:S(2)}) collective-permute-start(bf16[48,4096]{1,0:T(8,128)(2,1)} %get-tuple-element.86), channel_id=1, source_target_pairs={{0,2},{1,7},{2,0},{3,5},{4,6},{5,3},{6,4},{7,1},{8,10},{9,15},{10,... | collective-permute-start | bytes 1179656 | tf_op jit(solution)/shard_map/ppermute | solution.py:233
  19.9 64.7 %collective-permute-start.6 = (bf16[48,4096]{1,0:T(8,128)(2,1)}, bf16[48,4096]{1,0:T(8,128)(2,1)}, u32[]{:S(2)}, u32[]{:S(2)}) collective-permute-start(bf16[48,4096]{1,0:T(8,128)(2,1)} %get-tuple-element.92), channel_id=1, source_target_pairs={{0,4},{1,5},{2,6},{3,7},{4,0},{5,1},{6,2},{7,3},{8,12},{9,13},{10,... | collective-permute-start | bytes 1179656 | tf_op jit(solution)/shard_map/ppermute | solution.py:233
  49.0 35.7 %collective-permute-start.4 = (bf16[48,4096]{1,0:T(8,128)(2,1)}, bf16[48,4096]{1,0:T(8,128)(2,1)}, u32[]{:S(2)}, u32[]{:S(2)}) collective-permute-start(bf16[48,4096]{1,0:T(8,128)(2,1)} %get-tuple-element.88), channel_id=1, source_target_pairs={{0,7},{1,2},{2,1},{3,4},{4,3},{5,6},{6,5},{7,0},{8,15},{9,10},{10,... | collective-permute-start | bytes 1179656 | tf_op jit(solution)/shard_map/ppermute | solution.py:233
  49.0 35.7 %collective-permute-start.5 = (bf16[48,4096]{1,0:T(8,128)(2,1)}, bf16[48,4096]{1,0:T(8,128)(2,1)}, u32[]{:S(2)}, u32[]{:S(2)}) collective-permute-start(bf16[48,4096]{1,0:T(8,128)(2,1)} %get-tuple-element.90), channel_id=1, source_target_pairs={{0,3},{1,6},{2,5},{3,0},{4,7},{5,2},{6,1},{7,4},{8,11},{9,14},{10,... | collective-permute-start | bytes 1179656 | tf_op jit(solution)/shard_map/ppermute | solution.py:233
  56.9 27.8 %collective-permute-start.9 = (bf16[16,4096]{1,0:T(8,128)(2,1)}, bf16[16,4096]{1,0:T(8,128)(2,1)}, u32[]{:S(2)}, u32[]{:S(2)}) collective-permute-start(bf16[16,4096]{1,0:T(8,128)(2,1)} %get-tuple-element.101), channel_id=1, source_target_pairs={{0,5},{1,4},{2,3},{3,2},{4,1},{5,0},{6,7},{7,6},{8,13},{9,12},{10,... | collective-permute-start | bytes 393224 | tf_op jit(solution)/shard_map/ppermute | solution.py:233
  84.6 14.5 %collective-permute-start.10 = (bf16[16,4096]{1,0:T(8,128)(2,1)}, bf16[16,4096]{1,0:T(8,128)(2,1)}, u32[]{:S(2)}, u32[]{:S(2)}) collective-permute-start(bf16[16,4096]{1,0:T(8,128)(2,1)} %get-tuple-element.102), channel_id=1, source_target_pairs={{0,7},{1,2},{2,1},{3,4},{4,3},{5,6},{6,5},{7,0},{8,15},{9,10},{10,... | collective-permute-start | bytes 393224 | tf_op jit(solution)/shard_map/ppermute | solution.py:233
  84.6 19.8 %collective-permute-start.7 = (bf16[16,4096]{1,0:T(8,128)(2,1)}, bf16[16,4096]{1,0:T(8,128)(2,1)}, u32[]{:S(2)}, u32[]{:S(2)}) collective-permute-start(bf16[16,4096]{1,0:T(8,128)(2,1)} %get-tuple-element.96), channel_id=1, source_target_pairs={{0,2},{1,7},{2,0},{3,5},{4,6},{5,3},{6,4},{7,1},{8,10},{9,15},{10,... | collective-permute-start | bytes 393224 | tf_op jit(solution)/shard_map/ppermute | solution.py:233
  99.1 52.7 %collective-permute-start.11 = (bf16[48,4096]{1,0:T(8,128)(2,1)}, bf16[48,4096]{1,0:T(8,128)(2,1)}, u32[]{:S(2)}, u32[]{:S(2)}) collective-permute-start(bf16[48,4096]{1,0:T(8,128)(2,1)} %get-tuple-element.103), channel_id=1, source_target_pairs={{0,1},{1,0},{2,7},{3,6},{4,5},{5,4},{6,3},{7,2},{8,9},{9,8},{10,15... | collective-permute-start | bytes 1179656 | tf_op jit(solution)/shard_map/ppermute | solution.py:233
  104.5 47.4 %collective-permute-start.8 = (bf16[48,4096]{1,0:T(8,128)(2,1)}, bf16[48,4096]{1,0:T(8,128)(2,1)}, u32[]{:S(2)}, u32[]{:S(2)}) collective-permute-start(bf16[48,4096]{1,0:T(8,128)(2,1)} %get-tuple-element.97), channel_id=1, source_target_pairs={{0,5},{1,4},{2,3},{3,2},{4,1},{5,0},{6,7},{7,6},{8,13},{9,12},{10,... | collective-permute-start | bytes 1179656 | tf_op jit(solution)/shard_map/ppermute | solution.py:233
  104.5 11.1 %collective-permute-start.12 = (bf16[16,4096]{1,0:T(8,128)(2,1)}, bf16[16,4096]{1,0:T(8,128)(2,1)}, u32[]{:S(2)}, u32[]{:S(2)}) collective-permute-start(bf16[16,4096]{1,0:T(8,128)(2,1)} %get-tuple-element.107), channel_id=1, source_target_pairs={{0,1},{1,0},{2,7},{3,6},{4,5},{5,4},{6,3},{7,2},{8,9},{9,8},{10,15... | collective-permute-start | bytes 393224 | tf_op jit(solution)/shard_map/ppermute | solution.py:233
  104.6 15.0 %collective-permute-start.15 = (bf16[16,4096]{1,0:T(8,128)(2,1)}, bf16[16,4096]{1,0:T(8,128)(2,1)}, u32[]{:S(2)}, u32[]{:S(2)}) collective-permute-start(bf16[16,4096]{1,0:T(8,128)(2,1)} %get-tuple-element.113), channel_id=1, source_target_pairs={{0,6},{1,3},{2,4},{3,1},{4,2},{5,7},{6,0},{7,5},{8,14},{9,11},{10,... | collective-permute-start | bytes 393224 | tf_op jit(solution)/shard_map/ppermute | solution.py:233
  115.6 15.4 %collective-permute-start.13 = (bf16[16,4096]{1,0:T(8,128)(2,1)}, bf16[16,4096]{1,0:T(8,128)(2,1)}, u32[]{:S(2)}, u32[]{:S(2)}) collective-permute-start(bf16[16,4096]{1,0:T(8,128)(2,1)} %get-tuple-element.108), channel_id=1, source_target_pairs={{0,3},{1,6},{2,5},{3,0},{4,7},{5,2},{6,1},{7,4},{8,11},{9,14},{10,... | collective-permute-start | bytes 393224 | tf_op jit(solution)/shard_map/ppermute | solution.py:233
  119.6 16.9 %collective-permute-start.16 = (bf16[16,4096]{1,0:T(8,128)(2,1)}, bf16[16,4096]{1,0:T(8,128)(2,1)}, u32[]{:S(2)}, u32[]{:S(2)}) collective-permute-start(bf16[16,4096]{1,0:T(8,128)(2,1)} %get-tuple-element.114), channel_id=1, source_target_pairs={{0,4},{1,5},{2,6},{3,7},{4,0},{5,1},{6,2},{7,3},{8,12},{9,13},{10,... | collective-permute-start | bytes 393224 | tf_op jit(solution)/shard_map/ppermute | solution.py:233
  150.2 1.7 collective-permute-start.21
  151.9 7.0 %collective-permute-start.22 = (bf16[496,2176]{1,0:T(8,128)(2,1)}, bf16[496,2176]{1,0:T(8,128)(2,1)}, u32[]{:S(2)}, u32[]{:S(2)}) collective-permute-start(bf16[496,2176]{1,0:T(8,128)(2,1)} %get-tuple-element.136), channel_id=1, source_target_pairs={{0,8},{8,0},{16,24},{24,16},{1,9},{9,1},{17,25},{25,17},{2,10},{10... | collective-permute-start | bytes 6475784 | tf_op jit(solution)/shard_map/ppermute | solution.py:233
  152.0 13.6 %collective-permute-start.17 = (bf16[48,4096]{1,0:T(8,128)(2,1)}, bf16[48,4096]{1,0:T(8,128)(2,1)}, u32[]{:S(2)}, u32[]{:S(2)}) collective-permute-start(bf16[48,4096]{1,0:T(8,128)(2,1)} %get-tuple-element.115), channel_id=1, source_target_pairs={{0,2},{1,7},{2,0},{3,5},{4,6},{5,3},{6,4},{7,1},{8,10},{9,15},{10,... | collective-permute-start | bytes 1179656 | tf_op jit(solution)/shard_map/ppermute | solution.py:233
  152.1 21.0 %collective-permute-start.14 = (bf16[48,4096]{1,0:T(8,128)(2,1)}, bf16[48,4096]{1,0:T(8,128)(2,1)}, u32[]{:S(2)}, u32[]{:S(2)}) collective-permute-start(bf16[48,4096]{1,0:T(8,128)(2,1)} %get-tuple-element.109), channel_id=1, source_target_pairs={{0,6},{1,3},{2,4},{3,1},{4,2},{5,7},{6,0},{7,5},{8,14},{9,11},{10,... | collective-permute-start | bytes 1179656 | tf_op jit(solution)/shard_map/ppermute | solution.py:233
  164.0 9.0 %collective-permute-start.24 = (bf16[16,2176]{1,0:T(8,128)(2,1)}, bf16[16,2176]{1,0:T(8,128)(2,1)}, u32[]{:S(2)}, u32[]{:S(2)}) collective-permute-start(bf16[16,2176]{1,0:T(8,128)(2,1)} %get-tuple-element.137), channel_id=1, source_target_pairs={{0,16},{8,24},{16,0},{24,8},{1,17},{9,25},{17,1},{25,9},{2,18},{10... | collective-permute-start | bytes 208904 | tf_op jit(solution)/shard_map/ppermute | solution.py:233
  165.6 62.7 %collective-permute-start.23 = (bf16[512,2176]{1,0:T(8,128)(2,1)}, bf16[512,2176]{1,0:T(8,128)(2,1)}, u32[]{:S(2)}, u32[]{:S(2)}) collective-permute-start(bf16[512,2176]{1,0:T(8,128)(2,1)} %weight_part.5), channel_id=1, source_target_pairs={{0,8},{8,0},{16,24},{24,16},{1,9},{9,1},{17,25},{25,17},{2,10},{10... | collective-permute-start | bytes 6684680 | tf_op jit(solution)/shard_map/ppermute | solution.py:233
  173.0 55.3 %collective-permute-start.25 = (bf16[496,2176]{1,0:T(8,128)(2,1)}, bf16[496,2176]{1,0:T(8,128)(2,1)}, u32[]{:S(2)}, u32[]{:S(2)}) collective-permute-start(bf16[496,2176]{1,0:T(8,128)(2,1)} %get-tuple-element.140), channel_id=1, source_target_pairs={{0,16},{8,24},{16,0},{24,8},{1,17},{9,25},{17,1},{25,9},{2,18},{10... | collective-permute-start | bytes 6475784 | tf_op jit(solution)/shard_map/ppermute | solution.py:233
  174.5 22.6 %collective-permute-start.19 = (bf16[48,4096]{1,0:T(8,128)(2,1)}, bf16[48,4096]{1,0:T(8,128)(2,1)}, u32[]{:S(2)}, u32[]{:S(2)}) collective-permute-start(bf16[48,4096]{1,0:T(8,128)(2,1)} %get-tuple-element.119), channel_id=1, source_target_pairs={{0,3},{1,6},{2,5},{3,0},{4,7},{5,2},{6,1},{7,4},{8,11},{9,14},{10,... | collective-permute-start | bytes 1179656 | tf_op jit(solution)/shard_map/ppermute | solution.py:233
  175.0 31.7 %collective-permute-start.18 = (bf16[48,4096]{1,0:T(8,128)(2,1)}, bf16[48,4096]{1,0:T(8,128)(2,1)}, u32[]{:S(2)}, u32[]{:S(2)}) collective-permute-start(bf16[48,4096]{1,0:T(8,128)(2,1)} %get-tuple-element.117), channel_id=1, source_target_pairs={{0,7},{1,2},{2,1},{3,4},{4,3},{5,6},{6,5},{7,0},{8,15},{9,10},{10,... | collective-permute-start | bytes 1179656 | tf_op jit(solution)/shard_map/ppermute | solution.py:233
  178.8 37.0 %collective-permute-start.20 = (bf16[48,4096]{1,0:T(8,128)(2,1)}, bf16[48,4096]{1,0:T(8,128)(2,1)}, u32[]{:S(2)}, u32[]{:S(2)}) collective-permute-start(bf16[48,4096]{1,0:T(8,128)(2,1)} %get-tuple-element.121), channel_id=1, source_target_pairs={{0,4},{1,5},{2,6},{3,7},{4,0},{5,1},{6,2},{7,3},{8,12},{9,13},{10,... | collective-permute-start | bytes 1179656 | tf_op jit(solution)/shard_map/ppermute | solution.py:233
  197.1 19.1 %collective-permute-start.26 = (bf16[16,4096]{1,0:T(8,128)(2,1)}, bf16[16,4096]{1,0:T(8,128)(2,1)}, u32[]{:S(2)}, u32[]{:S(2)}) collective-permute-start(bf16[16,4096]{1,0:T(8,128)(2,1)} %get-tuple-element.144), channel_id=1, source_target_pairs={{0,5},{1,4},{2,3},{3,2},{4,1},{5,0},{6,7},{7,6},{8,13},{9,12},{10,... | collective-permute-start | bytes 393224 | tf_op jit(solution)/shard_map/ppermute | solution.py:233
  206.7 13.8 %collective-permute-start.27 = (bf16[16,4096]{1,0:T(8,128)(2,1)}, bf16[16,4096]{1,0:T(8,128)(2,1)}, u32[]{:S(2)}, u32[]{:S(2)}) collective-permute-start(bf16[16,4096]{1,0:T(8,128)(2,1)} %get-tuple-element.146), channel_id=1, source_target_pairs={{0,1},{1,0},{2,7},{3,6},{4,5},{5,4},{6,3},{7,2},{8,9},{9,8},{10,15... | collective-permute-start | bytes 393224 | tf_op jit(solution)/shard_map/ppermute | solution.py:233
  215.8 11.9 %collective-permute-start.28 = (bf16[16,4096]{1,0:T(8,128)(2,1)}, bf16[16,4096]{1,0:T(8,128)(2,1)}, u32[]{:S(2)}, u32[]{:S(2)}) collective-permute-start(bf16[16,4096]{1,0:T(8,128)(2,1)} %get-tuple-element.148), channel_id=1, source_target_pairs={{0,6},{1,3},{2,4},{3,1},{4,2},{5,7},{6,0},{7,5},{8,14},{9,11},{10,... | collective-permute-start | bytes 393224 | tf_op jit(solution)/shard_map/ppermute | solution.py:233
  216.2 11.5 %collective-permute-start.29 = (bf16[16,4096]{1,0:T(8,128)(2,1)}, bf16[16,4096]{1,0:T(8,128)(2,1)}, u32[]{:S(2)}, u32[]{:S(2)}) collective-permute-start(bf16[16,4096]{1,0:T(8,128)(2,1)} %get-tuple-element.150), channel_id=1, source_target_pairs={{0,2},{1,7},{2,0},{3,5},{4,6},{5,3},{6,4},{7,1},{8,10},{9,15},{10,... | collective-permute-start | bytes 393224 | tf_op jit(solution)/shard_map/ppermute | solution.py:233
  220.5 14.6 %collective-permute-start.30 = (bf16[16,4096]{1,0:T(8,128)(2,1)}, bf16[16,4096]{1,0:T(8,128)(2,1)}, u32[]{:S(2)}, u32[]{:S(2)}) collective-permute-start(bf16[16,4096]{1,0:T(8,128)(2,1)} %get-tuple-element.152), channel_id=1, source_target_pairs={{0,7},{1,2},{2,1},{3,4},{4,3},{5,6},{6,5},{7,0},{8,15},{9,10},{10,... | collective-permute-start | bytes 393224 | tf_op jit(solution)/shard_map/ppermute | solution.py:233
  227.7 7.5 %collective-permute-start.31 = (bf16[16,4096]{1,0:T(8,128)(2,1)}, bf16[16,4096]{1,0:T(8,128)(2,1)}, u32[]{:S(2)}, u32[]{:S(2)}) collective-permute-start(bf16[16,4096]{1,0:T(8,128)(2,1)} %get-tuple-element.154), channel_id=1, source_target_pairs={{0,3},{1,6},{2,5},{3,0},{4,7},{5,2},{6,1},{7,4},{8,11},{9,14},{10,... | collective-permute-start | bytes 393224 | tf_op jit(solution)/shard_map/ppermute | solution.py:233
  227.7 9.4 %collective-permute-start.32 = (bf16[16,4096]{1,0:T(8,128)(2,1)}, bf16[16,4096]{1,0:T(8,128)(2,1)}, u32[]{:S(2)}, u32[]{:S(2)}) collective-permute-start(bf16[16,4096]{1,0:T(8,128)(2,1)} %get-tuple-element.156), channel_id=1, source_target_pairs={{0,4},{1,5},{2,6},{3,7},{4,0},{5,1},{6,2},{7,3},{8,12},{9,13},{10,... | collective-permute-start | bytes 393224 | tf_op jit(solution)/shard_map/ppermute | solution.py:233

commit v12 on v11

--- a/solution.py
+++ b/solution.py
@@ -268,9 +268,8 @@
     experts = lax.axis_size("exp")
     groups = lax.axis_size("grp")
     capacity = 2 * rows // experts
-    first = capacity * 3 // 4
-    cuts = [(0, first), (first, capacity - first)] if capacity % 64 == 0 else [(0, capacity)]
-    parts = len(cuts)
+    parts = 2 if capacity % 32 == 0 else 1
+    cuts = [(part * capacity // parts, capacity // parts) for part in range(parts)]
     weight_one = gate_up_weight[0]
     weight_two = down_weight[0]
     wide = weight_two.shape[0]
@@ -359,7 +358,7 @@
 
     received = {q: [] for q in range(groups)}
     sums = kept[0][0]
-    held = {groups - 1: done[:2], 2: done[2:4]}
+    held = {groups - 1: done[:5], 2: done[5:7]}
     for q in sorted(range(1, groups), key=lambda q: (q & -q, -q)):
         low = q & -q
         sent = weight_part(group ^ q, [[sums, *kept[0][1:]], *kept[1:]], received[q], False, 16 if q in held else 0)

time: 241 us -> 219 us (0.909)
  waiting for transfers between devices: 88.7 us -> 73.8 us
  starting transfers between devices: 92.1 us -> 87.2 us
    ppermute x33, waiting for transfers between devices: 88.7 us -> 73.8 us  [send(): self.done.append(lax.ppermute(after(value, *earlier), axis, pairs))]
    ppermute x33, starting transfers between devices: 92.1 us -> 87.2 us  [send(): self.done.append(lax.ppermute(after(value, *earlier), axis, pairs))]
  transfers between devices with their start and end apart: 33 -> 33, of which waited for: 10 -> 9; matrix products, arithmetic and copies ran while one was open for 0% -> 0% of each run, Pallas kernels for 21% -> 23%
where the time goes in v12:
time: 219 us
  starting transfers between devices  87.2 us (40%)
  waiting for transfers between devices  73.8 us (34%)
  Pallas kernels  56.7 us (26%)
    ppermute x33, starting transfers between devices, send(): self.done.append(lax.ppermute(after(value, *earlier), axis, pairs))  87.2 us
    ppermute x33, waiting for transfers between devices, send(): self.done.append(lax.ppermute(after(value, *earlier), axis, pairs))  73.8 us
    pallas_call x10, Pallas kernels, call(): pl.pallas_call(kernel, in_specs=[pl.BlockSpec(memory_space=pltpu.SMEM)] *...  56.7 us
  transfers between devices with their start and end apart: 33, of which 9 were waited for; matrix products, arithmetic and copies ran while one was open for 0% of the time, Pallas kernels for 23%

profile of v12, /device:TPU:0, one launch (start us, length us, event | category | flops | bytes accessed | tf_op | source)
XLA Modules:
  0.0 218.7 jit_solution(444610356464467395)
XLA Ops:
  0.6 3.4 %place.2 = (bf16[32,4096]{1,0:T(8,128)(2,1)}, bf16[32,4096]{1,0:T(8,128)(2,1)}, bf16[32,4096]{1,0:T(8,128)(2,1)}, bf16[32,4096]{1,0:T(8,128)(2,1)}, bf16[32,4096...) custom-call(s32[1,256]{1,0:T(1,128)} %bitcast.13, ...), custom_call_target="tpu_custom_call" | custom-call | flops 1024 | bytes 1024 | tf_op jit(solution)/shard_map/place/pallas_call | solution.py:28
  4.1 5.1 %collective-permute-start = (bf16[32,4096]{1,0:T(8,128)(2,1)}, bf16[32,4096]{1,0:T(8,128)(2,1)}, u32[]{:S(2)}, u32[]{:S(2)}) collective-permute-start(bf16[32,4096]{1,0:T(8,128)(2,1)} %get-tuple-element.83), channel_id=1, source_target_pairs={{0,5},{1,4},{2,3},{3,2},{4,1},{5,0},{6,7},{7,6},{8,13},{9,12},{10,... | collective-permute-start | bytes 786440 | tf_op jit(solution)/shard_map/ppermute | solution.py:233
  9.1 0.5 collective-permute-start.1
  9.6 1.3 collective-permute-start.2
  11.0 0.2 collective-permute-start.3
  11.2 11.0 %collective-permute-done.refs_1_ = bf16[32,4096]{1,0:T(8,128)(2,1)} collective-permute-done((bf16[32,4096]{1,0:T(8,128)(2,1)}, bf16[32,4096]{1,0:T(8,128)(2,1)}, u32[]{:S(2)}, u32[]{:S(2)}) %collective-permute-start) | collective-permute-done | bytes 262176 | tf_op jit(solution)/shard_map/ppermute | solution.py:233
  22.2 0.0 collective-permute-start.4
  22.2 0.0 collective-permute-done.1.refs_2_
  22.2 7.0 %collective-permute-start.5 = (bf16[32,4096]{1,0:T(8,128)(2,1)}, bf16[32,4096]{1,0:T(8,128)(2,1)}, u32[]{:S(2)}, u32[]{:S(2)}) collective-permute-start(bf16[32,4096]{1,0:T(8,128)(2,1)} %get-tuple-element.90), channel_id=1, source_target_pairs={{0,3},{1,6},{2,5},{3,0},{4,7},{5,2},{6,1},{7,4},{8,11},{9,14},{10,... | collective-permute-start | bytes 786440 | tf_op jit(solution)/shard_map/ppermute | solution.py:233
  29.2 0.0 collective-permute-done.2.refs_3_
  29.2 11.7 %collective-permute-start.6 = (bf16[32,4096]{1,0:T(8,128)(2,1)}, bf16[32,4096]{1,0:T(8,128)(2,1)}, u32[]{:S(2)}, u32[]{:S(2)}) collective-permute-start(bf16[32,4096]{1,0:T(8,128)(2,1)} %get-tuple-element.92), channel_id=1, source_target_pairs={{0,4},{1,5},{2,6},{3,7},{4,0},{5,1},{6,2},{7,3},{8,12},{9,13},{10,... | collective-permute-start | bytes 786440 | tf_op jit(solution)/shard_map/ppermute | solution.py:233
  41.0 3.4 %place.3 = (bf16[32,4096]{1,0:T(8,128)(2,1)}, bf16[32,4096]{1,0:T(8,128)(2,1)}, bf16[32,4096]{1,0:T(8,128)(2,1)}, bf16[32,4096]{1,0:T(8,128)(2,1)}, bf16[32,4096...) custom-call(s32[1,256]{1,0:T(1,128)} %bitcast.14, ...), custom_call_target="tpu_custom_call" | custom-call | flops 1024 | bytes 1024 | tf_op jit(solution)/shard_map/place/pallas_call | solution.py:28
  44.4 0.0 collective-permute-done.3.refs_4_
  44.5 0.1 collective-permute-start.9
  44.5 0.0 collective-permute-done.4.refs_5_
  44.5 1.4 collective-permute-start.12
  46.0 0.0 collective-permute-done.5.refs_6_
  46.0 12.3 %collective-permute-start.15 = (bf16[32,4096]{1,0:T(8,128)(2,1)}, bf16[32,4096]{1,0:T(8,128)(2,1)}, u32[]{:S(2)}, u32[]{:S(2)}) collective-permute-start(bf16[32,4096]{1,0:T(8,128)(2,1)} %get-tuple-element.113), channel_id=1, source_target_pairs={{0,6},{1,3},{2,4},{3,1},{4,2},{5,7},{6,0},{7,5},{8,14},{9,11},{10,... | collective-permute-start | bytes 786440 | tf_op jit(solution)/shard_map/ppermute | solution.py:233
  58.3 0.0 collective-permute-done.6.refs_7_
  58.3 8.9 %collective-permute-start.7 = (bf16[32,4096]{1,0:T(8,128)(2,1)}, bf16[32,4096]{1,0:T(8,128)(2,1)}, u32[]{:S(2)}, u32[]{:S(2)}) collective-permute-start(bf16[32,4096]{1,0:T(8,128)(2,1)} %get-tuple-element.96), channel_id=1, source_target_pairs={{0,2},{1,7},{2,0},{3,5},{4,6},{5,3},{6,4},{7,1},{8,10},{9,15},{10,... | collective-permute-start | bytes 786440 | tf_op jit(solution)/shard_map/ppermute | solution.py:233
  67.2 8.5 %collective-permute-done.9.refs_1_ = bf16[32,4096]{1,0:T(8,128)(2,1)} collective-permute-done((bf16[32,4096]{1,0:T(8,128)(2,1)}, bf16[32,4096]{1,0:T(8,128)(2,1)}, u32[]{:S(2)}, u32[]{:S(2)}) %collective-permute-start.9) | collective-permute-done | bytes 262176 | tf_op jit(solution)/shard_map/ppermute | solution.py:233
  75.7 0.0 collective-permute-start.10
  75.7 10.9 %expert.2 = (bf16[32,4096]{1,0:T(8,128)(2,1)}, bf16[32,4096]{1,0:T(8,128)(2,1)}, bf16[32,4096]{1,0:T(8,128)(2,1)}, bf16[32,4096]{1,0:T(8,128)(2,1)}, bf16[32,409...) custom-call(bf16[32,4096]{1,0:T(8,128)(2,1)} %get-tuple-element.82.r, ...), custom_call_target="tpu_custom_call" | custom-call | flops 1024 | bytes 1024 | tf_op jit(solution)/shard_map/expert/pallas_call | solution.py:28
  86.6 0.0 collective-permute-done.12.refs_2_
  86.6 0.1 collective-permute-start.13
  86.7 0.0 collective-permute-done.15.refs_3_
  86.7 5.3 %collective-permute-start.16 = (bf16[32,4096]{1,0:T(8,128)(2,1)}, bf16[32,4096]{1,0:T(8,128)(2,1)}, u32[]{:S(2)}, u32[]{:S(2)}) collective-permute-start(bf16[32,4096]{1,0:T(8,128)(2,1)} %get-tuple-element.114), channel_id=1, source_target_pairs={{0,4},{1,5},{2,6},{3,7},{4,0},{5,1},{6,2},{7,3},{8,12},{9,13},{10,... | collective-permute-start | bytes 786440 | tf_op jit(solution)/shard_map/ppermute | solution.py:233
  92.0 0.0 collective-permute-done.10.refs_5_
  92.0 1.5 collective-permute-start.11
  93.5 0.9 collective-permute-done.13.refs_6_
  94.3 15.9 %collective-permute-done.16.refs_7_ = bf16[32,4096]{1,0:T(8,128)(2,1)} collective-permute-done((bf16[32,4096]{1,0:T(8,128)(2,1)}, bf16[32,4096]{1,0:T(8,128)(2,1)}, u32[]{:S(2)}, u32[]{:S(2)}) %collective-permute-start.16) | collective-permute-done | bytes 262176 | tf_op jit(solution)/shard_map/ppermute | solution.py:233
  110.2 0.3 collective-permute-start.17
  110.5 2.9 %collective-permute-start.14 = (bf16[32,4096]{1,0:T(8,128)(2,1)}, bf16[32,4096]{1,0:T(8,128)(2,1)}, u32[]{:S(2)}, u32[]{:S(2)}) collective-permute-start(bf16[32,4096]{1,0:T(8,128)(2,1)} %get-tuple-element.109), channel_id=1, source_target_pairs={{0,6},{1,3},{2,4},{3,1},{4,2},{5,7},{6,0},{7,5},{8,14},{9,11},{10,... | collective-permute-start | bytes 786440 | tf_op jit(solution)/shard_map/ppermute | solution.py:233
  113.4 8.5 %collective-permute-done.8.refs_4_ = bf16[32,4096]{1,0:T(8,128)(2,1)} collective-permute-done((bf16[32,4096]{1,0:T(8,128)(2,1)}, bf16[32,4096]{1,0:T(8,128)(2,1)}, u32[]{:S(2)}, u32[]{:S(2)}) %collective-permute-start.8) | collective-permute-done | bytes 262176 | tf_op jit(solution)/shard_map/ppermute | solution.py:233
  121.9 11.1 %expert.3 = (bf16[32,4096]{1,0:T(8,128)(2,1)}, bf16[32,4096]{1,0:T(8,128)(2,1)}, bf16[32,4096]{1,0:T(8,128)(2,1)}, bf16[32,4096]{1,0:T(8,128)(2,1)}, bf16[32,409...) custom-call(bf16[32,4096]{1,0:T(8,128)(2,1)} %get-tuple-element.124., ...), custom_call_target="tpu_custom_call" | custom-call | flops 1024 | bytes 1024 | tf_op jit(solution)/shard_map/expert/pallas_call | solution.py:28
  133.0 4.4 %weight_part.4 = (bf16[16,2176]{1,0:T(8,128)(2,1)}, bf16[496,2176]{1,0:T(8,128)(2,1)}) custom-call(s32[1]{0:T(128)} %bitcast.4.refs_0_, bf16[256,4096]{1,0:T(8,128)(2,1)} %get-tuple-element.138.refs_1_, bf16[256,1408]{1,0:T(8,128)(2,1)} %get-tuple-element.127.refs_2_, bf16[256,704]{1,0:T(8,128)(2,1)} %get-tuple-element.128.refs_3_, ...), custom_call_target="tpu_custom_call" | custom-call | flops 1024 | bytes 1024 | tf_op jit(solution)/shard_map/weight_part/pallas_call | solution.py:28
  137.4 0.1 collective-permute-start.21
  137.5 1.6 collective-permute-done.21.refs_7_
  139.0 0.0 collective-permute-done.14.refs_6_
  139.1 0.0 collective-permute-done.18.refs_8_
  139.1 0.2 collective-permute-start.22
  139.3 5.3 %collective-permute-start.20 = (bf16[32,4096]{1,0:T(8,128)(2,1)}, bf16[32,4096]{1,0:T(8,128)(2,1)}, u32[]{:S(2)}, u32[]{:S(2)}) collective-permute-start(bf16[32,4096]{1,0:T(8,128)(2,1)} %get-tuple-element.121), channel_id=1, source_target_pairs={{0,4},{1,5},{2,6},{3,7},{4,0},{5,1},{6,2},{7,3},{8,12},{9,13},{10,... | collective-permute-start | bytes 786440 | tf_op jit(solution)/shard_map/ppermute | solution.py:233
  144.6 4.3 %weight_part.5 = bf16[512,2176]{1,0:T(8,128)(2,1)} custom-call(s32[1]{0:T(128)} %bitcast.5.refs_0_, bf16[256,4096]{1,0:T(8,128)(2,1)} %get-tuple-element.138.refs_1_, bf16[256,1408]{1,0:T(8,128)(2,1)} %get-tuple-element.127.refs_2_, bf16[256,704]{1,0:T(8,128)(2,1)} %get-tuple-element.128.refs_3_, bf16[256,4096]{1,0:T(8,128)(2,1)} %get-tuple-element.129.refs_4_, ...), custom_call_target="tpu_custom_call" | custom-call | flops 1024 | bytes 1024 | tf_op jit(solution)/shard_map/weight_part/pallas_call | solution.py:28
  148.9 5.2 %weight_part.6 = (bf16[16,2176]{1,0:T(8,128)(2,1)}, bf16[496,2176]{1,0:T(8,128)(2,1)}) custom-call(s32[1]{0:T(128)} %bitcast.6.refs_0_, bf16[256,4096]{1,0:T(8,128)(2,1)} %get-tuple-element.138.refs_1_, bf16[256,1408]{1,0:T(8,128)(2,1)} %get-tuple-element.127.refs_2_, bf16[256,704]{1,0:T(8,128)(2,1)} %get-tuple-element.128.refs_3_, ...), custom_call_target="tpu_custom_call" | custom-call | flops 1024 | bytes 1024 | tf_op jit(solution)/shard_map/weight_part/pallas_call | solution.py:28
  154.1 1.7 collective-permute-start.24
  155.8 0.0 collective-permute-start.23
  155.8 0.0 collective-permute-done.19.refs_9_
  155.8 3.1 %collective-permute-done.20.refs_10_ = bf16[32,4096]{1,0:T(8,128)(2,1)} collective-permute-done((bf16[32,4096]{1,0:T(8,128)(2,1)}, bf16[32,4096]{1,0:T(8,128)(2,1)}, u32[]{:S(2)}, u32[]{:S(2)}) %collective-permute-start.20) | collective-permute-done | bytes 262176 | tf_op jit(solution)/shard_map/ppermute | solution.py:233
  158.9 1.5 collective-permute-start.25
  160.4 1.1 collective-permute-start.27
  161.5 0.3 collective-permute-start.26
  161.9 2.9 %collective-permute-start.28 = (bf16[32,4096]{1,0:T(8,128)(2,1)}, bf16[32,4096]{1,0:T(8,128)(2,1)}, u32[]{:S(2)}, u32[]{:S(2)}) collective-permute-start(bf16[32,4096]{1,0:T(8,128)(2,1)} %get-tuple-element.148), channel_id=1, source_target_pairs={{0,6},{1,3},{2,4},{3,1},{4,2},{5,7},{6,0},{7,5},{8,14},{9,11},{10,... | collective-permute-start | bytes 786440 | tf_op jit(solution)/shard_map/ppermute | solution.py:233
  164.8 4.0 %collective-permute-done.27.refs_5_ = bf16[32,4096]{1,0:T(8,128)(2,1)} collective-permute-done((bf16[32,4096]{1,0:T(8,128)(2,1)}, bf16[32,4096]{1,0:T(8,128)(2,1)}, u32[]{:S(2)}, u32[]{:S(2)}) %collective-permute-start.27) | collective-permute-done | bytes 262176 | tf_op jit(solution)/shard_map/ppermute | solution.py:233
  168.8 11.0 %collective-permute-start.29 = (bf16[32,4096]{1,0:T(8,128)(2,1)}, bf16[32,4096]{1,0:T(8,128)(2,1)}, u32[]{:S(2)}, u32[]{:S(2)}) collective-permute-start(bf16[32,4096]{1,0:T(8,128)(2,1)} %get-tuple-element.150), channel_id=1, source_target_pairs={{0,2},{1,7},{2,0},{3,5},{4,6},{5,3},{6,4},{7,1},{8,10},{9,15},{10,... | collective-permute-start | bytes 786440 | tf_op jit(solution)/shard_map/ppermute | solution.py:233
  179.8 3.6 %combine.2 = (bf16[256,2048]{1,0:T(8,128)(2,1)}, bf16[256,2048]{1,0:T(8,128)(2,1)}) custom-call(s32[1,256]{1,0:T(1,128)} %bitcast.15, bf16[256,2048]{1,0:T(8,128)(2,1)} %refs_1_.5, bf16[256,2048]{1,0:T(8,128)(2,1)} %refs_2_.5, bf16[32,4096]{1,0:T(8,128)(2,1)} %get-tuple-element.93.refs_3_, bf16[32,4096]{1,0:T(8,128)(2,1)} %collective-permute-done.8.refs_4_, ...), custom_call_target="tpu_custom_call" | custom-call | flops 1024 | bytes 1024 | tf_op jit(solution)/shard_map/combine/pallas_call | solution.py:28
  183.5 0.1 collective-permute-start.31
  183.5 0.0 collective-permute-done.28.refs_6_
  183.6 3.8 %collective-permute-start.30 = (bf16[32,4096]{1,0:T(8,128)(2,1)}, bf16[32,4096]{1,0:T(8,128)(2,1)}, u32[]{:S(2)}, u32[]{:S(2)}) collective-permute-start(bf16[32,4096]{1,0:T(8,128)(2,1)} %get-tuple-element.152), channel_id=1, source_target_pairs={{0,7},{1,2},{2,1},{3,4},{4,3},{5,6},{6,5},{7,0},{8,15},{9,10},{10,... | collective-permute-start | bytes 786440 | tf_op jit(solution)/shard_map/ppermute | solution.py:233
  187.3 0.0 collective-permute-done.29.refs_7_
  187.4 0.6 collective-permute-start.32
  187.9 20.2 %collective-permute-done.25.refs_9_ = bf16[496,2176]{1,0:T(8,128)(2,1)} collective-permute-done((bf16[496,2176]{1,0:T(8,128)(2,1)}, bf16[496,2176]{1,0:T(8,128)(2,1)}, u32[]{:S(2)}, u32[]{:S(2)}) %collective-permute-start.25) | collective-permute-done | bytes 2158624 | tf_op jit(solution)/shard_map/ppermute | solution.py:233
  208.1 6.8 %weight_part.7 = (f32[512,1408]{1,0:T(8,128)}, f32[704,512]{1,0:T(8,128)}) custom-call(s32[1]{0:T(128)} %bitcast.3.refs_0_, bf16[256,4096]{1,0:T(8,128)(2,1)} %get-tuple-element.138.refs_1_, bf16[256,1408]{1,0:T(8,128)(2,1)} %get-tuple-element.127.refs_2_, bf16[256,704]{1,0:T(8,128)(2,1)} %get-tuple-element.128.refs_3_, ...), custom_call_target="tpu_custom_call" | custom-call | flops 1024 | bytes 1024 | tf_op jit(solution)/shard_map/weight_part/pallas_call | solution.py:28
  214.9 0.0 collective-permute-done.32.refs_10_
  214.9 3.6 %combine.3 = (bf16[256,2048]{1,0:T(8,128)(2,1)}, bf16[256,2048]{1,0:T(8,128)(2,1)}) custom-call(s32[1,256]{1,0:T(1,128)} %bitcast.16, bf16[256,2048]{1,0:T(8,128)(2,1)} %get-tuple-element.122.refs_1_, bf16[256,2048]{1,0:T(8,128)(2,1)} %get-tuple-element.123.refs_2_, bf16[32,4096]{1,0:T(8,128)(2,1)} %get-tuple-element.142.refs_3_, ...), custom_call_target="tpu_custom_call" | custom-call | flops 1024 | bytes 1024 | tf_op jit(solution)/shard_map/combine/pallas_call | solution.py:28
  (12 shorter events, 0.0 us)
Async XLA Ops:
  4.1 18.2 %collective-permute-start = (bf16[32,4096]{1,0:T(8,128)(2,1)}, bf16[32,4096]{1,0:T(8,128)(2,1)}, u32[]{:S(2)}, u32[]{:S(2)}) collective-permute-start(bf16[32,4096]{1,0:T(8,128)(2,1)} %get-tuple-element.83), channel_id=1, source_target_pairs={{0,5},{1,4},{2,3},{3,2},{4,1},{5,0},{6,7},{7,6},{8,13},{9,12},{10,... | collective-permute-start | bytes 786440 | tf_op jit(solution)/shard_map/ppermute | solution.py:233
  9.1 13.1 %collective-permute-start.1 = (bf16[32,4096]{1,0:T(8,128)(2,1)}, bf16[32,4096]{1,0:T(8,128)(2,1)}, u32[]{:S(2)}, u32[]{:S(2)}) collective-permute-start(bf16[32,4096]{1,0:T(8,128)(2,1)} %get-tuple-element.84), channel_id=1, source_target_pairs={{0,1},{1,0},{2,7},{3,6},{4,5},{5,4},{6,3},{7,2},{8,9},{9,8},{10,15... | collective-permute-start | bytes 786440 | tf_op jit(solution)/shard_map/ppermute | solution.py:233
  9.6 19.6 %collective-permute-start.2 = (bf16[32,4096]{1,0:T(8,128)(2,1)}, bf16[32,4096]{1,0:T(8,128)(2,1)}, u32[]{:S(2)}, u32[]{:S(2)}) collective-permute-start(bf16[32,4096]{1,0:T(8,128)(2,1)} %get-tuple-element.85), channel_id=1, source_target_pairs={{0,6},{1,3},{2,4},{3,1},{4,2},{5,7},{6,0},{7,5},{8,14},{9,11},{10,... | collective-permute-start | bytes 786440 | tf_op jit(solution)/shard_map/ppermute | solution.py:233
  11.0 33.5 %collective-permute-start.3 = (bf16[32,4096]{1,0:T(8,128)(2,1)}, bf16[32,4096]{1,0:T(8,128)(2,1)}, u32[]{:S(2)}, u32[]{:S(2)}) collective-permute-start(bf16[32,4096]{1,0:T(8,128)(2,1)} %get-tuple-element.86), channel_id=1, source_target_pairs={{0,2},{1,7},{2,0},{3,5},{4,6},{5,3},{6,4},{7,1},{8,10},{9,15},{10,... | collective-permute-start | bytes 786440 | tf_op jit(solution)/shard_map/ppermute | solution.py:233
  22.2 22.3 %collective-permute-start.4 = (bf16[32,4096]{1,0:T(8,128)(2,1)}, bf16[32,4096]{1,0:T(8,128)(2,1)}, u32[]{:S(2)}, u32[]{:S(2)}) collective-permute-start(bf16[32,4096]{1,0:T(8,128)(2,1)} %get-tuple-element.88), channel_id=1, source_target_pairs={{0,7},{1,2},{2,1},{3,4},{4,3},{5,6},{6,5},{7,0},{8,15},{9,10},{10,... | collective-permute-start | bytes 786440 | tf_op jit(solution)/shard_map/ppermute | solution.py:233
  22.2 23.7 %collective-permute-start.5 = (bf16[32,4096]{1,0:T(8,128)(2,1)}, bf16[32,4096]{1,0:T(8,128)(2,1)}, u32[]{:S(2)}, u32[]{:S(2)}) collective-permute-start(bf16[32,4096]{1,0:T(8,128)(2,1)} %get-tuple-element.90), channel_id=1, source_target_pairs={{0,3},{1,6},{2,5},{3,0},{4,7},{5,2},{6,1},{7,4},{8,11},{9,14},{10,... | collective-permute-start | bytes 786440 | tf_op jit(solution)/shard_map/ppermute | solution.py:233
  29.2 29.0 %collective-permute-start.6 = (bf16[32,4096]{1,0:T(8,128)(2,1)}, bf16[32,4096]{1,0:T(8,128)(2,1)}, u32[]{:S(2)}, u32[]{:S(2)}) collective-permute-start(bf16[32,4096]{1,0:T(8,128)(2,1)} %get-tuple-element.92), channel_id=1, source_target_pairs={{0,4},{1,5},{2,6},{3,7},{4,0},{5,1},{6,2},{7,3},{8,12},{9,13},{10,... | collective-permute-start | bytes 786440 | tf_op jit(solution)/shard_map/ppermute | solution.py:233
  44.5 31.2 %collective-permute-start.9 = (bf16[32,4096]{1,0:T(8,128)(2,1)}, bf16[32,4096]{1,0:T(8,128)(2,1)}, u32[]{:S(2)}, u32[]{:S(2)}) collective-permute-start(bf16[32,4096]{1,0:T(8,128)(2,1)} %get-tuple-element.101), channel_id=1, source_target_pairs={{0,5},{1,4},{2,3},{3,2},{4,1},{5,0},{6,7},{7,6},{8,13},{9,12},{10,... | collective-permute-start | bytes 786440 | tf_op jit(solution)/shard_map/ppermute | solution.py:233
  44.5 42.0 %collective-permute-start.12 = (bf16[32,4096]{1,0:T(8,128)(2,1)}, bf16[32,4096]{1,0:T(8,128)(2,1)}, u32[]{:S(2)}, u32[]{:S(2)}) collective-permute-start(bf16[32,4096]{1,0:T(8,128)(2,1)} %get-tuple-element.107), channel_id=1, source_target_pairs={{0,1},{1,0},{2,7},{3,6},{4,5},{5,4},{6,3},{7,2},{8,9},{9,8},{10,15... | collective-permute-start | bytes 786440 | tf_op jit(solution)/shard_map/ppermute | solution.py:233
  46.0 40.7 %collective-permute-start.15 = (bf16[32,4096]{1,0:T(8,128)(2,1)}, bf16[32,4096]{1,0:T(8,128)(2,1)}, u32[]{:S(2)}, u32[]{:S(2)}) collective-permute-start(bf16[32,4096]{1,0:T(8,128)(2,1)} %get-tuple-element.113), channel_id=1, source_target_pairs={{0,6},{1,3},{2,4},{3,1},{4,2},{5,7},{6,0},{7,5},{8,14},{9,11},{10,... | collective-permute-start | bytes 786440 | tf_op jit(solution)/shard_map/ppermute | solution.py:233
  58.3 33.7 %collective-permute-start.7 = (bf16[32,4096]{1,0:T(8,128)(2,1)}, bf16[32,4096]{1,0:T(8,128)(2,1)}, u32[]{:S(2)}, u32[]{:S(2)}) collective-permute-start(bf16[32,4096]{1,0:T(8,128)(2,1)} %get-tuple-element.96), channel_id=1, source_target_pairs={{0,2},{1,7},{2,0},{3,5},{4,6},{5,3},{6,4},{7,1},{8,10},{9,15},{10,... | collective-permute-start | bytes 786440 | tf_op jit(solution)/shard_map/ppermute | solution.py:233
  75.7 16.3 %collective-permute-start.10 = (bf16[32,4096]{1,0:T(8,128)(2,1)}, bf16[32,4096]{1,0:T(8,128)(2,1)}, u32[]{:S(2)}, u32[]{:S(2)}) collective-permute-start(bf16[32,4096]{1,0:T(8,128)(2,1)} %get-tuple-element.102), channel_id=1, source_target_pairs={{0,7},{1,2},{2,1},{3,4},{4,3},{5,6},{6,5},{7,0},{8,15},{9,10},{10,... | collective-permute-start | bytes 786440 | tf_op jit(solution)/shard_map/ppermute | solution.py:233
  86.6 7.8 %collective-permute-start.13 = (bf16[32,4096]{1,0:T(8,128)(2,1)}, bf16[32,4096]{1,0:T(8,128)(2,1)}, u32[]{:S(2)}, u32[]{:S(2)}) collective-permute-start(bf16[32,4096]{1,0:T(8,128)(2,1)} %get-tuple-element.108), channel_id=1, source_target_pairs={{0,3},{1,6},{2,5},{3,0},{4,7},{5,2},{6,1},{7,4},{8,11},{9,14},{10,... | collective-permute-start | bytes 786440 | tf_op jit(solution)/shard_map/ppermute | solution.py:233
  86.7 23.6 %collective-permute-start.16 = (bf16[32,4096]{1,0:T(8,128)(2,1)}, bf16[32,4096]{1,0:T(8,128)(2,1)}, u32[]{:S(2)}, u32[]{:S(2)}) collective-permute-start(bf16[32,4096]{1,0:T(8,128)(2,1)} %get-tuple-element.114), channel_id=1, source_target_pairs={{0,4},{1,5},{2,6},{3,7},{4,0},{5,1},{6,2},{7,3},{8,12},{9,13},{10,... | collective-permute-start | bytes 786440 | tf_op jit(solution)/shard_map/ppermute | solution.py:233
  91.9 30.0 %collective-permute-start.8 = (bf16[32,4096]{1,0:T(8,128)(2,1)}, bf16[32,4096]{1,0:T(8,128)(2,1)}, u32[]{:S(2)}, u32[]{:S(2)}) collective-permute-start(bf16[32,4096]{1,0:T(8,128)(2,1)} %get-tuple-element.97), channel_id=1, source_target_pairs={{0,5},{1,4},{2,3},{3,2},{4,1},{5,0},{6,7},{7,6},{8,13},{9,12},{10,... | collective-permute-start | bytes 786440 | tf_op jit(solution)/shard_map/ppermute | solution.py:233
  92.0 45.5 %collective-permute-start.11 = (bf16[32,4096]{1,0:T(8,128)(2,1)}, bf16[32,4096]{1,0:T(8,128)(2,1)}, u32[]{:S(2)}, u32[]{:S(2)}) collective-permute-start(bf16[32,4096]{1,0:T(8,128)(2,1)} %get-tuple-element.103), channel_id=1, source_target_pairs={{0,1},{1,0},{2,7},{3,6},{4,5},{5,4},{6,3},{7,2},{8,9},{9,8},{10,15... | collective-permute-start | bytes 786440 | tf_op jit(solution)/shard_map/ppermute | solution.py:233
  110.2 28.8 %collective-permute-start.17 = (bf16[32,4096]{1,0:T(8,128)(2,1)}, bf16[32,4096]{1,0:T(8,128)(2,1)}, u32[]{:S(2)}, u32[]{:S(2)}) collective-permute-start(bf16[32,4096]{1,0:T(8,128)(2,1)} %get-tuple-element.115), channel_id=1, source_target_pairs={{0,2},{1,7},{2,0},{3,5},{4,6},{5,3},{6,4},{7,1},{8,10},{9,15},{10,... | collective-permute-start | bytes 786440 | tf_op jit(solution)/shard_map/ppermute | solution.py:233
  110.5 28.5 %collective-permute-start.14 = (bf16[32,4096]{1,0:T(8,128)(2,1)}, bf16[32,4096]{1,0:T(8,128)(2,1)}, u32[]{:S(2)}, u32[]{:S(2)}) collective-permute-start(bf16[32,4096]{1,0:T(8,128)(2,1)} %get-tuple-element.109), channel_id=1, source_target_pairs={{0,6},{1,3},{2,4},{3,1},{4,2},{5,7},{6,0},{7,5},{8,14},{9,11},{10,... | collective-permute-start | bytes 786440 | tf_op jit(solution)/shard_map/ppermute | solution.py:233
  121.9 17.1 %collective-permute-start.18 = (bf16[32,4096]{1,0:T(8,128)(2,1)}, bf16[32,4096]{1,0:T(8,128)(2,1)}, u32[]{:S(2)}, u32[]{:S(2)}) collective-permute-start(bf16[32,4096]{1,0:T(8,128)(2,1)} %get-tuple-element.117), channel_id=1, source_target_pairs={{0,7},{1,2},{2,1},{3,4},{4,3},{5,6},{6,5},{7,0},{8,15},{9,10},{10,... | collective-permute-start | bytes 786440 | tf_op jit(solution)/shard_map/ppermute | solution.py:233
  137.4 1.7 collective-permute-start.21
  139.1 9.8 %collective-permute-start.22 = (bf16[496,2176]{1,0:T(8,128)(2,1)}, bf16[496,2176]{1,0:T(8,128)(2,1)}, u32[]{:S(2)}, u32[]{:S(2)}) collective-permute-start(bf16[496,2176]{1,0:T(8,128)(2,1)} %get-tuple-element.136), channel_id=1, source_target_pairs={{0,8},{8,0},{16,24},{24,16},{1,9},{9,1},{17,25},{25,17},{2,10},{10... | collective-permute-start | bytes 6475784 | tf_op jit(solution)/shard_map/ppermute | solution.py:233
  139.3 16.5 %collective-permute-start.19 = (bf16[32,4096]{1,0:T(8,128)(2,1)}, bf16[32,4096]{1,0:T(8,128)(2,1)}, u32[]{:S(2)}, u32[]{:S(2)}) collective-permute-start(bf16[32,4096]{1,0:T(8,128)(2,1)} %get-tuple-element.119), channel_id=1, source_target_pairs={{0,3},{1,6},{2,5},{3,0},{4,7},{5,2},{6,1},{7,4},{8,11},{9,14},{10,... | collective-permute-start | bytes 786440 | tf_op jit(solution)/shard_map/ppermute | solution.py:233
  139.3 19.6 %collective-permute-start.20 = (bf16[32,4096]{1,0:T(8,128)(2,1)}, bf16[32,4096]{1,0:T(8,128)(2,1)}, u32[]{:S(2)}, u32[]{:S(2)}) collective-permute-start(bf16[32,4096]{1,0:T(8,128)(2,1)} %get-tuple-element.121), channel_id=1, source_target_pairs={{0,4},{1,5},{2,6},{3,7},{4,0},{5,1},{6,2},{7,3},{8,12},{9,13},{10,... | collective-permute-start | bytes 786440 | tf_op jit(solution)/shard_map/ppermute | solution.py:233
  154.1 4.8 %collective-permute-start.24 = (bf16[16,2176]{1,0:T(8,128)(2,1)}, bf16[16,2176]{1,0:T(8,128)(2,1)}, u32[]{:S(2)}, u32[]{:S(2)}) collective-permute-start(bf16[16,2176]{1,0:T(8,128)(2,1)} %get-tuple-element.137), channel_id=1, source_target_pairs={{0,16},{8,24},{16,0},{24,8},{1,17},{9,25},{17,1},{25,9},{2,18},{10... | collective-permute-start | bytes 208904 | tf_op jit(solution)/shard_map/ppermute | solution.py:233
  155.8 32.2 %collective-permute-start.23 = (bf16[512,2176]{1,0:T(8,128)(2,1)}, bf16[512,2176]{1,0:T(8,128)(2,1)}, u32[]{:S(2)}, u32[]{:S(2)}) collective-permute-start(bf16[512,2176]{1,0:T(8,128)(2,1)} %weight_part.5), channel_id=1, source_target_pairs={{0,8},{8,0},{16,24},{24,16},{1,9},{9,1},{17,25},{25,17},{2,10},{10... | collective-permute-start | bytes 6684680 | tf_op jit(solution)/shard_map/ppermute | solution.py:233
  158.9 49.2 %collective-permute-start.25 = (bf16[496,2176]{1,0:T(8,128)(2,1)}, bf16[496,2176]{1,0:T(8,128)(2,1)}, u32[]{:S(2)}, u32[]{:S(2)}) collective-permute-start(bf16[496,2176]{1,0:T(8,128)(2,1)} %get-tuple-element.140), channel_id=1, source_target_pairs={{0,16},{8,24},{16,0},{24,8},{1,17},{9,25},{17,1},{25,9},{2,18},{10... | collective-permute-start | bytes 6475784 | tf_op jit(solution)/shard_map/ppermute | solution.py:233
  160.4 8.4 %collective-permute-start.27 = (bf16[32,4096]{1,0:T(8,128)(2,1)}, bf16[32,4096]{1,0:T(8,128)(2,1)}, u32[]{:S(2)}, u32[]{:S(2)}) collective-permute-start(bf16[32,4096]{1,0:T(8,128)(2,1)} %get-tuple-element.146), channel_id=1, source_target_pairs={{0,1},{1,0},{2,7},{3,6},{4,5},{5,4},{6,3},{7,2},{8,9},{9,8},{10,15... | collective-permute-start | bytes 786440 | tf_op jit(solution)/shard_map/ppermute | solution.py:233
  161.5 21.9 %collective-permute-start.26 = (bf16[32,4096]{1,0:T(8,128)(2,1)}, bf16[32,4096]{1,0:T(8,128)(2,1)}, u32[]{:S(2)}, u32[]{:S(2)}) collective-permute-start(bf16[32,4096]{1,0:T(8,128)(2,1)} %get-tuple-element.144), channel_id=1, source_target_pairs={{0,5},{1,4},{2,3},{3,2},{4,1},{5,0},{6,7},{7,6},{8,13},{9,12},{10,... | collective-permute-start | bytes 786440 | tf_op jit(solution)/shard_map/ppermute | solution.py:233
  161.9 21.7 %collective-permute-start.28 = (bf16[32,4096]{1,0:T(8,128)(2,1)}, bf16[32,4096]{1,0:T(8,128)(2,1)}, u32[]{:S(2)}, u32[]{:S(2)}) collective-permute-start(bf16[32,4096]{1,0:T(8,128)(2,1)} %get-tuple-element.148), channel_id=1, source_target_pairs={{0,6},{1,3},{2,4},{3,1},{4,2},{5,7},{6,0},{7,5},{8,14},{9,11},{10,... | collective-permute-start | bytes 786440 | tf_op jit(solution)/shard_map/ppermute | solution.py:233
  168.8 18.5 %collective-permute-start.29 = (bf16[32,4096]{1,0:T(8,128)(2,1)}, bf16[32,4096]{1,0:T(8,128)(2,1)}, u32[]{:S(2)}, u32[]{:S(2)}) collective-permute-start(bf16[32,4096]{1,0:T(8,128)(2,1)} %get-tuple-element.150), channel_id=1, source_target_pairs={{0,2},{1,7},{2,0},{3,5},{4,6},{5,3},{6,4},{7,1},{8,10},{9,15},{10,... | collective-permute-start | bytes 786440 | tf_op jit(solution)/shard_map/ppermute | solution.py:233
  183.5 31.4 %collective-permute-start.31 = (bf16[32,4096]{1,0:T(8,128)(2,1)}, bf16[32,4096]{1,0:T(8,128)(2,1)}, u32[]{:S(2)}, u32[]{:S(2)}) collective-permute-start(bf16[32,4096]{1,0:T(8,128)(2,1)} %get-tuple-element.154), channel_id=1, source_target_pairs={{0,3},{1,6},{2,5},{3,0},{4,7},{5,2},{6,1},{7,4},{8,11},{9,14},{10,... | collective-permute-start | bytes 786440 | tf_op jit(solution)/shard_map/ppermute | solution.py:233
  183.6 31.4 %collective-permute-start.30 = (bf16[32,4096]{1,0:T(8,128)(2,1)}, bf16[32,4096]{1,0:T(8,128)(2,1)}, u32[]{:S(2)}, u32[]{:S(2)}) collective-permute-start(bf16[32,4096]{1,0:T(8,128)(2,1)} %get-tuple-element.152), channel_id=1, source_target_pairs={{0,7},{1,2},{2,1},{3,4},{4,3},{5,6},{6,5},{7,0},{8,15},{9,10},{10,... | collective-permute-start | bytes 786440 | tf_op jit(solution)/shard_map/ppermute | solution.py:233
  187.4 27.6 %collective-permute-start.32 = (bf16[32,4096]{1,0:T(8,128)(2,1)}, bf16[32,4096]{1,0:T(8,128)(2,1)}, u32[]{:S(2)}, u32[]{:S(2)}) collective-permute-start(bf16[32,4096]{1,0:T(8,128)(2,1)} %get-tuple-element.156), channel_id=1, source_target_pairs={{0,4},{1,5},{2,6},{3,7},{4,0},{5,1},{6,2},{7,3},{8,12},{9,13},{10,... | collective-permute-start | bytes 786440 | tf_op jit(solution)/shard_map/ppermute | solution.py:233

commit v13 on v12

--- a/solution.py
+++ b/solution.py
@@ -353,12 +353,13 @@
         if back:
             mixed, grad = combine(*cuts[part - 1], mixed, grad, back)
         blocks = results[part][0]
+        lane.window = 4 if part else 5
         back = [blocks[0]] + exchange(blocks, rounds, lane, numbers if part < parts - 1 else numbers[:-1])
     done = lane.done[count:]
 
     received = {q: [] for q in range(groups)}
     sums = kept[0][0]
-    held = {groups - 1: done[:5], 2: done[5:7]}
+    held = {groups - 1: done[:4], 2: done[4:6]}
     for q in sorted(range(1, groups), key=lambda q: (q & -q, -q)):
         low = q & -q
         sent = weight_part(group ^ q, [[sums, *kept[0][1:]], *kept[1:]], received[q], False, 16 if q in held else 0)

time: 219 us -> 211 us (0.963)
  waiting for transfers between devices: 73.8 us -> 57.7 us
  starting transfers between devices: 87.2 us -> 95.7 us
    ppermute x33, waiting for transfers between devices: 73.8 us -> 57.7 us  [send(): self.done.append(lax.ppermute(after(value, *earlier), axis, pairs))]
    ppermute x33, starting transfers between devices: 87.2 us -> 95.7 us  [send(): self.done.append(lax.ppermute(after(value, *earlier), axis, pairs))]
  transfers between devices with their start and end apart: 33 -> 33, of which waited for: 9 -> 11; matrix products, arithmetic and copies ran while one was open for 0% -> 0% of each run, Pallas kernels for 23% -> 24%
where the time goes in v13:
time: 211 us
  starting transfers between devices  95.7 us (45%)
  waiting for transfers between devices  57.7 us (27%)
  Pallas kernels  56.8 us (27%)
    ppermute x33, starting transfers between devices, send(): self.done.append(lax.ppermute(after(value, *earlier), axis, pairs))  95.7 us
    ppermute x33, waiting for transfers between devices, send(): self.done.append(lax.ppermute(after(value, *earlier), axis, pairs))  57.7 us
    pallas_call x10, Pallas kernels, call(): pl.pallas_call(kernel, in_specs=[pl.BlockSpec(memory_space=pltpu.SMEM)] *...  56.8 us
  transfers between devices with their start and end apart: 33, of which 11 were waited for; matrix products, arithmetic and copies ran while one was open for 0% of the time, Pallas kernels for 24%

profile of v13, /device:TPU:0, one launch (start us, length us, event | category | flops | bytes accessed | tf_op | source)
XLA Modules:
  0.0 211.1 jit_solution(16878584009093672610)
XLA Ops:
  0.6 3.4 %place.2 = (bf16[32,4096]{1,0:T(8,128)(2,1)}, bf16[32,4096]{1,0:T(8,128)(2,1)}, bf16[32,4096]{1,0:T(8,128)(2,1)}, bf16[32,4096]{1,0:T(8,128)(2,1)}, bf16[32,4096...) custom-call(s32[1,256]{1,0:T(1,128)} %bitcast.13, ...), custom_call_target="tpu_custom_call" | custom-call | flops 1024 | bytes 1024 | tf_op jit(solution)/shard_map/place/pallas_call | solution.py:28
  4.1 5.1 %collective-permute-start = (bf16[32,4096]{1,0:T(8,128)(2,1)}, bf16[32,4096]{1,0:T(8,128)(2,1)}, u32[]{:S(2)}, u32[]{:S(2)}) collective-permute-start(bf16[32,4096]{1,0:T(8,128)(2,1)} %get-tuple-element.83), channel_id=1, source_target_pairs={{0,5},{1,4},{2,3},{3,2},{4,1},{5,0},{6,7},{7,6},{8,13},{9,12},{10,... | collective-permute-start | bytes 786440 | tf_op jit(solution)/shard_map/ppermute | solution.py:233
  9.1 0.5 collective-permute-start.1
  9.6 1.3 collective-permute-start.2
  11.0 0.2 collective-permute-start.3
  11.2 11.0 %collective-permute-done.refs_1_ = bf16[32,4096]{1,0:T(8,128)(2,1)} collective-permute-done((bf16[32,4096]{1,0:T(8,128)(2,1)}, bf16[32,4096]{1,0:T(8,128)(2,1)}, u32[]{:S(2)}, u32[]{:S(2)}) %collective-permute-start) | collective-permute-done | bytes 262176 | tf_op jit(solution)/shard_map/ppermute | solution.py:233
  22.2 0.0 collective-permute-start.4
  22.2 0.0 collective-permute-done.1.refs_2_
  22.2 7.0 %collective-permute-start.5 = (bf16[32,4096]{1,0:T(8,128)(2,1)}, bf16[32,4096]{1,0:T(8,128)(2,1)}, u32[]{:S(2)}, u32[]{:S(2)}) collective-permute-start(bf16[32,4096]{1,0:T(8,128)(2,1)} %get-tuple-element.90), channel_id=1, source_target_pairs={{0,3},{1,6},{2,5},{3,0},{4,7},{5,2},{6,1},{7,4},{8,11},{9,14},{10,... | collective-permute-start | bytes 786440 | tf_op jit(solution)/shard_map/ppermute | solution.py:233
  29.2 3.4 %place.3 = (bf16[32,4096]{1,0:T(8,128)(2,1)}, bf16[32,4096]{1,0:T(8,128)(2,1)}, bf16[32,4096]{1,0:T(8,128)(2,1)}, bf16[32,4096]{1,0:T(8,128)(2,1)}, bf16[32,4096...) custom-call(s32[1,256]{1,0:T(1,128)} %bitcast.14, ...), custom_call_target="tpu_custom_call" | custom-call | flops 1024 | bytes 1024 | tf_op jit(solution)/shard_map/place/pallas_call | solution.py:28
  32.7 0.0 collective-permute-done.2.refs_3_
  32.7 8.3 %collective-permute-start.6 = (bf16[32,4096]{1,0:T(8,128)(2,1)}, bf16[32,4096]{1,0:T(8,128)(2,1)}, u32[]{:S(2)}, u32[]{:S(2)}) collective-permute-start(bf16[32,4096]{1,0:T(8,128)(2,1)} %get-tuple-element.92), channel_id=1, source_target_pairs={{0,4},{1,5},{2,6},{3,7},{4,0},{5,1},{6,2},{7,3},{8,12},{9,13},{10,... | collective-permute-start | bytes 786440 | tf_op jit(solution)/shard_map/ppermute | solution.py:233
  41.0 0.0 collective-permute-done.3.refs_4_
  41.0 1.7 collective-permute-start.14
  42.7 15.6 %collective-permute-start.7 = (bf16[32,4096]{1,0:T(8,128)(2,1)}, bf16[32,4096]{1,0:T(8,128)(2,1)}, u32[]{:S(2)}, u32[]{:S(2)}) collective-permute-start(bf16[32,4096]{1,0:T(8,128)(2,1)} %get-tuple-element.96), channel_id=1, source_target_pairs={{0,6},{1,3},{2,4},{3,1},{4,2},{5,7},{6,0},{7,5},{8,14},{9,11},{10,... | collective-permute-start | bytes 786440 | tf_op jit(solution)/shard_map/ppermute | solution.py:233
  58.3 8.9 %collective-permute-start.9 = (bf16[32,4096]{1,0:T(8,128)(2,1)}, bf16[32,4096]{1,0:T(8,128)(2,1)}, u32[]{:S(2)}, u32[]{:S(2)}) collective-permute-start(bf16[32,4096]{1,0:T(8,128)(2,1)} %get-tuple-element.100), channel_id=1, source_target_pairs={{0,2},{1,7},{2,0},{3,5},{4,6},{5,3},{6,4},{7,1},{8,10},{9,15},{10,... | collective-permute-start | bytes 786440 | tf_op jit(solution)/shard_map/ppermute | solution.py:233
  67.2 8.5 %collective-permute-done.11.refs_1_ = bf16[32,4096]{1,0:T(8,128)(2,1)} collective-permute-done((bf16[32,4096]{1,0:T(8,128)(2,1)}, bf16[32,4096]{1,0:T(8,128)(2,1)}, u32[]{:S(2)}, u32[]{:S(2)}) %collective-permute-start.11) | collective-permute-done | bytes 262176 | tf_op jit(solution)/shard_map/ppermute | solution.py:233
  75.7 0.0 collective-permute-start.12
  75.7 0.0 collective-permute-done.14.refs_2_
  75.7 0.0 collective-permute-start.15
  75.7 10.9 %expert.2 = (bf16[32,4096]{1,0:T(8,128)(2,1)}, bf16[32,4096]{1,0:T(8,128)(2,1)}, bf16[32,4096]{1,0:T(8,128)(2,1)}, bf16[32,4096]{1,0:T(8,128)(2,1)}, bf16[32,409...) custom-call(bf16[32,4096]{1,0:T(8,128)(2,1)} %get-tuple-element.82.r, ...), custom_call_target="tpu_custom_call" | custom-call | flops 1024 | bytes 1024 | tf_op jit(solution)/shard_map/expert/pallas_call | solution.py:28
  86.6 5.3 %collective-permute-start.17 = (bf16[32,4096]{1,0:T(8,128)(2,1)}, bf16[32,4096]{1,0:T(8,128)(2,1)}, u32[]{:S(2)}, u32[]{:S(2)}) collective-permute-start(bf16[32,4096]{1,0:T(8,128)(2,1)} %get-tuple-element.116), channel_id=1, source_target_pairs={{0,4},{1,5},{2,6},{3,7},{4,0},{5,1},{6,2},{7,3},{8,12},{9,13},{10,... | collective-permute-start | bytes 786440 | tf_op jit(solution)/shard_map/ppermute | solution.py:233
  92.0 0.0 collective-permute-done.12.refs_5_
  92.0 0.4 collective-permute-start.13
  92.4 14.9 %collective-permute-start.10 = (bf16[32,4096]{1,0:T(8,128)(2,1)}, bf16[32,4096]{1,0:T(8,128)(2,1)}, u32[]{:S(2)}, u32[]{:S(2)}) collective-permute-start(bf16[32,4096]{1,0:T(8,128)(2,1)} %get-tuple-element.101), channel_id=1, source_target_pairs={{0,1},{1,0},{2,7},{3,6},{4,5},{5,4},{6,3},{7,2},{8,9},{9,8},{10,15... | collective-permute-start | bytes 786440 | tf_op jit(solution)/shard_map/ppermute | solution.py:233
  107.2 0.0 collective-permute-start.8
  107.2 0.0 collective-permute-done.15.refs_6_
  107.2 0.0 collective-permute-start.16
  107.2 3.6 %collective-permute-done.17.refs_7_ = bf16[32,4096]{1,0:T(8,128)(2,1)} collective-permute-done((bf16[32,4096]{1,0:T(8,128)(2,1)}, bf16[32,4096]{1,0:T(8,128)(2,1)}, u32[]{:S(2)}, u32[]{:S(2)}) %collective-permute-start.17) | collective-permute-done | bytes 262176 | tf_op jit(solution)/shard_map/ppermute | solution.py:233
  110.8 11.1 %expert.3 = (bf16[32,4096]{1,0:T(8,128)(2,1)}, bf16[32,4096]{1,0:T(8,128)(2,1)}, bf16[32,4096]{1,0:T(8,128)(2,1)}, bf16[32,4096]{1,0:T(8,128)(2,1)}, bf16[32,409...) custom-call(bf16[32,4096]{1,0:T(8,128)(2,1)} %get-tuple-element.124., ...), custom_call_target="tpu_custom_call" | custom-call | flops 1024 | bytes 1024 | tf_op jit(solution)/shard_map/expert/pallas_call | solution.py:28
  121.9 4.4 %weight_part.4 = (bf16[16,2176]{1,0:T(8,128)(2,1)}, bf16[496,2176]{1,0:T(8,128)(2,1)}) custom-call(s32[1]{0:T(128)} %bitcast.4.refs_0_, bf16[256,4096]{1,0:T(8,128)(2,1)} %get-tuple-element.138.refs_1_, bf16[256,1408]{1,0:T(8,128)(2,1)} %get-tuple-element.127.refs_2_, bf16[256,704]{1,0:T(8,128)(2,1)} %get-tuple-element.128.refs_3_, ...), custom_call_target="tpu_custom_call" | custom-call | flops 1024 | bytes 1024 | tf_op jit(solution)/shard_map/weight_part/pallas_call | solution.py:28
  126.3 0.1 collective-permute-start.21
  126.3 0.0 collective-permute-done.13.refs_6_
  126.4 0.0 collective-permute-done.8.refs_4_
  126.4 1.6 collective-permute-done.21.refs_7_
  127.9 0.0 collective-permute-done.16.refs_7_
  127.9 0.2 collective-permute-start.22
  128.1 0.0 collective-permute-start.18
  128.1 1.0 collective-permute-start.19
  129.1 4.3 %weight_part.5 = bf16[512,2176]{1,0:T(8,128)(2,1)} custom-call(s32[1]{0:T(128)} %bitcast.5.refs_0_, bf16[256,4096]{1,0:T(8,128)(2,1)} %get-tuple-element.138.refs_1_, bf16[256,1408]{1,0:T(8,128)(2,1)} %get-tuple-element.127.refs_2_, bf16[256,704]{1,0:T(8,128)(2,1)} %get-tuple-element.128.refs_3_, bf16[256,4096]{1,0:T(8,128)(2,1)} %get-tuple-element.129.refs_4_, ...), custom_call_target="tpu_custom_call" | custom-call | flops 1024 | bytes 1024 | tf_op jit(solution)/shard_map/weight_part/pallas_call | solution.py:28
  133.5 5.2 %weight_part.6 = (bf16[16,2176]{1,0:T(8,128)(2,1)}, bf16[496,2176]{1,0:T(8,128)(2,1)}) custom-call(s32[1]{0:T(128)} %bitcast.6.refs_0_, bf16[256,4096]{1,0:T(8,128)(2,1)} %get-tuple-element.138.refs_1_, bf16[256,1408]{1,0:T(8,128)(2,1)} %get-tuple-element.127.refs_2_, bf16[256,704]{1,0:T(8,128)(2,1)} %get-tuple-element.128.refs_3_, ...), custom_call_target="tpu_custom_call" | custom-call | flops 1024 | bytes 1024 | tf_op jit(solution)/shard_map/weight_part/pallas_call | solution.py:28
  138.6 1.1 collective-permute-start.24
  139.7 0.6 collective-permute-done.18.refs_8_
  140.3 3.2 %collective-permute-done.19.refs_9_ = bf16[32,4096]{1,0:T(8,128)(2,1)} collective-permute-done((bf16[32,4096]{1,0:T(8,128)(2,1)}, bf16[32,4096]{1,0:T(8,128)(2,1)}, u32[]{:S(2)}, u32[]{:S(2)}) %collective-permute-start.19) | collective-permute-done | bytes 262176 | tf_op jit(solution)/shard_map/ppermute | solution.py:233
  143.5 1.0 collective-permute-start.25
  144.5 4.1 %collective-permute-start.20 = (bf16[32,4096]{1,0:T(8,128)(2,1)}, bf16[32,4096]{1,0:T(8,128)(2,1)}, u32[]{:S(2)}, u32[]{:S(2)}) collective-permute-start(bf16[32,4096]{1,0:T(8,128)(2,1)} %get-tuple-element.121), channel_id=1, source_target_pairs={{0,4},{1,5},{2,6},{3,7},{4,0},{5,1},{6,2},{7,3},{8,12},{9,13},{10,... | collective-permute-start | bytes 786440 | tf_op jit(solution)/shard_map/ppermute | solution.py:233
  148.6 10.8 %collective-permute-done.20.refs_10_ = bf16[32,4096]{1,0:T(8,128)(2,1)} collective-permute-done((bf16[32,4096]{1,0:T(8,128)(2,1)}, bf16[32,4096]{1,0:T(8,128)(2,1)}, u32[]{:S(2)}, u32[]{:S(2)}) %collective-permute-start.20) | collective-permute-done | bytes 262176 | tf_op jit(solution)/shard_map/ppermute | solution.py:233
  159.4 0.0 collective-permute-start.29
  159.4 1.5 collective-permute-start.28
  160.9 1.3 collective-permute-start.27
  162.2 8.9 %collective-permute-done.29.refs_7_ = bf16[32,4096]{1,0:T(8,128)(2,1)} collective-permute-done((bf16[32,4096]{1,0:T(8,128)(2,1)}, bf16[32,4096]{1,0:T(8,128)(2,1)}, u32[]{:S(2)}, u32[]{:S(2)}) %collective-permute-start.29) | collective-permute-done | bytes 262176 | tf_op jit(solution)/shard_map/ppermute | solution.py:233
  171.1 3.1 %collective-permute-start.26 = (bf16[32,4096]{1,0:T(8,128)(2,1)}, bf16[32,4096]{1,0:T(8,128)(2,1)}, u32[]{:S(2)}, u32[]{:S(2)}) collective-permute-start(bf16[32,4096]{1,0:T(8,128)(2,1)} %get-tuple-element.144), channel_id=1, source_target_pairs={{0,5},{1,4},{2,3},{3,2},{4,1},{5,0},{6,7},{7,6},{8,13},{9,12},{10,... | collective-permute-start | bytes 786440 | tf_op jit(solution)/shard_map/ppermute | solution.py:233
  174.2 3.6 %combine.2 = (bf16[256,2048]{1,0:T(8,128)(2,1)}, bf16[256,2048]{1,0:T(8,128)(2,1)}) custom-call(s32[1,256]{1,0:T(1,128)} %bitcast.15, bf16[256,2048]{1,0:T(8,128)(2,1)} %refs_1_.5, bf16[256,2048]{1,0:T(8,128)(2,1)} %refs_2_.5, bf16[32,4096]{1,0:T(8,128)(2,1)} %get-tuple-element.93.refs_3_, bf16[32,4096]{1,0:T(8,128)(2,1)} %collective-permute-done.8.refs_4_, ...), custom_call_target="tpu_custom_call" | custom-call | flops 1024 | bytes 1024 | tf_op jit(solution)/shard_map/combine/pallas_call | solution.py:28
  177.8 0.0 collective-permute-done.28.refs_6_
  177.8 7.2 %collective-permute-start.32 = (bf16[32,4096]{1,0:T(8,128)(2,1)}, bf16[32,4096]{1,0:T(8,128)(2,1)}, u32[]{:S(2)}, u32[]{:S(2)}) collective-permute-start(bf16[32,4096]{1,0:T(8,128)(2,1)} %get-tuple-element.156), channel_id=1, source_target_pairs={{0,4},{1,5},{2,6},{3,7},{4,0},{5,1},{6,2},{7,3},{8,12},{9,13},{10,... | collective-permute-start | bytes 786440 | tf_op jit(solution)/shard_map/ppermute | solution.py:233
  185.0 0.0 collective-permute-done.27.refs_5_
  185.0 4.1 %collective-permute-start.31 = (bf16[32,4096]{1,0:T(8,128)(2,1)}, bf16[32,4096]{1,0:T(8,128)(2,1)}, u32[]{:S(2)}, u32[]{:S(2)}) collective-permute-start(bf16[32,4096]{1,0:T(8,128)(2,1)} %get-tuple-element.154), channel_id=1, source_target_pairs={{0,3},{1,6},{2,5},{3,0},{4,7},{5,2},{6,1},{7,4},{8,11},{9,14},{10,... | collective-permute-start | bytes 786440 | tf_op jit(solution)/shard_map/ppermute | solution.py:233
  189.1 3.6 %collective-permute-done.26.refs_4_ = bf16[32,4096]{1,0:T(8,128)(2,1)} collective-permute-done((bf16[32,4096]{1,0:T(8,128)(2,1)}, bf16[32,4096]{1,0:T(8,128)(2,1)}, u32[]{:S(2)}, u32[]{:S(2)}) %collective-permute-start.26) | collective-permute-done | bytes 262176 | tf_op jit(solution)/shard_map/ppermute | solution.py:233
  192.7 1.9 collective-permute-start.30
  194.6 6.8 %weight_part.7 = (f32[512,1408]{1,0:T(8,128)}, f32[704,512]{1,0:T(8,128)}) custom-call(s32[1]{0:T(128)} %bitcast.3.refs_0_, bf16[256,4096]{1,0:T(8,128)(2,1)} %get-tuple-element.138.refs_1_, bf16[256,1408]{1,0:T(8,128)(2,1)} %get-tuple-element.127.refs_2_, bf16[256,704]{1,0:T(8,128)(2,1)} %get-tuple-element.128.refs_3_, ...), custom_call_target="tpu_custom_call" | custom-call | flops 1024 | bytes 1024 | tf_op jit(solution)/shard_map/weight_part/pallas_call | solution.py:28
  201.4 2.2 %collective-permute-done.32.refs_10_ = bf16[32,4096]{1,0:T(8,128)(2,1)} collective-permute-done((bf16[32,4096]{1,0:T(8,128)(2,1)}, bf16[32,4096]{1,0:T(8,128)(2,1)}, u32[]{:S(2)}, u32[]{:S(2)}) %collective-permute-start.32) | collective-permute-done | bytes 262176 | tf_op jit(solution)/shard_map/ppermute | solution.py:233
  203.5 3.8 %collective-permute-done.31.refs_9_ = bf16[32,4096]{1,0:T(8,128)(2,1)} collective-permute-done((bf16[32,4096]{1,0:T(8,128)(2,1)}, bf16[32,4096]{1,0:T(8,128)(2,1)}, u32[]{:S(2)}, u32[]{:S(2)}) %collective-permute-start.31) | collective-permute-done | bytes 262176 | tf_op jit(solution)/shard_map/ppermute | solution.py:233
  207.3 0.0 collective-permute-done.30.refs_8_
  207.3 3.7 %combine.3 = (bf16[256,2048]{1,0:T(8,128)(2,1)}, bf16[256,2048]{1,0:T(8,128)(2,1)}) custom-call(s32[1,256]{1,0:T(1,128)} %bitcast.16, bf16[256,2048]{1,0:T(8,128)(2,1)} %get-tuple-element.122.refs_1_, bf16[256,2048]{1,0:T(8,128)(2,1)} %get-tuple-element.123.refs_2_, bf16[32,4096]{1,0:T(8,128)(2,1)} %get-tuple-element.142.refs_3_, ...), custom_call_target="tpu_custom_call" | custom-call | flops 1024 | bytes 1024 | tf_op jit(solution)/shard_map/combine/pallas_call | solution.py:28
  (12 shorter events, 0.0 us)
Async XLA Ops:
  4.1 18.2 %collective-permute-start = (bf16[32,4096]{1,0:T(8,128)(2,1)}, bf16[32,4096]{1,0:T(8,128)(2,1)}, u32[]{:S(2)}, u32[]{:S(2)}) collective-permute-start(bf16[32,4096]{1,0:T(8,128)(2,1)} %get-tuple-element.83), channel_id=1, source_target_pairs={{0,5},{1,4},{2,3},{3,2},{4,1},{5,0},{6,7},{7,6},{8,13},{9,12},{10,... | collective-permute-start | bytes 786440 | tf_op jit(solution)/shard_map/ppermute | solution.py:233
  9.1 13.1 %collective-permute-start.1 = (bf16[32,4096]{1,0:T(8,128)(2,1)}, bf16[32,4096]{1,0:T(8,128)(2,1)}, u32[]{:S(2)}, u32[]{:S(2)}) collective-permute-start(bf16[32,4096]{1,0:T(8,128)(2,1)} %get-tuple-element.84), channel_id=1, source_target_pairs={{0,1},{1,0},{2,7},{3,6},{4,5},{5,4},{6,3},{7,2},{8,9},{9,8},{10,15... | collective-permute-start | bytes 786440 | tf_op jit(solution)/shard_map/ppermute | solution.py:233
  9.6 23.0 %collective-permute-start.2 = (bf16[32,4096]{1,0:T(8,128)(2,1)}, bf16[32,4096]{1,0:T(8,128)(2,1)}, u32[]{:S(2)}, u32[]{:S(2)}) collective-permute-start(bf16[32,4096]{1,0:T(8,128)(2,1)} %get-tuple-element.85), channel_id=1, source_target_pairs={{0,6},{1,3},{2,4},{3,1},{4,2},{5,7},{6,0},{7,5},{8,14},{9,11},{10,... | collective-permute-start | bytes 786440 | tf_op jit(solution)/shard_map/ppermute | solution.py:233
  11.0 30.0 %collective-permute-start.3 = (bf16[32,4096]{1,0:T(8,128)(2,1)}, bf16[32,4096]{1,0:T(8,128)(2,1)}, u32[]{:S(2)}, u32[]{:S(2)}) collective-permute-start(bf16[32,4096]{1,0:T(8,128)(2,1)} %get-tuple-element.86), channel_id=1, source_target_pairs={{0,2},{1,7},{2,0},{3,5},{4,6},{5,3},{6,4},{7,1},{8,10},{9,15},{10,... | collective-permute-start | bytes 786440 | tf_op jit(solution)/shard_map/ppermute | solution.py:233
  22.2 18.8 %collective-permute-start.4 = (bf16[32,4096]{1,0:T(8,128)(2,1)}, bf16[32,4096]{1,0:T(8,128)(2,1)}, u32[]{:S(2)}, u32[]{:S(2)}) collective-permute-start(bf16[32,4096]{1,0:T(8,128)(2,1)} %get-tuple-element.88), channel_id=1, source_target_pairs={{0,7},{1,2},{2,1},{3,4},{4,3},{5,6},{6,5},{7,0},{8,15},{9,10},{10,... | collective-permute-start | bytes 786440 | tf_op jit(solution)/shard_map/ppermute | solution.py:233
  22.2 20.4 %collective-permute-start.5 = (bf16[32,4096]{1,0:T(8,128)(2,1)}, bf16[32,4096]{1,0:T(8,128)(2,1)}, u32[]{:S(2)}, u32[]{:S(2)}) collective-permute-start(bf16[32,4096]{1,0:T(8,128)(2,1)} %get-tuple-element.90), channel_id=1, source_target_pairs={{0,3},{1,6},{2,5},{3,0},{4,7},{5,2},{6,1},{7,4},{8,11},{9,14},{10,... | collective-permute-start | bytes 786440 | tf_op jit(solution)/shard_map/ppermute | solution.py:233
  32.7 25.6 %collective-permute-start.6 = (bf16[32,4096]{1,0:T(8,128)(2,1)}, bf16[32,4096]{1,0:T(8,128)(2,1)}, u32[]{:S(2)}, u32[]{:S(2)}) collective-permute-start(bf16[32,4096]{1,0:T(8,128)(2,1)} %get-tuple-element.92), channel_id=1, source_target_pairs={{0,4},{1,5},{2,6},{3,7},{4,0},{5,1},{6,2},{7,3},{8,12},{9,13},{10,... | collective-permute-start | bytes 786440 | tf_op jit(solution)/shard_map/ppermute | solution.py:233
  41.0 34.7 %collective-permute-start.11 = (bf16[32,4096]{1,0:T(8,128)(2,1)}, bf16[32,4096]{1,0:T(8,128)(2,1)}, u32[]{:S(2)}, u32[]{:S(2)}) collective-permute-start(bf16[32,4096]{1,0:T(8,128)(2,1)} %get-tuple-element.105), channel_id=1, source_target_pairs={{0,5},{1,4},{2,3},{3,2},{4,1},{5,0},{6,7},{7,6},{8,13},{9,12},{10,... | collective-permute-start | bytes 786440 | tf_op jit(solution)/shard_map/ppermute | solution.py:233
  41.0 34.7 %collective-permute-start.14 = (bf16[32,4096]{1,0:T(8,128)(2,1)}, bf16[32,4096]{1,0:T(8,128)(2,1)}, u32[]{:S(2)}, u32[]{:S(2)}) collective-permute-start(bf16[32,4096]{1,0:T(8,128)(2,1)} %get-tuple-element.111), channel_id=1, source_target_pairs={{0,1},{1,0},{2,7},{3,6},{4,5},{5,4},{6,3},{7,2},{8,9},{9,8},{10,15... | collective-permute-start | bytes 786440 | tf_op jit(solution)/shard_map/ppermute | solution.py:233
  42.7 43.9 %collective-permute-start.7 = (bf16[32,4096]{1,0:T(8,128)(2,1)}, bf16[32,4096]{1,0:T(8,128)(2,1)}, u32[]{:S(2)}, u32[]{:S(2)}) collective-permute-start(bf16[32,4096]{1,0:T(8,128)(2,1)} %get-tuple-element.96), channel_id=1, source_target_pairs={{0,6},{1,3},{2,4},{3,1},{4,2},{5,7},{6,0},{7,5},{8,14},{9,11},{10,... | collective-permute-start | bytes 786440 | tf_op jit(solution)/shard_map/ppermute | solution.py:233
  58.3 33.7 %collective-permute-start.9 = (bf16[32,4096]{1,0:T(8,128)(2,1)}, bf16[32,4096]{1,0:T(8,128)(2,1)}, u32[]{:S(2)}, u32[]{:S(2)}) collective-permute-start(bf16[32,4096]{1,0:T(8,128)(2,1)} %get-tuple-element.100), channel_id=1, source_target_pairs={{0,2},{1,7},{2,0},{3,5},{4,6},{5,3},{6,4},{7,1},{8,10},{9,15},{10,... | collective-permute-start | bytes 786440 | tf_op jit(solution)/shard_map/ppermute | solution.py:233
  75.7 16.3 %collective-permute-start.12 = (bf16[32,4096]{1,0:T(8,128)(2,1)}, bf16[32,4096]{1,0:T(8,128)(2,1)}, u32[]{:S(2)}, u32[]{:S(2)}) collective-permute-start(bf16[32,4096]{1,0:T(8,128)(2,1)} %get-tuple-element.106), channel_id=1, source_target_pairs={{0,7},{1,2},{2,1},{3,4},{4,3},{5,6},{6,5},{7,0},{8,15},{9,10},{10,... | collective-permute-start | bytes 786440 | tf_op jit(solution)/shard_map/ppermute | solution.py:233
  75.7 31.5 %collective-permute-start.15 = (bf16[32,4096]{1,0:T(8,128)(2,1)}, bf16[32,4096]{1,0:T(8,128)(2,1)}, u32[]{:S(2)}, u32[]{:S(2)}) collective-permute-start(bf16[32,4096]{1,0:T(8,128)(2,1)} %get-tuple-element.112), channel_id=1, source_target_pairs={{0,3},{1,6},{2,5},{3,0},{4,7},{5,2},{6,1},{7,4},{8,11},{9,14},{10,... | collective-permute-start | bytes 786440 | tf_op jit(solution)/shard_map/ppermute | solution.py:233
  86.6 24.2 %collective-permute-start.17 = (bf16[32,4096]{1,0:T(8,128)(2,1)}, bf16[32,4096]{1,0:T(8,128)(2,1)}, u32[]{:S(2)}, u32[]{:S(2)}) collective-permute-start(bf16[32,4096]{1,0:T(8,128)(2,1)} %get-tuple-element.116), channel_id=1, source_target_pairs={{0,4},{1,5},{2,6},{3,7},{4,0},{5,1},{6,2},{7,3},{8,12},{9,13},{10,... | collective-permute-start | bytes 786440 | tf_op jit(solution)/shard_map/ppermute | solution.py:233
  92.0 34.4 %collective-permute-start.13 = (bf16[32,4096]{1,0:T(8,128)(2,1)}, bf16[32,4096]{1,0:T(8,128)(2,1)}, u32[]{:S(2)}, u32[]{:S(2)}) collective-permute-start(bf16[32,4096]{1,0:T(8,128)(2,1)} %get-tuple-element.107), channel_id=1, source_target_pairs={{0,6},{1,3},{2,4},{3,1},{4,2},{5,7},{6,0},{7,5},{8,14},{9,11},{10,... | collective-permute-start | bytes 786440 | tf_op jit(solution)/shard_map/ppermute | solution.py:233
  92.4 34.0 %collective-permute-start.10 = (bf16[32,4096]{1,0:T(8,128)(2,1)}, bf16[32,4096]{1,0:T(8,128)(2,1)}, u32[]{:S(2)}, u32[]{:S(2)}) collective-permute-start(bf16[32,4096]{1,0:T(8,128)(2,1)} %get-tuple-element.101), channel_id=1, source_target_pairs={{0,1},{1,0},{2,7},{3,6},{4,5},{5,4},{6,3},{7,2},{8,9},{9,8},{10,15... | collective-permute-start | bytes 786440 | tf_op jit(solution)/shard_map/ppermute | solution.py:233
  107.2 19.1 %collective-permute-start.8 = (bf16[32,4096]{1,0:T(8,128)(2,1)}, bf16[32,4096]{1,0:T(8,128)(2,1)}, u32[]{:S(2)}, u32[]{:S(2)}) collective-permute-start(bf16[32,4096]{1,0:T(8,128)(2,1)} %get-tuple-element.97), channel_id=1, source_target_pairs={{0,5},{1,4},{2,3},{3,2},{4,1},{5,0},{6,7},{7,6},{8,13},{9,12},{10,... | collective-permute-start | bytes 786440 | tf_op jit(solution)/shard_map/ppermute | solution.py:233
  107.2 20.7 %collective-permute-start.16 = (bf16[32,4096]{1,0:T(8,128)(2,1)}, bf16[32,4096]{1,0:T(8,128)(2,1)}, u32[]{:S(2)}, u32[]{:S(2)}) collective-permute-start(bf16[32,4096]{1,0:T(8,128)(2,1)} %get-tuple-element.113), channel_id=1, source_target_pairs={{0,2},{1,7},{2,0},{3,5},{4,6},{5,3},{6,4},{7,1},{8,10},{9,15},{10,... | collective-permute-start | bytes 786440 | tf_op jit(solution)/shard_map/ppermute | solution.py:233
  126.3 1.7 collective-permute-start.21
  127.9 5.5 %collective-permute-start.22 = (bf16[496,2176]{1,0:T(8,128)(2,1)}, bf16[496,2176]{1,0:T(8,128)(2,1)}, u32[]{:S(2)}, u32[]{:S(2)}) collective-permute-start(bf16[496,2176]{1,0:T(8,128)(2,1)} %get-tuple-element.136), channel_id=1, source_target_pairs={{0,8},{8,0},{16,24},{24,16},{1,9},{9,1},{17,25},{25,17},{2,10},{10... | collective-permute-start | bytes 6475784 | tf_op jit(solution)/shard_map/ppermute | solution.py:233
  128.1 12.2 %collective-permute-start.18 = (bf16[32,4096]{1,0:T(8,128)(2,1)}, bf16[32,4096]{1,0:T(8,128)(2,1)}, u32[]{:S(2)}, u32[]{:S(2)}) collective-permute-start(bf16[32,4096]{1,0:T(8,128)(2,1)} %get-tuple-element.117), channel_id=1, source_target_pairs={{0,7},{1,2},{2,1},{3,4},{4,3},{5,6},{6,5},{7,0},{8,15},{9,10},{10,... | collective-permute-start | bytes 786440 | tf_op jit(solution)/shard_map/ppermute | solution.py:233
  128.1 15.4 %collective-permute-start.19 = (bf16[32,4096]{1,0:T(8,128)(2,1)}, bf16[32,4096]{1,0:T(8,128)(2,1)}, u32[]{:S(2)}, u32[]{:S(2)}) collective-permute-start(bf16[32,4096]{1,0:T(8,128)(2,1)} %get-tuple-element.119), channel_id=1, source_target_pairs={{0,3},{1,6},{2,5},{3,0},{4,7},{5,2},{6,1},{7,4},{8,11},{9,14},{10,... | collective-permute-start | bytes 786440 | tf_op jit(solution)/shard_map/ppermute | solution.py:233
  138.6 4.9 %collective-permute-start.24 = (bf16[16,2176]{1,0:T(8,128)(2,1)}, bf16[16,2176]{1,0:T(8,128)(2,1)}, u32[]{:S(2)}, u32[]{:S(2)}) collective-permute-start(bf16[16,2176]{1,0:T(8,128)(2,1)} %get-tuple-element.137), channel_id=1, source_target_pairs={{0,16},{8,24},{16,0},{24,8},{1,17},{9,25},{17,1},{25,9},{2,18},{10... | collective-permute-start | bytes 208904 | tf_op jit(solution)/shard_map/ppermute | solution.py:233
  139.7 54.9 %collective-permute-start.23 = (bf16[512,2176]{1,0:T(8,128)(2,1)}, bf16[512,2176]{1,0:T(8,128)(2,1)}, u32[]{:S(2)}, u32[]{:S(2)}) collective-permute-start(bf16[512,2176]{1,0:T(8,128)(2,1)} %weight_part.5), channel_id=1, source_target_pairs={{0,8},{8,0},{16,24},{24,16},{1,9},{9,1},{17,25},{25,17},{2,10},{10... | collective-permute-start | bytes 6684680 | tf_op jit(solution)/shard_map/ppermute | solution.py:233
  143.5 51.1 %collective-permute-start.25 = (bf16[496,2176]{1,0:T(8,128)(2,1)}, bf16[496,2176]{1,0:T(8,128)(2,1)}, u32[]{:S(2)}, u32[]{:S(2)}) collective-permute-start(bf16[496,2176]{1,0:T(8,128)(2,1)} %get-tuple-element.140), channel_id=1, source_target_pairs={{0,16},{8,24},{16,0},{24,8},{1,17},{9,25},{17,1},{25,9},{2,18},{10... | collective-permute-start | bytes 6475784 | tf_op jit(solution)/shard_map/ppermute | solution.py:233
  144.5 14.8 %collective-permute-start.20 = (bf16[32,4096]{1,0:T(8,128)(2,1)}, bf16[32,4096]{1,0:T(8,128)(2,1)}, u32[]{:S(2)}, u32[]{:S(2)}) collective-permute-start(bf16[32,4096]{1,0:T(8,128)(2,1)} %get-tuple-element.121), channel_id=1, source_target_pairs={{0,4},{1,5},{2,6},{3,7},{4,0},{5,1},{6,2},{7,3},{8,12},{9,13},{10,... | collective-permute-start | bytes 786440 | tf_op jit(solution)/shard_map/ppermute | solution.py:233
  159.4 11.7 %collective-permute-start.29 = (bf16[32,4096]{1,0:T(8,128)(2,1)}, bf16[32,4096]{1,0:T(8,128)(2,1)}, u32[]{:S(2)}, u32[]{:S(2)}) collective-permute-start(bf16[32,4096]{1,0:T(8,128)(2,1)} %get-tuple-element.150), channel_id=1, source_target_pairs={{0,2},{1,7},{2,0},{3,5},{4,6},{5,3},{6,4},{7,1},{8,10},{9,15},{10,... | collective-permute-start | bytes 786440 | tf_op jit(solution)/shard_map/ppermute | solution.py:233
  159.4 18.5 %collective-permute-start.28 = (bf16[32,4096]{1,0:T(8,128)(2,1)}, bf16[32,4096]{1,0:T(8,128)(2,1)}, u32[]{:S(2)}, u32[]{:S(2)}) collective-permute-start(bf16[32,4096]{1,0:T(8,128)(2,1)} %get-tuple-element.148), channel_id=1, source_target_pairs={{0,6},{1,3},{2,4},{3,1},{4,2},{5,7},{6,0},{7,5},{8,14},{9,11},{10,... | collective-permute-start | bytes 786440 | tf_op jit(solution)/shard_map/ppermute | solution.py:233
  160.9 24.1 %collective-permute-start.27 = (bf16[32,4096]{1,0:T(8,128)(2,1)}, bf16[32,4096]{1,0:T(8,128)(2,1)}, u32[]{:S(2)}, u32[]{:S(2)}) collective-permute-start(bf16[32,4096]{1,0:T(8,128)(2,1)} %get-tuple-element.146), channel_id=1, source_target_pairs={{0,1},{1,0},{2,7},{3,6},{4,5},{5,4},{6,3},{7,2},{8,9},{9,8},{10,15... | collective-permute-start | bytes 786440 | tf_op jit(solution)/shard_map/ppermute | solution.py:233
  171.1 21.6 %collective-permute-start.26 = (bf16[32,4096]{1,0:T(8,128)(2,1)}, bf16[32,4096]{1,0:T(8,128)(2,1)}, u32[]{:S(2)}, u32[]{:S(2)}) collective-permute-start(bf16[32,4096]{1,0:T(8,128)(2,1)} %get-tuple-element.144), channel_id=1, source_target_pairs={{0,5},{1,4},{2,3},{3,2},{4,1},{5,0},{6,7},{7,6},{8,13},{9,12},{10,... | collective-permute-start | bytes 786440 | tf_op jit(solution)/shard_map/ppermute | solution.py:233
  177.8 25.7 %collective-permute-start.32 = (bf16[32,4096]{1,0:T(8,128)(2,1)}, bf16[32,4096]{1,0:T(8,128)(2,1)}, u32[]{:S(2)}, u32[]{:S(2)}) collective-permute-start(bf16[32,4096]{1,0:T(8,128)(2,1)} %get-tuple-element.156), channel_id=1, source_target_pairs={{0,4},{1,5},{2,6},{3,7},{4,0},{5,1},{6,2},{7,3},{8,12},{9,13},{10,... | collective-permute-start | bytes 786440 | tf_op jit(solution)/shard_map/ppermute | solution.py:233
  185.0 22.3 %collective-permute-start.31 = (bf16[32,4096]{1,0:T(8,128)(2,1)}, bf16[32,4096]{1,0:T(8,128)(2,1)}, u32[]{:S(2)}, u32[]{:S(2)}) collective-permute-start(bf16[32,4096]{1,0:T(8,128)(2,1)} %get-tuple-element.154), channel_id=1, source_target_pairs={{0,3},{1,6},{2,5},{3,0},{4,7},{5,2},{6,1},{7,4},{8,11},{9,14},{10,... | collective-permute-start | bytes 786440 | tf_op jit(solution)/shard_map/ppermute | solution.py:233
  192.7 14.6 %collective-permute-start.30 = (bf16[32,4096]{1,0:T(8,128)(2,1)}, bf16[32,4096]{1,0:T(8,128)(2,1)}, u32[]{:S(2)}, u32[]{:S(2)}) collective-permute-start(bf16[32,4096]{1,0:T(8,128)(2,1)} %get-tuple-element.152), channel_id=1, source_target_pairs={{0,7},{1,2},{2,1},{3,4},{4,3},{5,6},{6,5},{7,0},{8,15},{9,10},{10,... | collective-permute-start | bytes 786440 | tf_op jit(solution)/shard_map/ppermute | solution.py:233

commit v14 on v13

--- a/solution.py
+++ b/solution.py
@@ -246,13 +246,13 @@
     half = experts // 2
     near = mask % half
     if near == 0:
-        return experts - 1 if mask else 0
+        return 1 if mask else 0
     units = [unit for unit in range(1, half) if bin(unit & near).count("1") % 2 == 0]
     turn = 0
     for bit in range(half.bit_length() if units else 0):
         if units[0] >> bit & 1:
             turn = turn ^ ((place >> bit) & 1)
-    return 2 * near - 1 + (turn if mask >= half else 1 - turn)
+    return 2 * near + (turn if mask >= half else 1 - turn)
 
 
 def exchange(blocks, rounds, lane, numbers, *earlier):

time: 211 us -> 219 us (1.038)
  waiting for transfers between devices: 57.7 us -> 71.2 us
  starting transfers between devices: 95.7 us -> 90.3 us
    ppermute x33, waiting for transfers between devices: 57.7 us -> 71.2 us  [send(): self.done.append(lax.ppermute(after(value, *earlier), axis, pairs))]
    ppermute x33, starting transfers between devices: 95.7 us -> 90.3 us  [send(): self.done.append(lax.ppermute(after(value, *earlier), axis, pairs))]
  transfers between devices with their start and end apart: 33 -> 33, of which waited for: 11 -> 12; matrix products, arithmetic and copies ran while one was open for 0% -> 0% of each run, Pallas kernels for 24% -> 23%
where the time goes in v14:
time: 219 us
  starting transfers between devices  90.3 us (41%)
  waiting for transfers between devices  71.2 us (33%)
  Pallas kernels  56.8 us (26%)
    ppermute x33, starting transfers between devices, send(): self.done.append(lax.ppermute(after(value, *earlier), axis, pairs))  90.3 us
    ppermute x33, waiting for transfers between devices, send(): self.done.append(lax.ppermute(after(value, *earlier), axis, pairs))  71.2 us
    pallas_call x10, Pallas kernels, call(): pl.pallas_call(kernel, in_specs=[pl.BlockSpec(memory_space=pltpu.SMEM)] *...  56.8 us
  transfers between devices with their start and end apart: 33, of which 12 were waited for; matrix products, arithmetic and copies ran while one was open for 0% of the time, Pallas kernels for 23%

profile of v14, /device:TPU:0, one launch (start us, length us, event | category | flops | bytes accessed | tf_op | source)
XLA Modules:
  0.0 219.3 jit_solution(17623177598575391470)
XLA Ops:
  0.6 3.4 %place.2 = (bf16[32,4096]{1,0:T(8,128)(2,1)}, bf16[32,4096]{1,0:T(8,128)(2,1)}, bf16[32,4096]{1,0:T(8,128)(2,1)}, bf16[32,4096]{1,0:T(8,128)(2,1)}, bf16[32,4096...) custom-call(s32[1,256]{1,0:T(1,128)} %bitcast.13, ...), custom_call_target="tpu_custom_call" | custom-call | flops 1024 | bytes 1024 | tf_op jit(solution)/shard_map/place/pallas_call | solution.py:28
  4.1 4.1 %collective-permute-start = (bf16[32,4096]{1,0:T(8,128)(2,1)}, bf16[32,4096]{1,0:T(8,128)(2,1)}, u32[]{:S(2)}, u32[]{:S(2)}) collective-permute-start(bf16[32,4096]{1,0:T(8,128)(2,1)} %get-tuple-element.83), channel_id=1, source_target_pairs={{0,4},{1,5},{2,6},{3,7},{4,0},{5,1},{6,2},{7,3},{8,12},{9,13},{10,... | collective-permute-start | bytes 786440 | tf_op jit(solution)/shard_map/ppermute | solution.py:233
  8.2 1.3 collective-permute-start.1
  9.5 0.3 collective-permute-start.2
  9.7 3.9 %collective-permute-start.3 = (bf16[32,4096]{1,0:T(8,128)(2,1)}, bf16[32,4096]{1,0:T(8,128)(2,1)}, u32[]{:S(2)}, u32[]{:S(2)}) collective-permute-start(bf16[32,4096]{1,0:T(8,128)(2,1)} %get-tuple-element.86), channel_id=1, source_target_pairs={{0,6},{1,3},{2,4},{3,1},{4,2},{5,7},{6,0},{7,5},{8,14},{9,11},{10,... | collective-permute-start | bytes 786440 | tf_op jit(solution)/shard_map/ppermute | solution.py:233
  13.6 18.9 %collective-permute-done.refs_1_ = bf16[32,4096]{1,0:T(8,128)(2,1)} collective-permute-done((bf16[32,4096]{1,0:T(8,128)(2,1)}, bf16[32,4096]{1,0:T(8,128)(2,1)}, u32[]{:S(2)}, u32[]{:S(2)}) %collective-permute-start) | collective-permute-done | bytes 262176 | tf_op jit(solution)/shard_map/ppermute | solution.py:233
  32.5 0.0 collective-permute-start.4
  32.5 9.7 %collective-permute-done.1.refs_2_ = bf16[32,4096]{1,0:T(8,128)(2,1)} collective-permute-done((bf16[32,4096]{1,0:T(8,128)(2,1)}, bf16[32,4096]{1,0:T(8,128)(2,1)}, u32[]{:S(2)}, u32[]{:S(2)}) %collective-permute-start.1) | collective-permute-done | bytes 262176 | tf_op jit(solution)/shard_map/ppermute | solution.py:233
  42.2 0.0 collective-permute-start.5
  42.2 3.4 %place.3 = (bf16[32,4096]{1,0:T(8,128)(2,1)}, bf16[32,4096]{1,0:T(8,128)(2,1)}, bf16[32,4096]{1,0:T(8,128)(2,1)}, bf16[32,4096]{1,0:T(8,128)(2,1)}, bf16[32,4096...) custom-call(s32[1,256]{1,0:T(1,128)} %bitcast.14, ...), custom_call_target="tpu_custom_call" | custom-call | flops 1024 | bytes 1024 | tf_op jit(solution)/shard_map/place/pallas_call | solution.py:28
  45.6 0.0 collective-permute-done.2.refs_3_
  45.6 0.1 collective-permute-start.6
  45.7 0.0 collective-permute-done.3.refs_4_
  45.7 5.5 %collective-permute-start.11 = (bf16[32,4096]{1,0:T(8,128)(2,1)}, bf16[32,4096]{1,0:T(8,128)(2,1)}, u32[]{:S(2)}, u32[]{:S(2)}) collective-permute-start(bf16[32,4096]{1,0:T(8,128)(2,1)} %get-tuple-element.105), channel_id=1, source_target_pairs={{0,4},{1,5},{2,6},{3,7},{4,0},{5,1},{6,2},{7,3},{8,12},{9,13},{10,... | collective-permute-start | bytes 786440 | tf_op jit(solution)/shard_map/ppermute | solution.py:233
  51.3 0.0 collective-permute-done.4.refs_5_
  51.3 1.4 collective-permute-start.14
  52.7 1.3 collective-permute-start.7
  54.0 0.4 collective-permute-done.6.refs_7_
  54.4 15.1 %collective-permute-start.9 = (bf16[32,4096]{1,0:T(8,128)(2,1)}, bf16[32,4096]{1,0:T(8,128)(2,1)}, u32[]{:S(2)}, u32[]{:S(2)}) collective-permute-start(bf16[32,4096]{1,0:T(8,128)(2,1)} %get-tuple-element.100), channel_id=1, source_target_pairs={{0,6},{1,3},{2,4},{3,1},{4,2},{5,7},{6,0},{7,5},{8,14},{9,11},{10,... | collective-permute-start | bytes 786440 | tf_op jit(solution)/shard_map/ppermute | solution.py:233
  69.5 7.8 %collective-permute-start.12 = (bf16[32,4096]{1,0:T(8,128)(2,1)}, bf16[32,4096]{1,0:T(8,128)(2,1)}, u32[]{:S(2)}, u32[]{:S(2)}) collective-permute-start(bf16[32,4096]{1,0:T(8,128)(2,1)} %get-tuple-element.106), channel_id=1, source_target_pairs={{0,2},{1,7},{2,0},{3,5},{4,6},{5,3},{6,4},{7,1},{8,10},{9,15},{10,... | collective-permute-start | bytes 786440 | tf_op jit(solution)/shard_map/ppermute | solution.py:233
  77.4 9.5 %collective-permute-done.14.refs_2_ = bf16[32,4096]{1,0:T(8,128)(2,1)} collective-permute-done((bf16[32,4096]{1,0:T(8,128)(2,1)}, bf16[32,4096]{1,0:T(8,128)(2,1)}, u32[]{:S(2)}, u32[]{:S(2)}) %collective-permute-start.14) | collective-permute-done | bytes 262176 | tf_op jit(solution)/shard_map/ppermute | solution.py:233
  86.9 0.0 collective-permute-start.15
  86.9 10.9 %expert.2 = (bf16[32,4096]{1,0:T(8,128)(2,1)}, bf16[32,4096]{1,0:T(8,128)(2,1)}, bf16[32,4096]{1,0:T(8,128)(2,1)}, bf16[32,4096]{1,0:T(8,128)(2,1)}, bf16[32,409...) custom-call(bf16[32,4096]{1,0:T(8,128)(2,1)} %get-tuple-element.82.r, ...), custom_call_target="tpu_custom_call" | custom-call | flops 1024 | bytes 1024 | tf_op jit(solution)/shard_map/expert/pallas_call | solution.py:28
  97.8 0.0 collective-permute-done.7.refs_3_
  97.8 0.1 collective-permute-start.17
  97.9 0.0 collective-permute-done.9.refs_4_
  97.9 0.1 collective-permute-start.13
  98.0 6.6 %collective-permute-start.10 = (bf16[32,4096]{1,0:T(8,128)(2,1)}, bf16[32,4096]{1,0:T(8,128)(2,1)}, u32[]{:S(2)}, u32[]{:S(2)}) collective-permute-start(bf16[32,4096]{1,0:T(8,128)(2,1)} %get-tuple-element.101), channel_id=1, source_target_pairs={{0,5},{1,4},{2,3},{3,2},{4,1},{5,0},{6,7},{7,6},{8,13},{9,12},{10,... | collective-permute-start | bytes 786440 | tf_op jit(solution)/shard_map/ppermute | solution.py:233
  104.6 0.0 collective-permute-start.8
  104.6 0.0 collective-permute-done.15.refs_6_
  104.6 1.0 collective-permute-start.16
  105.6 1.7 collective-permute-done.17.refs_7_
  107.4 11.1 %expert.3 = (bf16[32,4096]{1,0:T(8,128)(2,1)}, bf16[32,4096]{1,0:T(8,128)(2,1)}, bf16[32,4096]{1,0:T(8,128)(2,1)}, bf16[32,4096]{1,0:T(8,128)(2,1)}, bf16[32,409...) custom-call(bf16[32,4096]{1,0:T(8,128)(2,1)} %get-tuple-element.124., ...), custom_call_target="tpu_custom_call" | custom-call | flops 1024 | bytes 1024 | tf_op jit(solution)/shard_map/expert/pallas_call | solution.py:28
  118.4 4.4 %weight_part.4 = (bf16[16,2176]{1,0:T(8,128)(2,1)}, bf16[496,2176]{1,0:T(8,128)(2,1)}) custom-call(s32[1]{0:T(128)} %bitcast.4.refs_0_, bf16[256,4096]{1,0:T(8,128)(2,1)} %get-tuple-element.138.refs_1_, bf16[256,1408]{1,0:T(8,128)(2,1)} %get-tuple-element.127.refs_2_, bf16[256,704]{1,0:T(8,128)(2,1)} %get-tuple-element.128.refs_3_, ...), custom_call_target="tpu_custom_call" | custom-call | flops 1024 | bytes 1024 | tf_op jit(solution)/shard_map/weight_part/pallas_call | solution.py:28
  122.8 0.1 collective-permute-start.21
  122.9 0.0 collective-permute-done.13.refs_6_
  122.9 0.0 collective-permute-done.10.refs_5_
  122.9 9.6 %collective-permute-done.8.refs_4_ = bf16[32,4096]{1,0:T(8,128)(2,1)} collective-permute-done((bf16[32,4096]{1,0:T(8,128)(2,1)}, bf16[32,4096]{1,0:T(8,128)(2,1)}, u32[]{:S(2)}, u32[]{:S(2)}) %collective-permute-start.8) | collective-permute-done | bytes 262176 | tf_op jit(solution)/shard_map/ppermute | solution.py:233
  132.6 6.3 %collective-permute-start.18 = (bf16[32,4096]{1,0:T(8,128)(2,1)}, bf16[32,4096]{1,0:T(8,128)(2,1)}, u32[]{:S(2)}, u32[]{:S(2)}) collective-permute-start(bf16[32,4096]{1,0:T(8,128)(2,1)} %get-tuple-element.117), channel_id=1, source_target_pairs={{0,2},{1,7},{2,0},{3,5},{4,6},{5,3},{6,4},{7,1},{8,10},{9,15},{10,... | collective-permute-start | bytes 786440 | tf_op jit(solution)/shard_map/ppermute | solution.py:233
  138.8 4.3 %weight_part.5 = bf16[512,2176]{1,0:T(8,128)(2,1)} custom-call(s32[1]{0:T(128)} %bitcast.5.refs_0_, bf16[256,4096]{1,0:T(8,128)(2,1)} %get-tuple-element.138.refs_1_, bf16[256,1408]{1,0:T(8,128)(2,1)} %get-tuple-element.127.refs_2_, bf16[256,704]{1,0:T(8,128)(2,1)} %get-tuple-element.128.refs_3_, bf16[256,4096]{1,0:T(8,128)(2,1)} %get-tuple-element.129.refs_4_, ...), custom_call_target="tpu_custom_call" | custom-call | flops 1024 | bytes 1024 | tf_op jit(solution)/shard_map/weight_part/pallas_call | solution.py:28
  143.2 5.2 %weight_part.6 = (bf16[16,2176]{1,0:T(8,128)(2,1)}, bf16[496,2176]{1,0:T(8,128)(2,1)}) custom-call(s32[1]{0:T(128)} %bitcast.6.refs_0_, bf16[256,4096]{1,0:T(8,128)(2,1)} %get-tuple-element.138.refs_1_, bf16[256,1408]{1,0:T(8,128)(2,1)} %get-tuple-element.127.refs_2_, bf16[256,704]{1,0:T(8,128)(2,1)} %get-tuple-element.128.refs_3_, ...), custom_call_target="tpu_custom_call" | custom-call | flops 1024 | bytes 1024 | tf_op jit(solution)/shard_map/weight_part/pallas_call | solution.py:28
  148.4 1.6 collective-permute-start.24
  150.0 0.9 collective-permute-done.19.refs_9_
  150.9 2.2 collective-permute-done.24.refs_8_
  153.0 1.5 collective-permute-start.25
  154.6 3.4 %collective-permute-start.20 = (bf16[32,4096]{1,0:T(8,128)(2,1)}, bf16[32,4096]{1,0:T(8,128)(2,1)}, u32[]{:S(2)}, u32[]{:S(2)}) collective-permute-start(bf16[32,4096]{1,0:T(8,128)(2,1)} %get-tuple-element.121), channel_id=1, source_target_pairs={{0,3},{1,6},{2,5},{3,0},{4,7},{5,2},{6,1},{7,4},{8,11},{9,14},{10,... | collective-permute-start | bytes 786440 | tf_op jit(solution)/shard_map/ppermute | solution.py:233
  158.0 5.4 %collective-permute-done.20.refs_10_ = bf16[32,4096]{1,0:T(8,128)(2,1)} collective-permute-done((bf16[32,4096]{1,0:T(8,128)(2,1)}, bf16[32,4096]{1,0:T(8,128)(2,1)}, u32[]{:S(2)}, u32[]{:S(2)}) %collective-permute-start.20) | collective-permute-done | bytes 262176 | tf_op jit(solution)/shard_map/ppermute | solution.py:233
  163.4 5.5 %collective-permute-start.29 = (bf16[32,4096]{1,0:T(8,128)(2,1)}, bf16[32,4096]{1,0:T(8,128)(2,1)}, u32[]{:S(2)}, u32[]{:S(2)}) collective-permute-start(bf16[32,4096]{1,0:T(8,128)(2,1)} %get-tuple-element.150), channel_id=1, source_target_pairs={{0,6},{1,3},{2,4},{3,1},{4,2},{5,7},{6,0},{7,5},{8,14},{9,11},{10,... | collective-permute-start | bytes 786440 | tf_op jit(solution)/shard_map/ppermute | solution.py:233
  168.9 7.2 %collective-permute-done.29.refs_7_ = bf16[32,4096]{1,0:T(8,128)(2,1)} collective-permute-done((bf16[32,4096]{1,0:T(8,128)(2,1)}, bf16[32,4096]{1,0:T(8,128)(2,1)}, u32[]{:S(2)}, u32[]{:S(2)}) %collective-permute-start.29) | collective-permute-done | bytes 262176 | tf_op jit(solution)/shard_map/ppermute | solution.py:233
  176.1 13.9 %collective-permute-start.26 = (bf16[32,4096]{1,0:T(8,128)(2,1)}, bf16[32,4096]{1,0:T(8,128)(2,1)}, u32[]{:S(2)}, u32[]{:S(2)}) collective-permute-start(bf16[32,4096]{1,0:T(8,128)(2,1)} %get-tuple-element.144), channel_id=1, source_target_pairs={{0,4},{1,5},{2,6},{3,7},{4,0},{5,1},{6,2},{7,3},{8,12},{9,13},{10,... | collective-permute-start | bytes 786440 | tf_op jit(solution)/shard_map/ppermute | solution.py:233
  190.1 3.6 %combine.2 = (bf16[256,2048]{1,0:T(8,128)(2,1)}, bf16[256,2048]{1,0:T(8,128)(2,1)}) custom-call(s32[1,256]{1,0:T(1,128)} %bitcast.15, bf16[256,2048]{1,0:T(8,128)(2,1)} %refs_1_.5, bf16[256,2048]{1,0:T(8,128)(2,1)} %refs_2_.5, bf16[32,4096]{1,0:T(8,128)(2,1)} %get-tuple-element.93.refs_3_, bf16[32,4096]{1,0:T(8,128)(2,1)} %collective-permute-done.8.refs_4_, ...), custom_call_target="tpu_custom_call" | custom-call | flops 1024 | bytes 1024 | tf_op jit(solution)/shard_map/combine/pallas_call | solution.py:28
  193.7 0.0 collective-permute-done.28.refs_6_
  193.7 0.1 collective-permute-start.32
  193.8 0.0 collective-permute-done.27.refs_5_
  193.8 9.3 %collective-permute-start.31 = (bf16[32,4096]{1,0:T(8,128)(2,1)}, bf16[32,4096]{1,0:T(8,128)(2,1)}, u32[]{:S(2)}, u32[]{:S(2)}) collective-permute-start(bf16[32,4096]{1,0:T(8,128)(2,1)} %get-tuple-element.154), channel_id=1, source_target_pairs={{0,7},{1,2},{2,1},{3,4},{4,3},{5,6},{6,5},{7,0},{8,15},{9,10},{10,... | collective-permute-start | bytes 786440 | tf_op jit(solution)/shard_map/ppermute | solution.py:233
  203.1 4.0 %collective-permute-done.26.refs_4_ = bf16[32,4096]{1,0:T(8,128)(2,1)} collective-permute-done((bf16[32,4096]{1,0:T(8,128)(2,1)}, bf16[32,4096]{1,0:T(8,128)(2,1)}, u32[]{:S(2)}, u32[]{:S(2)}) %collective-permute-start.26) | collective-permute-done | bytes 262176 | tf_op jit(solution)/shard_map/ppermute | solution.py:233
  207.2 0.0 collective-permute-start.30
  207.2 0.0 collective-permute-done.23.refs_7_
  207.2 0.0 collective-permute-done.25.refs_9_
  207.2 6.8 %weight_part.7 = (f32[512,1408]{1,0:T(8,128)}, f32[704,512]{1,0:T(8,128)}) custom-call(s32[1]{0:T(128)} %bitcast.3.refs_0_, bf16[256,4096]{1,0:T(8,128)(2,1)} %get-tuple-element.138.refs_1_, bf16[256,1408]{1,0:T(8,128)(2,1)} %get-tuple-element.127.refs_2_, bf16[256,704]{1,0:T(8,128)(2,1)} %get-tuple-element.128.refs_3_, ...), custom_call_target="tpu_custom_call" | custom-call | flops 1024 | bytes 1024 | tf_op jit(solution)/shard_map/weight_part/pallas_call | solution.py:28
  214.0 0.0 collective-permute-done.32.refs_10_
  214.0 0.0 collective-permute-done.31.refs_9_
  214.0 1.5 collective-permute-done.30.refs_8_
  215.4 3.7 %combine.3 = (bf16[256,2048]{1,0:T(8,128)(2,1)}, bf16[256,2048]{1,0:T(8,128)(2,1)}) custom-call(s32[1,256]{1,0:T(1,128)} %bitcast.16, bf16[256,2048]{1,0:T(8,128)(2,1)} %get-tuple-element.122.refs_1_, bf16[256,2048]{1,0:T(8,128)(2,1)} %get-tuple-element.123.refs_2_, bf16[32,4096]{1,0:T(8,128)(2,1)} %get-tuple-element.142.refs_3_, ...), custom_call_target="tpu_custom_call" | custom-call | flops 1024 | bytes 1024 | tf_op jit(solution)/shard_map/combine/pallas_call | solution.py:28
  (12 shorter events, 0.0 us)
Async XLA Ops:
  4.1 28.4 %collective-permute-start = (bf16[32,4096]{1,0:T(8,128)(2,1)}, bf16[32,4096]{1,0:T(8,128)(2,1)}, u32[]{:S(2)}, u32[]{:S(2)}) collective-permute-start(bf16[32,4096]{1,0:T(8,128)(2,1)} %get-tuple-element.83), channel_id=1, source_target_pairs={{0,4},{1,5},{2,6},{3,7},{4,0},{5,1},{6,2},{7,3},{8,12},{9,13},{10,... | collective-permute-start | bytes 786440 | tf_op jit(solution)/shard_map/ppermute | solution.py:233
  8.2 34.0 %collective-permute-start.1 = (bf16[32,4096]{1,0:T(8,128)(2,1)}, bf16[32,4096]{1,0:T(8,128)(2,1)}, u32[]{:S(2)}, u32[]{:S(2)}) collective-permute-start(bf16[32,4096]{1,0:T(8,128)(2,1)} %get-tuple-element.84), channel_id=1, source_target_pairs={{0,5},{1,4},{2,3},{3,2},{4,1},{5,0},{6,7},{7,6},{8,13},{9,12},{10,... | collective-permute-start | bytes 786440 | tf_op jit(solution)/shard_map/ppermute | solution.py:233
  9.5 36.2 %collective-permute-start.2 = (bf16[32,4096]{1,0:T(8,128)(2,1)}, bf16[32,4096]{1,0:T(8,128)(2,1)}, u32[]{:S(2)}, u32[]{:S(2)}) collective-permute-start(bf16[32,4096]{1,0:T(8,128)(2,1)} %get-tuple-element.85), channel_id=1, source_target_pairs={{0,1},{1,0},{2,7},{3,6},{4,5},{5,4},{6,3},{7,2},{8,9},{9,8},{10,15... | collective-permute-start | bytes 786440 | tf_op jit(solution)/shard_map/ppermute | solution.py:233
  9.7 36.0 %collective-permute-start.3 = (bf16[32,4096]{1,0:T(8,128)(2,1)}, bf16[32,4096]{1,0:T(8,128)(2,1)}, u32[]{:S(2)}, u32[]{:S(2)}) collective-permute-start(bf16[32,4096]{1,0:T(8,128)(2,1)} %get-tuple-element.86), channel_id=1, source_target_pairs={{0,6},{1,3},{2,4},{3,1},{4,2},{5,7},{6,0},{7,5},{8,14},{9,11},{10,... | collective-permute-start | bytes 786440 | tf_op jit(solution)/shard_map/ppermute | solution.py:233
  32.5 18.8 %collective-permute-start.4 = (bf16[32,4096]{1,0:T(8,128)(2,1)}, bf16[32,4096]{1,0:T(8,128)(2,1)}, u32[]{:S(2)}, u32[]{:S(2)}) collective-permute-start(bf16[32,4096]{1,0:T(8,128)(2,1)} %get-tuple-element.88), channel_id=1, source_target_pairs={{0,2},{1,7},{2,0},{3,5},{4,6},{5,3},{6,4},{7,1},{8,10},{9,15},{10,... | collective-permute-start | bytes 786440 | tf_op jit(solution)/shard_map/ppermute | solution.py:233
  42.2 10.5 %collective-permute-start.5 = (bf16[32,4096]{1,0:T(8,128)(2,1)}, bf16[32,4096]{1,0:T(8,128)(2,1)}, u32[]{:S(2)}, u32[]{:S(2)}) collective-permute-start(bf16[32,4096]{1,0:T(8,128)(2,1)} %get-tuple-element.90), channel_id=1, source_target_pairs={{0,7},{1,2},{2,1},{3,4},{4,3},{5,6},{6,5},{7,0},{8,15},{9,10},{10,... | collective-permute-start | bytes 786440 | tf_op jit(solution)/shard_map/ppermute | solution.py:233
  45.6 8.8 %collective-permute-start.6 = (bf16[32,4096]{1,0:T(8,128)(2,1)}, bf16[32,4096]{1,0:T(8,128)(2,1)}, u32[]{:S(2)}, u32[]{:S(2)}) collective-permute-start(bf16[32,4096]{1,0:T(8,128)(2,1)} %get-tuple-element.92), channel_id=1, source_target_pairs={{0,3},{1,6},{2,5},{3,0},{4,7},{5,2},{6,1},{7,4},{8,11},{9,14},{10,... | collective-permute-start | bytes 786440 | tf_op jit(solution)/shard_map/ppermute | solution.py:233
  45.7 23.8 %collective-permute-start.11 = (bf16[32,4096]{1,0:T(8,128)(2,1)}, bf16[32,4096]{1,0:T(8,128)(2,1)}, u32[]{:S(2)}, u32[]{:S(2)}) collective-permute-start(bf16[32,4096]{1,0:T(8,128)(2,1)} %get-tuple-element.105), channel_id=1, source_target_pairs={{0,4},{1,5},{2,6},{3,7},{4,0},{5,1},{6,2},{7,3},{8,12},{9,13},{10,... | collective-permute-start | bytes 786440 | tf_op jit(solution)/shard_map/ppermute | solution.py:233
  51.3 35.6 %collective-permute-start.14 = (bf16[32,4096]{1,0:T(8,128)(2,1)}, bf16[32,4096]{1,0:T(8,128)(2,1)}, u32[]{:S(2)}, u32[]{:S(2)}) collective-permute-start(bf16[32,4096]{1,0:T(8,128)(2,1)} %get-tuple-element.111), channel_id=1, source_target_pairs={{0,5},{1,4},{2,3},{3,2},{4,1},{5,0},{6,7},{7,6},{8,13},{9,12},{10,... | collective-permute-start | bytes 786440 | tf_op jit(solution)/shard_map/ppermute | solution.py:233
  52.7 45.1 %collective-permute-start.7 = (bf16[32,4096]{1,0:T(8,128)(2,1)}, bf16[32,4096]{1,0:T(8,128)(2,1)}, u32[]{:S(2)}, u32[]{:S(2)}) collective-permute-start(bf16[32,4096]{1,0:T(8,128)(2,1)} %get-tuple-element.96), channel_id=1, source_target_pairs={{0,1},{1,0},{2,7},{3,6},{4,5},{5,4},{6,3},{7,2},{8,9},{9,8},{10,15... | collective-permute-start | bytes 786440 | tf_op jit(solution)/shard_map/ppermute | solution.py:233
  54.4 43.5 %collective-permute-start.9 = (bf16[32,4096]{1,0:T(8,128)(2,1)}, bf16[32,4096]{1,0:T(8,128)(2,1)}, u32[]{:S(2)}, u32[]{:S(2)}) collective-permute-start(bf16[32,4096]{1,0:T(8,128)(2,1)} %get-tuple-element.100), channel_id=1, source_target_pairs={{0,6},{1,3},{2,4},{3,1},{4,2},{5,7},{6,0},{7,5},{8,14},{9,11},{10,... | collective-permute-start | bytes 786440 | tf_op jit(solution)/shard_map/ppermute | solution.py:233
  69.5 28.4 %collective-permute-start.12 = (bf16[32,4096]{1,0:T(8,128)(2,1)}, bf16[32,4096]{1,0:T(8,128)(2,1)}, u32[]{:S(2)}, u32[]{:S(2)}) collective-permute-start(bf16[32,4096]{1,0:T(8,128)(2,1)} %get-tuple-element.106), channel_id=1, source_target_pairs={{0,2},{1,7},{2,0},{3,5},{4,6},{5,3},{6,4},{7,1},{8,10},{9,15},{10,... | collective-permute-start | bytes 786440 | tf_op jit(solution)/shard_map/ppermute | solution.py:233
  86.9 17.7 %collective-permute-start.15 = (bf16[32,4096]{1,0:T(8,128)(2,1)}, bf16[32,4096]{1,0:T(8,128)(2,1)}, u32[]{:S(2)}, u32[]{:S(2)}) collective-permute-start(bf16[32,4096]{1,0:T(8,128)(2,1)} %get-tuple-element.112), channel_id=1, source_target_pairs={{0,7},{1,2},{2,1},{3,4},{4,3},{5,6},{6,5},{7,0},{8,15},{9,10},{10,... | collective-permute-start | bytes 786440 | tf_op jit(solution)/shard_map/ppermute | solution.py:233
  97.8 9.6 %collective-permute-start.17 = (bf16[32,4096]{1,0:T(8,128)(2,1)}, bf16[32,4096]{1,0:T(8,128)(2,1)}, u32[]{:S(2)}, u32[]{:S(2)}) collective-permute-start(bf16[32,4096]{1,0:T(8,128)(2,1)} %get-tuple-element.116), channel_id=1, source_target_pairs={{0,3},{1,6},{2,5},{3,0},{4,7},{5,2},{6,1},{7,4},{8,11},{9,14},{10,... | collective-permute-start | bytes 786440 | tf_op jit(solution)/shard_map/ppermute | solution.py:233
  97.9 25.0 %collective-permute-start.13 = (bf16[32,4096]{1,0:T(8,128)(2,1)}, bf16[32,4096]{1,0:T(8,128)(2,1)}, u32[]{:S(2)}, u32[]{:S(2)}) collective-permute-start(bf16[32,4096]{1,0:T(8,128)(2,1)} %get-tuple-element.107), channel_id=1, source_target_pairs={{0,1},{1,0},{2,7},{3,6},{4,5},{5,4},{6,3},{7,2},{8,9},{9,8},{10,15... | collective-permute-start | bytes 786440 | tf_op jit(solution)/shard_map/ppermute | solution.py:233
  98.0 24.9 %collective-permute-start.10 = (bf16[32,4096]{1,0:T(8,128)(2,1)}, bf16[32,4096]{1,0:T(8,128)(2,1)}, u32[]{:S(2)}, u32[]{:S(2)}) collective-permute-start(bf16[32,4096]{1,0:T(8,128)(2,1)} %get-tuple-element.101), channel_id=1, source_target_pairs={{0,5},{1,4},{2,3},{3,2},{4,1},{5,0},{6,7},{7,6},{8,13},{9,12},{10,... | collective-permute-start | bytes 786440 | tf_op jit(solution)/shard_map/ppermute | solution.py:233
  104.6 27.9 %collective-permute-start.8 = (bf16[32,4096]{1,0:T(8,128)(2,1)}, bf16[32,4096]{1,0:T(8,128)(2,1)}, u32[]{:S(2)}, u32[]{:S(2)}) collective-permute-start(bf16[32,4096]{1,0:T(8,128)(2,1)} %get-tuple-element.97), channel_id=1, source_target_pairs={{0,4},{1,5},{2,6},{3,7},{4,0},{5,1},{6,2},{7,3},{8,12},{9,13},{10,... | collective-permute-start | bytes 786440 | tf_op jit(solution)/shard_map/ppermute | solution.py:233
  104.6 27.9 %collective-permute-start.16 = (bf16[32,4096]{1,0:T(8,128)(2,1)}, bf16[32,4096]{1,0:T(8,128)(2,1)}, u32[]{:S(2)}, u32[]{:S(2)}) collective-permute-start(bf16[32,4096]{1,0:T(8,128)(2,1)} %get-tuple-element.113), channel_id=1, source_target_pairs={{0,6},{1,3},{2,4},{3,1},{4,2},{5,7},{6,0},{7,5},{8,14},{9,11},{10,... | collective-permute-start | bytes 786440 | tf_op jit(solution)/shard_map/ppermute | solution.py:233
  122.8 9.7 %collective-permute-start.21 = (bf16[16,2176]{1,0:T(8,128)(2,1)}, bf16[16,2176]{1,0:T(8,128)(2,1)}, u32[]{:S(2)}, u32[]{:S(2)}) collective-permute-start(bf16[16,2176]{1,0:T(8,128)(2,1)} %get-tuple-element.132), channel_id=1, source_target_pairs={{0,8},{8,0},{16,24},{24,16},{1,9},{9,1},{17,25},{25,17},{2,10},{10... | collective-permute-start | bytes 208904 | tf_op jit(solution)/shard_map/ppermute | solution.py:233
  132.6 10.6 %collective-permute-start.22 = (bf16[496,2176]{1,0:T(8,128)(2,1)}, bf16[496,2176]{1,0:T(8,128)(2,1)}, u32[]{:S(2)}, u32[]{:S(2)}) collective-permute-start(bf16[496,2176]{1,0:T(8,128)(2,1)} %get-tuple-element.136), channel_id=1, source_target_pairs={{0,8},{8,0},{16,24},{24,16},{1,9},{9,1},{17,25},{25,17},{2,10},{10... | collective-permute-start | bytes 6475784 | tf_op jit(solution)/shard_map/ppermute | solution.py:233
  132.6 17.4 %collective-permute-start.18 = (bf16[32,4096]{1,0:T(8,128)(2,1)}, bf16[32,4096]{1,0:T(8,128)(2,1)}, u32[]{:S(2)}, u32[]{:S(2)}) collective-permute-start(bf16[32,4096]{1,0:T(8,128)(2,1)} %get-tuple-element.117), channel_id=1, source_target_pairs={{0,2},{1,7},{2,0},{3,5},{4,6},{5,3},{6,4},{7,1},{8,10},{9,15},{10,... | collective-permute-start | bytes 786440 | tf_op jit(solution)/shard_map/ppermute | solution.py:233
  138.8 12.0 %collective-permute-start.19 = (bf16[32,4096]{1,0:T(8,128)(2,1)}, bf16[32,4096]{1,0:T(8,128)(2,1)}, u32[]{:S(2)}, u32[]{:S(2)}) collective-permute-start(bf16[32,4096]{1,0:T(8,128)(2,1)} %get-tuple-element.119), channel_id=1, source_target_pairs={{0,7},{1,2},{2,1},{3,4},{4,3},{5,6},{6,5},{7,0},{8,15},{9,10},{10,... | collective-permute-start | bytes 786440 | tf_op jit(solution)/shard_map/ppermute | solution.py:233
  148.4 4.7 %collective-permute-start.24 = (bf16[16,2176]{1,0:T(8,128)(2,1)}, bf16[16,2176]{1,0:T(8,128)(2,1)}, u32[]{:S(2)}, u32[]{:S(2)}) collective-permute-start(bf16[16,2176]{1,0:T(8,128)(2,1)} %get-tuple-element.137), channel_id=1, source_target_pairs={{0,16},{8,24},{16,0},{24,8},{1,17},{9,25},{17,1},{25,9},{2,18},{10... | collective-permute-start | bytes 208904 | tf_op jit(solution)/shard_map/ppermute | solution.py:233
  150.0 57.2 %collective-permute-start.23 = (bf16[512,2176]{1,0:T(8,128)(2,1)}, bf16[512,2176]{1,0:T(8,128)(2,1)}, u32[]{:S(2)}, u32[]{:S(2)}) collective-permute-start(bf16[512,2176]{1,0:T(8,128)(2,1)} %weight_part.5), channel_id=1, source_target_pairs={{0,8},{8,0},{16,24},{24,16},{1,9},{9,1},{17,25},{25,17},{2,10},{10... | collective-permute-start | bytes 6684680 | tf_op jit(solution)/shard_map/ppermute | solution.py:233
  153.0 54.1 %collective-permute-start.25 = (bf16[496,2176]{1,0:T(8,128)(2,1)}, bf16[496,2176]{1,0:T(8,128)(2,1)}, u32[]{:S(2)}, u32[]{:S(2)}) collective-permute-start(bf16[496,2176]{1,0:T(8,128)(2,1)} %get-tuple-element.140), channel_id=1, source_target_pairs={{0,16},{8,24},{16,0},{24,8},{1,17},{9,25},{17,1},{25,9},{2,18},{10... | collective-permute-start | bytes 6475784 | tf_op jit(solution)/shard_map/ppermute | solution.py:233
  154.6 8.8 %collective-permute-start.20 = (bf16[32,4096]{1,0:T(8,128)(2,1)}, bf16[32,4096]{1,0:T(8,128)(2,1)}, u32[]{:S(2)}, u32[]{:S(2)}) collective-permute-start(bf16[32,4096]{1,0:T(8,128)(2,1)} %get-tuple-element.121), channel_id=1, source_target_pairs={{0,3},{1,6},{2,5},{3,0},{4,7},{5,2},{6,1},{7,4},{8,11},{9,14},{10,... | collective-permute-start | bytes 786440 | tf_op jit(solution)/shard_map/ppermute | solution.py:233
  163.4 12.8 %collective-permute-start.29 = (bf16[32,4096]{1,0:T(8,128)(2,1)}, bf16[32,4096]{1,0:T(8,128)(2,1)}, u32[]{:S(2)}, u32[]{:S(2)}) collective-permute-start(bf16[32,4096]{1,0:T(8,128)(2,1)} %get-tuple-element.150), channel_id=1, source_target_pairs={{0,6},{1,3},{2,4},{3,1},{4,2},{5,7},{6,0},{7,5},{8,14},{9,11},{10,... | collective-permute-start | bytes 786440 | tf_op jit(solution)/shard_map/ppermute | solution.py:233
  168.9 24.8 %collective-permute-start.28 = (bf16[32,4096]{1,0:T(8,128)(2,1)}, bf16[32,4096]{1,0:T(8,128)(2,1)}, u32[]{:S(2)}, u32[]{:S(2)}) collective-permute-start(bf16[32,4096]{1,0:T(8,128)(2,1)} %get-tuple-element.148), channel_id=1, source_target_pairs={{0,1},{1,0},{2,7},{3,6},{4,5},{5,4},{6,3},{7,2},{8,9},{9,8},{10,15... | collective-permute-start | bytes 786440 | tf_op jit(solution)/shard_map/ppermute | solution.py:233
  168.9 24.9 %collective-permute-start.27 = (bf16[32,4096]{1,0:T(8,128)(2,1)}, bf16[32,4096]{1,0:T(8,128)(2,1)}, u32[]{:S(2)}, u32[]{:S(2)}) collective-permute-start(bf16[32,4096]{1,0:T(8,128)(2,1)} %get-tuple-element.146), channel_id=1, source_target_pairs={{0,5},{1,4},{2,3},{3,2},{4,1},{5,0},{6,7},{7,6},{8,13},{9,12},{10,... | collective-permute-start | bytes 786440 | tf_op jit(solution)/shard_map/ppermute | solution.py:233
  176.1 31.0 %collective-permute-start.26 = (bf16[32,4096]{1,0:T(8,128)(2,1)}, bf16[32,4096]{1,0:T(8,128)(2,1)}, u32[]{:S(2)}, u32[]{:S(2)}) collective-permute-start(bf16[32,4096]{1,0:T(8,128)(2,1)} %get-tuple-element.144), channel_id=1, source_target_pairs={{0,4},{1,5},{2,6},{3,7},{4,0},{5,1},{6,2},{7,3},{8,12},{9,13},{10,... | collective-permute-start | bytes 786440 | tf_op jit(solution)/shard_map/ppermute | solution.py:233
  193.7 20.2 %collective-permute-start.32 = (bf16[32,4096]{1,0:T(8,128)(2,1)}, bf16[32,4096]{1,0:T(8,128)(2,1)}, u32[]{:S(2)}, u32[]{:S(2)}) collective-permute-start(bf16[32,4096]{1,0:T(8,128)(2,1)} %get-tuple-element.156), channel_id=1, source_target_pairs={{0,3},{1,6},{2,5},{3,0},{4,7},{5,2},{6,1},{7,4},{8,11},{9,14},{10,... | collective-permute-start | bytes 786440 | tf_op jit(solution)/shard_map/ppermute | solution.py:233
  193.8 20.1 %collective-permute-start.31 = (bf16[32,4096]{1,0:T(8,128)(2,1)}, bf16[32,4096]{1,0:T(8,128)(2,1)}, u32[]{:S(2)}, u32[]{:S(2)}) collective-permute-start(bf16[32,4096]{1,0:T(8,128)(2,1)} %get-tuple-element.154), channel_id=1, source_target_pairs={{0,7},{1,2},{2,1},{3,4},{4,3},{5,6},{6,5},{7,0},{8,15},{9,10},{10,... | collective-permute-start | bytes 786440 | tf_op jit(solution)/shard_map/ppermute | solution.py:233
  207.2 8.3 %collective-permute-start.30 = (bf16[32,4096]{1,0:T(8,128)(2,1)}, bf16[32,4096]{1,0:T(8,128)(2,1)}, u32[]{:S(2)}, u32[]{:S(2)}) collective-permute-start(bf16[32,4096]{1,0:T(8,128)(2,1)} %get-tuple-element.152), channel_id=1, source_target_pairs={{0,2},{1,7},{2,0},{3,5},{4,6},{5,3},{6,4},{7,1},{8,10},{9,15},{10,... | collective-permute-start | bytes 786440 | tf_op jit(solution)/shard_map/ppermute | solution.py:233

commit v15 on v13

--- a/solution.py
+++ b/solution.py
@@ -353,7 +353,7 @@
         if back:
             mixed, grad = combine(*cuts[part - 1], mixed, grad, back)
         blocks = results[part][0]
-        lane.window = 4 if part else 5
+        lane.window = 3 if part else 5
         back = [blocks[0]] + exchange(blocks, rounds, lane, numbers if part < parts - 1 else numbers[:-1])
     done = lane.done[count:]
 

time: 211 us -> 217 us (1.028); the launches traced: 211 us -> 214 us
  starting transfers between devices: 95.7 us -> 101 us
  waiting for transfers between devices: 57.7 us -> 54.5 us
    ppermute x33, starting transfers between devices: 95.7 us -> 101 us  [send(): self.done.append(lax.ppermute(after(value, *earlier), axis, pairs))]
    ppermute x33, waiting for transfers between devices: 57.7 us -> 54.5 us  [send(): self.done.append(lax.ppermute(after(value, *earlier), axis, pairs))]
  transfers between devices with their start and end apart: 33 -> 33, of which waited for: 11 -> 10; matrix products, arithmetic and copies ran while one was open for 0% -> 0% of each run, Pallas kernels for 24% -> 23%
where the time goes in v15:
time: 217 us; the launch traced here: 214 us
  starting transfers between devices  101 us (47%)
  Pallas kernels  56.8 us (26%)
  waiting for transfers between devices  54.5 us (25%)
    ppermute x33, starting transfers between devices, send(): self.done.append(lax.ppermute(after(value, *earlier), axis, pairs))  101 us
    pallas_call x10, Pallas kernels, call(): pl.pallas_call(kernel, in_specs=[pl.BlockSpec(memory_space=pltpu.SMEM)] *...  56.8 us
    ppermute x33, waiting for transfers between devices, send(): self.done.append(lax.ppermute(after(value, *earlier), axis, pairs))  54.5 us
  transfers between devices with their start and end apart: 33, of which 10 were waited for; matrix products, arithmetic and copies ran while one was open for 0% of the time, Pallas kernels for 23%

profile of v15, /device:TPU:0, one launch (start us, length us, event | category | flops | bytes accessed | tf_op | source)
XLA Modules:
  0.0 213.8 jit_solution(133394177428700982)
XLA Ops:
  0.6 3.4 %place.2 = (bf16[32,4096]{1,0:T(8,128)(2,1)}, bf16[32,4096]{1,0:T(8,128)(2,1)}, bf16[32,4096]{1,0:T(8,128)(2,1)}, bf16[32,4096]{1,0:T(8,128)(2,1)}, bf16[32,4096...) custom-call(s32[1,256]{1,0:T(1,128)} %bitcast.13, ...), custom_call_target="tpu_custom_call" | custom-call | flops 1024 | bytes 1024 | tf_op jit(solution)/shard_map/place/pallas_call | solution.py:28
  4.1 5.1 %collective-permute-start = (bf16[32,4096]{1,0:T(8,128)(2,1)}, bf16[32,4096]{1,0:T(8,128)(2,1)}, u32[]{:S(2)}, u32[]{:S(2)}) collective-permute-start(bf16[32,4096]{1,0:T(8,128)(2,1)} %get-tuple-element.83), channel_id=1, source_target_pairs={{0,5},{1,4},{2,3},{3,2},{4,1},{5,0},{6,7},{7,6},{8,13},{9,12},{10,... | collective-permute-start | bytes 786440 | tf_op jit(solution)/shard_map/ppermute | solution.py:233
  9.1 0.5 collective-permute-start.1
  9.6 1.3 collective-permute-start.2
  11.0 0.2 collective-permute-start.3
  11.2 11.0 %collective-permute-done.refs_1_ = bf16[32,4096]{1,0:T(8,128)(2,1)} collective-permute-done((bf16[32,4096]{1,0:T(8,128)(2,1)}, bf16[32,4096]{1,0:T(8,128)(2,1)}, u32[]{:S(2)}, u32[]{:S(2)}) %collective-permute-start) | collective-permute-done | bytes 262176 | tf_op jit(solution)/shard_map/ppermute | solution.py:233
  22.2 0.0 collective-permute-start.4
  22.2 0.0 collective-permute-done.1.refs_2_
  22.2 7.0 %collective-permute-start.5 = (bf16[32,4096]{1,0:T(8,128)(2,1)}, bf16[32,4096]{1,0:T(8,128)(2,1)}, u32[]{:S(2)}, u32[]{:S(2)}) collective-permute-start(bf16[32,4096]{1,0:T(8,128)(2,1)} %get-tuple-element.90), channel_id=1, source_target_pairs={{0,3},{1,6},{2,5},{3,0},{4,7},{5,2},{6,1},{7,4},{8,11},{9,14},{10,... | collective-permute-start | bytes 786440 | tf_op jit(solution)/shard_map/ppermute | solution.py:233
  29.2 3.4 %place.3 = (bf16[32,4096]{1,0:T(8,128)(2,1)}, bf16[32,4096]{1,0:T(8,128)(2,1)}, bf16[32,4096]{1,0:T(8,128)(2,1)}, bf16[32,4096]{1,0:T(8,128)(2,1)}, bf16[32,4096...) custom-call(s32[1,256]{1,0:T(1,128)} %bitcast.14, ...), custom_call_target="tpu_custom_call" | custom-call | flops 1024 | bytes 1024 | tf_op jit(solution)/shard_map/place/pallas_call | solution.py:28
  32.7 0.0 collective-permute-done.2.refs_3_
  32.7 8.3 %collective-permute-start.6 = (bf16[32,4096]{1,0:T(8,128)(2,1)}, bf16[32,4096]{1,0:T(8,128)(2,1)}, u32[]{:S(2)}, u32[]{:S(2)}) collective-permute-start(bf16[32,4096]{1,0:T(8,128)(2,1)} %get-tuple-element.92), channel_id=1, source_target_pairs={{0,4},{1,5},{2,6},{3,7},{4,0},{5,1},{6,2},{7,3},{8,12},{9,13},{10,... | collective-permute-start | bytes 786440 | tf_op jit(solution)/shard_map/ppermute | solution.py:233
  41.0 0.0 collective-permute-done.3.refs_4_
  41.0 0.0 collective-permute-start.11
  41.0 0.0 collective-permute-done.4.refs_5_
  41.0 1.7 collective-permute-start.14
  42.7 15.6 %collective-permute-start.7 = (bf16[32,4096]{1,0:T(8,128)(2,1)}, bf16[32,4096]{1,0:T(8,128)(2,1)}, u32[]{:S(2)}, u32[]{:S(2)}) collective-permute-start(bf16[32,4096]{1,0:T(8,128)(2,1)} %get-tuple-element.96), channel_id=1, source_target_pairs={{0,6},{1,3},{2,4},{3,1},{4,2},{5,7},{6,0},{7,5},{8,14},{9,11},{10,... | collective-permute-start | bytes 786440 | tf_op jit(solution)/shard_map/ppermute | solution.py:233
  58.3 8.9 %collective-permute-start.9 = (bf16[32,4096]{1,0:T(8,128)(2,1)}, bf16[32,4096]{1,0:T(8,128)(2,1)}, u32[]{:S(2)}, u32[]{:S(2)}) collective-permute-start(bf16[32,4096]{1,0:T(8,128)(2,1)} %get-tuple-element.100), channel_id=1, source_target_pairs={{0,2},{1,7},{2,0},{3,5},{4,6},{5,3},{6,4},{7,1},{8,10},{9,15},{10,... | collective-permute-start | bytes 786440 | tf_op jit(solution)/shard_map/ppermute | solution.py:233
  67.2 8.5 %collective-permute-done.11.refs_1_ = bf16[32,4096]{1,0:T(8,128)(2,1)} collective-permute-done((bf16[32,4096]{1,0:T(8,128)(2,1)}, bf16[32,4096]{1,0:T(8,128)(2,1)}, u32[]{:S(2)}, u32[]{:S(2)}) %collective-permute-start.11) | collective-permute-done | bytes 262176 | tf_op jit(solution)/shard_map/ppermute | solution.py:233
  75.7 0.0 collective-permute-done.14.refs_2_
  75.7 0.0 collective-permute-start.15
  75.7 10.9 %expert.2 = (bf16[32,4096]{1,0:T(8,128)(2,1)}, bf16[32,4096]{1,0:T(8,128)(2,1)}, bf16[32,4096]{1,0:T(8,128)(2,1)}, bf16[32,4096]{1,0:T(8,128)(2,1)}, bf16[32,409...) custom-call(bf16[32,4096]{1,0:T(8,128)(2,1)} %get-tuple-element.82.r, ...), custom_call_target="tpu_custom_call" | custom-call | flops 1024 | bytes 1024 | tf_op jit(solution)/shard_map/expert/pallas_call | solution.py:28
  86.6 5.3 %collective-permute-start.17 = (bf16[32,4096]{1,0:T(8,128)(2,1)}, bf16[32,4096]{1,0:T(8,128)(2,1)}, u32[]{:S(2)}, u32[]{:S(2)}) collective-permute-start(bf16[32,4096]{1,0:T(8,128)(2,1)} %get-tuple-element.116), channel_id=1, source_target_pairs={{0,4},{1,5},{2,6},{3,7},{4,0},{5,1},{6,2},{7,3},{8,12},{9,13},{10,... | collective-permute-start | bytes 786440 | tf_op jit(solution)/shard_map/ppermute | solution.py:233
  92.0 0.4 collective-permute-start.13
  92.4 14.9 %collective-permute-start.10 = (bf16[32,4096]{1,0:T(8,128)(2,1)}, bf16[32,4096]{1,0:T(8,128)(2,1)}, u32[]{:S(2)}, u32[]{:S(2)}) collective-permute-start(bf16[32,4096]{1,0:T(8,128)(2,1)} %get-tuple-element.101), channel_id=1, source_target_pairs={{0,1},{1,0},{2,7},{3,6},{4,5},{5,4},{6,3},{7,2},{8,9},{9,8},{10,15... | collective-permute-start | bytes 786440 | tf_op jit(solution)/shard_map/ppermute | solution.py:233
  107.2 0.0 collective-permute-start.8
  107.2 0.0 collective-permute-done.15.refs_6_
  107.2 0.0 collective-permute-start.16
  107.2 3.6 %collective-permute-done.17.refs_7_ = bf16[32,4096]{1,0:T(8,128)(2,1)} collective-permute-done((bf16[32,4096]{1,0:T(8,128)(2,1)}, bf16[32,4096]{1,0:T(8,128)(2,1)}, u32[]{:S(2)}, u32[]{:S(2)}) %collective-permute-start.17) | collective-permute-done | bytes 262176 | tf_op jit(solution)/shard_map/ppermute | solution.py:233
  110.8 11.1 %expert.3 = (bf16[32,4096]{1,0:T(8,128)(2,1)}, bf16[32,4096]{1,0:T(8,128)(2,1)}, bf16[32,4096]{1,0:T(8,128)(2,1)}, bf16[32,4096]{1,0:T(8,128)(2,1)}, bf16[32,409...) custom-call(bf16[32,4096]{1,0:T(8,128)(2,1)} %get-tuple-element.124., ...), custom_call_target="tpu_custom_call" | custom-call | flops 1024 | bytes 1024 | tf_op jit(solution)/shard_map/expert/pallas_call | solution.py:28
  121.9 4.4 %weight_part.4 = (bf16[16,2176]{1,0:T(8,128)(2,1)}, bf16[496,2176]{1,0:T(8,128)(2,1)}) custom-call(s32[1]{0:T(128)} %bitcast.4.refs_0_, bf16[256,4096]{1,0:T(8,128)(2,1)} %get-tuple-element.138.refs_1_, bf16[256,1408]{1,0:T(8,128)(2,1)} %get-tuple-element.127.refs_2_, bf16[256,704]{1,0:T(8,128)(2,1)} %get-tuple-element.128.refs_3_, ...), custom_call_target="tpu_custom_call" | custom-call | flops 1024 | bytes 1024 | tf_op jit(solution)/shard_map/weight_part/pallas_call | solution.py:28
  126.3 0.1 collective-permute-start.21
  126.4 0.0 collective-permute-done.10.refs_5_
  126.4 0.0 collective-permute-done.8.refs_4_
  126.4 1.6 collective-permute-done.21.refs_7_
  128.0 0.2 collective-permute-start.22
  128.1 1.0 collective-permute-start.19
  129.1 4.3 %weight_part.5 = bf16[512,2176]{1,0:T(8,128)(2,1)} custom-call(s32[1]{0:T(128)} %bitcast.5.refs_0_, bf16[256,4096]{1,0:T(8,128)(2,1)} %get-tuple-element.138.refs_1_, bf16[256,1408]{1,0:T(8,128)(2,1)} %get-tuple-element.127.refs_2_, bf16[256,704]{1,0:T(8,128)(2,1)} %get-tuple-element.128.refs_3_, bf16[256,4096]{1,0:T(8,128)(2,1)} %get-tuple-element.129.refs_4_, ...), custom_call_target="tpu_custom_call" | custom-call | flops 1024 | bytes 1024 | tf_op jit(solution)/shard_map/weight_part/pallas_call | solution.py:28
  133.5 0.0 collective-permute-done.22.refs_8_
  133.5 5.2 %weight_part.6 = (bf16[16,2176]{1,0:T(8,128)(2,1)}, bf16[496,2176]{1,0:T(8,128)(2,1)}) custom-call(s32[1]{0:T(128)} %bitcast.6.refs_0_, bf16[256,4096]{1,0:T(8,128)(2,1)} %get-tuple-element.138.refs_1_, bf16[256,1408]{1,0:T(8,128)(2,1)} %get-tuple-element.127.refs_2_, bf16[256,704]{1,0:T(8,128)(2,1)} %get-tuple-element.128.refs_3_, ...), custom_call_target="tpu_custom_call" | custom-call | flops 1024 | bytes 1024 | tf_op jit(solution)/shard_map/weight_part/pallas_call | solution.py:28
  138.6 1.1 collective-permute-start.24
  139.7 0.6 collective-permute-done.18.refs_8_
  140.3 3.2 %collective-permute-done.19.refs_9_ = bf16[32,4096]{1,0:T(8,128)(2,1)} collective-permute-done((bf16[32,4096]{1,0:T(8,128)(2,1)}, bf16[32,4096]{1,0:T(8,128)(2,1)}, u32[]{:S(2)}, u32[]{:S(2)}) %collective-permute-start.19) | collective-permute-done | bytes 262176 | tf_op jit(solution)/shard_map/ppermute | solution.py:233
  143.5 0.0 collective-permute-done.24.refs_8_
  143.5 1.0 collective-permute-start.25
  144.5 4.1 %collective-permute-start.20 = (bf16[32,4096]{1,0:T(8,128)(2,1)}, bf16[32,4096]{1,0:T(8,128)(2,1)}, u32[]{:S(2)}, u32[]{:S(2)}) collective-permute-start(bf16[32,4096]{1,0:T(8,128)(2,1)} %get-tuple-element.121), channel_id=1, source_target_pairs={{0,4},{1,5},{2,6},{3,7},{4,0},{5,1},{6,2},{7,3},{8,12},{9,13},{10,... | collective-permute-start | bytes 786440 | tf_op jit(solution)/shard_map/ppermute | solution.py:233
  148.6 0.5 collective-permute-start.26
  149.1 11.3 %collective-permute-done.20.refs_10_ = bf16[32,4096]{1,0:T(8,128)(2,1)} collective-permute-done((bf16[32,4096]{1,0:T(8,128)(2,1)}, bf16[32,4096]{1,0:T(8,128)(2,1)}, u32[]{:S(2)}, u32[]{:S(2)}) %collective-permute-start.20) | collective-permute-done | bytes 262176 | tf_op jit(solution)/shard_map/ppermute | solution.py:233
  160.4 7.4 %collective-permute-start.28 = (bf16[32,4096]{1,0:T(8,128)(2,1)}, bf16[32,4096]{1,0:T(8,128)(2,1)}, u32[]{:S(2)}, u32[]{:S(2)}) collective-permute-start(bf16[32,4096]{1,0:T(8,128)(2,1)} %get-tuple-element.148), channel_id=1, source_target_pairs={{0,6},{1,3},{2,4},{3,1},{4,2},{5,7},{6,0},{7,5},{8,14},{9,11},{10,... | collective-permute-start | bytes 786440 | tf_op jit(solution)/shard_map/ppermute | solution.py:233
  167.8 0.0 collective-permute-start.27
  167.8 0.0 collective-permute-start.29
  167.9 3.6 %combine.2 = (bf16[256,2048]{1,0:T(8,128)(2,1)}, bf16[256,2048]{1,0:T(8,128)(2,1)}) custom-call(s32[1,256]{1,0:T(1,128)} %bitcast.15, bf16[256,2048]{1,0:T(8,128)(2,1)} %refs_1_.5, bf16[256,2048]{1,0:T(8,128)(2,1)} %refs_2_.5, bf16[32,4096]{1,0:T(8,128)(2,1)} %get-tuple-element.93.refs_3_, bf16[32,4096]{1,0:T(8,128)(2,1)} %collective-permute-done.8.refs_4_, ...), custom_call_target="tpu_custom_call" | custom-call | flops 1024 | bytes 1024 | tf_op jit(solution)/shard_map/combine/pallas_call | solution.py:28
  171.5 3.8 %collective-permute-done.28.refs_6_ = bf16[32,4096]{1,0:T(8,128)(2,1)} collective-permute-done((bf16[32,4096]{1,0:T(8,128)(2,1)}, bf16[32,4096]{1,0:T(8,128)(2,1)}, u32[]{:S(2)}, u32[]{:S(2)}) %collective-permute-start.28) | collective-permute-done | bytes 262176 | tf_op jit(solution)/shard_map/ppermute | solution.py:233
  175.3 0.0 collective-permute-start.31
  175.3 0.0 collective-permute-done.27.refs_5_
  175.4 16.3 %collective-permute-start.30 = (bf16[32,4096]{1,0:T(8,128)(2,1)}, bf16[32,4096]{1,0:T(8,128)(2,1)}, u32[]{:S(2)}, u32[]{:S(2)}) collective-permute-start(bf16[32,4096]{1,0:T(8,128)(2,1)} %get-tuple-element.152), channel_id=1, source_target_pairs={{0,7},{1,2},{2,1},{3,4},{4,3},{5,6},{6,5},{7,0},{8,15},{9,10},{10,... | collective-permute-start | bytes 786440 | tf_op jit(solution)/shard_map/ppermute | solution.py:233
  191.6 0.0 collective-permute-done.29.refs_7_
  191.6 0.6 collective-permute-start.32
  192.2 0.0 collective-permute-done.23.refs_7_
  192.2 0.0 collective-permute-done.25.refs_9_
  192.2 6.8 %weight_part.7 = (f32[512,1408]{1,0:T(8,128)}, f32[704,512]{1,0:T(8,128)}) custom-call(s32[1]{0:T(128)} %bitcast.3.refs_0_, bf16[256,4096]{1,0:T(8,128)(2,1)} %get-tuple-element.138.refs_1_, bf16[256,1408]{1,0:T(8,128)(2,1)} %get-tuple-element.127.refs_2_, bf16[256,704]{1,0:T(8,128)(2,1)} %get-tuple-element.128.refs_3_, ...), custom_call_target="tpu_custom_call" | custom-call | flops 1024 | bytes 1024 | tf_op jit(solution)/shard_map/weight_part/pallas_call | solution.py:28
  199.1 7.3 %collective-permute-done.30.refs_8_ = bf16[32,4096]{1,0:T(8,128)(2,1)} collective-permute-done((bf16[32,4096]{1,0:T(8,128)(2,1)}, bf16[32,4096]{1,0:T(8,128)(2,1)}, u32[]{:S(2)}, u32[]{:S(2)}) %collective-permute-start.30) | collective-permute-done | bytes 262176 | tf_op jit(solution)/shard_map/ppermute | solution.py:233
  206.4 3.6 %collective-permute-done.32.refs_10_ = bf16[32,4096]{1,0:T(8,128)(2,1)} collective-permute-done((bf16[32,4096]{1,0:T(8,128)(2,1)}, bf16[32,4096]{1,0:T(8,128)(2,1)}, u32[]{:S(2)}, u32[]{:S(2)}) %collective-permute-start.32) | collective-permute-done | bytes 262176 | tf_op jit(solution)/shard_map/ppermute | solution.py:233
  209.9 3.7 %combine.3 = (bf16[256,2048]{1,0:T(8,128)(2,1)}, bf16[256,2048]{1,0:T(8,128)(2,1)}) custom-call(s32[1,256]{1,0:T(1,128)} %bitcast.16, bf16[256,2048]{1,0:T(8,128)(2,1)} %get-tuple-element.122.refs_1_, bf16[256,2048]{1,0:T(8,128)(2,1)} %get-tuple-element.123.refs_2_, bf16[32,4096]{1,0:T(8,128)(2,1)} %get-tuple-element.142.refs_3_, ...), custom_call_target="tpu_custom_call" | custom-call | flops 1024 | bytes 1024 | tf_op jit(solution)/shard_map/combine/pallas_call | solution.py:28
  (12 shorter events, 0.0 us)
Async XLA Ops:
  4.1 18.2 %collective-permute-start = (bf16[32,4096]{1,0:T(8,128)(2,1)}, bf16[32,4096]{1,0:T(8,128)(2,1)}, u32[]{:S(2)}, u32[]{:S(2)}) collective-permute-start(bf16[32,4096]{1,0:T(8,128)(2,1)} %get-tuple-element.83), channel_id=1, source_target_pairs={{0,5},{1,4},{2,3},{3,2},{4,1},{5,0},{6,7},{7,6},{8,13},{9,12},{10,... | collective-permute-start | bytes 786440 | tf_op jit(solution)/shard_map/ppermute | solution.py:233
  9.1 13.1 %collective-permute-start.1 = (bf16[32,4096]{1,0:T(8,128)(2,1)}, bf16[32,4096]{1,0:T(8,128)(2,1)}, u32[]{:S(2)}, u32[]{:S(2)}) collective-permute-start(bf16[32,4096]{1,0:T(8,128)(2,1)} %get-tuple-element.84), channel_id=1, source_target_pairs={{0,1},{1,0},{2,7},{3,6},{4,5},{5,4},{6,3},{7,2},{8,9},{9,8},{10,15... | collective-permute-start | bytes 786440 | tf_op jit(solution)/shard_map/ppermute | solution.py:233
  9.6 23.0 %collective-permute-start.2 = (bf16[32,4096]{1,0:T(8,128)(2,1)}, bf16[32,4096]{1,0:T(8,128)(2,1)}, u32[]{:S(2)}, u32[]{:S(2)}) collective-permute-start(bf16[32,4096]{1,0:T(8,128)(2,1)} %get-tuple-element.85), channel_id=1, source_target_pairs={{0,6},{1,3},{2,4},{3,1},{4,2},{5,7},{6,0},{7,5},{8,14},{9,11},{10,... | collective-permute-start | bytes 786440 | tf_op jit(solution)/shard_map/ppermute | solution.py:233
  11.0 30.0 %collective-permute-start.3 = (bf16[32,4096]{1,0:T(8,128)(2,1)}, bf16[32,4096]{1,0:T(8,128)(2,1)}, u32[]{:S(2)}, u32[]{:S(2)}) collective-permute-start(bf16[32,4096]{1,0:T(8,128)(2,1)} %get-tuple-element.86), channel_id=1, source_target_pairs={{0,2},{1,7},{2,0},{3,5},{4,6},{5,3},{6,4},{7,1},{8,10},{9,15},{10,... | collective-permute-start | bytes 786440 | tf_op jit(solution)/shard_map/ppermute | solution.py:233
  22.2 18.8 %collective-permute-start.4 = (bf16[32,4096]{1,0:T(8,128)(2,1)}, bf16[32,4096]{1,0:T(8,128)(2,1)}, u32[]{:S(2)}, u32[]{:S(2)}) collective-permute-start(bf16[32,4096]{1,0:T(8,128)(2,1)} %get-tuple-element.88), channel_id=1, source_target_pairs={{0,7},{1,2},{2,1},{3,4},{4,3},{5,6},{6,5},{7,0},{8,15},{9,10},{10,... | collective-permute-start | bytes 786440 | tf_op jit(solution)/shard_map/ppermute | solution.py:233
  22.2 20.4 %collective-permute-start.5 = (bf16[32,4096]{1,0:T(8,128)(2,1)}, bf16[32,4096]{1,0:T(8,128)(2,1)}, u32[]{:S(2)}, u32[]{:S(2)}) collective-permute-start(bf16[32,4096]{1,0:T(8,128)(2,1)} %get-tuple-element.90), channel_id=1, source_target_pairs={{0,3},{1,6},{2,5},{3,0},{4,7},{5,2},{6,1},{7,4},{8,11},{9,14},{10,... | collective-permute-start | bytes 786440 | tf_op jit(solution)/shard_map/ppermute | solution.py:233
  32.7 25.6 %collective-permute-start.6 = (bf16[32,4096]{1,0:T(8,128)(2,1)}, bf16[32,4096]{1,0:T(8,128)(2,1)}, u32[]{:S(2)}, u32[]{:S(2)}) collective-permute-start(bf16[32,4096]{1,0:T(8,128)(2,1)} %get-tuple-element.92), channel_id=1, source_target_pairs={{0,4},{1,5},{2,6},{3,7},{4,0},{5,1},{6,2},{7,3},{8,12},{9,13},{10,... | collective-permute-start | bytes 786440 | tf_op jit(solution)/shard_map/ppermute | solution.py:233
  41.0 34.7 %collective-permute-start.11 = (bf16[32,4096]{1,0:T(8,128)(2,1)}, bf16[32,4096]{1,0:T(8,128)(2,1)}, u32[]{:S(2)}, u32[]{:S(2)}) collective-permute-start(bf16[32,4096]{1,0:T(8,128)(2,1)} %get-tuple-element.105), channel_id=1, source_target_pairs={{0,5},{1,4},{2,3},{3,2},{4,1},{5,0},{6,7},{7,6},{8,13},{9,12},{10,... | collective-permute-start | bytes 786440 | tf_op jit(solution)/shard_map/ppermute | solution.py:233
  41.0 34.7 %collective-permute-start.14 = (bf16[32,4096]{1,0:T(8,128)(2,1)}, bf16[32,4096]{1,0:T(8,128)(2,1)}, u32[]{:S(2)}, u32[]{:S(2)}) collective-permute-start(bf16[32,4096]{1,0:T(8,128)(2,1)} %get-tuple-element.111), channel_id=1, source_target_pairs={{0,1},{1,0},{2,7},{3,6},{4,5},{5,4},{6,3},{7,2},{8,9},{9,8},{10,15... | collective-permute-start | bytes 786440 | tf_op jit(solution)/shard_map/ppermute | solution.py:233
  42.7 43.9 %collective-permute-start.7 = (bf16[32,4096]{1,0:T(8,128)(2,1)}, bf16[32,4096]{1,0:T(8,128)(2,1)}, u32[]{:S(2)}, u32[]{:S(2)}) collective-permute-start(bf16[32,4096]{1,0:T(8,128)(2,1)} %get-tuple-element.96), channel_id=1, source_target_pairs={{0,6},{1,3},{2,4},{3,1},{4,2},{5,7},{6,0},{7,5},{8,14},{9,11},{10,... | collective-permute-start | bytes 786440 | tf_op jit(solution)/shard_map/ppermute | solution.py:233
  58.3 33.7 %collective-permute-start.9 = (bf16[32,4096]{1,0:T(8,128)(2,1)}, bf16[32,4096]{1,0:T(8,128)(2,1)}, u32[]{:S(2)}, u32[]{:S(2)}) collective-permute-start(bf16[32,4096]{1,0:T(8,128)(2,1)} %get-tuple-element.100), channel_id=1, source_target_pairs={{0,2},{1,7},{2,0},{3,5},{4,6},{5,3},{6,4},{7,1},{8,10},{9,15},{10,... | collective-permute-start | bytes 786440 | tf_op jit(solution)/shard_map/ppermute | solution.py:233
  75.7 16.3 %collective-permute-start.12 = (bf16[32,4096]{1,0:T(8,128)(2,1)}, bf16[32,4096]{1,0:T(8,128)(2,1)}, u32[]{:S(2)}, u32[]{:S(2)}) collective-permute-start(bf16[32,4096]{1,0:T(8,128)(2,1)} %get-tuple-element.106), channel_id=1, source_target_pairs={{0,7},{1,2},{2,1},{3,4},{4,3},{5,6},{6,5},{7,0},{8,15},{9,10},{10,... | collective-permute-start | bytes 786440 | tf_op jit(solution)/shard_map/ppermute | solution.py:233
  75.7 31.5 %collective-permute-start.15 = (bf16[32,4096]{1,0:T(8,128)(2,1)}, bf16[32,4096]{1,0:T(8,128)(2,1)}, u32[]{:S(2)}, u32[]{:S(2)}) collective-permute-start(bf16[32,4096]{1,0:T(8,128)(2,1)} %get-tuple-element.112), channel_id=1, source_target_pairs={{0,3},{1,6},{2,5},{3,0},{4,7},{5,2},{6,1},{7,4},{8,11},{9,14},{10,... | collective-permute-start | bytes 786440 | tf_op jit(solution)/shard_map/ppermute | solution.py:233
  86.6 24.2 %collective-permute-start.17 = (bf16[32,4096]{1,0:T(8,128)(2,1)}, bf16[32,4096]{1,0:T(8,128)(2,1)}, u32[]{:S(2)}, u32[]{:S(2)}) collective-permute-start(bf16[32,4096]{1,0:T(8,128)(2,1)} %get-tuple-element.116), channel_id=1, source_target_pairs={{0,4},{1,5},{2,6},{3,7},{4,0},{5,1},{6,2},{7,3},{8,12},{9,13},{10,... | collective-permute-start | bytes 786440 | tf_op jit(solution)/shard_map/ppermute | solution.py:233
  92.0 34.4 %collective-permute-start.13 = (bf16[32,4096]{1,0:T(8,128)(2,1)}, bf16[32,4096]{1,0:T(8,128)(2,1)}, u32[]{:S(2)}, u32[]{:S(2)}) collective-permute-start(bf16[32,4096]{1,0:T(8,128)(2,1)} %get-tuple-element.107), channel_id=1, source_target_pairs={{0,6},{1,3},{2,4},{3,1},{4,2},{5,7},{6,0},{7,5},{8,14},{9,11},{10,... | collective-permute-start | bytes 786440 | tf_op jit(solution)/shard_map/ppermute | solution.py:233
  92.4 34.0 %collective-permute-start.10 = (bf16[32,4096]{1,0:T(8,128)(2,1)}, bf16[32,4096]{1,0:T(8,128)(2,1)}, u32[]{:S(2)}, u32[]{:S(2)}) collective-permute-start(bf16[32,4096]{1,0:T(8,128)(2,1)} %get-tuple-element.101), channel_id=1, source_target_pairs={{0,1},{1,0},{2,7},{3,6},{4,5},{5,4},{6,3},{7,2},{8,9},{9,8},{10,15... | collective-permute-start | bytes 786440 | tf_op jit(solution)/shard_map/ppermute | solution.py:233
  107.2 19.2 %collective-permute-start.8 = (bf16[32,4096]{1,0:T(8,128)(2,1)}, bf16[32,4096]{1,0:T(8,128)(2,1)}, u32[]{:S(2)}, u32[]{:S(2)}) collective-permute-start(bf16[32,4096]{1,0:T(8,128)(2,1)} %get-tuple-element.97), channel_id=1, source_target_pairs={{0,5},{1,4},{2,3},{3,2},{4,1},{5,0},{6,7},{7,6},{8,13},{9,12},{10,... | collective-permute-start | bytes 786440 | tf_op jit(solution)/shard_map/ppermute | solution.py:233
  107.2 20.7 %collective-permute-start.16 = (bf16[32,4096]{1,0:T(8,128)(2,1)}, bf16[32,4096]{1,0:T(8,128)(2,1)}, u32[]{:S(2)}, u32[]{:S(2)}) collective-permute-start(bf16[32,4096]{1,0:T(8,128)(2,1)} %get-tuple-element.113), channel_id=1, source_target_pairs={{0,2},{1,7},{2,0},{3,5},{4,6},{5,3},{6,4},{7,1},{8,10},{9,15},{10,... | collective-permute-start | bytes 786440 | tf_op jit(solution)/shard_map/ppermute | solution.py:233
  126.3 1.7 collective-permute-start.21
  128.0 5.5 %collective-permute-start.22 = (bf16[496,2176]{1,0:T(8,128)(2,1)}, bf16[496,2176]{1,0:T(8,128)(2,1)}, u32[]{:S(2)}, u32[]{:S(2)}) collective-permute-start(bf16[496,2176]{1,0:T(8,128)(2,1)} %get-tuple-element.136), channel_id=1, source_target_pairs={{0,8},{8,0},{16,24},{24,16},{1,9},{9,1},{17,25},{25,17},{2,10},{10... | collective-permute-start | bytes 6475784 | tf_op jit(solution)/shard_map/ppermute | solution.py:233
  128.1 12.2 %collective-permute-start.18 = (bf16[32,4096]{1,0:T(8,128)(2,1)}, bf16[32,4096]{1,0:T(8,128)(2,1)}, u32[]{:S(2)}, u32[]{:S(2)}) collective-permute-start(bf16[32,4096]{1,0:T(8,128)(2,1)} %get-tuple-element.117), channel_id=1, source_target_pairs={{0,7},{1,2},{2,1},{3,4},{4,3},{5,6},{6,5},{7,0},{8,15},{9,10},{10,... | collective-permute-start | bytes 786440 | tf_op jit(solution)/shard_map/ppermute | solution.py:233
  128.1 15.4 %collective-permute-start.19 = (bf16[32,4096]{1,0:T(8,128)(2,1)}, bf16[32,4096]{1,0:T(8,128)(2,1)}, u32[]{:S(2)}, u32[]{:S(2)}) collective-permute-start(bf16[32,4096]{1,0:T(8,128)(2,1)} %get-tuple-element.119), channel_id=1, source_target_pairs={{0,3},{1,6},{2,5},{3,0},{4,7},{5,2},{6,1},{7,4},{8,11},{9,14},{10,... | collective-permute-start | bytes 786440 | tf_op jit(solution)/shard_map/ppermute | solution.py:233
  138.6 4.9 %collective-permute-start.24 = (bf16[16,2176]{1,0:T(8,128)(2,1)}, bf16[16,2176]{1,0:T(8,128)(2,1)}, u32[]{:S(2)}, u32[]{:S(2)}) collective-permute-start(bf16[16,2176]{1,0:T(8,128)(2,1)} %get-tuple-element.137), channel_id=1, source_target_pairs={{0,16},{8,24},{16,0},{24,8},{1,17},{9,25},{17,1},{25,9},{2,18},{10... | collective-permute-start | bytes 208904 | tf_op jit(solution)/shard_map/ppermute | solution.py:233
  139.7 52.5 %collective-permute-start.23 = (bf16[512,2176]{1,0:T(8,128)(2,1)}, bf16[512,2176]{1,0:T(8,128)(2,1)}, u32[]{:S(2)}, u32[]{:S(2)}) collective-permute-start(bf16[512,2176]{1,0:T(8,128)(2,1)} %weight_part.5), channel_id=1, source_target_pairs={{0,8},{8,0},{16,24},{24,16},{1,9},{9,1},{17,25},{25,17},{2,10},{10... | collective-permute-start | bytes 6684680 | tf_op jit(solution)/shard_map/ppermute | solution.py:233
  143.5 48.7 %collective-permute-start.25 = (bf16[496,2176]{1,0:T(8,128)(2,1)}, bf16[496,2176]{1,0:T(8,128)(2,1)}, u32[]{:S(2)}, u32[]{:S(2)}) collective-permute-start(bf16[496,2176]{1,0:T(8,128)(2,1)} %get-tuple-element.140), channel_id=1, source_target_pairs={{0,16},{8,24},{16,0},{24,8},{1,17},{9,25},{17,1},{25,9},{2,18},{10... | collective-permute-start | bytes 6475784 | tf_op jit(solution)/shard_map/ppermute | solution.py:233
  144.5 15.9 %collective-permute-start.20 = (bf16[32,4096]{1,0:T(8,128)(2,1)}, bf16[32,4096]{1,0:T(8,128)(2,1)}, u32[]{:S(2)}, u32[]{:S(2)}) collective-permute-start(bf16[32,4096]{1,0:T(8,128)(2,1)} %get-tuple-element.121), channel_id=1, source_target_pairs={{0,4},{1,5},{2,6},{3,7},{4,0},{5,1},{6,2},{7,3},{8,12},{9,13},{10,... | collective-permute-start | bytes 786440 | tf_op jit(solution)/shard_map/ppermute | solution.py:233
  148.6 19.2 %collective-permute-start.26 = (bf16[32,4096]{1,0:T(8,128)(2,1)}, bf16[32,4096]{1,0:T(8,128)(2,1)}, u32[]{:S(2)}, u32[]{:S(2)}) collective-permute-start(bf16[32,4096]{1,0:T(8,128)(2,1)} %get-tuple-element.144), channel_id=1, source_target_pairs={{0,5},{1,4},{2,3},{3,2},{4,1},{5,0},{6,7},{7,6},{8,13},{9,12},{10,... | collective-permute-start | bytes 786440 | tf_op jit(solution)/shard_map/ppermute | solution.py:233
  160.4 15.0 %collective-permute-start.28 = (bf16[32,4096]{1,0:T(8,128)(2,1)}, bf16[32,4096]{1,0:T(8,128)(2,1)}, u32[]{:S(2)}, u32[]{:S(2)}) collective-permute-start(bf16[32,4096]{1,0:T(8,128)(2,1)} %get-tuple-element.148), channel_id=1, source_target_pairs={{0,6},{1,3},{2,4},{3,1},{4,2},{5,7},{6,0},{7,5},{8,14},{9,11},{10,... | collective-permute-start | bytes 786440 | tf_op jit(solution)/shard_map/ppermute | solution.py:233
  167.8 7.5 %collective-permute-start.27 = (bf16[32,4096]{1,0:T(8,128)(2,1)}, bf16[32,4096]{1,0:T(8,128)(2,1)}, u32[]{:S(2)}, u32[]{:S(2)}) collective-permute-start(bf16[32,4096]{1,0:T(8,128)(2,1)} %get-tuple-element.146), channel_id=1, source_target_pairs={{0,1},{1,0},{2,7},{3,6},{4,5},{5,4},{6,3},{7,2},{8,9},{9,8},{10,15... | collective-permute-start | bytes 786440 | tf_op jit(solution)/shard_map/ppermute | solution.py:233
  167.8 23.8 %collective-permute-start.29 = (bf16[32,4096]{1,0:T(8,128)(2,1)}, bf16[32,4096]{1,0:T(8,128)(2,1)}, u32[]{:S(2)}, u32[]{:S(2)}) collective-permute-start(bf16[32,4096]{1,0:T(8,128)(2,1)} %get-tuple-element.150), channel_id=1, source_target_pairs={{0,2},{1,7},{2,0},{3,5},{4,6},{5,3},{6,4},{7,1},{8,10},{9,15},{10,... | collective-permute-start | bytes 786440 | tf_op jit(solution)/shard_map/ppermute | solution.py:233
  175.3 23.7 %collective-permute-start.31 = (bf16[32,4096]{1,0:T(8,128)(2,1)}, bf16[32,4096]{1,0:T(8,128)(2,1)}, u32[]{:S(2)}, u32[]{:S(2)}) collective-permute-start(bf16[32,4096]{1,0:T(8,128)(2,1)} %get-tuple-element.154), channel_id=1, source_target_pairs={{0,3},{1,6},{2,5},{3,0},{4,7},{5,2},{6,1},{7,4},{8,11},{9,14},{10,... | collective-permute-start | bytes 786440 | tf_op jit(solution)/shard_map/ppermute | solution.py:233
  175.4 31.0 %collective-permute-start.30 = (bf16[32,4096]{1,0:T(8,128)(2,1)}, bf16[32,4096]{1,0:T(8,128)(2,1)}, u32[]{:S(2)}, u32[]{:S(2)}) collective-permute-start(bf16[32,4096]{1,0:T(8,128)(2,1)} %get-tuple-element.152), channel_id=1, source_target_pairs={{0,7},{1,2},{2,1},{3,4},{4,3},{5,6},{6,5},{7,0},{8,15},{9,10},{10,... | collective-permute-start | bytes 786440 | tf_op jit(solution)/shard_map/ppermute | solution.py:233
  191.6 18.3 %collective-permute-start.32 = (bf16[32,4096]{1,0:T(8,128)(2,1)}, bf16[32,4096]{1,0:T(8,128)(2,1)}, u32[]{:S(2)}, u32[]{:S(2)}) collective-permute-start(bf16[32,4096]{1,0:T(8,128)(2,1)} %get-tuple-element.156), channel_id=1, source_target_pairs={{0,4},{1,5},{2,6},{3,7},{4,0},{5,1},{6,2},{7,3},{8,12},{9,13},{10,... | collective-permute-start | bytes 786440 | tf_op jit(solution)/shard_map/ppermute | solution.py:233

commit v16 on v13

--- a/solution.py
+++ b/solution.py
@@ -6,7 +6,7 @@
 from jax.sharding import PartitionSpec as P
 
 VMEM_BYTES = 64 * 1024 * 1024
-PIECES = 4
+PIECES = 2
 SMALL = pl.CostEstimate(flops=1024, bytes_accessed=1024, transcendentals=0)
 BF16 = jnp.bfloat16
 F32 = jnp.float32

time: 211 us -> 211 us (level)
  no operation moved by 1% of the time
where the time goes in v16:
time: 211 us
  starting transfers between devices  95.7 us (45%)
  waiting for transfers between devices  57.7 us (27%)
  Pallas kernels  56.8 us (27%)
    ppermute x33, starting transfers between devices, send(): self.done.append(lax.ppermute(after(value, *earlier), axis, pairs))  95.7 us
    ppermute x33, waiting for transfers between devices, send(): self.done.append(lax.ppermute(after(value, *earlier), axis, pairs))  57.7 us
    pallas_call x10, Pallas kernels, call(): pl.pallas_call(kernel, in_specs=[pl.BlockSpec(memory_space=pltpu.SMEM)] *...  56.8 us
  transfers between devices with their start and end apart: 33, of which 11 were waited for; matrix products, arithmetic and copies ran while one was open for 0% of the time, Pallas kernels for 24%

profile of v16, /device:TPU:0, one launch (start us, length us, event | category | flops | bytes accessed | tf_op | source)
XLA Modules:
  0.0 211.1 jit_solution(5984087606720935640)
XLA Ops:
  0.6 3.3 %place.2 = (bf16[32,4096]{1,0:T(8,128)(2,1)}, bf16[32,4096]{1,0:T(8,128)(2,1)}, bf16[32,4096]{1,0:T(8,128)(2,1)}, bf16[32,4096]{1,0:T(8,128)(2,1)}, bf16[32,4096...) custom-call(s32[1,256]{1,0:T(1,128)} %bitcast.13, ...), custom_call_target="tpu_custom_call" | custom-call | flops 1024 | bytes 1024 | tf_op jit(solution)/shard_map/place/pallas_call | solution.py:28
  3.9 5.1 %collective-permute-start = (bf16[32,4096]{1,0:T(8,128)(2,1)}, bf16[32,4096]{1,0:T(8,128)(2,1)}, u32[]{:S(2)}, u32[]{:S(2)}) collective-permute-start(bf16[32,4096]{1,0:T(8,128)(2,1)} %get-tuple-element.83), channel_id=1, source_target_pairs={{0,5},{1,4},{2,3},{3,2},{4,1},{5,0},{6,7},{7,6},{8,13},{9,12},{10,... | collective-permute-start | bytes 786440 | tf_op jit(solution)/shard_map/ppermute | solution.py:233
  9.0 0.5 collective-permute-start.1
  9.5 1.3 collective-permute-start.2
  10.8 0.2 collective-permute-start.3
  11.1 11.0 %collective-permute-done.refs_1_ = bf16[32,4096]{1,0:T(8,128)(2,1)} collective-permute-done((bf16[32,4096]{1,0:T(8,128)(2,1)}, bf16[32,4096]{1,0:T(8,128)(2,1)}, u32[]{:S(2)}, u32[]{:S(2)}) %collective-permute-start) | collective-permute-done | bytes 262176 | tf_op jit(solution)/shard_map/ppermute | solution.py:233
  22.1 0.0 collective-permute-start.4
  22.1 0.0 collective-permute-done.1.refs_2_
  22.1 7.0 %collective-permute-start.5 = (bf16[32,4096]{1,0:T(8,128)(2,1)}, bf16[32,4096]{1,0:T(8,128)(2,1)}, u32[]{:S(2)}, u32[]{:S(2)}) collective-permute-start(bf16[32,4096]{1,0:T(8,128)(2,1)} %get-tuple-element.90), channel_id=1, source_target_pairs={{0,3},{1,6},{2,5},{3,0},{4,7},{5,2},{6,1},{7,4},{8,11},{9,14},{10,... | collective-permute-start | bytes 786440 | tf_op jit(solution)/shard_map/ppermute | solution.py:233
  29.1 3.3 %place.3 = (bf16[32,4096]{1,0:T(8,128)(2,1)}, bf16[32,4096]{1,0:T(8,128)(2,1)}, bf16[32,4096]{1,0:T(8,128)(2,1)}, bf16[32,4096]{1,0:T(8,128)(2,1)}, bf16[32,4096...) custom-call(s32[1,256]{1,0:T(1,128)} %bitcast.14, ...), custom_call_target="tpu_custom_call" | custom-call | flops 1024 | bytes 1024 | tf_op jit(solution)/shard_map/place/pallas_call | solution.py:28
  32.4 0.0 collective-permute-done.2.refs_3_
  32.4 8.5 %collective-permute-start.6 = (bf16[32,4096]{1,0:T(8,128)(2,1)}, bf16[32,4096]{1,0:T(8,128)(2,1)}, u32[]{:S(2)}, u32[]{:S(2)}) collective-permute-start(bf16[32,4096]{1,0:T(8,128)(2,1)} %get-tuple-element.92), channel_id=1, source_target_pairs={{0,4},{1,5},{2,6},{3,7},{4,0},{5,1},{6,2},{7,3},{8,12},{9,13},{10,... | collective-permute-start | bytes 786440 | tf_op jit(solution)/shard_map/ppermute | solution.py:233
  40.8 0.0 collective-permute-done.3.refs_4_
  40.8 1.7 collective-permute-start.14
  42.5 15.6 %collective-permute-start.7 = (bf16[32,4096]{1,0:T(8,128)(2,1)}, bf16[32,4096]{1,0:T(8,128)(2,1)}, u32[]{:S(2)}, u32[]{:S(2)}) collective-permute-start(bf16[32,4096]{1,0:T(8,128)(2,1)} %get-tuple-element.96), channel_id=1, source_target_pairs={{0,6},{1,3},{2,4},{3,1},{4,2},{5,7},{6,0},{7,5},{8,14},{9,11},{10,... | collective-permute-start | bytes 786440 | tf_op jit(solution)/shard_map/ppermute | solution.py:233
  58.1 0.0 collective-permute-done.6.refs_7_
  58.1 8.9 %collective-permute-start.9 = (bf16[32,4096]{1,0:T(8,128)(2,1)}, bf16[32,4096]{1,0:T(8,128)(2,1)}, u32[]{:S(2)}, u32[]{:S(2)}) collective-permute-start(bf16[32,4096]{1,0:T(8,128)(2,1)} %get-tuple-element.100), channel_id=1, source_target_pairs={{0,2},{1,7},{2,0},{3,5},{4,6},{5,3},{6,4},{7,1},{8,10},{9,15},{10,... | collective-permute-start | bytes 786440 | tf_op jit(solution)/shard_map/ppermute | solution.py:233
  67.0 8.5 %collective-permute-done.11.refs_1_ = bf16[32,4096]{1,0:T(8,128)(2,1)} collective-permute-done((bf16[32,4096]{1,0:T(8,128)(2,1)}, bf16[32,4096]{1,0:T(8,128)(2,1)}, u32[]{:S(2)}, u32[]{:S(2)}) %collective-permute-start.11) | collective-permute-done | bytes 262176 | tf_op jit(solution)/shard_map/ppermute | solution.py:233
  75.5 0.0 collective-permute-start.12
  75.5 0.0 collective-permute-done.14.refs_2_
  75.5 0.0 collective-permute-start.15
  75.6 10.9 %expert.2 = (bf16[32,4096]{1,0:T(8,128)(2,1)}, bf16[32,4096]{1,0:T(8,128)(2,1)}, bf16[32,4096]{1,0:T(8,128)(2,1)}, bf16[32,4096]{1,0:T(8,128)(2,1)}, bf16[32,409...) custom-call(bf16[32,4096]{1,0:T(8,128)(2,1)} %get-tuple-element.82.r, ...), custom_call_target="tpu_custom_call" | custom-call | flops 1024 | bytes 1024 | tf_op jit(solution)/shard_map/expert/pallas_call | solution.py:28
  86.5 0.0 collective-permute-done.7.refs_3_
  86.5 5.3 %collective-permute-start.17 = (bf16[32,4096]{1,0:T(8,128)(2,1)}, bf16[32,4096]{1,0:T(8,128)(2,1)}, u32[]{:S(2)}, u32[]{:S(2)}) collective-permute-start(bf16[32,4096]{1,0:T(8,128)(2,1)} %get-tuple-element.116), channel_id=1, source_target_pairs={{0,4},{1,5},{2,6},{3,7},{4,0},{5,1},{6,2},{7,3},{8,12},{9,13},{10,... | collective-permute-start | bytes 786440 | tf_op jit(solution)/shard_map/ppermute | solution.py:233
  91.8 0.4 collective-permute-start.13
  92.2 14.9 %collective-permute-start.10 = (bf16[32,4096]{1,0:T(8,128)(2,1)}, bf16[32,4096]{1,0:T(8,128)(2,1)}, u32[]{:S(2)}, u32[]{:S(2)}) collective-permute-start(bf16[32,4096]{1,0:T(8,128)(2,1)} %get-tuple-element.101), channel_id=1, source_target_pairs={{0,1},{1,0},{2,7},{3,6},{4,5},{5,4},{6,3},{7,2},{8,9},{9,8},{10,15... | collective-permute-start | bytes 786440 | tf_op jit(solution)/shard_map/ppermute | solution.py:233
  107.1 0.0 collective-permute-start.8
  107.1 0.0 collective-permute-done.15.refs_6_
  107.1 0.0 collective-permute-start.16
  107.1 3.6 %collective-permute-done.17.refs_7_ = bf16[32,4096]{1,0:T(8,128)(2,1)} collective-permute-done((bf16[32,4096]{1,0:T(8,128)(2,1)}, bf16[32,4096]{1,0:T(8,128)(2,1)}, u32[]{:S(2)}, u32[]{:S(2)}) %collective-permute-start.17) | collective-permute-done | bytes 262176 | tf_op jit(solution)/shard_map/ppermute | solution.py:233
  110.7 11.1 %expert.3 = (bf16[32,4096]{1,0:T(8,128)(2,1)}, bf16[32,4096]{1,0:T(8,128)(2,1)}, bf16[32,4096]{1,0:T(8,128)(2,1)}, bf16[32,4096]{1,0:T(8,128)(2,1)}, bf16[32,409...) custom-call(bf16[32,4096]{1,0:T(8,128)(2,1)} %get-tuple-element.124., ...), custom_call_target="tpu_custom_call" | custom-call | flops 1024 | bytes 1024 | tf_op jit(solution)/shard_map/expert/pallas_call | solution.py:28
  121.7 4.4 %weight_part.4 = (bf16[16,2176]{1,0:T(8,128)(2,1)}, bf16[496,2176]{1,0:T(8,128)(2,1)}) custom-call(s32[1]{0:T(128)} %bitcast.4.refs_0_, bf16[256,4096]{1,0:T(8,128)(2,1)} %get-tuple-element.138.refs_1_, bf16[256,1408]{1,0:T(8,128)(2,1)} %get-tuple-element.127.refs_2_, bf16[256,704]{1,0:T(8,128)(2,1)} %get-tuple-element.128.refs_3_, ...), custom_call_target="tpu_custom_call" | custom-call | flops 1024 | bytes 1024 | tf_op jit(solution)/shard_map/weight_part/pallas_call | solution.py:28
  126.1 0.1 collective-permute-start.21
  126.2 0.0 collective-permute-done.10.refs_5_
  126.2 0.0 collective-permute-done.8.refs_4_
  126.2 1.6 collective-permute-done.21.refs_7_
  127.8 0.2 collective-permute-start.22
  127.9 1.0 collective-permute-start.19
  128.9 4.3 %weight_part.5 = bf16[512,2176]{1,0:T(8,128)(2,1)} custom-call(s32[1]{0:T(128)} %bitcast.5.refs_0_, bf16[256,4096]{1,0:T(8,128)(2,1)} %get-tuple-element.138.refs_1_, bf16[256,1408]{1,0:T(8,128)(2,1)} %get-tuple-element.127.refs_2_, bf16[256,704]{1,0:T(8,128)(2,1)} %get-tuple-element.128.refs_3_, bf16[256,4096]{1,0:T(8,128)(2,1)} %get-tuple-element.129.refs_4_, ...), custom_call_target="tpu_custom_call" | custom-call | flops 1024 | bytes 1024 | tf_op jit(solution)/shard_map/weight_part/pallas_call | solution.py:28
  133.3 5.2 %weight_part.6 = (bf16[16,2176]{1,0:T(8,128)(2,1)}, bf16[496,2176]{1,0:T(8,128)(2,1)}) custom-call(s32[1]{0:T(128)} %bitcast.6.refs_0_, bf16[256,4096]{1,0:T(8,128)(2,1)} %get-tuple-element.138.refs_1_, bf16[256,1408]{1,0:T(8,128)(2,1)} %get-tuple-element.127.refs_2_, bf16[256,704]{1,0:T(8,128)(2,1)} %get-tuple-element.128.refs_3_, ...), custom_call_target="tpu_custom_call" | custom-call | flops 1024 | bytes 1024 | tf_op jit(solution)/shard_map/weight_part/pallas_call | solution.py:28
  138.4 1.1 collective-permute-start.24
  139.6 0.6 collective-permute-done.18.refs_8_
  140.1 3.2 %collective-permute-done.19.refs_9_ = bf16[32,4096]{1,0:T(8,128)(2,1)} collective-permute-done((bf16[32,4096]{1,0:T(8,128)(2,1)}, bf16[32,4096]{1,0:T(8,128)(2,1)}, u32[]{:S(2)}, u32[]{:S(2)}) %collective-permute-start.19) | collective-permute-done | bytes 262176 | tf_op jit(solution)/shard_map/ppermute | solution.py:233
  143.3 0.0 collective-permute-done.24.refs_8_
  143.3 1.0 collective-permute-start.25
  144.4 4.1 %collective-permute-start.20 = (bf16[32,4096]{1,0:T(8,128)(2,1)}, bf16[32,4096]{1,0:T(8,128)(2,1)}, u32[]{:S(2)}, u32[]{:S(2)}) collective-permute-start(bf16[32,4096]{1,0:T(8,128)(2,1)} %get-tuple-element.121), channel_id=1, source_target_pairs={{0,4},{1,5},{2,6},{3,7},{4,0},{5,1},{6,2},{7,3},{8,12},{9,13},{10,... | collective-permute-start | bytes 786440 | tf_op jit(solution)/shard_map/ppermute | solution.py:233
  148.5 10.8 %collective-permute-done.20.refs_10_ = bf16[32,4096]{1,0:T(8,128)(2,1)} collective-permute-done((bf16[32,4096]{1,0:T(8,128)(2,1)}, bf16[32,4096]{1,0:T(8,128)(2,1)}, u32[]{:S(2)}, u32[]{:S(2)}) %collective-permute-start.20) | collective-permute-done | bytes 262176 | tf_op jit(solution)/shard_map/ppermute | solution.py:233
  159.2 0.0 collective-permute-start.29
  159.2 1.5 collective-permute-start.28
  160.7 1.3 collective-permute-start.27
  162.1 8.9 %collective-permute-done.29.refs_7_ = bf16[32,4096]{1,0:T(8,128)(2,1)} collective-permute-done((bf16[32,4096]{1,0:T(8,128)(2,1)}, bf16[32,4096]{1,0:T(8,128)(2,1)}, u32[]{:S(2)}, u32[]{:S(2)}) %collective-permute-start.29) | collective-permute-done | bytes 262176 | tf_op jit(solution)/shard_map/ppermute | solution.py:233
  170.9 3.1 %collective-permute-start.26 = (bf16[32,4096]{1,0:T(8,128)(2,1)}, bf16[32,4096]{1,0:T(8,128)(2,1)}, u32[]{:S(2)}, u32[]{:S(2)}) collective-permute-start(bf16[32,4096]{1,0:T(8,128)(2,1)} %get-tuple-element.144), channel_id=1, source_target_pairs={{0,5},{1,4},{2,3},{3,2},{4,1},{5,0},{6,7},{7,6},{8,13},{9,12},{10,... | collective-permute-start | bytes 786440 | tf_op jit(solution)/shard_map/ppermute | solution.py:233
  174.0 3.8 %combine.2 = (bf16[256,2048]{1,0:T(8,128)(2,1)}, bf16[256,2048]{1,0:T(8,128)(2,1)}) custom-call(s32[1,256]{1,0:T(1,128)} %bitcast.15, bf16[256,2048]{1,0:T(8,128)(2,1)} %refs_1_.5, bf16[256,2048]{1,0:T(8,128)(2,1)} %refs_2_.5, bf16[32,4096]{1,0:T(8,128)(2,1)} %get-tuple-element.93.refs_3_, bf16[32,4096]{1,0:T(8,128)(2,1)} %collective-permute-done.8.refs_4_, ...), custom_call_target="tpu_custom_call" | custom-call | flops 1024 | bytes 1024 | tf_op jit(solution)/shard_map/combine/pallas_call | solution.py:28
  177.9 0.0 collective-permute-done.28.refs_6_
  177.9 7.0 %collective-permute-start.32 = (bf16[32,4096]{1,0:T(8,128)(2,1)}, bf16[32,4096]{1,0:T(8,128)(2,1)}, u32[]{:S(2)}, u32[]{:S(2)}) collective-permute-start(bf16[32,4096]{1,0:T(8,128)(2,1)} %get-tuple-element.156), channel_id=1, source_target_pairs={{0,4},{1,5},{2,6},{3,7},{4,0},{5,1},{6,2},{7,3},{8,12},{9,13},{10,... | collective-permute-start | bytes 786440 | tf_op jit(solution)/shard_map/ppermute | solution.py:233
  184.9 4.1 %collective-permute-start.31 = (bf16[32,4096]{1,0:T(8,128)(2,1)}, bf16[32,4096]{1,0:T(8,128)(2,1)}, u32[]{:S(2)}, u32[]{:S(2)}) collective-permute-start(bf16[32,4096]{1,0:T(8,128)(2,1)} %get-tuple-element.154), channel_id=1, source_target_pairs={{0,3},{1,6},{2,5},{3,0},{4,7},{5,2},{6,1},{7,4},{8,11},{9,14},{10,... | collective-permute-start | bytes 786440 | tf_op jit(solution)/shard_map/ppermute | solution.py:233
  189.0 3.6 %collective-permute-done.26.refs_4_ = bf16[32,4096]{1,0:T(8,128)(2,1)} collective-permute-done((bf16[32,4096]{1,0:T(8,128)(2,1)}, bf16[32,4096]{1,0:T(8,128)(2,1)}, u32[]{:S(2)}, u32[]{:S(2)}) %collective-permute-start.26) | collective-permute-done | bytes 262176 | tf_op jit(solution)/shard_map/ppermute | solution.py:233
  192.6 1.9 collective-permute-start.30
  194.4 0.0 collective-permute-done.25.refs_9_
  194.4 6.8 %weight_part.7 = (f32[512,1408]{1,0:T(8,128)}, f32[704,512]{1,0:T(8,128)}) custom-call(s32[1]{0:T(128)} %bitcast.3.refs_0_, bf16[256,4096]{1,0:T(8,128)(2,1)} %get-tuple-element.138.refs_1_, bf16[256,1408]{1,0:T(8,128)(2,1)} %get-tuple-element.127.refs_2_, bf16[256,704]{1,0:T(8,128)(2,1)} %get-tuple-element.128.refs_3_, ...), custom_call_target="tpu_custom_call" | custom-call | flops 1024 | bytes 1024 | tf_op jit(solution)/shard_map/weight_part/pallas_call | solution.py:28
  201.2 2.2 %collective-permute-done.32.refs_10_ = bf16[32,4096]{1,0:T(8,128)(2,1)} collective-permute-done((bf16[32,4096]{1,0:T(8,128)(2,1)}, bf16[32,4096]{1,0:T(8,128)(2,1)}, u32[]{:S(2)}, u32[]{:S(2)}) %collective-permute-start.32) | collective-permute-done | bytes 262176 | tf_op jit(solution)/shard_map/ppermute | solution.py:233
  203.4 3.8 %collective-permute-done.31.refs_9_ = bf16[32,4096]{1,0:T(8,128)(2,1)} collective-permute-done((bf16[32,4096]{1,0:T(8,128)(2,1)}, bf16[32,4096]{1,0:T(8,128)(2,1)}, u32[]{:S(2)}, u32[]{:S(2)}) %collective-permute-start.31) | collective-permute-done | bytes 262176 | tf_op jit(solution)/shard_map/ppermute | solution.py:233
  207.2 0.0 collective-permute-done.30.refs_8_
  207.2 3.8 %combine.3 = (bf16[256,2048]{1,0:T(8,128)(2,1)}, bf16[256,2048]{1,0:T(8,128)(2,1)}) custom-call(s32[1,256]{1,0:T(1,128)} %bitcast.16, bf16[256,2048]{1,0:T(8,128)(2,1)} %get-tuple-element.122.refs_1_, bf16[256,2048]{1,0:T(8,128)(2,1)} %get-tuple-element.123.refs_2_, bf16[32,4096]{1,0:T(8,128)(2,1)} %get-tuple-element.142.refs_3_, ...), custom_call_target="tpu_custom_call" | custom-call | flops 1024 | bytes 1024 | tf_op jit(solution)/shard_map/combine/pallas_call | solution.py:28
  (12 shorter events, 0.0 us)
Async XLA Ops:
  3.9 18.2 %collective-permute-start = (bf16[32,4096]{1,0:T(8,128)(2,1)}, bf16[32,4096]{1,0:T(8,128)(2,1)}, u32[]{:S(2)}, u32[]{:S(2)}) collective-permute-start(bf16[32,4096]{1,0:T(8,128)(2,1)} %get-tuple-element.83), channel_id=1, source_target_pairs={{0,5},{1,4},{2,3},{3,2},{4,1},{5,0},{6,7},{7,6},{8,13},{9,12},{10,... | collective-permute-start | bytes 786440 | tf_op jit(solution)/shard_map/ppermute | solution.py:233
  9.0 13.1 %collective-permute-start.1 = (bf16[32,4096]{1,0:T(8,128)(2,1)}, bf16[32,4096]{1,0:T(8,128)(2,1)}, u32[]{:S(2)}, u32[]{:S(2)}) collective-permute-start(bf16[32,4096]{1,0:T(8,128)(2,1)} %get-tuple-element.84), channel_id=1, source_target_pairs={{0,1},{1,0},{2,7},{3,6},{4,5},{5,4},{6,3},{7,2},{8,9},{9,8},{10,15... | collective-permute-start | bytes 786440 | tf_op jit(solution)/shard_map/ppermute | solution.py:233
  9.5 22.9 %collective-permute-start.2 = (bf16[32,4096]{1,0:T(8,128)(2,1)}, bf16[32,4096]{1,0:T(8,128)(2,1)}, u32[]{:S(2)}, u32[]{:S(2)}) collective-permute-start(bf16[32,4096]{1,0:T(8,128)(2,1)} %get-tuple-element.85), channel_id=1, source_target_pairs={{0,6},{1,3},{2,4},{3,1},{4,2},{5,7},{6,0},{7,5},{8,14},{9,11},{10,... | collective-permute-start | bytes 786440 | tf_op jit(solution)/shard_map/ppermute | solution.py:233
  10.8 30.0 %collective-permute-start.3 = (bf16[32,4096]{1,0:T(8,128)(2,1)}, bf16[32,4096]{1,0:T(8,128)(2,1)}, u32[]{:S(2)}, u32[]{:S(2)}) collective-permute-start(bf16[32,4096]{1,0:T(8,128)(2,1)} %get-tuple-element.86), channel_id=1, source_target_pairs={{0,2},{1,7},{2,0},{3,5},{4,6},{5,3},{6,4},{7,1},{8,10},{9,15},{10,... | collective-permute-start | bytes 786440 | tf_op jit(solution)/shard_map/ppermute | solution.py:233
  22.1 18.8 %collective-permute-start.4 = (bf16[32,4096]{1,0:T(8,128)(2,1)}, bf16[32,4096]{1,0:T(8,128)(2,1)}, u32[]{:S(2)}, u32[]{:S(2)}) collective-permute-start(bf16[32,4096]{1,0:T(8,128)(2,1)} %get-tuple-element.88), channel_id=1, source_target_pairs={{0,7},{1,2},{2,1},{3,4},{4,3},{5,6},{6,5},{7,0},{8,15},{9,10},{10,... | collective-permute-start | bytes 786440 | tf_op jit(solution)/shard_map/ppermute | solution.py:233
  22.1 20.4 %collective-permute-start.5 = (bf16[32,4096]{1,0:T(8,128)(2,1)}, bf16[32,4096]{1,0:T(8,128)(2,1)}, u32[]{:S(2)}, u32[]{:S(2)}) collective-permute-start(bf16[32,4096]{1,0:T(8,128)(2,1)} %get-tuple-element.90), channel_id=1, source_target_pairs={{0,3},{1,6},{2,5},{3,0},{4,7},{5,2},{6,1},{7,4},{8,11},{9,14},{10,... | collective-permute-start | bytes 786440 | tf_op jit(solution)/shard_map/ppermute | solution.py:233
  32.4 25.8 %collective-permute-start.6 = (bf16[32,4096]{1,0:T(8,128)(2,1)}, bf16[32,4096]{1,0:T(8,128)(2,1)}, u32[]{:S(2)}, u32[]{:S(2)}) collective-permute-start(bf16[32,4096]{1,0:T(8,128)(2,1)} %get-tuple-element.92), channel_id=1, source_target_pairs={{0,4},{1,5},{2,6},{3,7},{4,0},{5,1},{6,2},{7,3},{8,12},{9,13},{10,... | collective-permute-start | bytes 786440 | tf_op jit(solution)/shard_map/ppermute | solution.py:233
  40.8 34.7 %collective-permute-start.11 = (bf16[32,4096]{1,0:T(8,128)(2,1)}, bf16[32,4096]{1,0:T(8,128)(2,1)}, u32[]{:S(2)}, u32[]{:S(2)}) collective-permute-start(bf16[32,4096]{1,0:T(8,128)(2,1)} %get-tuple-element.105), channel_id=1, source_target_pairs={{0,5},{1,4},{2,3},{3,2},{4,1},{5,0},{6,7},{7,6},{8,13},{9,12},{10,... | collective-permute-start | bytes 786440 | tf_op jit(solution)/shard_map/ppermute | solution.py:233
  40.8 34.7 %collective-permute-start.14 = (bf16[32,4096]{1,0:T(8,128)(2,1)}, bf16[32,4096]{1,0:T(8,128)(2,1)}, u32[]{:S(2)}, u32[]{:S(2)}) collective-permute-start(bf16[32,4096]{1,0:T(8,128)(2,1)} %get-tuple-element.111), channel_id=1, source_target_pairs={{0,1},{1,0},{2,7},{3,6},{4,5},{5,4},{6,3},{7,2},{8,9},{9,8},{10,15... | collective-permute-start | bytes 786440 | tf_op jit(solution)/shard_map/ppermute | solution.py:233
  42.5 43.9 %collective-permute-start.7 = (bf16[32,4096]{1,0:T(8,128)(2,1)}, bf16[32,4096]{1,0:T(8,128)(2,1)}, u32[]{:S(2)}, u32[]{:S(2)}) collective-permute-start(bf16[32,4096]{1,0:T(8,128)(2,1)} %get-tuple-element.96), channel_id=1, source_target_pairs={{0,6},{1,3},{2,4},{3,1},{4,2},{5,7},{6,0},{7,5},{8,14},{9,11},{10,... | collective-permute-start | bytes 786440 | tf_op jit(solution)/shard_map/ppermute | solution.py:233
  58.1 33.7 %collective-permute-start.9 = (bf16[32,4096]{1,0:T(8,128)(2,1)}, bf16[32,4096]{1,0:T(8,128)(2,1)}, u32[]{:S(2)}, u32[]{:S(2)}) collective-permute-start(bf16[32,4096]{1,0:T(8,128)(2,1)} %get-tuple-element.100), channel_id=1, source_target_pairs={{0,2},{1,7},{2,0},{3,5},{4,6},{5,3},{6,4},{7,1},{8,10},{9,15},{10,... | collective-permute-start | bytes 786440 | tf_op jit(solution)/shard_map/ppermute | solution.py:233
  75.5 16.3 %collective-permute-start.12 = (bf16[32,4096]{1,0:T(8,128)(2,1)}, bf16[32,4096]{1,0:T(8,128)(2,1)}, u32[]{:S(2)}, u32[]{:S(2)}) collective-permute-start(bf16[32,4096]{1,0:T(8,128)(2,1)} %get-tuple-element.106), channel_id=1, source_target_pairs={{0,7},{1,2},{2,1},{3,4},{4,3},{5,6},{6,5},{7,0},{8,15},{9,10},{10,... | collective-permute-start | bytes 786440 | tf_op jit(solution)/shard_map/ppermute | solution.py:233
  75.5 31.5 %collective-permute-start.15 = (bf16[32,4096]{1,0:T(8,128)(2,1)}, bf16[32,4096]{1,0:T(8,128)(2,1)}, u32[]{:S(2)}, u32[]{:S(2)}) collective-permute-start(bf16[32,4096]{1,0:T(8,128)(2,1)} %get-tuple-element.112), channel_id=1, source_target_pairs={{0,3},{1,6},{2,5},{3,0},{4,7},{5,2},{6,1},{7,4},{8,11},{9,14},{10,... | collective-permute-start | bytes 786440 | tf_op jit(solution)/shard_map/ppermute | solution.py:233
  86.5 24.2 %collective-permute-start.17 = (bf16[32,4096]{1,0:T(8,128)(2,1)}, bf16[32,4096]{1,0:T(8,128)(2,1)}, u32[]{:S(2)}, u32[]{:S(2)}) collective-permute-start(bf16[32,4096]{1,0:T(8,128)(2,1)} %get-tuple-element.116), channel_id=1, source_target_pairs={{0,4},{1,5},{2,6},{3,7},{4,0},{5,1},{6,2},{7,3},{8,12},{9,13},{10,... | collective-permute-start | bytes 786440 | tf_op jit(solution)/shard_map/ppermute | solution.py:233
  91.8 34.4 %collective-permute-start.13 = (bf16[32,4096]{1,0:T(8,128)(2,1)}, bf16[32,4096]{1,0:T(8,128)(2,1)}, u32[]{:S(2)}, u32[]{:S(2)}) collective-permute-start(bf16[32,4096]{1,0:T(8,128)(2,1)} %get-tuple-element.107), channel_id=1, source_target_pairs={{0,6},{1,3},{2,4},{3,1},{4,2},{5,7},{6,0},{7,5},{8,14},{9,11},{10,... | collective-permute-start | bytes 786440 | tf_op jit(solution)/shard_map/ppermute | solution.py:233
  92.2 34.0 %collective-permute-start.10 = (bf16[32,4096]{1,0:T(8,128)(2,1)}, bf16[32,4096]{1,0:T(8,128)(2,1)}, u32[]{:S(2)}, u32[]{:S(2)}) collective-permute-start(bf16[32,4096]{1,0:T(8,128)(2,1)} %get-tuple-element.101), channel_id=1, source_target_pairs={{0,1},{1,0},{2,7},{3,6},{4,5},{5,4},{6,3},{7,2},{8,9},{9,8},{10,15... | collective-permute-start | bytes 786440 | tf_op jit(solution)/shard_map/ppermute | solution.py:233
  107.1 19.1 %collective-permute-start.8 = (bf16[32,4096]{1,0:T(8,128)(2,1)}, bf16[32,4096]{1,0:T(8,128)(2,1)}, u32[]{:S(2)}, u32[]{:S(2)}) collective-permute-start(bf16[32,4096]{1,0:T(8,128)(2,1)} %get-tuple-element.97), channel_id=1, source_target_pairs={{0,5},{1,4},{2,3},{3,2},{4,1},{5,0},{6,7},{7,6},{8,13},{9,12},{10,... | collective-permute-start | bytes 786440 | tf_op jit(solution)/shard_map/ppermute | solution.py:233
  107.1 20.7 %collective-permute-start.16 = (bf16[32,4096]{1,0:T(8,128)(2,1)}, bf16[32,4096]{1,0:T(8,128)(2,1)}, u32[]{:S(2)}, u32[]{:S(2)}) collective-permute-start(bf16[32,4096]{1,0:T(8,128)(2,1)} %get-tuple-element.113), channel_id=1, source_target_pairs={{0,2},{1,7},{2,0},{3,5},{4,6},{5,3},{6,4},{7,1},{8,10},{9,15},{10,... | collective-permute-start | bytes 786440 | tf_op jit(solution)/shard_map/ppermute | solution.py:233
  126.1 1.7 collective-permute-start.21
  127.8 5.5 %collective-permute-start.22 = (bf16[496,2176]{1,0:T(8,128)(2,1)}, bf16[496,2176]{1,0:T(8,128)(2,1)}, u32[]{:S(2)}, u32[]{:S(2)}) collective-permute-start(bf16[496,2176]{1,0:T(8,128)(2,1)} %get-tuple-element.136), channel_id=1, source_target_pairs={{0,8},{8,0},{16,24},{24,16},{1,9},{9,1},{17,25},{25,17},{2,10},{10... | collective-permute-start | bytes 6475784 | tf_op jit(solution)/shard_map/ppermute | solution.py:233
  127.9 12.2 %collective-permute-start.18 = (bf16[32,4096]{1,0:T(8,128)(2,1)}, bf16[32,4096]{1,0:T(8,128)(2,1)}, u32[]{:S(2)}, u32[]{:S(2)}) collective-permute-start(bf16[32,4096]{1,0:T(8,128)(2,1)} %get-tuple-element.117), channel_id=1, source_target_pairs={{0,7},{1,2},{2,1},{3,4},{4,3},{5,6},{6,5},{7,0},{8,15},{9,10},{10,... | collective-permute-start | bytes 786440 | tf_op jit(solution)/shard_map/ppermute | solution.py:233
  127.9 15.4 %collective-permute-start.19 = (bf16[32,4096]{1,0:T(8,128)(2,1)}, bf16[32,4096]{1,0:T(8,128)(2,1)}, u32[]{:S(2)}, u32[]{:S(2)}) collective-permute-start(bf16[32,4096]{1,0:T(8,128)(2,1)} %get-tuple-element.119), channel_id=1, source_target_pairs={{0,3},{1,6},{2,5},{3,0},{4,7},{5,2},{6,1},{7,4},{8,11},{9,14},{10,... | collective-permute-start | bytes 786440 | tf_op jit(solution)/shard_map/ppermute | solution.py:233
  138.4 4.9 %collective-permute-start.24 = (bf16[16,2176]{1,0:T(8,128)(2,1)}, bf16[16,2176]{1,0:T(8,128)(2,1)}, u32[]{:S(2)}, u32[]{:S(2)}) collective-permute-start(bf16[16,2176]{1,0:T(8,128)(2,1)} %get-tuple-element.137), channel_id=1, source_target_pairs={{0,16},{8,24},{16,0},{24,8},{1,17},{9,25},{17,1},{25,9},{2,18},{10... | collective-permute-start | bytes 208904 | tf_op jit(solution)/shard_map/ppermute | solution.py:233
  139.6 54.9 %collective-permute-start.23 = (bf16[512,2176]{1,0:T(8,128)(2,1)}, bf16[512,2176]{1,0:T(8,128)(2,1)}, u32[]{:S(2)}, u32[]{:S(2)}) collective-permute-start(bf16[512,2176]{1,0:T(8,128)(2,1)} %weight_part.5), channel_id=1, source_target_pairs={{0,8},{8,0},{16,24},{24,16},{1,9},{9,1},{17,25},{25,17},{2,10},{10... | collective-permute-start | bytes 6684680 | tf_op jit(solution)/shard_map/ppermute | solution.py:233
  143.3 51.1 %collective-permute-start.25 = (bf16[496,2176]{1,0:T(8,128)(2,1)}, bf16[496,2176]{1,0:T(8,128)(2,1)}, u32[]{:S(2)}, u32[]{:S(2)}) collective-permute-start(bf16[496,2176]{1,0:T(8,128)(2,1)} %get-tuple-element.140), channel_id=1, source_target_pairs={{0,16},{8,24},{16,0},{24,8},{1,17},{9,25},{17,1},{25,9},{2,18},{10... | collective-permute-start | bytes 6475784 | tf_op jit(solution)/shard_map/ppermute | solution.py:233
  144.4 14.8 %collective-permute-start.20 = (bf16[32,4096]{1,0:T(8,128)(2,1)}, bf16[32,4096]{1,0:T(8,128)(2,1)}, u32[]{:S(2)}, u32[]{:S(2)}) collective-permute-start(bf16[32,4096]{1,0:T(8,128)(2,1)} %get-tuple-element.121), channel_id=1, source_target_pairs={{0,4},{1,5},{2,6},{3,7},{4,0},{5,1},{6,2},{7,3},{8,12},{9,13},{10,... | collective-permute-start | bytes 786440 | tf_op jit(solution)/shard_map/ppermute | solution.py:233
  159.2 11.7 %collective-permute-start.29 = (bf16[32,4096]{1,0:T(8,128)(2,1)}, bf16[32,4096]{1,0:T(8,128)(2,1)}, u32[]{:S(2)}, u32[]{:S(2)}) collective-permute-start(bf16[32,4096]{1,0:T(8,128)(2,1)} %get-tuple-element.150), channel_id=1, source_target_pairs={{0,2},{1,7},{2,0},{3,5},{4,6},{5,3},{6,4},{7,1},{8,10},{9,15},{10,... | collective-permute-start | bytes 786440 | tf_op jit(solution)/shard_map/ppermute | solution.py:233
  159.2 18.6 %collective-permute-start.28 = (bf16[32,4096]{1,0:T(8,128)(2,1)}, bf16[32,4096]{1,0:T(8,128)(2,1)}, u32[]{:S(2)}, u32[]{:S(2)}) collective-permute-start(bf16[32,4096]{1,0:T(8,128)(2,1)} %get-tuple-element.148), channel_id=1, source_target_pairs={{0,6},{1,3},{2,4},{3,1},{4,2},{5,7},{6,0},{7,5},{8,14},{9,11},{10,... | collective-permute-start | bytes 786440 | tf_op jit(solution)/shard_map/ppermute | solution.py:233
  160.7 24.1 %collective-permute-start.27 = (bf16[32,4096]{1,0:T(8,128)(2,1)}, bf16[32,4096]{1,0:T(8,128)(2,1)}, u32[]{:S(2)}, u32[]{:S(2)}) collective-permute-start(bf16[32,4096]{1,0:T(8,128)(2,1)} %get-tuple-element.146), channel_id=1, source_target_pairs={{0,1},{1,0},{2,7},{3,6},{4,5},{5,4},{6,3},{7,2},{8,9},{9,8},{10,15... | collective-permute-start | bytes 786440 | tf_op jit(solution)/shard_map/ppermute | solution.py:233
  170.9 21.6 %collective-permute-start.26 = (bf16[32,4096]{1,0:T(8,128)(2,1)}, bf16[32,4096]{1,0:T(8,128)(2,1)}, u32[]{:S(2)}, u32[]{:S(2)}) collective-permute-start(bf16[32,4096]{1,0:T(8,128)(2,1)} %get-tuple-element.144), channel_id=1, source_target_pairs={{0,5},{1,4},{2,3},{3,2},{4,1},{5,0},{6,7},{7,6},{8,13},{9,12},{10,... | collective-permute-start | bytes 786440 | tf_op jit(solution)/shard_map/ppermute | solution.py:233
  177.9 25.5 %collective-permute-start.32 = (bf16[32,4096]{1,0:T(8,128)(2,1)}, bf16[32,4096]{1,0:T(8,128)(2,1)}, u32[]{:S(2)}, u32[]{:S(2)}) collective-permute-start(bf16[32,4096]{1,0:T(8,128)(2,1)} %get-tuple-element.156), channel_id=1, source_target_pairs={{0,4},{1,5},{2,6},{3,7},{4,0},{5,1},{6,2},{7,3},{8,12},{9,13},{10,... | collective-permute-start | bytes 786440 | tf_op jit(solution)/shard_map/ppermute | solution.py:233
  184.9 22.3 %collective-permute-start.31 = (bf16[32,4096]{1,0:T(8,128)(2,1)}, bf16[32,4096]{1,0:T(8,128)(2,1)}, u32[]{:S(2)}, u32[]{:S(2)}) collective-permute-start(bf16[32,4096]{1,0:T(8,128)(2,1)} %get-tuple-element.154), channel_id=1, source_target_pairs={{0,3},{1,6},{2,5},{3,0},{4,7},{5,2},{6,1},{7,4},{8,11},{9,14},{10,... | collective-permute-start | bytes 786440 | tf_op jit(solution)/shard_map/ppermute | solution.py:233
  192.6 14.6 %collective-permute-start.30 = (bf16[32,4096]{1,0:T(8,128)(2,1)}, bf16[32,4096]{1,0:T(8,128)(2,1)}, u32[]{:S(2)}, u32[]{:S(2)}) collective-permute-start(bf16[32,4096]{1,0:T(8,128)(2,1)} %get-tuple-element.152), channel_id=1, source_target_pairs={{0,7},{1,2},{2,1},{3,4},{4,3},{5,6},{6,5},{7,0},{8,15},{9,10},{10,... | collective-permute-start | bytes 786440 | tf_op jit(solution)/shard_map/ppermute | solution.py:233
